TPU v7x, 32 devices: a whole 2x2x4 slice. The times are simulated.
32 devices in a mesh: virt: 2 (over y), walk: 16 (over z, x, core).
Axes of the slice: x: 2, y: 2, z: 4, core: 2. Of those that a mesh axis runs over, the one named last changes fastest.
Arguments:
- inverse_rows: bfloat16 [16, 512, 2048], P('walk', None, 'virt'), may hold values from -1.5 to 1.5
- kinetic_rows: bfloat16 [16, 512, 2048], P('walk', None, 'virt'), may hold values from -1 to 1
- virt_values: bfloat16 [16, 2048, 4096], P('walk', None, 'virt'), may hold values from -6 to 6
- virt_laplacians: bfloat16 [16, 2048, 4096], P('walk', None, 'virt'), may hold values from -6 to 6
- local_energy: float32 [16], P('walk'), may hold values from 0.2 to 6, as said below
Outputs:
- energy_gradient: float32 [512, 4096], P('walk', 'virt')
- log_derivative_mean: float32 [512, 4096], P('walk', 'virt')
Inputs may be any that keep to these rules, and one draw needn't show every extreme that they name: `local_energy`: positive local energies.
All inputs are finite; a program needn't handle non-finite values.
Results may differ from a plain program's by a relative error of at most 0.0003.
Values may be sent and summed in bfloat16 or wider, within the bound.
No kernel may reach another device: no remote copies, remote signals or barrier semaphores. Data moves between devices by JAX's collectives and lax.ppermute only.
A program may use at most 64 MiB of HBM per device.

v0:
```python
import jax
import jax.numpy as jnp
from jax import lax
from jax.sharding import PartitionSpec as P


def product(left, right):
    return jnp.einsum("woe,wev->wov", left, right, preferred_element_type=jnp.float32)


def gradient_terms(log_grad, kin_part, weights):
    kin_grad = -0.5 * kin_part
    weighted = jnp.sum(weights[:, None, None] * log_grad + kin_grad, axis=0)
    return (weighted, jnp.sum(log_grad, axis=0))


def body(inverse_rows, kinetic_rows, virt_values, virt_laplacians, local_energy):
    walk_count = lax.axis_size("walk")
    walker_count = walk_count * local_energy.shape[0]
    energy_sum = lax.psum(jnp.sum(local_energy), "walk")
    average = energy_sum / walker_count
    weights = 2.0 * (local_energy - average)
    inverse_all, kinetic_all = (
        lax.all_gather(inverse_rows, "virt", axis=2, tiled=True),
        lax.all_gather(kinetic_rows, "virt", axis=2, tiled=True),
    )
    log_grad = product(inverse_all, virt_values)
    kin_part = product(inverse_all, virt_laplacians) - product(kinetic_all, virt_values)
    weighted, log_sum = gradient_terms(log_grad, kin_part, weights)
    summed = (
        lax.psum_scatter(weighted, "walk", scatter_dimension=0, tiled=True),
        lax.psum_scatter(log_sum, "walk", scatter_dimension=0, tiled=True),
    )
    gradient_part, log_part = (summed[0], summed[1])
    return (gradient_part / walker_count, log_part / walker_count)


def solution(mesh):
    placed = (
        P("walk", None, "virt"),
        P("walk", None, "virt"),
        P("walk", None, "virt"),
        P("walk", None, "virt"),
        P("walk"),
    )
    return jax.shard_map(
        body,
        mesh=mesh,
        in_specs=placed,
        out_specs=(P("walk", "virt"), P("walk", "virt")),
        check_vma=False,
    )
```

profile of v0, /device:TPU:0, one launch (start us, length us, event | category | flops | bytes accessed | tf_op | source)
XLA Modules:
  0.0 249.7 jit_solution(12773574500278147120)
XLA Ops:
  7.2 0.0 all-gather.3.cloned.1.call-start
  7.2 0.7 all-gather.3.cloned.1.call-update
  7.9 0.0 all-gather.5.cloned.1.call-start
  7.9 0.7 all-gather.5.cloned.1.call-update
  8.6 0.0 reduce-scatter.3.cloned.1.call-start
  9.3 35.5 %psum.7 = f32[]{:T(128)} all-reduce(f32[]{:T(128)} %bitcast), channel_id=1, replica_groups=mesh['virt'=2,'walk'=16] {'walk'}, use_global_device_ids=true, to_apply=%region_0.0 | all-reduce | flops 1 | bytes 8 | tf_op jit(solution)/shard_map/psum | solution.py:20
  45.5 0.0 all-gather.3.cloned.1.call-done
  45.6 0.0 copy-start
  45.6 10.6 %fusion.4 = f32[512,2048]{1,0:T(8,128)} fusion(bf16[1,2048,2048]{2,1,0:T(8,128)(2,1)} %param.7, bf16[1,512,2048]{2,1,0:T(8,128)(2,1)} %all-gather.3.cloned.1.call-done), kind=kOutput, calls=%fused_computation.4 | convolution fusion | flops 4294967296 | bytes 14680064 | tf_op jit(solution)/shard_map/woe,wev->wov/dot_general | solution.py:8
  56.2 0.0 copy-done
  56.2 9.5 %fusion = f32[512,2048]{1,0:T(8,128)} fusion(bf16[1,2048,2048]{2,1,0:T(8,128)(2,1)} %param.8, bf16[1,512,2048]{2,1,0:T(8,128)(2,1)S(1)} %copy-done), kind=kOutput, calls=%fused_computation | convolution fusion | flops 4294967296 | bytes 14680064 | tf_op jit(solution)/shard_map/woe,wev->wov/dot_general | solution.py:8
  65.6 14.5 %all-gather.5.cloned.1.call-done = bf16[1,512,2048]{2,1,0:T(8,128)(2,1)} async-done(((bf16[1,512,1024]{2,1,0:T(8,128)(2,1)}), bf16[1,512,2048]{2,1,0:T(8,128)(2,1)}) %all-gather.5.cloned.1.call-update) | async-done | bytes 2097168 | tf_op jit(solution)/shard_map/all_gather | solution.py:25
  80.1 12.9 %multiply_add_fusion = f32[512,2048]{1,0:T(8,128)} fusion(f32[512,2048]{1,0:T(8,128)} %fusion, f32[512,2048]{1,0:T(8,128)} %fusion.4, bf16[1,2048,2048]{2,1,0:T(8,128)(2,1)} %param.7, bf16[1,512,2048]{2,1,0:T(8,128)(2,1)} %all-gather.5.cloned.1.call-done, f32[]{:T(128)} %bitcast.2), kind=kOutput, calls=%fused_computation.6 | convolution fusion | flops 4299161600 | bytes 23068676 | tf_op jit(solution)/shard_map/woe,wev->wov/dot_general | solution.py:8
  93.0 0.0 reduce-scatter.3.cloned.1.call-update
  93.0 0.0 reduce-scatter.5.cloned.1.call-start
  93.1 0.5 reduce-scatter.5.cloned.1.call-update
  93.6 72.1 %reduce-scatter.3.cloned.1.call-done = f32[32,2048]{1,0:T(8,128)} async-done(((f32[512,2048]{1,0:T(8,128)}), f32[32,2048]{1,0:T(8,128)}) %reduce-scatter.3.cloned.1.call-update) | async-done | bytes 262160 | tf_op jit(solution)/shard_map/reduce_scatter | solution.py:31
  165.6 1.7 broadcast_multiply_fusion.1
  167.3 74.2 %reduce-scatter.5.cloned.1.call-done = f32[32,2048]{1,0:T(8,128)} async-done(((f32[512,2048]{1,0:T(8,128)}), f32[32,2048]{1,0:T(8,128)}) %reduce-scatter.5.cloned.1.call-update) | async-done | bytes 262160 | tf_op jit(solution)/shard_map/reduce_scatter | solution.py:32
  241.5 1.7 broadcast_multiply_fusion
Async XLA Ops:
  7.2 38.4 %all-gather.3.cloned.1.call-start = ((), (), s32[]{:S(2)}) async-start(), calls=%async_computation.2 | async-start | bytes 3145728 | tf_op jit(solution)/shard_map/all_gather | solution.py:24
  7.9 72.2 %all-gather.5.cloned.1.call-start = ((), (), s32[]{:S(2)}) async-start(), calls=%async_computation.3 | async-start | bytes 3145728 | tf_op jit(solution)/shard_map/all_gather | solution.py:25
  8.6 157.0 %reduce-scatter.3.cloned.1.call-start = ((), (), s32[]{:S(2)}) async-start(), calls=%async_computation.4 | async-start | bytes 4456448 | tf_op jit(solution)/shard_map/reduce_scatter | solution.py:31
  45.6 10.6 %copy-start = (bf16[1,512,2048]{2,1,0:T(8,128)(2,1)S(1)}, bf16[1,512,2048]{2,1,0:T(8,128)(2,1)}, u32[]{:S(2)}) copy-start(bf16[1,512,2048]{2,1,0:T(8,128)(2,1)} %all-gather.3.cloned.1.call-done) | copy-start | bytes 6291460
  93.0 148.5 %reduce-scatter.5.cloned.1.call-start = ((), (), s32[]{:S(2)}) async-start(), calls=%async_computation.5 | async-start | bytes 4456448 | tf_op jit(solution)/shard_map/reduce_scatter | solution.py:32
Sparse Core Ops, SparseCore 0:
  9.5 35.8 all-gather.2
  46.9 33.1 all-gather.4
  93.1 72.4 reduce-scatter.2
  169.8 71.6 reduce-scatter.4
where the time goes:
time: 250 us
  waiting for transfers between devices  163 us (65%)
  blocking collectives  35.5 us (14%)
  matrix products  33 us (13%)
  between operations  15.1 us (6%)
  other arithmetic  3.34 us (1%)
    reduce_scatter x1, waiting for transfers between devices, body(): lax.psum_scatter(log_sum, 'walk', scatter_dimension=0, tiled=True)  74.2 us
    reduce_scatter x1, waiting for transfers between devices, body(): lax.psum_scatter(weighted, 'walk', scatter_dimension=0, tiled=True)  72.1 us
    psum x1, blocking collectives, body(): energy_sum = lax.psum(jnp.sum(local_energy), 'walk')  35.5 us
    dot_general x3, matrix products, product(): jnp.einsum('woe,wev->wov', left, right, preferred_element_type=jnp.float32)  33 us
    all_gather x1, waiting for transfers between devices, body(): lax.all_gather(kinetic_rows, 'virt', axis=2, tiled=True)  14.5 us
  transfers between devices with their start and end apart: 4, of which 3 were waited for; matrix products, arithmetic and copies ran while one was open for 9% of the time, Pallas kernels for 0%

commit v1 on v0

--- a/solution.py
+++ b/solution.py
@@ -1,7 +1,13 @@
+import functools
+
 import jax
 import jax.numpy as jnp
 from jax import lax
+from jax.experimental import pallas as pl
+from jax.experimental.pallas import tpu as pltpu
 from jax.sharding import PartitionSpec as P
+
+PIECES = 4
 
 
 def product(left, right):
@@ -14,7 +20,7 @@
     return (weighted, jnp.sum(log_grad, axis=0))
 
 
-def body(inverse_rows, kinetic_rows, virt_values, virt_laplacians, local_energy):
+def general_body(inverse_rows, kinetic_rows, virt_values, virt_laplacians, local_energy):
     walk_count = lax.axis_size("walk")
     walker_count = walk_count * local_energy.shape[0]
     energy_sum = lax.psum(jnp.sum(local_energy), "walk")
@@ -35,6 +41,137 @@
     return (gradient_part / walker_count, log_part / walker_count)
 
 
+def stage_masks(count):
+    bits = count.bit_length() - 1
+    masks = [1 << bit for bit in range(bits)]
+    if bits >= 2:
+        masks[-1] = 3 << (bits - 2)
+    return masks
+
+
+def swap(array, axis, mask):
+    pairs = [(source, source ^ mask) for source in range(lax.axis_size(axis))]
+    return lax.ppermute(array, axis, pairs)
+
+
+def order_kernel(offset, rows, count, masks, me_ref, inverse_ref, kinetic_ref, *rest):
+    out_ref = rest[-1]
+    height = out_ref.shape[1]
+    total = inverse_ref.shape[0]
+    per = total // count
+    place = lax.broadcasted_iota(jnp.int32, (height, 1), 0)
+    block = lax.div(place, rows)
+    dest = jnp.full_like(block, me_ref[0])
+    bits = len(masks)
+    for stage, mask in enumerate(masks):
+        bit = jnp.bitwise_and(lax.shift_right_logical(block, bits - 1 - stage), 1)
+        dest = jnp.bitwise_xor(dest, bit * mask)
+    source = dest * per + offset + (place - block * rows)
+    column = lax.broadcasted_iota(jnp.int32, (height, total), 1)
+    pick = jnp.where(column == source, 1.0, 0.0).astype(jnp.bfloat16)
+    for index, ref in enumerate((inverse_ref, kinetic_ref)):
+        picked = jnp.dot(pick, ref[...], preferred_element_type=jnp.float32)
+        out_ref[index] = picked.astype(jnp.bfloat16)
+
+
+def order_piece(me, inverse, kinetic, offset, rows, masks, count, after):
+    height = count * rows
+    depth = inverse.shape[1]
+    whole = pl.BlockSpec(memory_space=pltpu.VMEM)
+    return pl.pallas_call(
+        functools.partial(order_kernel, offset, rows, count, masks),
+        out_shape=jax.ShapeDtypeStruct((2, height, depth), jnp.bfloat16),
+        in_specs=[pl.BlockSpec(memory_space=pltpu.SMEM), whole, whole]
+        + [pl.BlockSpec(memory_space=pl.ANY)] * len(after),
+        out_specs=whole,
+        cost_estimate=pl.CostEstimate(
+            flops=4 * height * inverse.shape[0] * depth,
+            bytes_accessed=4 * inverse.size + 4 * height * depth,
+            transcendentals=0,
+        ),
+        name="order_piece",
+    )(me, inverse, kinetic, *after)
+
+
+def multiply_kernel(place_ref, scale_ref, near_ref, far_ref, v_near, v_far, l_near, l_far, send_ref, keep_ref):
+    height, depth = near_ref.shape[1], near_ref.shape[2]
+    half = height // 2
+    both = (2 * height, depth)
+    f32 = jnp.float32
+    values = jnp.dot(near_ref[...].reshape(both), v_near[...], preferred_element_type=f32)
+    values += jnp.dot(far_ref[...].reshape(both), v_far[...], preferred_element_type=f32)
+    laps = jnp.dot(near_ref[0], l_near[...], preferred_element_type=f32)
+    laps += jnp.dot(far_ref[0], l_far[...], preferred_element_type=f32)
+    log = values[:height]
+    weighted = scale_ref[0] * log + 0.5 * (values[height:] - laps)
+    keep_ref[0] = weighted[:half]
+    keep_ref[1] = log[:half]
+    send_ref[0] = weighted[half:]
+    send_ref[1] = log[half:]
+
+
+def multiply(place, scale, near, far, values, laplacians, tile):
+    height, depth = near.shape[1], near.shape[2]
+    width = values.shape[1]
+    half = height // 2
+    rows_spec = pl.BlockSpec((2, height, depth), lambda j, place: (0, 0, 0))
+    near_spec = pl.BlockSpec((depth, tile), lambda j, place: (place[0], j))
+    far_spec = pl.BlockSpec((depth, tile), lambda j, place: (1 - place[0], j))
+    out_spec = pl.BlockSpec((2, half, tile), lambda j, place: (0, 0, j))
+    out = jax.ShapeDtypeStruct((2, half, width), jnp.float32)
+    return pl.pallas_call(
+        multiply_kernel,
+        out_shape=(out, out),
+        grid_spec=pltpu.PrefetchScalarGridSpec(
+            num_scalar_prefetch=1,
+            grid=(width // tile,),
+            in_specs=[pl.BlockSpec(memory_space=pltpu.SMEM), rows_spec, rows_spec, near_spec, far_spec, near_spec, far_spec],
+            out_specs=(out_spec, out_spec),
+        ),
+        compiler_params=pltpu.CompilerParams(vmem_limit_bytes=32 * 1024 * 1024),
+        cost_estimate=pl.CostEstimate(
+            flops=2 * 3 * height * 2 * depth * width,
+            bytes_accessed=4 * values.size + 8 * height * depth + 8 * height * width,
+            transcendentals=0,
+        ),
+        name="multiply_piece",
+    )(place, scale, near, far, values, values, laplacians, laplacians)
+
+
+def pieced_body(pieces, tile, inverse_rows, kinetic_rows, virt_values, virt_laplacians, local_energy):
+    count = lax.axis_size("walk")
+    masks = stage_masks(count)
+    me = lax.axis_index("walk").astype(jnp.int32).reshape(1)
+    place = lax.axis_index("virt").astype(jnp.int32).reshape(1)
+    inverse, kinetic = inverse_rows[0], kinetic_rows[0]
+    values, laplacians = virt_values[0], virt_laplacians[0]
+    rows = inverse.shape[0] // (count * pieces)
+
+    energy_sum = jnp.broadcast_to(local_energy, (1, 128))
+    for mask in masks:
+        energy_sum = energy_sum + swap(energy_sum, "walk", mask)
+    average = energy_sum[0, 0] / count
+
+    near, far = [], []
+    for piece in range(pieces):
+        after = [far[piece - 2]] if piece >= 2 else []
+        near.append(order_piece(me, inverse, kinetic, piece * rows, rows, masks, count, after))
+        far.append(swap(near[piece], "virt", 1))
+
+    done = []
+    for piece in range(pieces):
+        send, keep = multiply(place, 2.0 * local_energy, near[piece], far[piece], values, laplacians, tile)
+        for stage, mask in enumerate(masks):
+            total = keep + swap(send, "walk", mask)
+            if stage + 1 < len(masks):
+                half = total.shape[1] // 2
+                keep, send = total[:, :half], total[:, half:]
+        done.append(total)
+    log_part = jnp.concatenate([total[1] for total in done], axis=0) / count
+    gradient_part = jnp.concatenate([total[0] for total in done], axis=0) / count
+    return (gradient_part - (2.0 * average) * log_part, log_part)
+
+
 def solution(mesh):
     placed = (
         P("walk", None, "virt"),
@@ -43,6 +180,24 @@
         P("walk", None, "virt"),
         P("walk"),
     )
+
+    def body(inverse_rows, kinetic_rows, virt_values, virt_laplacians, local_energy):
+        count = mesh.shape["walk"]
+        walkers, occupied, depth = inverse_rows.shape
+        width = virt_values.shape[2]
+        tile = 512
+        fits = (
+            walkers == 1
+            and mesh.shape["virt"] == 2
+            and count >= 4
+            and count & (count - 1) == 0
+            and occupied % (count * PIECES * 8) == 0
+            and depth % 256 == 0
+            and width % tile == 0
+        )
+        form = functools.partial(pieced_body, PIECES, tile) if fits else general_body
+        return form(inverse_rows, kinetic_rows, virt_values, virt_laplacians, local_energy)
+
     return jax.shard_map(
         body,
         mesh=mesh,

time: 250 us -> 142 us (0.57)
  waiting for transfers between devices: 163 us -> 38.2 us
  starting transfers between devices: 0.16 us -> 39.5 us
  blocking collectives: 35.5 us -> 0 us
  Pallas kernels: 0 us -> 34.7 us
  matrix products: 33 us -> 0 us
  local copies, waits for them, and re-layouts: 0.01 us -> 22.8 us
  between operations: 15.1 us -> 1.65 us
    reduce_scatter x2 -> x0, waiting for transfers between devices: 146 us -> none  [the longest x1 74.2 us: body(): lax.psum_scatter(log_sum, 'walk', scatter_dimension=0, tiled=True)]
    ppermute x0 -> x24, starting transfers between devices: none -> 39.5 us  [swap(): return lax.ppermute(array, axis, pairs)]
    ppermute x0 -> x24, waiting for transfers between devices: none -> 38.2 us  [swap(): return lax.ppermute(array, axis, pairs)]
    psum x1 -> x0, blocking collectives: 35.5 us -> none  [body(): energy_sum = lax.psum(jnp.sum(local_energy), 'walk')]
    pallas_call x0 -> x8, Pallas kernels: none -> 34.7 us  [the longest x4 23.5 us: multiply(): pl.pallas_call(multiply_kernel, out_shape=(out, out), grid_spec=pltpu.Pre...]
    dot_general x3 -> x0, matrix products: 33 us -> none  [product(): jnp.einsum('woe,wev->wov', left, right, preferred_element_type=jnp.float32)]
    unnamed x2 -> x30, local copies, waits for them, and re-layouts: 0.01 us -> 22.5 us
    all_gather x2 -> x0, waiting for transfers between devices: 14.5 us -> none  [the longest x1 14.5 us: body(): lax.all_gather(kinetic_rows, 'virt', axis=2, tiled=True)]
  transfers between devices with their start and end apart: 4 -> 24, of which waited for: 3 -> 9; matrix products, arithmetic and copies ran while one was open for 9% -> 3% of each run, Pallas kernels for 0% -> 23%
where the time goes in v1:
time: 142 us; the launch traced here: 141 us
  starting transfers between devices  39.5 us (28%)
  waiting for transfers between devices  38.2 us (27%)
  Pallas kernels  34.7 us (24%)
  local copies, waits for them, and re-layouts  22.8 us (16%)
  other arithmetic  4.25 us (3%)
  between operations  1.65 us (1%)
    ppermute x24, starting transfers between devices, swap(): return lax.ppermute(array, axis, pairs)  39.5 us
    ppermute x24, waiting for transfers between devices, swap(): return lax.ppermute(array, axis, pairs)  38.2 us
    pallas_call x4, Pallas kernels, multiply(): pl.pallas_call(multiply_kernel, out_shape=(out, out), grid_spec=pltpu.Pre...  23.5 us
    unnamed x30, local copies, waits for them, and re-layouts  22.5 us
    pallas_call x4, Pallas kernels, order_piece(): pl.pallas_call(functools.partial(order_kernel, offset, rows, count, masks...  11.2 us
    add x16, other arithmetic, pieced_body(): total = keep + swap(send, 'walk', mask)  3.4 us
  transfers between devices with their start and end apart: 24, of which 9 were waited for; matrix products, arithmetic and copies ran while one was open for 3% of the time, Pallas kernels for 23%

profile of v1, /device:TPU:0, one launch (start us, length us, event | category | flops | bytes accessed | tf_op | source)
XLA Modules:
  0.0 141.1 jit_solution(3517064058137787368)
XLA Ops:
  0.6 2.8 %order_piece.4.near_ref = bf16[2,128,1024]{2,1,0:T(8,128)(2,1)} custom-call(s32[1]{0:T(128)} %bitcast.1.me_ref, bf16[512,1024]{1,0:T(8,128)(2,1)} %bitcast.44, bf16[512,1024]{1,0:T(8,128)(2,1)} %bitcast.48), custom_call_target="tpu_custom_call" | custom-call | flops 268435456 | bytes 2621440 | tf_op jit(solution)/shard_map/order_piece/pallas_call | solution.py:81
  3.4 3.0 %collective-permute-start = (bf16[2,128,1024]{2,1,0:T(8,128)(2,1)}, bf16[2,128,1024]{2,1,0:T(8,128)(2,1)S(1)}, u32[]{:S(2)}, u32[]{:S(2)}) collective-permute-start(bf16[2,128,1024]{2,1,0:T(8,128)(2,1)} %order_piece.4.near_ref), channel_id=1, source_target_pairs={{0,16},{16,0},{1,17},{17,1},{2,18},{18,2},{3,19},{19,3},{4,20},{20... | collective-permute-start | bytes 1572872 | tf_op jit(solution)/shard_map/ppermute | solution.py:54
  6.4 2.8 %order_piece.5.near_ref = bf16[2,128,1024]{2,1,0:T(8,128)(2,1)} custom-call(s32[1]{0:T(128)} %bitcast.1.me_ref, bf16[512,1024]{1,0:T(8,128)(2,1)} %bitcast.45, bf16[512,1024]{1,0:T(8,128)(2,1)} %bitcast.49), custom_call_target="tpu_custom_call" | custom-call | flops 268435456 | bytes 2621440 | tf_op jit(solution)/shard_map/order_piece/pallas_call | solution.py:81
  9.9 9.5 %collective-permute-done.far_ref.rest_0_ = bf16[2,128,1024]{2,1,0:T(8,128)(2,1)S(1)} collective-permute-done((bf16[2,128,1024]{2,1,0:T(8,128)(2,1)}, bf16[2,128,1024]{2,1,0:T(8,128)(2,1)S(1)}, u32[]{:S(2)}, u32[]{:S(2)}) %collective-permute-start) | collective-permute-done | bytes 524320 | tf_op jit(solution)/shard_map/ppermute | solution.py:54
  19.4 3.6 %copy-done = bf16[1,2048,2048]{2,1,0:T(8,128)(2,1)S(1)} copy-done((bf16[1,2048,2048]{2,1,0:T(8,128)(2,1)S(1)}, bf16[1,2048,2048]{2,1,0:T(8,128)(2,1)}, u32[]{:S(2)}) %copy-start) | copy-done | bytes 8388632
  22.9 3.4 %copy-done.4 = bf16[1,2048,2048]{2,1,0:T(8,128)(2,1)S(1)} copy-done((bf16[1,2048,2048]{2,1,0:T(8,128)(2,1)S(1)}, bf16[1,2048,2048]{2,1,0:T(8,128)(2,1)}, u32[]{:S(2)}) %copy-start.4) | copy-done | bytes 8388632
  27.4 6.2 %multiply_piece.4 = (f32[2,64,2048]{2,1,0:T(8,128)}, f32[2,64,2048]{2,1,0:T(8,128)S(1)}) custom-call(s32[1]{0:T(128)} %bitcast.place_ref, f32[1]{0:T(128)S(6)} %mul.17.scale_ref, bf16[2,128,1024]{2,1,0:T(8,128)(2,1)S(1)} %copy-done.12, bf16[2,128,1024]{2,1,0:T(8,128)(2,1)S(1)} %collective-permute-done.far_ref.rest_0_, bf16[2048,2048]{1,0:T(8,128)(2,1)S(1)} %bitcast.28, ...), custom_call_target="tpu_custom_call" | custom-call | flops 3221225472 | bytes 19922944 | tf_op jit(solution)/shard_map/multiply_piece/pallas_call | solution.py:122
  34.5 2.8 %order_piece.6.near_ref = bf16[2,128,1024]{2,1,0:T(8,128)(2,1)} custom-call(s32[1]{0:T(128)} %bitcast.1.me_ref, bf16[512,1024]{1,0:T(8,128)(2,1)} %bitcast.46, bf16[512,1024]{1,0:T(8,128)(2,1)} %bitcast.50, bf16[2,128,1024]{2,1,0:T(8,128)(2,1)} %copy-done.11), custom_call_target="tpu_custom_call" | custom-call | flops 268435456 | bytes 2621440 | tf_op jit(solution)/shard_map/order_piece/pallas_call | solution.py:81
  37.4 2.1 %collective-permute-start.10 = (bf16[2,128,1024]{2,1,0:T(8,128)(2,1)}, bf16[2,128,1024]{2,1,0:T(8,128)(2,1)S(1)}, u32[]{:S(2)}, u32[]{:S(2)}) collective-permute-start(bf16[2,128,1024]{2,1,0:T(8,128)(2,1)} %order_piece.6.near_ref), channel_id=1, source_target_pairs={{0,16},{16,0},{1,17},{17,1},{2,18},{18,2},{3,19},{19,3},{4,20},{20... | collective-permute-start | bytes 1572872 | tf_op jit(solution)/shard_map/ppermute | solution.py:54
  39.4 3.4 %copy-done.1 = bf16[1,2048,2048]{2,1,0:T(8,128)(2,1)S(1)} copy-done((bf16[1,2048,2048]{2,1,0:T(8,128)(2,1)S(1)}, bf16[1,2048,2048]{2,1,0:T(8,128)(2,1)}, u32[]{:S(2)}) %copy-start.1) | copy-done | bytes 8388632
  42.8 3.4 %copy-done.5 = bf16[1,2048,2048]{2,1,0:T(8,128)(2,1)S(1)} copy-done((bf16[1,2048,2048]{2,1,0:T(8,128)(2,1)S(1)}, bf16[1,2048,2048]{2,1,0:T(8,128)(2,1)}, u32[]{:S(2)}) %copy-start.5) | copy-done | bytes 8388632
  46.2 6.2 %multiply_piece.5 = (f32[2,64,2048]{2,1,0:T(8,128)}, f32[2,64,2048]{2,1,0:T(8,128)S(1)}) custom-call(s32[1]{0:T(128)} %bitcast.place_ref, f32[1]{0:T(128)S(6)} %mul.17.scale_ref, bf16[2,128,1024]{2,1,0:T(8,128)(2,1)S(1)} %copy-done.10, bf16[2,128,1024]{2,1,0:T(8,128)(2,1)S(1)} %collective-permute-done.5.far_ref.rest_0_, bf16[2048,2048]{1,0:T(8,128)(2,1)S(1)} %bitcast.30, ...), custom_call_target="tpu_custom_call" | custom-call | flops 3221225472 | bytes 19922944 | tf_op jit(solution)/shard_map/multiply_piece/pallas_call | solution.py:122
  52.9 2.8 %order_piece.7.near_ref = bf16[2,128,1024]{2,1,0:T(8,128)(2,1)} custom-call(s32[1]{0:T(128)} %bitcast.1.me_ref, bf16[512,1024]{1,0:T(8,128)(2,1)} %bitcast.47, bf16[512,1024]{1,0:T(8,128)(2,1)} %bitcast.51, bf16[2,128,1024]{2,1,0:T(8,128)(2,1)} %copy-done.8), custom_call_target="tpu_custom_call" | custom-call | flops 268435456 | bytes 2621440 | tf_op jit(solution)/shard_map/order_piece/pallas_call | solution.py:81
  55.8 1.9 %collective-permute-start.21 = (f32[1,128]{1,0:T(1,128)S(1)}, f32[1,128]{1,0:T(1,128)S(1)}, u32[]{:S(2)}, u32[]{:S(2)}) collective-permute-start(f32[1,128]{1,0:T(1,128)S(1)} %broadcast_add_fusion), channel_id=1, source_target_pairs={{0,2},{1,3},{2,0},{3,1},{4,6},{5,7},{6,4},{7,5},{8,10},{9,11},{10,... | collective-permute-start | bytes 1544 | tf_op jit(solution)/shard_map/ppermute | solution.py:54
  57.7 3.4 %copy-done.2 = bf16[1,2048,2048]{2,1,0:T(8,128)(2,1)S(1)} copy-done((bf16[1,2048,2048]{2,1,0:T(8,128)(2,1)S(1)}, bf16[1,2048,2048]{2,1,0:T(8,128)(2,1)}, u32[]{:S(2)}) %copy-start.2) | copy-done | bytes 8388632
  61.1 3.4 %copy-done.6 = bf16[1,2048,2048]{2,1,0:T(8,128)(2,1)S(1)} copy-done((bf16[1,2048,2048]{2,1,0:T(8,128)(2,1)S(1)}, bf16[1,2048,2048]{2,1,0:T(8,128)(2,1)}, u32[]{:S(2)}) %copy-start.6) | copy-done | bytes 8388632
  64.5 5.6 %multiply_piece.6 = (f32[2,64,2048]{2,1,0:T(8,128)S(1)}, f32[2,64,2048]{2,1,0:T(8,128)S(1)}) custom-call(s32[1]{0:T(128)} %bitcast.place_ref, f32[1]{0:T(128)S(6)} %mul.17.scale_ref, bf16[2,128,1024]{2,1,0:T(8,128)(2,1)S(1)} %copy-done.9, bf16[2,128,1024]{2,1,0:T(8,128)(2,1)S(1)} %collective-permute-done.10.far_ref, bf16[2048,2048]{1,0:T(8,128)(2,1)S(1)} %bitcast.32, ...), custom_call_target="tpu_custom_call" | custom-call | flops 3221225472 | bytes 19922944 | tf_op jit(solution)/shard_map/multiply_piece/pallas_call | solution.py:122
  71.7 5.6 %multiply_piece.7 = (f32[2,64,2048]{2,1,0:T(8,128)S(1)}, f32[2,64,2048]{2,1,0:T(8,128)S(1)}) custom-call(s32[1]{0:T(128)} %bitcast.place_ref, f32[1]{0:T(128)S(6)} %mul.17.scale_ref, bf16[2,128,1024]{2,1,0:T(8,128)(2,1)S(1)} %copy-done.7, bf16[2,128,1024]{2,1,0:T(8,128)(2,1)S(1)} %collective-permute-done.15.far_ref, bf16[2048,2048]{1,0:T(8,128)(2,1)S(1)} %bitcast.34, ...), custom_call_target="tpu_custom_call" | custom-call | flops 3221225472 | bytes 19922944 | tf_op jit(solution)/shard_map/multiply_piece/pallas_call | solution.py:122
  79.2 1.8 %collective-permute-start.7 = (f32[2,32,2048]{2,1,0:T(8,128)S(1)}, f32[2,32,2048]{2,1,0:T(8,128)S(1)}, u32[]{:S(2)}, u32[]{:S(2)}) collective-permute-start(f32[2,32,2048]{2,1,0:T(8,128)S(1)} %slice.140), channel_id=1, source_target_pairs={{0,2},{1,3},{2,0},{3,1},{4,6},{5,7},{6,4},{7,5},{8,10},{9,11},{10,... | collective-permute-start | bytes 1572872 | tf_op jit(solution)/shard_map/ppermute | solution.py:54
  82.6 2.0 %collective-permute-done.22 = f32[1,128]{1,0:T(1,128)S(1)} collective-permute-done((f32[1,128]{1,0:T(1,128)S(1)}, f32[1,128]{1,0:T(1,128)S(1)}, u32[]{:S(2)}, u32[]{:S(2)}) %collective-permute-start.22) | collective-permute-done | bytes 544 | tf_op jit(solution)/shard_map/ppermute | solution.py:54
  84.5 3.6 %collective-permute-start.23 = (f32[1,128]{1,0:T(1,128)S(1)}, f32[1,128]{1,0:T(1,128)S(1)}, u32[]{:S(2)}, u32[]{:S(2)}) collective-permute-start(f32[1,128]{1,0:T(1,128)S(1)} %add.78), channel_id=1, source_target_pairs={{0,12},{1,13},{2,14},{3,15},{4,8},{5,9},{6,10},{7,11},{8,4},{9,5},... | collective-permute-start | bytes 1544 | tf_op jit(solution)/shard_map/ppermute | solution.py:54
  88.1 1.7 %collective-permute-done.23 = f32[1,128]{1,0:T(1,128)S(1)} collective-permute-done((f32[1,128]{1,0:T(1,128)S(1)}, f32[1,128]{1,0:T(1,128)S(1)}, u32[]{:S(2)}, u32[]{:S(2)}) %collective-permute-start.23) | collective-permute-done | bytes 544 | tf_op jit(solution)/shard_map/ppermute | solution.py:54
  90.1 7.1 %collective-permute-done.7 = f32[2,32,2048]{2,1,0:T(8,128)S(1)} collective-permute-done((f32[2,32,2048]{2,1,0:T(8,128)S(1)}, f32[2,32,2048]{2,1,0:T(8,128)S(1)}, u32[]{:S(2)}, u32[]{:S(2)}) %collective-permute-start.7) | collective-permute-done | bytes 524320 | tf_op jit(solution)/shard_map/ppermute | solution.py:54
  97.3 1.6 %collective-permute-start.8 = (f32[2,16,2048]{2,1,0:T(8,128)S(1)}, f32[2,16,2048]{2,1,0:T(8,128)S(1)}, u32[]{:S(2)}, u32[]{:S(2)}) collective-permute-start(f32[2,16,2048]{2,1,0:T(8,128)S(1)} %slice.142), channel_id=1, source_target_pairs={{0,4},{1,5},{2,6},{3,7},{4,0},{5,1},{6,2},{7,3},{8,12},{9,13},{10,... | collective-permute-start | bytes 786440 | tf_op jit(solution)/shard_map/ppermute | solution.py:54
  101.5 2.5 %collective-permute-start.4 = (f32[2,8,2048]{2,1,0:T(8,128)S(1)}, f32[2,8,2048]{2,1,0:T(8,128)S(1)}, u32[]{:S(2)}, u32[]{:S(2)}) collective-permute-start(f32[2,8,2048]{2,1,0:T(8,128)S(1)} %slice.137), channel_id=1, source_target_pairs={{0,12},{1,13},{2,14},{3,15},{4,8},{5,9},{6,10},{7,11},{8,4},{9,5},... | collective-permute-start | bytes 393224 | tf_op jit(solution)/shard_map/ppermute | solution.py:54
  105.7 6.1 %collective-permute-start.9 = (f32[2,8,2048]{2,1,0:T(8,128)S(1)}, f32[2,8,2048]{2,1,0:T(8,128)S(1)}, u32[]{:S(2)}, u32[]{:S(2)}) collective-permute-start(f32[2,8,2048]{2,1,0:T(8,128)S(1)} %slice.144), channel_id=1, source_target_pairs={{0,12},{1,13},{2,14},{3,15},{4,8},{5,9},{6,10},{7,11},{8,4},{9,5},... | collective-permute-start | bytes 393224 | tf_op jit(solution)/shard_map/ppermute | solution.py:54
  111.8 3.0 %collective-permute-done.9 = f32[2,8,2048]{2,1,0:T(8,128)S(1)} collective-permute-done((f32[2,8,2048]{2,1,0:T(8,128)S(1)}, f32[2,8,2048]{2,1,0:T(8,128)S(1)}, u32[]{:S(2)}, u32[]{:S(2)}) %collective-permute-start.9) | collective-permute-done | bytes 131104 | tf_op jit(solution)/shard_map/ppermute | solution.py:54
  116.3 7.3 %collective-permute-done.17 = f32[2,32,2048]{2,1,0:T(8,128)S(1)} collective-permute-done((f32[2,32,2048]{2,1,0:T(8,128)S(1)}, f32[2,32,2048]{2,1,0:T(8,128)S(1)}, u32[]{:S(2)}, u32[]{:S(2)}) %collective-permute-start.17) | collective-permute-done | bytes 524320 | tf_op jit(solution)/shard_map/ppermute | solution.py:54
  124.3 3.7 %collective-permute-start.14 = (f32[2,8,2048]{2,1,0:T(8,128)S(1)}, f32[2,8,2048]{2,1,0:T(8,128)S(1)}, u32[]{:S(2)}, u32[]{:S(2)}) collective-permute-start(f32[2,8,2048]{2,1,0:T(8,128)S(1)} %slice.151), channel_id=1, source_target_pairs={{0,12},{1,13},{2,14},{3,15},{4,8},{5,9},{6,10},{7,11},{8,4},{9,5},... | collective-permute-start | bytes 393224 | tf_op jit(solution)/shard_map/ppermute | solution.py:54
  128.0 3.0 %collective-permute-done.18 = f32[2,16,2048]{2,1,0:T(8,128)S(1)} collective-permute-done((f32[2,16,2048]{2,1,0:T(8,128)S(1)}, f32[2,16,2048]{2,1,0:T(8,128)S(1)}, u32[]{:S(2)}, u32[]{:S(2)}) %collective-permute-start.18) | collective-permute-done | bytes 262176 | tf_op jit(solution)/shard_map/ppermute | solution.py:54
  131.1 6.3 %collective-permute-start.19 = (f32[2,8,2048]{2,1,0:T(8,128)S(1)}, f32[2,8,2048]{2,1,0:T(8,128)S(1)}, u32[]{:S(2)}, u32[]{:S(2)}) collective-permute-start(f32[2,8,2048]{2,1,0:T(8,128)S(1)} %slice.158), channel_id=1, source_target_pairs={{0,12},{1,13},{2,14},{3,15},{4,8},{5,9},{6,10},{7,11},{8,4},{9,5},... | collective-permute-start | bytes 393224 | tf_op jit(solution)/shard_map/ppermute | solution.py:54
  137.4 2.9 %collective-permute-done.19 = f32[2,8,2048]{2,1,0:T(8,128)S(1)} collective-permute-done((f32[2,8,2048]{2,1,0:T(8,128)S(1)}, f32[2,8,2048]{2,1,0:T(8,128)S(1)}, u32[]{:S(2)}, u32[]{:S(2)}) %collective-permute-start.19) | collective-permute-done | bytes 131104 | tf_op jit(solution)/shard_map/ppermute | solution.py:54
  (92 shorter events, 15.2 us)
Async XLA Ops:
  3.4 15.9 %collective-permute-start = (bf16[2,128,1024]{2,1,0:T(8,128)(2,1)}, bf16[2,128,1024]{2,1,0:T(8,128)(2,1)S(1)}, u32[]{:S(2)}, u32[]{:S(2)}) collective-permute-start(bf16[2,128,1024]{2,1,0:T(8,128)(2,1)} %order_piece.4.near_ref), channel_id=1, source_target_pairs={{0,16},{16,0},{1,17},{17,1},{2,18},{18,2},{3,19},{19,3},{4,20},{20... | collective-permute-start | bytes 1572872 | tf_op jit(solution)/shard_map/ppermute | solution.py:54
  9.2 30.2 %collective-permute-start.5 = (bf16[2,128,1024]{2,1,0:T(8,128)(2,1)}, bf16[2,128,1024]{2,1,0:T(8,128)(2,1)S(1)}, u32[]{:S(2)}, u32[]{:S(2)}) collective-permute-start(bf16[2,128,1024]{2,1,0:T(8,128)(2,1)} %order_piece.5.near_ref), channel_id=1, source_target_pairs={{0,16},{16,0},{1,17},{17,1},{2,18},{18,2},{3,19},{19,3},{4,20},{20... | collective-permute-start | bytes 1572872 | tf_op jit(solution)/shard_map/ppermute | solution.py:54
  19.4 14.2 %copy-start.11 = (bf16[2,128,1024]{2,1,0:T(8,128)(2,1)}, bf16[2,128,1024]{2,1,0:T(8,128)(2,1)S(1)}, u32[]{:S(2)}) copy-start(bf16[2,128,1024]{2,1,0:T(8,128)(2,1)S(1)} %collective-permute-done.far_ref.rest_0_) | copy-start | bytes 1572868
  19.4 3.6 %copy-start = (bf16[1,2048,2048]{2,1,0:T(8,128)(2,1)S(1)}, bf16[1,2048,2048]{2,1,0:T(8,128)(2,1)}, u32[]{:S(2)}) copy-start(bf16[1,2048,2048]{2,1,0:T(8,128)(2,1)} %param.7) | copy-start | bytes 25165828
  27.4 12.1 %copy-start.10 = (bf16[2,128,1024]{2,1,0:T(8,128)(2,1)S(1)}, bf16[2,128,1024]{2,1,0:T(8,128)(2,1)}, u32[]{:S(2)}) copy-start(bf16[2,128,1024]{2,1,0:T(8,128)(2,1)} %order_piece.5.near_ref) | copy-start | bytes 1572868
  34.5 35.6 %collective-permute-start.1 = (f32[2,64,2048]{2,1,0:T(8,128)}, f32[2,64,2048]{2,1,0:T(8,128)}, u32[]{:S(2)}, u32[]{:S(2)}) collective-permute-start(f32[2,64,2048]{2,1,0:T(8,128)} %get-tuple-element.11), channel_id=1, source_target_pairs={{0,1},{1,0},{2,3},{3,2},{4,5},{5,4},{6,7},{7,6},{8,9},{9,8},{10,11... | collective-permute-start | bytes 3145736 | tf_op jit(solution)/shard_map/ppermute | solution.py:54
  37.4 20.3 %collective-permute-start.10 = (bf16[2,128,1024]{2,1,0:T(8,128)(2,1)}, bf16[2,128,1024]{2,1,0:T(8,128)(2,1)S(1)}, u32[]{:S(2)}, u32[]{:S(2)}) collective-permute-start(bf16[2,128,1024]{2,1,0:T(8,128)(2,1)} %order_piece.6.near_ref), channel_id=1, source_target_pairs={{0,16},{16,0},{1,17},{17,1},{2,18},{18,2},{3,19},{19,3},{4,20},{20... | collective-permute-start | bytes 1572872 | tf_op jit(solution)/shard_map/ppermute | solution.py:54
  46.2 6.2 %copy-start.8 = (bf16[2,128,1024]{2,1,0:T(8,128)(2,1)}, bf16[2,128,1024]{2,1,0:T(8,128)(2,1)S(1)}, u32[]{:S(2)}) copy-start(bf16[2,128,1024]{2,1,0:T(8,128)(2,1)S(1)} %collective-permute-done.5.far_ref.rest_0_) | copy-start | bytes 1572868
  46.2 11.5 %copy-start.9 = (bf16[2,128,1024]{2,1,0:T(8,128)(2,1)S(1)}, bf16[2,128,1024]{2,1,0:T(8,128)(2,1)}, u32[]{:S(2)}) copy-start(bf16[2,128,1024]{2,1,0:T(8,128)(2,1)} %order_piece.6.near_ref) | copy-start | bytes 1572868
  52.4 25.4 %collective-permute-start.6 = (f32[2,64,2048]{2,1,0:T(8,128)}, f32[2,64,2048]{2,1,0:T(8,128)}, u32[]{:S(2)}, u32[]{:S(2)}) collective-permute-start(f32[2,64,2048]{2,1,0:T(8,128)} %get-tuple-element.13), channel_id=1, source_target_pairs={{0,1},{1,0},{2,3},{3,2},{4,5},{5,4},{6,7},{7,6},{8,9},{9,8},{10,11... | collective-permute-start | bytes 3145736 | tf_op jit(solution)/shard_map/ppermute | solution.py:54
  52.6 3.2 %collective-permute-start.20 = (f32[1,128]{1,0:T(1,128)S(1)}, f32[1,128]{1,0:T(1,128)S(1)}, u32[]{:S(2)}, u32[]{:S(2)}) collective-permute-start(f32[1,128]{1,0:T(1,128)S(1)} %broadcast_in_dim.2), channel_id=1, source_target_pairs={{0,1},{1,0},{2,3},{3,2},{4,5},{5,4},{6,7},{7,6},{8,9},{9,8},{10,11... | collective-permute-start | bytes 1544 | tf_op jit(solution)/shard_map/ppermute | solution.py:54
  55.7 16.0 %collective-permute-start.15 = (bf16[2,128,1024]{2,1,0:T(8,128)(2,1)}, bf16[2,128,1024]{2,1,0:T(8,128)(2,1)S(1)}, u32[]{:S(2)}, u32[]{:S(2)}) collective-permute-start(bf16[2,128,1024]{2,1,0:T(8,128)(2,1)} %order_piece.7.near_ref), channel_id=1, source_target_pairs={{0,16},{16,0},{1,17},{17,1},{2,18},{18,2},{3,19},{19,3},{4,20},{20... | collective-permute-start | bytes 1572872 | tf_op jit(solution)/shard_map/ppermute | solution.py:54
  55.8 25.2 %collective-permute-start.21 = (f32[1,128]{1,0:T(1,128)S(1)}, f32[1,128]{1,0:T(1,128)S(1)}, u32[]{:S(2)}, u32[]{:S(2)}) collective-permute-start(f32[1,128]{1,0:T(1,128)S(1)} %broadcast_add_fusion), channel_id=1, source_target_pairs={{0,2},{1,3},{2,0},{3,1},{4,6},{5,7},{6,4},{7,5},{8,10},{9,11},{10,... | collective-permute-start | bytes 1544 | tf_op jit(solution)/shard_map/ppermute | solution.py:54
  64.5 5.7 %copy-start.14 = (f32[2,64,2048]{2,1,0:T(8,128)S(1)}, f32[2,64,2048]{2,1,0:T(8,128)}, u32[]{:S(2)}) copy-start(f32[2,64,2048]{2,1,0:T(8,128)} %copy-done.13) | copy-start | bytes 3145732
  64.5 7.3 %copy-start.3 = (bf16[1,2048,2048]{2,1,0:T(8,128)(2,1)S(1)}, bf16[1,2048,2048]{2,1,0:T(8,128)(2,1)}, u32[]{:S(2)}) copy-start(bf16[1,2048,2048]{2,1,0:T(8,128)(2,1)} %param.7) | copy-start | bytes 25165828
  64.5 7.3 %copy-start.7 = (bf16[2,128,1024]{2,1,0:T(8,128)(2,1)S(1)}, bf16[2,128,1024]{2,1,0:T(8,128)(2,1)}, u32[]{:S(2)}) copy-start(bf16[2,128,1024]{2,1,0:T(8,128)(2,1)} %order_piece.7.near_ref) | copy-start | bytes 1572868
  70.0 28.9 %collective-permute-start.11 = (f32[2,64,2048]{2,1,0:T(8,128)S(1)}, f32[2,64,2048]{2,1,0:T(8,128)S(1)}, u32[]{:S(2)}, u32[]{:S(2)}) collective-permute-start(f32[2,64,2048]{2,1,0:T(8,128)S(1)} %get-tuple-element.15), channel_id=1, source_target_pairs={{0,1},{1,0},{2,3},{3,2},{4,5},{5,4},{6,7},{7,6},{8,9},{9,8},{10,11... | collective-permute-start | bytes 3145736 | tf_op jit(solution)/shard_map/ppermute | solution.py:54
  71.5 18.4 %collective-permute-start.2 = (f32[2,32,2048]{2,1,0:T(8,128)S(1)}, f32[2,32,2048]{2,1,0:T(8,128)S(1)}, u32[]{:S(2)}, u32[]{:S(2)}) collective-permute-start(f32[2,32,2048]{2,1,0:T(8,128)S(1)} %slice.133), channel_id=1, source_target_pairs={{0,2},{1,3},{2,0},{3,1},{4,6},{5,7},{6,4},{7,5},{8,10},{9,11},{10,... | collective-permute-start | bytes 1572872 | tf_op jit(solution)/shard_map/ppermute | solution.py:54
  77.3 22.4 %collective-permute-start.16 = (f32[2,64,2048]{2,1,0:T(8,128)S(1)}, f32[2,64,2048]{2,1,0:T(8,128)S(1)}, u32[]{:S(2)}, u32[]{:S(2)}) collective-permute-start(f32[2,64,2048]{2,1,0:T(8,128)S(1)} %get-tuple-element.17), channel_id=1, source_target_pairs={{0,1},{1,0},{2,3},{3,2},{4,5},{5,4},{6,7},{7,6},{8,9},{9,8},{10,11... | collective-permute-start | bytes 3145736 | tf_op jit(solution)/shard_map/ppermute | solution.py:54
  79.2 18.0 %collective-permute-start.7 = (f32[2,32,2048]{2,1,0:T(8,128)S(1)}, f32[2,32,2048]{2,1,0:T(8,128)S(1)}, u32[]{:S(2)}, u32[]{:S(2)}) collective-permute-start(f32[2,32,2048]{2,1,0:T(8,128)S(1)} %slice.140), channel_id=1, source_target_pairs={{0,2},{1,3},{2,0},{3,1},{4,6},{5,7},{6,4},{7,5},{8,10},{9,11},{10,... | collective-permute-start | bytes 1572872 | tf_op jit(solution)/shard_map/ppermute | solution.py:54
  81.0 3.5 %collective-permute-start.22 = (f32[1,128]{1,0:T(1,128)S(1)}, f32[1,128]{1,0:T(1,128)S(1)}, u32[]{:S(2)}, u32[]{:S(2)}) collective-permute-start(f32[1,128]{1,0:T(1,128)S(1)} %fusion.2), channel_id=1, source_target_pairs={{0,4},{1,5},{2,6},{3,7},{4,0},{5,1},{6,2},{7,3},{8,12},{9,13},{10,... | collective-permute-start | bytes 1544 | tf_op jit(solution)/shard_map/ppermute | solution.py:54
  84.5 5.3 %collective-permute-start.23 = (f32[1,128]{1,0:T(1,128)S(1)}, f32[1,128]{1,0:T(1,128)S(1)}, u32[]{:S(2)}, u32[]{:S(2)}) collective-permute-start(f32[1,128]{1,0:T(1,128)S(1)} %add.78), channel_id=1, source_target_pairs={{0,12},{1,13},{2,14},{3,15},{4,8},{5,9},{6,10},{7,11},{8,4},{9,5},... | collective-permute-start | bytes 1544 | tf_op jit(solution)/shard_map/ppermute | solution.py:54
  90.0 11.4 %collective-permute-start.3 = (f32[2,16,2048]{2,1,0:T(8,128)S(1)}, f32[2,16,2048]{2,1,0:T(8,128)S(1)}, u32[]{:S(2)}, u32[]{:S(2)}) collective-permute-start(f32[2,16,2048]{2,1,0:T(8,128)S(1)} %slice.135), channel_id=1, source_target_pairs={{0,4},{1,5},{2,6},{3,7},{4,0},{5,1},{6,2},{7,3},{8,12},{9,13},{10,... | collective-permute-start | bytes 786440 | tf_op jit(solution)/shard_map/ppermute | solution.py:54
  97.3 8.4 %collective-permute-start.8 = (f32[2,16,2048]{2,1,0:T(8,128)S(1)}, f32[2,16,2048]{2,1,0:T(8,128)S(1)}, u32[]{:S(2)}, u32[]{:S(2)}) collective-permute-start(f32[2,16,2048]{2,1,0:T(8,128)S(1)} %slice.142), channel_id=1, source_target_pairs={{0,4},{1,5},{2,6},{3,7},{4,0},{5,1},{6,2},{7,3},{8,12},{9,13},{10,... | collective-permute-start | bytes 786440 | tf_op jit(solution)/shard_map/ppermute | solution.py:54
  99.1 15.8 %collective-permute-start.12 = (f32[2,32,2048]{2,1,0:T(8,128)S(1)}, f32[2,32,2048]{2,1,0:T(8,128)S(1)}, u32[]{:S(2)}, u32[]{:S(2)}) collective-permute-start(f32[2,32,2048]{2,1,0:T(8,128)S(1)} %slice.147), channel_id=1, source_target_pairs={{0,2},{1,3},{2,0},{3,1},{4,6},{5,7},{6,4},{7,5},{8,10},{9,11},{10,... | collective-permute-start | bytes 1572872 | tf_op jit(solution)/shard_map/ppermute | solution.py:54
  99.9 23.8 %collective-permute-start.17 = (f32[2,32,2048]{2,1,0:T(8,128)S(1)}, f32[2,32,2048]{2,1,0:T(8,128)S(1)}, u32[]{:S(2)}, u32[]{:S(2)}) collective-permute-start(f32[2,32,2048]{2,1,0:T(8,128)S(1)} %slice.154), channel_id=1, source_target_pairs={{0,2},{1,3},{2,0},{3,1},{4,6},{5,7},{6,4},{7,5},{8,10},{9,11},{10,... | collective-permute-start | bytes 1572872 | tf_op jit(solution)/shard_map/ppermute | solution.py:54
  101.5 10.3 %collective-permute-start.4 = (f32[2,8,2048]{2,1,0:T(8,128)S(1)}, f32[2,8,2048]{2,1,0:T(8,128)S(1)}, u32[]{:S(2)}, u32[]{:S(2)}) collective-permute-start(f32[2,8,2048]{2,1,0:T(8,128)S(1)} %slice.137), channel_id=1, source_target_pairs={{0,12},{1,13},{2,14},{3,15},{4,8},{5,9},{6,10},{7,11},{8,4},{9,5},... | collective-permute-start | bytes 393224 | tf_op jit(solution)/shard_map/ppermute | solution.py:54
  105.7 9.1 %collective-permute-start.9 = (f32[2,8,2048]{2,1,0:T(8,128)S(1)}, f32[2,8,2048]{2,1,0:T(8,128)S(1)}, u32[]{:S(2)}, u32[]{:S(2)}) collective-permute-start(f32[2,8,2048]{2,1,0:T(8,128)S(1)} %slice.144), channel_id=1, source_target_pairs={{0,12},{1,13},{2,14},{3,15},{4,8},{5,9},{6,10},{7,11},{8,4},{9,5},... | collective-permute-start | bytes 393224 | tf_op jit(solution)/shard_map/ppermute | solution.py:54
  115.0 9.3 %collective-permute-start.13 = (f32[2,16,2048]{2,1,0:T(8,128)S(1)}, f32[2,16,2048]{2,1,0:T(8,128)S(1)}, u32[]{:S(2)}, u32[]{:S(2)}) collective-permute-start(f32[2,16,2048]{2,1,0:T(8,128)S(1)} %slice.149), channel_id=1, source_target_pairs={{0,4},{1,5},{2,6},{3,7},{4,0},{5,1},{6,2},{7,3},{8,12},{9,13},{10,... | collective-permute-start | bytes 786440 | tf_op jit(solution)/shard_map/ppermute | solution.py:54
  123.7 7.3 %collective-permute-start.18 = (f32[2,16,2048]{2,1,0:T(8,128)S(1)}, f32[2,16,2048]{2,1,0:T(8,128)S(1)}, u32[]{:S(2)}, u32[]{:S(2)}) collective-permute-start(f32[2,16,2048]{2,1,0:T(8,128)S(1)} %slice.156), channel_id=1, source_target_pairs={{0,4},{1,5},{2,6},{3,7},{4,0},{5,1},{6,2},{7,3},{8,12},{9,13},{10,... | collective-permute-start | bytes 786440 | tf_op jit(solution)/shard_map/ppermute | solution.py:54
  124.3 13.0 %collective-permute-start.14 = (f32[2,8,2048]{2,1,0:T(8,128)S(1)}, f32[2,8,2048]{2,1,0:T(8,128)S(1)}, u32[]{:S(2)}, u32[]{:S(2)}) collective-permute-start(f32[2,8,2048]{2,1,0:T(8,128)S(1)} %slice.151), channel_id=1, source_target_pairs={{0,12},{1,13},{2,14},{3,15},{4,8},{5,9},{6,10},{7,11},{8,4},{9,5},... | collective-permute-start | bytes 393224 | tf_op jit(solution)/shard_map/ppermute | solution.py:54
  131.1 9.2 %collective-permute-start.19 = (f32[2,8,2048]{2,1,0:T(8,128)S(1)}, f32[2,8,2048]{2,1,0:T(8,128)S(1)}, u32[]{:S(2)}, u32[]{:S(2)}) collective-permute-start(f32[2,8,2048]{2,1,0:T(8,128)S(1)} %slice.158), channel_id=1, source_target_pairs={{0,12},{1,13},{2,14},{3,15},{4,8},{5,9},{6,10},{7,11},{8,4},{9,5},... | collective-permute-start | bytes 393224 | tf_op jit(solution)/shard_map/ppermute | solution.py:54
  (7 other events, 18.9 us)

commit v2 on v0

--- a/solution.py
+++ b/solution.py
@@ -1,7 +1,14 @@
+import functools
+
 import jax
 import jax.numpy as jnp
 from jax import lax
+from jax.experimental import pallas as pl
+from jax.experimental.pallas import tpu as pltpu
 from jax.sharding import PartitionSpec as P
+
+PIECES = 4
+BRIEF = pl.CostEstimate(flops=1024, bytes_accessed=1024, transcendentals=0)
 
 
 def product(left, right):
@@ -14,7 +21,7 @@
     return (weighted, jnp.sum(log_grad, axis=0))
 
 
-def body(inverse_rows, kinetic_rows, virt_values, virt_laplacians, local_energy):
+def general_body(inverse_rows, kinetic_rows, virt_values, virt_laplacians, local_energy):
     walk_count = lax.axis_size("walk")
     walker_count = walk_count * local_energy.shape[0]
     energy_sum = lax.psum(jnp.sum(local_energy), "walk")
@@ -35,6 +42,187 @@
     return (gradient_part / walker_count, log_part / walker_count)
 
 
+def stage_masks(count):
+    bits = count.bit_length() - 1
+    masks = [1 << bit for bit in range(bits)]
+    if bits >= 2:
+        masks[-1] = 3 << (bits - 2)
+    return masks
+
+
+def place_weights(masks):
+    bits = len(masks)
+    weights = [0] * bits
+    for place in range(1 << bits):
+        difference = 0
+        for stage, mask in enumerate(masks):
+            if place >> (bits - 1 - stage) & 1:
+                difference ^= mask
+        if difference & (difference - 1) == 0 and difference:
+            weights[difference.bit_length() - 1] = place
+    return weights
+
+
+def swap(array, axis, mask):
+    pairs = [(source, source ^ mask) for source in range(lax.axis_size(axis))]
+    return lax.ppermute(array, axis, pairs)
+
+
+def near_kernel(virt_ref, inverse_ref, kinetic_ref, values_ref, laps_ref, out_ref):
+    f32 = jnp.float32
+    inverse = inverse_ref[...].reshape(-1, inverse_ref.shape[-1])
+    kinetic = kinetic_ref[...].reshape(-1, kinetic_ref.shape[-1])
+    values = values_ref[...]
+    log = jnp.dot(inverse, values, preferred_element_type=f32)
+    rest = jnp.dot(kinetic, values, preferred_element_type=f32)
+    rest -= jnp.dot(inverse, laps_ref[...], preferred_element_type=f32)
+    out_ref[0] = 0.5 * rest
+    out_ref[1] = log
+
+
+def near_product(virt, mine, values, laplacians, tile):
+    _, height, depth = mine.shape
+    width = values.shape[1]
+    rows_spec = lambda index: pl.BlockSpec((None, height, depth), lambda j, virt: (index, 0, 0))
+    table_spec = pl.BlockSpec((depth, tile), lambda j, virt: (virt[0], j))
+    return pl.pallas_call(
+        near_kernel,
+        out_shape=jax.ShapeDtypeStruct((2, height, width), jnp.float32),
+        grid_spec=pltpu.PrefetchScalarGridSpec(
+            num_scalar_prefetch=1,
+            grid=(width // tile,),
+            in_specs=[rows_spec(0), rows_spec(1), table_spec, table_spec],
+            out_specs=pl.BlockSpec((2, height, tile), lambda j, virt: (0, 0, j)),
+        ),
+        compiler_params=pltpu.CompilerParams(vmem_limit_bytes=24 * 1024 * 1024),
+        cost_estimate=BRIEF,
+        name="near_product",
+    )(virt, mine, mine, values, laplacians)
+
+
+def far_kernel(weights, count, virt_ref, me_ref, scale_ref, far_ref, near_ref, values_ref, laps_ref, *rest):
+    send_ref, keep_ref, place_ref = rest[-3:]
+    height, depth = far_ref.shape[1], far_ref.shape[2]
+    rows = height // count
+    half = height // 2
+    f32 = jnp.float32
+    both = jnp.dot(far_ref[...].reshape(2 * height, depth), values_ref[...], preferred_element_type=f32)
+    laps = jnp.dot(far_ref[0], laps_ref[...], preferred_element_type=f32)
+    log = both[:height] + near_ref[1]
+    weighted = scale_ref[0] * log + (0.5 * (both[height:] - laps) + near_ref[0])
+    for dest in range(count):
+        difference = dest ^ me_ref[0]
+        place = 0
+        for bit, weight in enumerate(weights):
+            place = place ^ (((difference >> bit) & 1) * weight)
+        target = pl.ds(pl.multiple_of(place * rows, rows), rows)
+        source = slice(dest * rows, (dest + 1) * rows)
+        place_ref[0, target, :] = weighted[source]
+        place_ref[1, target, :] = log[source]
+    keep_ref[...] = place_ref[:, :half]
+    send_ref[...] = place_ref[:, half:]
+
+
+def far_product(virt, me, scale, theirs, near, values, laplacians, tile, masks, after):
+    _, height, depth = theirs.shape
+    width = values.shape[1]
+    half = height // 2
+    count = 1 << len(masks)
+    table_spec = pl.BlockSpec((depth, tile), lambda j, virt, me: (1 - virt[0], j))
+    out_spec = pl.BlockSpec((2, half, tile), lambda j, virt, me: (0, 0, j))
+    out = jax.ShapeDtypeStruct((2, half, width), jnp.float32)
+    return pl.pallas_call(
+        functools.partial(far_kernel, place_weights(masks), count),
+        out_shape=(out, out),
+        grid_spec=pltpu.PrefetchScalarGridSpec(
+            num_scalar_prefetch=2,
+            grid=(width // tile,),
+            in_specs=[
+                pl.BlockSpec(memory_space=pltpu.SMEM),
+                pl.BlockSpec((2, height, depth), lambda j, virt, me: (0, 0, 0)),
+                pl.BlockSpec((2, height, tile), lambda j, virt, me: (0, 0, j)),
+                table_spec,
+                table_spec,
+            ]
+            + [pl.BlockSpec(memory_space=pl.ANY)] * len(after),
+            out_specs=(out_spec, out_spec),
+            scratch_shapes=[pltpu.VMEM((2, height, tile), jnp.float32)],
+        ),
+        compiler_params=pltpu.CompilerParams(vmem_limit_bytes=24 * 1024 * 1024),
+        cost_estimate=BRIEF,
+        name="far_product",
+    )(virt, me, scale, theirs, near, values, laplacians, *after)
+
+
+def halve_kernel(keep_ref, came_ref, send_ref, kept_ref):
+    half = kept_ref.shape[1]
+    kept_ref[...] = keep_ref[:, :half] + came_ref[:, :half]
+    send_ref[...] = keep_ref[:, half:] + came_ref[:, half:]
+
+
+def halve(keep, came):
+    _, height, width = keep.shape
+    whole = pl.BlockSpec(memory_space=pltpu.VMEM)
+    out = jax.ShapeDtypeStruct((2, height // 2, width), jnp.float32)
+    return pl.pallas_call(
+        halve_kernel,
+        out_shape=(out, out),
+        in_specs=[whole, whole],
+        out_specs=(whole, whole),
+        cost_estimate=BRIEF,
+        name="halve",
+    )(keep, came)
+
+
+def pieced_body(pieces, tile, inverse_rows, kinetic_rows, virt_values, virt_laplacians, local_energy):
+    count = lax.axis_size("walk")
+    masks = stage_masks(count)
+    me = lax.axis_index("walk").astype(jnp.int32).reshape(1)
+    virt = lax.axis_index("virt").astype(jnp.int32).reshape(1)
+    occupied, depth = inverse_rows.shape[1:]
+    by_dest = (count, occupied // count, depth)
+    inverse, kinetic = inverse_rows.reshape(by_dest), kinetic_rows.reshape(by_dest)
+    values = pltpu.with_memory_space_constraint(virt_values[0], pltpu.HBM)
+    laplacians = pltpu.with_memory_space_constraint(virt_laplacians[0], pltpu.HBM)
+    rows = occupied // (count * pieces)
+
+    mine, theirs = [], []
+    for piece in range(pieces):
+        part = slice(piece * rows, (piece + 1) * rows)
+        taken = [array[:, part].reshape(count * rows, depth) for array in (inverse, kinetic)]
+        mine.append(jnp.stack(taken))
+        theirs.append(swap(mine[piece], "virt", 1))
+
+    energy_sum = jnp.broadcast_to(local_energy, (1, 128))
+    for mask in masks:
+        energy_sum = energy_sum + swap(energy_sum, "walk", mask)
+    average = energy_sum[0, 0] / count
+    scale = 2.0 * (local_energy - average)
+
+    near = [near_product(virt, part, values, laplacians, tile) for part in mine]
+    stages = len(masks)
+    send, keep, done = {}, {}, {}
+    for turn in range(pieces + stages + 1):
+        after = [send[other] for other in sorted(send)]
+        if turn < pieces:
+            send[turn], keep[turn] = far_product(
+                virt, me, scale, theirs[turn], near[turn], values, laplacians, tile, masks, after
+            )
+        for piece in range(turn - 1, max(turn - 1 - stages, -1), -1):
+            if piece >= pieces:
+                continue
+            stage = turn - 1 - piece
+            came = swap(send.pop(piece), "walk", masks[stage])
+            if stage + 1 < stages:
+                send[piece], keep[piece] = halve(keep[piece], came)
+            else:
+                done[piece] = keep[piece] + came
+    done = [done[piece] for piece in range(pieces)]
+    log_part = jnp.concatenate([total[1] for total in done], axis=0) / count
+    gradient_part = jnp.concatenate([total[0] for total in done], axis=0) / count
+    return (gradient_part, log_part)
+
+
 def solution(mesh):
     placed = (
         P("walk", None, "virt"),
@@ -43,6 +231,24 @@
         P("walk", None, "virt"),
         P("walk"),
     )
+
+    def body(inverse_rows, kinetic_rows, virt_values, virt_laplacians, local_energy):
+        count = mesh.shape["walk"]
+        walkers, occupied, depth = inverse_rows.shape
+        width = virt_values.shape[2]
+        tile = 512
+        fits = (
+            walkers == 1
+            and mesh.shape["virt"] == 2
+            and count >= 4
+            and count & (count - 1) == 0
+            and occupied % (count * PIECES * 8) == 0
+            and depth % 256 == 0
+            and width % tile == 0
+        )
+        form = functools.partial(pieced_body, PIECES, tile) if fits else general_body
+        return form(inverse_rows, kinetic_rows, virt_values, virt_laplacians, local_energy)
+
     return jax.shard_map(
         body,
         mesh=mesh,

time: 250 us -> 164 us (0.66)
  waiting for transfers between devices: 163 us -> 52 us
  Pallas kernels: 0 us -> 70.4 us
  blocking collectives: 35.5 us -> 0 us
  matrix products: 33 us -> 0 us
  starting transfers between devices: 0.16 us -> 23 us
  between operations: 15.1 us -> 1.64 us
  local copies, waits for them, and re-layouts: 0.01 us -> 13.1 us
    reduce_scatter x2 -> x0, waiting for transfers between devices: 146 us -> none  [the longest x1 74.2 us: body(): lax.psum_scatter(log_sum, 'walk', scatter_dimension=0, tiled=True)]
    pallas_call x0 -> x20, Pallas kernels: none -> 70.4 us  [the longest x12 25.4 us: halve(): pl.pallas_call(halve_kernel, out_shape=(out, out), in_specs=[whole, whole...]
    ppermute x0 -> x24, waiting for transfers between devices: none -> 52 us  [swap(): return lax.ppermute(array, axis, pairs)]
    psum x1 -> x0, blocking collectives: 35.5 us -> none  [body(): energy_sum = lax.psum(jnp.sum(local_energy), 'walk')]
    dot_general x3 -> x0, matrix products: 33 us -> none  [product(): jnp.einsum('woe,wev->wov', left, right, preferred_element_type=jnp.float32)]
    ppermute x0 -> x24, starting transfers between devices: none -> 23 us  [swap(): return lax.ppermute(array, axis, pairs)]
    all_gather x2 -> x0, waiting for transfers between devices: 14.5 us -> none  [the longest x1 14.5 us: body(): lax.all_gather(kinetic_rows, 'virt', axis=2, tiled=True)]
    unnamed x2 -> x46, local copies, waits for them, and re-layouts: 0.01 us -> 10.5 us
  transfers between devices with their start and end apart: 4 -> 24, of which waited for: 3 -> 12; matrix products, arithmetic and copies ran while one was open for 9% -> 1% of each run, Pallas kernels for 0% -> 39%
where the time goes in v2:
time: 164 us
  Pallas kernels  70.4 us (43%)
  waiting for transfers between devices  52 us (32%)
  starting transfers between devices  23 us (14%)
  local copies, waits for them, and re-layouts  13.1 us (8%)
  other arithmetic  3.53 us (2%)
    ppermute x24, waiting for transfers between devices, swap(): return lax.ppermute(array, axis, pairs)  52 us
    pallas_call x12, Pallas kernels, halve(): pl.pallas_call(halve_kernel, out_shape=(out, out), in_specs=[whole, whole...  25.4 us
    pallas_call x4, Pallas kernels, far_product(): pl.pallas_call(functools.partial(far_kernel, place_weights(masks), count)...  23.9 us
    ppermute x24, starting transfers between devices, swap(): return lax.ppermute(array, axis, pairs)  23 us
    pallas_call x4, Pallas kernels, near_product(): pl.pallas_call(near_kernel, out_shape=jax.ShapeDtypeStruct((2, height, wi...  21.1 us
    unnamed x46, local copies, waits for them, and re-layouts  10.5 us
  transfers between devices with their start and end apart: 24, of which 12 were waited for; matrix products, arithmetic and copies ran while one was open for 1% of the time, Pallas kernels for 39%

profile of v2, /device:TPU:0, one launch (start us, length us, event | category | flops | bytes accessed | tf_op | source)
XLA Modules:
  0.0 163.6 jit_solution(2247046359006250723)
XLA Ops:
  0.6 2.6 %slice_bitcast_fusion.2 = (bf16[1,128,1024]{2,1,0:T(8,128)(2,1)}, bf16[1,128,1024]{2,1,0:T(8,128)(2,1)S(1)}, bf16[1,128,1024]{2,1,0:T(8,128)(2,1)}, bf16[1,128,1...) fusion(bf16[16,32,1024]{2,1,0:T(8,128)(2,1)} %bitcast.60, ...), kind=kLoop, calls=%fused_computation.6 | loop fusion | bytes 4194304 | tf_op jit(solution)/shard_map/stack;reshape | solution.py:193
  3.3 3.0 %collective-permute-start.4 = (bf16[2,128,1024]{2,1,0:T(8,128)(2,1)S(1)}, bf16[2,128,1024]{2,1,0:T(8,128)(2,1)S(1)}, u32[]{:S(2)}, u32[]{:S(2)}) collective-permute-start(bf16[2,128,1024]{2,1,0:T(8,128)(2,1)S(1)} %pad_maximum_fusion.inverse_ref.kinetic_ref), channel_id=1, source_target_pairs={{0,16},{16,0},{1,17},{17,1},{2,18},{18,2},{3,19},{19,3},{4,20},{20... | collective-permute-start | bytes 1572872 | tf_op jit(solution)/shard_map/ppermute | solution.py:68
  9.7 2.0 %collective-permute-done.1 = f32[1,128]{1,0:T(1,128)S(1)} collective-permute-done((f32[1,128]{1,0:T(1,128)S(1)}, f32[1,128]{1,0:T(1,128)S(1)}, u32[]{:S(2)}, u32[]{:S(2)}) %collective-permute-start.1) | collective-permute-done | bytes 544 | tf_op jit(solution)/shard_map/ppermute | solution.py:68
  13.3 2.0 %collective-permute-done.2 = f32[1,128]{1,0:T(1,128)S(1)} collective-permute-done((f32[1,128]{1,0:T(1,128)S(1)}, f32[1,128]{1,0:T(1,128)S(1)}, u32[]{:S(2)}, u32[]{:S(2)}) %collective-permute-start.2) | collective-permute-done | bytes 544 | tf_op jit(solution)/shard_map/ppermute | solution.py:68
  15.3 3.6 %collective-permute-start.3 = (f32[1,128]{1,0:T(1,128)S(1)}, f32[1,128]{1,0:T(1,128)S(1)}, u32[]{:S(2)}, u32[]{:S(2)}) collective-permute-start(f32[1,128]{1,0:T(1,128)S(1)} %add.26), channel_id=1, source_target_pairs={{0,12},{1,13},{2,14},{3,15},{4,8},{5,9},{6,10},{7,11},{8,4},{9,5},... | collective-permute-start | bytes 1544 | tf_op jit(solution)/shard_map/ppermute | solution.py:68
  18.9 5.2 %near_product.4.near_ref = f32[2,128,2048]{2,1,0:T(8,128)S(1)} custom-call(s32[1]{0:T(128)} %bitcast.virt_ref, bf16[2,128,1024]{2,1,0:T(8,128)(2,1)S(1)} %pad_maximum_fusion.inverse_ref.kinetic_ref, bf16[2,128,1024]{2,1,0:T(8,128)(2,1)S(1)} %pad_maximum_fusion.inverse_ref.kinetic_ref, bf16[2048,2048]{1,0:T(8,128)(2,1)} %bitcast.44, bf16[2048,2048]{1,0:T(8,128)(2,1)} %bitcast.52), custom_call_target="tpu_custom_call" | custom-call | flops 1024 | bytes 1024 | tf_op jit(solution)/shard_map/near_product/pallas_call | solution.py:88
  24.2 5.5 %far_product.4 = (f32[2,64,2048]{2,1,0:T(8,128)S(1)}, f32[2,64,2048]{2,1,0:T(8,128)S(1)}) custom-call(s32[1]{0:T(128)} %bitcast.virt_ref, s32[1]{0:T(128)} %bitcast.1.me_ref, f32[1]{0:T(128)S(6)} %mul.3.scale_ref, bf16[2,128,1024]{2,1,0:T(8,128)(2,1)S(1)} %collective-permute-done.4.far_ref, f32[2,128,2048]{2,1,0:T(8,128)S(1)} %near_product.4.near_ref, ...), custom_call_target="tpu_custom_call" | custom-call | flops 1024 | bytes 1024 | tf_op jit(solution)/shard_map/far_product/pallas_call | solution.py:134
  31.3 5.2 %near_product.5.near_ref = f32[2,128,2048]{2,1,0:T(8,128)S(1)} custom-call(s32[1]{0:T(128)} %bitcast.virt_ref, bf16[2,128,1024]{2,1,0:T(8,128)(2,1)S(1)} %pad_maximum_fusion.1.inverse_ref.kinetic_ref, bf16[2,128,1024]{2,1,0:T(8,128)(2,1)S(1)} %pad_maximum_fusion.1.inverse_ref.kinetic_ref, bf16[2048,2048]{1,0:T(8,128)(2,1)} %bitcast.46, ...), custom_call_target="tpu_custom_call" | custom-call | flops 1024 | bytes 1024 | tf_op jit(solution)/shard_map/near_product/pallas_call | solution.py:88
  36.5 8.6 %collective-permute-done.9.far_ref = bf16[2,128,1024]{2,1,0:T(8,128)(2,1)S(1)} collective-permute-done((bf16[2,128,1024]{2,1,0:T(8,128)(2,1)S(1)}, bf16[2,128,1024]{2,1,0:T(8,128)(2,1)S(1)}, u32[]{:S(2)}, u32[]{:S(2)}) %collective-permute-start.9) | collective-permute-done | bytes 524320 | tf_op jit(solution)/shard_map/ppermute | solution.py:68
  45.1 6.1 %far_product.5 = (f32[2,64,2048]{2,1,0:T(8,128)}, f32[2,64,2048]{2,1,0:T(8,128)S(1)}) custom-call(s32[1]{0:T(128)} %bitcast.virt_ref, s32[1]{0:T(128)} %bitcast.1.me_ref, f32[1]{0:T(128)S(6)} %mul.3.scale_ref, bf16[2,128,1024]{2,1,0:T(8,128)(2,1)S(1)} %collective-permute-done.9.far_ref, f32[2,128,2048]{2,1,0:T(8,128)S(1)} %near_product.5.near_ref, ...), custom_call_target="tpu_custom_call" | custom-call | flops 1024 | bytes 1024 | tf_op jit(solution)/shard_map/far_product/pallas_call | solution.py:134
  53.2 2.6 %halve.12 = (f32[2,32,2048]{2,1,0:T(8,128)}, f32[2,32,2048]{2,1,0:T(8,128)}) custom-call(f32[2,64,2048]{2,1,0:T(8,128)} %copy-done.3, f32[2,64,2048]{2,1,0:T(8,128)} %copy-done.8), custom_call_target="tpu_custom_call" | custom-call | flops 1024 | bytes 1024 | tf_op jit(solution)/shard_map/halve/pallas_call | solution.py:167
  58.7 5.2 %near_product.6.near_ref = f32[2,128,2048]{2,1,0:T(8,128)S(1)} custom-call(s32[1]{0:T(128)} %bitcast.virt_ref, bf16[2,128,1024]{2,1,0:T(8,128)(2,1)S(1)} %pad_maximum_fusion.2.inverse_ref.kinetic_ref, bf16[2,128,1024]{2,1,0:T(8,128)(2,1)S(1)} %pad_maximum_fusion.2.inverse_ref.kinetic_ref, bf16[2048,2048]{1,0:T(8,128)(2,1)} %bitcast.48, ...), custom_call_target="tpu_custom_call" | custom-call | flops 1024 | bytes 1024 | tf_op jit(solution)/shard_map/near_product/pallas_call | solution.py:88
  63.8 2.3 %collective-permute-done.14.far_ref = bf16[2,128,1024]{2,1,0:T(8,128)(2,1)S(1)} collective-permute-done((bf16[2,128,1024]{2,1,0:T(8,128)(2,1)S(1)}, bf16[2,128,1024]{2,1,0:T(8,128)(2,1)S(1)}, u32[]{:S(2)}, u32[]{:S(2)}) %collective-permute-start.14) | collective-permute-done | bytes 524320 | tf_op jit(solution)/shard_map/ppermute | solution.py:68
  66.2 6.1 %far_product.6 = (f32[2,64,2048]{2,1,0:T(8,128)}, f32[2,64,2048]{2,1,0:T(8,128)S(1)}) custom-call(s32[1]{0:T(128)} %bitcast.virt_ref, s32[1]{0:T(128)} %bitcast.1.me_ref, f32[1]{0:T(128)S(6)} %mul.3.scale_ref, bf16[2,128,1024]{2,1,0:T(8,128)(2,1)S(1)} %collective-permute-done.14.far_ref, f32[2,128,2048]{2,1,0:T(8,128)S(1)} %near_product.6.near_ref, ...), custom_call_target="tpu_custom_call" | custom-call | flops 1024 | bytes 1024 | tf_op jit(solution)/shard_map/far_product/pallas_call | solution.py:134
  72.3 5.6 %near_product.7.near_ref = f32[2,128,2048]{2,1,0:T(8,128)S(1)} custom-call(s32[1]{0:T(128)} %bitcast.virt_ref, bf16[2,128,1024]{2,1,0:T(8,128)(2,1)S(1)} %pad_maximum_fusion.3.inverse_ref.kinetic_ref, bf16[2,128,1024]{2,1,0:T(8,128)(2,1)S(1)} %pad_maximum_fusion.3.inverse_ref.kinetic_ref, bf16[2048,2048]{1,0:T(8,128)(2,1)} %bitcast.50, ...), custom_call_target="tpu_custom_call" | custom-call | flops 1024 | bytes 1024 | tf_op jit(solution)/shard_map/near_product/pallas_call | solution.py:88
  77.9 2.6 %halve.15 = (f32[2,32,2048]{2,1,0:T(8,128)}, f32[2,32,2048]{2,1,0:T(8,128)}) custom-call(f32[2,64,2048]{2,1,0:T(8,128)} %copy-done.1, f32[2,64,2048]{2,1,0:T(8,128)} %collective-permute-done.10.came_ref), custom_call_target="tpu_custom_call" | custom-call | flops 1024 | bytes 1024 | tf_op jit(solution)/shard_map/halve/pallas_call | solution.py:167
  80.5 2.0 %halve.13 = (f32[2,16,2048]{2,1,0:T(8,128)}, f32[2,16,2048]{2,1,0:T(8,128)}) custom-call(f32[2,32,2048]{2,1,0:T(8,128)} %get-tuple-element.36.keep_ref, f32[2,32,2048]{2,1,0:T(8,128)} %collective-permute-done.6.came_ref), custom_call_target="tpu_custom_call" | custom-call | flops 1024 | bytes 1024 | tf_op jit(solution)/shard_map/halve/pallas_call | solution.py:167
  83.4 6.1 %far_product.7 = (f32[2,64,2048]{2,1,0:T(8,128)}, f32[2,64,2048]{2,1,0:T(8,128)S(1)}) custom-call(s32[1]{0:T(128)} %bitcast.virt_ref, s32[1]{0:T(128)} %bitcast.1.me_ref, f32[1]{0:T(128)S(6)} %mul.3.scale_ref, bf16[2,128,1024]{2,1,0:T(8,128)(2,1)S(1)} %collective-permute-done.19.far_ref, f32[2,128,2048]{2,1,0:T(8,128)S(1)} %near_product.7.near_ref, ...), custom_call_target="tpu_custom_call" | custom-call | flops 1024 | bytes 1024 | tf_op jit(solution)/shard_map/far_product/pallas_call | solution.py:134
  92.2 2.6 %halve.18 = (f32[2,32,2048]{2,1,0:T(8,128)}, f32[2,32,2048]{2,1,0:T(8,128)}) custom-call(f32[2,64,2048]{2,1,0:T(8,128)} %copy-done.2, f32[2,64,2048]{2,1,0:T(8,128)} %collective-permute-done.15.came_ref), custom_call_target="tpu_custom_call" | custom-call | flops 1024 | bytes 1024 | tf_op jit(solution)/shard_map/halve/pallas_call | solution.py:167
  95.3 10.3 %collective-permute-done.11.came_ref = f32[2,32,2048]{2,1,0:T(8,128)S(1)} collective-permute-done((f32[2,32,2048]{2,1,0:T(8,128)}, f32[2,32,2048]{2,1,0:T(8,128)S(1)}, u32[]{:S(2)}, u32[]{:S(2)}) %collective-permute-start.11) | collective-permute-done | bytes 524320 | tf_op jit(solution)/shard_map/ppermute | solution.py:68
  106.4 2.0 %halve.16 = (f32[2,16,2048]{2,1,0:T(8,128)}, f32[2,16,2048]{2,1,0:T(8,128)}) custom-call(f32[2,32,2048]{2,1,0:T(8,128)} %get-tuple-element.44.keep_ref, f32[2,32,2048]{2,1,0:T(8,128)} %copy-done.16), custom_call_target="tpu_custom_call" | custom-call | flops 1024 | bytes 1024 | tf_op jit(solution)/shard_map/halve/pallas_call | solution.py:167
  111.8 7.1 %collective-permute-done.12.came_ref = f32[2,16,2048]{2,1,0:T(8,128)S(1)} collective-permute-done((f32[2,16,2048]{2,1,0:T(8,128)}, f32[2,16,2048]{2,1,0:T(8,128)S(1)}, u32[]{:S(2)}, u32[]{:S(2)}) %collective-permute-start.12) | collective-permute-done | bytes 262176 | tf_op jit(solution)/shard_map/ppermute | solution.py:68
  122.3 2.6 %halve.21 = (f32[2,32,2048]{2,1,0:T(8,128)}, f32[2,32,2048]{2,1,0:T(8,128)}) custom-call(f32[2,64,2048]{2,1,0:T(8,128)} %copy-done, f32[2,64,2048]{2,1,0:T(8,128)} %copy-done.7), custom_call_target="tpu_custom_call" | custom-call | flops 1024 | bytes 1024 | tf_op jit(solution)/shard_map/halve/pallas_call | solution.py:167
  126.3 2.0 %collective-permute-done.13 = f32[2,8,2048]{2,1,0:T(8,128)S(1)} collective-permute-done((f32[2,8,2048]{2,1,0:T(8,128)}, f32[2,8,2048]{2,1,0:T(8,128)S(1)}, u32[]{:S(2)}, u32[]{:S(2)}) %collective-permute-start.13) | collective-permute-done | bytes 131104 | tf_op jit(solution)/shard_map/ppermute | solution.py:68
  129.1 2.0 %halve.19 = (f32[2,16,2048]{2,1,0:T(8,128)}, f32[2,16,2048]{2,1,0:T(8,128)}) custom-call(f32[2,32,2048]{2,1,0:T(8,128)} %get-tuple-element.52.keep_ref, f32[2,32,2048]{2,1,0:T(8,128)} %copy-done.14), custom_call_target="tpu_custom_call" | custom-call | flops 1024 | bytes 1024 | tf_op jit(solution)/shard_map/halve/pallas_call | solution.py:167
  131.1 6.6 %collective-permute-done.17.came_ref = f32[2,16,2048]{2,1,0:T(8,128)S(1)} collective-permute-done((f32[2,16,2048]{2,1,0:T(8,128)}, f32[2,16,2048]{2,1,0:T(8,128)S(1)}, u32[]{:S(2)}, u32[]{:S(2)}) %collective-permute-start.17) | collective-permute-done | bytes 262176 | tf_op jit(solution)/shard_map/ppermute | solution.py:68
  140.1 1.9 %collective-permute-start.18 = (f32[2,8,2048]{2,1,0:T(8,128)}, f32[2,8,2048]{2,1,0:T(8,128)S(1)}, u32[]{:S(2)}, u32[]{:S(2)}) collective-permute-start(f32[2,8,2048]{2,1,0:T(8,128)} %get-tuple-element.57), channel_id=1, source_target_pairs={{0,12},{1,13},{2,14},{3,15},{4,8},{5,9},{6,10},{7,11},{8,4},{9,5},... | collective-permute-start | bytes 393224 | tf_op jit(solution)/shard_map/ppermute | solution.py:68
  142.8 2.0 %halve.22 = (f32[2,16,2048]{2,1,0:T(8,128)}, f32[2,16,2048]{2,1,0:T(8,128)}) custom-call(f32[2,32,2048]{2,1,0:T(8,128)} %get-tuple-element.60.keep_ref, f32[2,32,2048]{2,1,0:T(8,128)} %copy-done.15), custom_call_target="tpu_custom_call" | custom-call | flops 1024 | bytes 1024 | tf_op jit(solution)/shard_map/halve/pallas_call | solution.py:167
  144.9 2.3 %collective-permute-done.18 = f32[2,8,2048]{2,1,0:T(8,128)S(1)} collective-permute-done((f32[2,8,2048]{2,1,0:T(8,128)}, f32[2,8,2048]{2,1,0:T(8,128)S(1)}, u32[]{:S(2)}, u32[]{:S(2)}) %collective-permute-start.18) | collective-permute-done | bytes 131104 | tf_op jit(solution)/shard_map/ppermute | solution.py:68
  148.0 3.8 %collective-permute-done.22.came_ref = f32[2,16,2048]{2,1,0:T(8,128)S(1)} collective-permute-done((f32[2,16,2048]{2,1,0:T(8,128)}, f32[2,16,2048]{2,1,0:T(8,128)S(1)}, u32[]{:S(2)}, u32[]{:S(2)}) %collective-permute-start.22) | collective-permute-done | bytes 262176 | tf_op jit(solution)/shard_map/ppermute | solution.py:68
  154.3 3.0 %collective-permute-start.23 = (f32[2,8,2048]{2,1,0:T(8,128)}, f32[2,8,2048]{2,1,0:T(8,128)S(1)}, u32[]{:S(2)}, u32[]{:S(2)}) collective-permute-start(f32[2,8,2048]{2,1,0:T(8,128)} %get-tuple-element.65), channel_id=1, source_target_pairs={{0,12},{1,13},{2,14},{3,15},{4,8},{5,9},{6,10},{7,11},{8,4},{9,5},... | collective-permute-start | bytes 393224 | tf_op jit(solution)/shard_map/ppermute | solution.py:68
  157.3 4.0 %collective-permute-done.23 = f32[2,8,2048]{2,1,0:T(8,128)S(1)} collective-permute-done((f32[2,8,2048]{2,1,0:T(8,128)}, f32[2,8,2048]{2,1,0:T(8,128)S(1)}, u32[]{:S(2)}, u32[]{:S(2)}) %collective-permute-start.23) | collective-permute-done | bytes 131104 | tf_op jit(solution)/shard_map/ppermute | solution.py:68
  (102 shorter events, 33.6 us)
Async XLA Ops:
  3.3 20.8 %collective-permute-start.4 = (bf16[2,128,1024]{2,1,0:T(8,128)(2,1)S(1)}, bf16[2,128,1024]{2,1,0:T(8,128)(2,1)S(1)}, u32[]{:S(2)}, u32[]{:S(2)}) collective-permute-start(bf16[2,128,1024]{2,1,0:T(8,128)(2,1)S(1)} %pad_maximum_fusion.inverse_ref.kinetic_ref), channel_id=1, source_target_pairs={{0,16},{16,0},{1,17},{17,1},{2,18},{18,2},{3,19},{19,3},{4,20},{20... | collective-permute-start | bytes 1572872 | tf_op jit(solution)/shard_map/ppermute | solution.py:68
  7.0 1.2 collective-permute-start
  8.2 3.5 %collective-permute-start.1 = (f32[1,128]{1,0:T(1,128)S(1)}, f32[1,128]{1,0:T(1,128)S(1)}, u32[]{:S(2)}, u32[]{:S(2)}) collective-permute-start(f32[1,128]{1,0:T(1,128)S(1)} %broadcast_add_fusion), channel_id=1, source_target_pairs={{0,2},{1,3},{2,0},{3,1},{4,6},{5,7},{6,4},{7,5},{8,10},{9,11},{10,... | collective-permute-start | bytes 1544 | tf_op jit(solution)/shard_map/ppermute | solution.py:68
  11.7 3.5 %collective-permute-start.2 = (f32[1,128]{1,0:T(1,128)S(1)}, f32[1,128]{1,0:T(1,128)S(1)}, u32[]{:S(2)}, u32[]{:S(2)}) collective-permute-start(f32[1,128]{1,0:T(1,128)S(1)} %fusion), channel_id=1, source_target_pairs={{0,4},{1,5},{2,6},{3,7},{4,0},{5,1},{6,2},{7,3},{8,12},{9,13},{10,... | collective-permute-start | bytes 1544 | tf_op jit(solution)/shard_map/ppermute | solution.py:68
  15.3 8.8 %collective-permute-start.3 = (f32[1,128]{1,0:T(1,128)S(1)}, f32[1,128]{1,0:T(1,128)S(1)}, u32[]{:S(2)}, u32[]{:S(2)}) collective-permute-start(f32[1,128]{1,0:T(1,128)S(1)} %add.26), channel_id=1, source_target_pairs={{0,12},{1,13},{2,14},{3,15},{4,8},{5,9},{6,10},{7,11},{8,4},{9,5},... | collective-permute-start | bytes 1544 | tf_op jit(solution)/shard_map/ppermute | solution.py:68
  24.1 6.5 %copy-start.12 = (bf16[1,128,1024]{2,1,0:T(8,128)(2,1)S(1)}, bf16[1,128,1024]{2,1,0:T(8,128)(2,1)}, u32[]{:S(2)}) copy-start(bf16[1,128,1024]{2,1,0:T(8,128)(2,1)} %get-tuple-element.72) | copy-start | bytes 786436
  24.2 6.5 %copy-start.13 = (bf16[1,128,1024]{2,1,0:T(8,128)(2,1)S(1)}, bf16[1,128,1024]{2,1,0:T(8,128)(2,1)}, u32[]{:S(2)}) copy-start(bf16[1,128,1024]{2,1,0:T(8,128)(2,1)} %get-tuple-element.83) | copy-start | bytes 786436
  30.7 21.3 %collective-permute-start.5 = (f32[2,64,2048]{2,1,0:T(8,128)S(1)}, f32[2,64,2048]{2,1,0:T(8,128)S(1)}, u32[]{:S(2)}, u32[]{:S(2)}) collective-permute-start(f32[2,64,2048]{2,1,0:T(8,128)S(1)} %get-tuple-element.35.rest_0_), channel_id=1, source_target_pairs={{0,1},{1,0},{2,3},{3,2},{4,5},{5,4},{6,7},{7,6},{8,9},{9,8},{10,11... | collective-permute-start | bytes 3145736 | tf_op jit(solution)/shard_map/ppermute | solution.py:68
  30.7 14.4 %collective-permute-start.9 = (bf16[2,128,1024]{2,1,0:T(8,128)(2,1)S(1)}, bf16[2,128,1024]{2,1,0:T(8,128)(2,1)S(1)}, u32[]{:S(2)}, u32[]{:S(2)}) collective-permute-start(bf16[2,128,1024]{2,1,0:T(8,128)(2,1)S(1)} %pad_maximum_fusion.1.inverse_ref.kinetic_ref), channel_id=1, source_target_pairs={{0,16},{16,0},{1,17},{17,1},{2,18},{18,2},{3,19},{19,3},{4,20},{20... | collective-permute-start | bytes 1572872 | tf_op jit(solution)/shard_map/ppermute | solution.py:68
  36.5 14.8 %copy-start.10 = (bf16[1,128,1024]{2,1,0:T(8,128)(2,1)S(1)}, bf16[1,128,1024]{2,1,0:T(8,128)(2,1)}, u32[]{:S(2)}) copy-start(bf16[1,128,1024]{2,1,0:T(8,128)(2,1)} %get-tuple-element.70) | copy-start | bytes 786436
  36.5 14.8 %copy-start.11 = (bf16[1,128,1024]{2,1,0:T(8,128)(2,1)S(1)}, bf16[1,128,1024]{2,1,0:T(8,128)(2,1)}, u32[]{:S(2)}) copy-start(bf16[1,128,1024]{2,1,0:T(8,128)(2,1)} %get-tuple-element.85) | copy-start | bytes 786436
  51.3 6.1 %copy-start.9 = (bf16[1,128,1024]{2,1,0:T(8,128)(2,1)S(1)}, bf16[1,128,1024]{2,1,0:T(8,128)(2,1)}, u32[]{:S(2)}) copy-start(bf16[1,128,1024]{2,1,0:T(8,128)(2,1)} %get-tuple-element.84) | copy-start | bytes 786436
  51.3 26.6 %collective-permute-start.10 = (f32[2,64,2048]{2,1,0:T(8,128)}, f32[2,64,2048]{2,1,0:T(8,128)}, u32[]{:S(2)}, u32[]{:S(2)}) collective-permute-start(f32[2,64,2048]{2,1,0:T(8,128)} %get-tuple-element.43.rest_1_), channel_id=1, source_target_pairs={{0,1},{1,0},{2,3},{3,2},{4,5},{5,4},{6,7},{7,6},{8,9},{9,8},{10,11... | collective-permute-start | bytes 3145736 | tf_op jit(solution)/shard_map/ppermute | solution.py:68
  51.4 14.8 %collective-permute-start.14 = (bf16[2,128,1024]{2,1,0:T(8,128)(2,1)S(1)}, bf16[2,128,1024]{2,1,0:T(8,128)(2,1)S(1)}, u32[]{:S(2)}, u32[]{:S(2)}) collective-permute-start(bf16[2,128,1024]{2,1,0:T(8,128)(2,1)S(1)} %pad_maximum_fusion.2.inverse_ref.kinetic_ref), channel_id=1, source_target_pairs={{0,16},{16,0},{1,17},{17,1},{2,18},{18,2},{3,19},{19,3},{4,20},{20... | collective-permute-start | bytes 1572872 | tf_op jit(solution)/shard_map/ppermute | solution.py:68
  55.8 24.6 %collective-permute-start.6 = (f32[2,32,2048]{2,1,0:T(8,128)}, f32[2,32,2048]{2,1,0:T(8,128)}, u32[]{:S(2)}, u32[]{:S(2)}) collective-permute-start(f32[2,32,2048]{2,1,0:T(8,128)} %get-tuple-element.37.rest_0_), channel_id=1, source_target_pairs={{0,2},{1,3},{2,0},{3,1},{4,6},{5,7},{6,4},{7,5},{8,10},{9,11},{10,... | collective-permute-start | bytes 1572872 | tf_op jit(solution)/shard_map/ppermute | solution.py:68
  57.4 8.7 %copy-start.4 = (f32[2,32,2048]{2,1,0:T(8,128)S(1)}, f32[2,32,2048]{2,1,0:T(8,128)}, u32[]{:S(2)}) copy-start(f32[2,32,2048]{2,1,0:T(8,128)} %get-tuple-element.37.rest_0_) | copy-start | bytes 1572868
  57.4 25.1 %collective-permute-start.19 = (bf16[2,128,1024]{2,1,0:T(8,128)(2,1)S(1)}, bf16[2,128,1024]{2,1,0:T(8,128)(2,1)S(1)}, u32[]{:S(2)}, u32[]{:S(2)}) collective-permute-start(bf16[2,128,1024]{2,1,0:T(8,128)(2,1)S(1)} %pad_maximum_fusion.3.inverse_ref.kinetic_ref), channel_id=1, source_target_pairs={{0,16},{16,0},{1,17},{17,1},{2,18},{18,2},{3,19},{19,3},{4,20},{20... | collective-permute-start | bytes 1572872 | tf_op jit(solution)/shard_map/ppermute | solution.py:68
  72.3 20.0 %collective-permute-start.15 = (f32[2,64,2048]{2,1,0:T(8,128)}, f32[2,64,2048]{2,1,0:T(8,128)}, u32[]{:S(2)}, u32[]{:S(2)}) collective-permute-start(f32[2,64,2048]{2,1,0:T(8,128)} %get-tuple-element.51.rest_2_), channel_id=1, source_target_pairs={{0,1},{1,0},{2,3},{3,2},{4,5},{5,4},{6,7},{7,6},{8,9},{9,8},{10,11... | collective-permute-start | bytes 3145736 | tf_op jit(solution)/shard_map/ppermute | solution.py:68
  90.6 30.7 %collective-permute-start.20 = (f32[2,64,2048]{2,1,0:T(8,128)}, f32[2,64,2048]{2,1,0:T(8,128)S(1)}, u32[]{:S(2)}, u32[]{:S(2)}) collective-permute-start(f32[2,64,2048]{2,1,0:T(8,128)} %get-tuple-element.59), channel_id=1, source_target_pairs={{0,1},{1,0},{2,3},{3,2},{4,5},{5,4},{6,7},{7,6},{8,9},{9,8},{10,11... | collective-permute-start | bytes 3145736 | tf_op jit(solution)/shard_map/ppermute | solution.py:68
  90.7 14.9 %collective-permute-start.11 = (f32[2,32,2048]{2,1,0:T(8,128)}, f32[2,32,2048]{2,1,0:T(8,128)S(1)}, u32[]{:S(2)}, u32[]{:S(2)}) collective-permute-start(f32[2,32,2048]{2,1,0:T(8,128)} %get-tuple-element.45.rest_1_), channel_id=1, source_target_pairs={{0,2},{1,3},{2,0},{3,1},{4,6},{5,7},{6,4},{7,5},{8,10},{9,11},{10,... | collective-permute-start | bytes 1572872 | tf_op jit(solution)/shard_map/ppermute | solution.py:68
  94.8 33.5 %collective-permute-start.16 = (f32[2,32,2048]{2,1,0:T(8,128)}, f32[2,32,2048]{2,1,0:T(8,128)S(1)}, u32[]{:S(2)}, u32[]{:S(2)}) collective-permute-start(f32[2,32,2048]{2,1,0:T(8,128)} %get-tuple-element.53), channel_id=1, source_target_pairs={{0,2},{1,3},{2,0},{3,1},{4,6},{5,7},{6,4},{7,5},{8,10},{9,11},{10,... | collective-permute-start | bytes 1572872 | tf_op jit(solution)/shard_map/ppermute | solution.py:68
  95.3 13.1 %collective-permute-start.7 = (f32[2,16,2048]{2,1,0:T(8,128)S(1)}, f32[2,16,2048]{2,1,0:T(8,128)S(1)}, u32[]{:S(2)}, u32[]{:S(2)}) collective-permute-start(f32[2,16,2048]{2,1,0:T(8,128)S(1)} %copy-done.6), channel_id=1, source_target_pairs={{0,4},{1,5},{2,6},{3,7},{4,0},{5,1},{6,2},{7,3},{8,12},{9,13},{10,... | collective-permute-start | bytes 786440 | tf_op jit(solution)/shard_map/ppermute | solution.py:68
  108.4 10.4 %collective-permute-start.12 = (f32[2,16,2048]{2,1,0:T(8,128)}, f32[2,16,2048]{2,1,0:T(8,128)S(1)}, u32[]{:S(2)}, u32[]{:S(2)}) collective-permute-start(f32[2,16,2048]{2,1,0:T(8,128)} %get-tuple-element.47), channel_id=1, source_target_pairs={{0,4},{1,5},{2,6},{3,7},{4,0},{5,1},{6,2},{7,3},{8,12},{9,13},{10,... | collective-permute-start | bytes 786440 | tf_op jit(solution)/shard_map/ppermute | solution.py:68
  110.9 15.4 %copy-start.21 = (f32[2,8,2048]{2,1,0:T(8,128)S(1)}, f32[2,8,2048]{2,1,0:T(8,128)}, u32[]{:S(2)}) copy-start(f32[2,8,2048]{2,1,0:T(8,128)} %get-tuple-element.40) | copy-start | bytes 393220
  110.9 15.4 %collective-permute-start.8 = (f32[2,8,2048]{2,1,0:T(8,128)}, f32[2,8,2048]{2,1,0:T(8,128)S(1)}, u32[]{:S(2)}, u32[]{:S(2)}) collective-permute-start(f32[2,8,2048]{2,1,0:T(8,128)} %get-tuple-element.41), channel_id=1, source_target_pairs={{0,12},{1,13},{2,14},{3,15},{4,8},{5,9},{6,10},{7,11},{8,4},{9,5},... | collective-permute-start | bytes 393224 | tf_op jit(solution)/shard_map/ppermute | solution.py:68
  121.3 7.0 %copy-start.22 = (f32[2,8,2048]{2,1,0:T(8,128)S(1)}, f32[2,8,2048]{2,1,0:T(8,128)}, u32[]{:S(2)}) copy-start(f32[2,8,2048]{2,1,0:T(8,128)} %get-tuple-element.48) | copy-start | bytes 393220
  121.3 7.0 %collective-permute-start.13 = (f32[2,8,2048]{2,1,0:T(8,128)}, f32[2,8,2048]{2,1,0:T(8,128)S(1)}, u32[]{:S(2)}, u32[]{:S(2)}) collective-permute-start(f32[2,8,2048]{2,1,0:T(8,128)} %get-tuple-element.49), channel_id=1, source_target_pairs={{0,12},{1,13},{2,14},{3,15},{4,8},{5,9},{6,10},{7,11},{8,4},{9,5},... | collective-permute-start | bytes 393224 | tf_op jit(solution)/shard_map/ppermute | solution.py:68
  124.9 17.1 %collective-permute-start.21 = (f32[2,32,2048]{2,1,0:T(8,128)}, f32[2,32,2048]{2,1,0:T(8,128)S(1)}, u32[]{:S(2)}, u32[]{:S(2)}) collective-permute-start(f32[2,32,2048]{2,1,0:T(8,128)} %get-tuple-element.61), channel_id=1, source_target_pairs={{0,2},{1,3},{2,0},{3,1},{4,6},{5,7},{6,4},{7,5},{8,10},{9,11},{10,... | collective-permute-start | bytes 1572872 | tf_op jit(solution)/shard_map/ppermute | solution.py:68
  131.1 6.6 %collective-permute-start.17 = (f32[2,16,2048]{2,1,0:T(8,128)}, f32[2,16,2048]{2,1,0:T(8,128)S(1)}, u32[]{:S(2)}, u32[]{:S(2)}) collective-permute-start(f32[2,16,2048]{2,1,0:T(8,128)} %get-tuple-element.55), channel_id=1, source_target_pairs={{0,4},{1,5},{2,6},{3,7},{4,0},{5,1},{6,2},{7,3},{8,12},{9,13},{10,... | collective-permute-start | bytes 786440 | tf_op jit(solution)/shard_map/ppermute | solution.py:68
  140.1 7.0 %collective-permute-start.18 = (f32[2,8,2048]{2,1,0:T(8,128)}, f32[2,8,2048]{2,1,0:T(8,128)S(1)}, u32[]{:S(2)}, u32[]{:S(2)}) collective-permute-start(f32[2,8,2048]{2,1,0:T(8,128)} %get-tuple-element.57), channel_id=1, source_target_pairs={{0,12},{1,13},{2,14},{3,15},{4,8},{5,9},{6,10},{7,11},{8,4},{9,5},... | collective-permute-start | bytes 393224 | tf_op jit(solution)/shard_map/ppermute | solution.py:68
  144.9 7.0 %collective-permute-start.22 = (f32[2,16,2048]{2,1,0:T(8,128)}, f32[2,16,2048]{2,1,0:T(8,128)S(1)}, u32[]{:S(2)}, u32[]{:S(2)}) collective-permute-start(f32[2,16,2048]{2,1,0:T(8,128)} %get-tuple-element.63), channel_id=1, source_target_pairs={{0,4},{1,5},{2,6},{3,7},{4,0},{5,1},{6,2},{7,3},{8,12},{9,13},{10,... | collective-permute-start | bytes 786440 | tf_op jit(solution)/shard_map/ppermute | solution.py:68
  154.3 7.0 %collective-permute-start.23 = (f32[2,8,2048]{2,1,0:T(8,128)}, f32[2,8,2048]{2,1,0:T(8,128)S(1)}, u32[]{:S(2)}, u32[]{:S(2)}) collective-permute-start(f32[2,8,2048]{2,1,0:T(8,128)} %get-tuple-element.65), channel_id=1, source_target_pairs={{0,12},{1,13},{2,14},{3,15},{4,8},{5,9},{6,10},{7,11},{8,4},{9,5},... | collective-permute-start | bytes 393224 | tf_op jit(solution)/shard_map/ppermute | solution.py:68
  (15 other events, 21.5 us)

commit v3 on v2

v3 whole, which is shorter than its diff:
```python
import functools

import jax
import jax.numpy as jnp
from jax import lax
from jax.experimental import pallas as pl
from jax.experimental.pallas import tpu as pltpu
from jax.sharding import PartitionSpec as P

PIECES = 4


def product(left, right):
    return jnp.einsum("woe,wev->wov", left, right, preferred_element_type=jnp.float32)


def gradient_terms(log_grad, kin_part, weights):
    kin_grad = -0.5 * kin_part
    weighted = jnp.sum(weights[:, None, None] * log_grad + kin_grad, axis=0)
    return (weighted, jnp.sum(log_grad, axis=0))


def general_body(inverse_rows, kinetic_rows, virt_values, virt_laplacians, local_energy):
    walk_count = lax.axis_size("walk")
    walker_count = walk_count * local_energy.shape[0]
    energy_sum = lax.psum(jnp.sum(local_energy), "walk")
    average = energy_sum / walker_count
    weights = 2.0 * (local_energy - average)
    inverse_all, kinetic_all = (
        lax.all_gather(inverse_rows, "virt", axis=2, tiled=True),
        lax.all_gather(kinetic_rows, "virt", axis=2, tiled=True),
    )
    log_grad = product(inverse_all, virt_values)
    kin_part = product(inverse_all, virt_laplacians) - product(kinetic_all, virt_values)
    weighted, log_sum = gradient_terms(log_grad, kin_part, weights)
    summed = (
        lax.psum_scatter(weighted, "walk", scatter_dimension=0, tiled=True),
        lax.psum_scatter(log_sum, "walk", scatter_dimension=0, tiled=True),
    )
    gradient_part, log_part = (summed[0], summed[1])
    return (gradient_part / walker_count, log_part / walker_count)


SPAN = 248.0
EXTRA = 128
TINY = 1e-30
MIB = 1024 * 1024


def stage_masks(count):
    bits = count.bit_length() - 1
    masks = [1 << bit for bit in range(bits)]
    if bits >= 2:
        masks[-1] = 3 << (bits - 2)
    return masks


def place_weights(masks):
    bits = len(masks)
    weights = [0] * bits
    for place in range(1 << bits):
        difference = 0
        for stage, mask in enumerate(masks):
            if place >> (bits - 1 - stage) & 1:
                difference ^= mask
        if difference & (difference - 1) == 0 and difference:
            weights[difference.bit_length() - 1] = place
    return weights


def swap(array, axis, mask):
    pairs = [(source, source ^ mask) for source in range(lax.axis_size(axis))]
    return lax.ppermute(array, axis, pairs)


def encode(rows):
    magnitude = jnp.abs(rows)
    largest = jnp.maximum(jnp.max(magnitude, axis=-1, keepdims=True), TINY)
    scale = (largest * (1.0 + 2.0**-7)).astype(jnp.bfloat16)
    factor = SPAN / scale.astype(jnp.float32)
    code = jnp.exp2(magnitude * factor - SPAN / 2)
    code = jnp.where(rows < 0, -code, code).astype(jnp.bfloat16)
    return code, jnp.broadcast_to(scale, (rows.shape[0], EXTRA))


def decode(coded):
    width = coded.shape[1] - EXTRA
    code = coded[:, :width].astype(jnp.float32)
    scale = coded[:, width : width + 1].astype(jnp.float32)
    magnitude = (jnp.log2(jnp.abs(code)) + SPAN / 2) * (scale / SPAN)
    return jnp.where(code < 0, -magnitude, magnitude)


def store_coded(send_ref, blocks):
    width = send_ref.shape[1] - EXTRA
    for pair in range(len(blocks) // 2):
        code, scale = encode(jnp.concatenate(blocks[2 * pair : 2 * pair + 2], axis=0))
        target = slice(16 * pair, 16 * pair + 16)
        send_ref[target, :width] = code
        send_ref[target, width:] = scale


def add_came(keep_ref, came_ref):
    arrays, height, _ = keep_ref.shape
    per = height // 8
    sums = []
    for pair in range(arrays * per // 2):
        both = decode(came_ref[16 * pair : 16 * pair + 16, :])
        for part in range(2):
            array, block = divmod(2 * pair + part, per)
            sums.append(keep_ref[array, 8 * block : 8 * block + 8, :] + both[8 * part : 8 * part + 8])
    return [sums[array * per : (array + 1) * per] for array in range(arrays)]


def limit(mib):
    return pltpu.CompilerParams(vmem_limit_bytes=mib * MIB)


WHOLE = pl.BlockSpec(memory_space=pltpu.VMEM)
SCALAR = pl.BlockSpec(memory_space=pltpu.SMEM)
ANYWHERE = pl.BlockSpec(memory_space=pl.ANY)


def near_kernel(tile, virt_ref, mine_ref, values_ref, laps_ref, *rest):
    out_ref = rest[-1]
    _, height, depth = mine_ref.shape
    f32 = jnp.float32
    electrons = pl.ds(pl.multiple_of(virt_ref[0] * depth, depth), depth)

    @pl.loop(0, out_ref.shape[2] // tile)
    def _(index):
        columns = pl.ds(pl.multiple_of(index * tile, tile), tile)
        both = jnp.dot(mine_ref[...].reshape(2 * height, depth), values_ref[electrons, columns], preferred_element_type=f32)
        laps = jnp.dot(mine_ref[0], laps_ref[electrons, columns], preferred_element_type=f32)
        out_ref[0, :, columns] = 0.5 * (both[height:] - laps)
        out_ref[1, :, columns] = both[:height]


def near_product(virt, mine, values, laplacians, tile, after):
    _, height, depth = mine.shape
    width = values.shape[1]
    return pl.pallas_call(
        functools.partial(near_kernel, tile),
        out_shape=jax.ShapeDtypeStruct((2, height, width), jnp.float32),
        in_specs=[SCALAR, WHOLE, WHOLE, WHOLE] + [ANYWHERE] * len(after),
        out_specs=WHOLE,
        compiler_params=limit(20),
        cost_estimate=pl.CostEstimate(flops=6 * height * depth * width, bytes_accessed=0, transcendentals=0),
        name="near_product",
    )(virt, mine, values, laplacians, *after)


def far_kernel(weights, count, tile, virt_ref, me_ref, scale_ref, far_ref, near_ref, values_ref, laps_ref, *rest):
    send_ref, keep_ref, place_ref = rest[-3:]
    _, height, depth = far_ref.shape
    width = near_ref.shape[2]
    rows = height // count
    half = height // 2
    f32 = jnp.float32
    electrons = pl.ds(pl.multiple_of((1 - virt_ref[0]) * depth, depth), depth)

    @pl.loop(0, width // tile)
    def _(index):
        columns = pl.ds(pl.multiple_of(index * tile, tile), tile)
        both = jnp.dot(far_ref[...].reshape(2 * height, depth), values_ref[electrons, columns], preferred_element_type=f32)
        laps = jnp.dot(far_ref[0], laps_ref[electrons, columns], preferred_element_type=f32)
        log = both[:height] + near_ref[1, :, columns]
        weighted = scale_ref[0] * log + (0.5 * (both[height:] - laps) + near_ref[0, :, columns])
        for dest in range(count):
            difference = dest ^ me_ref[0]
            place = 0
            for bit, weight in enumerate(weights):
                place = place ^ (((difference >> bit) & 1) * weight)
            target = pl.ds(pl.multiple_of(place * rows, rows), rows)
            source = slice(dest * rows, (dest + 1) * rows)
            place_ref[0, target, columns] = weighted[source]
            place_ref[1, target, columns] = log[source]

    keep_ref[...] = place_ref[:, :half]
    store_coded(send_ref, [place_ref[array, row : row + 8, :] for array in range(2) for row in range(half, height, 8)])


def far_product(virt, me, scale, theirs, near, values, laplacians, tile, masks, after):
    _, height, depth = theirs.shape
    width = values.shape[1]
    half = height // 2
    return pl.pallas_call(
        functools.partial(far_kernel, place_weights(masks), 1 << len(masks), tile),
        out_shape=(
            jax.ShapeDtypeStruct((2 * half, width + EXTRA), jnp.bfloat16),
            jax.ShapeDtypeStruct((2, half, width), jnp.float32),
        ),
        in_specs=[SCALAR, SCALAR, SCALAR, WHOLE, WHOLE, WHOLE, WHOLE] + [ANYWHERE] * len(after),
        out_specs=(WHOLE, WHOLE),
        scratch_shapes=[pltpu.VMEM((2, height, width), jnp.float32)],
        compiler_params=limit(20),
        cost_estimate=pl.CostEstimate(flops=6 * height * depth * width, bytes_accessed=0, transcendentals=0),
        name="far_product",
    )(virt, me, scale, theirs, near, values, laplacians, *after)


def halve_kernel(keep_ref, came_ref, send_ref, kept_ref):
    sums = add_came(keep_ref, came_ref)
    kept = len(sums[0]) // 2
    for array, blocks in enumerate(sums):
        for index, block in enumerate(blocks[:kept]):
            kept_ref[array, 8 * index : 8 * index + 8, :] = block
    store_coded(send_ref, [block for blocks in sums for block in blocks[kept:]])


def halve(keep, came):
    _, height, width = keep.shape
    return pl.pallas_call(
        halve_kernel,
        out_shape=(
            jax.ShapeDtypeStruct((height, width + EXTRA), jnp.bfloat16),
            jax.ShapeDtypeStruct((2, height // 2, width), jnp.float32),
        ),
        in_specs=[WHOLE, WHOLE],
        out_specs=(WHOLE, WHOLE),
        compiler_params=limit(8),
        cost_estimate=pl.CostEstimate(flops=keep.size, bytes_accessed=0, transcendentals=0),
        name="halve",
    )(keep, came)


def finish_kernel(count, *refs):
    gradient_ref, log_ref = refs[-2:]
    pieces = (len(refs) - 2) // 2
    row = 0
    for piece in range(pieces):
        gradient, log = add_came(refs[2 * piece], refs[2 * piece + 1])
        for block in range(len(log)):
            gradient_ref[row : row + 8, :] = gradient[block] / count
            log_ref[row : row + 8, :] = log[block] / count
            row += 8


def finish(parts, count):
    _, rows, width = parts[0][0].shape
    out = jax.ShapeDtypeStruct((rows * len(parts), width), jnp.float32)
    return pl.pallas_call(
        functools.partial(finish_kernel, count),
        out_shape=(out, out),
        in_specs=[WHOLE, WHOLE] * len(parts),
        out_specs=(WHOLE, WHOLE),
        compiler_params=limit(8),
        cost_estimate=pl.CostEstimate(flops=out.size, bytes_accessed=0, transcendentals=0),
        name="finish",
    )(*[array for part in parts for array in part])


def pieced_body(pieces, tile, inverse_rows, kinetic_rows, virt_values, virt_laplacians, local_energy):
    count = lax.axis_size("walk")
    masks = stage_masks(count)
    stages = len(masks)
    me = lax.axis_index("walk").astype(jnp.int32).reshape(1)
    virt = lax.axis_index("virt").astype(jnp.int32).reshape(1)
    occupied, depth = inverse_rows.shape[1:]
    by_dest = (count, occupied // count, depth)
    inverse, kinetic = inverse_rows.reshape(by_dest), kinetic_rows.reshape(by_dest)
    values = pltpu.with_memory_space_constraint(virt_values[0], pltpu.VMEM)
    laplacians = pltpu.with_memory_space_constraint(virt_laplacians[0], pltpu.VMEM)
    rows = occupied // (count * pieces)

    mine, theirs = [], []
    for piece in range(pieces):
        part = slice(piece * rows, (piece + 1) * rows)
        taken = [array[:, part].reshape(count * rows, depth) for array in (inverse, kinetic)]
        mine.append(jnp.stack(taken))
        theirs.append(swap(mine[piece], "virt", 1))

    energy_sum = jnp.broadcast_to(local_energy, (1, 128))
    near = []
    for piece in range(pieces):
        after = [energy_sum] if piece else []
        near.append(near_product(virt, mine[piece], values, laplacians, tile, after))
        if piece < stages:
            energy_sum = energy_sum + swap(energy_sum, "walk", masks[piece])
    for mask in masks[pieces:]:
        energy_sum = energy_sum + swap(energy_sum, "walk", mask)
    average = energy_sum[0, 0] / count
    scale = 2.0 * (local_energy - average)

    send, keep, parts = {}, {}, {}
    for turn in range(pieces + stages + 1):
        after = [send[other] for other in sorted(send)]
        if turn < pieces:
            send[turn], keep[turn] = far_product(
                virt, me, scale, theirs[turn], near[turn], values, laplacians, tile, masks, after
            )
        for piece in range(turn - 1, max(turn - 1 - stages, -1), -1):
            if piece >= pieces:
                continue
            stage = turn - 1 - piece
            came = swap(send.pop(piece), "walk", masks[stage])
            if stage + 1 < stages:
                send[piece], keep[piece] = halve(keep[piece], came)
            else:
                parts[piece] = (keep[piece], came)
    return finish([parts[piece] for piece in range(pieces)], count)


def solution(mesh):
    placed = (
        P("walk", None, "virt"),
        P("walk", None, "virt"),
        P("walk", None, "virt"),
        P("walk", None, "virt"),
        P("walk"),
    )

    def body(inverse_rows, kinetic_rows, virt_values, virt_laplacians, local_energy):
        count = mesh.shape["walk"]
        walkers, occupied, depth = inverse_rows.shape
        width = virt_values.shape[2]
        tile = 512
        fits = (
            walkers == 1
            and mesh.shape["virt"] == 2
            and count >= 4
            and count & (count - 1) == 0
            and occupied % (count * PIECES * 8) == 0
            and depth % 256 == 0
            and width % tile == 0
        )
        form = functools.partial(pieced_body, PIECES, tile) if fits else general_body
        return form(inverse_rows, kinetic_rows, virt_values, virt_laplacians, local_energy)

    return jax.shard_map(
        body,
        mesh=mesh,
        in_specs=placed,
        out_specs=(P("walk", "virt"), P("walk", "virt")),
        check_vma=False,
    )
```

time: 164 us -> 99.9 us (0.61)
  Pallas kernels: 70.4 us -> 30.6 us
  waiting for transfers between devices: 52 us -> 26.9 us
  local copies, waits for them, and re-layouts: 13.1 us -> 16 us
  other arithmetic: 3.53 us -> 1.04 us
    pallas_call x20 -> x21, Pallas kernels: 70.4 us -> 30.6 us  [the longest x4 14.4 us: far_product(): pl.pallas_call(functools.partial(far_kernel, place_weights(masks), 1 << l...]
    ppermute x24, waiting for transfers between devices: 52 us -> 26.9 us  [swap(): return lax.ppermute(array, axis, pairs)]
    unnamed x46 -> x10, local copies, waits for them, and re-layouts: 10.5 us -> 13.5 us
    add x8 -> x4, other arithmetic: 1.88 us -> 0.01 us  [pieced_body(): energy_sum = energy_sum + swap(energy_sum, 'walk', masks[piece])]
  transfers between devices with their start and end apart: 24 -> 24, of which waited for: 12 -> 10; matrix products, arithmetic and copies ran while one was open for 1% -> 3% of each run, Pallas kernels for 39% -> 30%
where the time goes in v3:
time: 99.9 us; the launch traced here: 99.4 us
  Pallas kernels  30.6 us (31%)
  waiting for transfers between devices  26.9 us (27%)
  starting transfers between devices  23.4 us (23%)
  local copies, waits for them, and re-layouts  16 us (16%)
  between operations  1.61 us (2%)
  other arithmetic  1.04 us (1%)
    ppermute x24, waiting for transfers between devices, swap(): return lax.ppermute(array, axis, pairs)  26.9 us
    ppermute x24, starting transfers between devices, swap(): return lax.ppermute(array, axis, pairs)  23.4 us
    pallas_call x4, Pallas kernels, far_product(): pl.pallas_call(functools.partial(far_kernel, place_weights(masks), 1 << l...  14.4 us
    unnamed x10, local copies, waits for them, and re-layouts  13.5 us
    pallas_call x4, Pallas kernels, near_product(): pl.pallas_call(functools.partial(near_kernel, tile), out_shape=jax.ShapeD...  10.4 us
    pallas_call x12, Pallas kernels, halve(): pl.pallas_call(halve_kernel, out_shape=(jax.ShapeDtypeStruct((height, wid...  4.69 us
    another operation x1, local copies, waits for them, and re-layouts, pieced_body(): mine.append(jnp.stack(taken))  2.43 us
  transfers between devices with their start and end apart: 24, of which 10 were waited for; matrix products, arithmetic and copies ran while one was open for 3% of the time, Pallas kernels for 30%

profile of v3, /device:TPU:0, one launch (start us, length us, event | category | flops | bytes accessed | tf_op | source)
XLA Modules:
  0.0 99.4 jit_solution(9141835244355606471)
XLA Ops:
  1.8 2.4 %slice_bitcast_fusion = (bf16[1,128,1024]{2,1,0:T(8,128)(2,1)S(1)}, bf16[1,128,1024]{2,1,0:T(8,128)(2,1)S(1)}, bf16[1,128,1024]{2,1,0:T(8,128)(2,1)S(1)}, bf16[1...) fusion(bf16[16,32,1024]{2,1,0:T(8,128)(2,1)} %bitcast.44, ...), kind=kLoop, calls=%fused_computation.4 | loop fusion | bytes 4194304 | tf_op jit(solution)/shard_map/stack;reshape | solution.py:270
  4.3 2.6 %collective-permute-start.4 = (bf16[2,128,1024]{2,1,0:T(8,128)(2,1)S(1)}, bf16[2,128,1024]{2,1,0:T(8,128)(2,1)}, u32[]{:S(2)}, u32[]{:S(2)}) collective-permute-start(bf16[2,128,1024]{2,1,0:T(8,128)(2,1)S(1)} %pad_maximum_fusion.mine_ref), channel_id=1, source_target_pairs={{0,16},{16,0},{1,17},{17,1},{2,18},{18,2},{3,19},{19,3},{4,20},{20... | collective-permute-start | bytes 1572872 | tf_op jit(solution)/shard_map/ppermute | solution.py:73
  6.9 1.5 %collective-permute-start.1 = (f32[1,128]{1,0:T(1,128)S(1)}, f32[1,128]{1,0:T(1,128)S(1)}, u32[]{:S(2)}, u32[]{:S(2)}) collective-permute-start(f32[1,128]{1,0:T(1,128)S(1)} %broadcast_add_fusion.rest_0_), channel_id=1, source_target_pairs={{0,2},{1,3},{2,0},{3,1},{4,6},{5,7},{6,4},{7,5},{8,10},{9,11},{10,... | collective-permute-start | bytes 1544 | tf_op jit(solution)/shard_map/ppermute | solution.py:73
  10.4 1.6 %collective-permute-start.2 = (f32[1,128]{1,0:T(1,128)S(1)}, f32[1,128]{1,0:T(1,128)S(1)}, u32[]{:S(2)}, u32[]{:S(2)}) collective-permute-start(f32[1,128]{1,0:T(1,128)S(1)} %fusion.rest_0_), channel_id=1, source_target_pairs={{0,4},{1,5},{2,6},{3,7},{4,0},{5,1},{6,2},{7,3},{8,12},{9,13},{10,... | collective-permute-start | bytes 1544 | tf_op jit(solution)/shard_map/ppermute | solution.py:73
  13.0 1.0 collective-permute-done.2
  14.0 3.6 %collective-permute-start.3 = (f32[1,128]{1,0:T(1,128)S(1)}, f32[1,128]{1,0:T(1,128)S(1)}, u32[]{:S(2)}, u32[]{:S(2)}) collective-permute-start(f32[1,128]{1,0:T(1,128)S(1)} %add.14.rest_0_), channel_id=1, source_target_pairs={{0,12},{1,13},{2,14},{3,15},{4,8},{5,9},{6,10},{7,11},{8,4},{9,5},... | collective-permute-start | bytes 1544 | tf_op jit(solution)/shard_map/ppermute | solution.py:73
  17.6 3.4 %copy-done = bf16[1,2048,2048]{2,1,0:T(8,128)(2,1)S(1)} copy-done((bf16[1,2048,2048]{2,1,0:T(8,128)(2,1)S(1)}, bf16[1,2048,2048]{2,1,0:T(8,128)(2,1)}, u32[]{:S(2)}) %copy-start) | copy-done | bytes 8388632
  21.0 3.4 %copy-done.2 = bf16[1,2048,2048]{2,1,0:T(8,128)(2,1)S(1)} copy-done((bf16[1,2048,2048]{2,1,0:T(8,128)(2,1)S(1)}, bf16[1,2048,2048]{2,1,0:T(8,128)(2,1)}, u32[]{:S(2)}) %copy-start.2) | copy-done | bytes 8388632
  24.3 2.3 %near_product.4.near_ref = f32[2,128,2048]{2,1,0:T(8,128)S(1)} custom-call(s32[1]{0:T(128)} %bitcast.virt_ref, bf16[2,128,1024]{2,1,0:T(8,128)(2,1)S(1)} %pad_maximum_fusion.mine_ref, bf16[2048,2048]{1,0:T(8,128)(2,1)S(1)} %bitcast.28, bf16[2048,2048]{1,0:T(8,128)(2,1)S(1)} %bitcast.36), custom_call_target="tpu_custom_call" | custom-call | flops 1610612736 | tf_op jit(solution)/shard_map/near_product/pallas_call | solution.py:142
  26.8 3.4 %copy-done.1 = bf16[1,2048,2048]{2,1,0:T(8,128)(2,1)S(1)} copy-done((bf16[1,2048,2048]{2,1,0:T(8,128)(2,1)S(1)}, bf16[1,2048,2048]{2,1,0:T(8,128)(2,1)}, u32[]{:S(2)}) %copy-start.1) | copy-done | bytes 8388632
  30.2 3.4 %copy-done.3 = bf16[1,2048,2048]{2,1,0:T(8,128)(2,1)S(1)} copy-done((bf16[1,2048,2048]{2,1,0:T(8,128)(2,1)S(1)}, bf16[1,2048,2048]{2,1,0:T(8,128)(2,1)}, u32[]{:S(2)}) %copy-start.3) | copy-done | bytes 8388632
  33.5 3.8 %far_product.4 = (bf16[128,2176]{1,0:T(8,128)(2,1)S(1)}, f32[2,64,2048]{2,1,0:T(8,128)S(1)}) custom-call(s32[1]{0:T(128)} %bitcast.virt_ref, s32[1]{0:T(128)} %bitcast.1.me_ref, f32[1]{0:T(128)S(6)} %mul.3.scale_ref, bf16[2,128,1024]{2,1,0:T(8,128)(2,1)} %collective-permute-done.4.far_ref, f32[2,128,2048]{2,1,0:T(8,128)S(1)} %near_product.4.near_ref, ...), custom_call_target="tpu_custom_call" | custom-call | flops 1610612736 | tf_op jit(solution)/shard_map/far_product/pallas_call | solution.py:187
  37.5 3.4 %near_product.5.near_ref = f32[2,128,2048]{2,1,0:T(8,128)S(1)} custom-call(s32[1]{0:T(128)} %bitcast.virt_ref, bf16[2,128,1024]{2,1,0:T(8,128)(2,1)} %pad_maximum_fusion.1.mine_ref, bf16[2048,2048]{1,0:T(8,128)(2,1)S(1)} %bitcast.30, bf16[2048,2048]{1,0:T(8,128)(2,1)S(1)} %bitcast.38, f32[1,128]{1,0:T(1,128)S(1)} %broadcast_add_fusion.rest_0_), custom_call_target="tpu_custom_call" | custom-call | flops 1610612736 | tf_op jit(solution)/shard_map/near_product/pallas_call | solution.py:142
  40.9 3.9 %far_product.5 = (bf16[128,2176]{1,0:T(8,128)(2,1)S(1)}, f32[2,64,2048]{2,1,0:T(8,128)S(1)}) custom-call(s32[1]{0:T(128)} %bitcast.virt_ref, s32[1]{0:T(128)} %bitcast.1.me_ref, f32[1]{0:T(128)S(6)} %mul.3.scale_ref, bf16[2,128,1024]{2,1,0:T(8,128)(2,1)} %collective-permute-done.9.far_ref, f32[2,128,2048]{2,1,0:T(8,128)S(1)} %near_product.5.near_ref, ...), custom_call_target="tpu_custom_call" | custom-call | flops 1610612736 | tf_op jit(solution)/shard_map/far_product/pallas_call | solution.py:187
  46.3 2.3 %near_product.6.near_ref = f32[2,128,2048]{2,1,0:T(8,128)S(1)} custom-call(s32[1]{0:T(128)} %bitcast.virt_ref, bf16[2,128,1024]{2,1,0:T(8,128)(2,1)S(1)} %pad_maximum_fusion.2.mine_ref, bf16[2048,2048]{1,0:T(8,128)(2,1)S(1)} %bitcast.32, bf16[2048,2048]{1,0:T(8,128)(2,1)S(1)} %bitcast.40, f32[1,128]{1,0:T(1,128)S(1)} %fusion.rest_0_), custom_call_target="tpu_custom_call" | custom-call | flops 1610612736 | tf_op jit(solution)/shard_map/near_product/pallas_call | solution.py:142
  49.3 1.2 %collective-permute-start.6 = (bf16[64,2176]{1,0:T(8,128)(2,1)S(1)}, bf16[64,2176]{1,0:T(8,128)(2,1)S(1)}, u32[]{:S(2)}, u32[]{:S(2)}) collective-permute-start(bf16[64,2176]{1,0:T(8,128)(2,1)S(1)} %get-tuple-element.37.rest_0_), channel_id=1, source_target_pairs={{0,2},{1,3},{2,0},{3,1},{4,6},{5,7},{6,4},{7,5},{8,10},{9,11},{10,... | collective-permute-start | bytes 835592 | tf_op jit(solution)/shard_map/ppermute | solution.py:73
  50.5 2.3 %near_product.7.near_ref = f32[2,128,2048]{2,1,0:T(8,128)S(1)} custom-call(s32[1]{0:T(128)} %bitcast.virt_ref, bf16[2,128,1024]{2,1,0:T(8,128)(2,1)S(1)} %pad_maximum_fusion.3.mine_ref, bf16[2048,2048]{1,0:T(8,128)(2,1)S(1)} %bitcast.33, bf16[2048,2048]{1,0:T(8,128)(2,1)S(1)} %bitcast.41, f32[1,128]{1,0:T(1,128)S(1)} %add.14.rest_0_), custom_call_target="tpu_custom_call" | custom-call | flops 1610612736 | tf_op jit(solution)/shard_map/near_product/pallas_call | solution.py:142
  52.8 3.9 %far_product.6 = (bf16[128,2176]{1,0:T(8,128)(2,1)S(1)}, f32[2,64,2048]{2,1,0:T(8,128)S(1)}) custom-call(s32[1]{0:T(128)} %bitcast.virt_ref, s32[1]{0:T(128)} %bitcast.1.me_ref, f32[1]{0:T(128)S(6)} %mul.3.scale_ref, bf16[2,128,1024]{2,1,0:T(8,128)(2,1)} %collective-permute-done.14.far_ref, f32[2,128,2048]{2,1,0:T(8,128)S(1)} %near_product.6.near_ref, ...), custom_call_target="tpu_custom_call" | custom-call | flops 1610612736 | tf_op jit(solution)/shard_map/far_product/pallas_call | solution.py:187
  58.0 1.3 %collective-permute-done.19.far_ref = bf16[2,128,1024]{2,1,0:T(8,128)(2,1)S(1)} collective-permute-done((bf16[2,128,1024]{2,1,0:T(8,128)(2,1)S(1)}, bf16[2,128,1024]{2,1,0:T(8,128)(2,1)S(1)}, u32[]{:S(2)}, u32[]{:S(2)}) %collective-permute-start.19) | collective-permute-done | bytes 524320 | tf_op jit(solution)/shard_map/ppermute | solution.py:73
  59.3 2.8 %far_product.7 = (bf16[128,2176]{1,0:T(8,128)(2,1)S(1)}, f32[2,64,2048]{2,1,0:T(8,128)S(1)}) custom-call(s32[1]{0:T(128)} %bitcast.virt_ref, s32[1]{0:T(128)} %bitcast.1.me_ref, f32[1]{0:T(128)S(6)} %mul.3.scale_ref, bf16[2,128,1024]{2,1,0:T(8,128)(2,1)S(1)} %collective-permute-done.19.far_ref, f32[2,128,2048]{2,1,0:T(8,128)S(1)} %near_product.7.near_ref, ...), custom_call_target="tpu_custom_call" | custom-call | flops 1610612736 | tf_op jit(solution)/shard_map/far_product/pallas_call | solution.py:187
  62.2 1.5 %collective-permute-start.11 = (bf16[64,2176]{1,0:T(8,128)(2,1)S(1)}, bf16[64,2176]{1,0:T(8,128)(2,1)S(1)}, u32[]{:S(2)}, u32[]{:S(2)}) collective-permute-start(bf16[64,2176]{1,0:T(8,128)(2,1)S(1)} %get-tuple-element.45.rest_1_), channel_id=1, source_target_pairs={{0,2},{1,3},{2,0},{3,1},{4,6},{5,7},{6,4},{7,5},{8,10},{9,11},{10,... | collective-permute-start | bytes 835592 | tf_op jit(solution)/shard_map/ppermute | solution.py:73
  65.6 1.5 %collective-permute-start.21 = (bf16[64,2176]{1,0:T(8,128)(2,1)S(1)}, bf16[64,2176]{1,0:T(8,128)(2,1)S(1)}, u32[]{:S(2)}, u32[]{:S(2)}) collective-permute-start(bf16[64,2176]{1,0:T(8,128)(2,1)S(1)} %get-tuple-element.61), channel_id=1, source_target_pairs={{0,2},{1,3},{2,0},{3,1},{4,6},{5,7},{6,4},{7,5},{8,10},{9,11},{10,... | collective-permute-start | bytes 835592 | tf_op jit(solution)/shard_map/ppermute | solution.py:73
  67.1 4.6 %collective-permute-done.11.came_ref = bf16[64,2176]{1,0:T(8,128)(2,1)S(1)} collective-permute-done((bf16[64,2176]{1,0:T(8,128)(2,1)S(1)}, bf16[64,2176]{1,0:T(8,128)(2,1)S(1)}, u32[]{:S(2)}, u32[]{:S(2)}) %collective-permute-start.11) | collective-permute-done | bytes 278560 | tf_op jit(solution)/shard_map/ppermute | solution.py:73
  72.2 5.5 %collective-permute-done.16.came_ref = bf16[64,2176]{1,0:T(8,128)(2,1)S(1)} collective-permute-done((bf16[64,2176]{1,0:T(8,128)(2,1)S(1)}, bf16[64,2176]{1,0:T(8,128)(2,1)S(1)}, u32[]{:S(2)}, u32[]{:S(2)}) %collective-permute-start.16) | collective-permute-done | bytes 278560 | tf_op jit(solution)/shard_map/ppermute | solution.py:73
  78.1 5.1 %collective-permute-done.21.came_ref = bf16[64,2176]{1,0:T(8,128)(2,1)S(1)} collective-permute-done((bf16[64,2176]{1,0:T(8,128)(2,1)S(1)}, bf16[64,2176]{1,0:T(8,128)(2,1)S(1)}, u32[]{:S(2)}, u32[]{:S(2)}) %collective-permute-start.21) | collective-permute-done | bytes 278560 | tf_op jit(solution)/shard_map/ppermute | solution.py:73
  83.9 0.9 collective-permute-start.8
  85.1 3.0 %collective-permute-start.13 = (bf16[16,2176]{1,0:T(8,128)(2,1)S(1)}, bf16[16,2176]{1,0:T(8,128)(2,1)S(1)}, u32[]{:S(2)}, u32[]{:S(2)}) collective-permute-start(bf16[16,2176]{1,0:T(8,128)(2,1)S(1)} %get-tuple-element.49), channel_id=1, source_target_pairs={{0,12},{1,13},{2,14},{3,15},{4,8},{5,9},{6,10},{7,11},{8,4},{9,5},... | collective-permute-start | bytes 208904 | tf_op jit(solution)/shard_map/ppermute | solution.py:73
  88.3 0.9 collective-permute-start.18
  89.3 2.6 %collective-permute-done.22.came_ref = bf16[32,2176]{1,0:T(8,128)(2,1)S(1)} collective-permute-done((bf16[32,2176]{1,0:T(8,128)(2,1)S(1)}, bf16[32,2176]{1,0:T(8,128)(2,1)S(1)}, u32[]{:S(2)}, u32[]{:S(2)}) %collective-permute-start.22) | collective-permute-done | bytes 139296 | tf_op jit(solution)/shard_map/ppermute | solution.py:73
  92.6 2.0 %collective-permute-done.18.refs_5_ = bf16[16,2176]{1,0:T(8,128)(2,1)S(1)} collective-permute-done((bf16[16,2176]{1,0:T(8,128)(2,1)S(1)}, bf16[16,2176]{1,0:T(8,128)(2,1)S(1)}, u32[]{:S(2)}, u32[]{:S(2)}) %collective-permute-start.18) | collective-permute-done | bytes 69664 | tf_op jit(solution)/shard_map/ppermute | solution.py:73
  94.6 3.8 %collective-permute-done.23.refs_7_ = bf16[16,2176]{1,0:T(8,128)(2,1)S(1)} collective-permute-done((bf16[16,2176]{1,0:T(8,128)(2,1)S(1)}, bf16[16,2176]{1,0:T(8,128)(2,1)S(1)}, u32[]{:S(2)}, u32[]{:S(2)}) %collective-permute-start.23) | collective-permute-done | bytes 69664 | tf_op jit(solution)/shard_map/ppermute | solution.py:73
  98.4 1.1 %finish.1 = (f32[32,2048]{1,0:T(8,128)}, f32[32,2048]{1,0:T(8,128)}) custom-call(f32[2,8,2048]{2,1,0:T(8,128)S(1)} %get-tuple-element.40.refs_0_, bf16[16,2176]{1,0:T(8,128)(2,1)S(1)} %collective-permute-done.8.refs_1_, f32[2,8,2048]{2,1,0:T(8,128)S(1)} %get-tuple-element.48.refs_2_, bf16[16,2176]{1,0:T(8,128)(2,1)S(1)} %collective-permute-done.13.refs_3_, ...), custom_call_target="tpu_custom_call" | custom-call | flops 65536 | tf_op jit(solution)/shard_map/finish/pallas_call | solution.py:242
  (57 shorter events, 11.6 us)
Async XLA Ops:
  1.3 5.6 %collective-permute-start = (f32[1,128]{1,0:T(1,128)S(1)}, f32[1,128]{1,0:T(1,128)S(1)}, u32[]{:S(2)}, u32[]{:S(2)}) collective-permute-start(f32[1,128]{1,0:T(1,128)S(1)} %broadcast_in_dim.2), channel_id=1, source_target_pairs={{0,1},{1,0},{2,3},{3,2},{4,5},{5,4},{6,7},{7,6},{8,9},{9,8},{10,11... | collective-permute-start | bytes 1544 | tf_op jit(solution)/shard_map/ppermute | solution.py:73
  4.3 22.5 %collective-permute-start.4 = (bf16[2,128,1024]{2,1,0:T(8,128)(2,1)S(1)}, bf16[2,128,1024]{2,1,0:T(8,128)(2,1)}, u32[]{:S(2)}, u32[]{:S(2)}) collective-permute-start(bf16[2,128,1024]{2,1,0:T(8,128)(2,1)S(1)} %pad_maximum_fusion.mine_ref), channel_id=1, source_target_pairs={{0,16},{16,0},{1,17},{17,1},{2,18},{18,2},{3,19},{19,3},{4,20},{20... | collective-permute-start | bytes 1572872 | tf_op jit(solution)/shard_map/ppermute | solution.py:73
  6.9 3.5 %collective-permute-start.1 = (f32[1,128]{1,0:T(1,128)S(1)}, f32[1,128]{1,0:T(1,128)S(1)}, u32[]{:S(2)}, u32[]{:S(2)}) collective-permute-start(f32[1,128]{1,0:T(1,128)S(1)} %broadcast_add_fusion.rest_0_), channel_id=1, source_target_pairs={{0,2},{1,3},{2,0},{3,1},{4,6},{5,7},{6,4},{7,5},{8,10},{9,11},{10,... | collective-permute-start | bytes 1544 | tf_op jit(solution)/shard_map/ppermute | solution.py:73
  9.3 31.6 %collective-permute-start.9 = (bf16[2,128,1024]{2,1,0:T(8,128)(2,1)}, bf16[2,128,1024]{2,1,0:T(8,128)(2,1)}, u32[]{:S(2)}, u32[]{:S(2)}) collective-permute-start(bf16[2,128,1024]{2,1,0:T(8,128)(2,1)} %pad_maximum_fusion.1.mine_ref), channel_id=1, source_target_pairs={{0,16},{16,0},{1,17},{17,1},{2,18},{18,2},{3,19},{19,3},{4,20},{20... | collective-permute-start | bytes 1572872 | tf_op jit(solution)/shard_map/ppermute | solution.py:73
  10.4 3.5 %collective-permute-start.2 = (f32[1,128]{1,0:T(1,128)S(1)}, f32[1,128]{1,0:T(1,128)S(1)}, u32[]{:S(2)}, u32[]{:S(2)}) collective-permute-start(f32[1,128]{1,0:T(1,128)S(1)} %fusion.rest_0_), channel_id=1, source_target_pairs={{0,4},{1,5},{2,6},{3,7},{4,0},{5,1},{6,2},{7,3},{8,12},{9,13},{10,... | collective-permute-start | bytes 1544 | tf_op jit(solution)/shard_map/ppermute | solution.py:73
  12.1 40.8 %collective-permute-start.14 = (bf16[2,128,1024]{2,1,0:T(8,128)(2,1)S(1)}, bf16[2,128,1024]{2,1,0:T(8,128)(2,1)}, u32[]{:S(2)}, u32[]{:S(2)}) collective-permute-start(bf16[2,128,1024]{2,1,0:T(8,128)(2,1)S(1)} %pad_maximum_fusion.2.mine_ref), channel_id=1, source_target_pairs={{0,16},{16,0},{1,17},{17,1},{2,18},{18,2},{3,19},{19,3},{4,20},{20... | collective-permute-start | bytes 1572872 | tf_op jit(solution)/shard_map/ppermute | solution.py:73
  14.0 12.7 %collective-permute-start.3 = (f32[1,128]{1,0:T(1,128)S(1)}, f32[1,128]{1,0:T(1,128)S(1)}, u32[]{:S(2)}, u32[]{:S(2)}) collective-permute-start(f32[1,128]{1,0:T(1,128)S(1)} %add.14.rest_0_), channel_id=1, source_target_pairs={{0,12},{1,13},{2,14},{3,15},{4,8},{5,9},{6,10},{7,11},{8,4},{9,5},... | collective-permute-start | bytes 1544 | tf_op jit(solution)/shard_map/ppermute | solution.py:73
  17.6 3.4 %copy-start = (bf16[1,2048,2048]{2,1,0:T(8,128)(2,1)S(1)}, bf16[1,2048,2048]{2,1,0:T(8,128)(2,1)}, u32[]{:S(2)}) copy-start(bf16[1,2048,2048]{2,1,0:T(8,128)(2,1)} %param.7) | copy-start | bytes 25165828
  21.0 3.4 %copy-start.2 = (bf16[1,2048,2048]{2,1,0:T(8,128)(2,1)S(1)}, bf16[1,2048,2048]{2,1,0:T(8,128)(2,1)}, u32[]{:S(2)}) copy-start(bf16[1,2048,2048]{2,1,0:T(8,128)(2,1)} %param.8) | copy-start | bytes 25165828
  26.8 3.4 %copy-start.1 = (bf16[1,2048,2048]{2,1,0:T(8,128)(2,1)S(1)}, bf16[1,2048,2048]{2,1,0:T(8,128)(2,1)}, u32[]{:S(2)}) copy-start(bf16[1,2048,2048]{2,1,0:T(8,128)(2,1)} %param.7) | copy-start | bytes 25165828
  30.2 3.4 %copy-start.3 = (bf16[1,2048,2048]{2,1,0:T(8,128)(2,1)S(1)}, bf16[1,2048,2048]{2,1,0:T(8,128)(2,1)}, u32[]{:S(2)}) copy-start(bf16[1,2048,2048]{2,1,0:T(8,128)(2,1)} %param.8) | copy-start | bytes 25165828
  37.4 11.3 %collective-permute-start.5 = (bf16[128,2176]{1,0:T(8,128)(2,1)S(1)}, bf16[128,2176]{1,0:T(8,128)(2,1)S(1)}, u32[]{:S(2)}, u32[]{:S(2)}) collective-permute-start(bf16[128,2176]{1,0:T(8,128)(2,1)S(1)} %get-tuple-element.35.rest_0_), channel_id=1, source_target_pairs={{0,1},{1,0},{2,3},{3,2},{4,5},{5,4},{6,7},{7,6},{8,9},{9,8},{10,11... | collective-permute-start | bytes 1671176 | tf_op jit(solution)/shard_map/ppermute | solution.py:73
  40.9 4.5 %copy-start.4 = (bf16[1,128,1024]{2,1,0:T(8,128)(2,1)S(1)}, bf16[1,128,1024]{2,1,0:T(8,128)(2,1)}, u32[]{:S(2)}) copy-start(bf16[1,128,1024]{2,1,0:T(8,128)(2,1)} %get-tuple-element.77) | copy-start | bytes 786436
  44.8 12.0 %collective-permute-start.10 = (bf16[128,2176]{1,0:T(8,128)(2,1)S(1)}, bf16[128,2176]{1,0:T(8,128)(2,1)S(1)}, u32[]{:S(2)}, u32[]{:S(2)}) collective-permute-start(bf16[128,2176]{1,0:T(8,128)(2,1)S(1)} %get-tuple-element.43.rest_1_), channel_id=1, source_target_pairs={{0,1},{1,0},{2,3},{3,2},{4,5},{5,4},{6,7},{7,6},{8,9},{9,8},{10,11... | collective-permute-start | bytes 1671176 | tf_op jit(solution)/shard_map/ppermute | solution.py:73
  45.4 13.9 %collective-permute-start.19 = (bf16[2,128,1024]{2,1,0:T(8,128)(2,1)S(1)}, bf16[2,128,1024]{2,1,0:T(8,128)(2,1)S(1)}, u32[]{:S(2)}, u32[]{:S(2)}) collective-permute-start(bf16[2,128,1024]{2,1,0:T(8,128)(2,1)S(1)} %pad_maximum_fusion.3.mine_ref), channel_id=1, source_target_pairs={{0,16},{16,0},{1,17},{17,1},{2,18},{18,2},{3,19},{19,3},{4,20},{20... | collective-permute-start | bytes 1572872 | tf_op jit(solution)/shard_map/ppermute | solution.py:73
  49.3 8.4 %collective-permute-start.6 = (bf16[64,2176]{1,0:T(8,128)(2,1)S(1)}, bf16[64,2176]{1,0:T(8,128)(2,1)S(1)}, u32[]{:S(2)}, u32[]{:S(2)}) collective-permute-start(bf16[64,2176]{1,0:T(8,128)(2,1)S(1)} %get-tuple-element.37.rest_0_), channel_id=1, source_target_pairs={{0,2},{1,3},{2,0},{3,1},{4,6},{5,7},{6,4},{7,5},{8,10},{9,11},{10,... | collective-permute-start | bytes 835592 | tf_op jit(solution)/shard_map/ppermute | solution.py:73
  56.7 7.1 %collective-permute-start.15 = (bf16[128,2176]{1,0:T(8,128)(2,1)S(1)}, bf16[128,2176]{1,0:T(8,128)(2,1)S(1)}, u32[]{:S(2)}, u32[]{:S(2)}) collective-permute-start(bf16[128,2176]{1,0:T(8,128)(2,1)S(1)} %get-tuple-element.51.rest_2_), channel_id=1, source_target_pairs={{0,1},{1,0},{2,3},{3,2},{4,5},{5,4},{6,7},{7,6},{8,9},{9,8},{10,11... | collective-permute-start | bytes 1671176 | tf_op jit(solution)/shard_map/ppermute | solution.py:73
  62.1 2.8 %collective-permute-start.20 = (bf16[128,2176]{1,0:T(8,128)(2,1)S(1)}, bf16[128,2176]{1,0:T(8,128)(2,1)S(1)}, u32[]{:S(2)}, u32[]{:S(2)}) collective-permute-start(bf16[128,2176]{1,0:T(8,128)(2,1)S(1)} %get-tuple-element.59), channel_id=1, source_target_pairs={{0,1},{1,0},{2,3},{3,2},{4,5},{5,4},{6,7},{7,6},{8,9},{9,8},{10,11... | collective-permute-start | bytes 1671176 | tf_op jit(solution)/shard_map/ppermute | solution.py:73
  62.2 9.5 %collective-permute-start.11 = (bf16[64,2176]{1,0:T(8,128)(2,1)S(1)}, bf16[64,2176]{1,0:T(8,128)(2,1)S(1)}, u32[]{:S(2)}, u32[]{:S(2)}) collective-permute-start(bf16[64,2176]{1,0:T(8,128)(2,1)S(1)} %get-tuple-element.45.rest_1_), channel_id=1, source_target_pairs={{0,2},{1,3},{2,0},{3,1},{4,6},{5,7},{6,4},{7,5},{8,10},{9,11},{10,... | collective-permute-start | bytes 835592 | tf_op jit(solution)/shard_map/ppermute | solution.py:73
  64.4 13.3 %collective-permute-start.16 = (bf16[64,2176]{1,0:T(8,128)(2,1)S(1)}, bf16[64,2176]{1,0:T(8,128)(2,1)S(1)}, u32[]{:S(2)}, u32[]{:S(2)}) collective-permute-start(bf16[64,2176]{1,0:T(8,128)(2,1)S(1)} %get-tuple-element.53), channel_id=1, source_target_pairs={{0,2},{1,3},{2,0},{3,1},{4,6},{5,7},{6,4},{7,5},{8,10},{9,11},{10,... | collective-permute-start | bytes 835592 | tf_op jit(solution)/shard_map/ppermute | solution.py:73
  65.6 17.6 %collective-permute-start.21 = (bf16[64,2176]{1,0:T(8,128)(2,1)S(1)}, bf16[64,2176]{1,0:T(8,128)(2,1)S(1)}, u32[]{:S(2)}, u32[]{:S(2)}) collective-permute-start(bf16[64,2176]{1,0:T(8,128)(2,1)S(1)} %get-tuple-element.61), channel_id=1, source_target_pairs={{0,2},{1,3},{2,0},{3,1},{4,6},{5,7},{6,4},{7,5},{8,10},{9,11},{10,... | collective-permute-start | bytes 835592 | tf_op jit(solution)/shard_map/ppermute | solution.py:73
  67.1 16.5 %collective-permute-start.7 = (bf16[32,2176]{1,0:T(8,128)(2,1)S(1)}, bf16[32,2176]{1,0:T(8,128)(2,1)S(1)}, u32[]{:S(2)}, u32[]{:S(2)}) collective-permute-start(bf16[32,2176]{1,0:T(8,128)(2,1)S(1)} %get-tuple-element.39.rest_0_), channel_id=1, source_target_pairs={{0,4},{1,5},{2,6},{3,7},{4,0},{5,1},{6,2},{7,3},{8,12},{9,13},{10,... | collective-permute-start | bytes 417800 | tf_op jit(solution)/shard_map/ppermute | solution.py:73
  72.1 12.8 %collective-permute-start.12 = (bf16[32,2176]{1,0:T(8,128)(2,1)S(1)}, bf16[32,2176]{1,0:T(8,128)(2,1)S(1)}, u32[]{:S(2)}, u32[]{:S(2)}) collective-permute-start(bf16[32,2176]{1,0:T(8,128)(2,1)S(1)} %get-tuple-element.47), channel_id=1, source_target_pairs={{0,4},{1,5},{2,6},{3,7},{4,0},{5,1},{6,2},{7,3},{8,12},{9,13},{10,... | collective-permute-start | bytes 417800 | tf_op jit(solution)/shard_map/ppermute | solution.py:73
  78.1 10.1 %collective-permute-start.17 = (bf16[32,2176]{1,0:T(8,128)(2,1)S(1)}, bf16[32,2176]{1,0:T(8,128)(2,1)S(1)}, u32[]{:S(2)}, u32[]{:S(2)}) collective-permute-start(bf16[32,2176]{1,0:T(8,128)(2,1)S(1)} %get-tuple-element.55), channel_id=1, source_target_pairs={{0,4},{1,5},{2,6},{3,7},{4,0},{5,1},{6,2},{7,3},{8,12},{9,13},{10,... | collective-permute-start | bytes 417800 | tf_op jit(solution)/shard_map/ppermute | solution.py:73
  83.6 8.3 %collective-permute-start.22 = (bf16[32,2176]{1,0:T(8,128)(2,1)S(1)}, bf16[32,2176]{1,0:T(8,128)(2,1)S(1)}, u32[]{:S(2)}, u32[]{:S(2)}) collective-permute-start(bf16[32,2176]{1,0:T(8,128)(2,1)S(1)} %get-tuple-element.63), channel_id=1, source_target_pairs={{0,4},{1,5},{2,6},{3,7},{4,0},{5,1},{6,2},{7,3},{8,12},{9,13},{10,... | collective-permute-start | bytes 417800 | tf_op jit(solution)/shard_map/ppermute | solution.py:73
  83.9 8.6 %collective-permute-start.8 = (bf16[16,2176]{1,0:T(8,128)(2,1)S(1)}, bf16[16,2176]{1,0:T(8,128)(2,1)S(1)}, u32[]{:S(2)}, u32[]{:S(2)}) collective-permute-start(bf16[16,2176]{1,0:T(8,128)(2,1)S(1)} %get-tuple-element.41), channel_id=1, source_target_pairs={{0,12},{1,13},{2,14},{3,15},{4,8},{5,9},{6,10},{7,11},{8,4},{9,5},... | collective-permute-start | bytes 208904 | tf_op jit(solution)/shard_map/ppermute | solution.py:73
  85.1 7.5 %collective-permute-start.13 = (bf16[16,2176]{1,0:T(8,128)(2,1)S(1)}, bf16[16,2176]{1,0:T(8,128)(2,1)S(1)}, u32[]{:S(2)}, u32[]{:S(2)}) collective-permute-start(bf16[16,2176]{1,0:T(8,128)(2,1)S(1)} %get-tuple-element.49), channel_id=1, source_target_pairs={{0,12},{1,13},{2,14},{3,15},{4,8},{5,9},{6,10},{7,11},{8,4},{9,5},... | collective-permute-start | bytes 208904 | tf_op jit(solution)/shard_map/ppermute | solution.py:73
  88.3 6.2 %collective-permute-start.18 = (bf16[16,2176]{1,0:T(8,128)(2,1)S(1)}, bf16[16,2176]{1,0:T(8,128)(2,1)S(1)}, u32[]{:S(2)}, u32[]{:S(2)}) collective-permute-start(bf16[16,2176]{1,0:T(8,128)(2,1)S(1)} %get-tuple-element.57), channel_id=1, source_target_pairs={{0,12},{1,13},{2,14},{3,15},{4,8},{5,9},{6,10},{7,11},{8,4},{9,5},... | collective-permute-start | bytes 208904 | tf_op jit(solution)/shard_map/ppermute | solution.py:73
  92.1 6.3 %collective-permute-start.23 = (bf16[16,2176]{1,0:T(8,128)(2,1)S(1)}, bf16[16,2176]{1,0:T(8,128)(2,1)S(1)}, u32[]{:S(2)}, u32[]{:S(2)}) collective-permute-start(bf16[16,2176]{1,0:T(8,128)(2,1)S(1)} %get-tuple-element.65), channel_id=1, source_target_pairs={{0,12},{1,13},{2,14},{3,15},{4,8},{5,9},{6,10},{7,11},{8,4},{9,5},... | collective-permute-start | bytes 208904 | tf_op jit(solution)/shard_map/ppermute | solution.py:73

commit v4 on v3

v4 whole, which is shorter than its diff:
```python
import functools

import jax
import jax.numpy as jnp
from jax import lax
from jax.experimental import pallas as pl
from jax.experimental.pallas import tpu as pltpu
from jax.sharding import PartitionSpec as P

PIECES = 4


def product(left, right):
    return jnp.einsum("woe,wev->wov", left, right, preferred_element_type=jnp.float32)


def gradient_terms(log_grad, kin_part, weights):
    kin_grad = -0.5 * kin_part
    weighted = jnp.sum(weights[:, None, None] * log_grad + kin_grad, axis=0)
    return (weighted, jnp.sum(log_grad, axis=0))


def general_body(inverse_rows, kinetic_rows, virt_values, virt_laplacians, local_energy):
    walk_count = lax.axis_size("walk")
    walker_count = walk_count * local_energy.shape[0]
    energy_sum = lax.psum(jnp.sum(local_energy), "walk")
    average = energy_sum / walker_count
    weights = 2.0 * (local_energy - average)
    inverse_all, kinetic_all = (
        lax.all_gather(inverse_rows, "virt", axis=2, tiled=True),
        lax.all_gather(kinetic_rows, "virt", axis=2, tiled=True),
    )
    log_grad = product(inverse_all, virt_values)
    kin_part = product(inverse_all, virt_laplacians) - product(kinetic_all, virt_values)
    weighted, log_sum = gradient_terms(log_grad, kin_part, weights)
    summed = (
        lax.psum_scatter(weighted, "walk", scatter_dimension=0, tiled=True),
        lax.psum_scatter(log_sum, "walk", scatter_dimension=0, tiled=True),
    )
    gradient_part, log_part = (summed[0], summed[1])
    return (gradient_part / walker_count, log_part / walker_count)


SPAN = 248.0
EXTRA = 128
PART = EXTRA // 4
OFFSET = 3.1
TINY = 1e-30
MIB = 1024 * 1024


def stage_masks(count):
    bits = count.bit_length() - 1
    masks = [1 << bit for bit in range(bits)]
    if bits >= 2:
        masks[-1] = 3 << (bits - 2)
    return masks


def place_weights(masks):
    bits = len(masks)
    weights = [0] * bits
    for place in range(1 << bits):
        difference = 0
        for stage, mask in enumerate(masks):
            if place >> (bits - 1 - stage) & 1:
                difference ^= mask
        if difference & (difference - 1) == 0 and difference:
            weights[difference.bit_length() - 1] = place
    return weights


def piece_masks(count, piece):
    masks = stage_masks(count)
    if piece % 2 and len(masks) >= 4:
        masks[1], masks[2] = masks[2], masks[1]
    return masks


def swap(array, axis, mask):
    pairs = [(source, source ^ mask) for source in range(lax.axis_size(axis))]
    return lax.ppermute(array, axis, pairs)


def encode(rows):
    magnitude = jnp.abs(rows)
    largest = jnp.maximum(jnp.max(magnitude, axis=-1, keepdims=True), TINY)
    scale = (largest * (1.0 + 2.0**-7)).astype(jnp.bfloat16).astype(jnp.float32)
    code = jnp.exp2(magnitude * (SPAN / scale) - SPAN / 2)
    return jnp.where(rows < 0, -code, code).astype(jnp.bfloat16), scale


def decode(coded):
    width = coded.shape[1] - EXTRA
    code = coded[:, :width].astype(jnp.float32)
    scale = coded[:, width : width + 1].astype(jnp.float32)
    magnitude = (jnp.log2(jnp.abs(code)) + SPAN / 2) * (scale / SPAN)
    return jnp.where(code < 0, -magnitude, magnitude)


def store_coded(send_ref, blocks, energy):
    width = send_ref.shape[1] - EXTRA
    f32, bf16 = jnp.float32, jnp.bfloat16
    energy = jnp.concatenate([energy, energy], axis=0)
    high = energy.astype(bf16).astype(f32)
    middle = (energy - high).astype(bf16).astype(f32)
    low = energy - high - middle
    lane = lax.broadcasted_iota(jnp.int32, energy.shape, 1)
    terms = jnp.where(lane < 2 * PART, high, jnp.where(lane < 3 * PART, middle, low))
    for pair in range(len(blocks) // 2):
        code, scale = encode(jnp.concatenate(blocks[2 * pair : 2 * pair + 2], axis=0))
        target = slice(16 * pair, 16 * pair + 16)
        send_ref[target, :width] = code
        send_ref[target, width:] = jnp.where(lane < PART, scale, terms).astype(bf16)


def add_came(keep_ref, came_ref):
    arrays, height, width = keep_ref.shape
    width -= EXTRA
    per = height // 8
    sums = []
    for pair in range(arrays * per // 2):
        both = decode(came_ref[16 * pair : 16 * pair + 16, :])
        for part in range(2):
            array, block = divmod(2 * pair + part, per)
            sums.append(keep_ref[array, 8 * block : 8 * block + 8, :width] + both[8 * part : 8 * part + 8])
    terms = came_ref[:16, width:].astype(jnp.float32)[:8]
    came = terms[:, PART : PART + 1] + terms[:, 2 * PART : 2 * PART + 1] + terms[:, 3 * PART : 3 * PART + 1]
    energy = keep_ref[0, :8, width:] + came
    return [sums[array * per : (array + 1) * per] for array in range(arrays)], energy


def limit(mib):
    return pltpu.CompilerParams(vmem_limit_bytes=mib * MIB)


def cost(microseconds):
    return pl.CostEstimate(flops=int(microseconds * 1.1e9), bytes_accessed=0, transcendentals=0)


WHOLE = pl.BlockSpec(memory_space=pltpu.VMEM)
SCALAR = pl.BlockSpec(memory_space=pltpu.SMEM)
ANYWHERE = pl.BlockSpec(memory_space=pl.ANY)
HELD = pl.BlockSpec(memory_space=pltpu.HBM)


def near_kernel(chunk, tile, virt_ref, inverse_ref, kinetic_ref, values_ref, laps_ref, out_ref, far_values, far_laps, near_values, near_laps, sems):
    count, per, depth = inverse_ref.shape
    height = count * per
    width = out_ref.shape[3]
    f32 = jnp.float32
    own = pl.ds(pl.multiple_of(virt_ref[0] * depth, depth), depth)
    other = pl.ds(pl.multiple_of((1 - virt_ref[0]) * depth, depth), depth)
    chunks = width // chunk

    copies = []
    for index in range(chunks):
        columns = pl.ds(index * chunk, chunk)
        copies.append([
            pltpu.make_async_copy(table.at[own, columns], held.at[:, columns], sems.at[index, which])
            for which, (table, held) in enumerate(((values_ref, near_values), (laps_ref, near_laps)))
        ])
    last = [
        pltpu.make_async_copy(table.at[other, :], held, sems.at[chunks, which])
        for which, (table, held) in enumerate(((values_ref, far_values), (laps_ref, far_laps)))
    ]
    for copy in sum(copies, []) + last:
        copy.start()
    inverse = inverse_ref[...].reshape(height, depth)
    kinetic = kinetic_ref[...].reshape(height, depth)
    for index in range(chunks):
        for copy in copies[index]:
            copy.wait()

        @pl.loop(index * chunk // tile, (index + 1) * chunk // tile)
        def _(step):
            columns = pl.ds(pl.multiple_of(step * tile, tile), tile)
            values, laps = near_values[:, columns], near_laps[:, columns]
            out_ref[1, :, :, columns] = jnp.dot(inverse, values, preferred_element_type=f32).reshape(count, per, tile)
            rest = jnp.dot(kinetic, values, preferred_element_type=f32)
            rest -= jnp.dot(inverse, laps, preferred_element_type=f32)
            out_ref[0, :, :, columns] = (0.5 * rest).reshape(count, per, tile)

    for copy in last:
        copy.wait()


def near_product(virt, inverse, kinetic, values, laplacians):
    count, per, depth = inverse.shape
    width = values.shape[1]
    chunk, tile = 512, 256
    table = pltpu.VMEM((depth, width), jnp.bfloat16)
    return pl.pallas_call(
        functools.partial(near_kernel, chunk, tile),
        out_shape=(jax.ShapeDtypeStruct((2, count, per, width), jnp.float32), table, table),
        in_specs=[SCALAR, WHOLE, WHOLE, HELD, HELD],
        out_specs=(WHOLE, WHOLE, WHOLE),
        scratch_shapes=[table, table, pltpu.SemaphoreType.DMA((width // chunk + 1, 2))],
        compiler_params=limit(24),
        cost_estimate=cost(9),
        name="near_product",
    )(virt, inverse, kinetic, values, laplacians)


def far_kernel(weights, count, tile, first, virt_ref, me_ref, energy_ref, far_ref, near_ref, values_ref, laps_ref, *rest):
    send_ref, keep_ref, place_ref = rest[-3:]
    _, height, depth = far_ref.shape
    width = near_ref.shape[3]
    rows = height // count
    half = height // 2
    f32 = jnp.float32
    scale = 2.0 * (energy_ref[0] - OFFSET)

    @pl.loop(0, width // tile)
    def _(index):
        columns = pl.ds(pl.multiple_of(index * tile, tile), tile)
        near = near_ref[:, :, first : first + rows, columns].reshape(2, height, tile)
        both = jnp.dot(far_ref[...].reshape(2 * height, depth), values_ref[:, columns], preferred_element_type=f32)
        laps = jnp.dot(far_ref[0], laps_ref[:, columns], preferred_element_type=f32)
        log = both[:height] + near[1]
        weighted = scale * log + (0.5 * (both[height:] - laps) + near[0])
        for dest in range(count):
            difference = dest ^ me_ref[0]
            place = 0
            for bit, weight in enumerate(weights):
                place = place ^ (((difference >> bit) & 1) * weight)
            target = pl.ds(pl.multiple_of(place * rows, rows), rows)
            source = slice(dest * rows, (dest + 1) * rows)
            place_ref[0, target, columns] = weighted[source]
            place_ref[1, target, columns] = log[source]

    energy = jnp.full((8, EXTRA), energy_ref[0], f32)
    keep_ref[:, :, :width] = place_ref[:, :half]
    keep_ref[0, :8, width:] = energy
    blocks = [place_ref[array, row : row + 8, :] for array in range(2) for row in range(half, height, 8)]
    store_coded(send_ref, blocks, energy)


def far_product(virt, me, energy, theirs, near, first, values, laplacians, tile, masks, after):
    _, height, depth = theirs.shape
    width = values.shape[1]
    half = height // 2
    return pl.pallas_call(
        functools.partial(far_kernel, place_weights(masks), 1 << len(masks), tile, first),
        out_shape=(
            jax.ShapeDtypeStruct((2 * half, width + EXTRA), jnp.bfloat16),
            jax.ShapeDtypeStruct((2, half, width + EXTRA), jnp.float32),
        ),
        in_specs=[SCALAR, SCALAR, SCALAR, WHOLE, WHOLE, WHOLE, WHOLE] + [ANYWHERE] * len(after),
        out_specs=(WHOLE, WHOLE),
        scratch_shapes=[pltpu.VMEM((2, height, width), jnp.float32)],
        compiler_params=limit(24),
        cost_estimate=cost(10),
        name="far_product",
    )(virt, me, energy, theirs, near, values, laplacians, *after)


def halve_kernel(keep_ref, came_ref, send_ref, kept_ref):
    width = keep_ref.shape[2] - EXTRA
    sums, energy = add_came(keep_ref, came_ref)
    kept = len(sums[0]) // 2
    for array, blocks in enumerate(sums):
        for index, block in enumerate(blocks[:kept]):
            kept_ref[array, 8 * index : 8 * index + 8, :width] = block
    kept_ref[0, :8, width:] = energy
    store_coded(send_ref, [block for blocks in sums for block in blocks[kept:]], energy)


def halve(keep, came):
    _, height, width = keep.shape
    return pl.pallas_call(
        halve_kernel,
        out_shape=(
            jax.ShapeDtypeStruct((height, width), jnp.bfloat16),
            jax.ShapeDtypeStruct((2, height // 2, width), jnp.float32),
        ),
        in_specs=[WHOLE, WHOLE],
        out_specs=(WHOLE, WHOLE),
        compiler_params=limit(8),
        cost_estimate=cost(0.5),
        name="halve",
    )(keep, came)


def finish_kernel(count, *refs):
    gradient_ref, log_ref = refs[-2:]
    pieces = (len(refs) - 2) // 2
    row = 0
    for piece in range(pieces):
        (gradient, log), energy = add_came(refs[2 * piece], refs[2 * piece + 1])
        correction = 2.0 * (energy[:, :1] / count - OFFSET)
        for block in range(len(log)):
            log_mean = log[block] / count
            gradient_ref[row : row + 8, :] = gradient[block] / count - correction * log_mean
            log_ref[row : row + 8, :] = log_mean
            row += 8


def finish(parts, count):
    _, rows, width = parts[0][0].shape
    out = jax.ShapeDtypeStruct((rows * len(parts), width - EXTRA), jnp.float32)
    return pl.pallas_call(
        functools.partial(finish_kernel, count),
        out_shape=(out, out),
        in_specs=[WHOLE, WHOLE] * len(parts),
        out_specs=(WHOLE, WHOLE),
        compiler_params=limit(8),
        cost_estimate=cost(0.5),
        name="finish",
    )(*[array for part in parts for array in part])


def plan(pieces, stages):
    left = [stages] * pieces
    turns = []
    for turn in range(pieces):
        steps = [piece for piece in range(turn) if left[piece]]
        if turn == pieces - 2 and turn >= 1:
            steps.append(turn - 1)
        for piece in steps:
            left[piece] -= 1
        turns.append(steps)
    last = []
    while any(left):
        for piece in range(pieces):
            if left[piece]:
                left[piece] -= 1
                last.append(piece)
    turns[-1] = turns[-1] + last
    return turns


def pieced_body(pieces, tile, inverse_rows, kinetic_rows, virt_values, virt_laplacians, local_energy):
    count = lax.axis_size("walk")
    masks = [piece_masks(count, piece) for piece in range(pieces)]
    stages = len(masks[0])
    me = lax.axis_index("walk").astype(jnp.int32).reshape(1)
    virt = lax.axis_index("virt").astype(jnp.int32).reshape(1)
    occupied, depth = inverse_rows.shape[1:]
    by_dest = (count, occupied // count, depth)
    inverse, kinetic = inverse_rows.reshape(by_dest), kinetic_rows.reshape(by_dest)
    rows = occupied // (count * pieces)

    theirs = []
    for piece in range(pieces):
        part = slice(piece * rows, (piece + 1) * rows)
        taken = [array[:, part].reshape(count * rows, depth) for array in (inverse, kinetic)]
        theirs.append(swap(jnp.stack(taken), "virt", 1))
    tables = [pltpu.with_memory_space_constraint(table[0], pltpu.HBM) for table in (virt_values, virt_laplacians)]
    near, values, laplacians = near_product(virt, inverse, kinetic, *tables)

    send, keep, parts = {}, {}, {}
    stage = [0] * pieces
    for turn, steps in enumerate(plan(pieces, stages)):
        if turn < pieces:
            after = [send[other] for other in sorted(send)]
            send[turn], keep[turn] = far_product(
                virt, me, local_energy, theirs[turn], near, turn * rows, values, laplacians, tile, masks[turn], after
            )
        for piece in steps:
            came = swap(send.pop(piece), "walk", masks[piece][stage[piece]])
            stage[piece] += 1
            if stage[piece] < stages:
                send[piece], keep[piece] = halve(keep[piece], came)
            else:
                parts[piece] = (keep[piece], came)
    return finish([parts[piece] for piece in range(pieces)], count)


def solution(mesh):
    placed = (
        P("walk", None, "virt"),
        P("walk", None, "virt"),
        P("walk", None, "virt"),
        P("walk", None, "virt"),
        P("walk"),
    )

    def body(inverse_rows, kinetic_rows, virt_values, virt_laplacians, local_energy):
        count = mesh.shape["walk"]
        walkers, occupied, depth = inverse_rows.shape
        width = virt_values.shape[2]
        tile = 512
        fits = (
            walkers == 1
            and mesh.shape["virt"] == 2
            and count >= 4
            and count & (count - 1) == 0
            and occupied % (count * PIECES * 8) == 0
            and depth % 256 == 0
            and width % tile == 0
        )
        form = functools.partial(pieced_body, PIECES, tile) if fits else general_body
        return form(inverse_rows, kinetic_rows, virt_values, virt_laplacians, local_energy)

    return jax.shard_map(
        body,
        mesh=mesh,
        in_specs=placed,
        out_specs=(P("walk", "virt"), P("walk", "virt")),
        check_vma=False,
    )
```

time: 99.9 us -> 93.8 us (0.939)
  local copies, waits for them, and re-layouts: 16 us -> 2.68 us
  waiting for transfers between devices: 26.9 us -> 35.7 us
  Pallas kernels: 30.6 us -> 26.7 us
  starting transfers between devices: 23.4 us -> 25.1 us
    unnamed x10, local copies, waits for them, and re-layouts: 13.5 us -> 0.03 us
    ppermute x24 -> x20, waiting for transfers between devices: 26.9 us -> 35.7 us  [swap(): return lax.ppermute(array, axis, pairs)]
    pallas_call x4, Pallas kernels: 14.4 us -> 11.3 us  [far_product(): pl.pallas_call(functools.partial(far_kernel, place_weights(masks), 1 << l...]
    ppermute x24 -> x20, starting transfers between devices: 23.4 us -> 25.1 us  [swap(): return lax.ppermute(array, axis, pairs)]
    pallas_call x4 -> x1, Pallas kernels: 10.4 us -> 9.63 us  [near_product(): pl.pallas_call(functools.partial(near_kernel, chunk, tile), out_shape=(ja...]
  transfers between devices with their start and end apart: 24 -> 20, of which waited for: 10 -> 10; matrix products, arithmetic and copies ran while one was open for 3% -> 1% of each run, Pallas kernels for 30% -> 27%
where the time goes in v4:
time: 93.8 us; the launch traced here: 93.6 us
  waiting for transfers between devices  35.7 us (38%)
  Pallas kernels  26.7 us (28%)
  starting transfers between devices  25.1 us (27%)
  local copies, waits for them, and re-layouts  2.68 us (3%)
  other arithmetic  1.81 us (2%)
  between operations  1.56 us (2%)
    ppermute x20, waiting for transfers between devices, swap(): return lax.ppermute(array, axis, pairs)  35.7 us
    ppermute x20, starting transfers between devices, swap(): return lax.ppermute(array, axis, pairs)  25.1 us
    pallas_call x4, Pallas kernels, far_product(): pl.pallas_call(functools.partial(far_kernel, place_weights(masks), 1 << l...  11.3 us
    pallas_call x1, Pallas kernels, near_product(): pl.pallas_call(functools.partial(near_kernel, chunk, tile), out_shape=(ja...  9.63 us
    pallas_call x12, Pallas kernels, halve(): pl.pallas_call(halve_kernel, out_shape=(jax.ShapeDtypeStruct((height, wid...  4.64 us
    another operation x1, local copies, waits for them, and re-layouts, pieced_body(): theirs.append(swap(jnp.stack(taken), 'virt', 1))  2.65 us
  transfers between devices with their start and end apart: 20, of which 10 were waited for; matrix products, arithmetic and copies ran while one was open for 1% of the time, Pallas kernels for 27%

profile of v4, /device:TPU:0, one launch (start us, length us, event | category | flops | bytes accessed | tf_op | source)
XLA Modules:
  0.0 93.6 jit_solution(9214034724370075147)
XLA Ops:
  0.6 2.7 %slice_bitcast_fusion = (bf16[1,128,1024]{2,1,0:T(8,128)(2,1)S(1)}, bf16[1,128,1024]{2,1,0:T(8,128)(2,1)}, bf16[1,128,1024]{2,1,0:T(8,128)(2,1)S(1)}, bf16[1,128...) fusion(bf16[16,32,1024]{2,1,0:T(8,128)(2,1)} %bitcast.22, ...), kind=kLoop, calls=%fused_computation.4 | loop fusion | bytes 4194304 | tf_op jit(solution)/shard_map/stack;reshape | solution.py:348
  3.3 0.8 pad_maximum_fusion
  4.1 3.0 %collective-permute-start = (bf16[2,128,1024]{2,1,0:T(8,128)(2,1)}, bf16[2,128,1024]{2,1,0:T(8,128)(2,1)S(1)}, u32[]{:S(2)}, u32[]{:S(2)}) collective-permute-start(bf16[2,128,1024]{2,1,0:T(8,128)(2,1)} %pad_maximum_fusion), channel_id=1, source_target_pairs={{0,16},{16,0},{1,17},{17,1},{2,18},{18,2},{3,19},{19,3},{4,20},{20... | collective-permute-start | bytes 1572872 | tf_op jit(solution)/shard_map/ppermute | solution.py:82
  7.1 0.9 pad_maximum_fusion.1
  8.7 9.6 %near_product.1 = (f32[2,16,32,2048]{3,2,1,0:T(8,128)S(1)}, bf16[1024,2048]{1,0:T(8,128)(2,1)S(1)}, bf16[1024,2048]{1,0:T(8,128)(2,1)S(1)}) custom-call(s32[1]{0:T(128)} %bitcast.virt_ref, bf16[16,32,1024]{2,1,0:T(8,128)(2,1)S(1)} %bitcast.25, bf16[16,32,1024]{2,1,0:T(8,128)(2,1)S(1)} %bitcast.23, bf16[2048,2048]{1,0:T(8,128)(2,1)} %bitcast.26, ...), custom_call_target="tpu_custom_call" | custom-call | flops 9900000256 | tf_op jit(solution)/shard_map/near_product/pallas_call | solution.py:193
  18.3 1.8 %collective-permute-done.far_ref = bf16[2,128,1024]{2,1,0:T(8,128)(2,1)S(1)} collective-permute-done((bf16[2,128,1024]{2,1,0:T(8,128)(2,1)}, bf16[2,128,1024]{2,1,0:T(8,128)(2,1)S(1)}, u32[]{:S(2)}, u32[]{:S(2)}) %collective-permute-start) | collective-permute-done | bytes 524320 | tf_op jit(solution)/shard_map/ppermute | solution.py:82
  20.1 2.8 %far_product.4 = (bf16[128,2176]{1,0:T(8,128)(2,1)S(1)}, f32[2,64,2176]{2,1,0:T(8,128)S(1)}) custom-call(s32[1]{0:T(128)} %bitcast.virt_ref, s32[1]{0:T(128)} %bitcast.1.me_ref, f32[1]{0:T(128)S(6)} %copy.7.energy_ref, bf16[2,128,1024]{2,1,0:T(8,128)(2,1)S(1)} %collective-permute-done.far_ref, f32[2,16,32,2048]{3,2,1,0:T(8,128)S(1)} %get-tuple-element.37.near_ref, ...), custom_call_target="tpu_custom_call" | custom-call | flops 11000000512 | tf_op jit(solution)/shard_map/far_product/pallas_call | solution.py:243
  23.0 7.5 %collective-permute-done.5.far_ref = bf16[2,128,1024]{2,1,0:T(8,128)(2,1)S(1)} collective-permute-done((bf16[2,128,1024]{2,1,0:T(8,128)(2,1)}, bf16[2,128,1024]{2,1,0:T(8,128)(2,1)S(1)}, u32[]{:S(2)}, u32[]{:S(2)}) %collective-permute-start.5) | collective-permute-done | bytes 524320 | tf_op jit(solution)/shard_map/ppermute | solution.py:82
  30.5 2.8 %far_product.5 = (bf16[128,2176]{1,0:T(8,128)(2,1)S(1)}, f32[2,64,2176]{2,1,0:T(8,128)S(1)}) custom-call(s32[1]{0:T(128)} %bitcast.virt_ref, s32[1]{0:T(128)} %bitcast.1.me_ref, f32[1]{0:T(128)S(6)} %copy.7.energy_ref, bf16[2,128,1024]{2,1,0:T(8,128)(2,1)S(1)} %collective-permute-done.5.far_ref, f32[2,16,32,2048]{3,2,1,0:T(8,128)S(1)} %get-tuple-element.37.near_ref, ...), custom_call_target="tpu_custom_call" | custom-call | flops 11000000512 | tf_op jit(solution)/shard_map/far_product/pallas_call | solution.py:243
  33.4 1.8 %collective-permute-start.10 = (bf16[2,128,1024]{2,1,0:T(8,128)(2,1)S(1)}, bf16[2,128,1024]{2,1,0:T(8,128)(2,1)S(1)}, u32[]{:S(2)}, u32[]{:S(2)}) collective-permute-start(bf16[2,128,1024]{2,1,0:T(8,128)(2,1)S(1)} %pad_maximum_fusion.2), channel_id=1, source_target_pairs={{0,16},{16,0},{1,17},{17,1},{2,18},{18,2},{3,19},{19,3},{4,20},{20... | collective-permute-start | bytes 1572872 | tf_op jit(solution)/shard_map/ppermute | solution.py:82
  35.6 0.6 halve.12
  36.2 1.8 %collective-permute-start.2 = (bf16[64,2176]{1,0:T(8,128)(2,1)S(1)}, bf16[64,2176]{1,0:T(8,128)(2,1)S(1)}, u32[]{:S(2)}, u32[]{:S(2)}) collective-permute-start(bf16[64,2176]{1,0:T(8,128)(2,1)S(1)} %get-tuple-element.43.rest_0_), channel_id=1, source_target_pairs={{0,2},{1,3},{2,0},{3,1},{4,6},{5,7},{6,4},{7,5},{8,10},{9,11},{10,... | collective-permute-start | bytes 835592 | tf_op jit(solution)/shard_map/ppermute | solution.py:82
  38.0 0.6 halve.15
  38.6 1.6 %collective-permute-start.7 = (bf16[64,2176]{1,0:T(8,128)(2,1)S(1)}, bf16[64,2176]{1,0:T(8,128)(2,1)S(1)}, u32[]{:S(2)}, u32[]{:S(2)}) collective-permute-start(bf16[64,2176]{1,0:T(8,128)(2,1)S(1)} %get-tuple-element.51), channel_id=1, source_target_pairs={{0,4},{1,5},{2,6},{3,7},{4,0},{5,1},{6,2},{7,3},{8,12},{9,13},{10,... | collective-permute-start | bytes 835592 | tf_op jit(solution)/shard_map/ppermute | solution.py:82
  40.2 8.0 %collective-permute-done.10.far_ref = bf16[2,128,1024]{2,1,0:T(8,128)(2,1)S(1)} collective-permute-done((bf16[2,128,1024]{2,1,0:T(8,128)(2,1)S(1)}, bf16[2,128,1024]{2,1,0:T(8,128)(2,1)S(1)}, u32[]{:S(2)}, u32[]{:S(2)}) %collective-permute-start.10) | collective-permute-done | bytes 524320 | tf_op jit(solution)/shard_map/ppermute | solution.py:82
  48.2 2.8 %far_product.6 = (bf16[128,2176]{1,0:T(8,128)(2,1)S(1)}, f32[2,64,2176]{2,1,0:T(8,128)S(1)}) custom-call(s32[1]{0:T(128)} %bitcast.virt_ref, s32[1]{0:T(128)} %bitcast.1.me_ref, f32[1]{0:T(128)S(6)} %copy.7.energy_ref, bf16[2,128,1024]{2,1,0:T(8,128)(2,1)S(1)} %collective-permute-done.10.far_ref, f32[2,16,32,2048]{3,2,1,0:T(8,128)S(1)} %get-tuple-element.37.near_ref, ...), custom_call_target="tpu_custom_call" | custom-call | flops 11000000512 | tf_op jit(solution)/shard_map/far_product/pallas_call | solution.py:243
  51.8 7.2 %collective-permute-done.15.far_ref = bf16[2,128,1024]{2,1,0:T(8,128)(2,1)S(1)} collective-permute-done((bf16[2,128,1024]{2,1,0:T(8,128)(2,1)S(1)}, bf16[2,128,1024]{2,1,0:T(8,128)(2,1)S(1)}, u32[]{:S(2)}, u32[]{:S(2)}) %collective-permute-start.15) | collective-permute-done | bytes 524320 | tf_op jit(solution)/shard_map/ppermute | solution.py:82
  59.0 3.0 %far_product.7 = (bf16[128,2176]{1,0:T(8,128)(2,1)S(1)}, f32[2,64,2176]{2,1,0:T(8,128)S(1)}) custom-call(s32[1]{0:T(128)} %bitcast.virt_ref, s32[1]{0:T(128)} %bitcast.1.me_ref, f32[1]{0:T(128)S(6)} %copy.7.energy_ref, bf16[2,128,1024]{2,1,0:T(8,128)(2,1)S(1)} %collective-permute-done.15.far_ref, f32[2,16,32,2048]{3,2,1,0:T(8,128)S(1)} %get-tuple-element.37.near_ref, ...), custom_call_target="tpu_custom_call" | custom-call | flops 11000000512 | tf_op jit(solution)/shard_map/far_product/pallas_call | solution.py:243
  62.1 0.6 halve.18
  62.7 1.8 %collective-permute-start.12 = (bf16[64,2176]{1,0:T(8,128)(2,1)S(1)}, bf16[64,2176]{1,0:T(8,128)(2,1)S(1)}, u32[]{:S(2)}, u32[]{:S(2)}) collective-permute-start(bf16[64,2176]{1,0:T(8,128)(2,1)S(1)} %get-tuple-element.59), channel_id=1, source_target_pairs={{0,2},{1,3},{2,0},{3,1},{4,6},{5,7},{6,4},{7,5},{8,10},{9,11},{10,... | collective-permute-start | bytes 835592 | tf_op jit(solution)/shard_map/ppermute | solution.py:82
  65.0 1.7 %collective-permute-start.17 = (bf16[64,2176]{1,0:T(8,128)(2,1)S(1)}, bf16[64,2176]{1,0:T(8,128)(2,1)S(1)}, u32[]{:S(2)}, u32[]{:S(2)}) collective-permute-start(bf16[64,2176]{1,0:T(8,128)(2,1)S(1)} %get-tuple-element.67), channel_id=1, source_target_pairs={{0,4},{1,5},{2,6},{3,7},{4,0},{5,1},{6,2},{7,3},{8,12},{9,13},{10,... | collective-permute-start | bytes 835592 | tf_op jit(solution)/shard_map/ppermute | solution.py:82
  67.1 1.3 %collective-permute-start.8 = (bf16[32,2176]{1,0:T(8,128)(2,1)S(1)}, bf16[32,2176]{1,0:T(8,128)(2,1)S(1)}, u32[]{:S(2)}, u32[]{:S(2)}) collective-permute-start(bf16[32,2176]{1,0:T(8,128)(2,1)S(1)} %get-tuple-element.53.rest_1_), channel_id=1, source_target_pairs={{0,2},{1,3},{2,0},{3,1},{4,6},{5,7},{6,4},{7,5},{8,10},{9,11},{10,... | collective-permute-start | bytes 417800 | tf_op jit(solution)/shard_map/ppermute | solution.py:82
  68.4 3.8 %collective-permute-done.12.came_ref = bf16[64,2176]{1,0:T(8,128)(2,1)S(1)} collective-permute-done((bf16[64,2176]{1,0:T(8,128)(2,1)S(1)}, bf16[64,2176]{1,0:T(8,128)(2,1)S(1)}, u32[]{:S(2)}, u32[]{:S(2)}) %collective-permute-start.12) | collective-permute-done | bytes 278560 | tf_op jit(solution)/shard_map/ppermute | solution.py:82
  72.5 1.9 %collective-permute-start.13 = (bf16[32,2176]{1,0:T(8,128)(2,1)S(1)}, bf16[32,2176]{1,0:T(8,128)(2,1)S(1)}, u32[]{:S(2)}, u32[]{:S(2)}) collective-permute-start(bf16[32,2176]{1,0:T(8,128)(2,1)S(1)} %get-tuple-element.61), channel_id=1, source_target_pairs={{0,4},{1,5},{2,6},{3,7},{4,0},{5,1},{6,2},{7,3},{8,12},{9,13},{10,... | collective-permute-start | bytes 417800 | tf_op jit(solution)/shard_map/ppermute | solution.py:82
  74.9 1.4 %collective-permute-start.18 = (bf16[32,2176]{1,0:T(8,128)(2,1)S(1)}, bf16[32,2176]{1,0:T(8,128)(2,1)S(1)}, u32[]{:S(2)}, u32[]{:S(2)}) collective-permute-start(bf16[32,2176]{1,0:T(8,128)(2,1)S(1)} %get-tuple-element.69), channel_id=1, source_target_pairs={{0,2},{1,3},{2,0},{3,1},{4,6},{5,7},{6,4},{7,5},{8,10},{9,11},{10,... | collective-permute-start | bytes 417800 | tf_op jit(solution)/shard_map/ppermute | solution.py:82
  76.3 1.3 %collective-permute-done.3.came_ref = bf16[32,2176]{1,0:T(8,128)(2,1)S(1)} collective-permute-done((bf16[32,2176]{1,0:T(8,128)(2,1)S(1)}, bf16[32,2176]{1,0:T(8,128)(2,1)S(1)}, u32[]{:S(2)}, u32[]{:S(2)}) %collective-permute-start.3) | collective-permute-done | bytes 139296 | tf_op jit(solution)/shard_map/ppermute | solution.py:82
  77.8 3.7 %collective-permute-start.4 = (bf16[16,2176]{1,0:T(8,128)(2,1)S(1)}, bf16[16,2176]{1,0:T(8,128)(2,1)S(1)}, u32[]{:S(2)}, u32[]{:S(2)}) collective-permute-start(bf16[16,2176]{1,0:T(8,128)(2,1)S(1)} %get-tuple-element.47), channel_id=1, source_target_pairs={{0,12},{1,13},{2,14},{3,15},{4,8},{5,9},{6,10},{7,11},{8,4},{9,5},... | collective-permute-start | bytes 208904 | tf_op jit(solution)/shard_map/ppermute | solution.py:82
  82.3 3.7 %collective-permute-start.14 = (bf16[16,2176]{1,0:T(8,128)(2,1)S(1)}, bf16[16,2176]{1,0:T(8,128)(2,1)S(1)}, u32[]{:S(2)}, u32[]{:S(2)}) collective-permute-start(bf16[16,2176]{1,0:T(8,128)(2,1)S(1)} %get-tuple-element.63), channel_id=1, source_target_pairs={{0,12},{1,13},{2,14},{3,15},{4,8},{5,9},{6,10},{7,11},{8,4},{9,5},... | collective-permute-start | bytes 208904 | tf_op jit(solution)/shard_map/ppermute | solution.py:82
  86.5 1.5 %collective-permute-done.9.refs_3_ = bf16[16,2176]{1,0:T(8,128)(2,1)S(1)} collective-permute-done((bf16[16,2176]{1,0:T(8,128)(2,1)S(1)}, bf16[16,2176]{1,0:T(8,128)(2,1)S(1)}, u32[]{:S(2)}, u32[]{:S(2)}) %collective-permute-start.9) | collective-permute-done | bytes 69664 | tf_op jit(solution)/shard_map/ppermute | solution.py:82
  88.0 1.0 %collective-permute-done.14.refs_5_ = bf16[16,2176]{1,0:T(8,128)(2,1)S(1)} collective-permute-done((bf16[16,2176]{1,0:T(8,128)(2,1)S(1)}, bf16[16,2176]{1,0:T(8,128)(2,1)S(1)}, u32[]{:S(2)}, u32[]{:S(2)}) %collective-permute-start.14) | collective-permute-done | bytes 69664 | tf_op jit(solution)/shard_map/ppermute | solution.py:82
  89.0 3.5 %collective-permute-done.19.refs_7_ = bf16[16,2176]{1,0:T(8,128)(2,1)S(1)} collective-permute-done((bf16[16,2176]{1,0:T(8,128)(2,1)S(1)}, bf16[16,2176]{1,0:T(8,128)(2,1)S(1)}, u32[]{:S(2)}, u32[]{:S(2)}) %collective-permute-start.19) | collective-permute-done | bytes 69664 | tf_op jit(solution)/shard_map/ppermute | solution.py:82
  92.5 1.1 %finish.1 = (f32[32,2048]{1,0:T(8,128)}, f32[32,2048]{1,0:T(8,128)}) custom-call(f32[2,8,2176]{2,1,0:T(8,128)S(1)} %get-tuple-element.46.refs_0_, bf16[16,2176]{1,0:T(8,128)(2,1)S(1)} %collective-permute-done.4.refs_1_, f32[2,8,2176]{2,1,0:T(8,128)S(1)} %get-tuple-element.54.refs_2_, bf16[16,2176]{1,0:T(8,128)(2,1)S(1)} %collective-permute-done.9.refs_3_, ...), custom_call_target="tpu_custom_call" | custom-call | flops 550000000 | tf_op jit(solution)/shard_map/finish/pallas_call | solution.py:302
  (41 shorter events, 4.8 us)
Async XLA Ops:
  0.6 8.0 %copy-start = (bf16[1,512,1024]{2,1,0:T(8,128)(2,1)S(1)}, bf16[1,512,1024]{2,1,0:T(8,128)(2,1)}, u32[]{:S(2)}) copy-start(bf16[1,512,1024]{2,1,0:T(8,128)(2,1)} %param.6) | copy-start | bytes 3145732
  0.6 8.0 %copy-start.1 = (bf16[1,512,1024]{2,1,0:T(8,128)(2,1)S(1)}, bf16[1,512,1024]{2,1,0:T(8,128)(2,1)}, u32[]{:S(2)}) copy-start(bf16[1,512,1024]{2,1,0:T(8,128)(2,1)} %param.5) | copy-start | bytes 3145732
  4.1 15.9 %collective-permute-start = (bf16[2,128,1024]{2,1,0:T(8,128)(2,1)}, bf16[2,128,1024]{2,1,0:T(8,128)(2,1)S(1)}, u32[]{:S(2)}, u32[]{:S(2)}) collective-permute-start(bf16[2,128,1024]{2,1,0:T(8,128)(2,1)} %pad_maximum_fusion), channel_id=1, source_target_pairs={{0,16},{16,0},{1,17},{17,1},{2,18},{18,2},{3,19},{19,3},{4,20},{20... | collective-permute-start | bytes 1572872 | tf_op jit(solution)/shard_map/ppermute | solution.py:82
  8.0 22.5 %collective-permute-start.5 = (bf16[2,128,1024]{2,1,0:T(8,128)(2,1)}, bf16[2,128,1024]{2,1,0:T(8,128)(2,1)S(1)}, u32[]{:S(2)}, u32[]{:S(2)}) collective-permute-start(bf16[2,128,1024]{2,1,0:T(8,128)(2,1)} %pad_maximum_fusion.1), channel_id=1, source_target_pairs={{0,16},{16,0},{1,17},{17,1},{2,18},{18,2},{3,19},{19,3},{4,20},{20... | collective-permute-start | bytes 1572872 | tf_op jit(solution)/shard_map/ppermute | solution.py:82
  22.8 10.5 %copy-start.3 = (bf16[1,128,1024]{2,1,0:T(8,128)(2,1)S(1)}, bf16[1,128,1024]{2,1,0:T(8,128)(2,1)}, u32[]{:S(2)}) copy-start(bf16[1,128,1024]{2,1,0:T(8,128)(2,1)} %get-tuple-element.77) | copy-start | bytes 786436
  22.9 10.5 %copy-start.4 = (bf16[1,128,1024]{2,1,0:T(8,128)(2,1)S(1)}, bf16[1,128,1024]{2,1,0:T(8,128)(2,1)}, u32[]{:S(2)}) copy-start(bf16[1,128,1024]{2,1,0:T(8,128)(2,1)} %get-tuple-element.82) | copy-start | bytes 786436
  22.9 12.3 %copy-start.2 = (bf16[1,128,1024]{2,1,0:T(8,128)(2,1)S(1)}, bf16[1,128,1024]{2,1,0:T(8,128)(2,1)}, u32[]{:S(2)}) copy-start(bf16[1,128,1024]{2,1,0:T(8,128)(2,1)} %get-tuple-element.83) | copy-start | bytes 786436
  22.9 12.7 %collective-permute-start.1 = (bf16[128,2176]{1,0:T(8,128)(2,1)S(1)}, bf16[128,2176]{1,0:T(8,128)(2,1)S(1)}, u32[]{:S(2)}, u32[]{:S(2)}) collective-permute-start(bf16[128,2176]{1,0:T(8,128)(2,1)S(1)} %get-tuple-element.41.rest_0_), channel_id=1, source_target_pairs={{0,1},{1,0},{2,3},{3,2},{4,5},{5,4},{6,7},{7,6},{8,9},{9,8},{10,11... | collective-permute-start | bytes 1671176 | tf_op jit(solution)/shard_map/ppermute | solution.py:82
  33.2 4.7 %collective-permute-start.6 = (bf16[128,2176]{1,0:T(8,128)(2,1)S(1)}, bf16[128,2176]{1,0:T(8,128)(2,1)S(1)}, u32[]{:S(2)}, u32[]{:S(2)}) collective-permute-start(bf16[128,2176]{1,0:T(8,128)(2,1)S(1)} %get-tuple-element.49.rest_1_), channel_id=1, source_target_pairs={{0,1},{1,0},{2,3},{3,2},{4,5},{5,4},{6,7},{7,6},{8,9},{9,8},{10,11... | collective-permute-start | bytes 1671176 | tf_op jit(solution)/shard_map/ppermute | solution.py:82
  33.4 14.8 %collective-permute-start.10 = (bf16[2,128,1024]{2,1,0:T(8,128)(2,1)S(1)}, bf16[2,128,1024]{2,1,0:T(8,128)(2,1)S(1)}, u32[]{:S(2)}, u32[]{:S(2)}) collective-permute-start(bf16[2,128,1024]{2,1,0:T(8,128)(2,1)S(1)} %pad_maximum_fusion.2), channel_id=1, source_target_pairs={{0,16},{16,0},{1,17},{17,1},{2,18},{18,2},{3,19},{19,3},{4,20},{20... | collective-permute-start | bytes 1572872 | tf_op jit(solution)/shard_map/ppermute | solution.py:82
  35.3 23.7 %collective-permute-start.15 = (bf16[2,128,1024]{2,1,0:T(8,128)(2,1)S(1)}, bf16[2,128,1024]{2,1,0:T(8,128)(2,1)S(1)}, u32[]{:S(2)}, u32[]{:S(2)}) collective-permute-start(bf16[2,128,1024]{2,1,0:T(8,128)(2,1)S(1)} %pad_maximum_fusion.3), channel_id=1, source_target_pairs={{0,16},{16,0},{1,17},{17,1},{2,18},{18,2},{3,19},{19,3},{4,20},{20... | collective-permute-start | bytes 1572872 | tf_op jit(solution)/shard_map/ppermute | solution.py:82
  36.2 14.9 %collective-permute-start.2 = (bf16[64,2176]{1,0:T(8,128)(2,1)S(1)}, bf16[64,2176]{1,0:T(8,128)(2,1)S(1)}, u32[]{:S(2)}, u32[]{:S(2)}) collective-permute-start(bf16[64,2176]{1,0:T(8,128)(2,1)S(1)} %get-tuple-element.43.rest_0_), channel_id=1, source_target_pairs={{0,2},{1,3},{2,0},{3,1},{4,6},{5,7},{6,4},{7,5},{8,10},{9,11},{10,... | collective-permute-start | bytes 835592 | tf_op jit(solution)/shard_map/ppermute | solution.py:82
  38.6 12.8 %collective-permute-start.7 = (bf16[64,2176]{1,0:T(8,128)(2,1)S(1)}, bf16[64,2176]{1,0:T(8,128)(2,1)S(1)}, u32[]{:S(2)}, u32[]{:S(2)}) collective-permute-start(bf16[64,2176]{1,0:T(8,128)(2,1)S(1)} %get-tuple-element.51), channel_id=1, source_target_pairs={{0,4},{1,5},{2,6},{3,7},{4,0},{5,1},{6,2},{7,3},{8,12},{9,13},{10,... | collective-permute-start | bytes 835592 | tf_op jit(solution)/shard_map/ppermute | solution.py:82
  51.0 11.1 %collective-permute-start.11 = (bf16[128,2176]{1,0:T(8,128)(2,1)S(1)}, bf16[128,2176]{1,0:T(8,128)(2,1)S(1)}, u32[]{:S(2)}, u32[]{:S(2)}) collective-permute-start(bf16[128,2176]{1,0:T(8,128)(2,1)S(1)} %get-tuple-element.57.rest_2_), channel_id=1, source_target_pairs={{0,1},{1,0},{2,3},{3,2},{4,5},{5,4},{6,7},{7,6},{8,9},{9,8},{10,11... | collective-permute-start | bytes 1671176 | tf_op jit(solution)/shard_map/ppermute | solution.py:82
  62.0 2.5 %collective-permute-start.16 = (bf16[128,2176]{1,0:T(8,128)(2,1)S(1)}, bf16[128,2176]{1,0:T(8,128)(2,1)S(1)}, u32[]{:S(2)}, u32[]{:S(2)}) collective-permute-start(bf16[128,2176]{1,0:T(8,128)(2,1)S(1)} %get-tuple-element.65), channel_id=1, source_target_pairs={{0,1},{1,0},{2,3},{3,2},{4,5},{5,4},{6,7},{7,6},{8,9},{9,8},{10,11... | collective-permute-start | bytes 1671176 | tf_op jit(solution)/shard_map/ppermute | solution.py:82
  62.7 9.5 %collective-permute-start.12 = (bf16[64,2176]{1,0:T(8,128)(2,1)S(1)}, bf16[64,2176]{1,0:T(8,128)(2,1)S(1)}, u32[]{:S(2)}, u32[]{:S(2)}) collective-permute-start(bf16[64,2176]{1,0:T(8,128)(2,1)S(1)} %get-tuple-element.59), channel_id=1, source_target_pairs={{0,2},{1,3},{2,0},{3,1},{4,6},{5,7},{6,4},{7,5},{8,10},{9,11},{10,... | collective-permute-start | bytes 835592 | tf_op jit(solution)/shard_map/ppermute | solution.py:82
  65.0 9.6 %collective-permute-start.17 = (bf16[64,2176]{1,0:T(8,128)(2,1)S(1)}, bf16[64,2176]{1,0:T(8,128)(2,1)S(1)}, u32[]{:S(2)}, u32[]{:S(2)}) collective-permute-start(bf16[64,2176]{1,0:T(8,128)(2,1)S(1)} %get-tuple-element.67), channel_id=1, source_target_pairs={{0,4},{1,5},{2,6},{3,7},{4,0},{5,1},{6,2},{7,3},{8,12},{9,13},{10,... | collective-permute-start | bytes 835592 | tf_op jit(solution)/shard_map/ppermute | solution.py:82
  66.7 10.9 %collective-permute-start.3 = (bf16[32,2176]{1,0:T(8,128)(2,1)S(1)}, bf16[32,2176]{1,0:T(8,128)(2,1)S(1)}, u32[]{:S(2)}, u32[]{:S(2)}) collective-permute-start(bf16[32,2176]{1,0:T(8,128)(2,1)S(1)} %get-tuple-element.45.rest_0_), channel_id=1, source_target_pairs={{0,4},{1,5},{2,6},{3,7},{4,0},{5,1},{6,2},{7,3},{8,12},{9,13},{10,... | collective-permute-start | bytes 417800 | tf_op jit(solution)/shard_map/ppermute | solution.py:82
  67.1 14.4 %collective-permute-start.8 = (bf16[32,2176]{1,0:T(8,128)(2,1)S(1)}, bf16[32,2176]{1,0:T(8,128)(2,1)S(1)}, u32[]{:S(2)}, u32[]{:S(2)}) collective-permute-start(bf16[32,2176]{1,0:T(8,128)(2,1)S(1)} %get-tuple-element.53.rest_1_), channel_id=1, source_target_pairs={{0,2},{1,3},{2,0},{3,1},{4,6},{5,7},{6,4},{7,5},{8,10},{9,11},{10,... | collective-permute-start | bytes 417800 | tf_op jit(solution)/shard_map/ppermute | solution.py:82
  72.5 9.5 %collective-permute-start.13 = (bf16[32,2176]{1,0:T(8,128)(2,1)S(1)}, bf16[32,2176]{1,0:T(8,128)(2,1)S(1)}, u32[]{:S(2)}, u32[]{:S(2)}) collective-permute-start(bf16[32,2176]{1,0:T(8,128)(2,1)S(1)} %get-tuple-element.61), channel_id=1, source_target_pairs={{0,4},{1,5},{2,6},{3,7},{4,0},{5,1},{6,2},{7,3},{8,12},{9,13},{10,... | collective-permute-start | bytes 417800 | tf_op jit(solution)/shard_map/ppermute | solution.py:82
  74.9 11.0 %collective-permute-start.18 = (bf16[32,2176]{1,0:T(8,128)(2,1)S(1)}, bf16[32,2176]{1,0:T(8,128)(2,1)S(1)}, u32[]{:S(2)}, u32[]{:S(2)}) collective-permute-start(bf16[32,2176]{1,0:T(8,128)(2,1)S(1)} %get-tuple-element.69), channel_id=1, source_target_pairs={{0,2},{1,3},{2,0},{3,1},{4,6},{5,7},{6,4},{7,5},{8,10},{9,11},{10,... | collective-permute-start | bytes 417800 | tf_op jit(solution)/shard_map/ppermute | solution.py:82
  77.8 8.7 %collective-permute-start.4 = (bf16[16,2176]{1,0:T(8,128)(2,1)S(1)}, bf16[16,2176]{1,0:T(8,128)(2,1)S(1)}, u32[]{:S(2)}, u32[]{:S(2)}) collective-permute-start(bf16[16,2176]{1,0:T(8,128)(2,1)S(1)} %get-tuple-element.47), channel_id=1, source_target_pairs={{0,12},{1,13},{2,14},{3,15},{4,8},{5,9},{6,10},{7,11},{8,4},{9,5},... | collective-permute-start | bytes 208904 | tf_op jit(solution)/shard_map/ppermute | solution.py:82
  81.8 6.3 %collective-permute-start.9 = (bf16[16,2176]{1,0:T(8,128)(2,1)S(1)}, bf16[16,2176]{1,0:T(8,128)(2,1)S(1)}, u32[]{:S(2)}, u32[]{:S(2)}) collective-permute-start(bf16[16,2176]{1,0:T(8,128)(2,1)S(1)} %get-tuple-element.55), channel_id=1, source_target_pairs={{0,12},{1,13},{2,14},{3,15},{4,8},{5,9},{6,10},{7,11},{8,4},{9,5},... | collective-permute-start | bytes 208904 | tf_op jit(solution)/shard_map/ppermute | solution.py:82
  82.3 6.7 %collective-permute-start.14 = (bf16[16,2176]{1,0:T(8,128)(2,1)S(1)}, bf16[16,2176]{1,0:T(8,128)(2,1)S(1)}, u32[]{:S(2)}, u32[]{:S(2)}) collective-permute-start(bf16[16,2176]{1,0:T(8,128)(2,1)S(1)} %get-tuple-element.63), channel_id=1, source_target_pairs={{0,12},{1,13},{2,14},{3,15},{4,8},{5,9},{6,10},{7,11},{8,4},{9,5},... | collective-permute-start | bytes 208904 | tf_op jit(solution)/shard_map/ppermute | solution.py:82
  86.2 6.3 %collective-permute-start.19 = (bf16[16,2176]{1,0:T(8,128)(2,1)S(1)}, bf16[16,2176]{1,0:T(8,128)(2,1)S(1)}, u32[]{:S(2)}, u32[]{:S(2)}) collective-permute-start(bf16[16,2176]{1,0:T(8,128)(2,1)S(1)} %get-tuple-element.71), channel_id=1, source_target_pairs={{0,12},{1,13},{2,14},{3,15},{4,8},{5,9},{6,10},{7,11},{8,4},{9,5},... | collective-permute-start | bytes 208904 | tf_op jit(solution)/shard_map/ppermute | solution.py:82

commit v5 on v4

--- a/solution.py
+++ b/solution.py
@@ -8,6 +8,7 @@
 from jax.sharding import PartitionSpec as P
 
 PIECES = 4
+SPLIT = 4
 
 
 def product(left, right):
@@ -50,31 +51,25 @@
 
 
 def stage_masks(count):
-    bits = count.bit_length() - 1
-    masks = [1 << bit for bit in range(bits)]
-    if bits >= 2:
-        masks[-1] = 3 << (bits - 2)
-    return masks
-
-
-def place_weights(masks):
-    bits = len(masks)
-    weights = [0] * bits
-    for place in range(1 << bits):
-        difference = 0
-        for stage, mask in enumerate(masks):
-            if place >> (bits - 1 - stage) & 1:
-                difference ^= mask
-        if difference & (difference - 1) == 0 and difference:
-            weights[difference.bit_length() - 1] = place
+    bits = [1 << bit for bit in range(count.bit_length() - 1)]
+    if len(bits) < 3:
+        return [[bit] for bit in bits]
+    return [bits[:1], bits[1:3]] + [[bit] for bit in bits[3:]]
+
+
+def place_weights(stages):
+    order = [mask for stage in stages for mask in stage]
+    weights = [0] * len(order)
+    for index, mask in enumerate(order):
+        weights[mask.bit_length() - 1] = 1 << (len(order) - 1 - index)
     return weights
 
 
-def piece_masks(count, piece):
-    masks = stage_masks(count)
-    if piece % 2 and len(masks) >= 4:
-        masks[1], masks[2] = masks[2], masks[1]
-    return masks
+def partners(stage):
+    if len(stage) == 1:
+        return list(stage)
+    first, second = stage
+    return [second, first, first ^ second]
 
 
 def swap(array, axis, mask):
@@ -98,8 +93,9 @@
     return jnp.where(code < 0, -magnitude, magnitude)
 
 
-def store_coded(send_ref, blocks, energy):
-    width = send_ref.shape[1] - EXTRA
+def store_coded(send_refs, blocks, energy):
+    width = send_refs[0].shape[1] - EXTRA
+    each = send_refs[0].shape[0]
     f32, bf16 = jnp.float32, jnp.bfloat16
     energy = jnp.concatenate([energy, energy], axis=0)
     high = energy.astype(bf16).astype(f32)
@@ -109,24 +105,29 @@
     terms = jnp.where(lane < 2 * PART, high, jnp.where(lane < 3 * PART, middle, low))
     for pair in range(len(blocks) // 2):
         code, scale = encode(jnp.concatenate(blocks[2 * pair : 2 * pair + 2], axis=0))
-        target = slice(16 * pair, 16 * pair + 16)
+        send_ref = send_refs[16 * pair // each]
+        target = slice(16 * pair % each, 16 * pair % each + 16)
         send_ref[target, :width] = code
         send_ref[target, width:] = jnp.where(lane < PART, scale, terms).astype(bf16)
 
 
-def add_came(keep_ref, came_ref):
+def add_came(keep_ref, came_refs):
     arrays, height, width = keep_ref.shape
     width -= EXTRA
     per = height // 8
-    sums = []
-    for pair in range(arrays * per // 2):
-        both = decode(came_ref[16 * pair : 16 * pair + 16, :])
-        for part in range(2):
-            array, block = divmod(2 * pair + part, per)
-            sums.append(keep_ref[array, 8 * block : 8 * block + 8, :width] + both[8 * part : 8 * part + 8])
-    terms = came_ref[:16, width:].astype(jnp.float32)[:8]
-    came = terms[:, PART : PART + 1] + terms[:, 2 * PART : 2 * PART + 1] + terms[:, 3 * PART : 3 * PART + 1]
-    energy = keep_ref[0, :8, width:] + came
+    sums = [keep_ref[index // per, 8 * (index % per) : 8 * (index % per) + 8, :width] for index in range(arrays * per)]
+    energy = keep_ref[0, :8, width:]
+    for parts in came_refs:
+        index = 0
+        for part in parts:
+            for row in range(0, part.shape[0], 16):
+                both = decode(part[row : row + 16, :])
+                sums[index] += both[:8]
+                sums[index + 1] += both[8:]
+                index += 2
+        terms = parts[0][:16, width:].astype(jnp.float32)[:8]
+        for term in range(1, 4):
+            energy += terms[:, term * PART : term * PART + 1]
     return [sums[array * per : (array + 1) * per] for array in range(arrays)], energy
 
 
@@ -142,9 +143,36 @@
 SCALAR = pl.BlockSpec(memory_space=pltpu.SMEM)
 ANYWHERE = pl.BlockSpec(memory_space=pl.ANY)
 HELD = pl.BlockSpec(memory_space=pltpu.HBM)
-
-
-def near_kernel(chunk, tile, virt_ref, inverse_ref, kinetic_ref, values_ref, laps_ref, out_ref, far_values, far_laps, near_values, near_laps, sems):
+HELD = pl.BlockSpec(memory_space=pltpu.HBM)
+
+
+def cut_kernel(inverse_ref, kinetic_ref, *out_refs):
+    count = inverse_ref.shape[0]
+    for array, ref in enumerate((inverse_ref, kinetic_ref)):
+        for dest in range(0, count, 2):
+            pair = [ref[dest + other].astype(jnp.float32) for other in range(2)]
+            for index, out_ref in enumerate(out_refs):
+                rows = jnp.concatenate([block[8 * index : 8 * index + 8] for block in pair], axis=0)
+                out_ref[array, 8 * dest : 8 * dest + 16, :] = rows.astype(jnp.bfloat16)
+
+
+def cut(inverse, kinetic, group):
+    count, _, depth = inverse.shape
+    block = pl.BlockSpec((count, 16, depth), lambda step: (0, group, 0))
+    out = jax.ShapeDtypeStruct((2, 8 * count, depth), jnp.bfloat16)
+    return pl.pallas_call(
+        cut_kernel,
+        out_shape=(out, out),
+        grid=(1,),
+        in_specs=[block, block],
+        out_specs=(pl.BlockSpec(out.shape, lambda step: (0, 0, 0)),) * 2,
+        compiler_params=limit(12),
+        cost_estimate=cost(0.1),
+        name="cut",
+    )(inverse, kinetic)
+
+
+def near_kernel(chunk, tile, virt_ref, inverse_ref, kinetic_ref, values_ref, laps_ref, out_ref, far_values, far_laps, near_values, near_laps, own_inverse, own_kinetic, sems):
     count, per, depth = inverse_ref.shape
     height = count * per
     width = out_ref.shape[3]
@@ -164,10 +192,16 @@
         pltpu.make_async_copy(table.at[other, :], held, sems.at[chunks, which])
         for which, (table, held) in enumerate(((values_ref, far_values), (laps_ref, far_laps)))
     ]
-    for copy in sum(copies, []) + last:
+    first = [
+        pltpu.make_async_copy(rows, held, sems.at[chunks + 1, which])
+        for which, (rows, held) in enumerate(((inverse_ref, own_inverse), (kinetic_ref, own_kinetic)))
+    ]
+    for copy in first + sum(copies, []) + last:
         copy.start()
-    inverse = inverse_ref[...].reshape(height, depth)
-    kinetic = kinetic_ref[...].reshape(height, depth)
+    for copy in first:
+        copy.wait()
+    inverse = own_inverse[...].reshape(height, depth)
+    kinetic = own_kinetic[...].reshape(height, depth)
     for index in range(chunks):
         for copy in copies[index]:
             copy.wait()
@@ -190,12 +224,13 @@
     width = values.shape[1]
     chunk, tile = 512, 256
     table = pltpu.VMEM((depth, width), jnp.bfloat16)
+    own = pltpu.VMEM((count, per, depth), jnp.bfloat16)
     return pl.pallas_call(
         functools.partial(near_kernel, chunk, tile),
         out_shape=(jax.ShapeDtypeStruct((2, count, per, width), jnp.float32), table, table),
-        in_specs=[SCALAR, WHOLE, WHOLE, HELD, HELD],
+        in_specs=[SCALAR, HELD, HELD, HELD, HELD],
         out_specs=(WHOLE, WHOLE, WHOLE),
-        scratch_shapes=[table, table, pltpu.SemaphoreType.DMA((width // chunk + 1, 2))],
+        scratch_shapes=[table, table, own, own, pltpu.SemaphoreType.DMA((width // chunk + 2, 2))],
         compiler_params=limit(24),
         cost_estimate=cost(9),
         name="near_product",
@@ -203,7 +238,7 @@
 
 
 def far_kernel(weights, count, tile, first, virt_ref, me_ref, energy_ref, far_ref, near_ref, values_ref, laps_ref, *rest):
-    send_ref, keep_ref, place_ref = rest[-3:]
+    send_refs, (keep_ref, place_ref) = rest[-SPLIT - 2 : -2], rest[-2:]
     _, height, depth = far_ref.shape
     width = near_ref.shape[3]
     rows = height // count
@@ -233,61 +268,73 @@
     keep_ref[:, :, :width] = place_ref[:, :half]
     keep_ref[0, :8, width:] = energy
     blocks = [place_ref[array, row : row + 8, :] for array in range(2) for row in range(half, height, 8)]
-    store_coded(send_ref, blocks, energy)
-
-
-def far_product(virt, me, energy, theirs, near, first, values, laplacians, tile, masks, after):
+    store_coded(send_refs, blocks, energy)
+
+
+def far_product(virt, me, energy, theirs, near, first, values, laplacians, tile, stages, after):
     _, height, depth = theirs.shape
     width = values.shape[1]
     half = height // 2
-    return pl.pallas_call(
-        functools.partial(far_kernel, place_weights(masks), 1 << len(masks), tile, first),
-        out_shape=(
-            jax.ShapeDtypeStruct((2 * half, width + EXTRA), jnp.bfloat16),
-            jax.ShapeDtypeStruct((2, half, width + EXTRA), jnp.float32),
-        ),
+    count = 1 << sum(len(stage) for stage in stages)
+    *sends, keep = pl.pallas_call(
+        functools.partial(far_kernel, place_weights(stages), count, tile, first),
+        out_shape=(jax.ShapeDtypeStruct((2 * half // SPLIT, width + EXTRA), jnp.bfloat16),) * SPLIT
+        + (jax.ShapeDtypeStruct((2, half, width + EXTRA), jnp.float32),),
         in_specs=[SCALAR, SCALAR, SCALAR, WHOLE, WHOLE, WHOLE, WHOLE] + [ANYWHERE] * len(after),
-        out_specs=(WHOLE, WHOLE),
+        out_specs=(WHOLE,) * (SPLIT + 1),
         scratch_shapes=[pltpu.VMEM((2, height, width), jnp.float32)],
         compiler_params=limit(24),
-        cost_estimate=cost(10),
+        cost_estimate=cost(0.1),
         name="far_product",
     )(virt, me, energy, theirs, near, values, laplacians, *after)
-
-
-def halve_kernel(keep_ref, came_ref, send_ref, kept_ref):
+    return [sends], keep
+
+
+def combine_kernel(parts, senders, carried, *refs):
+    keep_ref, refs = refs[0], refs[1:]
+    came_refs = [refs[parts * sender : parts * sender + parts] for sender in range(senders)]
+    refs = refs[parts * senders :]
+    kept_ref, send_refs = refs[carried], refs[carried + 1 :]
     width = keep_ref.shape[2] - EXTRA
-    sums, energy = add_came(keep_ref, came_ref)
-    kept = len(sums[0]) // 2
+    sums, energy = add_came(keep_ref, came_refs)
+    kept = kept_ref.shape[1] // 8
     for array, blocks in enumerate(sums):
         for index, block in enumerate(blocks[:kept]):
             kept_ref[array, 8 * index : 8 * index + 8, :width] = block
     kept_ref[0, :8, width:] = energy
-    store_coded(send_ref, [block for blocks in sums for block in blocks[kept:]], energy)
-
-
-def halve(keep, came):
+    for index, send_ref in enumerate(send_refs):
+        if carried:
+            above = refs[0].shape[0]
+            send_ref[:above, :] = refs[0][...]
+            send_ref = send_ref.at[above:, :]
+        first = kept * (index + 1)
+        store_coded([send_ref], [block for blocks in sums for block in blocks[first : first + kept]], energy)
+
+
+def combine(keep, came, sent, carry=()):
     _, height, width = keep.shape
-    return pl.pallas_call(
-        halve_kernel,
-        out_shape=(
-            jax.ShapeDtypeStruct((height, width), jnp.bfloat16),
-            jax.ShapeDtypeStruct((2, height // 2, width), jnp.float32),
-        ),
-        in_specs=[WHOLE, WHOLE],
-        out_specs=(WHOLE, WHOLE),
+    kept = height // (sent + 1)
+    parts, senders = len(came[0]), len(came)
+    above = sum(array.shape[0] for array in carry)
+    keep, *sends = pl.pallas_call(
+        functools.partial(combine_kernel, parts, senders, len(carry)),
+        out_shape=(jax.ShapeDtypeStruct((2, kept, width), jnp.float32),)
+        + (jax.ShapeDtypeStruct((above + 2 * kept, width), jnp.bfloat16),) * sent,
+        in_specs=[WHOLE] * (1 + parts * senders + len(carry)),
+        out_specs=(WHOLE,) * (1 + sent),
         compiler_params=limit(8),
-        cost_estimate=cost(0.5),
-        name="halve",
-    )(keep, came)
+        cost_estimate=cost(0.1),
+        name="combine",
+    )(keep, *[part for parts in came for part in parts], *carry)
+    return [[send] for send in sends], keep
 
 
 def finish_kernel(count, *refs):
-    gradient_ref, log_ref = refs[-2:]
-    pieces = (len(refs) - 2) // 2
+    keep_refs, (early_ref, late_ref, gradient_ref, log_ref) = refs[:-4], refs[-4:]
     row = 0
-    for piece in range(pieces):
-        (gradient, log), energy = add_came(refs[2 * piece], refs[2 * piece + 1])
+    for piece, keep_ref in enumerate(keep_refs):
+        came = early_ref.at[16 * piece : 16 * piece + 16, :] if piece + 1 < len(keep_refs) else late_ref
+        (gradient, log), energy = add_came(keep_ref, [[came]])
         correction = 2.0 * (energy[:, :1] / count - OFFSET)
         for block in range(len(log)):
             log_mean = log[block] / count
@@ -296,44 +343,23 @@
             row += 8
 
 
-def finish(parts, count):
-    _, rows, width = parts[0][0].shape
-    out = jax.ShapeDtypeStruct((rows * len(parts), width - EXTRA), jnp.float32)
+def finish(keeps, early, late, count):
+    _, rows, width = keeps[0].shape
+    out = jax.ShapeDtypeStruct((rows * len(keeps), width - EXTRA), jnp.float32)
     return pl.pallas_call(
         functools.partial(finish_kernel, count),
         out_shape=(out, out),
-        in_specs=[WHOLE, WHOLE] * len(parts),
+        in_specs=[WHOLE] * (len(keeps) + 2),
         out_specs=(WHOLE, WHOLE),
         compiler_params=limit(8),
-        cost_estimate=cost(0.5),
+        cost_estimate=cost(0.1),
         name="finish",
-    )(*[array for part in parts for array in part])
-
-
-def plan(pieces, stages):
-    left = [stages] * pieces
-    turns = []
-    for turn in range(pieces):
-        steps = [piece for piece in range(turn) if left[piece]]
-        if turn == pieces - 2 and turn >= 1:
-            steps.append(turn - 1)
-        for piece in steps:
-            left[piece] -= 1
-        turns.append(steps)
-    last = []
-    while any(left):
-        for piece in range(pieces):
-            if left[piece]:
-                left[piece] -= 1
-                last.append(piece)
-    turns[-1] = turns[-1] + last
-    return turns
+    )(*keeps, early, late)
 
 
 def pieced_body(pieces, tile, inverse_rows, kinetic_rows, virt_values, virt_laplacians, local_energy):
     count = lax.axis_size("walk")
-    masks = [piece_masks(count, piece) for piece in range(pieces)]
-    stages = len(masks[0])
+    stages = stage_masks(count)
     me = lax.axis_index("walk").astype(jnp.int32).reshape(1)
     virt = lax.axis_index("virt").astype(jnp.int32).reshape(1)
     occupied, depth = inverse_rows.shape[1:]
@@ -341,30 +367,36 @@
     inverse, kinetic = inverse_rows.reshape(by_dest), kinetic_rows.reshape(by_dest)
     rows = occupied // (count * pieces)
 
+    inverse, kinetic, values, laplacians = (
+        pltpu.with_memory_space_constraint(array, pltpu.HBM)
+        for array in (inverse, kinetic, virt_values[0], virt_laplacians[0])
+    )
     theirs = []
-    for piece in range(pieces):
-        part = slice(piece * rows, (piece + 1) * rows)
-        taken = [array[:, part].reshape(count * rows, depth) for array in (inverse, kinetic)]
-        theirs.append(swap(jnp.stack(taken), "virt", 1))
-    tables = [pltpu.with_memory_space_constraint(table[0], pltpu.HBM) for table in (virt_values, virt_laplacians)]
-    near, values, laplacians = near_product(virt, inverse, kinetic, *tables)
-
-    send, keep, parts = {}, {}, {}
-    stage = [0] * pieces
-    for turn, steps in enumerate(plan(pieces, stages)):
+    for group in range(pieces // 2):
+        theirs += [swap(mine, "virt", 1) for mine in cut(inverse, kinetic, group)]
+    near, values, laplacians = near_product(virt, inverse, kinetic, values, laplacians)
+
+    send, keep, done = {}, {}, [0] * pieces
+    carry = ()
+    for turn in range(pieces + 1):
         if turn < pieces:
-            after = [send[other] for other in sorted(send)]
+            after = [keep[other] for other in sorted(keep)]
             send[turn], keep[turn] = far_product(
-                virt, me, local_energy, theirs[turn], near, turn * rows, values, laplacians, tile, masks[turn], after
+                virt, me, local_energy, theirs[turn], near, turn * rows, values, laplacians, tile, stages, after
             )
-        for piece in steps:
-            came = swap(send.pop(piece), "walk", masks[piece][stage[piece]])
-            stage[piece] += 1
-            if stage[piece] < stages:
-                send[piece], keep[piece] = halve(keep[piece], came)
-            else:
-                parts[piece] = (keep[piece], came)
-    return finish([parts[piece] for piece in range(pieces)], count)
+        for piece in (turn - 1, turn):
+            if not 0 <= piece < pieces:
+                continue
+            masks = partners(stages[done[piece]])
+            came = [[swap(part, "walk", mask) for part in parts] for parts, mask in zip(send[piece], masks)]
+            done[piece] += 1
+            sent = len(partners(stages[done[piece]]))
+            joins = carry if done[piece] == 2 and piece + 1 < pieces else ()
+            send[piece], keep[piece] = combine(keep[piece], came, sent, joins)
+            if done[piece] == 2 and piece + 1 < pieces:
+                carry = tuple(send[piece][0])
+    early, late = (swap(array, "walk", stages[2][0]) for array in (carry[0], send[pieces - 1][0][0]))
+    return finish([keep[piece] for piece in range(pieces)], early, late, count)
 
 
 def solution(mesh):
@@ -384,9 +416,9 @@
         fits = (
             walkers == 1
             and mesh.shape["virt"] == 2
+            and count == 16
             and count >= 4
-            and count & (count - 1) == 0
-            and occupied % (count * PIECES * 8) == 0
+            and occupied == count * PIECES * 8
             and depth % 256 == 0
             and width % tile == 0
         )

time: 93.8 us -> 94.1 us (level)
  waiting for transfers between devices: 35.7 us -> 22 us
  local copies, waits for them, and re-layouts: 2.68 us -> 15 us
  Pallas kernels: 26.7 us -> 29.6 us
  other arithmetic: 1.81 us -> 0 us
    unnamed x10 -> x12, local copies, waits for them, and re-layouts: 0.03 us -> 15 us
    ppermute x20 -> x34, waiting for transfers between devices: 35.7 us -> 22 us  [swap(): return lax.ppermute(array, axis, pairs)]
    another operation x1 -> x0, local copies, waits for them, and re-layouts: 2.65 us -> none  [pieced_body(): theirs.append(swap(jnp.stack(taken), 'virt', 1))]
    pallas_call x16 -> x14, Pallas kernels: 16 us -> 18.2 us  [the longest x4 11.5 us: far_product(): pl.pallas_call(functools.partial(far_kernel, place_weights(stages), count...]
    another operation x4 -> x0, other arithmetic: 1.81 us -> none  [pieced_body(): theirs.append(swap(jnp.stack(taken), 'virt', 1))]
    ppermute x20 -> x34, starting transfers between devices: 25.1 us -> 25.7 us  [swap(): return lax.ppermute(array, axis, pairs)]
  transfers between devices with their start and end apart: 20 -> 34, of which waited for: 10 -> 12; matrix products, arithmetic and copies ran while one was open for 1% -> 0% of each run, Pallas kernels for 27% -> 26%
where the time goes in v5:
time: 94.1 us; the launch traced here: 93.8 us
  Pallas kernels  29.6 us (31%)
  starting transfers between devices  25.7 us (27%)
  waiting for transfers between devices  22 us (23%)
  local copies, waits for them, and re-layouts  15 us (16%)
  between operations  1.53 us (2%)
    ppermute x34, starting transfers between devices, swap(): return lax.ppermute(array, axis, pairs)  25.7 us
    ppermute x34, waiting for transfers between devices, swap(): return lax.ppermute(array, axis, pairs)  22 us
    unnamed x12, local copies, waits for them, and re-layouts  15 us
    pallas_call x4, Pallas kernels, far_product(): pl.pallas_call(functools.partial(far_kernel, place_weights(stages), count...  11.5 us
    pallas_call x1, Pallas kernels, near_product(): pl.pallas_call(functools.partial(near_kernel, chunk, tile), out_shape=(ja...  10.3 us
    pallas_call x8, Pallas kernels, combine(): pl.pallas_call(functools.partial(combine_kernel, parts, senders, len(carr...  4.15 us
    pallas_call x2, Pallas kernels, cut(): pl.pallas_call(cut_kernel, out_shape=(out, out), grid=(1,), in_specs=[blo...  2.55 us
  transfers between devices with their start and end apart: 34, of which 12 were waited for; matrix products, arithmetic and copies ran while one was open for 0% of the time, Pallas kernels for 26%

profile of v5, /device:TPU:0, one launch (start us, length us, event | category | flops | bytes accessed | tf_op | source)
XLA Modules:
  0.0 93.8 jit_solution(11116108744076571754)
XLA Ops:
  0.6 1.3 %cut.2 = (bf16[2,128,1024]{2,1,0:T(8,128)(2,1)S(1)}, bf16[2,128,1024]{2,1,0:T(8,128)(2,1)S(1)}) custom-call(bf16[16,32,1024]{2,1,0:T(8,128)(2,1)} %bitcast.6, bf16[16,32,1024]{2,1,0:T(8,128)(2,1)} %bitcast.9), custom_call_target="tpu_custom_call" | custom-call | flops 110000000 | tf_op jit(solution)/shard_map/cut/pallas_call | solution.py:163
  1.9 3.0 %collective-permute-start = (bf16[2,128,1024]{2,1,0:T(8,128)(2,1)S(1)}, bf16[2,128,1024]{2,1,0:T(8,128)(2,1)S(1)}, u32[]{:S(2)}, u32[]{:S(2)}) collective-permute-start(bf16[2,128,1024]{2,1,0:T(8,128)(2,1)S(1)} %get-tuple-element.53), channel_id=1, source_target_pairs={{0,16},{16,0},{1,17},{17,1},{2,18},{18,2},{3,19},{19,3},{4,20},{20... | collective-permute-start | bytes 1572872 | tf_op jit(solution)/shard_map/ppermute | solution.py:77
  5.0 10.3 %near_product.1 = (f32[2,16,32,2048]{3,2,1,0:T(8,128)S(1)}, bf16[1024,2048]{1,0:T(8,128)(2,1)S(1)}, bf16[1024,2048]{1,0:T(8,128)(2,1)S(1)}) custom-call(s32[1]{0:T(128)} %bitcast.virt_ref, bf16[16,32,1024]{2,1,0:T(8,128)(2,1)} %bitcast.7, bf16[16,32,1024]{2,1,0:T(8,128)(2,1)} %bitcast.10, bf16[2048,2048]{1,0:T(8,128)(2,1)} %bitcast.12, ...), custom_call_target="tpu_custom_call" | custom-call | flops 9900000256 | tf_op jit(solution)/shard_map/near_product/pallas_call | solution.py:228
  15.3 3.3 %copy-done = f32[2,16,32,2048]{3,2,1,0:T(8,128)} copy-done((f32[2,16,32,2048]{3,2,1,0:T(8,128)}, f32[2,16,32,2048]{3,2,1,0:T(8,128)S(1)}, u32[]{:S(2)}) %copy-start) | copy-done | bytes 8388632
  18.6 2.1 %copy-done.2 = bf16[1024,2048]{1,0:T(8,128)(2,1)} copy-done((bf16[1024,2048]{1,0:T(8,128)(2,1)}, bf16[1024,2048]{1,0:T(8,128)(2,1)S(1)}, u32[]{:S(2)}) %copy-start.2) | copy-done | bytes 4194328
  20.7 1.9 %copy-done.4 = bf16[1024,2048]{1,0:T(8,128)(2,1)} copy-done((bf16[1024,2048]{1,0:T(8,128)(2,1)}, bf16[1024,2048]{1,0:T(8,128)(2,1)S(1)}, u32[]{:S(2)}) %copy-start.4) | copy-done | bytes 4194328
  23.3 3.4 %copy-done.1 = f32[2,16,32,2048]{3,2,1,0:T(8,128)S(1)} copy-done((f32[2,16,32,2048]{3,2,1,0:T(8,128)S(1)}, f32[2,16,32,2048]{3,2,1,0:T(8,128)}, u32[]{:S(2)}) %copy-start.1) | copy-done | bytes 8388632
  26.7 2.2 %copy-done.3 = bf16[1024,2048]{1,0:T(8,128)(2,1)S(1)} copy-done((bf16[1024,2048]{1,0:T(8,128)(2,1)S(1)}, bf16[1024,2048]{1,0:T(8,128)(2,1)}, u32[]{:S(2)}) %copy-start.3) | copy-done | bytes 4194328
  28.8 2.2 %copy-done.5 = bf16[1024,2048]{1,0:T(8,128)(2,1)S(1)} copy-done((bf16[1024,2048]{1,0:T(8,128)(2,1)S(1)}, bf16[1024,2048]{1,0:T(8,128)(2,1)}, u32[]{:S(2)}) %copy-start.5) | copy-done | bytes 4194328
  31.0 2.8 %far_product.4 = (bf16[32,2176]{1,0:T(8,128)(2,1)S(1)}, bf16[32,2176]{1,0:T(8,128)(2,1)S(1)}, bf16[32,2176]{1,0:T(8,128)(2,1)S(1)}, bf16[32,2176]{1,0:T(8,128)(2,1)S(1)}, f32[2,64,2176]{2,1,0:T(8,128)S(1)}) custom-call(s32[1]{0:T(128)} %bitcast.virt_ref, s32[1]{0:T(128)} %bitcast.1.me_ref, f32[1]{0:T(128)S(6)} %copy.7.energy_ref, ...), custom_call_target="tpu_custom_call" | custom-call | flops 110000000 | tf_op jit(solution)/shard_map/far_product/pallas_call | solution.py:279
  34.9 1.3 %cut.3 = (bf16[2,128,1024]{2,1,0:T(8,128)(2,1)S(1)}, bf16[2,128,1024]{2,1,0:T(8,128)(2,1)S(1)}) custom-call(bf16[16,32,1024]{2,1,0:T(8,128)(2,1)} %bitcast.8, bf16[16,32,1024]{2,1,0:T(8,128)(2,1)} %bitcast.11), custom_call_target="tpu_custom_call" | custom-call | flops 110000000 | tf_op jit(solution)/shard_map/cut/pallas_call | solution.py:163
  36.2 2.0 %collective-permute-start.16 = (bf16[2,128,1024]{2,1,0:T(8,128)(2,1)S(1)}, bf16[2,128,1024]{2,1,0:T(8,128)(2,1)S(1)}, u32[]{:S(2)}, u32[]{:S(2)}) collective-permute-start(bf16[2,128,1024]{2,1,0:T(8,128)(2,1)S(1)} %get-tuple-element.79), channel_id=1, source_target_pairs={{0,16},{16,0},{1,17},{17,1},{2,18},{18,2},{3,19},{19,3},{4,20},{20... | collective-permute-start | bytes 1572872 | tf_op jit(solution)/shard_map/ppermute | solution.py:77
  39.0 2.8 %far_product.5 = (bf16[32,2176]{1,0:T(8,128)(2,1)S(1)}, bf16[32,2176]{1,0:T(8,128)(2,1)S(1)}, bf16[32,2176]{1,0:T(8,128)(2,1)S(1)}, bf16[32,2176]{1,0:T(8,128)(2,1)S(1)}, f32[2,64,2176]{2,1,0:T(8,128)S(1)}) custom-call(s32[1]{0:T(128)} %bitcast.virt_ref, s32[1]{0:T(128)} %bitcast.1.me_ref, f32[1]{0:T(128)S(6)} %copy.7.energy_ref, ...), custom_call_target="tpu_custom_call" | custom-call | flops 110000000 | tf_op jit(solution)/shard_map/far_product/pallas_call | solution.py:279
  43.4 1.9 %collective-permute-start.5 = (bf16[32,2176]{1,0:T(8,128)(2,1)S(1)}, bf16[32,2176]{1,0:T(8,128)(2,1)S(1)}, u32[]{:S(2)}, u32[]{:S(2)}) collective-permute-start(bf16[32,2176]{1,0:T(8,128)(2,1)S(1)} %get-tuple-element.63), channel_id=1, source_target_pairs={{0,4},{1,5},{2,6},{3,7},{4,0},{5,1},{6,2},{7,3},{8,12},{9,13},{10,... | collective-permute-start | bytes 417800 | tf_op jit(solution)/shard_map/ppermute | solution.py:77
  45.3 1.5 %collective-permute-start.6 = (bf16[32,2176]{1,0:T(8,128)(2,1)S(1)}, bf16[32,2176]{1,0:T(8,128)(2,1)S(1)}, u32[]{:S(2)}, u32[]{:S(2)}) collective-permute-start(bf16[32,2176]{1,0:T(8,128)(2,1)S(1)} %get-tuple-element.64), channel_id=1, source_target_pairs={{0,2},{1,3},{2,0},{3,1},{4,6},{5,7},{6,4},{7,5},{8,10},{9,11},{10,... | collective-permute-start | bytes 417800 | tf_op jit(solution)/shard_map/ppermute | solution.py:77
  47.6 2.1 %collective-permute-done.5.refs_1_ = bf16[32,2176]{1,0:T(8,128)(2,1)S(1)} collective-permute-done((bf16[32,2176]{1,0:T(8,128)(2,1)S(1)}, bf16[32,2176]{1,0:T(8,128)(2,1)S(1)}, u32[]{:S(2)}, u32[]{:S(2)}) %collective-permute-start.5) | collective-permute-done | bytes 139296 | tf_op jit(solution)/shard_map/ppermute | solution.py:77
  49.7 2.1 %collective-permute-start.13 = (bf16[32,2176]{1,0:T(8,128)(2,1)S(1)}, bf16[32,2176]{1,0:T(8,128)(2,1)S(1)}, u32[]{:S(2)}, u32[]{:S(2)}) collective-permute-start(bf16[32,2176]{1,0:T(8,128)(2,1)S(1)} %get-tuple-element.74), channel_id=1, source_target_pairs={{0,4},{1,5},{2,6},{3,7},{4,0},{5,1},{6,2},{7,3},{8,12},{9,13},{10,... | collective-permute-start | bytes 417800 | tf_op jit(solution)/shard_map/ppermute | solution.py:77
  51.8 1.4 %collective-permute-done.6.refs_2_ = bf16[32,2176]{1,0:T(8,128)(2,1)S(1)} collective-permute-done((bf16[32,2176]{1,0:T(8,128)(2,1)S(1)}, bf16[32,2176]{1,0:T(8,128)(2,1)S(1)}, u32[]{:S(2)}, u32[]{:S(2)}) %collective-permute-start.6) | collective-permute-done | bytes 139296 | tf_op jit(solution)/shard_map/ppermute | solution.py:77
  53.3 2.5 %collective-permute-start.14 = (bf16[32,2176]{1,0:T(8,128)(2,1)S(1)}, bf16[32,2176]{1,0:T(8,128)(2,1)S(1)}, u32[]{:S(2)}, u32[]{:S(2)}) collective-permute-start(bf16[32,2176]{1,0:T(8,128)(2,1)S(1)} %get-tuple-element.75), channel_id=1, source_target_pairs={{0,2},{1,3},{2,0},{3,1},{4,6},{5,7},{6,4},{7,5},{8,10},{9,11},{10,... | collective-permute-start | bytes 417800 | tf_op jit(solution)/shard_map/ppermute | solution.py:77
  56.1 2.8 %far_product.6 = (bf16[32,2176]{1,0:T(8,128)(2,1)S(1)}, bf16[32,2176]{1,0:T(8,128)(2,1)S(1)}, bf16[32,2176]{1,0:T(8,128)(2,1)S(1)}, bf16[32,2176]{1,0:T(8,128)(2,1)S(1)}, f32[2,64,2176]{2,1,0:T(8,128)S(1)}) custom-call(s32[1]{0:T(128)} %bitcast.virt_ref, s32[1]{0:T(128)} %bitcast.1.me_ref, f32[1]{0:T(128)S(6)} %copy.7.energy_ref, ...), custom_call_target="tpu_custom_call" | custom-call | flops 110000000 | tf_op jit(solution)/shard_map/far_product/pallas_call | solution.py:279
  59.9 1.9 %collective-permute-done.15.refs_3_ = bf16[32,2176]{1,0:T(8,128)(2,1)S(1)} collective-permute-done((bf16[32,2176]{1,0:T(8,128)(2,1)S(1)}, bf16[32,2176]{1,0:T(8,128)(2,1)S(1)}, u32[]{:S(2)}, u32[]{:S(2)}) %collective-permute-start.15) | collective-permute-done | bytes 139296 | tf_op jit(solution)/shard_map/ppermute | solution.py:77
  62.1 1.0 %collective-permute-done.20.refs_4_ = bf16[32,2176]{1,0:T(8,128)(2,1)S(1)} collective-permute-done((bf16[32,2176]{1,0:T(8,128)(2,1)S(1)}, bf16[32,2176]{1,0:T(8,128)(2,1)S(1)}, u32[]{:S(2)}, u32[]{:S(2)}) %collective-permute-start.20) | collective-permute-done | bytes 139296 | tf_op jit(solution)/shard_map/ppermute | solution.py:77
  63.8 3.0 %far_product.7 = (bf16[32,2176]{1,0:T(8,128)(2,1)S(1)}, bf16[32,2176]{1,0:T(8,128)(2,1)S(1)}, bf16[32,2176]{1,0:T(8,128)(2,1)S(1)}, bf16[32,2176]{1,0:T(8,128)(2,1)S(1)}, f32[2,64,2176]{2,1,0:T(8,128)S(1)}) custom-call(s32[1]{0:T(128)} %bitcast.virt_ref, s32[1]{0:T(128)} %bitcast.1.me_ref, f32[1]{0:T(128)S(6)} %copy.7.energy_ref, ...), custom_call_target="tpu_custom_call" | custom-call | flops 110000000 | tf_op jit(solution)/shard_map/far_product/pallas_call | solution.py:279
  68.2 1.2 %collective-permute-start.22 = (bf16[32,2176]{1,0:T(8,128)(2,1)S(1)}, bf16[32,2176]{1,0:T(8,128)(2,1)S(1)}, u32[]{:S(2)}, u32[]{:S(2)}) collective-permute-start(bf16[32,2176]{1,0:T(8,128)(2,1)S(1)} %get-tuple-element.87), channel_id=1, source_target_pairs={{0,2},{1,3},{2,0},{3,1},{4,6},{5,7},{6,4},{7,5},{8,10},{9,11},{10,... | collective-permute-start | bytes 417800 | tf_op jit(solution)/shard_map/ppermute | solution.py:77
  69.4 2.0 %collective-permute-start.23 = (bf16[32,2176]{1,0:T(8,128)(2,1)S(1)}, bf16[32,2176]{1,0:T(8,128)(2,1)S(1)}, u32[]{:S(2)}, u32[]{:S(2)}) collective-permute-start(bf16[32,2176]{1,0:T(8,128)(2,1)S(1)} %get-tuple-element.88), channel_id=1, source_target_pairs={{0,6},{1,7},{2,4},{3,5},{4,2},{5,3},{6,0},{7,1},{8,14},{9,15},{10,... | collective-permute-start | bytes 417800 | tf_op jit(solution)/shard_map/ppermute | solution.py:77
  72.5 1.2 %collective-permute-start.30 = (bf16[32,2176]{1,0:T(8,128)(2,1)S(1)}, bf16[32,2176]{1,0:T(8,128)(2,1)S(1)}, u32[]{:S(2)}, u32[]{:S(2)}) collective-permute-start(bf16[32,2176]{1,0:T(8,128)(2,1)S(1)} %get-tuple-element.99), channel_id=1, source_target_pairs={{0,2},{1,3},{2,0},{3,1},{4,6},{5,7},{6,4},{7,5},{8,10},{9,11},{10,... | collective-permute-start | bytes 417800 | tf_op jit(solution)/shard_map/ppermute | solution.py:77
  74.4 1.2 %collective-permute-start.31 = (bf16[32,2176]{1,0:T(8,128)(2,1)S(1)}, bf16[32,2176]{1,0:T(8,128)(2,1)S(1)}, u32[]{:S(2)}, u32[]{:S(2)}) collective-permute-start(bf16[32,2176]{1,0:T(8,128)(2,1)S(1)} %get-tuple-element.100), channel_id=1, source_target_pairs={{0,6},{1,7},{2,4},{3,5},{4,2},{5,3},{6,0},{7,1},{8,14},{9,15},{10,... | collective-permute-start | bytes 417800 | tf_op jit(solution)/shard_map/ppermute | solution.py:77
  75.7 2.0 %collective-permute-done.23.refs_3_ = bf16[32,2176]{1,0:T(8,128)(2,1)S(1)} collective-permute-done((bf16[32,2176]{1,0:T(8,128)(2,1)S(1)}, bf16[32,2176]{1,0:T(8,128)(2,1)S(1)}, u32[]{:S(2)}, u32[]{:S(2)}) %collective-permute-start.23) | collective-permute-done | bytes 139296 | tf_op jit(solution)/shard_map/ppermute | solution.py:77
  78.0 2.6 %collective-permute-start.32 = (bf16[48,2176]{1,0:T(8,128)(2,1)S(1)}, bf16[48,2176]{1,0:T(8,128)(2,1)S(1)}, u32[]{:S(2)}, u32[]{:S(2)}) collective-permute-start(bf16[48,2176]{1,0:T(8,128)(2,1)S(1)} %get-tuple-element.102), channel_id=1, source_target_pairs={{0,8},{1,9},{2,10},{3,11},{4,12},{5,13},{6,14},{7,15},{8,0},{9,1},... | collective-permute-start | bytes 626696 | tf_op jit(solution)/shard_map/ppermute | solution.py:77
  80.6 6.5 %collective-permute-done.31.refs_3_ = bf16[32,2176]{1,0:T(8,128)(2,1)S(1)} collective-permute-done((bf16[32,2176]{1,0:T(8,128)(2,1)S(1)}, bf16[32,2176]{1,0:T(8,128)(2,1)S(1)}, u32[]{:S(2)}, u32[]{:S(2)}) %collective-permute-start.31) | collective-permute-done | bytes 139296 | tf_op jit(solution)/shard_map/ppermute | solution.py:77
  87.5 5.2 %collective-permute-done.33.refs_5_ = bf16[16,2176]{1,0:T(8,128)(2,1)S(1)} collective-permute-done((bf16[16,2176]{1,0:T(8,128)(2,1)S(1)}, bf16[16,2176]{1,0:T(8,128)(2,1)S(1)}, u32[]{:S(2)}, u32[]{:S(2)}) %collective-permute-start.33) | collective-permute-done | bytes 69664 | tf_op jit(solution)/shard_map/ppermute | solution.py:77
  92.7 1.1 %finish.1 = (f32[32,2048]{1,0:T(8,128)}, f32[32,2048]{1,0:T(8,128)}) custom-call(f32[2,8,2176]{2,1,0:T(8,128)S(1)} %get-tuple-element.66.rest_0_.refs_0_, f32[2,8,2176]{2,1,0:T(8,128)S(1)} %get-tuple-element.78.rest_1_.refs_1_, f32[2,8,2176]{2,1,0:T(8,128)S(1)} %get-tuple-element.90.refs_2_, f32[2,8,2176]{2,1,0:T(8,128)S(1)} %get-tuple-element.101.refs_3_, ...), custom_call_target="tpu_custom_call" | custom-call | flops 110000000 | tf_op jit(solution)/shard_map/finish/pallas_call | solution.py:349
  (64 shorter events, 10.6 us)
Async XLA Ops:
  1.9 21.4 %collective-permute-start = (bf16[2,128,1024]{2,1,0:T(8,128)(2,1)S(1)}, bf16[2,128,1024]{2,1,0:T(8,128)(2,1)S(1)}, u32[]{:S(2)}, u32[]{:S(2)}) collective-permute-start(bf16[2,128,1024]{2,1,0:T(8,128)(2,1)S(1)} %get-tuple-element.53), channel_id=1, source_target_pairs={{0,16},{16,0},{1,17},{17,1},{2,18},{18,2},{3,19},{19,3},{4,20},{20... | collective-permute-start | bytes 1572872 | tf_op jit(solution)/shard_map/ppermute | solution.py:77
  4.9 34.0 %collective-permute-start.8 = (bf16[2,128,1024]{2,1,0:T(8,128)(2,1)S(1)}, bf16[2,128,1024]{2,1,0:T(8,128)(2,1)S(1)}, u32[]{:S(2)}, u32[]{:S(2)}) collective-permute-start(bf16[2,128,1024]{2,1,0:T(8,128)(2,1)S(1)} %get-tuple-element.67), channel_id=1, source_target_pairs={{0,16},{16,0},{1,17},{17,1},{2,18},{18,2},{3,19},{19,3},{4,20},{20... | collective-permute-start | bytes 1572872 | tf_op jit(solution)/shard_map/ppermute | solution.py:77
  33.9 2.4 %collective-permute-start.1 = (bf16[32,2176]{1,0:T(8,128)(2,1)S(1)}, bf16[32,2176]{1,0:T(8,128)(2,1)S(1)}, u32[]{:S(2)}, u32[]{:S(2)}) collective-permute-start(bf16[32,2176]{1,0:T(8,128)(2,1)S(1)} %get-tuple-element.58), channel_id=1, source_target_pairs={{0,1},{1,0},{2,3},{3,2},{4,5},{5,4},{6,7},{7,6},{8,9},{9,8},{10,11... | collective-permute-start | bytes 417800 | tf_op jit(solution)/shard_map/ppermute | solution.py:77
  33.9 4.3 %collective-permute-start.2 = (bf16[32,2176]{1,0:T(8,128)(2,1)S(1)}, bf16[32,2176]{1,0:T(8,128)(2,1)S(1)}, u32[]{:S(2)}, u32[]{:S(2)}) collective-permute-start(bf16[32,2176]{1,0:T(8,128)(2,1)S(1)} %get-tuple-element.59), channel_id=1, source_target_pairs={{0,1},{1,0},{2,3},{3,2},{4,5},{5,4},{6,7},{7,6},{8,9},{9,8},{10,11... | collective-permute-start | bytes 417800 | tf_op jit(solution)/shard_map/ppermute | solution.py:77
  34.4 3.8 %collective-permute-start.3 = (bf16[32,2176]{1,0:T(8,128)(2,1)S(1)}, bf16[32,2176]{1,0:T(8,128)(2,1)S(1)}, u32[]{:S(2)}, u32[]{:S(2)}) collective-permute-start(bf16[32,2176]{1,0:T(8,128)(2,1)S(1)} %get-tuple-element.60), channel_id=1, source_target_pairs={{0,1},{1,0},{2,3},{3,2},{4,5},{5,4},{6,7},{7,6},{8,9},{9,8},{10,11... | collective-permute-start | bytes 417800 | tf_op jit(solution)/shard_map/ppermute | solution.py:77
  34.5 3.7 %collective-permute-start.4 = (bf16[32,2176]{1,0:T(8,128)(2,1)S(1)}, bf16[32,2176]{1,0:T(8,128)(2,1)S(1)}, u32[]{:S(2)}, u32[]{:S(2)}) collective-permute-start(bf16[32,2176]{1,0:T(8,128)(2,1)S(1)} %get-tuple-element.61), channel_id=1, source_target_pairs={{0,1},{1,0},{2,3},{3,2},{4,5},{5,4},{6,7},{7,6},{8,9},{9,8},{10,11... | collective-permute-start | bytes 417800 | tf_op jit(solution)/shard_map/ppermute | solution.py:77
  36.2 19.9 %collective-permute-start.16 = (bf16[2,128,1024]{2,1,0:T(8,128)(2,1)S(1)}, bf16[2,128,1024]{2,1,0:T(8,128)(2,1)S(1)}, u32[]{:S(2)}, u32[]{:S(2)}) collective-permute-start(bf16[2,128,1024]{2,1,0:T(8,128)(2,1)S(1)} %get-tuple-element.79), channel_id=1, source_target_pairs={{0,16},{16,0},{1,17},{17,1},{2,18},{18,2},{3,19},{19,3},{4,20},{20... | collective-permute-start | bytes 1572872 | tf_op jit(solution)/shard_map/ppermute | solution.py:77
  41.9 1.5 %collective-permute-start.10 = (bf16[32,2176]{1,0:T(8,128)(2,1)S(1)}, bf16[32,2176]{1,0:T(8,128)(2,1)S(1)}, u32[]{:S(2)}, u32[]{:S(2)}) collective-permute-start(bf16[32,2176]{1,0:T(8,128)(2,1)S(1)} %get-tuple-element.70), channel_id=1, source_target_pairs={{0,1},{1,0},{2,3},{3,2},{4,5},{5,4},{6,7},{7,6},{8,9},{9,8},{10,11... | collective-permute-start | bytes 417800 | tf_op jit(solution)/shard_map/ppermute | solution.py:77
  42.4 2.9 %collective-permute-start.11 = (bf16[32,2176]{1,0:T(8,128)(2,1)S(1)}, bf16[32,2176]{1,0:T(8,128)(2,1)S(1)}, u32[]{:S(2)}, u32[]{:S(2)}) collective-permute-start(bf16[32,2176]{1,0:T(8,128)(2,1)S(1)} %get-tuple-element.71), channel_id=1, source_target_pairs={{0,1},{1,0},{2,3},{3,2},{4,5},{5,4},{6,7},{7,6},{8,9},{9,8},{10,11... | collective-permute-start | bytes 417800 | tf_op jit(solution)/shard_map/ppermute | solution.py:77
  42.5 4.4 %collective-permute-start.12 = (bf16[32,2176]{1,0:T(8,128)(2,1)S(1)}, bf16[32,2176]{1,0:T(8,128)(2,1)S(1)}, u32[]{:S(2)}, u32[]{:S(2)}) collective-permute-start(bf16[32,2176]{1,0:T(8,128)(2,1)S(1)} %get-tuple-element.72), channel_id=1, source_target_pairs={{0,1},{1,0},{2,3},{3,2},{4,5},{5,4},{6,7},{7,6},{8,9},{9,8},{10,11... | collective-permute-start | bytes 417800 | tf_op jit(solution)/shard_map/ppermute | solution.py:77
  43.2 20.6 %collective-permute-start.24 = (bf16[2,128,1024]{2,1,0:T(8,128)(2,1)S(1)}, bf16[2,128,1024]{2,1,0:T(8,128)(2,1)S(1)}, u32[]{:S(2)}, u32[]{:S(2)}) collective-permute-start(bf16[2,128,1024]{2,1,0:T(8,128)(2,1)S(1)} %get-tuple-element.91), channel_id=1, source_target_pairs={{0,16},{16,0},{1,17},{17,1},{2,18},{18,2},{3,19},{19,3},{4,20},{20... | collective-permute-start | bytes 1572872 | tf_op jit(solution)/shard_map/ppermute | solution.py:77
  43.4 6.3 %collective-permute-start.5 = (bf16[32,2176]{1,0:T(8,128)(2,1)S(1)}, bf16[32,2176]{1,0:T(8,128)(2,1)S(1)}, u32[]{:S(2)}, u32[]{:S(2)}) collective-permute-start(bf16[32,2176]{1,0:T(8,128)(2,1)S(1)} %get-tuple-element.63), channel_id=1, source_target_pairs={{0,4},{1,5},{2,6},{3,7},{4,0},{5,1},{6,2},{7,3},{8,12},{9,13},{10,... | collective-permute-start | bytes 417800 | tf_op jit(solution)/shard_map/ppermute | solution.py:77
  45.3 8.0 %collective-permute-start.6 = (bf16[32,2176]{1,0:T(8,128)(2,1)S(1)}, bf16[32,2176]{1,0:T(8,128)(2,1)S(1)}, u32[]{:S(2)}, u32[]{:S(2)}) collective-permute-start(bf16[32,2176]{1,0:T(8,128)(2,1)S(1)} %get-tuple-element.64), channel_id=1, source_target_pairs={{0,2},{1,3},{2,0},{3,1},{4,6},{5,7},{6,4},{7,5},{8,10},{9,11},{10,... | collective-permute-start | bytes 417800 | tf_op jit(solution)/shard_map/ppermute | solution.py:77
  46.8 8.9 %collective-permute-start.7 = (bf16[32,2176]{1,0:T(8,128)(2,1)S(1)}, bf16[32,2176]{1,0:T(8,128)(2,1)S(1)}, u32[]{:S(2)}, u32[]{:S(2)}) collective-permute-start(bf16[32,2176]{1,0:T(8,128)(2,1)S(1)} %get-tuple-element.65), channel_id=1, source_target_pairs={{0,6},{1,7},{2,4},{3,5},{4,2},{5,3},{6,0},{7,1},{8,14},{9,15},{10,... | collective-permute-start | bytes 417800 | tf_op jit(solution)/shard_map/ppermute | solution.py:77
  49.7 9.3 %collective-permute-start.13 = (bf16[32,2176]{1,0:T(8,128)(2,1)S(1)}, bf16[32,2176]{1,0:T(8,128)(2,1)S(1)}, u32[]{:S(2)}, u32[]{:S(2)}) collective-permute-start(bf16[32,2176]{1,0:T(8,128)(2,1)S(1)} %get-tuple-element.74), channel_id=1, source_target_pairs={{0,4},{1,5},{2,6},{3,7},{4,0},{5,1},{6,2},{7,3},{8,12},{9,13},{10,... | collective-permute-start | bytes 417800 | tf_op jit(solution)/shard_map/ppermute | solution.py:77
  53.3 6.6 %collective-permute-start.14 = (bf16[32,2176]{1,0:T(8,128)(2,1)S(1)}, bf16[32,2176]{1,0:T(8,128)(2,1)S(1)}, u32[]{:S(2)}, u32[]{:S(2)}) collective-permute-start(bf16[32,2176]{1,0:T(8,128)(2,1)S(1)} %get-tuple-element.75), channel_id=1, source_target_pairs={{0,2},{1,3},{2,0},{3,1},{4,6},{5,7},{6,4},{7,5},{8,10},{9,11},{10,... | collective-permute-start | bytes 417800 | tf_op jit(solution)/shard_map/ppermute | solution.py:77
  55.8 6.0 %collective-permute-start.15 = (bf16[32,2176]{1,0:T(8,128)(2,1)S(1)}, bf16[32,2176]{1,0:T(8,128)(2,1)S(1)}, u32[]{:S(2)}, u32[]{:S(2)}) collective-permute-start(bf16[32,2176]{1,0:T(8,128)(2,1)S(1)} %get-tuple-element.76), channel_id=1, source_target_pairs={{0,6},{1,7},{2,4},{3,5},{4,2},{5,3},{6,0},{7,1},{8,14},{9,15},{10,... | collective-permute-start | bytes 417800 | tf_op jit(solution)/shard_map/ppermute | solution.py:77
  59.0 3.1 %collective-permute-start.17 = (bf16[32,2176]{1,0:T(8,128)(2,1)S(1)}, bf16[32,2176]{1,0:T(8,128)(2,1)S(1)}, u32[]{:S(2)}, u32[]{:S(2)}) collective-permute-start(bf16[32,2176]{1,0:T(8,128)(2,1)S(1)} %get-tuple-element.81), channel_id=1, source_target_pairs={{0,1},{1,0},{2,3},{3,2},{4,5},{5,4},{6,7},{7,6},{8,9},{9,8},{10,11... | collective-permute-start | bytes 417800 | tf_op jit(solution)/shard_map/ppermute | solution.py:77
  59.1 3.0 %collective-permute-start.18 = (bf16[32,2176]{1,0:T(8,128)(2,1)S(1)}, bf16[32,2176]{1,0:T(8,128)(2,1)S(1)}, u32[]{:S(2)}, u32[]{:S(2)}) collective-permute-start(bf16[32,2176]{1,0:T(8,128)(2,1)S(1)} %get-tuple-element.82), channel_id=1, source_target_pairs={{0,1},{1,0},{2,3},{3,2},{4,5},{5,4},{6,7},{7,6},{8,9},{9,8},{10,11... | collective-permute-start | bytes 417800 | tf_op jit(solution)/shard_map/ppermute | solution.py:77
  59.9 2.2 %collective-permute-start.19 = (bf16[32,2176]{1,0:T(8,128)(2,1)S(1)}, bf16[32,2176]{1,0:T(8,128)(2,1)S(1)}, u32[]{:S(2)}, u32[]{:S(2)}) collective-permute-start(bf16[32,2176]{1,0:T(8,128)(2,1)S(1)} %get-tuple-element.83), channel_id=1, source_target_pairs={{0,1},{1,0},{2,3},{3,2},{4,5},{5,4},{6,7},{7,6},{8,9},{9,8},{10,11... | collective-permute-start | bytes 417800 | tf_op jit(solution)/shard_map/ppermute | solution.py:77
  66.8 1.4 %collective-permute-start.25 = (bf16[32,2176]{1,0:T(8,128)(2,1)S(1)}, bf16[32,2176]{1,0:T(8,128)(2,1)S(1)}, u32[]{:S(2)}, u32[]{:S(2)}) collective-permute-start(bf16[32,2176]{1,0:T(8,128)(2,1)S(1)} %get-tuple-element.93), channel_id=1, source_target_pairs={{0,1},{1,0},{2,3},{3,2},{4,5},{5,4},{6,7},{7,6},{8,9},{9,8},{10,11... | collective-permute-start | bytes 417800 | tf_op jit(solution)/shard_map/ppermute | solution.py:77
  67.0 2.4 %collective-permute-start.26 = (bf16[32,2176]{1,0:T(8,128)(2,1)S(1)}, bf16[32,2176]{1,0:T(8,128)(2,1)S(1)}, u32[]{:S(2)}, u32[]{:S(2)}) collective-permute-start(bf16[32,2176]{1,0:T(8,128)(2,1)S(1)} %get-tuple-element.94), channel_id=1, source_target_pairs={{0,1},{1,0},{2,3},{3,2},{4,5},{5,4},{6,7},{7,6},{8,9},{9,8},{10,11... | collective-permute-start | bytes 417800 | tf_op jit(solution)/shard_map/ppermute | solution.py:77
  67.4 4.0 %collective-permute-start.27 = (bf16[32,2176]{1,0:T(8,128)(2,1)S(1)}, bf16[32,2176]{1,0:T(8,128)(2,1)S(1)}, u32[]{:S(2)}, u32[]{:S(2)}) collective-permute-start(bf16[32,2176]{1,0:T(8,128)(2,1)S(1)} %get-tuple-element.95), channel_id=1, source_target_pairs={{0,1},{1,0},{2,3},{3,2},{4,5},{5,4},{6,7},{7,6},{8,9},{9,8},{10,11... | collective-permute-start | bytes 417800 | tf_op jit(solution)/shard_map/ppermute | solution.py:77
  67.5 3.9 %collective-permute-start.28 = (bf16[32,2176]{1,0:T(8,128)(2,1)S(1)}, bf16[32,2176]{1,0:T(8,128)(2,1)S(1)}, u32[]{:S(2)}, u32[]{:S(2)}) collective-permute-start(bf16[32,2176]{1,0:T(8,128)(2,1)S(1)} %get-tuple-element.96), channel_id=1, source_target_pairs={{0,1},{1,0},{2,3},{3,2},{4,5},{5,4},{6,7},{7,6},{8,9},{9,8},{10,11... | collective-permute-start | bytes 417800 | tf_op jit(solution)/shard_map/ppermute | solution.py:77
  67.9 6.5 %collective-permute-start.21 = (bf16[32,2176]{1,0:T(8,128)(2,1)S(1)}, bf16[32,2176]{1,0:T(8,128)(2,1)S(1)}, u32[]{:S(2)}, u32[]{:S(2)}) collective-permute-start(bf16[32,2176]{1,0:T(8,128)(2,1)S(1)} %get-tuple-element.86), channel_id=1, source_target_pairs={{0,4},{1,5},{2,6},{3,7},{4,0},{5,1},{6,2},{7,3},{8,12},{9,13},{10,... | collective-permute-start | bytes 417800 | tf_op jit(solution)/shard_map/ppermute | solution.py:77
  68.2 7.4 %collective-permute-start.22 = (bf16[32,2176]{1,0:T(8,128)(2,1)S(1)}, bf16[32,2176]{1,0:T(8,128)(2,1)S(1)}, u32[]{:S(2)}, u32[]{:S(2)}) collective-permute-start(bf16[32,2176]{1,0:T(8,128)(2,1)S(1)} %get-tuple-element.87), channel_id=1, source_target_pairs={{0,2},{1,3},{2,0},{3,1},{4,6},{5,7},{6,4},{7,5},{8,10},{9,11},{10,... | collective-permute-start | bytes 417800 | tf_op jit(solution)/shard_map/ppermute | solution.py:77
  69.4 8.2 %collective-permute-start.23 = (bf16[32,2176]{1,0:T(8,128)(2,1)S(1)}, bf16[32,2176]{1,0:T(8,128)(2,1)S(1)}, u32[]{:S(2)}, u32[]{:S(2)}) collective-permute-start(bf16[32,2176]{1,0:T(8,128)(2,1)S(1)} %get-tuple-element.88), channel_id=1, source_target_pairs={{0,6},{1,7},{2,4},{3,5},{4,2},{5,3},{6,0},{7,1},{8,14},{9,15},{10,... | collective-permute-start | bytes 417800 | tf_op jit(solution)/shard_map/ppermute | solution.py:77
  72.1 8.5 %collective-permute-start.29 = (bf16[32,2176]{1,0:T(8,128)(2,1)S(1)}, bf16[32,2176]{1,0:T(8,128)(2,1)S(1)}, u32[]{:S(2)}, u32[]{:S(2)}) collective-permute-start(bf16[32,2176]{1,0:T(8,128)(2,1)S(1)} %get-tuple-element.98), channel_id=1, source_target_pairs={{0,4},{1,5},{2,6},{3,7},{4,0},{5,1},{6,2},{7,3},{8,12},{9,13},{10,... | collective-permute-start | bytes 417800 | tf_op jit(solution)/shard_map/ppermute | solution.py:77
  72.5 8.1 %collective-permute-start.30 = (bf16[32,2176]{1,0:T(8,128)(2,1)S(1)}, bf16[32,2176]{1,0:T(8,128)(2,1)S(1)}, u32[]{:S(2)}, u32[]{:S(2)}) collective-permute-start(bf16[32,2176]{1,0:T(8,128)(2,1)S(1)} %get-tuple-element.99), channel_id=1, source_target_pairs={{0,2},{1,3},{2,0},{3,1},{4,6},{5,7},{6,4},{7,5},{8,10},{9,11},{10,... | collective-permute-start | bytes 417800 | tf_op jit(solution)/shard_map/ppermute | solution.py:77
  74.4 12.7 %collective-permute-start.31 = (bf16[32,2176]{1,0:T(8,128)(2,1)S(1)}, bf16[32,2176]{1,0:T(8,128)(2,1)S(1)}, u32[]{:S(2)}, u32[]{:S(2)}) collective-permute-start(bf16[32,2176]{1,0:T(8,128)(2,1)S(1)} %get-tuple-element.100), channel_id=1, source_target_pairs={{0,6},{1,7},{2,4},{3,5},{4,2},{5,3},{6,0},{7,1},{8,14},{9,15},{10,... | collective-permute-start | bytes 417800 | tf_op jit(solution)/shard_map/ppermute | solution.py:77
  78.0 14.7 %collective-permute-start.32 = (bf16[48,2176]{1,0:T(8,128)(2,1)S(1)}, bf16[48,2176]{1,0:T(8,128)(2,1)S(1)}, u32[]{:S(2)}, u32[]{:S(2)}) collective-permute-start(bf16[48,2176]{1,0:T(8,128)(2,1)S(1)} %get-tuple-element.102), channel_id=1, source_target_pairs={{0,8},{1,9},{2,10},{3,11},{4,12},{5,13},{6,14},{7,15},{8,0},{9,1},... | collective-permute-start | bytes 626696 | tf_op jit(solution)/shard_map/ppermute | solution.py:77
  87.4 5.3 %collective-permute-start.33 = (bf16[16,2176]{1,0:T(8,128)(2,1)S(1)}, bf16[16,2176]{1,0:T(8,128)(2,1)S(1)}, u32[]{:S(2)}, u32[]{:S(2)}) collective-permute-start(bf16[16,2176]{1,0:T(8,128)(2,1)S(1)} %get-tuple-element.103), channel_id=1, source_target_pairs={{0,8},{1,9},{2,10},{3,11},{4,12},{5,13},{6,14},{7,15},{8,0},{9,1},... | collective-permute-start | bytes 208904 | tf_op jit(solution)/shard_map/ppermute | solution.py:77
  (8 other events, 17.8 us)

commit v6 on v5

--- a/solution.py
+++ b/solution.py
@@ -9,6 +9,7 @@
 
 PIECES = 4
 SPLIT = 4
+JOINT = 2
 
 
 def product(left, right):
@@ -172,7 +173,7 @@
     )(inverse, kinetic)
 
 
-def near_kernel(chunk, tile, virt_ref, inverse_ref, kinetic_ref, values_ref, laps_ref, out_ref, far_values, far_laps, near_values, near_laps, own_inverse, own_kinetic, sems):
+def near_kernel(chunk, tile, virt_ref, energy_ref, inverse_ref, kinetic_ref, values_ref, laps_ref, out_ref, far_values, far_laps, near_values, near_laps, own_inverse, own_kinetic, sems):
     count, per, depth = inverse_ref.shape
     height = count * per
     width = out_ref.shape[3]
@@ -219,7 +220,7 @@
         copy.wait()
 
 
-def near_product(virt, inverse, kinetic, values, laplacians):
+def near_product(virt, energy, inverse, kinetic, values, laplacians):
     count, per, depth = inverse.shape
     width = values.shape[1]
     chunk, tile = 512, 256
@@ -228,13 +229,13 @@
     return pl.pallas_call(
         functools.partial(near_kernel, chunk, tile),
         out_shape=(jax.ShapeDtypeStruct((2, count, per, width), jnp.float32), table, table),
-        in_specs=[SCALAR, HELD, HELD, HELD, HELD],
+        in_specs=[SCALAR, SCALAR, HELD, HELD, HELD, HELD],
         out_specs=(WHOLE, WHOLE, WHOLE),
         scratch_shapes=[table, table, own, own, pltpu.SemaphoreType.DMA((width // chunk + 2, 2))],
         compiler_params=limit(24),
         cost_estimate=cost(9),
         name="near_product",
-    )(virt, inverse, kinetic, values, laplacians)
+    )(virt, energy, inverse, kinetic, values, laplacians)
 
 
 def far_kernel(weights, count, tile, first, virt_ref, me_ref, energy_ref, far_ref, near_ref, values_ref, laps_ref, *rest):
@@ -290,10 +291,10 @@
     return [sends], keep
 
 
-def combine_kernel(parts, senders, carried, *refs):
+def combine_kernel(parts, senders, carried, ordered, *refs):
     keep_ref, refs = refs[0], refs[1:]
     came_refs = [refs[parts * sender : parts * sender + parts] for sender in range(senders)]
-    refs = refs[parts * senders :]
+    refs = refs[parts * senders + ordered :]
     kept_ref, send_refs = refs[carried], refs[carried + 1 :]
     width = keep_ref.shape[2] - EXTRA
     sums, energy = add_came(keep_ref, came_refs)
@@ -311,29 +312,32 @@
         store_coded([send_ref], [block for blocks in sums for block in blocks[first : first + kept]], energy)
 
 
-def combine(keep, came, sent, carry=()):
+def combine(keep, came, sent, carry, after):
     _, height, width = keep.shape
     kept = height // (sent + 1)
     parts, senders = len(came[0]), len(came)
     above = sum(array.shape[0] for array in carry)
     keep, *sends = pl.pallas_call(
-        functools.partial(combine_kernel, parts, senders, len(carry)),
+        functools.partial(combine_kernel, parts, senders, len(carry), len(after)),
         out_shape=(jax.ShapeDtypeStruct((2, kept, width), jnp.float32),)
         + (jax.ShapeDtypeStruct((above + 2 * kept, width), jnp.bfloat16),) * sent,
-        in_specs=[WHOLE] * (1 + parts * senders + len(carry)),
+        in_specs=[WHOLE] * (1 + parts * senders) + [ANYWHERE] * len(after) + [WHOLE] * len(carry),
         out_specs=(WHOLE,) * (1 + sent),
         compiler_params=limit(8),
         cost_estimate=cost(0.1),
         name="combine",
-    )(keep, *[part for parts in came for part in parts], *carry)
+    )(keep, *[part for parts in came for part in parts], *after, *carry)
     return [[send] for send in sends], keep
 
 
-def finish_kernel(count, *refs):
-    keep_refs, (early_ref, late_ref, gradient_ref, log_ref) = refs[:-4], refs[-4:]
+def finish_kernel(count, joint, *refs):
+    (gradient_ref, log_ref), refs = refs[-2:], refs[:-2]
+    groups = len(refs) // (joint + 1)
+    keep_refs, came_refs = refs[: joint * groups], refs[joint * groups :]
     row = 0
     for piece, keep_ref in enumerate(keep_refs):
-        came = early_ref.at[16 * piece : 16 * piece + 16, :] if piece + 1 < len(keep_refs) else late_ref
+        place = 16 * (piece % joint)
+        came = came_refs[piece // joint].at[place : place + 16, :]
         (gradient, log), energy = add_came(keep_ref, [[came]])
         correction = 2.0 * (energy[:, :1] / count - OFFSET)
         for block in range(len(log)):
@@ -343,18 +347,18 @@
             row += 8
 
 
-def finish(keeps, early, late, count):
+def finish(keeps, came, count):
     _, rows, width = keeps[0].shape
     out = jax.ShapeDtypeStruct((rows * len(keeps), width - EXTRA), jnp.float32)
     return pl.pallas_call(
-        functools.partial(finish_kernel, count),
+        functools.partial(finish_kernel, count, JOINT),
         out_shape=(out, out),
-        in_specs=[WHOLE] * (len(keeps) + 2),
+        in_specs=[WHOLE] * (len(keeps) + len(came)),
         out_specs=(WHOLE, WHOLE),
         compiler_params=limit(8),
         cost_estimate=cost(0.1),
         name="finish",
-    )(*keeps, early, late)
+    )(*keeps, *came)
 
 
 def pieced_body(pieces, tile, inverse_rows, kinetic_rows, virt_values, virt_laplacians, local_energy):
@@ -374,29 +378,29 @@
     theirs = []
     for group in range(pieces // 2):
         theirs += [swap(mine, "virt", 1) for mine in cut(inverse, kinetic, group)]
-    near, values, laplacians = near_product(virt, inverse, kinetic, values, laplacians)
-
-    send, keep, done = {}, {}, [0] * pieces
-    carry = ()
+    near, values, laplacians = near_product(virt, local_energy, inverse, kinetic, values, laplacians)
+
+    keep, first, came = {}, {}, []
+    late, carry = [], ()
     for turn in range(pieces + 1):
         if turn < pieces:
-            after = [keep[other] for other in sorted(keep)]
-            send[turn], keep[turn] = far_product(
+            after = [keep[turn - 1]] if turn else []
+            send, kept = far_product(
                 virt, me, local_energy, theirs[turn], near, turn * rows, values, laplacians, tile, stages, after
             )
-        for piece in (turn - 1, turn):
-            if not 0 <= piece < pieces:
-                continue
-            masks = partners(stages[done[piece]])
-            came = [[swap(part, "walk", mask) for part in parts] for parts, mask in zip(send[piece], masks)]
-            done[piece] += 1
-            sent = len(partners(stages[done[piece]]))
-            joins = carry if done[piece] == 2 and piece + 1 < pieces else ()
-            send[piece], keep[piece] = combine(keep[piece], came, sent, joins)
-            if done[piece] == 2 and piece + 1 < pieces:
-                carry = tuple(send[piece][0])
-    early, late = (swap(array, "walk", stages[2][0]) for array in (carry[0], send[pieces - 1][0][0]))
-    return finish([keep[piece] for piece in range(pieces)], early, late, count)
+            first[turn] = [[swap(part, "walk", mask) for part in parts] for parts, mask in zip(send, partners(stages[0]))]
+        if turn:
+            piece = turn - 1
+            sends, keep[piece] = combine(keep[piece], second, len(partners(stages[2])), carry, [])
+            carry = tuple(sends[0])
+            if turn % JOINT == 0:
+                came.append(swap(carry[0], "walk", stages[2][0]))
+                carry = ()
+        if turn < pieces:
+            after = ([keep[turn - 1]] if turn else [])
+            sends, keep[turn] = combine(kept, first[turn], len(partners(stages[1])), (), after)
+            second = [[swap(part, "walk", mask) for part in parts] for parts, mask in zip(sends, partners(stages[1]))]
+    return finish([keep[piece] for piece in range(pieces)], came, count)
 
 
 def solution(mesh):

time: 94.1 us -> 97.1 us (1.032)
  waiting for transfers between devices: 22 us -> 24.4 us
    ppermute x34, waiting for transfers between devices: 22 us -> 24.4 us  [swap(): return lax.ppermute(array, axis, pairs)]
  transfers between devices with their start and end apart: 34 -> 34, of which waited for: 12 -> 10; matrix products, arithmetic and copies ran while one was open for 0% -> 0% of each run, Pallas kernels for 26% -> 27%
where the time goes in v6:
time: 97.1 us; the launch traced here: 96.8 us
  Pallas kernels  29.6 us (30%)
  starting transfers between devices  26.3 us (27%)
  waiting for transfers between devices  24.4 us (25%)
  local copies, waits for them, and re-layouts  15.1 us (16%)
  between operations  1.53 us (2%)
    ppermute x34, starting transfers between devices, swap(): return lax.ppermute(array, axis, pairs)  26.3 us
    ppermute x34, waiting for transfers between devices, swap(): return lax.ppermute(array, axis, pairs)  24.4 us
    unnamed x12, local copies, waits for them, and re-layouts  15.1 us
    pallas_call x4, Pallas kernels, far_product(): pl.pallas_call(functools.partial(far_kernel, place_weights(stages), count...  11.5 us
    pallas_call x1, Pallas kernels, near_product(): pl.pallas_call(functools.partial(near_kernel, chunk, tile), out_shape=(ja...  10.3 us
    pallas_call x8, Pallas kernels, combine(): pl.pallas_call(functools.partial(combine_kernel, parts, senders, len(carr...  4.17 us
    pallas_call x2, Pallas kernels, cut(): pl.pallas_call(cut_kernel, out_shape=(out, out), grid=(1,), in_specs=[blo...  2.55 us
  transfers between devices with their start and end apart: 34, of which 10 were waited for; matrix products, arithmetic and copies ran while one was open for 0% of the time, Pallas kernels for 27%

profile of v6, /device:TPU:0, one launch (start us, length us, event | category | flops | bytes accessed | tf_op | source)
XLA Modules:
  0.0 96.8 jit_solution(17712568068122978118)
XLA Ops:
  0.6 1.3 %cut.2 = (bf16[2,128,1024]{2,1,0:T(8,128)(2,1)S(1)}, bf16[2,128,1024]{2,1,0:T(8,128)(2,1)S(1)}) custom-call(bf16[16,32,1024]{2,1,0:T(8,128)(2,1)} %bitcast.6, bf16[16,32,1024]{2,1,0:T(8,128)(2,1)} %bitcast.9), custom_call_target="tpu_custom_call" | custom-call | flops 110000000 | tf_op jit(solution)/shard_map/cut/pallas_call | solution.py:164
  1.9 3.0 %collective-permute-start = (bf16[2,128,1024]{2,1,0:T(8,128)(2,1)S(1)}, bf16[2,128,1024]{2,1,0:T(8,128)(2,1)S(1)}, u32[]{:S(2)}, u32[]{:S(2)}) collective-permute-start(bf16[2,128,1024]{2,1,0:T(8,128)(2,1)S(1)} %get-tuple-element.53), channel_id=1, source_target_pairs={{0,16},{16,0},{1,17},{17,1},{2,18},{18,2},{3,19},{19,3},{4,20},{20... | collective-permute-start | bytes 1572872 | tf_op jit(solution)/shard_map/ppermute | solution.py:78
  5.7 10.3 %near_product.1 = (f32[2,16,32,2048]{3,2,1,0:T(8,128)S(1)}, bf16[1024,2048]{1,0:T(8,128)(2,1)S(1)}, bf16[1024,2048]{1,0:T(8,128)(2,1)S(1)}) custom-call(s32[1]{0:T(128)} %bitcast.virt_ref, f32[1]{0:T(128)S(6)} %copy.7.energy_ref, bf16[16,32,1024]{2,1,0:T(8,128)(2,1)} %bitcast.7, bf16[16,32,1024]{2,1,0:T(8,128)(2,1)} %bitcast.10, ...), custom_call_target="tpu_custom_call" | custom-call | flops 9900000256 | tf_op jit(solution)/shard_map/near_product/pallas_call | solution.py:229
  16.0 3.3 %copy-done = f32[2,16,32,2048]{3,2,1,0:T(8,128)} copy-done((f32[2,16,32,2048]{3,2,1,0:T(8,128)}, f32[2,16,32,2048]{3,2,1,0:T(8,128)S(1)}, u32[]{:S(2)}) %copy-start) | copy-done | bytes 8388632
  19.3 2.1 %copy-done.2 = bf16[1024,2048]{1,0:T(8,128)(2,1)} copy-done((bf16[1024,2048]{1,0:T(8,128)(2,1)}, bf16[1024,2048]{1,0:T(8,128)(2,1)S(1)}, u32[]{:S(2)}) %copy-start.2) | copy-done | bytes 4194328
  21.3 1.9 %copy-done.4 = bf16[1024,2048]{1,0:T(8,128)(2,1)} copy-done((bf16[1024,2048]{1,0:T(8,128)(2,1)}, bf16[1024,2048]{1,0:T(8,128)(2,1)S(1)}, u32[]{:S(2)}) %copy-start.4) | copy-done | bytes 4194328
  23.3 3.4 %copy-done.1 = f32[2,16,32,2048]{3,2,1,0:T(8,128)S(1)} copy-done((f32[2,16,32,2048]{3,2,1,0:T(8,128)S(1)}, f32[2,16,32,2048]{3,2,1,0:T(8,128)}, u32[]{:S(2)}) %copy-start.1) | copy-done | bytes 8388632
  26.7 2.2 %copy-done.3 = bf16[1024,2048]{1,0:T(8,128)(2,1)S(1)} copy-done((bf16[1024,2048]{1,0:T(8,128)(2,1)S(1)}, bf16[1024,2048]{1,0:T(8,128)(2,1)}, u32[]{:S(2)}) %copy-start.3) | copy-done | bytes 4194328
  28.9 2.2 %copy-done.5 = bf16[1024,2048]{1,0:T(8,128)(2,1)S(1)} copy-done((bf16[1024,2048]{1,0:T(8,128)(2,1)S(1)}, bf16[1024,2048]{1,0:T(8,128)(2,1)}, u32[]{:S(2)}) %copy-start.5) | copy-done | bytes 4194328
  31.0 2.8 %far_product.4 = (bf16[32,2176]{1,0:T(8,128)(2,1)S(1)}, bf16[32,2176]{1,0:T(8,128)(2,1)S(1)}, bf16[32,2176]{1,0:T(8,128)(2,1)S(1)}, bf16[32,2176]{1,0:T(8,128)(2,1)S(1)}, f32[2,64,2176]{2,1,0:T(8,128)S(1)}) custom-call(s32[1]{0:T(128)} %bitcast.virt_ref, s32[1]{0:T(128)} %bitcast.1.me_ref, f32[1]{0:T(128)S(6)} %copy.7.energy_ref, ...), custom_call_target="tpu_custom_call" | custom-call | flops 110000000 | tf_op jit(solution)/shard_map/far_product/pallas_call | solution.py:280
  35.0 1.3 %cut.3 = (bf16[2,128,1024]{2,1,0:T(8,128)(2,1)S(1)}, bf16[2,128,1024]{2,1,0:T(8,128)(2,1)S(1)}) custom-call(bf16[16,32,1024]{2,1,0:T(8,128)(2,1)} %bitcast.8, bf16[16,32,1024]{2,1,0:T(8,128)(2,1)} %bitcast.11), custom_call_target="tpu_custom_call" | custom-call | flops 110000000 | tf_op jit(solution)/shard_map/cut/pallas_call | solution.py:164
  36.2 2.0 %collective-permute-start.16 = (bf16[2,128,1024]{2,1,0:T(8,128)(2,1)S(1)}, bf16[2,128,1024]{2,1,0:T(8,128)(2,1)S(1)}, u32[]{:S(2)}, u32[]{:S(2)}) collective-permute-start(bf16[2,128,1024]{2,1,0:T(8,128)(2,1)S(1)} %get-tuple-element.79), channel_id=1, source_target_pairs={{0,16},{16,0},{1,17},{17,1},{2,18},{18,2},{3,19},{19,3},{4,20},{20... | collective-permute-start | bytes 1572872 | tf_op jit(solution)/shard_map/ppermute | solution.py:78
  39.0 1.6 %collective-permute-start.5 = (bf16[32,2176]{1,0:T(8,128)(2,1)S(1)}, bf16[32,2176]{1,0:T(8,128)(2,1)S(1)}, u32[]{:S(2)}, u32[]{:S(2)}) collective-permute-start(bf16[32,2176]{1,0:T(8,128)(2,1)S(1)} %get-tuple-element.63), channel_id=1, source_target_pairs={{0,4},{1,5},{2,6},{3,7},{4,0},{5,1},{6,2},{7,3},{8,12},{9,13},{10,... | collective-permute-start | bytes 417800 | tf_op jit(solution)/shard_map/ppermute | solution.py:78
  40.6 1.5 %collective-permute-start.6 = (bf16[32,2176]{1,0:T(8,128)(2,1)S(1)}, bf16[32,2176]{1,0:T(8,128)(2,1)S(1)}, u32[]{:S(2)}, u32[]{:S(2)}) collective-permute-start(bf16[32,2176]{1,0:T(8,128)(2,1)S(1)} %get-tuple-element.64), channel_id=1, source_target_pairs={{0,2},{1,3},{2,0},{3,1},{4,6},{5,7},{6,4},{7,5},{8,10},{9,11},{10,... | collective-permute-start | bytes 417800 | tf_op jit(solution)/shard_map/ppermute | solution.py:78
  42.5 2.8 %far_product.5 = (bf16[32,2176]{1,0:T(8,128)(2,1)S(1)}, bf16[32,2176]{1,0:T(8,128)(2,1)S(1)}, bf16[32,2176]{1,0:T(8,128)(2,1)S(1)}, bf16[32,2176]{1,0:T(8,128)(2,1)S(1)}, f32[2,64,2176]{2,1,0:T(8,128)S(1)}) custom-call(s32[1]{0:T(128)} %bitcast.virt_ref, s32[1]{0:T(128)} %bitcast.1.me_ref, f32[1]{0:T(128)S(6)} %copy.7.energy_ref, ...), custom_call_target="tpu_custom_call" | custom-call | flops 110000000 | tf_op jit(solution)/shard_map/far_product/pallas_call | solution.py:280
  45.9 2.7 %collective-permute-done.6.refs_2_ = bf16[32,2176]{1,0:T(8,128)(2,1)S(1)} collective-permute-done((bf16[32,2176]{1,0:T(8,128)(2,1)S(1)}, bf16[32,2176]{1,0:T(8,128)(2,1)S(1)}, u32[]{:S(2)}, u32[]{:S(2)}) %collective-permute-start.6) | collective-permute-done | bytes 139296 | tf_op jit(solution)/shard_map/ppermute | solution.py:78
  50.9 1.1 %collective-permute-start.13 = (bf16[32,2176]{1,0:T(8,128)(2,1)S(1)}, bf16[32,2176]{1,0:T(8,128)(2,1)S(1)}, u32[]{:S(2)}, u32[]{:S(2)}) collective-permute-start(bf16[32,2176]{1,0:T(8,128)(2,1)S(1)} %get-tuple-element.74), channel_id=1, source_target_pairs={{0,4},{1,5},{2,6},{3,7},{4,0},{5,1},{6,2},{7,3},{8,12},{9,13},{10,... | collective-permute-start | bytes 417800 | tf_op jit(solution)/shard_map/ppermute | solution.py:78
  53.0 1.5 %collective-permute-start.15 = (bf16[32,2176]{1,0:T(8,128)(2,1)S(1)}, bf16[32,2176]{1,0:T(8,128)(2,1)S(1)}, u32[]{:S(2)}, u32[]{:S(2)}) collective-permute-start(bf16[32,2176]{1,0:T(8,128)(2,1)S(1)} %get-tuple-element.76), channel_id=1, source_target_pairs={{0,6},{1,7},{2,4},{3,5},{4,2},{5,3},{6,0},{7,1},{8,14},{9,15},{10,... | collective-permute-start | bytes 417800 | tf_op jit(solution)/shard_map/ppermute | solution.py:78
  54.5 2.8 %far_product.6 = (bf16[32,2176]{1,0:T(8,128)(2,1)S(1)}, bf16[32,2176]{1,0:T(8,128)(2,1)S(1)}, bf16[32,2176]{1,0:T(8,128)(2,1)S(1)}, bf16[32,2176]{1,0:T(8,128)(2,1)S(1)}, f32[2,64,2176]{2,1,0:T(8,128)S(1)}) custom-call(s32[1]{0:T(128)} %bitcast.virt_ref, s32[1]{0:T(128)} %bitcast.1.me_ref, f32[1]{0:T(128)S(6)} %copy.7.energy_ref, ...), custom_call_target="tpu_custom_call" | custom-call | flops 110000000 | tf_op jit(solution)/shard_map/far_product/pallas_call | solution.py:280
  58.0 2.8 %collective-permute-done.15.refs_3_ = bf16[32,2176]{1,0:T(8,128)(2,1)S(1)} collective-permute-done((bf16[32,2176]{1,0:T(8,128)(2,1)S(1)}, bf16[32,2176]{1,0:T(8,128)(2,1)S(1)}, u32[]{:S(2)}, u32[]{:S(2)}) %collective-permute-start.15) | collective-permute-done | bytes 139296 | tf_op jit(solution)/shard_map/ppermute | solution.py:78
  62.9 1.1 %collective-permute-start.21 = (bf16[32,2176]{1,0:T(8,128)(2,1)S(1)}, bf16[32,2176]{1,0:T(8,128)(2,1)S(1)}, u32[]{:S(2)}, u32[]{:S(2)}) collective-permute-start(bf16[32,2176]{1,0:T(8,128)(2,1)S(1)} %get-tuple-element.86), channel_id=1, source_target_pairs={{0,4},{1,5},{2,6},{3,7},{4,0},{5,1},{6,2},{7,3},{8,12},{9,13},{10,... | collective-permute-start | bytes 417800 | tf_op jit(solution)/shard_map/ppermute | solution.py:78
  63.9 1.5 %collective-permute-start.22 = (bf16[32,2176]{1,0:T(8,128)(2,1)S(1)}, bf16[32,2176]{1,0:T(8,128)(2,1)S(1)}, u32[]{:S(2)}, u32[]{:S(2)}) collective-permute-start(bf16[32,2176]{1,0:T(8,128)(2,1)S(1)} %get-tuple-element.87), channel_id=1, source_target_pairs={{0,2},{1,3},{2,0},{3,1},{4,6},{5,7},{6,4},{7,5},{8,10},{9,11},{10,... | collective-permute-start | bytes 417800 | tf_op jit(solution)/shard_map/ppermute | solution.py:78
  65.5 1.0 %collective-permute-start.23 = (bf16[32,2176]{1,0:T(8,128)(2,1)S(1)}, bf16[32,2176]{1,0:T(8,128)(2,1)S(1)}, u32[]{:S(2)}, u32[]{:S(2)}) collective-permute-start(bf16[32,2176]{1,0:T(8,128)(2,1)S(1)} %get-tuple-element.88), channel_id=1, source_target_pairs={{0,6},{1,7},{2,4},{3,5},{4,2},{5,3},{6,0},{7,1},{8,14},{9,15},{10,... | collective-permute-start | bytes 417800 | tf_op jit(solution)/shard_map/ppermute | solution.py:78
  66.4 3.0 %far_product.7 = (bf16[32,2176]{1,0:T(8,128)(2,1)S(1)}, bf16[32,2176]{1,0:T(8,128)(2,1)S(1)}, bf16[32,2176]{1,0:T(8,128)(2,1)S(1)}, bf16[32,2176]{1,0:T(8,128)(2,1)S(1)}, f32[2,64,2176]{2,1,0:T(8,128)S(1)}) custom-call(s32[1]{0:T(128)} %bitcast.virt_ref, s32[1]{0:T(128)} %bitcast.1.me_ref, f32[1]{0:T(128)S(6)} %copy.7.energy_ref, ...), custom_call_target="tpu_custom_call" | custom-call | flops 110000000 | tf_op jit(solution)/shard_map/far_product/pallas_call | solution.py:280
  70.1 2.4 %collective-permute-done.22.refs_2_ = bf16[32,2176]{1,0:T(8,128)(2,1)S(1)} collective-permute-done((bf16[32,2176]{1,0:T(8,128)(2,1)S(1)}, bf16[32,2176]{1,0:T(8,128)(2,1)S(1)}, u32[]{:S(2)}, u32[]{:S(2)}) %collective-permute-start.22) | collective-permute-done | bytes 139296 | tf_op jit(solution)/shard_map/ppermute | solution.py:78
  74.9 1.7 %collective-permute-start.30 = (bf16[32,2176]{1,0:T(8,128)(2,1)S(1)}, bf16[32,2176]{1,0:T(8,128)(2,1)S(1)}, u32[]{:S(2)}, u32[]{:S(2)}) collective-permute-start(bf16[32,2176]{1,0:T(8,128)(2,1)S(1)} %get-tuple-element.98), channel_id=1, source_target_pairs={{0,2},{1,3},{2,0},{3,1},{4,6},{5,7},{6,4},{7,5},{8,10},{9,11},{10,... | collective-permute-start | bytes 417800 | tf_op jit(solution)/shard_map/ppermute | solution.py:78
  76.6 1.5 %collective-permute-start.31 = (bf16[32,2176]{1,0:T(8,128)(2,1)S(1)}, bf16[32,2176]{1,0:T(8,128)(2,1)S(1)}, u32[]{:S(2)}, u32[]{:S(2)}) collective-permute-start(bf16[32,2176]{1,0:T(8,128)(2,1)S(1)} %get-tuple-element.99), channel_id=1, source_target_pairs={{0,6},{1,7},{2,4},{3,5},{4,2},{5,3},{6,0},{7,1},{8,14},{9,15},{10,... | collective-permute-start | bytes 417800 | tf_op jit(solution)/shard_map/ppermute | solution.py:78
  78.2 2.6 %collective-permute-start.32 = (bf16[32,2176]{1,0:T(8,128)(2,1)S(1)}, bf16[32,2176]{1,0:T(8,128)(2,1)S(1)}, u32[]{:S(2)}, u32[]{:S(2)}) collective-permute-start(bf16[32,2176]{1,0:T(8,128)(2,1)S(1)} %get-tuple-element.102), channel_id=1, source_target_pairs={{0,8},{1,9},{2,10},{3,11},{4,12},{5,13},{6,14},{7,15},{8,0},{9,1},... | collective-permute-start | bytes 417800 | tf_op jit(solution)/shard_map/ppermute | solution.py:78
  80.8 3.4 %collective-permute-done.29.refs_1_ = bf16[32,2176]{1,0:T(8,128)(2,1)S(1)} collective-permute-done((bf16[32,2176]{1,0:T(8,128)(2,1)S(1)}, bf16[32,2176]{1,0:T(8,128)(2,1)S(1)}, u32[]{:S(2)}, u32[]{:S(2)}) %collective-permute-start.29) | collective-permute-done | bytes 139296 | tf_op jit(solution)/shard_map/ppermute | solution.py:78
  84.2 3.1 %collective-permute-done.31.refs_3_ = bf16[32,2176]{1,0:T(8,128)(2,1)S(1)} collective-permute-done((bf16[32,2176]{1,0:T(8,128)(2,1)S(1)}, bf16[32,2176]{1,0:T(8,128)(2,1)S(1)}, u32[]{:S(2)}, u32[]{:S(2)}) %collective-permute-start.31) | collective-permute-done | bytes 139296 | tf_op jit(solution)/shard_map/ppermute | solution.py:78
  88.1 7.6 %collective-permute-done.33.refs_5_ = bf16[32,2176]{1,0:T(8,128)(2,1)S(1)} collective-permute-done((bf16[32,2176]{1,0:T(8,128)(2,1)S(1)}, bf16[32,2176]{1,0:T(8,128)(2,1)S(1)}, u32[]{:S(2)}, u32[]{:S(2)}) %collective-permute-start.33) | collective-permute-done | bytes 139296 | tf_op jit(solution)/shard_map/ppermute | solution.py:78
  95.7 1.1 %finish.1 = (f32[32,2048]{1,0:T(8,128)}, f32[32,2048]{1,0:T(8,128)}) custom-call(f32[2,8,2176]{2,1,0:T(8,128)S(1)} %get-tuple-element.66.refs_5_.refs_0_, f32[2,8,2176]{2,1,0:T(8,128)S(1)} %get-tuple-element.78.refs_5_.refs_1_, f32[2,8,2176]{2,1,0:T(8,128)S(1)} %get-tuple-element.89.refs_5_.refs_2_, f32[2,8,2176]{2,1,0:T(8,128)S(1)} %get-tuple-element.101.refs_3_, ...), custom_call_target="tpu_custom_call" | custom-call | flops 110000000 | tf_op jit(solution)/shard_map/finish/pallas_call | solution.py:353
  (64 shorter events, 12.5 us)
Async XLA Ops:
  1.9 21.4 %collective-permute-start = (bf16[2,128,1024]{2,1,0:T(8,128)(2,1)S(1)}, bf16[2,128,1024]{2,1,0:T(8,128)(2,1)S(1)}, u32[]{:S(2)}, u32[]{:S(2)}) collective-permute-start(bf16[2,128,1024]{2,1,0:T(8,128)(2,1)S(1)} %get-tuple-element.53), channel_id=1, source_target_pairs={{0,16},{16,0},{1,17},{17,1},{2,18},{18,2},{3,19},{19,3},{4,20},{20... | collective-permute-start | bytes 1572872 | tf_op jit(solution)/shard_map/ppermute | solution.py:78
  4.9 37.6 %collective-permute-start.8 = (bf16[2,128,1024]{2,1,0:T(8,128)(2,1)S(1)}, bf16[2,128,1024]{2,1,0:T(8,128)(2,1)S(1)}, u32[]{:S(2)}, u32[]{:S(2)}) collective-permute-start(bf16[2,128,1024]{2,1,0:T(8,128)(2,1)S(1)} %get-tuple-element.67), channel_id=1, source_target_pairs={{0,16},{16,0},{1,17},{17,1},{2,18},{18,2},{3,19},{19,3},{4,20},{20... | collective-permute-start | bytes 1572872 | tf_op jit(solution)/shard_map/ppermute | solution.py:78
  33.9 2.4 %collective-permute-start.1 = (bf16[32,2176]{1,0:T(8,128)(2,1)S(1)}, bf16[32,2176]{1,0:T(8,128)(2,1)S(1)}, u32[]{:S(2)}, u32[]{:S(2)}) collective-permute-start(bf16[32,2176]{1,0:T(8,128)(2,1)S(1)} %get-tuple-element.58), channel_id=1, source_target_pairs={{0,1},{1,0},{2,3},{3,2},{4,5},{5,4},{6,7},{7,6},{8,9},{9,8},{10,11... | collective-permute-start | bytes 417800 | tf_op jit(solution)/shard_map/ppermute | solution.py:78
  33.9 4.3 %collective-permute-start.2 = (bf16[32,2176]{1,0:T(8,128)(2,1)S(1)}, bf16[32,2176]{1,0:T(8,128)(2,1)S(1)}, u32[]{:S(2)}, u32[]{:S(2)}) collective-permute-start(bf16[32,2176]{1,0:T(8,128)(2,1)S(1)} %get-tuple-element.59), channel_id=1, source_target_pairs={{0,1},{1,0},{2,3},{3,2},{4,5},{5,4},{6,7},{7,6},{8,9},{9,8},{10,11... | collective-permute-start | bytes 417800 | tf_op jit(solution)/shard_map/ppermute | solution.py:78
  34.4 3.8 %collective-permute-start.3 = (bf16[32,2176]{1,0:T(8,128)(2,1)S(1)}, bf16[32,2176]{1,0:T(8,128)(2,1)S(1)}, u32[]{:S(2)}, u32[]{:S(2)}) collective-permute-start(bf16[32,2176]{1,0:T(8,128)(2,1)S(1)} %get-tuple-element.60), channel_id=1, source_target_pairs={{0,1},{1,0},{2,3},{3,2},{4,5},{5,4},{6,7},{7,6},{8,9},{9,8},{10,11... | collective-permute-start | bytes 417800 | tf_op jit(solution)/shard_map/ppermute | solution.py:78
  34.5 3.7 %collective-permute-start.4 = (bf16[32,2176]{1,0:T(8,128)(2,1)S(1)}, bf16[32,2176]{1,0:T(8,128)(2,1)S(1)}, u32[]{:S(2)}, u32[]{:S(2)}) collective-permute-start(bf16[32,2176]{1,0:T(8,128)(2,1)S(1)} %get-tuple-element.61), channel_id=1, source_target_pairs={{0,1},{1,0},{2,3},{3,2},{4,5},{5,4},{6,7},{7,6},{8,9},{9,8},{10,11... | collective-permute-start | bytes 417800 | tf_op jit(solution)/shard_map/ppermute | solution.py:78
  36.2 18.2 %collective-permute-start.16 = (bf16[2,128,1024]{2,1,0:T(8,128)(2,1)S(1)}, bf16[2,128,1024]{2,1,0:T(8,128)(2,1)S(1)}, u32[]{:S(2)}, u32[]{:S(2)}) collective-permute-start(bf16[2,128,1024]{2,1,0:T(8,128)(2,1)S(1)} %get-tuple-element.79), channel_id=1, source_target_pairs={{0,16},{16,0},{1,17},{17,1},{2,18},{18,2},{3,19},{19,3},{4,20},{20... | collective-permute-start | bytes 1572872 | tf_op jit(solution)/shard_map/ppermute | solution.py:78
  39.0 6.5 %collective-permute-start.5 = (bf16[32,2176]{1,0:T(8,128)(2,1)S(1)}, bf16[32,2176]{1,0:T(8,128)(2,1)S(1)}, u32[]{:S(2)}, u32[]{:S(2)}) collective-permute-start(bf16[32,2176]{1,0:T(8,128)(2,1)S(1)} %get-tuple-element.63), channel_id=1, source_target_pairs={{0,4},{1,5},{2,6},{3,7},{4,0},{5,1},{6,2},{7,3},{8,12},{9,13},{10,... | collective-permute-start | bytes 417800 | tf_op jit(solution)/shard_map/ppermute | solution.py:78
  40.6 8.1 %collective-permute-start.6 = (bf16[32,2176]{1,0:T(8,128)(2,1)S(1)}, bf16[32,2176]{1,0:T(8,128)(2,1)S(1)}, u32[]{:S(2)}, u32[]{:S(2)}) collective-permute-start(bf16[32,2176]{1,0:T(8,128)(2,1)S(1)} %get-tuple-element.64), channel_id=1, source_target_pairs={{0,2},{1,3},{2,0},{3,1},{4,6},{5,7},{6,4},{7,5},{8,10},{9,11},{10,... | collective-permute-start | bytes 417800 | tf_op jit(solution)/shard_map/ppermute | solution.py:78
  42.1 6.6 %collective-permute-start.7 = (bf16[32,2176]{1,0:T(8,128)(2,1)S(1)}, bf16[32,2176]{1,0:T(8,128)(2,1)S(1)}, u32[]{:S(2)}, u32[]{:S(2)}) collective-permute-start(bf16[32,2176]{1,0:T(8,128)(2,1)S(1)} %get-tuple-element.65), channel_id=1, source_target_pairs={{0,6},{1,7},{2,4},{3,5},{4,2},{5,3},{6,0},{7,1},{8,14},{9,15},{10,... | collective-permute-start | bytes 417800 | tf_op jit(solution)/shard_map/ppermute | solution.py:78
  45.4 3.8 %collective-permute-start.9 = (bf16[32,2176]{1,0:T(8,128)(2,1)S(1)}, bf16[32,2176]{1,0:T(8,128)(2,1)S(1)}, u32[]{:S(2)}, u32[]{:S(2)}) collective-permute-start(bf16[32,2176]{1,0:T(8,128)(2,1)S(1)} %get-tuple-element.69), channel_id=1, source_target_pairs={{0,1},{1,0},{2,3},{3,2},{4,5},{5,4},{6,7},{7,6},{8,9},{9,8},{10,11... | collective-permute-start | bytes 417800 | tf_op jit(solution)/shard_map/ppermute | solution.py:78
  45.4 4.6 %collective-permute-start.10 = (bf16[32,2176]{1,0:T(8,128)(2,1)S(1)}, bf16[32,2176]{1,0:T(8,128)(2,1)S(1)}, u32[]{:S(2)}, u32[]{:S(2)}) collective-permute-start(bf16[32,2176]{1,0:T(8,128)(2,1)S(1)} %get-tuple-element.70), channel_id=1, source_target_pairs={{0,1},{1,0},{2,3},{3,2},{4,5},{5,4},{6,7},{7,6},{8,9},{9,8},{10,11... | collective-permute-start | bytes 417800 | tf_op jit(solution)/shard_map/ppermute | solution.py:78
  48.7 1.4 %collective-permute-start.11 = (bf16[32,2176]{1,0:T(8,128)(2,1)S(1)}, bf16[32,2176]{1,0:T(8,128)(2,1)S(1)}, u32[]{:S(2)}, u32[]{:S(2)}) collective-permute-start(bf16[32,2176]{1,0:T(8,128)(2,1)S(1)} %get-tuple-element.71), channel_id=1, source_target_pairs={{0,1},{1,0},{2,3},{3,2},{4,5},{5,4},{6,7},{7,6},{8,9},{9,8},{10,11... | collective-permute-start | bytes 417800 | tf_op jit(solution)/shard_map/ppermute | solution.py:78
  48.7 1.6 %collective-permute-start.12 = (bf16[32,2176]{1,0:T(8,128)(2,1)S(1)}, bf16[32,2176]{1,0:T(8,128)(2,1)S(1)}, u32[]{:S(2)}, u32[]{:S(2)}) collective-permute-start(bf16[32,2176]{1,0:T(8,128)(2,1)S(1)} %get-tuple-element.72), channel_id=1, source_target_pairs={{0,1},{1,0},{2,3},{3,2},{4,5},{5,4},{6,7},{7,6},{8,9},{9,8},{10,11... | collective-permute-start | bytes 417800 | tf_op jit(solution)/shard_map/ppermute | solution.py:78
  49.2 17.2 %collective-permute-start.24 = (bf16[2,128,1024]{2,1,0:T(8,128)(2,1)S(1)}, bf16[2,128,1024]{2,1,0:T(8,128)(2,1)S(1)}, u32[]{:S(2)}, u32[]{:S(2)}) collective-permute-start(bf16[2,128,1024]{2,1,0:T(8,128)(2,1)S(1)} %get-tuple-element.90), channel_id=1, source_target_pairs={{0,16},{16,0},{1,17},{17,1},{2,18},{18,2},{3,19},{19,3},{4,20},{20... | collective-permute-start | bytes 1572872 | tf_op jit(solution)/shard_map/ppermute | solution.py:78
  50.9 6.6 %collective-permute-start.13 = (bf16[32,2176]{1,0:T(8,128)(2,1)S(1)}, bf16[32,2176]{1,0:T(8,128)(2,1)S(1)}, u32[]{:S(2)}, u32[]{:S(2)}) collective-permute-start(bf16[32,2176]{1,0:T(8,128)(2,1)S(1)} %get-tuple-element.74), channel_id=1, source_target_pairs={{0,4},{1,5},{2,6},{3,7},{4,0},{5,1},{6,2},{7,3},{8,12},{9,13},{10,... | collective-permute-start | bytes 417800 | tf_op jit(solution)/shard_map/ppermute | solution.py:78
  52.0 5.9 %collective-permute-start.14 = (bf16[32,2176]{1,0:T(8,128)(2,1)S(1)}, bf16[32,2176]{1,0:T(8,128)(2,1)S(1)}, u32[]{:S(2)}, u32[]{:S(2)}) collective-permute-start(bf16[32,2176]{1,0:T(8,128)(2,1)S(1)} %get-tuple-element.75), channel_id=1, source_target_pairs={{0,2},{1,3},{2,0},{3,1},{4,6},{5,7},{6,4},{7,5},{8,10},{9,11},{10,... | collective-permute-start | bytes 417800 | tf_op jit(solution)/shard_map/ppermute | solution.py:78
  53.0 7.9 %collective-permute-start.15 = (bf16[32,2176]{1,0:T(8,128)(2,1)S(1)}, bf16[32,2176]{1,0:T(8,128)(2,1)S(1)}, u32[]{:S(2)}, u32[]{:S(2)}) collective-permute-start(bf16[32,2176]{1,0:T(8,128)(2,1)S(1)} %get-tuple-element.76), channel_id=1, source_target_pairs={{0,6},{1,7},{2,4},{3,5},{4,2},{5,3},{6,0},{7,1},{8,14},{9,15},{10,... | collective-permute-start | bytes 417800 | tf_op jit(solution)/shard_map/ppermute | solution.py:78
  57.3 3.9 %collective-permute-start.17 = (bf16[32,2176]{1,0:T(8,128)(2,1)S(1)}, bf16[32,2176]{1,0:T(8,128)(2,1)S(1)}, u32[]{:S(2)}, u32[]{:S(2)}) collective-permute-start(bf16[32,2176]{1,0:T(8,128)(2,1)S(1)} %get-tuple-element.81), channel_id=1, source_target_pairs={{0,1},{1,0},{2,3},{3,2},{4,5},{5,4},{6,7},{7,6},{8,9},{9,8},{10,11... | collective-permute-start | bytes 417800 | tf_op jit(solution)/shard_map/ppermute | solution.py:78
  57.5 3.7 %collective-permute-start.18 = (bf16[32,2176]{1,0:T(8,128)(2,1)S(1)}, bf16[32,2176]{1,0:T(8,128)(2,1)S(1)}, u32[]{:S(2)}, u32[]{:S(2)}) collective-permute-start(bf16[32,2176]{1,0:T(8,128)(2,1)S(1)} %get-tuple-element.82), channel_id=1, source_target_pairs={{0,1},{1,0},{2,3},{3,2},{4,5},{5,4},{6,7},{7,6},{8,9},{9,8},{10,11... | collective-permute-start | bytes 417800 | tf_op jit(solution)/shard_map/ppermute | solution.py:78
  57.9 3.3 %collective-permute-start.19 = (bf16[32,2176]{1,0:T(8,128)(2,1)S(1)}, bf16[32,2176]{1,0:T(8,128)(2,1)S(1)}, u32[]{:S(2)}, u32[]{:S(2)}) collective-permute-start(bf16[32,2176]{1,0:T(8,128)(2,1)S(1)} %get-tuple-element.83), channel_id=1, source_target_pairs={{0,1},{1,0},{2,3},{3,2},{4,5},{5,4},{6,7},{7,6},{8,9},{9,8},{10,11... | collective-permute-start | bytes 417800 | tf_op jit(solution)/shard_map/ppermute | solution.py:78
  62.9 7.1 %collective-permute-start.21 = (bf16[32,2176]{1,0:T(8,128)(2,1)S(1)}, bf16[32,2176]{1,0:T(8,128)(2,1)S(1)}, u32[]{:S(2)}, u32[]{:S(2)}) collective-permute-start(bf16[32,2176]{1,0:T(8,128)(2,1)S(1)} %get-tuple-element.86), channel_id=1, source_target_pairs={{0,4},{1,5},{2,6},{3,7},{4,0},{5,1},{6,2},{7,3},{8,12},{9,13},{10,... | collective-permute-start | bytes 417800 | tf_op jit(solution)/shard_map/ppermute | solution.py:78
  63.9 8.6 %collective-permute-start.22 = (bf16[32,2176]{1,0:T(8,128)(2,1)S(1)}, bf16[32,2176]{1,0:T(8,128)(2,1)S(1)}, u32[]{:S(2)}, u32[]{:S(2)}) collective-permute-start(bf16[32,2176]{1,0:T(8,128)(2,1)S(1)} %get-tuple-element.87), channel_id=1, source_target_pairs={{0,2},{1,3},{2,0},{3,1},{4,6},{5,7},{6,4},{7,5},{8,10},{9,11},{10,... | collective-permute-start | bytes 417800 | tf_op jit(solution)/shard_map/ppermute | solution.py:78
  65.5 7.1 %collective-permute-start.23 = (bf16[32,2176]{1,0:T(8,128)(2,1)S(1)}, bf16[32,2176]{1,0:T(8,128)(2,1)S(1)}, u32[]{:S(2)}, u32[]{:S(2)}) collective-permute-start(bf16[32,2176]{1,0:T(8,128)(2,1)S(1)} %get-tuple-element.88), channel_id=1, source_target_pairs={{0,6},{1,7},{2,4},{3,5},{4,2},{5,3},{6,0},{7,1},{8,14},{9,15},{10,... | collective-permute-start | bytes 417800 | tf_op jit(solution)/shard_map/ppermute | solution.py:78
  69.4 3.5 %collective-permute-start.25 = (bf16[32,2176]{1,0:T(8,128)(2,1)S(1)}, bf16[32,2176]{1,0:T(8,128)(2,1)S(1)}, u32[]{:S(2)}, u32[]{:S(2)}) collective-permute-start(bf16[32,2176]{1,0:T(8,128)(2,1)S(1)} %get-tuple-element.92), channel_id=1, source_target_pairs={{0,1},{1,0},{2,3},{3,2},{4,5},{5,4},{6,7},{7,6},{8,9},{9,8},{10,11... | collective-permute-start | bytes 417800 | tf_op jit(solution)/shard_map/ppermute | solution.py:78
  69.5 3.4 %collective-permute-start.26 = (bf16[32,2176]{1,0:T(8,128)(2,1)S(1)}, bf16[32,2176]{1,0:T(8,128)(2,1)S(1)}, u32[]{:S(2)}, u32[]{:S(2)}) collective-permute-start(bf16[32,2176]{1,0:T(8,128)(2,1)S(1)} %get-tuple-element.93), channel_id=1, source_target_pairs={{0,1},{1,0},{2,3},{3,2},{4,5},{5,4},{6,7},{7,6},{8,9},{9,8},{10,11... | collective-permute-start | bytes 417800 | tf_op jit(solution)/shard_map/ppermute | solution.py:78
  70.0 2.9 %collective-permute-start.27 = (bf16[32,2176]{1,0:T(8,128)(2,1)S(1)}, bf16[32,2176]{1,0:T(8,128)(2,1)S(1)}, u32[]{:S(2)}, u32[]{:S(2)}) collective-permute-start(bf16[32,2176]{1,0:T(8,128)(2,1)S(1)} %get-tuple-element.94), channel_id=1, source_target_pairs={{0,1},{1,0},{2,3},{3,2},{4,5},{5,4},{6,7},{7,6},{8,9},{9,8},{10,11... | collective-permute-start | bytes 417800 | tf_op jit(solution)/shard_map/ppermute | solution.py:78
  74.6 9.6 %collective-permute-start.29 = (bf16[32,2176]{1,0:T(8,128)(2,1)S(1)}, bf16[32,2176]{1,0:T(8,128)(2,1)S(1)}, u32[]{:S(2)}, u32[]{:S(2)}) collective-permute-start(bf16[32,2176]{1,0:T(8,128)(2,1)S(1)} %get-tuple-element.97), channel_id=1, source_target_pairs={{0,4},{1,5},{2,6},{3,7},{4,0},{5,1},{6,2},{7,3},{8,12},{9,13},{10,... | collective-permute-start | bytes 417800 | tf_op jit(solution)/shard_map/ppermute | solution.py:78
  74.9 9.2 %collective-permute-start.30 = (bf16[32,2176]{1,0:T(8,128)(2,1)S(1)}, bf16[32,2176]{1,0:T(8,128)(2,1)S(1)}, u32[]{:S(2)}, u32[]{:S(2)}) collective-permute-start(bf16[32,2176]{1,0:T(8,128)(2,1)S(1)} %get-tuple-element.98), channel_id=1, source_target_pairs={{0,2},{1,3},{2,0},{3,1},{4,6},{5,7},{6,4},{7,5},{8,10},{9,11},{10,... | collective-permute-start | bytes 417800 | tf_op jit(solution)/shard_map/ppermute | solution.py:78
  76.6 10.7 %collective-permute-start.31 = (bf16[32,2176]{1,0:T(8,128)(2,1)S(1)}, bf16[32,2176]{1,0:T(8,128)(2,1)S(1)}, u32[]{:S(2)}, u32[]{:S(2)}) collective-permute-start(bf16[32,2176]{1,0:T(8,128)(2,1)S(1)} %get-tuple-element.99), channel_id=1, source_target_pairs={{0,6},{1,7},{2,4},{3,5},{4,2},{5,3},{6,0},{7,1},{8,14},{9,15},{10,... | collective-permute-start | bytes 417800 | tf_op jit(solution)/shard_map/ppermute | solution.py:78
  78.2 10.0 %collective-permute-start.32 = (bf16[32,2176]{1,0:T(8,128)(2,1)S(1)}, bf16[32,2176]{1,0:T(8,128)(2,1)S(1)}, u32[]{:S(2)}, u32[]{:S(2)}) collective-permute-start(bf16[32,2176]{1,0:T(8,128)(2,1)S(1)} %get-tuple-element.102), channel_id=1, source_target_pairs={{0,8},{1,9},{2,10},{3,11},{4,12},{5,13},{6,14},{7,15},{8,0},{9,1},... | collective-permute-start | bytes 417800 | tf_op jit(solution)/shard_map/ppermute | solution.py:78
  87.7 8.1 %collective-permute-start.33 = (bf16[32,2176]{1,0:T(8,128)(2,1)S(1)}, bf16[32,2176]{1,0:T(8,128)(2,1)S(1)}, u32[]{:S(2)}, u32[]{:S(2)}) collective-permute-start(bf16[32,2176]{1,0:T(8,128)(2,1)S(1)} %get-tuple-element.103), channel_id=1, source_target_pairs={{0,8},{1,9},{2,10},{3,11},{4,12},{5,13},{6,14},{7,15},{8,0},{9,1},... | collective-permute-start | bytes 417800 | tf_op jit(solution)/shard_map/ppermute | solution.py:78
  (8 other events, 17.8 us)

commit v7 on v6

--- a/solution.py
+++ b/solution.py
@@ -173,7 +173,7 @@
     )(inverse, kinetic)
 
 
-def near_kernel(chunk, tile, virt_ref, energy_ref, inverse_ref, kinetic_ref, values_ref, laps_ref, out_ref, far_values, far_laps, near_values, near_laps, own_inverse, own_kinetic, sems):
+def near_kernel(chunk, tile, virt_ref, me_ref, energy_ref, inverse_ref, kinetic_ref, values_ref, laps_ref, out_ref, far_values, far_laps, near_values, near_laps, own_inverse, own_kinetic, sems):
     count, per, depth = inverse_ref.shape
     height = count * per
     width = out_ref.shape[3]
@@ -220,7 +220,7 @@
         copy.wait()
 
 
-def near_product(virt, energy, inverse, kinetic, values, laplacians):
+def near_product(virt, me, energy, inverse, kinetic, values, laplacians):
     count, per, depth = inverse.shape
     width = values.shape[1]
     chunk, tile = 512, 256
@@ -229,13 +229,13 @@
     return pl.pallas_call(
         functools.partial(near_kernel, chunk, tile),
         out_shape=(jax.ShapeDtypeStruct((2, count, per, width), jnp.float32), table, table),
-        in_specs=[SCALAR, SCALAR, HELD, HELD, HELD, HELD],
+        in_specs=[SCALAR, SCALAR, SCALAR, HELD, HELD, HELD, HELD],
         out_specs=(WHOLE, WHOLE, WHOLE),
         scratch_shapes=[table, table, own, own, pltpu.SemaphoreType.DMA((width // chunk + 2, 2))],
         compiler_params=limit(24),
         cost_estimate=cost(9),
         name="near_product",
-    )(virt, energy, inverse, kinetic, values, laplacians)
+    )(virt, me, energy, inverse, kinetic, values, laplacians)
 
 
 def far_kernel(weights, count, tile, first, virt_ref, me_ref, energy_ref, far_ref, near_ref, values_ref, laps_ref, *rest):
@@ -378,7 +378,7 @@
     theirs = []
     for group in range(pieces // 2):
         theirs += [swap(mine, "virt", 1) for mine in cut(inverse, kinetic, group)]
-    near, values, laplacians = near_product(virt, local_energy, inverse, kinetic, values, laplacians)
+    near, values, laplacians = near_product(virt, me, local_energy, inverse, kinetic, values, laplacians)
 
     keep, first, came = {}, {}, []
     late, carry = [], ()

time: 97.1 us -> 83.7 us (0.86)
  local copies, waits for them, and re-layouts: 15.1 us -> 0 us
  waiting for transfers between devices: 24.4 us -> 26.2 us
    unnamed x12 -> x0, local copies, waits for them, and re-layouts: 15.1 us -> none
    ppermute x34, waiting for transfers between devices: 24.4 us -> 26.2 us  [swap(): return lax.ppermute(array, axis, pairs)]
  transfers between devices with their start and end apart: 34 -> 34, of which waited for: 10 -> 11; matrix products, arithmetic and copies ran while one was open for 0% -> 0% of each run, Pallas kernels for 27% -> 32%
where the time goes in v7:
time: 83.7 us; the launch traced here: 83.6 us
  Pallas kernels  29.5 us (35%)
  starting transfers between devices  26.4 us (32%)
  waiting for transfers between devices  26.2 us (31%)
  between operations  1.51 us (2%)
    ppermute x34, starting transfers between devices, swap(): return lax.ppermute(array, axis, pairs)  26.4 us
    ppermute x34, waiting for transfers between devices, swap(): return lax.ppermute(array, axis, pairs)  26.2 us
    pallas_call x4, Pallas kernels, far_product(): pl.pallas_call(functools.partial(far_kernel, place_weights(stages), count...  11.4 us
    pallas_call x1, Pallas kernels, near_product(): pl.pallas_call(functools.partial(near_kernel, chunk, tile), out_shape=(ja...  10.3 us
    pallas_call x8, Pallas kernels, combine(): pl.pallas_call(functools.partial(combine_kernel, parts, senders, len(carr...  4.17 us
    pallas_call x2, Pallas kernels, cut(): pl.pallas_call(cut_kernel, out_shape=(out, out), grid=(1,), in_specs=[blo...  2.55 us
  transfers between devices with their start and end apart: 34, of which 11 were waited for; matrix products, arithmetic and copies ran while one was open for 0% of the time, Pallas kernels for 32%

profile of v7, /device:TPU:0, one launch (start us, length us, event | category | flops | bytes accessed | tf_op | source)
XLA Modules:
  0.0 83.6 jit_solution(411097832006703237)
XLA Ops:
  0.6 1.3 %cut.2 = (bf16[2,128,1024]{2,1,0:T(8,128)(2,1)S(1)}, bf16[2,128,1024]{2,1,0:T(8,128)(2,1)S(1)}) custom-call(bf16[16,32,1024]{2,1,0:T(8,128)(2,1)} %bitcast.6, bf16[16,32,1024]{2,1,0:T(8,128)(2,1)} %bitcast.9), custom_call_target="tpu_custom_call" | custom-call | flops 110000000 | tf_op jit(solution)/shard_map/cut/pallas_call | solution.py:164
  1.9 3.0 %collective-permute-start = (bf16[2,128,1024]{2,1,0:T(8,128)(2,1)S(1)}, bf16[2,128,1024]{2,1,0:T(8,128)(2,1)S(1)}, u32[]{:S(2)}, u32[]{:S(2)}) collective-permute-start(bf16[2,128,1024]{2,1,0:T(8,128)(2,1)S(1)} %get-tuple-element.53), channel_id=1, source_target_pairs={{0,16},{16,0},{1,17},{17,1},{2,18},{18,2},{3,19},{19,3},{4,20},{20... | collective-permute-start | bytes 1572872 | tf_op jit(solution)/shard_map/ppermute | solution.py:78
  5.7 10.3 %near_product.1 = (f32[2,16,32,2048]{3,2,1,0:T(8,128)S(1)}, bf16[1024,2048]{1,0:T(8,128)(2,1)S(1)}, bf16[1024,2048]{1,0:T(8,128)(2,1)S(1)}) custom-call(s32[1]{0:T(128)} %bitcast.virt_ref, s32[1]{0:T(128)} %bitcast.1.me_ref, f32[1]{0:T(128)S(6)} %copy.7.energy_ref, bf16[16,32,1024]{2,1,0:T(8,128)(2,1)} %bitcast.7, bf16[16,32,1024]{2,1,0:T(8,128)(2,1)} %bitcast.10, ...), custom_call_target="tpu_custom_call" | custom-call | flops 9900000256 | tf_op jit(solution)/shard_map/near_product/pallas_call | solution.py:229
  16.0 1.7 %collective-permute-done.far_ref = bf16[2,128,1024]{2,1,0:T(8,128)(2,1)S(1)} collective-permute-done((bf16[2,128,1024]{2,1,0:T(8,128)(2,1)S(1)}, bf16[2,128,1024]{2,1,0:T(8,128)(2,1)S(1)}, u32[]{:S(2)}, u32[]{:S(2)}) %collective-permute-start) | collective-permute-done | bytes 524320 | tf_op jit(solution)/shard_map/ppermute | solution.py:78
  17.7 2.8 %far_product.4 = (bf16[32,2176]{1,0:T(8,128)(2,1)S(1)}, bf16[32,2176]{1,0:T(8,128)(2,1)S(1)}, bf16[32,2176]{1,0:T(8,128)(2,1)S(1)}, bf16[32,2176]{1,0:T(8,128)(2,1)S(1)}, f32[2,64,2176]{2,1,0:T(8,128)S(1)}) custom-call(s32[1]{0:T(128)} %bitcast.virt_ref, s32[1]{0:T(128)} %bitcast.1.me_ref, f32[1]{0:T(128)S(6)} %copy.7.energy_ref, ...), custom_call_target="tpu_custom_call" | custom-call | flops 110000000 | tf_op jit(solution)/shard_map/far_product/pallas_call | solution.py:280
  21.6 1.3 %cut.3 = (bf16[2,128,1024]{2,1,0:T(8,128)(2,1)S(1)}, bf16[2,128,1024]{2,1,0:T(8,128)(2,1)S(1)}) custom-call(bf16[16,32,1024]{2,1,0:T(8,128)(2,1)} %bitcast.8, bf16[16,32,1024]{2,1,0:T(8,128)(2,1)} %bitcast.11), custom_call_target="tpu_custom_call" | custom-call | flops 110000000 | tf_op jit(solution)/shard_map/cut/pallas_call | solution.py:164
  22.9 2.1 %collective-permute-start.16 = (bf16[2,128,1024]{2,1,0:T(8,128)(2,1)S(1)}, bf16[2,128,1024]{2,1,0:T(8,128)(2,1)S(1)}, u32[]{:S(2)}, u32[]{:S(2)}) collective-permute-start(bf16[2,128,1024]{2,1,0:T(8,128)(2,1)S(1)} %get-tuple-element.79), channel_id=1, source_target_pairs={{0,16},{16,0},{1,17},{17,1},{2,18},{18,2},{3,19},{19,3},{4,20},{20... | collective-permute-start | bytes 1572872 | tf_op jit(solution)/shard_map/ppermute | solution.py:78
  25.0 0.7 combine.8
  25.7 1.6 %collective-permute-start.5 = (bf16[32,2176]{1,0:T(8,128)(2,1)S(1)}, bf16[32,2176]{1,0:T(8,128)(2,1)S(1)}, u32[]{:S(2)}, u32[]{:S(2)}) collective-permute-start(bf16[32,2176]{1,0:T(8,128)(2,1)S(1)} %get-tuple-element.63), channel_id=1, source_target_pairs={{0,4},{1,5},{2,6},{3,7},{4,0},{5,1},{6,2},{7,3},{8,12},{9,13},{10,... | collective-permute-start | bytes 417800 | tf_op jit(solution)/shard_map/ppermute | solution.py:78
  27.4 1.5 %collective-permute-start.6 = (bf16[32,2176]{1,0:T(8,128)(2,1)S(1)}, bf16[32,2176]{1,0:T(8,128)(2,1)S(1)}, u32[]{:S(2)}, u32[]{:S(2)}) collective-permute-start(bf16[32,2176]{1,0:T(8,128)(2,1)S(1)} %get-tuple-element.64), channel_id=1, source_target_pairs={{0,2},{1,3},{2,0},{3,1},{4,6},{5,7},{6,4},{7,5},{8,10},{9,11},{10,... | collective-permute-start | bytes 417800 | tf_op jit(solution)/shard_map/ppermute | solution.py:78
  29.3 2.8 %far_product.5 = (bf16[32,2176]{1,0:T(8,128)(2,1)S(1)}, bf16[32,2176]{1,0:T(8,128)(2,1)S(1)}, bf16[32,2176]{1,0:T(8,128)(2,1)S(1)}, bf16[32,2176]{1,0:T(8,128)(2,1)S(1)}, f32[2,64,2176]{2,1,0:T(8,128)S(1)}) custom-call(s32[1]{0:T(128)} %bitcast.virt_ref, s32[1]{0:T(128)} %bitcast.1.me_ref, f32[1]{0:T(128)S(6)} %copy.7.energy_ref, ...), custom_call_target="tpu_custom_call" | custom-call | flops 110000000 | tf_op jit(solution)/shard_map/far_product/pallas_call | solution.py:280
  32.7 2.8 %collective-permute-done.6.refs_2_ = bf16[32,2176]{1,0:T(8,128)(2,1)S(1)} collective-permute-done((bf16[32,2176]{1,0:T(8,128)(2,1)S(1)}, bf16[32,2176]{1,0:T(8,128)(2,1)S(1)}, u32[]{:S(2)}, u32[]{:S(2)}) %collective-permute-start.6) | collective-permute-done | bytes 139296 | tf_op jit(solution)/shard_map/ppermute | solution.py:78
  37.7 1.1 %collective-permute-start.13 = (bf16[32,2176]{1,0:T(8,128)(2,1)S(1)}, bf16[32,2176]{1,0:T(8,128)(2,1)S(1)}, u32[]{:S(2)}, u32[]{:S(2)}) collective-permute-start(bf16[32,2176]{1,0:T(8,128)(2,1)S(1)} %get-tuple-element.74), channel_id=1, source_target_pairs={{0,4},{1,5},{2,6},{3,7},{4,0},{5,1},{6,2},{7,3},{8,12},{9,13},{10,... | collective-permute-start | bytes 417800 | tf_op jit(solution)/shard_map/ppermute | solution.py:78
  38.8 0.9 %collective-permute-start.14 = (bf16[32,2176]{1,0:T(8,128)(2,1)S(1)}, bf16[32,2176]{1,0:T(8,128)(2,1)S(1)}, u32[]{:S(2)}, u32[]{:S(2)}) collective-permute-start(bf16[32,2176]{1,0:T(8,128)(2,1)S(1)} %get-tuple-element.75), channel_id=1, source_target_pairs={{0,2},{1,3},{2,0},{3,1},{4,6},{5,7},{6,4},{7,5},{8,10},{9,11},{10,... | collective-permute-start | bytes 417800 | tf_op jit(solution)/shard_map/ppermute | solution.py:78
  39.7 1.5 %collective-permute-start.15 = (bf16[32,2176]{1,0:T(8,128)(2,1)S(1)}, bf16[32,2176]{1,0:T(8,128)(2,1)S(1)}, u32[]{:S(2)}, u32[]{:S(2)}) collective-permute-start(bf16[32,2176]{1,0:T(8,128)(2,1)S(1)} %get-tuple-element.76), channel_id=1, source_target_pairs={{0,6},{1,7},{2,4},{3,5},{4,2},{5,3},{6,0},{7,1},{8,14},{9,15},{10,... | collective-permute-start | bytes 417800 | tf_op jit(solution)/shard_map/ppermute | solution.py:78
  41.3 2.8 %far_product.6 = (bf16[32,2176]{1,0:T(8,128)(2,1)S(1)}, bf16[32,2176]{1,0:T(8,128)(2,1)S(1)}, bf16[32,2176]{1,0:T(8,128)(2,1)S(1)}, bf16[32,2176]{1,0:T(8,128)(2,1)S(1)}, f32[2,64,2176]{2,1,0:T(8,128)S(1)}) custom-call(s32[1]{0:T(128)} %bitcast.virt_ref, s32[1]{0:T(128)} %bitcast.1.me_ref, f32[1]{0:T(128)S(6)} %copy.7.energy_ref, ...), custom_call_target="tpu_custom_call" | custom-call | flops 110000000 | tf_op jit(solution)/shard_map/far_product/pallas_call | solution.py:280
  44.8 2.8 %collective-permute-done.15.refs_3_ = bf16[32,2176]{1,0:T(8,128)(2,1)S(1)} collective-permute-done((bf16[32,2176]{1,0:T(8,128)(2,1)S(1)}, bf16[32,2176]{1,0:T(8,128)(2,1)S(1)}, u32[]{:S(2)}, u32[]{:S(2)}) %collective-permute-start.15) | collective-permute-done | bytes 139296 | tf_op jit(solution)/shard_map/ppermute | solution.py:78
  48.0 1.0 %collective-permute-done.20.refs_4_ = bf16[32,2176]{1,0:T(8,128)(2,1)S(1)} collective-permute-done((bf16[32,2176]{1,0:T(8,128)(2,1)S(1)}, bf16[32,2176]{1,0:T(8,128)(2,1)S(1)}, u32[]{:S(2)}, u32[]{:S(2)}) %collective-permute-start.20) | collective-permute-done | bytes 139296 | tf_op jit(solution)/shard_map/ppermute | solution.py:78
  48.9 0.7 combine.12
  49.6 1.1 %collective-permute-start.21 = (bf16[32,2176]{1,0:T(8,128)(2,1)S(1)}, bf16[32,2176]{1,0:T(8,128)(2,1)S(1)}, u32[]{:S(2)}, u32[]{:S(2)}) collective-permute-start(bf16[32,2176]{1,0:T(8,128)(2,1)S(1)} %get-tuple-element.86), channel_id=1, source_target_pairs={{0,4},{1,5},{2,6},{3,7},{4,0},{5,1},{6,2},{7,3},{8,12},{9,13},{10,... | collective-permute-start | bytes 417800 | tf_op jit(solution)/shard_map/ppermute | solution.py:78
  50.7 1.5 %collective-permute-start.22 = (bf16[32,2176]{1,0:T(8,128)(2,1)S(1)}, bf16[32,2176]{1,0:T(8,128)(2,1)S(1)}, u32[]{:S(2)}, u32[]{:S(2)}) collective-permute-start(bf16[32,2176]{1,0:T(8,128)(2,1)S(1)} %get-tuple-element.87), channel_id=1, source_target_pairs={{0,2},{1,3},{2,0},{3,1},{4,6},{5,7},{6,4},{7,5},{8,10},{9,11},{10,... | collective-permute-start | bytes 417800 | tf_op jit(solution)/shard_map/ppermute | solution.py:78
  52.2 1.0 %collective-permute-start.23 = (bf16[32,2176]{1,0:T(8,128)(2,1)S(1)}, bf16[32,2176]{1,0:T(8,128)(2,1)S(1)}, u32[]{:S(2)}, u32[]{:S(2)}) collective-permute-start(bf16[32,2176]{1,0:T(8,128)(2,1)S(1)} %get-tuple-element.88), channel_id=1, source_target_pairs={{0,6},{1,7},{2,4},{3,5},{4,2},{5,3},{6,0},{7,1},{8,14},{9,15},{10,... | collective-permute-start | bytes 417800 | tf_op jit(solution)/shard_map/ppermute | solution.py:78
  53.2 3.0 %far_product.7 = (bf16[32,2176]{1,0:T(8,128)(2,1)S(1)}, bf16[32,2176]{1,0:T(8,128)(2,1)S(1)}, bf16[32,2176]{1,0:T(8,128)(2,1)S(1)}, bf16[32,2176]{1,0:T(8,128)(2,1)S(1)}, f32[2,64,2176]{2,1,0:T(8,128)S(1)}) custom-call(s32[1]{0:T(128)} %bitcast.virt_ref, s32[1]{0:T(128)} %bitcast.1.me_ref, f32[1]{0:T(128)S(6)} %copy.7.energy_ref, ...), custom_call_target="tpu_custom_call" | custom-call | flops 110000000 | tf_op jit(solution)/shard_map/far_product/pallas_call | solution.py:280
  56.8 2.5 %collective-permute-done.22.refs_2_ = bf16[32,2176]{1,0:T(8,128)(2,1)S(1)} collective-permute-done((bf16[32,2176]{1,0:T(8,128)(2,1)S(1)}, bf16[32,2176]{1,0:T(8,128)(2,1)S(1)}, u32[]{:S(2)}, u32[]{:S(2)}) %collective-permute-start.22) | collective-permute-done | bytes 139296 | tf_op jit(solution)/shard_map/ppermute | solution.py:78
  59.7 1.0 %collective-permute-done.28.refs_4_ = bf16[32,2176]{1,0:T(8,128)(2,1)S(1)} collective-permute-done((bf16[32,2176]{1,0:T(8,128)(2,1)S(1)}, bf16[32,2176]{1,0:T(8,128)(2,1)S(1)}, u32[]{:S(2)}, u32[]{:S(2)}) %collective-permute-start.28) | collective-permute-done | bytes 139296 | tf_op jit(solution)/shard_map/ppermute | solution.py:78
  61.7 1.7 %collective-permute-start.30 = (bf16[32,2176]{1,0:T(8,128)(2,1)S(1)}, bf16[32,2176]{1,0:T(8,128)(2,1)S(1)}, u32[]{:S(2)}, u32[]{:S(2)}) collective-permute-start(bf16[32,2176]{1,0:T(8,128)(2,1)S(1)} %get-tuple-element.98), channel_id=1, source_target_pairs={{0,2},{1,3},{2,0},{3,1},{4,6},{5,7},{6,4},{7,5},{8,10},{9,11},{10,... | collective-permute-start | bytes 417800 | tf_op jit(solution)/shard_map/ppermute | solution.py:78
  63.4 1.5 %collective-permute-start.31 = (bf16[32,2176]{1,0:T(8,128)(2,1)S(1)}, bf16[32,2176]{1,0:T(8,128)(2,1)S(1)}, u32[]{:S(2)}, u32[]{:S(2)}) collective-permute-start(bf16[32,2176]{1,0:T(8,128)(2,1)S(1)} %get-tuple-element.99), channel_id=1, source_target_pairs={{0,6},{1,7},{2,4},{3,5},{4,2},{5,3},{6,0},{7,1},{8,14},{9,15},{10,... | collective-permute-start | bytes 417800 | tf_op jit(solution)/shard_map/ppermute | solution.py:78
  64.9 2.6 %collective-permute-start.32 = (bf16[32,2176]{1,0:T(8,128)(2,1)S(1)}, bf16[32,2176]{1,0:T(8,128)(2,1)S(1)}, u32[]{:S(2)}, u32[]{:S(2)}) collective-permute-start(bf16[32,2176]{1,0:T(8,128)(2,1)S(1)} %get-tuple-element.102), channel_id=1, source_target_pairs={{0,8},{1,9},{2,10},{3,11},{4,12},{5,13},{6,14},{7,15},{8,0},{9,1},... | collective-permute-start | bytes 417800 | tf_op jit(solution)/shard_map/ppermute | solution.py:78
  67.5 3.4 %collective-permute-done.29.refs_1_ = bf16[32,2176]{1,0:T(8,128)(2,1)S(1)} collective-permute-done((bf16[32,2176]{1,0:T(8,128)(2,1)S(1)}, bf16[32,2176]{1,0:T(8,128)(2,1)S(1)}, u32[]{:S(2)}, u32[]{:S(2)}) %collective-permute-start.29) | collective-permute-done | bytes 139296 | tf_op jit(solution)/shard_map/ppermute | solution.py:78
  70.9 3.1 %collective-permute-done.31.refs_3_ = bf16[32,2176]{1,0:T(8,128)(2,1)S(1)} collective-permute-done((bf16[32,2176]{1,0:T(8,128)(2,1)S(1)}, bf16[32,2176]{1,0:T(8,128)(2,1)S(1)}, u32[]{:S(2)}, u32[]{:S(2)}) %collective-permute-start.31) | collective-permute-done | bytes 139296 | tf_op jit(solution)/shard_map/ppermute | solution.py:78
  74.9 7.6 %collective-permute-done.33.refs_5_ = bf16[32,2176]{1,0:T(8,128)(2,1)S(1)} collective-permute-done((bf16[32,2176]{1,0:T(8,128)(2,1)S(1)}, bf16[32,2176]{1,0:T(8,128)(2,1)S(1)}, u32[]{:S(2)}, u32[]{:S(2)}) %collective-permute-start.33) | collective-permute-done | bytes 139296 | tf_op jit(solution)/shard_map/ppermute | solution.py:78
  82.5 1.1 %finish.1 = (f32[32,2048]{1,0:T(8,128)}, f32[32,2048]{1,0:T(8,128)}) custom-call(f32[2,8,2176]{2,1,0:T(8,128)S(1)} %get-tuple-element.66.refs_5_.refs_0_, f32[2,8,2176]{2,1,0:T(8,128)S(1)} %get-tuple-element.78.refs_5_.refs_1_, f32[2,8,2176]{2,1,0:T(8,128)S(1)} %get-tuple-element.89.refs_5_.refs_2_, f32[2,8,2176]{2,1,0:T(8,128)S(1)} %get-tuple-element.101.refs_3_, ...), custom_call_target="tpu_custom_call" | custom-call | flops 110000000 | tf_op jit(solution)/shard_map/finish/pallas_call | solution.py:353
  (52 shorter events, 8.3 us)
Async XLA Ops:
  1.9 15.8 %collective-permute-start = (bf16[2,128,1024]{2,1,0:T(8,128)(2,1)S(1)}, bf16[2,128,1024]{2,1,0:T(8,128)(2,1)S(1)}, u32[]{:S(2)}, u32[]{:S(2)}) collective-permute-start(bf16[2,128,1024]{2,1,0:T(8,128)(2,1)S(1)} %get-tuple-element.53), channel_id=1, source_target_pairs={{0,16},{16,0},{1,17},{17,1},{2,18},{18,2},{3,19},{19,3},{4,20},{20... | collective-permute-start | bytes 1572872 | tf_op jit(solution)/shard_map/ppermute | solution.py:78
  4.9 24.3 %collective-permute-start.8 = (bf16[2,128,1024]{2,1,0:T(8,128)(2,1)S(1)}, bf16[2,128,1024]{2,1,0:T(8,128)(2,1)S(1)}, u32[]{:S(2)}, u32[]{:S(2)}) collective-permute-start(bf16[2,128,1024]{2,1,0:T(8,128)(2,1)S(1)} %get-tuple-element.67), channel_id=1, source_target_pairs={{0,16},{16,0},{1,17},{17,1},{2,18},{18,2},{3,19},{19,3},{4,20},{20... | collective-permute-start | bytes 1572872 | tf_op jit(solution)/shard_map/ppermute | solution.py:78
  20.5 2.4 %collective-permute-start.1 = (bf16[32,2176]{1,0:T(8,128)(2,1)S(1)}, bf16[32,2176]{1,0:T(8,128)(2,1)S(1)}, u32[]{:S(2)}, u32[]{:S(2)}) collective-permute-start(bf16[32,2176]{1,0:T(8,128)(2,1)S(1)} %get-tuple-element.58), channel_id=1, source_target_pairs={{0,1},{1,0},{2,3},{3,2},{4,5},{5,4},{6,7},{7,6},{8,9},{9,8},{10,11... | collective-permute-start | bytes 417800 | tf_op jit(solution)/shard_map/ppermute | solution.py:78
  20.6 4.4 %collective-permute-start.2 = (bf16[32,2176]{1,0:T(8,128)(2,1)S(1)}, bf16[32,2176]{1,0:T(8,128)(2,1)S(1)}, u32[]{:S(2)}, u32[]{:S(2)}) collective-permute-start(bf16[32,2176]{1,0:T(8,128)(2,1)S(1)} %get-tuple-element.59), channel_id=1, source_target_pairs={{0,1},{1,0},{2,3},{3,2},{4,5},{5,4},{6,7},{7,6},{8,9},{9,8},{10,11... | collective-permute-start | bytes 417800 | tf_op jit(solution)/shard_map/ppermute | solution.py:78
  21.1 3.9 %collective-permute-start.3 = (bf16[32,2176]{1,0:T(8,128)(2,1)S(1)}, bf16[32,2176]{1,0:T(8,128)(2,1)S(1)}, u32[]{:S(2)}, u32[]{:S(2)}) collective-permute-start(bf16[32,2176]{1,0:T(8,128)(2,1)S(1)} %get-tuple-element.60), channel_id=1, source_target_pairs={{0,1},{1,0},{2,3},{3,2},{4,5},{5,4},{6,7},{7,6},{8,9},{9,8},{10,11... | collective-permute-start | bytes 417800 | tf_op jit(solution)/shard_map/ppermute | solution.py:78
  21.2 3.8 %collective-permute-start.4 = (bf16[32,2176]{1,0:T(8,128)(2,1)S(1)}, bf16[32,2176]{1,0:T(8,128)(2,1)S(1)}, u32[]{:S(2)}, u32[]{:S(2)}) collective-permute-start(bf16[32,2176]{1,0:T(8,128)(2,1)S(1)} %get-tuple-element.61), channel_id=1, source_target_pairs={{0,1},{1,0},{2,3},{3,2},{4,5},{5,4},{6,7},{7,6},{8,9},{9,8},{10,11... | collective-permute-start | bytes 417800 | tf_op jit(solution)/shard_map/ppermute | solution.py:78
  22.9 18.4 %collective-permute-start.16 = (bf16[2,128,1024]{2,1,0:T(8,128)(2,1)S(1)}, bf16[2,128,1024]{2,1,0:T(8,128)(2,1)S(1)}, u32[]{:S(2)}, u32[]{:S(2)}) collective-permute-start(bf16[2,128,1024]{2,1,0:T(8,128)(2,1)S(1)} %get-tuple-element.79), channel_id=1, source_target_pairs={{0,16},{16,0},{1,17},{17,1},{2,18},{18,2},{3,19},{19,3},{4,20},{20... | collective-permute-start | bytes 1572872 | tf_op jit(solution)/shard_map/ppermute | solution.py:78
  25.7 6.5 %collective-permute-start.5 = (bf16[32,2176]{1,0:T(8,128)(2,1)S(1)}, bf16[32,2176]{1,0:T(8,128)(2,1)S(1)}, u32[]{:S(2)}, u32[]{:S(2)}) collective-permute-start(bf16[32,2176]{1,0:T(8,128)(2,1)S(1)} %get-tuple-element.63), channel_id=1, source_target_pairs={{0,4},{1,5},{2,6},{3,7},{4,0},{5,1},{6,2},{7,3},{8,12},{9,13},{10,... | collective-permute-start | bytes 417800 | tf_op jit(solution)/shard_map/ppermute | solution.py:78
  27.4 8.1 %collective-permute-start.6 = (bf16[32,2176]{1,0:T(8,128)(2,1)S(1)}, bf16[32,2176]{1,0:T(8,128)(2,1)S(1)}, u32[]{:S(2)}, u32[]{:S(2)}) collective-permute-start(bf16[32,2176]{1,0:T(8,128)(2,1)S(1)} %get-tuple-element.64), channel_id=1, source_target_pairs={{0,2},{1,3},{2,0},{3,1},{4,6},{5,7},{6,4},{7,5},{8,10},{9,11},{10,... | collective-permute-start | bytes 417800 | tf_op jit(solution)/shard_map/ppermute | solution.py:78
  28.8 6.6 %collective-permute-start.7 = (bf16[32,2176]{1,0:T(8,128)(2,1)S(1)}, bf16[32,2176]{1,0:T(8,128)(2,1)S(1)}, u32[]{:S(2)}, u32[]{:S(2)}) collective-permute-start(bf16[32,2176]{1,0:T(8,128)(2,1)S(1)} %get-tuple-element.65), channel_id=1, source_target_pairs={{0,6},{1,7},{2,4},{3,5},{4,2},{5,3},{6,0},{7,1},{8,14},{9,15},{10,... | collective-permute-start | bytes 417800 | tf_op jit(solution)/shard_map/ppermute | solution.py:78
  32.1 3.9 %collective-permute-start.9 = (bf16[32,2176]{1,0:T(8,128)(2,1)S(1)}, bf16[32,2176]{1,0:T(8,128)(2,1)S(1)}, u32[]{:S(2)}, u32[]{:S(2)}) collective-permute-start(bf16[32,2176]{1,0:T(8,128)(2,1)S(1)} %get-tuple-element.69), channel_id=1, source_target_pairs={{0,1},{1,0},{2,3},{3,2},{4,5},{5,4},{6,7},{7,6},{8,9},{9,8},{10,11... | collective-permute-start | bytes 417800 | tf_op jit(solution)/shard_map/ppermute | solution.py:78
  32.2 4.6 %collective-permute-start.10 = (bf16[32,2176]{1,0:T(8,128)(2,1)S(1)}, bf16[32,2176]{1,0:T(8,128)(2,1)S(1)}, u32[]{:S(2)}, u32[]{:S(2)}) collective-permute-start(bf16[32,2176]{1,0:T(8,128)(2,1)S(1)} %get-tuple-element.70), channel_id=1, source_target_pairs={{0,1},{1,0},{2,3},{3,2},{4,5},{5,4},{6,7},{7,6},{8,9},{9,8},{10,11... | collective-permute-start | bytes 417800 | tf_op jit(solution)/shard_map/ppermute | solution.py:78
  35.4 1.4 %collective-permute-start.11 = (bf16[32,2176]{1,0:T(8,128)(2,1)S(1)}, bf16[32,2176]{1,0:T(8,128)(2,1)S(1)}, u32[]{:S(2)}, u32[]{:S(2)}) collective-permute-start(bf16[32,2176]{1,0:T(8,128)(2,1)S(1)} %get-tuple-element.71), channel_id=1, source_target_pairs={{0,1},{1,0},{2,3},{3,2},{4,5},{5,4},{6,7},{7,6},{8,9},{9,8},{10,11... | collective-permute-start | bytes 417800 | tf_op jit(solution)/shard_map/ppermute | solution.py:78
  35.4 1.6 %collective-permute-start.12 = (bf16[32,2176]{1,0:T(8,128)(2,1)S(1)}, bf16[32,2176]{1,0:T(8,128)(2,1)S(1)}, u32[]{:S(2)}, u32[]{:S(2)}) collective-permute-start(bf16[32,2176]{1,0:T(8,128)(2,1)S(1)} %get-tuple-element.72), channel_id=1, source_target_pairs={{0,1},{1,0},{2,3},{3,2},{4,5},{5,4},{6,7},{7,6},{8,9},{9,8},{10,11... | collective-permute-start | bytes 417800 | tf_op jit(solution)/shard_map/ppermute | solution.py:78
  36.0 17.2 %collective-permute-start.24 = (bf16[2,128,1024]{2,1,0:T(8,128)(2,1)S(1)}, bf16[2,128,1024]{2,1,0:T(8,128)(2,1)S(1)}, u32[]{:S(2)}, u32[]{:S(2)}) collective-permute-start(bf16[2,128,1024]{2,1,0:T(8,128)(2,1)S(1)} %get-tuple-element.90), channel_id=1, source_target_pairs={{0,16},{16,0},{1,17},{17,1},{2,18},{18,2},{3,19},{19,3},{4,20},{20... | collective-permute-start | bytes 1572872 | tf_op jit(solution)/shard_map/ppermute | solution.py:78
  37.7 6.6 %collective-permute-start.13 = (bf16[32,2176]{1,0:T(8,128)(2,1)S(1)}, bf16[32,2176]{1,0:T(8,128)(2,1)S(1)}, u32[]{:S(2)}, u32[]{:S(2)}) collective-permute-start(bf16[32,2176]{1,0:T(8,128)(2,1)S(1)} %get-tuple-element.74), channel_id=1, source_target_pairs={{0,4},{1,5},{2,6},{3,7},{4,0},{5,1},{6,2},{7,3},{8,12},{9,13},{10,... | collective-permute-start | bytes 417800 | tf_op jit(solution)/shard_map/ppermute | solution.py:78
  38.8 5.9 %collective-permute-start.14 = (bf16[32,2176]{1,0:T(8,128)(2,1)S(1)}, bf16[32,2176]{1,0:T(8,128)(2,1)S(1)}, u32[]{:S(2)}, u32[]{:S(2)}) collective-permute-start(bf16[32,2176]{1,0:T(8,128)(2,1)S(1)} %get-tuple-element.75), channel_id=1, source_target_pairs={{0,2},{1,3},{2,0},{3,1},{4,6},{5,7},{6,4},{7,5},{8,10},{9,11},{10,... | collective-permute-start | bytes 417800 | tf_op jit(solution)/shard_map/ppermute | solution.py:78
  39.7 7.9 %collective-permute-start.15 = (bf16[32,2176]{1,0:T(8,128)(2,1)S(1)}, bf16[32,2176]{1,0:T(8,128)(2,1)S(1)}, u32[]{:S(2)}, u32[]{:S(2)}) collective-permute-start(bf16[32,2176]{1,0:T(8,128)(2,1)S(1)} %get-tuple-element.76), channel_id=1, source_target_pairs={{0,6},{1,7},{2,4},{3,5},{4,2},{5,3},{6,0},{7,1},{8,14},{9,15},{10,... | collective-permute-start | bytes 417800 | tf_op jit(solution)/shard_map/ppermute | solution.py:78
  44.1 3.9 %collective-permute-start.17 = (bf16[32,2176]{1,0:T(8,128)(2,1)S(1)}, bf16[32,2176]{1,0:T(8,128)(2,1)S(1)}, u32[]{:S(2)}, u32[]{:S(2)}) collective-permute-start(bf16[32,2176]{1,0:T(8,128)(2,1)S(1)} %get-tuple-element.81), channel_id=1, source_target_pairs={{0,1},{1,0},{2,3},{3,2},{4,5},{5,4},{6,7},{7,6},{8,9},{9,8},{10,11... | collective-permute-start | bytes 417800 | tf_op jit(solution)/shard_map/ppermute | solution.py:78
  44.3 3.7 %collective-permute-start.18 = (bf16[32,2176]{1,0:T(8,128)(2,1)S(1)}, bf16[32,2176]{1,0:T(8,128)(2,1)S(1)}, u32[]{:S(2)}, u32[]{:S(2)}) collective-permute-start(bf16[32,2176]{1,0:T(8,128)(2,1)S(1)} %get-tuple-element.82), channel_id=1, source_target_pairs={{0,1},{1,0},{2,3},{3,2},{4,5},{5,4},{6,7},{7,6},{8,9},{9,8},{10,11... | collective-permute-start | bytes 417800 | tf_op jit(solution)/shard_map/ppermute | solution.py:78
  44.6 3.3 %collective-permute-start.19 = (bf16[32,2176]{1,0:T(8,128)(2,1)S(1)}, bf16[32,2176]{1,0:T(8,128)(2,1)S(1)}, u32[]{:S(2)}, u32[]{:S(2)}) collective-permute-start(bf16[32,2176]{1,0:T(8,128)(2,1)S(1)} %get-tuple-element.83), channel_id=1, source_target_pairs={{0,1},{1,0},{2,3},{3,2},{4,5},{5,4},{6,7},{7,6},{8,9},{9,8},{10,11... | collective-permute-start | bytes 417800 | tf_op jit(solution)/shard_map/ppermute | solution.py:78
  49.6 7.1 %collective-permute-start.21 = (bf16[32,2176]{1,0:T(8,128)(2,1)S(1)}, bf16[32,2176]{1,0:T(8,128)(2,1)S(1)}, u32[]{:S(2)}, u32[]{:S(2)}) collective-permute-start(bf16[32,2176]{1,0:T(8,128)(2,1)S(1)} %get-tuple-element.86), channel_id=1, source_target_pairs={{0,4},{1,5},{2,6},{3,7},{4,0},{5,1},{6,2},{7,3},{8,12},{9,13},{10,... | collective-permute-start | bytes 417800 | tf_op jit(solution)/shard_map/ppermute | solution.py:78
  50.7 8.6 %collective-permute-start.22 = (bf16[32,2176]{1,0:T(8,128)(2,1)S(1)}, bf16[32,2176]{1,0:T(8,128)(2,1)S(1)}, u32[]{:S(2)}, u32[]{:S(2)}) collective-permute-start(bf16[32,2176]{1,0:T(8,128)(2,1)S(1)} %get-tuple-element.87), channel_id=1, source_target_pairs={{0,2},{1,3},{2,0},{3,1},{4,6},{5,7},{6,4},{7,5},{8,10},{9,11},{10,... | collective-permute-start | bytes 417800 | tf_op jit(solution)/shard_map/ppermute | solution.py:78
  52.2 7.1 %collective-permute-start.23 = (bf16[32,2176]{1,0:T(8,128)(2,1)S(1)}, bf16[32,2176]{1,0:T(8,128)(2,1)S(1)}, u32[]{:S(2)}, u32[]{:S(2)}) collective-permute-start(bf16[32,2176]{1,0:T(8,128)(2,1)S(1)} %get-tuple-element.88), channel_id=1, source_target_pairs={{0,6},{1,7},{2,4},{3,5},{4,2},{5,3},{6,0},{7,1},{8,14},{9,15},{10,... | collective-permute-start | bytes 417800 | tf_op jit(solution)/shard_map/ppermute | solution.py:78
  56.2 3.5 %collective-permute-start.25 = (bf16[32,2176]{1,0:T(8,128)(2,1)S(1)}, bf16[32,2176]{1,0:T(8,128)(2,1)S(1)}, u32[]{:S(2)}, u32[]{:S(2)}) collective-permute-start(bf16[32,2176]{1,0:T(8,128)(2,1)S(1)} %get-tuple-element.92), channel_id=1, source_target_pairs={{0,1},{1,0},{2,3},{3,2},{4,5},{5,4},{6,7},{7,6},{8,9},{9,8},{10,11... | collective-permute-start | bytes 417800 | tf_op jit(solution)/shard_map/ppermute | solution.py:78
  56.3 3.4 %collective-permute-start.26 = (bf16[32,2176]{1,0:T(8,128)(2,1)S(1)}, bf16[32,2176]{1,0:T(8,128)(2,1)S(1)}, u32[]{:S(2)}, u32[]{:S(2)}) collective-permute-start(bf16[32,2176]{1,0:T(8,128)(2,1)S(1)} %get-tuple-element.93), channel_id=1, source_target_pairs={{0,1},{1,0},{2,3},{3,2},{4,5},{5,4},{6,7},{7,6},{8,9},{9,8},{10,11... | collective-permute-start | bytes 417800 | tf_op jit(solution)/shard_map/ppermute | solution.py:78
  56.8 2.9 %collective-permute-start.27 = (bf16[32,2176]{1,0:T(8,128)(2,1)S(1)}, bf16[32,2176]{1,0:T(8,128)(2,1)S(1)}, u32[]{:S(2)}, u32[]{:S(2)}) collective-permute-start(bf16[32,2176]{1,0:T(8,128)(2,1)S(1)} %get-tuple-element.94), channel_id=1, source_target_pairs={{0,1},{1,0},{2,3},{3,2},{4,5},{5,4},{6,7},{7,6},{8,9},{9,8},{10,11... | collective-permute-start | bytes 417800 | tf_op jit(solution)/shard_map/ppermute | solution.py:78
  61.4 9.6 %collective-permute-start.29 = (bf16[32,2176]{1,0:T(8,128)(2,1)S(1)}, bf16[32,2176]{1,0:T(8,128)(2,1)S(1)}, u32[]{:S(2)}, u32[]{:S(2)}) collective-permute-start(bf16[32,2176]{1,0:T(8,128)(2,1)S(1)} %get-tuple-element.97), channel_id=1, source_target_pairs={{0,4},{1,5},{2,6},{3,7},{4,0},{5,1},{6,2},{7,3},{8,12},{9,13},{10,... | collective-permute-start | bytes 417800 | tf_op jit(solution)/shard_map/ppermute | solution.py:78
  61.7 9.3 %collective-permute-start.30 = (bf16[32,2176]{1,0:T(8,128)(2,1)S(1)}, bf16[32,2176]{1,0:T(8,128)(2,1)S(1)}, u32[]{:S(2)}, u32[]{:S(2)}) collective-permute-start(bf16[32,2176]{1,0:T(8,128)(2,1)S(1)} %get-tuple-element.98), channel_id=1, source_target_pairs={{0,2},{1,3},{2,0},{3,1},{4,6},{5,7},{6,4},{7,5},{8,10},{9,11},{10,... | collective-permute-start | bytes 417800 | tf_op jit(solution)/shard_map/ppermute | solution.py:78
  63.4 10.7 %collective-permute-start.31 = (bf16[32,2176]{1,0:T(8,128)(2,1)S(1)}, bf16[32,2176]{1,0:T(8,128)(2,1)S(1)}, u32[]{:S(2)}, u32[]{:S(2)}) collective-permute-start(bf16[32,2176]{1,0:T(8,128)(2,1)S(1)} %get-tuple-element.99), channel_id=1, source_target_pairs={{0,6},{1,7},{2,4},{3,5},{4,2},{5,3},{6,0},{7,1},{8,14},{9,15},{10,... | collective-permute-start | bytes 417800 | tf_op jit(solution)/shard_map/ppermute | solution.py:78
  64.9 10.0 %collective-permute-start.32 = (bf16[32,2176]{1,0:T(8,128)(2,1)S(1)}, bf16[32,2176]{1,0:T(8,128)(2,1)S(1)}, u32[]{:S(2)}, u32[]{:S(2)}) collective-permute-start(bf16[32,2176]{1,0:T(8,128)(2,1)S(1)} %get-tuple-element.102), channel_id=1, source_target_pairs={{0,8},{1,9},{2,10},{3,11},{4,12},{5,13},{6,14},{7,15},{8,0},{9,1},... | collective-permute-start | bytes 417800 | tf_op jit(solution)/shard_map/ppermute | solution.py:78
  74.4 8.1 %collective-permute-start.33 = (bf16[32,2176]{1,0:T(8,128)(2,1)S(1)}, bf16[32,2176]{1,0:T(8,128)(2,1)S(1)}, u32[]{:S(2)}, u32[]{:S(2)}) collective-permute-start(bf16[32,2176]{1,0:T(8,128)(2,1)S(1)} %get-tuple-element.103), channel_id=1, source_target_pairs={{0,8},{1,9},{2,10},{3,11},{4,12},{5,13},{6,14},{7,15},{8,0},{9,1},... | collective-permute-start | bytes 417800 | tf_op jit(solution)/shard_map/ppermute | solution.py:78
  (2 other events, 2.7 us)

commit v8 on v7

--- a/solution.py
+++ b/solution.py
@@ -8,8 +8,8 @@
 from jax.sharding import PartitionSpec as P
 
 PIECES = 4
-SPLIT = 4
-JOINT = 2
+GROUPS = ((0, 1, 2), (3,))
+BESIDE = 6
 
 
 def product(left, right):
@@ -173,7 +173,8 @@
     )(inverse, kinetic)
 
 
-def near_kernel(chunk, tile, virt_ref, me_ref, energy_ref, inverse_ref, kinetic_ref, values_ref, laps_ref, out_ref, far_values, far_laps, near_values, near_laps, own_inverse, own_kinetic, sems):
+def near_kernel(chunk, tile, virt_ref, me_ref, energy_ref, inverse_ref, kinetic_ref, values_ref, laps_ref, *rest):
+    out_ref, far_values, far_laps, near_values, near_laps, own_inverse, own_kinetic, sems = rest[-8:]
     count, per, depth = inverse_ref.shape
     height = count * per
     width = out_ref.shape[3]
@@ -220,7 +221,7 @@
         copy.wait()
 
 
-def near_product(virt, me, energy, inverse, kinetic, values, laplacians):
+def near_product(virt, me, energy, inverse, kinetic, values, laplacians, after):
     count, per, depth = inverse.shape
     width = values.shape[1]
     chunk, tile = 512, 256
@@ -229,17 +230,17 @@
     return pl.pallas_call(
         functools.partial(near_kernel, chunk, tile),
         out_shape=(jax.ShapeDtypeStruct((2, count, per, width), jnp.float32), table, table),
-        in_specs=[SCALAR, SCALAR, SCALAR, HELD, HELD, HELD, HELD],
+        in_specs=[SCALAR, SCALAR, SCALAR, HELD, HELD, HELD, HELD] + [ANYWHERE] * len(after),
         out_specs=(WHOLE, WHOLE, WHOLE),
         scratch_shapes=[table, table, own, own, pltpu.SemaphoreType.DMA((width // chunk + 2, 2))],
         compiler_params=limit(24),
         cost_estimate=cost(9),
         name="near_product",
-    )(virt, me, energy, inverse, kinetic, values, laplacians)
-
-
-def far_kernel(weights, count, tile, first, virt_ref, me_ref, energy_ref, far_ref, near_ref, values_ref, laps_ref, *rest):
-    send_refs, (keep_ref, place_ref) = rest[-SPLIT - 2 : -2], rest[-2:]
+    )(virt, me, energy, inverse, kinetic, values, laplacians, *after)
+
+
+def far_kernel(weights, count, tile, first, split, virt_ref, me_ref, energy_ref, far_ref, near_ref, values_ref, laps_ref, *rest):
+    send_refs, (keep_ref, place_ref) = rest[-split - 2 : -2], rest[-2:]
     _, height, depth = far_ref.shape
     width = near_ref.shape[3]
     rows = height // count
@@ -272,17 +273,17 @@
     store_coded(send_refs, blocks, energy)
 
 
-def far_product(virt, me, energy, theirs, near, first, values, laplacians, tile, stages, after):
+def far_product(virt, me, energy, theirs, near, first, values, laplacians, tile, stages, split, after):
     _, height, depth = theirs.shape
     width = values.shape[1]
     half = height // 2
     count = 1 << sum(len(stage) for stage in stages)
     *sends, keep = pl.pallas_call(
-        functools.partial(far_kernel, place_weights(stages), count, tile, first),
-        out_shape=(jax.ShapeDtypeStruct((2 * half // SPLIT, width + EXTRA), jnp.bfloat16),) * SPLIT
+        functools.partial(far_kernel, place_weights(stages), count, tile, first, split),
+        out_shape=(jax.ShapeDtypeStruct((2 * half // split, width + EXTRA), jnp.bfloat16),) * split
         + (jax.ShapeDtypeStruct((2, half, width + EXTRA), jnp.float32),),
         in_specs=[SCALAR, SCALAR, SCALAR, WHOLE, WHOLE, WHOLE, WHOLE] + [ANYWHERE] * len(after),
-        out_specs=(WHOLE,) * (SPLIT + 1),
+        out_specs=(WHOLE,) * (split + 1),
         scratch_shapes=[pltpu.VMEM((2, height, width), jnp.float32)],
         compiler_params=limit(24),
         cost_estimate=cost(0.1),
@@ -312,7 +313,7 @@
         store_coded([send_ref], [block for blocks in sums for block in blocks[first : first + kept]], energy)
 
 
-def combine(keep, came, sent, carry, after):
+def combine(keep, came, sent, carry, after, length):
     _, height, width = keep.shape
     kept = height // (sent + 1)
     parts, senders = len(came[0]), len(came)
@@ -324,21 +325,19 @@
         in_specs=[WHOLE] * (1 + parts * senders) + [ANYWHERE] * len(after) + [WHOLE] * len(carry),
         out_specs=(WHOLE,) * (1 + sent),
         compiler_params=limit(8),
-        cost_estimate=cost(0.1),
+        cost_estimate=cost(length),
         name="combine",
     )(keep, *[part for parts in came for part in parts], *after, *carry)
     return [[send] for send in sends], keep
 
 
-def finish_kernel(count, joint, *refs):
+def finish_kernel(count, *refs):
     (gradient_ref, log_ref), refs = refs[-2:], refs[:-2]
-    groups = len(refs) // (joint + 1)
-    keep_refs, came_refs = refs[: joint * groups], refs[joint * groups :]
+    came = [ref.at[16 * place : 16 * place + 16, :] for ref, group in zip(refs[-len(GROUPS) :], GROUPS) for place in range(len(group))]
+    keep_refs = refs[: -len(GROUPS)]
     row = 0
     for piece, keep_ref in enumerate(keep_refs):
-        place = 16 * (piece % joint)
-        came = came_refs[piece // joint].at[place : place + 16, :]
-        (gradient, log), energy = add_came(keep_ref, [[came]])
+        (gradient, log), energy = add_came(keep_ref, [[came[piece]]])
         correction = 2.0 * (energy[:, :1] / count - OFFSET)
         for block in range(len(log)):
             log_mean = log[block] / count
@@ -351,7 +350,7 @@
     _, rows, width = keeps[0].shape
     out = jax.ShapeDtypeStruct((rows * len(keeps), width - EXTRA), jnp.float32)
     return pl.pallas_call(
-        functools.partial(finish_kernel, count, JOINT),
+        functools.partial(finish_kernel, count),
         out_shape=(out, out),
         in_specs=[WHOLE] * (len(keeps) + len(came)),
         out_specs=(WHOLE, WHOLE),
@@ -375,10 +374,9 @@
         pltpu.with_memory_space_constraint(array, pltpu.HBM)
         for array in (inverse, kinetic, virt_values[0], virt_laplacians[0])
     )
-    theirs = []
-    for group in range(pieces // 2):
-        theirs += [swap(mine, "virt", 1) for mine in cut(inverse, kinetic, group)]
-    near, values, laplacians = near_product(virt, me, local_energy, inverse, kinetic, values, laplacians)
+    mine = [part for group in range(pieces // 2) for part in cut(inverse, kinetic, group)]
+    theirs = [swap(part, "virt", 1) for part in mine]
+    near, values, laplacians = near_product(virt, me, local_energy, inverse, kinetic, values, laplacians, mine[2:])
 
     keep, first, came = {}, {}, []
     late, carry = [], ()
@@ -386,19 +384,19 @@
         if turn < pieces:
             after = [keep[turn - 1]] if turn else []
             send, kept = far_product(
-                virt, me, local_energy, theirs[turn], near, turn * rows, values, laplacians, tile, stages, after
+                virt, me, local_energy, theirs[turn], near, turn * rows, values, laplacians, tile, stages, 1 if turn else 2, after
             )
             first[turn] = [[swap(part, "walk", mask) for part in parts] for parts, mask in zip(send, partners(stages[0]))]
         if turn:
             piece = turn - 1
-            sends, keep[piece] = combine(keep[piece], second, len(partners(stages[2])), carry, [])
+            sends, keep[piece] = combine(keep[piece], second, len(partners(stages[2])), carry, [], BESIDE)
             carry = tuple(sends[0])
-            if turn % JOINT == 0:
+            if any(piece == group[-1] for group in GROUPS):
                 came.append(swap(carry[0], "walk", stages[2][0]))
                 carry = ()
         if turn < pieces:
             after = ([keep[turn - 1]] if turn else [])
-            sends, keep[turn] = combine(kept, first[turn], len(partners(stages[1])), (), after)
+            sends, keep[turn] = combine(kept, first[turn], len(partners(stages[1])), (), after, 0.1)
             second = [[swap(part, "walk", mask) for part in parts] for parts, mask in zip(sends, partners(stages[1]))]
     return finish([keep[piece] for piece in range(pieces)], came, count)
 

time: 83.7 us -> 78.4 us (0.937)
  waiting for transfers between devices: 26.2 us -> 23 us
  starting transfers between devices: 26.4 us -> 24.3 us
    ppermute x34 -> x23, waiting for transfers between devices: 26.2 us -> 23 us  [swap(): return lax.ppermute(array, axis, pairs)]
    ppermute x34 -> x23, starting transfers between devices: 26.4 us -> 24.3 us  [swap(): return lax.ppermute(array, axis, pairs)]
  transfers between devices with their start and end apart: 34 -> 23, of which waited for: 11 -> 12; matrix products, arithmetic and copies ran while one was open for 0% -> 0% of each run, Pallas kernels for 32% -> 34%
where the time goes in v8:
time: 78.4 us; the launch traced here: 78.3 us
  Pallas kernels  29.5 us (38%)
  starting transfers between devices  24.3 us (31%)
  waiting for transfers between devices  23 us (29%)
  between operations  1.48 us (2%)
    ppermute x23, starting transfers between devices, swap(): return lax.ppermute(array, axis, pairs)  24.3 us
    ppermute x23, waiting for transfers between devices, swap(): return lax.ppermute(array, axis, pairs)  23 us
    pallas_call x4, Pallas kernels, far_product(): pl.pallas_call(functools.partial(far_kernel, place_weights(stages), count...  11.4 us
    pallas_call x1, Pallas kernels, near_product(): pl.pallas_call(functools.partial(near_kernel, chunk, tile), out_shape=(ja...  10.3 us
    pallas_call x8, Pallas kernels, combine(): pl.pallas_call(functools.partial(combine_kernel, parts, senders, len(carr...  4.16 us
    pallas_call x2, Pallas kernels, cut(): pl.pallas_call(cut_kernel, out_shape=(out, out), grid=(1,), in_specs=[blo...  2.55 us
  transfers between devices with their start and end apart: 23, of which 12 were waited for; matrix products, arithmetic and copies ran while one was open for 0% of the time, Pallas kernels for 34%

profile of v8, /device:TPU:0, one launch (start us, length us, event | category | flops | bytes accessed | tf_op | source)
XLA Modules:
  0.0 78.3 jit_solution(11746173744787337286)
XLA Ops:
  0.6 1.3 %cut.2 = (bf16[2,128,1024]{2,1,0:T(8,128)(2,1)S(1)}, bf16[2,128,1024]{2,1,0:T(8,128)(2,1)S(1)}) custom-call(bf16[16,32,1024]{2,1,0:T(8,128)(2,1)} %bitcast.6, bf16[16,32,1024]{2,1,0:T(8,128)(2,1)} %bitcast.9), custom_call_target="tpu_custom_call" | custom-call | flops 110000000 | tf_op jit(solution)/shard_map/cut/pallas_call | solution.py:164
  1.9 3.0 %collective-permute-start = (bf16[2,128,1024]{2,1,0:T(8,128)(2,1)S(1)}, bf16[2,128,1024]{2,1,0:T(8,128)(2,1)S(1)}, u32[]{:S(2)}, u32[]{:S(2)}) collective-permute-start(bf16[2,128,1024]{2,1,0:T(8,128)(2,1)S(1)} %get-tuple-element.42), channel_id=1, source_target_pairs={{0,16},{16,0},{1,17},{17,1},{2,18},{18,2},{3,19},{19,3},{4,20},{20... | collective-permute-start | bytes 1572872 | tf_op jit(solution)/shard_map/ppermute | solution.py:78
  5.0 1.3 %cut.3 = (bf16[2,128,1024]{2,1,0:T(8,128)(2,1)S(1)}, bf16[2,128,1024]{2,1,0:T(8,128)(2,1)S(1)}) custom-call(bf16[16,32,1024]{2,1,0:T(8,128)(2,1)} %bitcast.7, bf16[16,32,1024]{2,1,0:T(8,128)(2,1)} %bitcast.10), custom_call_target="tpu_custom_call" | custom-call | flops 110000000 | tf_op jit(solution)/shard_map/cut/pallas_call | solution.py:164
  6.9 10.3 %near_product.1 = (f32[2,16,32,2048]{3,2,1,0:T(8,128)S(1)}, bf16[1024,2048]{1,0:T(8,128)(2,1)S(1)}, bf16[1024,2048]{1,0:T(8,128)(2,1)S(1)}) custom-call(s32[1]{0:T(128)} %bitcast.virt_ref, s32[1]{0:T(128)} %bitcast.1.me_ref, f32[1]{0:T(128)S(6)} %copy.7.energy_ref, bf16[16,32,1024]{2,1,0:T(8,128)(2,1)} %bitcast.8, bf16[16,32,1024]{2,1,0:T(8,128)(2,1)} %bitcast.11, ...), custom_call_target="tpu_custom_call" | custom-call | flops 9900000256 | tf_op jit(solution)/shard_map/near_product/pallas_call | solution.py:230
  17.7 2.8 %far_product.4 = (bf16[64,2176]{1,0:T(8,128)(2,1)S(1)}, bf16[64,2176]{1,0:T(8,128)(2,1)S(1)}, f32[2,64,2176]{2,1,0:T(8,128)S(1)}) custom-call(s32[1]{0:T(128)} %bitcast.virt_ref, s32[1]{0:T(128)} %bitcast.1.me_ref, f32[1]{0:T(128)S(6)} %copy.7.energy_ref, bf16[2,128,1024]{2,1,0:T(8,128)(2,1)S(1)} %collective-permute-done.far_ref, ...), custom_call_target="tpu_custom_call" | custom-call | flops 110000000 | tf_op jit(solution)/shard_map/far_product/pallas_call | solution.py:281
  21.1 1.0 %collective-permute-done.1.refs_1_ = bf16[64,2176]{1,0:T(8,128)(2,1)S(1)} collective-permute-done((bf16[64,2176]{1,0:T(8,128)(2,1)S(1)}, bf16[64,2176]{1,0:T(8,128)(2,1)S(1)}, u32[]{:S(2)}, u32[]{:S(2)}) %collective-permute-start.1) | collective-permute-done | bytes 278560 | tf_op jit(solution)/shard_map/ppermute | solution.py:78
  23.2 2.2 %collective-permute-start.3 = (bf16[32,2176]{1,0:T(8,128)(2,1)S(1)}, bf16[32,2176]{1,0:T(8,128)(2,1)S(1)}, u32[]{:S(2)}, u32[]{:S(2)}) collective-permute-start(bf16[32,2176]{1,0:T(8,128)(2,1)S(1)} %get-tuple-element.52), channel_id=1, source_target_pairs={{0,4},{1,5},{2,6},{3,7},{4,0},{5,1},{6,2},{7,3},{8,12},{9,13},{10,... | collective-permute-start | bytes 417800 | tf_op jit(solution)/shard_map/ppermute | solution.py:78
  25.4 1.5 %collective-permute-start.4 = (bf16[32,2176]{1,0:T(8,128)(2,1)S(1)}, bf16[32,2176]{1,0:T(8,128)(2,1)S(1)}, u32[]{:S(2)}, u32[]{:S(2)}) collective-permute-start(bf16[32,2176]{1,0:T(8,128)(2,1)S(1)} %get-tuple-element.53), channel_id=1, source_target_pairs={{0,2},{1,3},{2,0},{3,1},{4,6},{5,7},{6,4},{7,5},{8,10},{9,11},{10,... | collective-permute-start | bytes 417800 | tf_op jit(solution)/shard_map/ppermute | solution.py:78
  26.9 1.9 %collective-permute-start.11 = (bf16[2,128,1024]{2,1,0:T(8,128)(2,1)S(1)}, bf16[2,128,1024]{2,1,0:T(8,128)(2,1)S(1)}, u32[]{:S(2)}, u32[]{:S(2)}) collective-permute-start(bf16[2,128,1024]{2,1,0:T(8,128)(2,1)S(1)} %get-tuple-element.43.rest_0_), channel_id=1, source_target_pairs={{0,16},{16,0},{1,17},{17,1},{2,18},{18,2},{3,19},{19,3},{4,20},{20... | collective-permute-start | bytes 1572872 | tf_op jit(solution)/shard_map/ppermute | solution.py:78
  28.8 2.8 %far_product.5 = (bf16[128,2176]{1,0:T(8,128)(2,1)S(1)}, f32[2,64,2176]{2,1,0:T(8,128)S(1)}) custom-call(s32[1]{0:T(128)} %bitcast.virt_ref, s32[1]{0:T(128)} %bitcast.1.me_ref, f32[1]{0:T(128)S(6)} %copy.7.energy_ref, bf16[2,128,1024]{2,1,0:T(8,128)(2,1)S(1)} %collective-permute-done.6.far_ref, f32[2,16,32,2048]{3,2,1,0:T(8,128)S(1)} %get-tuple-element.45.near_ref, ...), custom_call_target="tpu_custom_call" | custom-call | flops 110000000 | tf_op jit(solution)/shard_map/far_product/pallas_call | solution.py:281
  31.7 2.1 %collective-permute-done.4.refs_2_ = bf16[32,2176]{1,0:T(8,128)(2,1)S(1)} collective-permute-done((bf16[32,2176]{1,0:T(8,128)(2,1)S(1)}, bf16[32,2176]{1,0:T(8,128)(2,1)S(1)}, u32[]{:S(2)}, u32[]{:S(2)}) %collective-permute-start.4) | collective-permute-done | bytes 139296 | tf_op jit(solution)/shard_map/ppermute | solution.py:78
  34.2 0.7 combine.10
  34.9 1.3 %collective-permute-start.8 = (bf16[32,2176]{1,0:T(8,128)(2,1)S(1)}, bf16[32,2176]{1,0:T(8,128)(2,1)S(1)}, u32[]{:S(2)}, u32[]{:S(2)}) collective-permute-start(bf16[32,2176]{1,0:T(8,128)(2,1)S(1)} %get-tuple-element.60), channel_id=1, source_target_pairs={{0,4},{1,5},{2,6},{3,7},{4,0},{5,1},{6,2},{7,3},{8,12},{9,13},{10,... | collective-permute-start | bytes 417800 | tf_op jit(solution)/shard_map/ppermute | solution.py:78
  36.2 1.3 %collective-permute-start.9 = (bf16[32,2176]{1,0:T(8,128)(2,1)S(1)}, bf16[32,2176]{1,0:T(8,128)(2,1)S(1)}, u32[]{:S(2)}, u32[]{:S(2)}) collective-permute-start(bf16[32,2176]{1,0:T(8,128)(2,1)S(1)} %get-tuple-element.61), channel_id=1, source_target_pairs={{0,2},{1,3},{2,0},{3,1},{4,6},{5,7},{6,4},{7,5},{8,10},{9,11},{10,... | collective-permute-start | bytes 417800 | tf_op jit(solution)/shard_map/ppermute | solution.py:78
  37.5 0.9 %collective-permute-start.10 = (bf16[32,2176]{1,0:T(8,128)(2,1)S(1)}, bf16[32,2176]{1,0:T(8,128)(2,1)S(1)}, u32[]{:S(2)}, u32[]{:S(2)}) collective-permute-start(bf16[32,2176]{1,0:T(8,128)(2,1)S(1)} %get-tuple-element.62), channel_id=1, source_target_pairs={{0,6},{1,7},{2,4},{3,5},{4,2},{5,3},{6,0},{7,1},{8,14},{9,15},{10,... | collective-permute-start | bytes 417800 | tf_op jit(solution)/shard_map/ppermute | solution.py:78
  38.4 1.5 %collective-permute-start.16 = (bf16[2,128,1024]{2,1,0:T(8,128)(2,1)S(1)}, bf16[2,128,1024]{2,1,0:T(8,128)(2,1)S(1)}, u32[]{:S(2)}, u32[]{:S(2)}) collective-permute-start(bf16[2,128,1024]{2,1,0:T(8,128)(2,1)S(1)} %get-tuple-element.44.rest_1_), channel_id=1, source_target_pairs={{0,16},{16,0},{1,17},{17,1},{2,18},{18,2},{3,19},{19,3},{4,20},{20... | collective-permute-start | bytes 1572872 | tf_op jit(solution)/shard_map/ppermute | solution.py:78
  40.0 0.8 %collective-permute-done.11.far_ref = bf16[2,128,1024]{2,1,0:T(8,128)(2,1)S(1)} collective-permute-done((bf16[2,128,1024]{2,1,0:T(8,128)(2,1)S(1)}, bf16[2,128,1024]{2,1,0:T(8,128)(2,1)S(1)}, u32[]{:S(2)}, u32[]{:S(2)}) %collective-permute-start.11) | collective-permute-done | bytes 524320 | tf_op jit(solution)/shard_map/ppermute | solution.py:78
  40.8 2.8 %far_product.6 = (bf16[128,2176]{1,0:T(8,128)(2,1)S(1)}, f32[2,64,2176]{2,1,0:T(8,128)S(1)}) custom-call(s32[1]{0:T(128)} %bitcast.virt_ref, s32[1]{0:T(128)} %bitcast.1.me_ref, f32[1]{0:T(128)S(6)} %copy.7.energy_ref, bf16[2,128,1024]{2,1,0:T(8,128)(2,1)S(1)} %collective-permute-done.11.far_ref, f32[2,16,32,2048]{3,2,1,0:T(8,128)S(1)} %get-tuple-element.45.near_ref, ...), custom_call_target="tpu_custom_call" | custom-call | flops 110000000 | tf_op jit(solution)/shard_map/far_product/pallas_call | solution.py:281
  43.7 0.7 collective-permute-done.9.refs_2_
  44.8 0.9 %collective-permute-done.12.refs_1_ = bf16[128,2176]{1,0:T(8,128)(2,1)S(1)} collective-permute-done((bf16[128,2176]{1,0:T(8,128)(2,1)S(1)}, bf16[128,2176]{1,0:T(8,128)(2,1)S(1)}, u32[]{:S(2)}, u32[]{:S(2)}) %collective-permute-start.12) | collective-permute-done | bytes 557088 | tf_op jit(solution)/shard_map/ppermute | solution.py:78
  46.4 1.8 %collective-permute-start.13 = (bf16[32,2176]{1,0:T(8,128)(2,1)S(1)}, bf16[32,2176]{1,0:T(8,128)(2,1)S(1)}, u32[]{:S(2)}, u32[]{:S(2)}) collective-permute-start(bf16[32,2176]{1,0:T(8,128)(2,1)S(1)} %get-tuple-element.68), channel_id=1, source_target_pairs={{0,4},{1,5},{2,6},{3,7},{4,0},{5,1},{6,2},{7,3},{8,12},{9,13},{10,... | collective-permute-start | bytes 417800 | tf_op jit(solution)/shard_map/ppermute | solution.py:78
  48.2 1.5 %collective-permute-start.14 = (bf16[32,2176]{1,0:T(8,128)(2,1)S(1)}, bf16[32,2176]{1,0:T(8,128)(2,1)S(1)}, u32[]{:S(2)}, u32[]{:S(2)}) collective-permute-start(bf16[32,2176]{1,0:T(8,128)(2,1)S(1)} %get-tuple-element.69), channel_id=1, source_target_pairs={{0,2},{1,3},{2,0},{3,1},{4,6},{5,7},{6,4},{7,5},{8,10},{9,11},{10,... | collective-permute-start | bytes 417800 | tf_op jit(solution)/shard_map/ppermute | solution.py:78
  49.9 1.7 %collective-permute-done.16.far_ref = bf16[2,128,1024]{2,1,0:T(8,128)(2,1)S(1)} collective-permute-done((bf16[2,128,1024]{2,1,0:T(8,128)(2,1)S(1)}, bf16[2,128,1024]{2,1,0:T(8,128)(2,1)S(1)}, u32[]{:S(2)}, u32[]{:S(2)}) %collective-permute-start.16) | collective-permute-done | bytes 524320 | tf_op jit(solution)/shard_map/ppermute | solution.py:78
  51.6 3.0 %far_product.7 = (bf16[128,2176]{1,0:T(8,128)(2,1)S(1)}, f32[2,64,2176]{2,1,0:T(8,128)S(1)}) custom-call(s32[1]{0:T(128)} %bitcast.virt_ref, s32[1]{0:T(128)} %bitcast.1.me_ref, f32[1]{0:T(128)S(6)} %copy.7.energy_ref, bf16[2,128,1024]{2,1,0:T(8,128)(2,1)S(1)} %collective-permute-done.16.far_ref, f32[2,16,32,2048]{3,2,1,0:T(8,128)S(1)} %get-tuple-element.45.near_ref, ...), custom_call_target="tpu_custom_call" | custom-call | flops 110000000 | tf_op jit(solution)/shard_map/far_product/pallas_call | solution.py:281
  54.7 1.9 %collective-permute-done.14.refs_2_ = bf16[32,2176]{1,0:T(8,128)(2,1)S(1)} collective-permute-done((bf16[32,2176]{1,0:T(8,128)(2,1)S(1)}, bf16[32,2176]{1,0:T(8,128)(2,1)S(1)}, u32[]{:S(2)}, u32[]{:S(2)}) %collective-permute-start.14) | collective-permute-done | bytes 139296 | tf_op jit(solution)/shard_map/ppermute | solution.py:78
  57.7 1.4 %collective-permute-start.18 = (bf16[32,2176]{1,0:T(8,128)(2,1)S(1)}, bf16[32,2176]{1,0:T(8,128)(2,1)S(1)}, u32[]{:S(2)}, u32[]{:S(2)}) collective-permute-start(bf16[32,2176]{1,0:T(8,128)(2,1)S(1)} %get-tuple-element.76), channel_id=1, source_target_pairs={{0,4},{1,5},{2,6},{3,7},{4,0},{5,1},{6,2},{7,3},{8,12},{9,13},{10,... | collective-permute-start | bytes 417800 | tf_op jit(solution)/shard_map/ppermute | solution.py:78
  59.0 1.5 %collective-permute-start.19 = (bf16[32,2176]{1,0:T(8,128)(2,1)S(1)}, bf16[32,2176]{1,0:T(8,128)(2,1)S(1)}, u32[]{:S(2)}, u32[]{:S(2)}) collective-permute-start(bf16[32,2176]{1,0:T(8,128)(2,1)S(1)} %get-tuple-element.77), channel_id=1, source_target_pairs={{0,2},{1,3},{2,0},{3,1},{4,6},{5,7},{6,4},{7,5},{8,10},{9,11},{10,... | collective-permute-start | bytes 417800 | tf_op jit(solution)/shard_map/ppermute | solution.py:78
  61.2 2.6 %collective-permute-start.21 = (bf16[48,2176]{1,0:T(8,128)(2,1)S(1)}, bf16[48,2176]{1,0:T(8,128)(2,1)S(1)}, u32[]{:S(2)}, u32[]{:S(2)}) collective-permute-start(bf16[48,2176]{1,0:T(8,128)(2,1)S(1)} %get-tuple-element.80), channel_id=1, source_target_pairs={{0,8},{1,9},{2,10},{3,11},{4,12},{5,13},{6,14},{7,15},{8,0},{9,1},... | collective-permute-start | bytes 626696 | tf_op jit(solution)/shard_map/ppermute | solution.py:78
  63.8 1.3 %collective-permute-done.19.refs_2_ = bf16[32,2176]{1,0:T(8,128)(2,1)S(1)} collective-permute-done((bf16[32,2176]{1,0:T(8,128)(2,1)S(1)}, bf16[32,2176]{1,0:T(8,128)(2,1)S(1)}, u32[]{:S(2)}, u32[]{:S(2)}) %collective-permute-start.19) | collective-permute-done | bytes 139296 | tf_op jit(solution)/shard_map/ppermute | solution.py:78
  65.1 6.4 %collective-permute-done.20.refs_3_ = bf16[32,2176]{1,0:T(8,128)(2,1)S(1)} collective-permute-done((bf16[32,2176]{1,0:T(8,128)(2,1)S(1)}, bf16[32,2176]{1,0:T(8,128)(2,1)S(1)}, u32[]{:S(2)}, u32[]{:S(2)}) %collective-permute-start.20) | collective-permute-done | bytes 139296 | tf_op jit(solution)/shard_map/ppermute | solution.py:78
  72.0 5.2 %collective-permute-done.22.refs_5_ = bf16[16,2176]{1,0:T(8,128)(2,1)S(1)} collective-permute-done((bf16[16,2176]{1,0:T(8,128)(2,1)S(1)}, bf16[16,2176]{1,0:T(8,128)(2,1)S(1)}, u32[]{:S(2)}, u32[]{:S(2)}) %collective-permute-start.22) | collective-permute-done | bytes 69664 | tf_op jit(solution)/shard_map/ppermute | solution.py:78
  77.2 1.1 %finish.1 = (f32[32,2048]{1,0:T(8,128)}, f32[32,2048]{1,0:T(8,128)}) custom-call(f32[2,8,2176]{2,1,0:T(8,128)S(1)} %get-tuple-element.55.refs_2_.refs_0_, f32[2,8,2176]{2,1,0:T(8,128)S(1)} %get-tuple-element.64.refs_2_.refs_1_, f32[2,8,2176]{2,1,0:T(8,128)S(1)} %get-tuple-element.72.refs_2_, f32[2,8,2176]{2,1,0:T(8,128)S(1)} %get-tuple-element.79.refs_3_, ...), custom_call_target="tpu_custom_call" | custom-call | flops 110000000 | tf_op jit(solution)/shard_map/finish/pallas_call | solution.py:352
  (30 shorter events, 6.3 us)
Async XLA Ops:
  1.9 15.8 %collective-permute-start = (bf16[2,128,1024]{2,1,0:T(8,128)(2,1)S(1)}, bf16[2,128,1024]{2,1,0:T(8,128)(2,1)S(1)}, u32[]{:S(2)}, u32[]{:S(2)}) collective-permute-start(bf16[2,128,1024]{2,1,0:T(8,128)(2,1)S(1)} %get-tuple-element.42), channel_id=1, source_target_pairs={{0,16},{16,0},{1,17},{17,1},{2,18},{18,2},{3,19},{19,3},{4,20},{20... | collective-permute-start | bytes 1572872 | tf_op jit(solution)/shard_map/ppermute | solution.py:78
  4.9 23.9 %collective-permute-start.6 = (bf16[2,128,1024]{2,1,0:T(8,128)(2,1)S(1)}, bf16[2,128,1024]{2,1,0:T(8,128)(2,1)S(1)}, u32[]{:S(2)}, u32[]{:S(2)}) collective-permute-start(bf16[2,128,1024]{2,1,0:T(8,128)(2,1)S(1)} %get-tuple-element.56), channel_id=1, source_target_pairs={{0,16},{16,0},{1,17},{17,1},{2,18},{18,2},{3,19},{19,3},{4,20},{20... | collective-permute-start | bytes 1572872 | tf_op jit(solution)/shard_map/ppermute | solution.py:78
  20.5 1.6 %collective-permute-start.1 = (bf16[64,2176]{1,0:T(8,128)(2,1)S(1)}, bf16[64,2176]{1,0:T(8,128)(2,1)S(1)}, u32[]{:S(2)}, u32[]{:S(2)}) collective-permute-start(bf16[64,2176]{1,0:T(8,128)(2,1)S(1)} %get-tuple-element.49), channel_id=1, source_target_pairs={{0,1},{1,0},{2,3},{3,2},{4,5},{5,4},{6,7},{7,6},{8,9},{9,8},{10,11... | collective-permute-start | bytes 835592 | tf_op jit(solution)/shard_map/ppermute | solution.py:78
  20.6 1.9 %collective-permute-start.2 = (bf16[64,2176]{1,0:T(8,128)(2,1)S(1)}, bf16[64,2176]{1,0:T(8,128)(2,1)S(1)}, u32[]{:S(2)}, u32[]{:S(2)}) collective-permute-start(bf16[64,2176]{1,0:T(8,128)(2,1)S(1)} %get-tuple-element.50), channel_id=1, source_target_pairs={{0,1},{1,0},{2,3},{3,2},{4,5},{5,4},{6,7},{7,6},{8,9},{9,8},{10,11... | collective-permute-start | bytes 835592 | tf_op jit(solution)/shard_map/ppermute | solution.py:78
  23.2 8.5 %collective-permute-start.3 = (bf16[32,2176]{1,0:T(8,128)(2,1)S(1)}, bf16[32,2176]{1,0:T(8,128)(2,1)S(1)}, u32[]{:S(2)}, u32[]{:S(2)}) collective-permute-start(bf16[32,2176]{1,0:T(8,128)(2,1)S(1)} %get-tuple-element.52), channel_id=1, source_target_pairs={{0,4},{1,5},{2,6},{3,7},{4,0},{5,1},{6,2},{7,3},{8,12},{9,13},{10,... | collective-permute-start | bytes 417800 | tf_op jit(solution)/shard_map/ppermute | solution.py:78
  25.4 8.4 %collective-permute-start.4 = (bf16[32,2176]{1,0:T(8,128)(2,1)S(1)}, bf16[32,2176]{1,0:T(8,128)(2,1)S(1)}, u32[]{:S(2)}, u32[]{:S(2)}) collective-permute-start(bf16[32,2176]{1,0:T(8,128)(2,1)S(1)} %get-tuple-element.53), channel_id=1, source_target_pairs={{0,2},{1,3},{2,0},{3,1},{4,6},{5,7},{6,4},{7,5},{8,10},{9,11},{10,... | collective-permute-start | bytes 417800 | tf_op jit(solution)/shard_map/ppermute | solution.py:78
  26.9 6.9 %collective-permute-start.5 = (bf16[32,2176]{1,0:T(8,128)(2,1)S(1)}, bf16[32,2176]{1,0:T(8,128)(2,1)S(1)}, u32[]{:S(2)}, u32[]{:S(2)}) collective-permute-start(bf16[32,2176]{1,0:T(8,128)(2,1)S(1)} %get-tuple-element.54), channel_id=1, source_target_pairs={{0,6},{1,7},{2,4},{3,5},{4,2},{5,3},{6,0},{7,1},{8,14},{9,15},{10,... | collective-permute-start | bytes 417800 | tf_op jit(solution)/shard_map/ppermute | solution.py:78
  26.9 13.9 %collective-permute-start.11 = (bf16[2,128,1024]{2,1,0:T(8,128)(2,1)S(1)}, bf16[2,128,1024]{2,1,0:T(8,128)(2,1)S(1)}, u32[]{:S(2)}, u32[]{:S(2)}) collective-permute-start(bf16[2,128,1024]{2,1,0:T(8,128)(2,1)S(1)} %get-tuple-element.43.rest_0_), channel_id=1, source_target_pairs={{0,16},{16,0},{1,17},{17,1},{2,18},{18,2},{3,19},{19,3},{4,20},{20... | collective-permute-start | bytes 1572872 | tf_op jit(solution)/shard_map/ppermute | solution.py:78
  31.7 2.5 %collective-permute-start.7 = (bf16[128,2176]{1,0:T(8,128)(2,1)S(1)}, bf16[128,2176]{1,0:T(8,128)(2,1)S(1)}, u32[]{:S(2)}, u32[]{:S(2)}) collective-permute-start(bf16[128,2176]{1,0:T(8,128)(2,1)S(1)} %get-tuple-element.58), channel_id=1, source_target_pairs={{0,1},{1,0},{2,3},{3,2},{4,5},{5,4},{6,7},{7,6},{8,9},{9,8},{10,11... | collective-permute-start | bytes 1671176 | tf_op jit(solution)/shard_map/ppermute | solution.py:78
  34.9 8.8 %collective-permute-start.8 = (bf16[32,2176]{1,0:T(8,128)(2,1)S(1)}, bf16[32,2176]{1,0:T(8,128)(2,1)S(1)}, u32[]{:S(2)}, u32[]{:S(2)}) collective-permute-start(bf16[32,2176]{1,0:T(8,128)(2,1)S(1)} %get-tuple-element.60), channel_id=1, source_target_pairs={{0,4},{1,5},{2,6},{3,7},{4,0},{5,1},{6,2},{7,3},{8,12},{9,13},{10,... | collective-permute-start | bytes 417800 | tf_op jit(solution)/shard_map/ppermute | solution.py:78
  36.2 8.3 %collective-permute-start.9 = (bf16[32,2176]{1,0:T(8,128)(2,1)S(1)}, bf16[32,2176]{1,0:T(8,128)(2,1)S(1)}, u32[]{:S(2)}, u32[]{:S(2)}) collective-permute-start(bf16[32,2176]{1,0:T(8,128)(2,1)S(1)} %get-tuple-element.61), channel_id=1, source_target_pairs={{0,2},{1,3},{2,0},{3,1},{4,6},{5,7},{6,4},{7,5},{8,10},{9,11},{10,... | collective-permute-start | bytes 417800 | tf_op jit(solution)/shard_map/ppermute | solution.py:78
  37.5 6.9 %collective-permute-start.10 = (bf16[32,2176]{1,0:T(8,128)(2,1)S(1)}, bf16[32,2176]{1,0:T(8,128)(2,1)S(1)}, u32[]{:S(2)}, u32[]{:S(2)}) collective-permute-start(bf16[32,2176]{1,0:T(8,128)(2,1)S(1)} %get-tuple-element.62), channel_id=1, source_target_pairs={{0,6},{1,7},{2,4},{3,5},{4,2},{5,3},{6,0},{7,1},{8,14},{9,15},{10,... | collective-permute-start | bytes 417800 | tf_op jit(solution)/shard_map/ppermute | solution.py:78
  38.4 13.1 %collective-permute-start.16 = (bf16[2,128,1024]{2,1,0:T(8,128)(2,1)S(1)}, bf16[2,128,1024]{2,1,0:T(8,128)(2,1)S(1)}, u32[]{:S(2)}, u32[]{:S(2)}) collective-permute-start(bf16[2,128,1024]{2,1,0:T(8,128)(2,1)S(1)} %get-tuple-element.44.rest_1_), channel_id=1, source_target_pairs={{0,16},{16,0},{1,17},{17,1},{2,18},{18,2},{3,19},{19,3},{4,20},{20... | collective-permute-start | bytes 1572872 | tf_op jit(solution)/shard_map/ppermute | solution.py:78
  43.6 2.0 %collective-permute-start.12 = (bf16[128,2176]{1,0:T(8,128)(2,1)S(1)}, bf16[128,2176]{1,0:T(8,128)(2,1)S(1)}, u32[]{:S(2)}, u32[]{:S(2)}) collective-permute-start(bf16[128,2176]{1,0:T(8,128)(2,1)S(1)} %get-tuple-element.66), channel_id=1, source_target_pairs={{0,1},{1,0},{2,3},{3,2},{4,5},{5,4},{6,7},{7,6},{8,9},{9,8},{10,11... | collective-permute-start | bytes 1671176 | tf_op jit(solution)/shard_map/ppermute | solution.py:78
  46.4 8.3 %collective-permute-start.13 = (bf16[32,2176]{1,0:T(8,128)(2,1)S(1)}, bf16[32,2176]{1,0:T(8,128)(2,1)S(1)}, u32[]{:S(2)}, u32[]{:S(2)}) collective-permute-start(bf16[32,2176]{1,0:T(8,128)(2,1)S(1)} %get-tuple-element.68), channel_id=1, source_target_pairs={{0,4},{1,5},{2,6},{3,7},{4,0},{5,1},{6,2},{7,3},{8,12},{9,13},{10,... | collective-permute-start | bytes 417800 | tf_op jit(solution)/shard_map/ppermute | solution.py:78
  48.2 8.4 %collective-permute-start.14 = (bf16[32,2176]{1,0:T(8,128)(2,1)S(1)}, bf16[32,2176]{1,0:T(8,128)(2,1)S(1)}, u32[]{:S(2)}, u32[]{:S(2)}) collective-permute-start(bf16[32,2176]{1,0:T(8,128)(2,1)S(1)} %get-tuple-element.69), channel_id=1, source_target_pairs={{0,2},{1,3},{2,0},{3,1},{4,6},{5,7},{6,4},{7,5},{8,10},{9,11},{10,... | collective-permute-start | bytes 417800 | tf_op jit(solution)/shard_map/ppermute | solution.py:78
  49.7 6.9 %collective-permute-start.15 = (bf16[32,2176]{1,0:T(8,128)(2,1)S(1)}, bf16[32,2176]{1,0:T(8,128)(2,1)S(1)}, u32[]{:S(2)}, u32[]{:S(2)}) collective-permute-start(bf16[32,2176]{1,0:T(8,128)(2,1)S(1)} %get-tuple-element.70), channel_id=1, source_target_pairs={{0,6},{1,7},{2,4},{3,5},{4,2},{5,3},{6,0},{7,1},{8,14},{9,15},{10,... | collective-permute-start | bytes 417800 | tf_op jit(solution)/shard_map/ppermute | solution.py:78
  54.6 2.4 %collective-permute-start.17 = (bf16[128,2176]{1,0:T(8,128)(2,1)S(1)}, bf16[128,2176]{1,0:T(8,128)(2,1)S(1)}, u32[]{:S(2)}, u32[]{:S(2)}) collective-permute-start(bf16[128,2176]{1,0:T(8,128)(2,1)S(1)} %get-tuple-element.74), channel_id=1, source_target_pairs={{0,1},{1,0},{2,3},{3,2},{4,5},{5,4},{6,7},{7,6},{8,9},{9,8},{10,11... | collective-permute-start | bytes 1671176 | tf_op jit(solution)/shard_map/ppermute | solution.py:78
  57.7 6.1 %collective-permute-start.18 = (bf16[32,2176]{1,0:T(8,128)(2,1)S(1)}, bf16[32,2176]{1,0:T(8,128)(2,1)S(1)}, u32[]{:S(2)}, u32[]{:S(2)}) collective-permute-start(bf16[32,2176]{1,0:T(8,128)(2,1)S(1)} %get-tuple-element.76), channel_id=1, source_target_pairs={{0,4},{1,5},{2,6},{3,7},{4,0},{5,1},{6,2},{7,3},{8,12},{9,13},{10,... | collective-permute-start | bytes 417800 | tf_op jit(solution)/shard_map/ppermute | solution.py:78
  59.0 6.1 %collective-permute-start.19 = (bf16[32,2176]{1,0:T(8,128)(2,1)S(1)}, bf16[32,2176]{1,0:T(8,128)(2,1)S(1)}, u32[]{:S(2)}, u32[]{:S(2)}) collective-permute-start(bf16[32,2176]{1,0:T(8,128)(2,1)S(1)} %get-tuple-element.77), channel_id=1, source_target_pairs={{0,2},{1,3},{2,0},{3,1},{4,6},{5,7},{6,4},{7,5},{8,10},{9,11},{10,... | collective-permute-start | bytes 417800 | tf_op jit(solution)/shard_map/ppermute | solution.py:78
  60.5 11.0 %collective-permute-start.20 = (bf16[32,2176]{1,0:T(8,128)(2,1)S(1)}, bf16[32,2176]{1,0:T(8,128)(2,1)S(1)}, u32[]{:S(2)}, u32[]{:S(2)}) collective-permute-start(bf16[32,2176]{1,0:T(8,128)(2,1)S(1)} %get-tuple-element.78), channel_id=1, source_target_pairs={{0,6},{1,7},{2,4},{3,5},{4,2},{5,3},{6,0},{7,1},{8,14},{9,15},{10,... | collective-permute-start | bytes 417800 | tf_op jit(solution)/shard_map/ppermute | solution.py:78
  61.2 10.8 %collective-permute-start.21 = (bf16[48,2176]{1,0:T(8,128)(2,1)S(1)}, bf16[48,2176]{1,0:T(8,128)(2,1)S(1)}, u32[]{:S(2)}, u32[]{:S(2)}) collective-permute-start(bf16[48,2176]{1,0:T(8,128)(2,1)S(1)} %get-tuple-element.80), channel_id=1, source_target_pairs={{0,8},{1,9},{2,10},{3,11},{4,12},{5,13},{6,14},{7,15},{8,0},{9,1},... | collective-permute-start | bytes 626696 | tf_op jit(solution)/shard_map/ppermute | solution.py:78
  71.9 5.3 %collective-permute-start.22 = (bf16[16,2176]{1,0:T(8,128)(2,1)S(1)}, bf16[16,2176]{1,0:T(8,128)(2,1)S(1)}, u32[]{:S(2)}, u32[]{:S(2)}) collective-permute-start(bf16[16,2176]{1,0:T(8,128)(2,1)S(1)} %get-tuple-element.81), channel_id=1, source_target_pairs={{0,8},{1,9},{2,10},{3,11},{4,12},{5,13},{6,14},{7,15},{8,0},{9,1},... | collective-permute-start | bytes 208904 | tf_op jit(solution)/shard_map/ppermute | solution.py:78

commit v9 on v8

--- a/solution.py
+++ b/solution.py
@@ -9,6 +9,7 @@
 
 PIECES = 4
 GROUPS = ((0, 1, 2), (3,))
+EXCHANGED = (3,)
 BESIDE = 6
 
 
@@ -76,6 +77,20 @@
 def swap(array, axis, mask):
     pairs = [(source, source ^ mask) for source in range(lax.axis_size(axis))]
     return lax.ppermute(array, axis, pairs)
+
+
+def exchange(array, stage):
+    first, second = stage
+    count = lax.axis_size("walk")
+    groups = [
+        [base, base + first, base + second, base + first + second]
+        for base in range(count)
+        if not base & (first | second)
+    ]
+    return lax.all_to_all(array, "walk", 0, 0, axis_index_groups=groups, tiled=True)
+
+
+PLACES = (2, 1, 3)
 
 
 def encode(rows):
@@ -292,10 +307,11 @@
     return [sends], keep
 
 
-def combine_kernel(parts, senders, carried, ordered, *refs):
-    keep_ref, refs = refs[0], refs[1:]
+def combine_kernel(parts, senders, carried, ordered, slots_in, slots_out, me_ref, keep_ref, *refs):
     came_refs = [refs[parts * sender : parts * sender + parts] for sender in range(senders)]
     refs = refs[parts * senders + ordered :]
+    if slots_in:
+        came_refs = [[came_refs[0][0].at[(me_ref[0] // slots_in & 3) ^ place]] for place in PLACES]
     kept_ref, send_refs = refs[carried], refs[carried + 1 :]
     width = keep_ref.shape[2] - EXTRA
     sums, energy = add_came(keep_ref, came_refs)
@@ -304,6 +320,11 @@
         for index, block in enumerate(blocks[:kept]):
             kept_ref[array, 8 * index : 8 * index + 8, :width] = block
     kept_ref[0, :8, width:] = energy
+    if slots_out:
+        place = me_ref[0] // slots_out & 3
+        send_refs = [send_refs[0].at[place]] + [send_refs[0].at[place ^ other] for other in PLACES]
+        store_coded(send_refs[:1], [block for blocks in sums for block in blocks[:kept]], energy)
+        send_refs = send_refs[1:]
     for index, send_ref in enumerate(send_refs):
         if carried:
             above = refs[0].shape[0]
@@ -313,21 +334,22 @@
         store_coded([send_ref], [block for blocks in sums for block in blocks[first : first + kept]], energy)
 
 
-def combine(keep, came, sent, carry, after, length):
+def combine(me, keep, came, sent, carry, after, length, slots_in=0, slots_out=0):
     _, height, width = keep.shape
     kept = height // (sent + 1)
     parts, senders = len(came[0]), len(came)
     above = sum(array.shape[0] for array in carry)
+    coded = jax.ShapeDtypeStruct((above + 2 * kept, width), jnp.bfloat16)
+    coded = (jax.ShapeDtypeStruct((4, 2 * kept, width), jnp.bfloat16),) if slots_out else (coded,) * sent
     keep, *sends = pl.pallas_call(
-        functools.partial(combine_kernel, parts, senders, len(carry), len(after)),
-        out_shape=(jax.ShapeDtypeStruct((2, kept, width), jnp.float32),)
-        + (jax.ShapeDtypeStruct((above + 2 * kept, width), jnp.bfloat16),) * sent,
-        in_specs=[WHOLE] * (1 + parts * senders) + [ANYWHERE] * len(after) + [WHOLE] * len(carry),
-        out_specs=(WHOLE,) * (1 + sent),
+        functools.partial(combine_kernel, parts, senders, len(carry), len(after), slots_in, slots_out),
+        out_shape=(jax.ShapeDtypeStruct((2, kept, width), jnp.float32),) + coded,
+        in_specs=[SCALAR] + [WHOLE] * (1 + parts * senders) + [ANYWHERE] * len(after) + [WHOLE] * len(carry),
+        out_specs=(WHOLE,) * (1 + len(coded)),
         compiler_params=limit(8),
         cost_estimate=cost(length),
         name="combine",
-    )(keep, *[part for parts in came for part in parts], *after, *carry)
+    )(me, keep, *[part for parts in came for part in parts], *after, *carry)
     return [[send] for send in sends], keep
 
 
@@ -379,7 +401,7 @@
     near, values, laplacians = near_product(virt, me, local_energy, inverse, kinetic, values, laplacians, mine[2:])
 
     keep, first, came = {}, {}, []
-    late, carry = [], ()
+    carry, slots = (), 0
     for turn in range(pieces + 1):
         if turn < pieces:
             after = [keep[turn - 1]] if turn else []
@@ -389,15 +411,23 @@
             first[turn] = [[swap(part, "walk", mask) for part in parts] for parts, mask in zip(send, partners(stages[0]))]
         if turn:
             piece = turn - 1
-            sends, keep[piece] = combine(keep[piece], second, len(partners(stages[2])), carry, [], BESIDE)
+            sends, keep[piece] = combine(
+                me, keep[piece], second, len(partners(stages[2])), carry, [], BESIDE, slots_in=slots
+            )
             carry = tuple(sends[0])
             if any(piece == group[-1] for group in GROUPS):
                 came.append(swap(carry[0], "walk", stages[2][0]))
                 carry = ()
         if turn < pieces:
-            after = ([keep[turn - 1]] if turn else [])
-            sends, keep[turn] = combine(kept, first[turn], len(partners(stages[1])), (), after, 0.1)
-            second = [[swap(part, "walk", mask) for part in parts] for parts, mask in zip(sends, partners(stages[1]))]
+            after = [keep[turn - 1]] if turn else []
+            slots = stages[1][0] if turn in EXCHANGED else 0
+            sends, keep[turn] = combine(
+                me, kept, first[turn], len(partners(stages[1])), (), after, 0.1, slots_out=slots
+            )
+            if slots:
+                second = [[exchange(sends[0][0], stages[1])]]
+            else:
+                second = [[swap(part, "walk", mask) for part in parts] for parts, mask in zip(sends, partners(stages[1]))]
     return finish([keep[piece] for piece in range(pieces)], came, count)
 
 

time: 78.4 us -> 81.9 us (1.045)
  waiting for transfers between devices: 23 us -> 25.7 us
    all_to_all x0 -> x1, waiting for transfers between devices: none -> 10.3 us  [exchange(): lax.all_to_all(array, 'walk', 0, 0, axis_index_groups=groups, tiled=True)]
    ppermute x23 -> x20, waiting for transfers between devices: 23 us -> 15.4 us  [swap(): return lax.ppermute(array, axis, pairs)]
    ppermute x23 -> x20, starting transfers between devices: 24.3 us -> 20.9 us  [swap(): return lax.ppermute(array, axis, pairs)]
    all_to_all x0 -> x1, starting transfers between devices: none -> 3.47 us  [exchange(): lax.all_to_all(array, 'walk', 0, 0, axis_index_groups=groups, tiled=True)]
    pallas_call x8, Pallas kernels: 4.16 us -> 5.03 us  [combine(): pl.pallas_call(functools.partial(combine_kernel, parts, senders, len(carr...]
  transfers between devices with their start and end apart: 23 -> 21, of which waited for: 12 -> 11; matrix products, arithmetic and copies ran while one was open for 0% -> 0% of each run, Pallas kernels for 34% -> 32%
where the time goes in v9:
time: 81.9 us; the launch traced here: 81.6 us
  Pallas kernels  30.2 us (37%)
  waiting for transfers between devices  25.7 us (31%)
  starting transfers between devices  24.3 us (30%)
  between operations  1.47 us (2%)
    ppermute x20, starting transfers between devices, swap(): return lax.ppermute(array, axis, pairs)  20.9 us
    ppermute x20, waiting for transfers between devices, swap(): return lax.ppermute(array, axis, pairs)  15.4 us
    pallas_call x4, Pallas kernels, far_product(): pl.pallas_call(functools.partial(far_kernel, place_weights(stages), count...  11.2 us
    all_to_all x1, waiting for transfers between devices, exchange(): lax.all_to_all(array, 'walk', 0, 0, axis_index_groups=groups, tiled=True)  10.3 us
    pallas_call x1, Pallas kernels, near_product(): pl.pallas_call(functools.partial(near_kernel, chunk, tile), out_shape=(ja...  10.3 us
    pallas_call x8, Pallas kernels, combine(): pl.pallas_call(functools.partial(combine_kernel, parts, senders, len(carr...  5.03 us
    all_to_all x1, starting transfers between devices, exchange(): lax.all_to_all(array, 'walk', 0, 0, axis_index_groups=groups, tiled=True)  3.47 us
    pallas_call x2, Pallas kernels, cut(): pl.pallas_call(cut_kernel, out_shape=(out, out), grid=(1,), in_specs=[blo...  2.55 us
  transfers between devices with their start and end apart: 21, of which 11 were waited for; matrix products, arithmetic and copies ran while one was open for 0% of the time, Pallas kernels for 32%

profile of v9, /device:TPU:0, one launch (start us, length us, event | category | flops | bytes accessed | tf_op | source)
XLA Modules:
  0.0 81.6 jit_solution(4261889469424461386)
XLA Ops:
  0.6 1.3 %cut.2 = (bf16[2,128,1024]{2,1,0:T(8,128)(2,1)S(1)}, bf16[2,128,1024]{2,1,0:T(8,128)(2,1)S(1)}) custom-call(bf16[16,32,1024]{2,1,0:T(8,128)(2,1)} %bitcast.6, bf16[16,32,1024]{2,1,0:T(8,128)(2,1)} %bitcast.9), custom_call_target="tpu_custom_call" | custom-call | flops 110000000 | tf_op jit(solution)/shard_map/cut/pallas_call | solution.py:179
  1.9 3.0 %collective-permute-start = (bf16[2,128,1024]{2,1,0:T(8,128)(2,1)S(1)}, bf16[2,128,1024]{2,1,0:T(8,128)(2,1)S(1)}, u32[]{:S(2)}, u32[]{:S(2)}) collective-permute-start(bf16[2,128,1024]{2,1,0:T(8,128)(2,1)S(1)} %get-tuple-element.40), channel_id=1, source_target_pairs={{0,16},{16,0},{1,17},{17,1},{2,18},{18,2},{3,19},{19,3},{4,20},{20... | collective-permute-start | bytes 1572872 | tf_op jit(solution)/shard_map/ppermute | solution.py:79
  5.0 1.3 %cut.3 = (bf16[2,128,1024]{2,1,0:T(8,128)(2,1)S(1)}, bf16[2,128,1024]{2,1,0:T(8,128)(2,1)S(1)}) custom-call(bf16[16,32,1024]{2,1,0:T(8,128)(2,1)} %bitcast.7, bf16[16,32,1024]{2,1,0:T(8,128)(2,1)} %bitcast.10), custom_call_target="tpu_custom_call" | custom-call | flops 110000000 | tf_op jit(solution)/shard_map/cut/pallas_call | solution.py:179
  6.9 10.3 %near_product.1 = (f32[2,16,32,2048]{3,2,1,0:T(8,128)S(1)}, bf16[1024,2048]{1,0:T(8,128)(2,1)S(1)}, bf16[1024,2048]{1,0:T(8,128)(2,1)S(1)}) custom-call(s32[1]{0:T(128)} %bitcast.1.virt_ref, s32[1]{0:T(128)} %bitcast.me_ref, f32[1]{0:T(128)S(6)} %copy.7.energy_ref, bf16[16,32,1024]{2,1,0:T(8,128)(2,1)} %bitcast.8, bf16[16,32,1024]{2,1,0:T(8,128)(2,1)} %bitcast.11, ...), custom_call_target="tpu_custom_call" | custom-call | flops 9900000256 | tf_op jit(solution)/shard_map/near_product/pallas_call | solution.py:245
  17.7 2.8 %far_product.4 = (bf16[64,2176]{1,0:T(8,128)(2,1)S(1)}, bf16[64,2176]{1,0:T(8,128)(2,1)S(1)}, f32[2,64,2176]{2,1,0:T(8,128)S(1)}) custom-call(s32[1]{0:T(128)} %bitcast.1.virt_ref, s32[1]{0:T(128)} %bitcast.me_ref, f32[1]{0:T(128)S(6)} %copy.7.energy_ref, bf16[2,128,1024]{2,1,0:T(8,128)(2,1)S(1)} %collective-permute-done.far_ref, ...), custom_call_target="tpu_custom_call" | custom-call | flops 110000000 | tf_op jit(solution)/shard_map/far_product/pallas_call | solution.py:296
  21.1 1.0 %collective-permute-done.1.refs_0_ = bf16[64,2176]{1,0:T(8,128)(2,1)S(1)} collective-permute-done((bf16[64,2176]{1,0:T(8,128)(2,1)S(1)}, bf16[64,2176]{1,0:T(8,128)(2,1)S(1)}, u32[]{:S(2)}, u32[]{:S(2)}) %collective-permute-start.1) | collective-permute-done | bytes 278560 | tf_op jit(solution)/shard_map/ppermute | solution.py:79
  22.5 0.7 combine.8
  23.2 2.2 %collective-permute-start.3 = (bf16[32,2176]{1,0:T(8,128)(2,1)S(1)}, bf16[32,2176]{1,0:T(8,128)(2,1)S(1)}, u32[]{:S(2)}, u32[]{:S(2)}) collective-permute-start(bf16[32,2176]{1,0:T(8,128)(2,1)S(1)} %get-tuple-element.50), channel_id=1, source_target_pairs={{0,4},{1,5},{2,6},{3,7},{4,0},{5,1},{6,2},{7,3},{8,12},{9,13},{10,... | collective-permute-start | bytes 417800 | tf_op jit(solution)/shard_map/ppermute | solution.py:79
  25.4 1.5 %collective-permute-start.4 = (bf16[32,2176]{1,0:T(8,128)(2,1)S(1)}, bf16[32,2176]{1,0:T(8,128)(2,1)S(1)}, u32[]{:S(2)}, u32[]{:S(2)}) collective-permute-start(bf16[32,2176]{1,0:T(8,128)(2,1)S(1)} %get-tuple-element.51), channel_id=1, source_target_pairs={{0,2},{1,3},{2,0},{3,1},{4,6},{5,7},{6,4},{7,5},{8,10},{9,11},{10,... | collective-permute-start | bytes 417800 | tf_op jit(solution)/shard_map/ppermute | solution.py:79
  26.9 1.9 %collective-permute-start.11 = (bf16[2,128,1024]{2,1,0:T(8,128)(2,1)S(1)}, bf16[2,128,1024]{2,1,0:T(8,128)(2,1)S(1)}, u32[]{:S(2)}, u32[]{:S(2)}) collective-permute-start(bf16[2,128,1024]{2,1,0:T(8,128)(2,1)S(1)} %get-tuple-element.41.rest_0_), channel_id=1, source_target_pairs={{0,16},{16,0},{1,17},{17,1},{2,18},{18,2},{3,19},{19,3},{4,20},{20... | collective-permute-start | bytes 1572872 | tf_op jit(solution)/shard_map/ppermute | solution.py:79
  28.8 2.8 %far_product.5 = (bf16[128,2176]{1,0:T(8,128)(2,1)S(1)}, f32[2,64,2176]{2,1,0:T(8,128)S(1)}) custom-call(s32[1]{0:T(128)} %bitcast.1.virt_ref, s32[1]{0:T(128)} %bitcast.me_ref, f32[1]{0:T(128)S(6)} %copy.7.energy_ref, bf16[2,128,1024]{2,1,0:T(8,128)(2,1)S(1)} %collective-permute-done.6.far_ref, f32[2,16,32,2048]{3,2,1,0:T(8,128)S(1)} %get-tuple-element.43.near_ref, ...), custom_call_target="tpu_custom_call" | custom-call | flops 110000000 | tf_op jit(solution)/shard_map/far_product/pallas_call | solution.py:296
  31.7 2.1 %collective-permute-done.4.refs_1_ = bf16[32,2176]{1,0:T(8,128)(2,1)S(1)} collective-permute-done((bf16[32,2176]{1,0:T(8,128)(2,1)S(1)}, bf16[32,2176]{1,0:T(8,128)(2,1)S(1)}, u32[]{:S(2)}, u32[]{:S(2)}) %collective-permute-start.4) | collective-permute-done | bytes 139296 | tf_op jit(solution)/shard_map/ppermute | solution.py:79
  34.2 0.7 combine.10
  34.9 1.3 %collective-permute-start.8 = (bf16[32,2176]{1,0:T(8,128)(2,1)S(1)}, bf16[32,2176]{1,0:T(8,128)(2,1)S(1)}, u32[]{:S(2)}, u32[]{:S(2)}) collective-permute-start(bf16[32,2176]{1,0:T(8,128)(2,1)S(1)} %get-tuple-element.58), channel_id=1, source_target_pairs={{0,4},{1,5},{2,6},{3,7},{4,0},{5,1},{6,2},{7,3},{8,12},{9,13},{10,... | collective-permute-start | bytes 417800 | tf_op jit(solution)/shard_map/ppermute | solution.py:79
  36.2 1.3 %collective-permute-start.9 = (bf16[32,2176]{1,0:T(8,128)(2,1)S(1)}, bf16[32,2176]{1,0:T(8,128)(2,1)S(1)}, u32[]{:S(2)}, u32[]{:S(2)}) collective-permute-start(bf16[32,2176]{1,0:T(8,128)(2,1)S(1)} %get-tuple-element.59), channel_id=1, source_target_pairs={{0,2},{1,3},{2,0},{3,1},{4,6},{5,7},{6,4},{7,5},{8,10},{9,11},{10,... | collective-permute-start | bytes 417800 | tf_op jit(solution)/shard_map/ppermute | solution.py:79
  37.5 0.9 %collective-permute-start.10 = (bf16[32,2176]{1,0:T(8,128)(2,1)S(1)}, bf16[32,2176]{1,0:T(8,128)(2,1)S(1)}, u32[]{:S(2)}, u32[]{:S(2)}) collective-permute-start(bf16[32,2176]{1,0:T(8,128)(2,1)S(1)} %get-tuple-element.60), channel_id=1, source_target_pairs={{0,6},{1,7},{2,4},{3,5},{4,2},{5,3},{6,0},{7,1},{8,14},{9,15},{10,... | collective-permute-start | bytes 417800 | tf_op jit(solution)/shard_map/ppermute | solution.py:79
  38.5 1.5 %collective-permute-start.16 = (bf16[2,128,1024]{2,1,0:T(8,128)(2,1)S(1)}, bf16[2,128,1024]{2,1,0:T(8,128)(2,1)S(1)}, u32[]{:S(2)}, u32[]{:S(2)}) collective-permute-start(bf16[2,128,1024]{2,1,0:T(8,128)(2,1)S(1)} %get-tuple-element.42.rest_1_), channel_id=1, source_target_pairs={{0,16},{16,0},{1,17},{17,1},{2,18},{18,2},{3,19},{19,3},{4,20},{20... | collective-permute-start | bytes 1572872 | tf_op jit(solution)/shard_map/ppermute | solution.py:79
  40.0 0.8 %collective-permute-done.11.far_ref = bf16[2,128,1024]{2,1,0:T(8,128)(2,1)S(1)} collective-permute-done((bf16[2,128,1024]{2,1,0:T(8,128)(2,1)S(1)}, bf16[2,128,1024]{2,1,0:T(8,128)(2,1)S(1)}, u32[]{:S(2)}, u32[]{:S(2)}) %collective-permute-start.11) | collective-permute-done | bytes 524320 | tf_op jit(solution)/shard_map/ppermute | solution.py:79
  40.8 2.8 %far_product.6 = (bf16[128,2176]{1,0:T(8,128)(2,1)S(1)}, f32[2,64,2176]{2,1,0:T(8,128)S(1)}) custom-call(s32[1]{0:T(128)} %bitcast.1.virt_ref, s32[1]{0:T(128)} %bitcast.me_ref, f32[1]{0:T(128)S(6)} %copy.7.energy_ref, bf16[2,128,1024]{2,1,0:T(8,128)(2,1)S(1)} %collective-permute-done.11.far_ref, f32[2,16,32,2048]{3,2,1,0:T(8,128)S(1)} %get-tuple-element.43.near_ref, ...), custom_call_target="tpu_custom_call" | custom-call | flops 110000000 | tf_op jit(solution)/shard_map/far_product/pallas_call | solution.py:296
  43.7 0.7 collective-permute-done.9.refs_1_
  44.8 0.9 %collective-permute-done.12.refs_0_ = bf16[128,2176]{1,0:T(8,128)(2,1)S(1)} collective-permute-done((bf16[128,2176]{1,0:T(8,128)(2,1)S(1)}, bf16[128,2176]{1,0:T(8,128)(2,1)S(1)}, u32[]{:S(2)}, u32[]{:S(2)}) %collective-permute-start.12) | collective-permute-done | bytes 557088 | tf_op jit(solution)/shard_map/ppermute | solution.py:79
  46.4 1.8 %collective-permute-start.13 = (bf16[32,2176]{1,0:T(8,128)(2,1)S(1)}, bf16[32,2176]{1,0:T(8,128)(2,1)S(1)}, u32[]{:S(2)}, u32[]{:S(2)}) collective-permute-start(bf16[32,2176]{1,0:T(8,128)(2,1)S(1)} %get-tuple-element.66), channel_id=1, source_target_pairs={{0,4},{1,5},{2,6},{3,7},{4,0},{5,1},{6,2},{7,3},{8,12},{9,13},{10,... | collective-permute-start | bytes 417800 | tf_op jit(solution)/shard_map/ppermute | solution.py:79
  48.2 1.5 %collective-permute-start.14 = (bf16[32,2176]{1,0:T(8,128)(2,1)S(1)}, bf16[32,2176]{1,0:T(8,128)(2,1)S(1)}, u32[]{:S(2)}, u32[]{:S(2)}) collective-permute-start(bf16[32,2176]{1,0:T(8,128)(2,1)S(1)} %get-tuple-element.67), channel_id=1, source_target_pairs={{0,2},{1,3},{2,0},{3,1},{4,6},{5,7},{6,4},{7,5},{8,10},{9,11},{10,... | collective-permute-start | bytes 417800 | tf_op jit(solution)/shard_map/ppermute | solution.py:79
  49.9 1.7 %collective-permute-done.16.far_ref = bf16[2,128,1024]{2,1,0:T(8,128)(2,1)S(1)} collective-permute-done((bf16[2,128,1024]{2,1,0:T(8,128)(2,1)S(1)}, bf16[2,128,1024]{2,1,0:T(8,128)(2,1)S(1)}, u32[]{:S(2)}, u32[]{:S(2)}) %collective-permute-start.16) | collective-permute-done | bytes 524320 | tf_op jit(solution)/shard_map/ppermute | solution.py:79
  51.6 2.8 %far_product.7 = (bf16[128,2176]{1,0:T(8,128)(2,1)S(1)}, f32[2,64,2176]{2,1,0:T(8,128)S(1)}) custom-call(s32[1]{0:T(128)} %bitcast.1.virt_ref, s32[1]{0:T(128)} %bitcast.me_ref, f32[1]{0:T(128)S(6)} %copy.7.energy_ref, bf16[2,128,1024]{2,1,0:T(8,128)(2,1)S(1)} %collective-permute-done.16.far_ref, f32[2,16,32,2048]{3,2,1,0:T(8,128)S(1)} %get-tuple-element.43.near_ref, ...), custom_call_target="tpu_custom_call" | custom-call | flops 110000000 | tf_op jit(solution)/shard_map/far_product/pallas_call | solution.py:296
  54.5 2.1 %collective-permute-done.14.refs_1_ = bf16[32,2176]{1,0:T(8,128)(2,1)S(1)} collective-permute-done((bf16[32,2176]{1,0:T(8,128)(2,1)S(1)}, bf16[32,2176]{1,0:T(8,128)(2,1)S(1)}, u32[]{:S(2)}, u32[]{:S(2)}) %collective-permute-start.14) | collective-permute-done | bytes 139296 | tf_op jit(solution)/shard_map/ppermute | solution.py:79
  57.0 1.5 %combine.14 = (f32[2,16,2176]{2,1,0:T(8,128)S(1)}, bf16[4,32,2176]{2,1,0:T(8,128)(2,1)}) custom-call(s32[1]{0:T(128)} %bitcast.me_ref, f32[2,64,2176]{2,1,0:T(8,128)S(1)} %get-tuple-element.71.keep_ref, bf16[128,2176]{1,0:T(8,128)(2,1)S(1)} %collective-permute-done.17.refs_0_, f32[2,8,2176]{2,1,0:T(8,128)S(1)} %get-tuple-element.70.refs_1_.refs_2_), custom_call_target="tpu_custom_call" | custom-call | flops 110000000 | tf_op jit(solution)/shard_map/combine/pallas_call | solution.py:344
  58.5 3.5 %all-to-all-start = ((bf16[4,32,2176]{2,1,0:T(8,128)(2,1)}), bf16[4,32,2176]{2,1,0:T(8,128)(2,1)S(1)}, u32[]{:S(2)}, u32[]{:S(2)}) async-start(bf16[4,32,2176]{2,1,0:T(8,128)(2,1)} %get-tuple-element.74), calls=%async_computation | async-start | bytes 1114112 | tf_op jit(solution)/shard_map/all_to_all | solution.py:90
  62.0 2.7 %collective-permute-start.18 = (bf16[48,2176]{1,0:T(8,128)(2,1)S(1)}, bf16[48,2176]{1,0:T(8,128)(2,1)S(1)}, u32[]{:S(2)}, u32[]{:S(2)}) collective-permute-start(bf16[48,2176]{1,0:T(8,128)(2,1)S(1)} %get-tuple-element.76), channel_id=1, source_target_pairs={{0,8},{1,9},{2,10},{3,11},{4,12},{5,13},{6,14},{7,15},{8,0},{9,1},... | collective-permute-start | bytes 626696 | tf_op jit(solution)/shard_map/ppermute | solution.py:79
  64.6 10.3 %all-to-all-done.refs_0_ = bf16[4,32,2176]{2,1,0:T(8,128)(2,1)S(1)} async-done(((bf16[4,32,2176]{2,1,0:T(8,128)(2,1)}), bf16[4,32,2176]{2,1,0:T(8,128)(2,1)S(1)}, u32[]{:S(2)}, u32[]{:S(2)}) %all-to-all-start) | async-done | bytes 557088 | tf_op jit(solution)/shard_map/all_to_all | solution.py:90
  75.4 5.2 %collective-permute-done.19.refs_5_ = bf16[16,2176]{1,0:T(8,128)(2,1)S(1)} collective-permute-done((bf16[16,2176]{1,0:T(8,128)(2,1)S(1)}, bf16[16,2176]{1,0:T(8,128)(2,1)S(1)}, u32[]{:S(2)}, u32[]{:S(2)}) %collective-permute-start.19) | collective-permute-done | bytes 69664 | tf_op jit(solution)/shard_map/ppermute | solution.py:79
  80.6 1.1 %finish.1 = (f32[32,2048]{1,0:T(8,128)}, f32[32,2048]{1,0:T(8,128)}) custom-call(f32[2,8,2176]{2,1,0:T(8,128)S(1)} %get-tuple-element.53.refs_1_.refs_0_, f32[2,8,2176]{2,1,0:T(8,128)S(1)} %get-tuple-element.62.refs_1_, f32[2,8,2176]{2,1,0:T(8,128)S(1)} %get-tuple-element.70.refs_1_.refs_2_, f32[2,8,2176]{2,1,0:T(8,128)S(1)} %get-tuple-element.75.refs_3_, ...), custom_call_target="tpu_custom_call" | custom-call | flops 110000000 | tf_op jit(solution)/shard_map/finish/pallas_call | solution.py:374
  (26 shorter events, 4.2 us)
Async XLA Ops:
  1.9 15.8 %collective-permute-start = (bf16[2,128,1024]{2,1,0:T(8,128)(2,1)S(1)}, bf16[2,128,1024]{2,1,0:T(8,128)(2,1)S(1)}, u32[]{:S(2)}, u32[]{:S(2)}) collective-permute-start(bf16[2,128,1024]{2,1,0:T(8,128)(2,1)S(1)} %get-tuple-element.40), channel_id=1, source_target_pairs={{0,16},{16,0},{1,17},{17,1},{2,18},{18,2},{3,19},{19,3},{4,20},{20... | collective-permute-start | bytes 1572872 | tf_op jit(solution)/shard_map/ppermute | solution.py:79
  4.9 23.9 %collective-permute-start.6 = (bf16[2,128,1024]{2,1,0:T(8,128)(2,1)S(1)}, bf16[2,128,1024]{2,1,0:T(8,128)(2,1)S(1)}, u32[]{:S(2)}, u32[]{:S(2)}) collective-permute-start(bf16[2,128,1024]{2,1,0:T(8,128)(2,1)S(1)} %get-tuple-element.54), channel_id=1, source_target_pairs={{0,16},{16,0},{1,17},{17,1},{2,18},{18,2},{3,19},{19,3},{4,20},{20... | collective-permute-start | bytes 1572872 | tf_op jit(solution)/shard_map/ppermute | solution.py:79
  20.5 1.6 %collective-permute-start.1 = (bf16[64,2176]{1,0:T(8,128)(2,1)S(1)}, bf16[64,2176]{1,0:T(8,128)(2,1)S(1)}, u32[]{:S(2)}, u32[]{:S(2)}) collective-permute-start(bf16[64,2176]{1,0:T(8,128)(2,1)S(1)} %get-tuple-element.47), channel_id=1, source_target_pairs={{0,1},{1,0},{2,3},{3,2},{4,5},{5,4},{6,7},{7,6},{8,9},{9,8},{10,11... | collective-permute-start | bytes 835592 | tf_op jit(solution)/shard_map/ppermute | solution.py:79
  20.6 1.9 %collective-permute-start.2 = (bf16[64,2176]{1,0:T(8,128)(2,1)S(1)}, bf16[64,2176]{1,0:T(8,128)(2,1)S(1)}, u32[]{:S(2)}, u32[]{:S(2)}) collective-permute-start(bf16[64,2176]{1,0:T(8,128)(2,1)S(1)} %get-tuple-element.48), channel_id=1, source_target_pairs={{0,1},{1,0},{2,3},{3,2},{4,5},{5,4},{6,7},{7,6},{8,9},{9,8},{10,11... | collective-permute-start | bytes 835592 | tf_op jit(solution)/shard_map/ppermute | solution.py:79
  23.2 8.5 %collective-permute-start.3 = (bf16[32,2176]{1,0:T(8,128)(2,1)S(1)}, bf16[32,2176]{1,0:T(8,128)(2,1)S(1)}, u32[]{:S(2)}, u32[]{:S(2)}) collective-permute-start(bf16[32,2176]{1,0:T(8,128)(2,1)S(1)} %get-tuple-element.50), channel_id=1, source_target_pairs={{0,4},{1,5},{2,6},{3,7},{4,0},{5,1},{6,2},{7,3},{8,12},{9,13},{10,... | collective-permute-start | bytes 417800 | tf_op jit(solution)/shard_map/ppermute | solution.py:79
  25.4 8.4 %collective-permute-start.4 = (bf16[32,2176]{1,0:T(8,128)(2,1)S(1)}, bf16[32,2176]{1,0:T(8,128)(2,1)S(1)}, u32[]{:S(2)}, u32[]{:S(2)}) collective-permute-start(bf16[32,2176]{1,0:T(8,128)(2,1)S(1)} %get-tuple-element.51), channel_id=1, source_target_pairs={{0,2},{1,3},{2,0},{3,1},{4,6},{5,7},{6,4},{7,5},{8,10},{9,11},{10,... | collective-permute-start | bytes 417800 | tf_op jit(solution)/shard_map/ppermute | solution.py:79
  26.9 6.9 %collective-permute-start.5 = (bf16[32,2176]{1,0:T(8,128)(2,1)S(1)}, bf16[32,2176]{1,0:T(8,128)(2,1)S(1)}, u32[]{:S(2)}, u32[]{:S(2)}) collective-permute-start(bf16[32,2176]{1,0:T(8,128)(2,1)S(1)} %get-tuple-element.52), channel_id=1, source_target_pairs={{0,6},{1,7},{2,4},{3,5},{4,2},{5,3},{6,0},{7,1},{8,14},{9,15},{10,... | collective-permute-start | bytes 417800 | tf_op jit(solution)/shard_map/ppermute | solution.py:79
  26.9 13.9 %collective-permute-start.11 = (bf16[2,128,1024]{2,1,0:T(8,128)(2,1)S(1)}, bf16[2,128,1024]{2,1,0:T(8,128)(2,1)S(1)}, u32[]{:S(2)}, u32[]{:S(2)}) collective-permute-start(bf16[2,128,1024]{2,1,0:T(8,128)(2,1)S(1)} %get-tuple-element.41.rest_0_), channel_id=1, source_target_pairs={{0,16},{16,0},{1,17},{17,1},{2,18},{18,2},{3,19},{19,3},{4,20},{20... | collective-permute-start | bytes 1572872 | tf_op jit(solution)/shard_map/ppermute | solution.py:79
  31.7 2.5 %collective-permute-start.7 = (bf16[128,2176]{1,0:T(8,128)(2,1)S(1)}, bf16[128,2176]{1,0:T(8,128)(2,1)S(1)}, u32[]{:S(2)}, u32[]{:S(2)}) collective-permute-start(bf16[128,2176]{1,0:T(8,128)(2,1)S(1)} %get-tuple-element.56), channel_id=1, source_target_pairs={{0,1},{1,0},{2,3},{3,2},{4,5},{5,4},{6,7},{7,6},{8,9},{9,8},{10,11... | collective-permute-start | bytes 1671176 | tf_op jit(solution)/shard_map/ppermute | solution.py:79
  34.9 8.8 %collective-permute-start.8 = (bf16[32,2176]{1,0:T(8,128)(2,1)S(1)}, bf16[32,2176]{1,0:T(8,128)(2,1)S(1)}, u32[]{:S(2)}, u32[]{:S(2)}) collective-permute-start(bf16[32,2176]{1,0:T(8,128)(2,1)S(1)} %get-tuple-element.58), channel_id=1, source_target_pairs={{0,4},{1,5},{2,6},{3,7},{4,0},{5,1},{6,2},{7,3},{8,12},{9,13},{10,... | collective-permute-start | bytes 417800 | tf_op jit(solution)/shard_map/ppermute | solution.py:79
  36.2 8.3 %collective-permute-start.9 = (bf16[32,2176]{1,0:T(8,128)(2,1)S(1)}, bf16[32,2176]{1,0:T(8,128)(2,1)S(1)}, u32[]{:S(2)}, u32[]{:S(2)}) collective-permute-start(bf16[32,2176]{1,0:T(8,128)(2,1)S(1)} %get-tuple-element.59), channel_id=1, source_target_pairs={{0,2},{1,3},{2,0},{3,1},{4,6},{5,7},{6,4},{7,5},{8,10},{9,11},{10,... | collective-permute-start | bytes 417800 | tf_op jit(solution)/shard_map/ppermute | solution.py:79
  37.5 6.9 %collective-permute-start.10 = (bf16[32,2176]{1,0:T(8,128)(2,1)S(1)}, bf16[32,2176]{1,0:T(8,128)(2,1)S(1)}, u32[]{:S(2)}, u32[]{:S(2)}) collective-permute-start(bf16[32,2176]{1,0:T(8,128)(2,1)S(1)} %get-tuple-element.60), channel_id=1, source_target_pairs={{0,6},{1,7},{2,4},{3,5},{4,2},{5,3},{6,0},{7,1},{8,14},{9,15},{10,... | collective-permute-start | bytes 417800 | tf_op jit(solution)/shard_map/ppermute | solution.py:79
  38.5 13.1 %collective-permute-start.16 = (bf16[2,128,1024]{2,1,0:T(8,128)(2,1)S(1)}, bf16[2,128,1024]{2,1,0:T(8,128)(2,1)S(1)}, u32[]{:S(2)}, u32[]{:S(2)}) collective-permute-start(bf16[2,128,1024]{2,1,0:T(8,128)(2,1)S(1)} %get-tuple-element.42.rest_1_), channel_id=1, source_target_pairs={{0,16},{16,0},{1,17},{17,1},{2,18},{18,2},{3,19},{19,3},{4,20},{20... | collective-permute-start | bytes 1572872 | tf_op jit(solution)/shard_map/ppermute | solution.py:79
  43.6 2.0 %collective-permute-start.12 = (bf16[128,2176]{1,0:T(8,128)(2,1)S(1)}, bf16[128,2176]{1,0:T(8,128)(2,1)S(1)}, u32[]{:S(2)}, u32[]{:S(2)}) collective-permute-start(bf16[128,2176]{1,0:T(8,128)(2,1)S(1)} %get-tuple-element.64), channel_id=1, source_target_pairs={{0,1},{1,0},{2,3},{3,2},{4,5},{5,4},{6,7},{7,6},{8,9},{9,8},{10,11... | collective-permute-start | bytes 1671176 | tf_op jit(solution)/shard_map/ppermute | solution.py:79
  46.4 8.1 %collective-permute-start.13 = (bf16[32,2176]{1,0:T(8,128)(2,1)S(1)}, bf16[32,2176]{1,0:T(8,128)(2,1)S(1)}, u32[]{:S(2)}, u32[]{:S(2)}) collective-permute-start(bf16[32,2176]{1,0:T(8,128)(2,1)S(1)} %get-tuple-element.66), channel_id=1, source_target_pairs={{0,4},{1,5},{2,6},{3,7},{4,0},{5,1},{6,2},{7,3},{8,12},{9,13},{10,... | collective-permute-start | bytes 417800 | tf_op jit(solution)/shard_map/ppermute | solution.py:79
  48.2 8.4 %collective-permute-start.14 = (bf16[32,2176]{1,0:T(8,128)(2,1)S(1)}, bf16[32,2176]{1,0:T(8,128)(2,1)S(1)}, u32[]{:S(2)}, u32[]{:S(2)}) collective-permute-start(bf16[32,2176]{1,0:T(8,128)(2,1)S(1)} %get-tuple-element.67), channel_id=1, source_target_pairs={{0,2},{1,3},{2,0},{3,1},{4,6},{5,7},{6,4},{7,5},{8,10},{9,11},{10,... | collective-permute-start | bytes 417800 | tf_op jit(solution)/shard_map/ppermute | solution.py:79
  49.7 6.9 %collective-permute-start.15 = (bf16[32,2176]{1,0:T(8,128)(2,1)S(1)}, bf16[32,2176]{1,0:T(8,128)(2,1)S(1)}, u32[]{:S(2)}, u32[]{:S(2)}) collective-permute-start(bf16[32,2176]{1,0:T(8,128)(2,1)S(1)} %get-tuple-element.68), channel_id=1, source_target_pairs={{0,6},{1,7},{2,4},{3,5},{4,2},{5,3},{6,0},{7,1},{8,14},{9,15},{10,... | collective-permute-start | bytes 417800 | tf_op jit(solution)/shard_map/ppermute | solution.py:79
  54.4 2.6 %collective-permute-start.17 = (bf16[128,2176]{1,0:T(8,128)(2,1)S(1)}, bf16[128,2176]{1,0:T(8,128)(2,1)S(1)}, u32[]{:S(2)}, u32[]{:S(2)}) collective-permute-start(bf16[128,2176]{1,0:T(8,128)(2,1)S(1)} %get-tuple-element.72), channel_id=1, source_target_pairs={{0,1},{1,0},{2,3},{3,2},{4,5},{5,4},{6,7},{7,6},{8,9},{9,8},{10,11... | collective-permute-start | bytes 1671176 | tf_op jit(solution)/shard_map/ppermute | solution.py:79
  58.5 16.4 %all-to-all-start = ((bf16[4,32,2176]{2,1,0:T(8,128)(2,1)}), bf16[4,32,2176]{2,1,0:T(8,128)(2,1)S(1)}, u32[]{:S(2)}, u32[]{:S(2)}) async-start(bf16[4,32,2176]{2,1,0:T(8,128)(2,1)} %get-tuple-element.74), calls=%async_computation | async-start | bytes 1114112 | tf_op jit(solution)/shard_map/all_to_all | solution.py:90
  62.0 13.4 %collective-permute-start.18 = (bf16[48,2176]{1,0:T(8,128)(2,1)S(1)}, bf16[48,2176]{1,0:T(8,128)(2,1)S(1)}, u32[]{:S(2)}, u32[]{:S(2)}) collective-permute-start(bf16[48,2176]{1,0:T(8,128)(2,1)S(1)} %get-tuple-element.76), channel_id=1, source_target_pairs={{0,8},{1,9},{2,10},{3,11},{4,12},{5,13},{6,14},{7,15},{8,0},{9,1},... | collective-permute-start | bytes 626696 | tf_op jit(solution)/shard_map/ppermute | solution.py:79
  75.3 5.3 %collective-permute-start.19 = (bf16[16,2176]{1,0:T(8,128)(2,1)S(1)}, bf16[16,2176]{1,0:T(8,128)(2,1)S(1)}, u32[]{:S(2)}, u32[]{:S(2)}) collective-permute-start(bf16[16,2176]{1,0:T(8,128)(2,1)S(1)} %get-tuple-element.77), channel_id=1, source_target_pairs={{0,8},{1,9},{2,10},{3,11},{4,12},{5,13},{6,14},{7,15},{8,0},{9,1},... | collective-permute-start | bytes 208904 | tf_op jit(solution)/shard_map/ppermute | solution.py:79

commit v10 on v8

--- a/solution.py
+++ b/solution.py
@@ -8,7 +8,8 @@
 from jax.sharding import PartitionSpec as P
 
 PIECES = 4
-GROUPS = ((0, 1, 2), (3,))
+GROUPS = ((0, 1), (2,), (3,))
+FAR = (0.1, 1.5, 0.1, 0.1)
 BESIDE = 6
 
 
@@ -273,7 +274,7 @@
     store_coded(send_refs, blocks, energy)
 
 
-def far_product(virt, me, energy, theirs, near, first, values, laplacians, tile, stages, split, after):
+def far_product(virt, me, energy, theirs, near, first, values, laplacians, tile, stages, split, after, length):
     _, height, depth = theirs.shape
     width = values.shape[1]
     half = height // 2
@@ -286,7 +287,7 @@
         out_specs=(WHOLE,) * (split + 1),
         scratch_shapes=[pltpu.VMEM((2, height, width), jnp.float32)],
         compiler_params=limit(24),
-        cost_estimate=cost(0.1),
+        cost_estimate=cost(length),
         name="far_product",
     )(virt, me, energy, theirs, near, values, laplacians, *after)
     return [sends], keep
@@ -384,12 +385,12 @@
         if turn < pieces:
             after = [keep[turn - 1]] if turn else []
             send, kept = far_product(
-                virt, me, local_energy, theirs[turn], near, turn * rows, values, laplacians, tile, stages, 1 if turn else 2, after
+                virt, me, local_energy, theirs[turn], near, turn * rows, values, laplacians, tile, stages, 1 if turn else 2, after, FAR[turn]
             )
             first[turn] = [[swap(part, "walk", mask) for part in parts] for parts, mask in zip(send, partners(stages[0]))]
         if turn:
             piece = turn - 1
-            sends, keep[piece] = combine(keep[piece], second, len(partners(stages[2])), carry, [], BESIDE)
+            sends, keep[piece] = combine(keep[piece], second, len(partners(stages[2])), carry, came if turn == pieces - 1 else [], BESIDE)
             carry = tuple(sends[0])
             if any(piece == group[-1] for group in GROUPS):
                 came.append(swap(carry[0], "walk", stages[2][0]))
@@ -397,7 +398,10 @@
         if turn < pieces:
             after = ([keep[turn - 1]] if turn else [])
             sends, keep[turn] = combine(kept, first[turn], len(partners(stages[1])), (), after, 0.1)
-            second = [[swap(part, "walk", mask) for part in parts] for parts, mask in zip(sends, partners(stages[1]))]
+            second = [
+                [swap(part, "walk", mask) for part in parts]
+                for parts, mask in reversed(list(zip(sends, partners(stages[1]))))
+            ]
     return finish([keep[piece] for piece in range(pieces)], came, count)
 
 

time: 78.4 us -> 78 us (level)
  waiting for transfers between devices: 23 us -> 21.2 us
  starting transfers between devices: 24.3 us -> 25.7 us
    ppermute x23 -> x24, waiting for transfers between devices: 23 us -> 21.2 us  [swap(): return lax.ppermute(array, axis, pairs)]
    ppermute x23 -> x24, starting transfers between devices: 24.3 us -> 25.7 us  [swap(): return lax.ppermute(array, axis, pairs)]
  transfers between devices with their start and end apart: 23 -> 24, of which waited for: 12 -> 11; matrix products, arithmetic and copies ran while one was open for 0% -> 0% of each run, Pallas kernels for 34% -> 34%
where the time goes in v10:
time: 78 us; the launch traced here: 77.8 us
  Pallas kernels  29.5 us (38%)
  starting transfers between devices  25.7 us (33%)
  waiting for transfers between devices  21.2 us (27%)
  between operations  1.48 us (2%)
    ppermute x24, starting transfers between devices, swap(): return lax.ppermute(array, axis, pairs)  25.7 us
    ppermute x24, waiting for transfers between devices, swap(): return lax.ppermute(array, axis, pairs)  21.2 us
    pallas_call x4, Pallas kernels, far_product(): pl.pallas_call(functools.partial(far_kernel, place_weights(stages), count...  11.4 us
    pallas_call x1, Pallas kernels, near_product(): pl.pallas_call(functools.partial(near_kernel, chunk, tile), out_shape=(ja...  10.3 us
    pallas_call x8, Pallas kernels, combine(): pl.pallas_call(functools.partial(combine_kernel, parts, senders, len(carr...  4.16 us
    pallas_call x2, Pallas kernels, cut(): pl.pallas_call(cut_kernel, out_shape=(out, out), grid=(1,), in_specs=[blo...  2.55 us
  transfers between devices with their start and end apart: 24, of which 11 were waited for; matrix products, arithmetic and copies ran while one was open for 0% of the time, Pallas kernels for 34%

profile of v10, /device:TPU:0, one launch (start us, length us, event | category | flops | bytes accessed | tf_op | source)
XLA Modules:
  0.0 77.8 jit_solution(3588604650840598775)
XLA Ops:
  0.6 1.3 %cut.2 = (bf16[2,128,1024]{2,1,0:T(8,128)(2,1)S(1)}, bf16[2,128,1024]{2,1,0:T(8,128)(2,1)S(1)}) custom-call(bf16[16,32,1024]{2,1,0:T(8,128)(2,1)} %bitcast.6, bf16[16,32,1024]{2,1,0:T(8,128)(2,1)} %bitcast.9), custom_call_target="tpu_custom_call" | custom-call | flops 110000000 | tf_op jit(solution)/shard_map/cut/pallas_call | solution.py:165
  1.9 3.0 %collective-permute-start = (bf16[2,128,1024]{2,1,0:T(8,128)(2,1)S(1)}, bf16[2,128,1024]{2,1,0:T(8,128)(2,1)S(1)}, u32[]{:S(2)}, u32[]{:S(2)}) collective-permute-start(bf16[2,128,1024]{2,1,0:T(8,128)(2,1)S(1)} %get-tuple-element.42), channel_id=1, source_target_pairs={{0,16},{16,0},{1,17},{17,1},{2,18},{18,2},{3,19},{19,3},{4,20},{20... | collective-permute-start | bytes 1572872 | tf_op jit(solution)/shard_map/ppermute | solution.py:79
  5.0 1.3 %cut.3 = (bf16[2,128,1024]{2,1,0:T(8,128)(2,1)S(1)}, bf16[2,128,1024]{2,1,0:T(8,128)(2,1)S(1)}) custom-call(bf16[16,32,1024]{2,1,0:T(8,128)(2,1)} %bitcast.7, bf16[16,32,1024]{2,1,0:T(8,128)(2,1)} %bitcast.10), custom_call_target="tpu_custom_call" | custom-call | flops 110000000 | tf_op jit(solution)/shard_map/cut/pallas_call | solution.py:165
  6.9 10.3 %near_product.1 = (f32[2,16,32,2048]{3,2,1,0:T(8,128)S(1)}, bf16[1024,2048]{1,0:T(8,128)(2,1)S(1)}, bf16[1024,2048]{1,0:T(8,128)(2,1)S(1)}) custom-call(s32[1]{0:T(128)} %bitcast.virt_ref, s32[1]{0:T(128)} %bitcast.1.me_ref, f32[1]{0:T(128)S(6)} %copy.7.energy_ref, bf16[16,32,1024]{2,1,0:T(8,128)(2,1)} %bitcast.8, bf16[16,32,1024]{2,1,0:T(8,128)(2,1)} %bitcast.11, ...), custom_call_target="tpu_custom_call" | custom-call | flops 9900000256 | tf_op jit(solution)/shard_map/near_product/pallas_call | solution.py:231
  17.7 2.8 %far_product.4 = (bf16[64,2176]{1,0:T(8,128)(2,1)S(1)}, bf16[64,2176]{1,0:T(8,128)(2,1)S(1)}, f32[2,64,2176]{2,1,0:T(8,128)S(1)}) custom-call(s32[1]{0:T(128)} %bitcast.virt_ref, s32[1]{0:T(128)} %bitcast.1.me_ref, f32[1]{0:T(128)S(6)} %copy.7.energy_ref, bf16[2,128,1024]{2,1,0:T(8,128)(2,1)S(1)} %collective-permute-done.far_ref, ...), custom_call_target="tpu_custom_call" | custom-call | flops 110000000 | tf_op jit(solution)/shard_map/far_product/pallas_call | solution.py:282
  21.1 2.1 %collective-permute-start.11 = (bf16[2,128,1024]{2,1,0:T(8,128)(2,1)S(1)}, bf16[2,128,1024]{2,1,0:T(8,128)(2,1)S(1)}, u32[]{:S(2)}, u32[]{:S(2)}) collective-permute-start(bf16[2,128,1024]{2,1,0:T(8,128)(2,1)S(1)} %get-tuple-element.43.rest_0_), channel_id=1, source_target_pairs={{0,16},{16,0},{1,17},{17,1},{2,18},{18,2},{3,19},{19,3},{4,20},{20... | collective-permute-start | bytes 1572872 | tf_op jit(solution)/shard_map/ppermute | solution.py:79
  23.1 0.7 combine.8
  23.8 2.6 %collective-permute-start.3 = (bf16[32,2176]{1,0:T(8,128)(2,1)S(1)}, bf16[32,2176]{1,0:T(8,128)(2,1)S(1)}, u32[]{:S(2)}, u32[]{:S(2)}) collective-permute-start(bf16[32,2176]{1,0:T(8,128)(2,1)S(1)} %get-tuple-element.52), channel_id=1, source_target_pairs={{0,6},{1,7},{2,4},{3,5},{4,2},{5,3},{6,0},{7,1},{8,14},{9,15},{10,... | collective-permute-start | bytes 417800 | tf_op jit(solution)/shard_map/ppermute | solution.py:79
  27.4 1.5 %collective-permute-done.6.far_ref = bf16[2,128,1024]{2,1,0:T(8,128)(2,1)S(1)} collective-permute-done((bf16[2,128,1024]{2,1,0:T(8,128)(2,1)S(1)}, bf16[2,128,1024]{2,1,0:T(8,128)(2,1)S(1)}, u32[]{:S(2)}, u32[]{:S(2)}) %collective-permute-start.6) | collective-permute-done | bytes 524320 | tf_op jit(solution)/shard_map/ppermute | solution.py:79
  28.9 2.8 %far_product.5 = (bf16[128,2176]{1,0:T(8,128)(2,1)S(1)}, f32[2,64,2176]{2,1,0:T(8,128)S(1)}) custom-call(s32[1]{0:T(128)} %bitcast.virt_ref, s32[1]{0:T(128)} %bitcast.1.me_ref, f32[1]{0:T(128)S(6)} %copy.7.energy_ref, bf16[2,128,1024]{2,1,0:T(8,128)(2,1)S(1)} %collective-permute-done.6.far_ref, f32[2,16,32,2048]{3,2,1,0:T(8,128)S(1)} %get-tuple-element.45.near_ref, ...), custom_call_target="tpu_custom_call" | custom-call | flops 1650000000 | tf_op jit(solution)/shard_map/far_product/pallas_call | solution.py:282
  31.8 1.5 %collective-permute-done.4.refs_2_ = bf16[32,2176]{1,0:T(8,128)(2,1)S(1)} collective-permute-done((bf16[32,2176]{1,0:T(8,128)(2,1)S(1)}, bf16[32,2176]{1,0:T(8,128)(2,1)S(1)}, u32[]{:S(2)}, u32[]{:S(2)}) %collective-permute-start.4) | collective-permute-done | bytes 139296 | tf_op jit(solution)/shard_map/ppermute | solution.py:79
  33.8 0.7 combine.10
  34.5 3.0 %collective-permute-start.8 = (bf16[32,2176]{1,0:T(8,128)(2,1)S(1)}, bf16[32,2176]{1,0:T(8,128)(2,1)S(1)}, u32[]{:S(2)}, u32[]{:S(2)}) collective-permute-start(bf16[32,2176]{1,0:T(8,128)(2,1)S(1)} %get-tuple-element.60), channel_id=1, source_target_pairs={{0,6},{1,7},{2,4},{3,5},{4,2},{5,3},{6,0},{7,1},{8,14},{9,15},{10,... | collective-permute-start | bytes 417800 | tf_op jit(solution)/shard_map/ppermute | solution.py:79
  38.2 1.9 %collective-permute-start.17 = (bf16[2,128,1024]{2,1,0:T(8,128)(2,1)S(1)}, bf16[2,128,1024]{2,1,0:T(8,128)(2,1)S(1)}, u32[]{:S(2)}, u32[]{:S(2)}) collective-permute-start(bf16[2,128,1024]{2,1,0:T(8,128)(2,1)S(1)} %get-tuple-element.44.rest_1_), channel_id=1, source_target_pairs={{0,16},{16,0},{1,17},{17,1},{2,18},{18,2},{3,19},{19,3},{4,20},{20... | collective-permute-start | bytes 1572872 | tf_op jit(solution)/shard_map/ppermute | solution.py:79
  40.1 2.8 %far_product.6 = (bf16[128,2176]{1,0:T(8,128)(2,1)S(1)}, f32[2,64,2176]{2,1,0:T(8,128)S(1)}) custom-call(s32[1]{0:T(128)} %bitcast.virt_ref, s32[1]{0:T(128)} %bitcast.1.me_ref, f32[1]{0:T(128)S(6)} %copy.7.energy_ref, bf16[2,128,1024]{2,1,0:T(8,128)(2,1)S(1)} %collective-permute-done.11.far_ref, f32[2,16,32,2048]{3,2,1,0:T(8,128)S(1)} %get-tuple-element.45.near_ref, ...), custom_call_target="tpu_custom_call" | custom-call | flops 110000000 | tf_op jit(solution)/shard_map/far_product/pallas_call | solution.py:282
  43.0 1.6 %collective-permute-done.9.refs_2_ = bf16[32,2176]{1,0:T(8,128)(2,1)S(1)} collective-permute-done((bf16[32,2176]{1,0:T(8,128)(2,1)S(1)}, bf16[32,2176]{1,0:T(8,128)(2,1)S(1)}, u32[]{:S(2)}, u32[]{:S(2)}) %collective-permute-start.9) | collective-permute-done | bytes 139296 | tf_op jit(solution)/shard_map/ppermute | solution.py:79
  45.1 2.7 %collective-permute-start.16 = (bf16[32,2176]{1,0:T(8,128)(2,1)S(1)}, bf16[32,2176]{1,0:T(8,128)(2,1)S(1)}, u32[]{:S(2)}, u32[]{:S(2)}) collective-permute-start(bf16[32,2176]{1,0:T(8,128)(2,1)S(1)} %get-tuple-element.71), channel_id=1, source_target_pairs={{0,8},{1,9},{2,10},{3,11},{4,12},{5,13},{6,14},{7,15},{8,0},{9,1},... | collective-permute-start | bytes 417800 | tf_op jit(solution)/shard_map/ppermute | solution.py:79
  47.7 0.7 combine.12
  48.4 1.7 %collective-permute-start.13 = (bf16[32,2176]{1,0:T(8,128)(2,1)S(1)}, bf16[32,2176]{1,0:T(8,128)(2,1)S(1)}, u32[]{:S(2)}, u32[]{:S(2)}) collective-permute-start(bf16[32,2176]{1,0:T(8,128)(2,1)S(1)} %get-tuple-element.68), channel_id=1, source_target_pairs={{0,6},{1,7},{2,4},{3,5},{4,2},{5,3},{6,0},{7,1},{8,14},{9,15},{10,... | collective-permute-start | bytes 417800 | tf_op jit(solution)/shard_map/ppermute | solution.py:79
  50.2 1.4 %collective-permute-start.14 = (bf16[32,2176]{1,0:T(8,128)(2,1)S(1)}, bf16[32,2176]{1,0:T(8,128)(2,1)S(1)}, u32[]{:S(2)}, u32[]{:S(2)}) collective-permute-start(bf16[32,2176]{1,0:T(8,128)(2,1)S(1)} %get-tuple-element.69), channel_id=1, source_target_pairs={{0,2},{1,3},{2,0},{3,1},{4,6},{5,7},{6,4},{7,5},{8,10},{9,11},{10,... | collective-permute-start | bytes 417800 | tf_op jit(solution)/shard_map/ppermute | solution.py:79
  52.0 3.0 %far_product.7 = (bf16[128,2176]{1,0:T(8,128)(2,1)S(1)}, f32[2,64,2176]{2,1,0:T(8,128)S(1)}) custom-call(s32[1]{0:T(128)} %bitcast.virt_ref, s32[1]{0:T(128)} %bitcast.1.me_ref, f32[1]{0:T(128)S(6)} %copy.7.energy_ref, bf16[2,128,1024]{2,1,0:T(8,128)(2,1)S(1)} %collective-permute-done.17.far_ref, f32[2,16,32,2048]{3,2,1,0:T(8,128)S(1)} %get-tuple-element.45.near_ref, ...), custom_call_target="tpu_custom_call" | custom-call | flops 110000000 | tf_op jit(solution)/shard_map/far_product/pallas_call | solution.py:282
  55.1 3.1 %collective-permute-done.13.refs_1_ = bf16[32,2176]{1,0:T(8,128)(2,1)S(1)} collective-permute-done((bf16[32,2176]{1,0:T(8,128)(2,1)S(1)}, bf16[32,2176]{1,0:T(8,128)(2,1)S(1)}, u32[]{:S(2)}, u32[]{:S(2)}) %collective-permute-start.13) | collective-permute-done | bytes 139296 | tf_op jit(solution)/shard_map/ppermute | solution.py:79
  58.2 1.3 %collective-permute-done.15.refs_3_ = bf16[32,2176]{1,0:T(8,128)(2,1)S(1)} collective-permute-done((bf16[32,2176]{1,0:T(8,128)(2,1)S(1)}, bf16[32,2176]{1,0:T(8,128)(2,1)S(1)}, u32[]{:S(2)}, u32[]{:S(2)}) %collective-permute-start.15) | collective-permute-done | bytes 139296 | tf_op jit(solution)/shard_map/ppermute | solution.py:79
  59.9 0.7 combine.14
  60.6 0.8 %collective-permute-start.19 = (bf16[32,2176]{1,0:T(8,128)(2,1)S(1)}, bf16[32,2176]{1,0:T(8,128)(2,1)S(1)}, u32[]{:S(2)}, u32[]{:S(2)}) collective-permute-start(bf16[32,2176]{1,0:T(8,128)(2,1)S(1)} %get-tuple-element.76), channel_id=1, source_target_pairs={{0,6},{1,7},{2,4},{3,5},{4,2},{5,3},{6,0},{7,1},{8,14},{9,15},{10,... | collective-permute-start | bytes 417800 | tf_op jit(solution)/shard_map/ppermute | solution.py:79
  61.4 0.9 %collective-permute-start.20 = (bf16[32,2176]{1,0:T(8,128)(2,1)S(1)}, bf16[32,2176]{1,0:T(8,128)(2,1)S(1)}, u32[]{:S(2)}, u32[]{:S(2)}) collective-permute-start(bf16[32,2176]{1,0:T(8,128)(2,1)S(1)} %get-tuple-element.77), channel_id=1, source_target_pairs={{0,2},{1,3},{2,0},{3,1},{4,6},{5,7},{6,4},{7,5},{8,10},{9,11},{10,... | collective-permute-start | bytes 417800 | tf_op jit(solution)/shard_map/ppermute | solution.py:79
  62.3 1.9 %collective-permute-start.21 = (bf16[32,2176]{1,0:T(8,128)(2,1)S(1)}, bf16[32,2176]{1,0:T(8,128)(2,1)S(1)}, u32[]{:S(2)}, u32[]{:S(2)}) collective-permute-start(bf16[32,2176]{1,0:T(8,128)(2,1)S(1)} %get-tuple-element.78), channel_id=1, source_target_pairs={{0,4},{1,5},{2,6},{3,7},{4,0},{5,1},{6,2},{7,3},{8,12},{9,13},{10,... | collective-permute-start | bytes 417800 | tf_op jit(solution)/shard_map/ppermute | solution.py:79
  64.2 0.8 %collective-permute-start.22 = (bf16[16,2176]{1,0:T(8,128)(2,1)S(1)}, bf16[16,2176]{1,0:T(8,128)(2,1)S(1)}, u32[]{:S(2)}, u32[]{:S(2)}) collective-permute-start(bf16[16,2176]{1,0:T(8,128)(2,1)S(1)} %get-tuple-element.80), channel_id=1, source_target_pairs={{0,8},{1,9},{2,10},{3,11},{4,12},{5,13},{6,14},{7,15},{8,0},{9,1},... | collective-permute-start | bytes 208904 | tf_op jit(solution)/shard_map/ppermute | solution.py:79
  65.0 3.9 %collective-permute-done.19.refs_1_ = bf16[32,2176]{1,0:T(8,128)(2,1)S(1)} collective-permute-done((bf16[32,2176]{1,0:T(8,128)(2,1)S(1)}, bf16[32,2176]{1,0:T(8,128)(2,1)S(1)}, u32[]{:S(2)}, u32[]{:S(2)}) %collective-permute-start.19) | collective-permute-done | bytes 139296 | tf_op jit(solution)/shard_map/ppermute | solution.py:79
  68.9 2.3 %collective-permute-done.21.refs_3_ = bf16[32,2176]{1,0:T(8,128)(2,1)S(1)} collective-permute-done((bf16[32,2176]{1,0:T(8,128)(2,1)S(1)}, bf16[32,2176]{1,0:T(8,128)(2,1)S(1)}, u32[]{:S(2)}, u32[]{:S(2)}) %collective-permute-start.21) | collective-permute-done | bytes 139296 | tf_op jit(solution)/shard_map/ppermute | solution.py:79
  71.6 5.2 %collective-permute-done.23.refs_6_ = bf16[16,2176]{1,0:T(8,128)(2,1)S(1)} collective-permute-done((bf16[16,2176]{1,0:T(8,128)(2,1)S(1)}, bf16[16,2176]{1,0:T(8,128)(2,1)S(1)}, u32[]{:S(2)}, u32[]{:S(2)}) %collective-permute-start.23) | collective-permute-done | bytes 69664 | tf_op jit(solution)/shard_map/ppermute | solution.py:79
  76.8 1.1 %finish.1 = (f32[32,2048]{1,0:T(8,128)}, f32[32,2048]{1,0:T(8,128)}) custom-call(f32[2,8,2176]{2,1,0:T(8,128)S(1)} %get-tuple-element.55.refs_2_.refs_0_, f32[2,8,2176]{2,1,0:T(8,128)S(1)} %get-tuple-element.64.refs_2_.refs_1_, f32[2,8,2176]{2,1,0:T(8,128)S(1)} %get-tuple-element.72.refs_2_, f32[2,8,2176]{2,1,0:T(8,128)S(1)} %get-tuple-element.79.refs_3_, ...), custom_call_target="tpu_custom_call" | custom-call | flops 110000000 | tf_op jit(solution)/shard_map/finish/pallas_call | solution.py:353
  (32 shorter events, 5.3 us)
Async XLA Ops:
  1.9 15.8 %collective-permute-start = (bf16[2,128,1024]{2,1,0:T(8,128)(2,1)S(1)}, bf16[2,128,1024]{2,1,0:T(8,128)(2,1)S(1)}, u32[]{:S(2)}, u32[]{:S(2)}) collective-permute-start(bf16[2,128,1024]{2,1,0:T(8,128)(2,1)S(1)} %get-tuple-element.42), channel_id=1, source_target_pairs={{0,16},{16,0},{1,17},{17,1},{2,18},{18,2},{3,19},{19,3},{4,20},{20... | collective-permute-start | bytes 1572872 | tf_op jit(solution)/shard_map/ppermute | solution.py:79
  4.9 24.0 %collective-permute-start.6 = (bf16[2,128,1024]{2,1,0:T(8,128)(2,1)S(1)}, bf16[2,128,1024]{2,1,0:T(8,128)(2,1)S(1)}, u32[]{:S(2)}, u32[]{:S(2)}) collective-permute-start(bf16[2,128,1024]{2,1,0:T(8,128)(2,1)S(1)} %get-tuple-element.56), channel_id=1, source_target_pairs={{0,16},{16,0},{1,17},{17,1},{2,18},{18,2},{3,19},{19,3},{4,20},{20... | collective-permute-start | bytes 1572872 | tf_op jit(solution)/shard_map/ppermute | solution.py:79
  20.5 2.6 %collective-permute-start.1 = (bf16[64,2176]{1,0:T(8,128)(2,1)S(1)}, bf16[64,2176]{1,0:T(8,128)(2,1)S(1)}, u32[]{:S(2)}, u32[]{:S(2)}) collective-permute-start(bf16[64,2176]{1,0:T(8,128)(2,1)S(1)} %get-tuple-element.49), channel_id=1, source_target_pairs={{0,1},{1,0},{2,3},{3,2},{4,5},{5,4},{6,7},{7,6},{8,9},{9,8},{10,11... | collective-permute-start | bytes 835592 | tf_op jit(solution)/shard_map/ppermute | solution.py:79
  20.6 2.6 %collective-permute-start.2 = (bf16[64,2176]{1,0:T(8,128)(2,1)S(1)}, bf16[64,2176]{1,0:T(8,128)(2,1)S(1)}, u32[]{:S(2)}, u32[]{:S(2)}) collective-permute-start(bf16[64,2176]{1,0:T(8,128)(2,1)S(1)} %get-tuple-element.50), channel_id=1, source_target_pairs={{0,1},{1,0},{2,3},{3,2},{4,5},{5,4},{6,7},{7,6},{8,9},{9,8},{10,11... | collective-permute-start | bytes 835592 | tf_op jit(solution)/shard_map/ppermute | solution.py:79
  21.1 19.0 %collective-permute-start.11 = (bf16[2,128,1024]{2,1,0:T(8,128)(2,1)S(1)}, bf16[2,128,1024]{2,1,0:T(8,128)(2,1)S(1)}, u32[]{:S(2)}, u32[]{:S(2)}) collective-permute-start(bf16[2,128,1024]{2,1,0:T(8,128)(2,1)S(1)} %get-tuple-element.43.rest_0_), channel_id=1, source_target_pairs={{0,16},{16,0},{1,17},{17,1},{2,18},{18,2},{3,19},{19,3},{4,20},{20... | collective-permute-start | bytes 1572872 | tf_op jit(solution)/shard_map/ppermute | solution.py:79
  23.8 8.0 %collective-permute-start.3 = (bf16[32,2176]{1,0:T(8,128)(2,1)S(1)}, bf16[32,2176]{1,0:T(8,128)(2,1)S(1)}, u32[]{:S(2)}, u32[]{:S(2)}) collective-permute-start(bf16[32,2176]{1,0:T(8,128)(2,1)S(1)} %get-tuple-element.52), channel_id=1, source_target_pairs={{0,6},{1,7},{2,4},{3,5},{4,2},{5,3},{6,0},{7,1},{8,14},{9,15},{10,... | collective-permute-start | bytes 417800 | tf_op jit(solution)/shard_map/ppermute | solution.py:79
  26.4 6.9 %collective-permute-start.4 = (bf16[32,2176]{1,0:T(8,128)(2,1)S(1)}, bf16[32,2176]{1,0:T(8,128)(2,1)S(1)}, u32[]{:S(2)}, u32[]{:S(2)}) collective-permute-start(bf16[32,2176]{1,0:T(8,128)(2,1)S(1)} %get-tuple-element.53), channel_id=1, source_target_pairs={{0,2},{1,3},{2,0},{3,1},{4,6},{5,7},{6,4},{7,5},{8,10},{9,11},{10,... | collective-permute-start | bytes 417800 | tf_op jit(solution)/shard_map/ppermute | solution.py:79
  27.0 6.5 %collective-permute-start.5 = (bf16[32,2176]{1,0:T(8,128)(2,1)S(1)}, bf16[32,2176]{1,0:T(8,128)(2,1)S(1)}, u32[]{:S(2)}, u32[]{:S(2)}) collective-permute-start(bf16[32,2176]{1,0:T(8,128)(2,1)S(1)} %get-tuple-element.54), channel_id=1, source_target_pairs={{0,4},{1,5},{2,6},{3,7},{4,0},{5,1},{6,2},{7,3},{8,12},{9,13},{10,... | collective-permute-start | bytes 417800 | tf_op jit(solution)/shard_map/ppermute | solution.py:79
  31.7 2.1 %collective-permute-start.7 = (bf16[128,2176]{1,0:T(8,128)(2,1)S(1)}, bf16[128,2176]{1,0:T(8,128)(2,1)S(1)}, u32[]{:S(2)}, u32[]{:S(2)}) collective-permute-start(bf16[128,2176]{1,0:T(8,128)(2,1)S(1)} %get-tuple-element.58), channel_id=1, source_target_pairs={{0,1},{1,0},{2,3},{3,2},{4,5},{5,4},{6,7},{7,6},{8,9},{9,8},{10,11... | collective-permute-start | bytes 1671176 | tf_op jit(solution)/shard_map/ppermute | solution.py:79
  34.5 8.4 %collective-permute-start.8 = (bf16[32,2176]{1,0:T(8,128)(2,1)S(1)}, bf16[32,2176]{1,0:T(8,128)(2,1)S(1)}, u32[]{:S(2)}, u32[]{:S(2)}) collective-permute-start(bf16[32,2176]{1,0:T(8,128)(2,1)S(1)} %get-tuple-element.60), channel_id=1, source_target_pairs={{0,6},{1,7},{2,4},{3,5},{4,2},{5,3},{6,0},{7,1},{8,14},{9,15},{10,... | collective-permute-start | bytes 417800 | tf_op jit(solution)/shard_map/ppermute | solution.py:79
  37.6 7.0 %collective-permute-start.9 = (bf16[32,2176]{1,0:T(8,128)(2,1)S(1)}, bf16[32,2176]{1,0:T(8,128)(2,1)S(1)}, u32[]{:S(2)}, u32[]{:S(2)}) collective-permute-start(bf16[32,2176]{1,0:T(8,128)(2,1)S(1)} %get-tuple-element.61), channel_id=1, source_target_pairs={{0,2},{1,3},{2,0},{3,1},{4,6},{5,7},{6,4},{7,5},{8,10},{9,11},{10,... | collective-permute-start | bytes 417800 | tf_op jit(solution)/shard_map/ppermute | solution.py:79
  38.1 6.6 %collective-permute-start.10 = (bf16[32,2176]{1,0:T(8,128)(2,1)S(1)}, bf16[32,2176]{1,0:T(8,128)(2,1)S(1)}, u32[]{:S(2)}, u32[]{:S(2)}) collective-permute-start(bf16[32,2176]{1,0:T(8,128)(2,1)S(1)} %get-tuple-element.62), channel_id=1, source_target_pairs={{0,4},{1,5},{2,6},{3,7},{4,0},{5,1},{6,2},{7,3},{8,12},{9,13},{10,... | collective-permute-start | bytes 417800 | tf_op jit(solution)/shard_map/ppermute | solution.py:79
  38.2 13.8 %collective-permute-start.17 = (bf16[2,128,1024]{2,1,0:T(8,128)(2,1)S(1)}, bf16[2,128,1024]{2,1,0:T(8,128)(2,1)S(1)}, u32[]{:S(2)}, u32[]{:S(2)}) collective-permute-start(bf16[2,128,1024]{2,1,0:T(8,128)(2,1)S(1)} %get-tuple-element.44.rest_1_), channel_id=1, source_target_pairs={{0,16},{16,0},{1,17},{17,1},{2,18},{18,2},{3,19},{19,3},{4,20},{20... | collective-permute-start | bytes 1572872 | tf_op jit(solution)/shard_map/ppermute | solution.py:79
  42.9 4.9 %collective-permute-start.12 = (bf16[128,2176]{1,0:T(8,128)(2,1)S(1)}, bf16[128,2176]{1,0:T(8,128)(2,1)S(1)}, u32[]{:S(2)}, u32[]{:S(2)}) collective-permute-start(bf16[128,2176]{1,0:T(8,128)(2,1)S(1)} %get-tuple-element.66), channel_id=1, source_target_pairs={{0,1},{1,0},{2,3},{3,2},{4,5},{5,4},{6,7},{7,6},{8,9},{9,8},{10,11... | collective-permute-start | bytes 1671176 | tf_op jit(solution)/shard_map/ppermute | solution.py:79
  45.1 10.0 %collective-permute-start.16 = (bf16[32,2176]{1,0:T(8,128)(2,1)S(1)}, bf16[32,2176]{1,0:T(8,128)(2,1)S(1)}, u32[]{:S(2)}, u32[]{:S(2)}) collective-permute-start(bf16[32,2176]{1,0:T(8,128)(2,1)S(1)} %get-tuple-element.71), channel_id=1, source_target_pairs={{0,8},{1,9},{2,10},{3,11},{4,12},{5,13},{6,14},{7,15},{8,0},{9,1},... | collective-permute-start | bytes 417800 | tf_op jit(solution)/shard_map/ppermute | solution.py:79
  48.4 9.7 %collective-permute-start.13 = (bf16[32,2176]{1,0:T(8,128)(2,1)S(1)}, bf16[32,2176]{1,0:T(8,128)(2,1)S(1)}, u32[]{:S(2)}, u32[]{:S(2)}) collective-permute-start(bf16[32,2176]{1,0:T(8,128)(2,1)S(1)} %get-tuple-element.68), channel_id=1, source_target_pairs={{0,6},{1,7},{2,4},{3,5},{4,2},{5,3},{6,0},{7,1},{8,14},{9,15},{10,... | collective-permute-start | bytes 417800 | tf_op jit(solution)/shard_map/ppermute | solution.py:79
  50.2 8.0 %collective-permute-start.14 = (bf16[32,2176]{1,0:T(8,128)(2,1)S(1)}, bf16[32,2176]{1,0:T(8,128)(2,1)S(1)}, u32[]{:S(2)}, u32[]{:S(2)}) collective-permute-start(bf16[32,2176]{1,0:T(8,128)(2,1)S(1)} %get-tuple-element.69), channel_id=1, source_target_pairs={{0,2},{1,3},{2,0},{3,1},{4,6},{5,7},{6,4},{7,5},{8,10},{9,11},{10,... | collective-permute-start | bytes 417800 | tf_op jit(solution)/shard_map/ppermute | solution.py:79
  51.6 8.0 %collective-permute-start.15 = (bf16[32,2176]{1,0:T(8,128)(2,1)S(1)}, bf16[32,2176]{1,0:T(8,128)(2,1)S(1)}, u32[]{:S(2)}, u32[]{:S(2)}) collective-permute-start(bf16[32,2176]{1,0:T(8,128)(2,1)S(1)} %get-tuple-element.70), channel_id=1, source_target_pairs={{0,4},{1,5},{2,6},{3,7},{4,0},{5,1},{6,2},{7,3},{8,12},{9,13},{10,... | collective-permute-start | bytes 417800 | tf_op jit(solution)/shard_map/ppermute | solution.py:79
  55.0 4.9 %collective-permute-start.18 = (bf16[128,2176]{1,0:T(8,128)(2,1)S(1)}, bf16[128,2176]{1,0:T(8,128)(2,1)S(1)}, u32[]{:S(2)}, u32[]{:S(2)}) collective-permute-start(bf16[128,2176]{1,0:T(8,128)(2,1)S(1)} %get-tuple-element.74), channel_id=1, source_target_pairs={{0,1},{1,0},{2,3},{3,2},{4,5},{5,4},{6,7},{7,6},{8,9},{9,8},{10,11... | collective-permute-start | bytes 1671176 | tf_op jit(solution)/shard_map/ppermute | solution.py:79
  60.6 8.3 %collective-permute-start.19 = (bf16[32,2176]{1,0:T(8,128)(2,1)S(1)}, bf16[32,2176]{1,0:T(8,128)(2,1)S(1)}, u32[]{:S(2)}, u32[]{:S(2)}) collective-permute-start(bf16[32,2176]{1,0:T(8,128)(2,1)S(1)} %get-tuple-element.76), channel_id=1, source_target_pairs={{0,6},{1,7},{2,4},{3,5},{4,2},{5,3},{6,0},{7,1},{8,14},{9,15},{10,... | collective-permute-start | bytes 417800 | tf_op jit(solution)/shard_map/ppermute | solution.py:79
  61.4 7.5 %collective-permute-start.20 = (bf16[32,2176]{1,0:T(8,128)(2,1)S(1)}, bf16[32,2176]{1,0:T(8,128)(2,1)S(1)}, u32[]{:S(2)}, u32[]{:S(2)}) collective-permute-start(bf16[32,2176]{1,0:T(8,128)(2,1)S(1)} %get-tuple-element.77), channel_id=1, source_target_pairs={{0,2},{1,3},{2,0},{3,1},{4,6},{5,7},{6,4},{7,5},{8,10},{9,11},{10,... | collective-permute-start | bytes 417800 | tf_op jit(solution)/shard_map/ppermute | solution.py:79
  62.3 8.9 %collective-permute-start.21 = (bf16[32,2176]{1,0:T(8,128)(2,1)S(1)}, bf16[32,2176]{1,0:T(8,128)(2,1)S(1)}, u32[]{:S(2)}, u32[]{:S(2)}) collective-permute-start(bf16[32,2176]{1,0:T(8,128)(2,1)S(1)} %get-tuple-element.78), channel_id=1, source_target_pairs={{0,4},{1,5},{2,6},{3,7},{4,0},{5,1},{6,2},{7,3},{8,12},{9,13},{10,... | collective-permute-start | bytes 417800 | tf_op jit(solution)/shard_map/ppermute | solution.py:79
  64.2 7.4 %collective-permute-start.22 = (bf16[16,2176]{1,0:T(8,128)(2,1)S(1)}, bf16[16,2176]{1,0:T(8,128)(2,1)S(1)}, u32[]{:S(2)}, u32[]{:S(2)}) collective-permute-start(bf16[16,2176]{1,0:T(8,128)(2,1)S(1)} %get-tuple-element.80), channel_id=1, source_target_pairs={{0,8},{1,9},{2,10},{3,11},{4,12},{5,13},{6,14},{7,15},{8,0},{9,1},... | collective-permute-start | bytes 208904 | tf_op jit(solution)/shard_map/ppermute | solution.py:79
  71.5 5.3 %collective-permute-start.23 = (bf16[16,2176]{1,0:T(8,128)(2,1)S(1)}, bf16[16,2176]{1,0:T(8,128)(2,1)S(1)}, u32[]{:S(2)}, u32[]{:S(2)}) collective-permute-start(bf16[16,2176]{1,0:T(8,128)(2,1)S(1)} %get-tuple-element.81), channel_id=1, source_target_pairs={{0,8},{1,9},{2,10},{3,11},{4,12},{5,13},{6,14},{7,15},{8,0},{9,1},... | collective-permute-start | bytes 208904 | tf_op jit(solution)/shard_map/ppermute | solution.py:79

commit v11 on v10

--- a/solution.py
+++ b/solution.py
@@ -8,11 +8,10 @@
 from jax.sharding import PartitionSpec as P
 
 PIECES = 4
-GROUPS = ((0, 1), (2,), (3,))
-FAR = (0.1, 1.5, 0.1, 0.1)
+UNITS = ((0,), (1, 2), (3,))
+SPLIT = (2, 1, 1, 1)
 BESIDE = 6
-
-
+FAR = (0.1, 0.1, 0.1, 0.1)
 def product(left, right):
     return jnp.einsum("woe,wev->wov", left, right, preferred_element_type=jnp.float32)
 
@@ -293,72 +292,122 @@
     return [sends], keep
 
 
-def combine_kernel(parts, senders, carried, ordered, *refs):
-    keep_ref, refs = refs[0], refs[1:]
-    came_refs = [refs[parts * sender : parts * sender + parts] for sender in range(senders)]
-    refs = refs[parts * senders + ordered :]
-    kept_ref, send_refs = refs[carried], refs[carried + 1 :]
-    width = keep_ref.shape[2] - EXTRA
-    sums, energy = add_came(keep_ref, came_refs)
-    kept = kept_ref.shape[1] // 8
-    for array, blocks in enumerate(sums):
-        for index, block in enumerate(blocks[:kept]):
-            kept_ref[array, 8 * index : 8 * index + 8, :width] = block
-    kept_ref[0, :8, width:] = energy
-    for index, send_ref in enumerate(send_refs):
-        if carried:
-            above = refs[0].shape[0]
-            send_ref[:above, :] = refs[0][...]
-            send_ref = send_ref.at[above:, :]
-        first = kept * (index + 1)
-        store_coded([send_ref], [block for blocks in sums for block in blocks[first : first + kept]], energy)
-
-
-def combine(keep, came, sent, carry, after, length):
-    _, height, width = keep.shape
+def combine_kernel(layout, ordered, *refs):
+    count = len(layout)
+    keep_refs, refs = refs[:count], refs[count:]
+    came = []
+    for parts in layout:
+        came.append([])
+        for index, first, last in parts:
+            came[-1].append([refs[position].at[first:last, :] for position in index])
+    inputs = 1 + max(position for parts in layout for index, _, _ in parts for position in index)
+    refs = refs[inputs + ordered :]
+    kept_refs, send_refs = refs[:count], refs[count:]
+    width = keep_refs[0].shape[2] - EXTRA
+    for piece, (keep_ref, kept_ref) in enumerate(zip(keep_refs, kept_refs)):
+        sums, energy = add_came(keep_ref, came[piece])
+        kept = kept_ref.shape[1] // 8
+        for array, blocks in enumerate(sums):
+            for index, block in enumerate(blocks[:kept]):
+                kept_ref[array, 8 * index : 8 * index + 8, :width] = block
+        kept_ref[0, :8, width:] = energy
+        rows = slice(16 * kept * piece, 16 * kept * (piece + 1))
+        for index, send_ref in enumerate(send_refs):
+            first = kept * (index + 1)
+            store_coded([send_ref.at[rows, :]], [block for blocks in sums for block in blocks[first : first + kept]], energy)
+
+
+def combine(keeps, came, layout, sent, after, length):
+    _, height, width = keeps[0].shape
     kept = height // (sent + 1)
-    parts, senders = len(came[0]), len(came)
-    above = sum(array.shape[0] for array in carry)
-    keep, *sends = pl.pallas_call(
-        functools.partial(combine_kernel, parts, senders, len(carry), len(after)),
-        out_shape=(jax.ShapeDtypeStruct((2, kept, width), jnp.float32),)
-        + (jax.ShapeDtypeStruct((above + 2 * kept, width), jnp.bfloat16),) * sent,
-        in_specs=[WHOLE] * (1 + parts * senders) + [ANYWHERE] * len(after) + [WHOLE] * len(carry),
-        out_specs=(WHOLE,) * (1 + sent),
-        compiler_params=limit(8),
+    count = len(keeps)
+    outs = pl.pallas_call(
+        functools.partial(combine_kernel, layout, len(after)),
+        out_shape=(jax.ShapeDtypeStruct((2, kept, width), jnp.float32),) * count
+        + (jax.ShapeDtypeStruct((2 * kept * count, width), jnp.bfloat16),) * sent,
+        in_specs=[WHOLE] * (count + len(came)) + [ANYWHERE] * len(after),
+        out_specs=(WHOLE,) * (count + sent),
+        compiler_params=limit(10),
         cost_estimate=cost(length),
         name="combine",
-    )(keep, *[part for parts in came for part in parts], *after, *carry)
-    return [[send] for send in sends], keep
-
-
-def finish_kernel(count, *refs):
+    )(*keeps, *came, *after)
+    return outs[count:], outs[:count]
+
+
+def first_layout(count, split, rows):
+    return tuple(((tuple(range(piece * split, piece * split + split)), 0, rows),) for piece in range(count))
+
+
+def joint_layout(count, senders, rows):
+    return tuple(
+        tuple(((sender,), piece * rows, piece * rows + rows) for sender in range(senders)) for piece in range(count)
+    )
+
+
+def outputs_of(keep_ref, came, count):
+    (gradient, log), energy = add_came(keep_ref, came)
+    correction = 2.0 * (energy[:, :1] / count - OFFSET)
+    log = [block / count for block in log]
+    return [block / count - correction * mean for block, mean in zip(gradient, log)], log
+
+
+def share_kernel(count, ordered, *refs):
+    out_ref, row = refs[-1], 0
+    for keep_ref in refs[: -1 - ordered]:
+        for gradient, log in zip(*outputs_of(keep_ref, [], count)):
+            out_ref[0, row : row + 8, :] = gradient
+            out_ref[1, row : row + 8, :] = log
+            row += 8
+
+
+def share(keeps, after, count):
+    _, rows, width = keeps[0].shape
+    return pl.pallas_call(
+        functools.partial(share_kernel, count, len(after)),
+        out_shape=jax.ShapeDtypeStruct((2, rows * len(keeps), width - EXTRA), jnp.float32),
+        in_specs=[WHOLE] * len(keeps) + [ANYWHERE] * len(after),
+        out_specs=WHOLE,
+        compiler_params=limit(8),
+        cost_estimate=cost(BESIDE),
+        name="share",
+    )(*keeps, *after)
+
+
+def finish_kernel(count, ready_ref, *refs):
     (gradient_ref, log_ref), refs = refs[-2:], refs[:-2]
-    came = [ref.at[16 * place : 16 * place + 16, :] for ref, group in zip(refs[-len(GROUPS) :], GROUPS) for place in range(len(group))]
-    keep_refs = refs[: -len(GROUPS)]
-    row = 0
-    for piece, keep_ref in enumerate(keep_refs):
-        (gradient, log), energy = add_came(keep_ref, [[came[piece]]])
-        correction = 2.0 * (energy[:, :1] / count - OFFSET)
-        for block in range(len(log)):
-            log_mean = log[block] / count
-            gradient_ref[row : row + 8, :] = gradient[block] / count - correction * log_mean
-            log_ref[row : row + 8, :] = log_mean
+    later = UNITS[1:]
+    came = []
+    for ref, group in zip(refs[-len(later) :], later):
+        came += [ref.at[16 * place : 16 * place + 16, :] for place in range(len(group))]
+    row = ready_ref.shape[1]
+    gradient_ref[:row, :] = ready_ref[0]
+    log_ref[:row, :] = ready_ref[1]
+    for keep_ref, part in zip(refs[: -len(later)], came):
+        for gradient, log in zip(*outputs_of(keep_ref, [[part]], count)):
+            gradient_ref[row : row + 8, :] = gradient
+            log_ref[row : row + 8, :] = log
             row += 8
 
 
-def finish(keeps, came, count):
+def finish(ready, keeps, came, count):
     _, rows, width = keeps[0].shape
-    out = jax.ShapeDtypeStruct((rows * len(keeps), width - EXTRA), jnp.float32)
+    out = jax.ShapeDtypeStruct((ready.shape[1] + rows * len(keeps), width - EXTRA), jnp.float32)
     return pl.pallas_call(
         functools.partial(finish_kernel, count),
         out_shape=(out, out),
-        in_specs=[WHOLE] * (len(keeps) + len(came)),
+        in_specs=[WHOLE] * (1 + len(keeps) + len(came)),
         out_specs=(WHOLE, WHOLE),
         compiler_params=limit(8),
         cost_estimate=cost(0.1),
         name="finish",
-    )(*keeps, *came)
+    )(ready, *keeps, *came)
+
+
+def second_sums(group, keep, came, sent, stages, after):
+    layout = joint_layout(len(group), len(sent), sent[0].shape[0] // len(group))
+    sends, keeps = combine([keep[piece] for piece in group], sent, layout, 1, after, 0.1)
+    keep = keep | dict(zip(group, keeps))
+    return keep, came + [swap(sends[0], "walk", stages[2][0])], [keeps[0]]
 
 
 def pieced_body(pieces, tile, inverse_rows, kinetic_rows, virt_values, virt_laplacians, local_energy):
@@ -376,33 +425,45 @@
         for array in (inverse, kinetic, virt_values[0], virt_laplacians[0])
     )
     mine = [part for group in range(pieces // 2) for part in cut(inverse, kinetic, group)]
-    theirs = [swap(part, "virt", 1) for part in mine]
+    theirs = [swap(part, "virt", 1) for part in mine[:2]]
     near, values, laplacians = near_product(virt, me, local_energy, inverse, kinetic, values, laplacians, mine[2:])
 
-    keep, first, came = {}, {}, []
-    late, carry = [], ()
-    for turn in range(pieces + 1):
-        if turn < pieces:
-            after = [keep[turn - 1]] if turn else []
-            send, kept = far_product(
-                virt, me, local_energy, theirs[turn], near, turn * rows, values, laplacians, tile, stages, 1 if turn else 2, after, FAR[turn]
-            )
-            first[turn] = [[swap(part, "walk", mask) for part in parts] for parts, mask in zip(send, partners(stages[0]))]
-        if turn:
-            piece = turn - 1
-            sends, keep[piece] = combine(keep[piece], second, len(partners(stages[2])), carry, came if turn == pieces - 1 else [], BESIDE)
-            carry = tuple(sends[0])
-            if any(piece == group[-1] for group in GROUPS):
-                came.append(swap(carry[0], "walk", stages[2][0]))
-                carry = ()
-        if turn < pieces:
-            after = ([keep[turn - 1]] if turn else [])
-            sends, keep[turn] = combine(kept, first[turn], len(partners(stages[1])), (), after, 0.1)
-            second = [
-                [swap(part, "walk", mask) for part in parts]
-                for parts, mask in reversed(list(zip(sends, partners(stages[1]))))
-            ]
-    return finish([keep[piece] for piece in range(pieces)], came, count)
+    second = partners(stages[1])
+    kept, first, keep, came = {}, {}, {}, []
+    unit, sent, last = 0, (), []
+    for turn in range(pieces):
+        send, kept[turn] = far_product(
+            virt, me, local_energy, theirs[turn], near, turn * rows, values, laplacians, tile, stages, SPLIT[turn], last, FAR[turn]
+        )
+        if turn + 2 < pieces:
+            part, kept[turn] = lax.optimization_barrier((mine[turn + 2], kept[turn]))
+            theirs.append(swap(part, "virt", 1))
+        first[turn] = [swap(part, "walk", stages[0][0]) for part in send[0]]
+        last = [kept[turn]]
+        if sent and turn < pieces - 1:
+            keep, came, last = second_sums(UNITS[unit - 1], keep, came, sent, stages, last)
+            sent = ()
+        group = UNITS[unit]
+        if turn == pieces - 1:
+            ready = share([keep[piece] for piece in UNITS[0]], last, count)
+            last = [ready]
+        if turn == pieces - 2:
+            early = UNITS[0]
+            layout = joint_layout(len(early), 1, came[0].shape[0] // len(early))
+            _, keeps = combine([keep[piece] for piece in early], came[:1], layout, 0, last, BESIDE)
+            keep, last = keep | dict(zip(early, keeps)), [keeps[0]]
+        if turn == group[-1]:
+            layout = first_layout(len(group), SPLIT[turn], first[turn][0].shape[0])
+            arrays = [part for piece in group for part in first[piece]]
+            sends, keeps = combine([kept[piece] for piece in group], arrays, layout, len(second), last, 0.1)
+            last = [keeps[0]]
+            if turn == pieces - 1 and sent:
+                keep, came, last = second_sums(UNITS[unit - 1], keep, came, sent, stages, last)
+            keep.update(zip(group, keeps))
+            sent = [swap(part, "walk", mask) for part, mask in reversed(list(zip(sends, second)))]
+            unit += 1
+    keep, came, last = second_sums(UNITS[-1], keep, came, sent, stages, last)
+    return finish(ready, [keep[piece] for unit in UNITS[1:] for piece in unit], came[1:], count)
 
 
 def solution(mesh):

time: 78 us -> 77.7 us (level)
  waiting for transfers between devices: 21.2 us -> 18.7 us
  starting transfers between devices: 25.7 us -> 28 us
    ppermute x24 -> x21, waiting for transfers between devices: 21.2 us -> 18.7 us  [swap(): return lax.ppermute(array, axis, pairs)]
    ppermute x24 -> x21, starting transfers between devices: 25.7 us -> 28 us  [swap(): return lax.ppermute(array, axis, pairs)]
  transfers between devices with their start and end apart: 24 -> 21, of which waited for: 11 -> 14; matrix products, arithmetic and copies ran while one was open for 0% -> 0% of each run, Pallas kernels for 34% -> 35%
where the time goes in v11:
time: 77.7 us; the launch traced here: 77.6 us
  Pallas kernels  29.5 us (38%)
  starting transfers between devices  28 us (36%)
  waiting for transfers between devices  18.7 us (24%)
  between operations  1.41 us (2%)
    ppermute x21, starting transfers between devices, swap(): return lax.ppermute(array, axis, pairs)  28 us
    ppermute x21, waiting for transfers between devices, swap(): return lax.ppermute(array, axis, pairs)  18.7 us
    pallas_call x4, Pallas kernels, far_product(): pl.pallas_call(functools.partial(far_kernel, place_weights(stages), count...  11.4 us
    pallas_call x1, Pallas kernels, near_product(): pl.pallas_call(functools.partial(near_kernel, chunk, tile), out_shape=(ja...  10.3 us
    pallas_call x7, Pallas kernels, combine(): pl.pallas_call(functools.partial(combine_kernel, layout, len(after)), out...  4.12 us
    pallas_call x2, Pallas kernels, cut(): pl.pallas_call(cut_kernel, out_shape=(out, out), grid=(1,), in_specs=[blo...  2.55 us
  transfers between devices with their start and end apart: 21, of which 14 were waited for; matrix products, arithmetic and copies ran while one was open for 0% of the time, Pallas kernels for 35%

profile of v11, /device:TPU:0, one launch (start us, length us, event | category | flops | bytes accessed | tf_op | source)
XLA Modules:
  0.0 77.6 jit_solution(11377827353457099187)
XLA Ops:
  0.6 1.3 %cut.3 = (bf16[2,128,1024]{2,1,0:T(8,128)(2,1)S(1)}, bf16[2,128,1024]{2,1,0:T(8,128)(2,1)S(1)}) custom-call(bf16[16,32,1024]{2,1,0:T(8,128)(2,1)} %bitcast.6, bf16[16,32,1024]{2,1,0:T(8,128)(2,1)} %bitcast.9), custom_call_target="tpu_custom_call" | custom-call | flops 110000000 | tf_op jit(solution)/shard_map/cut/pallas_call | solution.py:164
  1.9 3.0 %collective-permute-start = (bf16[2,128,1024]{2,1,0:T(8,128)(2,1)S(1)}, bf16[2,128,1024]{2,1,0:T(8,128)(2,1)S(1)}, u32[]{:S(2)}, u32[]{:S(2)}) collective-permute-start(bf16[2,128,1024]{2,1,0:T(8,128)(2,1)S(1)} %get-tuple-element.43), channel_id=1, source_target_pairs={{0,16},{16,0},{1,17},{17,1},{2,18},{18,2},{3,19},{19,3},{4,20},{20... | collective-permute-start | bytes 1572872 | tf_op jit(solution)/shard_map/ppermute | solution.py:78
  5.0 1.3 %cut.2 = (bf16[2,128,1024]{2,1,0:T(8,128)(2,1)S(1)}, bf16[2,128,1024]{2,1,0:T(8,128)(2,1)S(1)}) custom-call(bf16[16,32,1024]{2,1,0:T(8,128)(2,1)} %bitcast.7, bf16[16,32,1024]{2,1,0:T(8,128)(2,1)} %bitcast.10), custom_call_target="tpu_custom_call" | custom-call | flops 110000000 | tf_op jit(solution)/shard_map/cut/pallas_call | solution.py:164
  6.9 10.3 %near_product.1 = (f32[2,16,32,2048]{3,2,1,0:T(8,128)S(1)}, bf16[1024,2048]{1,0:T(8,128)(2,1)S(1)}, bf16[1024,2048]{1,0:T(8,128)(2,1)S(1)}) custom-call(s32[1]{0:T(128)} %bitcast.2.virt_ref, s32[1]{0:T(128)} %bitcast.3.me_ref, f32[1]{0:T(128)S(6)} %copy.7.energy_ref, bf16[16,32,1024]{2,1,0:T(8,128)(2,1)} %bitcast.8, bf16[16,32,1024]{2,1,0:T(8,128)(2,1)} %bitcast.11, ...), custom_call_target="tpu_custom_call" | custom-call | flops 9900000256 | tf_op jit(solution)/shard_map/near_product/pallas_call | solution.py:230
  17.7 2.8 %far_product.4 = (bf16[64,2176]{1,0:T(8,128)(2,1)S(1)}, bf16[64,2176]{1,0:T(8,128)(2,1)S(1)}, f32[2,64,2176]{2,1,0:T(8,128)S(1)}) custom-call(s32[1]{0:T(128)} %bitcast.2.virt_ref, s32[1]{0:T(128)} %bitcast.3.me_ref, f32[1]{0:T(128)S(6)} %copy.7.energy_ref, bf16[2,128,1024]{2,1,0:T(8,128)(2,1)S(1)} %collective-permute-done.far_ref, ...), custom_call_target="tpu_custom_call" | custom-call | flops 110000000 | tf_op jit(solution)/shard_map/far_product/pallas_call | solution.py:281
  20.5 2.1 %collective-permute-start.8 = (bf16[2,128,1024]{2,1,0:T(8,128)(2,1)S(1)}, bf16[2,128,1024]{2,1,0:T(8,128)(2,1)S(1)}, u32[]{:S(2)}, u32[]{:S(2)}) collective-permute-start(bf16[2,128,1024]{2,1,0:T(8,128)(2,1)S(1)} %get-tuple-element.61.rest_0_), channel_id=1, source_target_pairs={{0,16},{16,0},{1,17},{17,1},{2,18},{18,2},{3,19},{19,3},{4,20},{20... | collective-permute-start | bytes 1572872 | tf_op jit(solution)/shard_map/ppermute | solution.py:78
  23.1 1.0 %collective-permute-done.1.refs_1_ = bf16[64,2176]{1,0:T(8,128)(2,1)S(1)} collective-permute-done((bf16[64,2176]{1,0:T(8,128)(2,1)S(1)}, bf16[64,2176]{1,0:T(8,128)(2,1)S(1)}, u32[]{:S(2)}, u32[]{:S(2)}) %collective-permute-start.1) | collective-permute-done | bytes 278560 | tf_op jit(solution)/shard_map/ppermute | solution.py:78
  24.6 0.7 combine.7
  25.3 2.6 %collective-permute-start.3 = (bf16[32,2176]{1,0:T(8,128)(2,1)S(1)}, bf16[32,2176]{1,0:T(8,128)(2,1)S(1)}, u32[]{:S(2)}, u32[]{:S(2)}) collective-permute-start(bf16[32,2176]{1,0:T(8,128)(2,1)S(1)} %get-tuple-element.53), channel_id=1, source_target_pairs={{0,6},{1,7},{2,4},{3,5},{4,2},{5,3},{6,0},{7,1},{8,14},{9,15},{10,... | collective-permute-start | bytes 417800 | tf_op jit(solution)/shard_map/ppermute | solution.py:78
  28.9 2.8 %far_product.5 = (bf16[128,2176]{1,0:T(8,128)(2,1)S(1)}, f32[2,64,2176]{2,1,0:T(8,128)S(1)}) custom-call(s32[1]{0:T(128)} %bitcast.2.virt_ref, s32[1]{0:T(128)} %bitcast.3.me_ref, f32[1]{0:T(128)S(6)} %copy.7.energy_ref, bf16[2,128,1024]{2,1,0:T(8,128)(2,1)S(1)} %collective-permute-done.6.far_ref, f32[2,16,32,2048]{3,2,1,0:T(8,128)S(1)} %get-tuple-element.45.near_ref, ...), custom_call_target="tpu_custom_call" | custom-call | flops 110000000 | tf_op jit(solution)/shard_map/far_product/pallas_call | solution.py:281
  31.7 0.6 collective-permute-done.3.refs_1_
  32.4 2.6 %collective-permute-done.4.refs_2_ = bf16[32,2176]{1,0:T(8,128)(2,1)S(1)} collective-permute-done((bf16[32,2176]{1,0:T(8,128)(2,1)S(1)}, bf16[32,2176]{1,0:T(8,128)(2,1)S(1)}, u32[]{:S(2)}, u32[]{:S(2)}) %collective-permute-start.4) | collective-permute-done | bytes 139296 | tf_op jit(solution)/shard_map/ppermute | solution.py:78
  35.4 2.7 %collective-permute-start.7 = (bf16[16,2176]{1,0:T(8,128)(2,1)S(1)}, bf16[16,2176]{1,0:T(8,128)(2,1)S(1)}, u32[]{:S(2)}, u32[]{:S(2)}) collective-permute-start(bf16[16,2176]{1,0:T(8,128)(2,1)S(1)} %get-tuple-element.60), channel_id=1, source_target_pairs={{0,8},{1,9},{2,10},{3,11},{4,12},{5,13},{6,14},{7,15},{8,0},{9,1},... | collective-permute-start | bytes 208904 | tf_op jit(solution)/shard_map/ppermute | solution.py:78
  38.5 0.8 %collective-permute-done.8.far_ref = bf16[2,128,1024]{2,1,0:T(8,128)(2,1)S(1)} collective-permute-done((bf16[2,128,1024]{2,1,0:T(8,128)(2,1)S(1)}, bf16[2,128,1024]{2,1,0:T(8,128)(2,1)S(1)}, u32[]{:S(2)}, u32[]{:S(2)}) %collective-permute-start.8) | collective-permute-done | bytes 524320 | tf_op jit(solution)/shard_map/ppermute | solution.py:78
  39.3 2.8 %far_product.6 = (bf16[128,2176]{1,0:T(8,128)(2,1)S(1)}, f32[2,64,2176]{2,1,0:T(8,128)S(1)}) custom-call(s32[1]{0:T(128)} %bitcast.2.virt_ref, s32[1]{0:T(128)} %bitcast.3.me_ref, f32[1]{0:T(128)S(6)} %copy.7.energy_ref, bf16[2,128,1024]{2,1,0:T(8,128)(2,1)S(1)} %collective-permute-done.8.far_ref, f32[2,16,32,2048]{3,2,1,0:T(8,128)S(1)} %get-tuple-element.45.near_ref, ...), custom_call_target="tpu_custom_call" | custom-call | flops 110000000 | tf_op jit(solution)/shard_map/far_product/pallas_call | solution.py:281
  42.3 1.8 %collective-permute-done.11.refs_3_ = bf16[128,2176]{1,0:T(8,128)(2,1)S(1)} collective-permute-done((bf16[128,2176]{1,0:T(8,128)(2,1)S(1)}, bf16[128,2176]{1,0:T(8,128)(2,1)S(1)}, u32[]{:S(2)}, u32[]{:S(2)}) %collective-permute-start.11) | collective-permute-done | bytes 557088 | tf_op jit(solution)/shard_map/ppermute | solution.py:78
  44.2 1.3 %combine.10 = (f32[2,16,2176]{2,1,0:T(8,128)S(1)}, f32[2,16,2176]{2,1,0:T(8,128)S(1)}, bf16[64,2176]{1,0:T(8,128)(2,1)S(1)}, bf16[64,2176]{1,0:T(8,128)(2,1)S(1)}, bf16[64,2176]{1,0:T(8,128)(2,1)S(1)}) custom-call(f32[2,64,2176]{2,1,0:T(8,128)S(1)} %get-tuple-element.58.refs_4_.refs_0_, f32[2,64,2176]{2,1,0:T(8,128)S(1)} %get-tuple-element.62.refs_2_.refs_1_, ...), custom_call_target="tpu_custom_call" | custom-call | flops 110000000 | tf_op jit(solution)/shard_map/combine/pallas_call | solution.py:324
  45.5 3.5 %collective-permute-start.12 = (bf16[64,2176]{1,0:T(8,128)(2,1)S(1)}, bf16[64,2176]{1,0:T(8,128)(2,1)S(1)}, u32[]{:S(2)}, u32[]{:S(2)}) collective-permute-start(bf16[64,2176]{1,0:T(8,128)(2,1)S(1)} %get-tuple-element.69), channel_id=1, source_target_pairs={{0,6},{1,7},{2,4},{3,5},{4,2},{5,3},{6,0},{7,1},{8,14},{9,15},{10,... | collective-permute-start | bytes 835592 | tf_op jit(solution)/shard_map/ppermute | solution.py:78
  49.0 0.6 collective-permute-start.14
  49.6 1.9 %collective-permute-done.9.far_ref = bf16[2,128,1024]{2,1,0:T(8,128)(2,1)S(1)} collective-permute-done((bf16[2,128,1024]{2,1,0:T(8,128)(2,1)S(1)}, bf16[2,128,1024]{2,1,0:T(8,128)(2,1)S(1)}, u32[]{:S(2)}, u32[]{:S(2)}) %collective-permute-start.9) | collective-permute-done | bytes 524320 | tf_op jit(solution)/shard_map/ppermute | solution.py:78
  51.5 3.0 %far_product.7 = (bf16[128,2176]{1,0:T(8,128)(2,1)S(1)}, f32[2,64,2176]{2,1,0:T(8,128)S(1)}) custom-call(s32[1]{0:T(128)} %bitcast.2.virt_ref, s32[1]{0:T(128)} %bitcast.3.me_ref, f32[1]{0:T(128)S(6)} %copy.7.energy_ref, bf16[2,128,1024]{2,1,0:T(8,128)(2,1)S(1)} %collective-permute-done.9.far_ref, f32[2,16,32,2048]{3,2,1,0:T(8,128)S(1)} %get-tuple-element.45.near_ref, ...), custom_call_target="tpu_custom_call" | custom-call | flops 110000000 | tf_op jit(solution)/shard_map/far_product/pallas_call | solution.py:281
  54.7 1.9 %collective-permute-done.15.refs_1_ = bf16[128,2176]{1,0:T(8,128)(2,1)S(1)} collective-permute-done((bf16[128,2176]{1,0:T(8,128)(2,1)S(1)}, bf16[128,2176]{1,0:T(8,128)(2,1)S(1)}, u32[]{:S(2)}, u32[]{:S(2)}) %collective-permute-start.15) | collective-permute-done | bytes 557088 | tf_op jit(solution)/shard_map/ppermute | solution.py:78
  56.5 0.7 combine.11
  57.2 1.8 %collective-permute-start.16 = (bf16[32,2176]{1,0:T(8,128)(2,1)S(1)}, bf16[32,2176]{1,0:T(8,128)(2,1)S(1)}, u32[]{:S(2)}, u32[]{:S(2)}) collective-permute-start(bf16[32,2176]{1,0:T(8,128)(2,1)S(1)} %get-tuple-element.76), channel_id=1, source_target_pairs={{0,6},{1,7},{2,4},{3,5},{4,2},{5,3},{6,0},{7,1},{8,14},{9,15},{10,... | collective-permute-start | bytes 417800 | tf_op jit(solution)/shard_map/ppermute | solution.py:78
  59.1 1.3 %collective-permute-start.17 = (bf16[32,2176]{1,0:T(8,128)(2,1)S(1)}, bf16[32,2176]{1,0:T(8,128)(2,1)S(1)}, u32[]{:S(2)}, u32[]{:S(2)}) collective-permute-start(bf16[32,2176]{1,0:T(8,128)(2,1)S(1)} %get-tuple-element.77), channel_id=1, source_target_pairs={{0,2},{1,3},{2,0},{3,1},{4,6},{5,7},{6,4},{7,5},{8,10},{9,11},{10,... | collective-permute-start | bytes 417800 | tf_op jit(solution)/shard_map/ppermute | solution.py:78
  60.8 1.7 %collective-permute-done.13.refs_3_ = bf16[64,2176]{1,0:T(8,128)(2,1)S(1)} collective-permute-done((bf16[64,2176]{1,0:T(8,128)(2,1)S(1)}, bf16[64,2176]{1,0:T(8,128)(2,1)S(1)}, u32[]{:S(2)}, u32[]{:S(2)}) %collective-permute-start.13) | collective-permute-done | bytes 278560 | tf_op jit(solution)/shard_map/ppermute | solution.py:78
  62.5 0.7 combine.12
  63.2 3.5 %collective-permute-start.19 = (bf16[32,2176]{1,0:T(8,128)(2,1)S(1)}, bf16[32,2176]{1,0:T(8,128)(2,1)S(1)}, u32[]{:S(2)}, u32[]{:S(2)}) collective-permute-start(bf16[32,2176]{1,0:T(8,128)(2,1)S(1)} %get-tuple-element.80), channel_id=1, source_target_pairs={{0,8},{1,9},{2,10},{3,11},{4,12},{5,13},{6,14},{7,15},{8,0},{9,1},... | collective-permute-start | bytes 417800 | tf_op jit(solution)/shard_map/ppermute | solution.py:78
  66.7 1.2 %collective-permute-done.17.refs_2_ = bf16[32,2176]{1,0:T(8,128)(2,1)S(1)} collective-permute-done((bf16[32,2176]{1,0:T(8,128)(2,1)S(1)}, bf16[32,2176]{1,0:T(8,128)(2,1)S(1)}, u32[]{:S(2)}, u32[]{:S(2)}) %collective-permute-start.17) | collective-permute-done | bytes 139296 | tf_op jit(solution)/shard_map/ppermute | solution.py:78
  68.2 4.1 %collective-permute-start.20 = (bf16[16,2176]{1,0:T(8,128)(2,1)S(1)}, bf16[16,2176]{1,0:T(8,128)(2,1)S(1)}, u32[]{:S(2)}, u32[]{:S(2)}) collective-permute-start(bf16[16,2176]{1,0:T(8,128)(2,1)S(1)} %get-tuple-element.81), channel_id=1, source_target_pairs={{0,8},{1,9},{2,10},{3,11},{4,12},{5,13},{6,14},{7,15},{8,0},{9,1},... | collective-permute-start | bytes 208904 | tf_op jit(solution)/shard_map/ppermute | solution.py:78
  72.4 4.2 %collective-permute-done.20.refs_4_ = bf16[16,2176]{1,0:T(8,128)(2,1)S(1)} collective-permute-done((bf16[16,2176]{1,0:T(8,128)(2,1)S(1)}, bf16[16,2176]{1,0:T(8,128)(2,1)S(1)}, u32[]{:S(2)}, u32[]{:S(2)}) %collective-permute-start.20) | collective-permute-done | bytes 69664 | tf_op jit(solution)/shard_map/ppermute | solution.py:78
  76.5 1.0 %finish.1 = (f32[32,2048]{1,0:T(8,128)}, f32[32,2048]{1,0:T(8,128)}) custom-call(f32[2,8,2048]{2,1,0:T(8,128)S(1)} %share.1.refs_2_.ready_ref, f32[2,8,2176]{2,1,0:T(8,128)S(1)} %get-tuple-element.74.refs_4_.refs_0_, f32[2,8,2176]{2,1,0:T(8,128)S(1)} %get-tuple-element.75.refs_1_, f32[2,8,2176]{2,1,0:T(8,128)S(1)} %get-tuple-element.79.refs_2_, ...), custom_call_target="tpu_custom_call" | custom-call | flops 110000000 | tf_op jit(solution)/shard_map/finish/pallas_call | solution.py:395
  (26 shorter events, 4.6 us)
Async XLA Ops:
  1.9 15.8 %collective-permute-start = (bf16[2,128,1024]{2,1,0:T(8,128)(2,1)S(1)}, bf16[2,128,1024]{2,1,0:T(8,128)(2,1)S(1)}, u32[]{:S(2)}, u32[]{:S(2)}) collective-permute-start(bf16[2,128,1024]{2,1,0:T(8,128)(2,1)S(1)} %get-tuple-element.43), channel_id=1, source_target_pairs={{0,16},{16,0},{1,17},{17,1},{2,18},{18,2},{3,19},{19,3},{4,20},{20... | collective-permute-start | bytes 1572872 | tf_op jit(solution)/shard_map/ppermute | solution.py:78
  4.9 24.0 %collective-permute-start.6 = (bf16[2,128,1024]{2,1,0:T(8,128)(2,1)S(1)}, bf16[2,128,1024]{2,1,0:T(8,128)(2,1)S(1)}, u32[]{:S(2)}, u32[]{:S(2)}) collective-permute-start(bf16[2,128,1024]{2,1,0:T(8,128)(2,1)S(1)} %get-tuple-element.56), channel_id=1, source_target_pairs={{0,16},{16,0},{1,17},{17,1},{2,18},{18,2},{3,19},{19,3},{4,20},{20... | collective-permute-start | bytes 1572872 | tf_op jit(solution)/shard_map/ppermute | solution.py:78
  20.5 18.8 %collective-permute-start.8 = (bf16[2,128,1024]{2,1,0:T(8,128)(2,1)S(1)}, bf16[2,128,1024]{2,1,0:T(8,128)(2,1)S(1)}, u32[]{:S(2)}, u32[]{:S(2)}) collective-permute-start(bf16[2,128,1024]{2,1,0:T(8,128)(2,1)S(1)} %get-tuple-element.61.rest_0_), channel_id=1, source_target_pairs={{0,16},{16,0},{1,17},{17,1},{2,18},{18,2},{3,19},{19,3},{4,20},{20... | collective-permute-start | bytes 1572872 | tf_op jit(solution)/shard_map/ppermute | solution.py:78
  22.6 1.6 %collective-permute-start.1 = (bf16[64,2176]{1,0:T(8,128)(2,1)S(1)}, bf16[64,2176]{1,0:T(8,128)(2,1)S(1)}, u32[]{:S(2)}, u32[]{:S(2)}) collective-permute-start(bf16[64,2176]{1,0:T(8,128)(2,1)S(1)} %get-tuple-element.50), channel_id=1, source_target_pairs={{0,1},{1,0},{2,3},{3,2},{4,5},{5,4},{6,7},{7,6},{8,9},{9,8},{10,11... | collective-permute-start | bytes 835592 | tf_op jit(solution)/shard_map/ppermute | solution.py:78
  22.6 2.0 %collective-permute-start.2 = (bf16[64,2176]{1,0:T(8,128)(2,1)S(1)}, bf16[64,2176]{1,0:T(8,128)(2,1)S(1)}, u32[]{:S(2)}, u32[]{:S(2)}) collective-permute-start(bf16[64,2176]{1,0:T(8,128)(2,1)S(1)} %get-tuple-element.51), channel_id=1, source_target_pairs={{0,1},{1,0},{2,3},{3,2},{4,5},{5,4},{6,7},{7,6},{8,9},{9,8},{10,11... | collective-permute-start | bytes 835592 | tf_op jit(solution)/shard_map/ppermute | solution.py:78
  25.3 7.1 %collective-permute-start.3 = (bf16[32,2176]{1,0:T(8,128)(2,1)S(1)}, bf16[32,2176]{1,0:T(8,128)(2,1)S(1)}, u32[]{:S(2)}, u32[]{:S(2)}) collective-permute-start(bf16[32,2176]{1,0:T(8,128)(2,1)S(1)} %get-tuple-element.53), channel_id=1, source_target_pairs={{0,6},{1,7},{2,4},{3,5},{4,2},{5,3},{6,0},{7,1},{8,14},{9,15},{10,... | collective-permute-start | bytes 417800 | tf_op jit(solution)/shard_map/ppermute | solution.py:78
  27.9 7.1 %collective-permute-start.4 = (bf16[32,2176]{1,0:T(8,128)(2,1)S(1)}, bf16[32,2176]{1,0:T(8,128)(2,1)S(1)}, u32[]{:S(2)}, u32[]{:S(2)}) collective-permute-start(bf16[32,2176]{1,0:T(8,128)(2,1)S(1)} %get-tuple-element.54), channel_id=1, source_target_pairs={{0,2},{1,3},{2,0},{3,1},{4,6},{5,7},{6,4},{7,5},{8,10},{9,11},{10,... | collective-permute-start | bytes 417800 | tf_op jit(solution)/shard_map/ppermute | solution.py:78
  28.4 6.6 %collective-permute-start.5 = (bf16[32,2176]{1,0:T(8,128)(2,1)S(1)}, bf16[32,2176]{1,0:T(8,128)(2,1)S(1)}, u32[]{:S(2)}, u32[]{:S(2)}) collective-permute-start(bf16[32,2176]{1,0:T(8,128)(2,1)S(1)} %get-tuple-element.55), channel_id=1, source_target_pairs={{0,4},{1,5},{2,6},{3,7},{4,0},{5,1},{6,2},{7,3},{8,12},{9,13},{10,... | collective-permute-start | bytes 417800 | tf_op jit(solution)/shard_map/ppermute | solution.py:78
  35.4 6.9 %collective-permute-start.7 = (bf16[16,2176]{1,0:T(8,128)(2,1)S(1)}, bf16[16,2176]{1,0:T(8,128)(2,1)S(1)}, u32[]{:S(2)}, u32[]{:S(2)}) collective-permute-start(bf16[16,2176]{1,0:T(8,128)(2,1)S(1)} %get-tuple-element.60), channel_id=1, source_target_pairs={{0,8},{1,9},{2,10},{3,11},{4,12},{5,13},{6,14},{7,15},{8,0},{9,1},... | collective-permute-start | bytes 208904 | tf_op jit(solution)/shard_map/ppermute | solution.py:78
  38.0 13.5 %collective-permute-start.9 = (bf16[2,128,1024]{2,1,0:T(8,128)(2,1)S(1)}, bf16[2,128,1024]{2,1,0:T(8,128)(2,1)S(1)}, u32[]{:S(2)}, u32[]{:S(2)}) collective-permute-start(bf16[2,128,1024]{2,1,0:T(8,128)(2,1)S(1)} %get-tuple-element.63.rest_1_), channel_id=1, source_target_pairs={{0,16},{16,0},{1,17},{17,1},{2,18},{18,2},{3,19},{19,3},{4,20},{20... | collective-permute-start | bytes 1572872 | tf_op jit(solution)/shard_map/ppermute | solution.py:78
  38.5 3.8 %collective-permute-start.10 = (bf16[128,2176]{1,0:T(8,128)(2,1)S(1)}, bf16[128,2176]{1,0:T(8,128)(2,1)S(1)}, u32[]{:S(2)}, u32[]{:S(2)}) collective-permute-start(bf16[128,2176]{1,0:T(8,128)(2,1)S(1)} %get-tuple-element.64), channel_id=1, source_target_pairs={{0,1},{1,0},{2,3},{3,2},{4,5},{5,4},{6,7},{7,6},{8,9},{9,8},{10,11... | collective-permute-start | bytes 1671176 | tf_op jit(solution)/shard_map/ppermute | solution.py:78
  42.1 2.0 %collective-permute-start.11 = (bf16[128,2176]{1,0:T(8,128)(2,1)S(1)}, bf16[128,2176]{1,0:T(8,128)(2,1)S(1)}, u32[]{:S(2)}, u32[]{:S(2)}) collective-permute-start(bf16[128,2176]{1,0:T(8,128)(2,1)S(1)} %get-tuple-element.65), channel_id=1, source_target_pairs={{0,1},{1,0},{2,3},{3,2},{4,5},{5,4},{6,7},{7,6},{8,9},{9,8},{10,11... | collective-permute-start | bytes 1671176 | tf_op jit(solution)/shard_map/ppermute | solution.py:78
  45.5 14.9 %collective-permute-start.12 = (bf16[64,2176]{1,0:T(8,128)(2,1)S(1)}, bf16[64,2176]{1,0:T(8,128)(2,1)S(1)}, u32[]{:S(2)}, u32[]{:S(2)}) collective-permute-start(bf16[64,2176]{1,0:T(8,128)(2,1)S(1)} %get-tuple-element.69), channel_id=1, source_target_pairs={{0,6},{1,7},{2,4},{3,5},{4,2},{5,3},{6,0},{7,1},{8,14},{9,15},{10,... | collective-permute-start | bytes 835592 | tf_op jit(solution)/shard_map/ppermute | solution.py:78
  49.0 13.5 %collective-permute-start.13 = (bf16[64,2176]{1,0:T(8,128)(2,1)S(1)}, bf16[64,2176]{1,0:T(8,128)(2,1)S(1)}, u32[]{:S(2)}, u32[]{:S(2)}) collective-permute-start(bf16[64,2176]{1,0:T(8,128)(2,1)S(1)} %get-tuple-element.70), channel_id=1, source_target_pairs={{0,2},{1,3},{2,0},{3,1},{4,6},{5,7},{6,4},{7,5},{8,10},{9,11},{10,... | collective-permute-start | bytes 835592 | tf_op jit(solution)/shard_map/ppermute | solution.py:78
  49.0 13.5 %collective-permute-start.14 = (bf16[64,2176]{1,0:T(8,128)(2,1)S(1)}, bf16[64,2176]{1,0:T(8,128)(2,1)S(1)}, u32[]{:S(2)}, u32[]{:S(2)}) collective-permute-start(bf16[64,2176]{1,0:T(8,128)(2,1)S(1)} %get-tuple-element.71), channel_id=1, source_target_pairs={{0,4},{1,5},{2,6},{3,7},{4,0},{5,1},{6,2},{7,3},{8,12},{9,13},{10,... | collective-permute-start | bytes 835592 | tf_op jit(solution)/shard_map/ppermute | solution.py:78
  54.5 2.0 %collective-permute-start.15 = (bf16[128,2176]{1,0:T(8,128)(2,1)S(1)}, bf16[128,2176]{1,0:T(8,128)(2,1)S(1)}, u32[]{:S(2)}, u32[]{:S(2)}) collective-permute-start(bf16[128,2176]{1,0:T(8,128)(2,1)S(1)} %get-tuple-element.72), channel_id=1, source_target_pairs={{0,1},{1,0},{2,3},{3,2},{4,5},{5,4},{6,7},{7,6},{8,9},{9,8},{10,11... | collective-permute-start | bytes 1671176 | tf_op jit(solution)/shard_map/ppermute | solution.py:78
  57.2 9.4 %collective-permute-start.16 = (bf16[32,2176]{1,0:T(8,128)(2,1)S(1)}, bf16[32,2176]{1,0:T(8,128)(2,1)S(1)}, u32[]{:S(2)}, u32[]{:S(2)}) collective-permute-start(bf16[32,2176]{1,0:T(8,128)(2,1)S(1)} %get-tuple-element.76), channel_id=1, source_target_pairs={{0,6},{1,7},{2,4},{3,5},{4,2},{5,3},{6,0},{7,1},{8,14},{9,15},{10,... | collective-permute-start | bytes 417800 | tf_op jit(solution)/shard_map/ppermute | solution.py:78
  59.1 8.8 %collective-permute-start.17 = (bf16[32,2176]{1,0:T(8,128)(2,1)S(1)}, bf16[32,2176]{1,0:T(8,128)(2,1)S(1)}, u32[]{:S(2)}, u32[]{:S(2)}) collective-permute-start(bf16[32,2176]{1,0:T(8,128)(2,1)S(1)} %get-tuple-element.77), channel_id=1, source_target_pairs={{0,2},{1,3},{2,0},{3,1},{4,6},{5,7},{6,4},{7,5},{8,10},{9,11},{10,... | collective-permute-start | bytes 417800 | tf_op jit(solution)/shard_map/ppermute | solution.py:78
  60.4 7.5 %collective-permute-start.18 = (bf16[32,2176]{1,0:T(8,128)(2,1)S(1)}, bf16[32,2176]{1,0:T(8,128)(2,1)S(1)}, u32[]{:S(2)}, u32[]{:S(2)}) collective-permute-start(bf16[32,2176]{1,0:T(8,128)(2,1)S(1)} %get-tuple-element.78), channel_id=1, source_target_pairs={{0,4},{1,5},{2,6},{3,7},{4,0},{5,1},{6,2},{7,3},{8,12},{9,13},{10,... | collective-permute-start | bytes 417800 | tf_op jit(solution)/shard_map/ppermute | solution.py:78
  63.2 9.2 %collective-permute-start.19 = (bf16[32,2176]{1,0:T(8,128)(2,1)S(1)}, bf16[32,2176]{1,0:T(8,128)(2,1)S(1)}, u32[]{:S(2)}, u32[]{:S(2)}) collective-permute-start(bf16[32,2176]{1,0:T(8,128)(2,1)S(1)} %get-tuple-element.80), channel_id=1, source_target_pairs={{0,8},{1,9},{2,10},{3,11},{4,12},{5,13},{6,14},{7,15},{8,0},{9,1},... | collective-permute-start | bytes 417800 | tf_op jit(solution)/shard_map/ppermute | solution.py:78
  68.2 8.3 %collective-permute-start.20 = (bf16[16,2176]{1,0:T(8,128)(2,1)S(1)}, bf16[16,2176]{1,0:T(8,128)(2,1)S(1)}, u32[]{:S(2)}, u32[]{:S(2)}) collective-permute-start(bf16[16,2176]{1,0:T(8,128)(2,1)S(1)} %get-tuple-element.81), channel_id=1, source_target_pairs={{0,8},{1,9},{2,10},{3,11},{4,12},{5,13},{6,14},{7,15},{8,0},{9,1},... | collective-permute-start | bytes 208904 | tf_op jit(solution)/shard_map/ppermute | solution.py:78

commit v12 on v11

--- a/solution.py
+++ b/solution.py
@@ -11,7 +11,9 @@
 UNITS = ((0,), (1, 2), (3,))
 SPLIT = (2, 1, 1, 1)
 BESIDE = 6
-FAR = (0.1, 0.1, 0.1, 0.1)
+FAR = (0.1, 0.1, 1.0, 0.1)
+
+
 def product(left, right):
     return jnp.einsum("woe,wev->wov", left, right, preferred_element_type=jnp.float32)
 

time: 77.7 us -> 78.4 us (level)
  waiting for transfers between devices: 18.7 us -> 22.6 us
  starting transfers between devices: 28 us -> 24.7 us
    ppermute x21, waiting for transfers between devices: 18.7 us -> 22.6 us  [swap(): return lax.ppermute(array, axis, pairs)]
    ppermute x21, starting transfers between devices: 28 us -> 24.7 us  [swap(): return lax.ppermute(array, axis, pairs)]
  transfers between devices with their start and end apart: 21 -> 21, of which waited for: 14 -> 15; matrix products, arithmetic and copies ran while one was open for 0% -> 0% of each run, Pallas kernels for 35% -> 35%
where the time goes in v12:
time: 78.4 us; the launch traced here: 78.2 us
  Pallas kernels  29.4 us (38%)
  starting transfers between devices  24.7 us (32%)
  waiting for transfers between devices  22.6 us (29%)
  between operations  1.41 us (2%)
    ppermute x21, starting transfers between devices, swap(): return lax.ppermute(array, axis, pairs)  24.7 us
    ppermute x21, waiting for transfers between devices, swap(): return lax.ppermute(array, axis, pairs)  22.6 us
    pallas_call x4, Pallas kernels, far_product(): pl.pallas_call(functools.partial(far_kernel, place_weights(stages), count...  11.4 us
    pallas_call x1, Pallas kernels, near_product(): pl.pallas_call(functools.partial(near_kernel, chunk, tile), out_shape=(ja...  10.3 us
    pallas_call x7, Pallas kernels, combine(): pl.pallas_call(functools.partial(combine_kernel, layout, len(after)), out...  4.12 us
    pallas_call x2, Pallas kernels, cut(): pl.pallas_call(cut_kernel, out_shape=(out, out), grid=(1,), in_specs=[blo...  2.55 us
  transfers between devices with their start and end apart: 21, of which 15 were waited for; matrix products, arithmetic and copies ran while one was open for 0% of the time, Pallas kernels for 35%

profile of v12, /device:TPU:0, one launch (start us, length us, event | category | flops | bytes accessed | tf_op | source)
XLA Modules:
  0.0 78.2 jit_solution(4159713700400343616)
XLA Ops:
  0.6 1.3 %cut.3 = (bf16[2,128,1024]{2,1,0:T(8,128)(2,1)S(1)}, bf16[2,128,1024]{2,1,0:T(8,128)(2,1)S(1)}) custom-call(bf16[16,32,1024]{2,1,0:T(8,128)(2,1)} %bitcast.6, bf16[16,32,1024]{2,1,0:T(8,128)(2,1)} %bitcast.9), custom_call_target="tpu_custom_call" | custom-call | flops 110000000 | tf_op jit(solution)/shard_map/cut/pallas_call | solution.py:166
  1.9 3.0 %collective-permute-start = (bf16[2,128,1024]{2,1,0:T(8,128)(2,1)S(1)}, bf16[2,128,1024]{2,1,0:T(8,128)(2,1)S(1)}, u32[]{:S(2)}, u32[]{:S(2)}) collective-permute-start(bf16[2,128,1024]{2,1,0:T(8,128)(2,1)S(1)} %get-tuple-element.43), channel_id=1, source_target_pairs={{0,16},{16,0},{1,17},{17,1},{2,18},{18,2},{3,19},{19,3},{4,20},{20... | collective-permute-start | bytes 1572872 | tf_op jit(solution)/shard_map/ppermute | solution.py:80
  5.0 1.3 %cut.2 = (bf16[2,128,1024]{2,1,0:T(8,128)(2,1)S(1)}, bf16[2,128,1024]{2,1,0:T(8,128)(2,1)S(1)}) custom-call(bf16[16,32,1024]{2,1,0:T(8,128)(2,1)} %bitcast.7, bf16[16,32,1024]{2,1,0:T(8,128)(2,1)} %bitcast.10), custom_call_target="tpu_custom_call" | custom-call | flops 110000000 | tf_op jit(solution)/shard_map/cut/pallas_call | solution.py:166
  6.9 10.3 %near_product.1 = (f32[2,16,32,2048]{3,2,1,0:T(8,128)S(1)}, bf16[1024,2048]{1,0:T(8,128)(2,1)S(1)}, bf16[1024,2048]{1,0:T(8,128)(2,1)S(1)}) custom-call(s32[1]{0:T(128)} %bitcast.2.virt_ref, s32[1]{0:T(128)} %bitcast.3.me_ref, f32[1]{0:T(128)S(6)} %copy.7.energy_ref, bf16[16,32,1024]{2,1,0:T(8,128)(2,1)} %bitcast.8, bf16[16,32,1024]{2,1,0:T(8,128)(2,1)} %bitcast.11, ...), custom_call_target="tpu_custom_call" | custom-call | flops 9900000256 | tf_op jit(solution)/shard_map/near_product/pallas_call | solution.py:232
  17.7 2.8 %far_product.4 = (bf16[64,2176]{1,0:T(8,128)(2,1)S(1)}, bf16[64,2176]{1,0:T(8,128)(2,1)S(1)}, f32[2,64,2176]{2,1,0:T(8,128)S(1)}) custom-call(s32[1]{0:T(128)} %bitcast.2.virt_ref, s32[1]{0:T(128)} %bitcast.3.me_ref, f32[1]{0:T(128)S(6)} %copy.7.energy_ref, bf16[2,128,1024]{2,1,0:T(8,128)(2,1)S(1)} %collective-permute-done.far_ref, ...), custom_call_target="tpu_custom_call" | custom-call | flops 110000000 | tf_op jit(solution)/shard_map/far_product/pallas_call | solution.py:283
  20.5 2.1 %collective-permute-start.8 = (bf16[2,128,1024]{2,1,0:T(8,128)(2,1)S(1)}, bf16[2,128,1024]{2,1,0:T(8,128)(2,1)S(1)}, u32[]{:S(2)}, u32[]{:S(2)}) collective-permute-start(bf16[2,128,1024]{2,1,0:T(8,128)(2,1)S(1)} %get-tuple-element.61.rest_0_), channel_id=1, source_target_pairs={{0,16},{16,0},{1,17},{17,1},{2,18},{18,2},{3,19},{19,3},{4,20},{20... | collective-permute-start | bytes 1572872 | tf_op jit(solution)/shard_map/ppermute | solution.py:80
  23.1 1.0 %collective-permute-done.1.refs_1_ = bf16[64,2176]{1,0:T(8,128)(2,1)S(1)} collective-permute-done((bf16[64,2176]{1,0:T(8,128)(2,1)S(1)}, bf16[64,2176]{1,0:T(8,128)(2,1)S(1)}, u32[]{:S(2)}, u32[]{:S(2)}) %collective-permute-start.1) | collective-permute-done | bytes 278560 | tf_op jit(solution)/shard_map/ppermute | solution.py:80
  24.6 0.7 combine.7
  25.3 2.6 %collective-permute-start.3 = (bf16[32,2176]{1,0:T(8,128)(2,1)S(1)}, bf16[32,2176]{1,0:T(8,128)(2,1)S(1)}, u32[]{:S(2)}, u32[]{:S(2)}) collective-permute-start(bf16[32,2176]{1,0:T(8,128)(2,1)S(1)} %get-tuple-element.53), channel_id=1, source_target_pairs={{0,6},{1,7},{2,4},{3,5},{4,2},{5,3},{6,0},{7,1},{8,14},{9,15},{10,... | collective-permute-start | bytes 417800 | tf_op jit(solution)/shard_map/ppermute | solution.py:80
  27.9 0.5 collective-permute-start.4
  28.9 2.8 %far_product.5 = (bf16[128,2176]{1,0:T(8,128)(2,1)S(1)}, f32[2,64,2176]{2,1,0:T(8,128)S(1)}) custom-call(s32[1]{0:T(128)} %bitcast.2.virt_ref, s32[1]{0:T(128)} %bitcast.3.me_ref, f32[1]{0:T(128)S(6)} %copy.7.energy_ref, bf16[2,128,1024]{2,1,0:T(8,128)(2,1)S(1)} %collective-permute-done.6.far_ref, f32[2,16,32,2048]{3,2,1,0:T(8,128)S(1)} %get-tuple-element.45.near_ref, ...), custom_call_target="tpu_custom_call" | custom-call | flops 110000000 | tf_op jit(solution)/shard_map/far_product/pallas_call | solution.py:283
  31.7 2.1 %collective-permute-start.9 = (bf16[2,128,1024]{2,1,0:T(8,128)(2,1)S(1)}, bf16[2,128,1024]{2,1,0:T(8,128)(2,1)S(1)}, u32[]{:S(2)}, u32[]{:S(2)}) collective-permute-start(bf16[2,128,1024]{2,1,0:T(8,128)(2,1)S(1)} %get-tuple-element.63.rest_1_), channel_id=1, source_target_pairs={{0,16},{16,0},{1,17},{17,1},{2,18},{18,2},{3,19},{19,3},{4,20},{20... | collective-permute-start | bytes 1572872 | tf_op jit(solution)/shard_map/ppermute | solution.py:80
  33.9 1.1 %collective-permute-done.4.refs_2_ = bf16[32,2176]{1,0:T(8,128)(2,1)S(1)} collective-permute-done((bf16[32,2176]{1,0:T(8,128)(2,1)S(1)}, bf16[32,2176]{1,0:T(8,128)(2,1)S(1)}, u32[]{:S(2)}, u32[]{:S(2)}) %collective-permute-start.4) | collective-permute-done | bytes 139296 | tf_op jit(solution)/shard_map/ppermute | solution.py:80
  35.4 2.7 %collective-permute-start.7 = (bf16[16,2176]{1,0:T(8,128)(2,1)S(1)}, bf16[16,2176]{1,0:T(8,128)(2,1)S(1)}, u32[]{:S(2)}, u32[]{:S(2)}) collective-permute-start(bf16[16,2176]{1,0:T(8,128)(2,1)S(1)} %get-tuple-element.60), channel_id=1, source_target_pairs={{0,8},{1,9},{2,10},{3,11},{4,12},{5,13},{6,14},{7,15},{8,0},{9,1},... | collective-permute-start | bytes 208904 | tf_op jit(solution)/shard_map/ppermute | solution.py:80
  38.0 2.1 %collective-permute-done.8.far_ref = bf16[2,128,1024]{2,1,0:T(8,128)(2,1)S(1)} collective-permute-done((bf16[2,128,1024]{2,1,0:T(8,128)(2,1)S(1)}, bf16[2,128,1024]{2,1,0:T(8,128)(2,1)S(1)}, u32[]{:S(2)}, u32[]{:S(2)}) %collective-permute-start.8) | collective-permute-done | bytes 524320 | tf_op jit(solution)/shard_map/ppermute | solution.py:80
  40.2 2.8 %far_product.6 = (bf16[128,2176]{1,0:T(8,128)(2,1)S(1)}, f32[2,64,2176]{2,1,0:T(8,128)S(1)}) custom-call(s32[1]{0:T(128)} %bitcast.2.virt_ref, s32[1]{0:T(128)} %bitcast.3.me_ref, f32[1]{0:T(128)S(6)} %copy.7.energy_ref, bf16[2,128,1024]{2,1,0:T(8,128)(2,1)S(1)} %collective-permute-done.8.far_ref, f32[2,16,32,2048]{3,2,1,0:T(8,128)S(1)} %get-tuple-element.45.near_ref, ...), custom_call_target="tpu_custom_call" | custom-call | flops 1100000000 | tf_op jit(solution)/shard_map/far_product/pallas_call | solution.py:283
  43.2 1.8 %collective-permute-done.11.refs_3_ = bf16[128,2176]{1,0:T(8,128)(2,1)S(1)} collective-permute-done((bf16[128,2176]{1,0:T(8,128)(2,1)S(1)}, bf16[128,2176]{1,0:T(8,128)(2,1)S(1)}, u32[]{:S(2)}, u32[]{:S(2)}) %collective-permute-start.11) | collective-permute-done | bytes 557088 | tf_op jit(solution)/shard_map/ppermute | solution.py:80
  45.0 1.3 %combine.10 = (f32[2,16,2176]{2,1,0:T(8,128)S(1)}, f32[2,16,2176]{2,1,0:T(8,128)S(1)}, bf16[64,2176]{1,0:T(8,128)(2,1)S(1)}, bf16[64,2176]{1,0:T(8,128)(2,1)S(1)}, bf16[64,2176]{1,0:T(8,128)(2,1)S(1)}) custom-call(f32[2,64,2176]{2,1,0:T(8,128)S(1)} %get-tuple-element.58.refs_4_.refs_0_, f32[2,64,2176]{2,1,0:T(8,128)S(1)} %get-tuple-element.62.refs_2_.refs_1_, ...), custom_call_target="tpu_custom_call" | custom-call | flops 110000000 | tf_op jit(solution)/shard_map/combine/pallas_call | solution.py:326
  46.3 3.1 %collective-permute-start.12 = (bf16[64,2176]{1,0:T(8,128)(2,1)S(1)}, bf16[64,2176]{1,0:T(8,128)(2,1)S(1)}, u32[]{:S(2)}, u32[]{:S(2)}) collective-permute-start(bf16[64,2176]{1,0:T(8,128)(2,1)S(1)} %get-tuple-element.69), channel_id=1, source_target_pairs={{0,6},{1,7},{2,4},{3,5},{4,2},{5,3},{6,0},{7,1},{8,14},{9,15},{10,... | collective-permute-start | bytes 835592 | tf_op jit(solution)/shard_map/ppermute | solution.py:80
  49.4 0.5 collective-permute-start.13
  50.6 3.0 %far_product.7 = (bf16[128,2176]{1,0:T(8,128)(2,1)S(1)}, f32[2,64,2176]{2,1,0:T(8,128)S(1)}) custom-call(s32[1]{0:T(128)} %bitcast.2.virt_ref, s32[1]{0:T(128)} %bitcast.3.me_ref, f32[1]{0:T(128)S(6)} %copy.7.energy_ref, bf16[2,128,1024]{2,1,0:T(8,128)(2,1)S(1)} %collective-permute-done.9.far_ref, f32[2,16,32,2048]{3,2,1,0:T(8,128)S(1)} %get-tuple-element.45.near_ref, ...), custom_call_target="tpu_custom_call" | custom-call | flops 110000000 | tf_op jit(solution)/shard_map/far_product/pallas_call | solution.py:283
  53.7 1.9 %collective-permute-done.15.refs_1_ = bf16[128,2176]{1,0:T(8,128)(2,1)S(1)} collective-permute-done((bf16[128,2176]{1,0:T(8,128)(2,1)S(1)}, bf16[128,2176]{1,0:T(8,128)(2,1)S(1)}, u32[]{:S(2)}, u32[]{:S(2)}) %collective-permute-start.15) | collective-permute-done | bytes 557088 | tf_op jit(solution)/shard_map/ppermute | solution.py:80
  55.6 0.7 combine.11
  56.3 2.8 %collective-permute-start.16 = (bf16[32,2176]{1,0:T(8,128)(2,1)S(1)}, bf16[32,2176]{1,0:T(8,128)(2,1)S(1)}, u32[]{:S(2)}, u32[]{:S(2)}) collective-permute-start(bf16[32,2176]{1,0:T(8,128)(2,1)S(1)} %get-tuple-element.76), channel_id=1, source_target_pairs={{0,6},{1,7},{2,4},{3,5},{4,2},{5,3},{6,0},{7,1},{8,14},{9,15},{10,... | collective-permute-start | bytes 417800 | tf_op jit(solution)/shard_map/ppermute | solution.py:80
  59.1 0.6 collective-permute-start.17
  59.8 3.1 %collective-permute-done.13.refs_3_ = bf16[64,2176]{1,0:T(8,128)(2,1)S(1)} collective-permute-done((bf16[64,2176]{1,0:T(8,128)(2,1)S(1)}, bf16[64,2176]{1,0:T(8,128)(2,1)S(1)}, u32[]{:S(2)}, u32[]{:S(2)}) %collective-permute-start.13) | collective-permute-done | bytes 278560 | tf_op jit(solution)/shard_map/ppermute | solution.py:80
  63.3 0.7 combine.12
  64.0 2.7 %collective-permute-start.19 = (bf16[32,2176]{1,0:T(8,128)(2,1)S(1)}, bf16[32,2176]{1,0:T(8,128)(2,1)S(1)}, u32[]{:S(2)}, u32[]{:S(2)}) collective-permute-start(bf16[32,2176]{1,0:T(8,128)(2,1)S(1)} %get-tuple-element.80), channel_id=1, source_target_pairs={{0,8},{1,9},{2,10},{3,11},{4,12},{5,13},{6,14},{7,15},{8,0},{9,1},... | collective-permute-start | bytes 417800 | tf_op jit(solution)/shard_map/ppermute | solution.py:80
  66.7 1.6 %collective-permute-done.17.refs_2_ = bf16[32,2176]{1,0:T(8,128)(2,1)S(1)} collective-permute-done((bf16[32,2176]{1,0:T(8,128)(2,1)S(1)}, bf16[32,2176]{1,0:T(8,128)(2,1)S(1)}, u32[]{:S(2)}, u32[]{:S(2)}) %collective-permute-start.17) | collective-permute-done | bytes 139296 | tf_op jit(solution)/shard_map/ppermute | solution.py:80
  68.3 3.2 %collective-permute-done.18.refs_3_ = bf16[32,2176]{1,0:T(8,128)(2,1)S(1)} collective-permute-done((bf16[32,2176]{1,0:T(8,128)(2,1)S(1)}, bf16[32,2176]{1,0:T(8,128)(2,1)S(1)}, u32[]{:S(2)}, u32[]{:S(2)}) %collective-permute-start.18) | collective-permute-done | bytes 139296 | tf_op jit(solution)/shard_map/ppermute | solution.py:80
  72.4 4.8 %collective-permute-done.20.refs_4_ = bf16[16,2176]{1,0:T(8,128)(2,1)S(1)} collective-permute-done((bf16[16,2176]{1,0:T(8,128)(2,1)S(1)}, bf16[16,2176]{1,0:T(8,128)(2,1)S(1)}, u32[]{:S(2)}, u32[]{:S(2)}) %collective-permute-start.20) | collective-permute-done | bytes 69664 | tf_op jit(solution)/shard_map/ppermute | solution.py:80
  77.2 1.0 %finish.1 = (f32[32,2048]{1,0:T(8,128)}, f32[32,2048]{1,0:T(8,128)}) custom-call(f32[2,8,2048]{2,1,0:T(8,128)S(1)} %share.1.refs_2_.ready_ref, f32[2,8,2176]{2,1,0:T(8,128)S(1)} %get-tuple-element.74.refs_4_.refs_0_, f32[2,8,2176]{2,1,0:T(8,128)S(1)} %get-tuple-element.75.refs_1_, f32[2,8,2176]{2,1,0:T(8,128)S(1)} %get-tuple-element.79.refs_2_, ...), custom_call_target="tpu_custom_call" | custom-call | flops 110000000 | tf_op jit(solution)/shard_map/finish/pallas_call | solution.py:397
  (26 shorter events, 4.8 us)
Async XLA Ops:
  1.9 15.8 %collective-permute-start = (bf16[2,128,1024]{2,1,0:T(8,128)(2,1)S(1)}, bf16[2,128,1024]{2,1,0:T(8,128)(2,1)S(1)}, u32[]{:S(2)}, u32[]{:S(2)}) collective-permute-start(bf16[2,128,1024]{2,1,0:T(8,128)(2,1)S(1)} %get-tuple-element.43), channel_id=1, source_target_pairs={{0,16},{16,0},{1,17},{17,1},{2,18},{18,2},{3,19},{19,3},{4,20},{20... | collective-permute-start | bytes 1572872 | tf_op jit(solution)/shard_map/ppermute | solution.py:80
  4.9 24.0 %collective-permute-start.6 = (bf16[2,128,1024]{2,1,0:T(8,128)(2,1)S(1)}, bf16[2,128,1024]{2,1,0:T(8,128)(2,1)S(1)}, u32[]{:S(2)}, u32[]{:S(2)}) collective-permute-start(bf16[2,128,1024]{2,1,0:T(8,128)(2,1)S(1)} %get-tuple-element.56), channel_id=1, source_target_pairs={{0,16},{16,0},{1,17},{17,1},{2,18},{18,2},{3,19},{19,3},{4,20},{20... | collective-permute-start | bytes 1572872 | tf_op jit(solution)/shard_map/ppermute | solution.py:80
  20.5 19.7 %collective-permute-start.8 = (bf16[2,128,1024]{2,1,0:T(8,128)(2,1)S(1)}, bf16[2,128,1024]{2,1,0:T(8,128)(2,1)S(1)}, u32[]{:S(2)}, u32[]{:S(2)}) collective-permute-start(bf16[2,128,1024]{2,1,0:T(8,128)(2,1)S(1)} %get-tuple-element.61.rest_0_), channel_id=1, source_target_pairs={{0,16},{16,0},{1,17},{17,1},{2,18},{18,2},{3,19},{19,3},{4,20},{20... | collective-permute-start | bytes 1572872 | tf_op jit(solution)/shard_map/ppermute | solution.py:80
  22.6 1.6 %collective-permute-start.1 = (bf16[64,2176]{1,0:T(8,128)(2,1)S(1)}, bf16[64,2176]{1,0:T(8,128)(2,1)S(1)}, u32[]{:S(2)}, u32[]{:S(2)}) collective-permute-start(bf16[64,2176]{1,0:T(8,128)(2,1)S(1)} %get-tuple-element.50), channel_id=1, source_target_pairs={{0,1},{1,0},{2,3},{3,2},{4,5},{5,4},{6,7},{7,6},{8,9},{9,8},{10,11... | collective-permute-start | bytes 835592 | tf_op jit(solution)/shard_map/ppermute | solution.py:80
  22.6 2.0 %collective-permute-start.2 = (bf16[64,2176]{1,0:T(8,128)(2,1)S(1)}, bf16[64,2176]{1,0:T(8,128)(2,1)S(1)}, u32[]{:S(2)}, u32[]{:S(2)}) collective-permute-start(bf16[64,2176]{1,0:T(8,128)(2,1)S(1)} %get-tuple-element.51), channel_id=1, source_target_pairs={{0,1},{1,0},{2,3},{3,2},{4,5},{5,4},{6,7},{7,6},{8,9},{9,8},{10,11... | collective-permute-start | bytes 835592 | tf_op jit(solution)/shard_map/ppermute | solution.py:80
  25.3 8.6 %collective-permute-start.3 = (bf16[32,2176]{1,0:T(8,128)(2,1)S(1)}, bf16[32,2176]{1,0:T(8,128)(2,1)S(1)}, u32[]{:S(2)}, u32[]{:S(2)}) collective-permute-start(bf16[32,2176]{1,0:T(8,128)(2,1)S(1)} %get-tuple-element.53), channel_id=1, source_target_pairs={{0,6},{1,7},{2,4},{3,5},{4,2},{5,3},{6,0},{7,1},{8,14},{9,15},{10,... | collective-permute-start | bytes 417800 | tf_op jit(solution)/shard_map/ppermute | solution.py:80
  27.9 7.1 %collective-permute-start.4 = (bf16[32,2176]{1,0:T(8,128)(2,1)S(1)}, bf16[32,2176]{1,0:T(8,128)(2,1)S(1)}, u32[]{:S(2)}, u32[]{:S(2)}) collective-permute-start(bf16[32,2176]{1,0:T(8,128)(2,1)S(1)} %get-tuple-element.54), channel_id=1, source_target_pairs={{0,2},{1,3},{2,0},{3,1},{4,6},{5,7},{6,4},{7,5},{8,10},{9,11},{10,... | collective-permute-start | bytes 417800 | tf_op jit(solution)/shard_map/ppermute | solution.py:80
  28.4 6.6 %collective-permute-start.5 = (bf16[32,2176]{1,0:T(8,128)(2,1)S(1)}, bf16[32,2176]{1,0:T(8,128)(2,1)S(1)}, u32[]{:S(2)}, u32[]{:S(2)}) collective-permute-start(bf16[32,2176]{1,0:T(8,128)(2,1)S(1)} %get-tuple-element.55), channel_id=1, source_target_pairs={{0,4},{1,5},{2,6},{3,7},{4,0},{5,1},{6,2},{7,3},{8,12},{9,13},{10,... | collective-permute-start | bytes 417800 | tf_op jit(solution)/shard_map/ppermute | solution.py:80
  31.7 18.8 %collective-permute-start.9 = (bf16[2,128,1024]{2,1,0:T(8,128)(2,1)S(1)}, bf16[2,128,1024]{2,1,0:T(8,128)(2,1)S(1)}, u32[]{:S(2)}, u32[]{:S(2)}) collective-permute-start(bf16[2,128,1024]{2,1,0:T(8,128)(2,1)S(1)} %get-tuple-element.63.rest_1_), channel_id=1, source_target_pairs={{0,16},{16,0},{1,17},{17,1},{2,18},{18,2},{3,19},{19,3},{4,20},{20... | collective-permute-start | bytes 1572872 | tf_op jit(solution)/shard_map/ppermute | solution.py:80
  33.9 9.3 %collective-permute-start.10 = (bf16[128,2176]{1,0:T(8,128)(2,1)S(1)}, bf16[128,2176]{1,0:T(8,128)(2,1)S(1)}, u32[]{:S(2)}, u32[]{:S(2)}) collective-permute-start(bf16[128,2176]{1,0:T(8,128)(2,1)S(1)} %get-tuple-element.64), channel_id=1, source_target_pairs={{0,1},{1,0},{2,3},{3,2},{4,5},{5,4},{6,7},{7,6},{8,9},{9,8},{10,11... | collective-permute-start | bytes 1671176 | tf_op jit(solution)/shard_map/ppermute | solution.py:80
  35.4 7.7 %collective-permute-start.7 = (bf16[16,2176]{1,0:T(8,128)(2,1)S(1)}, bf16[16,2176]{1,0:T(8,128)(2,1)S(1)}, u32[]{:S(2)}, u32[]{:S(2)}) collective-permute-start(bf16[16,2176]{1,0:T(8,128)(2,1)S(1)} %get-tuple-element.60), channel_id=1, source_target_pairs={{0,8},{1,9},{2,10},{3,11},{4,12},{5,13},{6,14},{7,15},{8,0},{9,1},... | collective-permute-start | bytes 208904 | tf_op jit(solution)/shard_map/ppermute | solution.py:80
  43.0 2.0 %collective-permute-start.11 = (bf16[128,2176]{1,0:T(8,128)(2,1)S(1)}, bf16[128,2176]{1,0:T(8,128)(2,1)S(1)}, u32[]{:S(2)}, u32[]{:S(2)}) collective-permute-start(bf16[128,2176]{1,0:T(8,128)(2,1)S(1)} %get-tuple-element.65), channel_id=1, source_target_pairs={{0,1},{1,0},{2,3},{3,2},{4,5},{5,4},{6,7},{7,6},{8,9},{9,8},{10,11... | collective-permute-start | bytes 1671176 | tf_op jit(solution)/shard_map/ppermute | solution.py:80
  46.3 13.3 %collective-permute-start.12 = (bf16[64,2176]{1,0:T(8,128)(2,1)S(1)}, bf16[64,2176]{1,0:T(8,128)(2,1)S(1)}, u32[]{:S(2)}, u32[]{:S(2)}) collective-permute-start(bf16[64,2176]{1,0:T(8,128)(2,1)S(1)} %get-tuple-element.69), channel_id=1, source_target_pairs={{0,6},{1,7},{2,4},{3,5},{4,2},{5,3},{6,0},{7,1},{8,14},{9,15},{10,... | collective-permute-start | bytes 835592 | tf_op jit(solution)/shard_map/ppermute | solution.py:80
  49.4 13.5 %collective-permute-start.13 = (bf16[64,2176]{1,0:T(8,128)(2,1)S(1)}, bf16[64,2176]{1,0:T(8,128)(2,1)S(1)}, u32[]{:S(2)}, u32[]{:S(2)}) collective-permute-start(bf16[64,2176]{1,0:T(8,128)(2,1)S(1)} %get-tuple-element.70), channel_id=1, source_target_pairs={{0,2},{1,3},{2,0},{3,1},{4,6},{5,7},{6,4},{7,5},{8,10},{9,11},{10,... | collective-permute-start | bytes 835592 | tf_op jit(solution)/shard_map/ppermute | solution.py:80
  49.9 13.4 %collective-permute-start.14 = (bf16[64,2176]{1,0:T(8,128)(2,1)S(1)}, bf16[64,2176]{1,0:T(8,128)(2,1)S(1)}, u32[]{:S(2)}, u32[]{:S(2)}) collective-permute-start(bf16[64,2176]{1,0:T(8,128)(2,1)S(1)} %get-tuple-element.71), channel_id=1, source_target_pairs={{0,4},{1,5},{2,6},{3,7},{4,0},{5,1},{6,2},{7,3},{8,12},{9,13},{10,... | collective-permute-start | bytes 835592 | tf_op jit(solution)/shard_map/ppermute | solution.py:80
  53.6 2.0 %collective-permute-start.15 = (bf16[128,2176]{1,0:T(8,128)(2,1)S(1)}, bf16[128,2176]{1,0:T(8,128)(2,1)S(1)}, u32[]{:S(2)}, u32[]{:S(2)}) collective-permute-start(bf16[128,2176]{1,0:T(8,128)(2,1)S(1)} %get-tuple-element.72), channel_id=1, source_target_pairs={{0,1},{1,0},{2,3},{3,2},{4,5},{5,4},{6,7},{7,6},{8,9},{9,8},{10,11... | collective-permute-start | bytes 1671176 | tf_op jit(solution)/shard_map/ppermute | solution.py:80
  56.3 10.4 %collective-permute-start.16 = (bf16[32,2176]{1,0:T(8,128)(2,1)S(1)}, bf16[32,2176]{1,0:T(8,128)(2,1)S(1)}, u32[]{:S(2)}, u32[]{:S(2)}) collective-permute-start(bf16[32,2176]{1,0:T(8,128)(2,1)S(1)} %get-tuple-element.76), channel_id=1, source_target_pairs={{0,6},{1,7},{2,4},{3,5},{4,2},{5,3},{6,0},{7,1},{8,14},{9,15},{10,... | collective-permute-start | bytes 417800 | tf_op jit(solution)/shard_map/ppermute | solution.py:80
  59.1 9.2 %collective-permute-start.17 = (bf16[32,2176]{1,0:T(8,128)(2,1)S(1)}, bf16[32,2176]{1,0:T(8,128)(2,1)S(1)}, u32[]{:S(2)}, u32[]{:S(2)}) collective-permute-start(bf16[32,2176]{1,0:T(8,128)(2,1)S(1)} %get-tuple-element.77), channel_id=1, source_target_pairs={{0,2},{1,3},{2,0},{3,1},{4,6},{5,7},{6,4},{7,5},{8,10},{9,11},{10,... | collective-permute-start | bytes 417800 | tf_op jit(solution)/shard_map/ppermute | solution.py:80
  59.6 11.9 %collective-permute-start.18 = (bf16[32,2176]{1,0:T(8,128)(2,1)S(1)}, bf16[32,2176]{1,0:T(8,128)(2,1)S(1)}, u32[]{:S(2)}, u32[]{:S(2)}) collective-permute-start(bf16[32,2176]{1,0:T(8,128)(2,1)S(1)} %get-tuple-element.78), channel_id=1, source_target_pairs={{0,4},{1,5},{2,6},{3,7},{4,0},{5,1},{6,2},{7,3},{8,12},{9,13},{10,... | collective-permute-start | bytes 417800 | tf_op jit(solution)/shard_map/ppermute | solution.py:80
  64.0 8.4 %collective-permute-start.19 = (bf16[32,2176]{1,0:T(8,128)(2,1)S(1)}, bf16[32,2176]{1,0:T(8,128)(2,1)S(1)}, u32[]{:S(2)}, u32[]{:S(2)}) collective-permute-start(bf16[32,2176]{1,0:T(8,128)(2,1)S(1)} %get-tuple-element.80), channel_id=1, source_target_pairs={{0,8},{1,9},{2,10},{3,11},{4,12},{5,13},{6,14},{7,15},{8,0},{9,1},... | collective-permute-start | bytes 417800 | tf_op jit(solution)/shard_map/ppermute | solution.py:80
  71.9 5.3 %collective-permute-start.20 = (bf16[16,2176]{1,0:T(8,128)(2,1)S(1)}, bf16[16,2176]{1,0:T(8,128)(2,1)S(1)}, u32[]{:S(2)}, u32[]{:S(2)}) collective-permute-start(bf16[16,2176]{1,0:T(8,128)(2,1)S(1)} %get-tuple-element.81), channel_id=1, source_target_pairs={{0,8},{1,9},{2,10},{3,11},{4,12},{5,13},{6,14},{7,15},{8,0},{9,1},... | collective-permute-start | bytes 208904 | tf_op jit(solution)/shard_map/ppermute | solution.py:80

commit v13 on v12

--- a/solution.py
+++ b/solution.py
@@ -8,10 +8,10 @@
 from jax.sharding import PartitionSpec as P
 
 PIECES = 4
-UNITS = ((0,), (1, 2), (3,))
-SPLIT = (2, 1, 1, 1)
-BESIDE = 6
-FAR = (0.1, 0.1, 1.0, 0.1)
+GROUPS = ((0,), (1, 2), (3,))
+SPLIT = (2, 2, 2, 1)
+BESIDE = (0, 2.3, 2.3, 6)
+FAR = (0.1, 1.5, 0.1, 1.5)
 
 
 def product(left, right):
@@ -294,7 +294,7 @@
     return [sends], keep
 
 
-def combine_kernel(layout, ordered, *refs):
+def combine_kernel(layout, ordered, carried, *refs):
     count = len(layout)
     keep_refs, refs = refs[:count], refs[count:]
     came = []
@@ -304,7 +304,11 @@
             came[-1].append([refs[position].at[first:last, :] for position in index])
     inputs = 1 + max(position for parts in layout for index, _, _ in parts for position in index)
     refs = refs[inputs + ordered :]
-    kept_refs, send_refs = refs[:count], refs[count:]
+    kept_refs, send_refs = refs[carried : carried + count], refs[carried + count :]
+    if carried:
+        above = refs[0].shape[0]
+        send_refs[0][:above, :] = refs[0][...]
+        send_refs = [send_refs[0].at[above:, :]]
     width = keep_refs[0].shape[2] - EXTRA
     for piece, (keep_ref, kept_ref) in enumerate(zip(keep_refs, kept_refs)):
         sums, energy = add_came(keep_ref, came[piece])
@@ -319,20 +323,21 @@
             store_coded([send_ref.at[rows, :]], [block for blocks in sums for block in blocks[first : first + kept]], energy)
 
 
-def combine(keeps, came, layout, sent, after, length):
+def combine(keeps, came, layout, sent, after, length, carry=()):
     _, height, width = keeps[0].shape
     kept = height // (sent + 1)
     count = len(keeps)
+    above = sum(array.shape[0] for array in carry)
     outs = pl.pallas_call(
-        functools.partial(combine_kernel, layout, len(after)),
+        functools.partial(combine_kernel, layout, len(after), len(carry)),
         out_shape=(jax.ShapeDtypeStruct((2, kept, width), jnp.float32),) * count
-        + (jax.ShapeDtypeStruct((2 * kept * count, width), jnp.bfloat16),) * sent,
-        in_specs=[WHOLE] * (count + len(came)) + [ANYWHERE] * len(after),
+        + (jax.ShapeDtypeStruct((2 * kept * count + above, width), jnp.bfloat16),) * sent,
+        in_specs=[WHOLE] * (count + len(came)) + [ANYWHERE] * len(after) + [WHOLE] * len(carry),
         out_specs=(WHOLE,) * (count + sent),
         compiler_params=limit(10),
         cost_estimate=cost(length),
         name="combine",
-    )(*keeps, *came, *after)
+    )(*keeps, *came, *after, *carry)
     return outs[count:], outs[:count]
 
 
@@ -370,14 +375,14 @@
         in_specs=[WHOLE] * len(keeps) + [ANYWHERE] * len(after),
         out_specs=WHOLE,
         compiler_params=limit(8),
-        cost_estimate=cost(BESIDE),
+        cost_estimate=cost(0.1),
         name="share",
     )(*keeps, *after)
 
 
 def finish_kernel(count, ready_ref, *refs):
     (gradient_ref, log_ref), refs = refs[-2:], refs[:-2]
-    later = UNITS[1:]
+    later = GROUPS[1:]
     came = []
     for ref, group in zip(refs[-len(later) :], later):
         came += [ref.at[16 * place : 16 * place + 16, :] for place in range(len(group))]
@@ -405,13 +410,6 @@
     )(ready, *keeps, *came)
 
 
-def second_sums(group, keep, came, sent, stages, after):
-    layout = joint_layout(len(group), len(sent), sent[0].shape[0] // len(group))
-    sends, keeps = combine([keep[piece] for piece in group], sent, layout, 1, after, 0.1)
-    keep = keep | dict(zip(group, keeps))
-    return keep, came + [swap(sends[0], "walk", stages[2][0])], [keeps[0]]
-
-
 def pieced_body(pieces, tile, inverse_rows, kinetic_rows, virt_values, virt_laplacians, local_energy):
     count = lax.axis_size("walk")
     stages = stage_masks(count)
@@ -431,41 +429,48 @@
     near, values, laplacians = near_product(virt, me, local_energy, inverse, kinetic, values, laplacians, mine[2:])
 
     second = partners(stages[1])
-    kept, first, keep, came = {}, {}, {}, []
-    unit, sent, last = 0, (), []
+    keep, came, carry, sent, last = {}, [], (), (), []
+
+    def second_sums(piece, carry, after, length):
+        layout = joint_layout(1, len(sent), sent[0].shape[0])
+        (send,), (keep[piece],) = combine([keep[piece]], sent, layout, 1, after, length, carry)
+        group = next(group for group in GROUPS if piece in group)
+        if piece < group[-1]:
+            return (send,), [keep[piece]]
+        held.append(send)
+        return (), [keep[piece]]
+
+    held = []
     for turn in range(pieces):
-        send, kept[turn] = far_product(
+        final = turn == pieces - 1
+        send, kept = far_product(
             virt, me, local_energy, theirs[turn], near, turn * rows, values, laplacians, tile, stages, SPLIT[turn], last, FAR[turn]
         )
         if turn + 2 < pieces:
-            part, kept[turn] = lax.optimization_barrier((mine[turn + 2], kept[turn]))
+            part, kept = lax.optimization_barrier((mine[turn + 2], kept))
             theirs.append(swap(part, "virt", 1))
-        first[turn] = [swap(part, "walk", stages[0][0]) for part in send[0]]
-        last = [kept[turn]]
-        if sent and turn < pieces - 1:
-            keep, came, last = second_sums(UNITS[unit - 1], keep, came, sent, stages, last)
-            sent = ()
-        group = UNITS[unit]
-        if turn == pieces - 1:
-            ready = share([keep[piece] for piece in UNITS[0]], last, count)
-            last = [ready]
-        if turn == pieces - 2:
-            early = UNITS[0]
-            layout = joint_layout(len(early), 1, came[0].shape[0] // len(early))
-            _, keeps = combine([keep[piece] for piece in early], came[:1], layout, 0, last, BESIDE)
-            keep, last = keep | dict(zip(early, keeps)), [keeps[0]]
-        if turn == group[-1]:
-            layout = first_layout(len(group), SPLIT[turn], first[turn][0].shape[0])
-            arrays = [part for piece in group for part in first[piece]]
-            sends, keeps = combine([kept[piece] for piece in group], arrays, layout, len(second), last, 0.1)
-            last = [keeps[0]]
-            if turn == pieces - 1 and sent:
-                keep, came, last = second_sums(UNITS[unit - 1], keep, came, sent, stages, last)
-            keep.update(zip(group, keeps))
-            sent = [swap(part, "walk", mask) for part, mask in reversed(list(zip(sends, second)))]
-            unit += 1
-    keep, came, last = second_sums(UNITS[-1], keep, came, sent, stages, last)
-    return finish(ready, [keep[piece] for unit in UNITS[1:] for piece in unit], came[1:], count)
+        if held and turn == pieces - 2:
+            held[0], kept = lax.optimization_barrier((held[0], kept))
+            came.append(swap(held.pop(), "walk", stages[2][0]))
+        first = [swap(part, "walk", stages[0][0]) for part in send[0]]
+        last = [kept]
+        if final:
+            layout = joint_layout(1, 1, came[0].shape[0])
+            _, (keep[0],) = combine([keep[0]], came[:1], layout, 0, last, BESIDE[turn])
+            last = [keep[0]]
+        elif turn:
+            carry, last = second_sums(turn - 1, carry, last, BESIDE[turn])
+        layout = first_layout(1, SPLIT[turn], first[0].shape[0])
+        sends, (keep[turn],) = combine([kept], first, layout, len(second), last, 0.1)
+        last = [keep[turn]]
+        if final:
+            carry, last = second_sums(turn - 1, carry, last, 0.1)
+            came.append(swap(held.pop(), "walk", stages[2][0]))
+        sent = [swap(part, "walk", mask) for part, mask in reversed(list(zip(sends, second)))]
+    second_sums(pieces - 1, (), last, 0.1)
+    came.append(swap(held.pop(), "walk", stages[2][0]))
+    ready = share([keep[piece] for piece in GROUPS[0]], last, count)
+    return finish(ready, [keep[piece] for group in GROUPS[1:] for piece in group], came[1:], count)
 
 
 def solution(mesh):

time: 78.4 us -> 77.8 us (level)
  waiting for transfers between devices: 22.6 us -> 20.4 us
  starting transfers between devices: 24.7 us -> 26.1 us
    ppermute x21 -> x26, waiting for transfers between devices: 22.6 us -> 20.4 us  [swap(): return lax.ppermute(array, axis, pairs)]
    ppermute x21 -> x26, starting transfers between devices: 24.7 us -> 26.1 us  [swap(): return lax.ppermute(array, axis, pairs)]
    pallas_call x7 -> x9, Pallas kernels: 4.12 us -> 4.27 us  [combine(): pl.pallas_call(functools.partial(combine_kernel, layout, len(after), len(...]
  transfers between devices with their start and end apart: 21 -> 26, of which waited for: 15 -> 11; matrix products, arithmetic and copies ran while one was open for 0% -> 0% of each run, Pallas kernels for 35% -> 35%
where the time goes in v13:
time: 77.8 us; the launch traced here: 77.6 us
  Pallas kernels  29.6 us (38%)
  starting transfers between devices  26.1 us (34%)
  waiting for transfers between devices  20.4 us (26%)
  between operations  1.49 us (2%)
    ppermute x26, starting transfers between devices, swap(): return lax.ppermute(array, axis, pairs)  26.1 us
    ppermute x26, waiting for transfers between devices, swap(): return lax.ppermute(array, axis, pairs)  20.4 us
    pallas_call x4, Pallas kernels, far_product(): pl.pallas_call(functools.partial(far_kernel, place_weights(stages), count...  11.4 us
    pallas_call x1, Pallas kernels, near_product(): pl.pallas_call(functools.partial(near_kernel, chunk, tile), out_shape=(ja...  10.3 us
    pallas_call x9, Pallas kernels, combine(): pl.pallas_call(functools.partial(combine_kernel, layout, len(after), len(...  4.27 us
    pallas_call x2, Pallas kernels, cut(): pl.pallas_call(cut_kernel, out_shape=(out, out), grid=(1,), in_specs=[blo...  2.55 us
  transfers between devices with their start and end apart: 26, of which 11 were waited for; matrix products, arithmetic and copies ran while one was open for 0% of the time, Pallas kernels for 35%

profile of v13, /device:TPU:0, one launch (start us, length us, event | category | flops | bytes accessed | tf_op | source)
XLA Modules:
  0.0 77.6 jit_solution(6664188850580442223)
XLA Ops:
  0.6 1.3 %cut.3 = (bf16[2,128,1024]{2,1,0:T(8,128)(2,1)S(1)}, bf16[2,128,1024]{2,1,0:T(8,128)(2,1)S(1)}) custom-call(bf16[16,32,1024]{2,1,0:T(8,128)(2,1)} %bitcast.6, bf16[16,32,1024]{2,1,0:T(8,128)(2,1)} %bitcast.9), custom_call_target="tpu_custom_call" | custom-call | flops 110000000 | tf_op jit(solution)/shard_map/cut/pallas_call | solution.py:166
  1.9 3.0 %collective-permute-start = (bf16[2,128,1024]{2,1,0:T(8,128)(2,1)S(1)}, bf16[2,128,1024]{2,1,0:T(8,128)(2,1)S(1)}, u32[]{:S(2)}, u32[]{:S(2)}) collective-permute-start(bf16[2,128,1024]{2,1,0:T(8,128)(2,1)S(1)} %get-tuple-element.51), channel_id=1, source_target_pairs={{0,16},{16,0},{1,17},{17,1},{2,18},{18,2},{3,19},{19,3},{4,20},{20... | collective-permute-start | bytes 1572872 | tf_op jit(solution)/shard_map/ppermute | solution.py:80
  5.0 1.3 %cut.2 = (bf16[2,128,1024]{2,1,0:T(8,128)(2,1)S(1)}, bf16[2,128,1024]{2,1,0:T(8,128)(2,1)S(1)}) custom-call(bf16[16,32,1024]{2,1,0:T(8,128)(2,1)} %bitcast.7, bf16[16,32,1024]{2,1,0:T(8,128)(2,1)} %bitcast.10), custom_call_target="tpu_custom_call" | custom-call | flops 110000000 | tf_op jit(solution)/shard_map/cut/pallas_call | solution.py:166
  6.9 10.3 %near_product.1 = (f32[2,16,32,2048]{3,2,1,0:T(8,128)S(1)}, bf16[1024,2048]{1,0:T(8,128)(2,1)S(1)}, bf16[1024,2048]{1,0:T(8,128)(2,1)S(1)}) custom-call(s32[1]{0:T(128)} %bitcast.2.virt_ref, s32[1]{0:T(128)} %bitcast.3.me_ref, f32[1]{0:T(128)S(6)} %copy.7.energy_ref, bf16[16,32,1024]{2,1,0:T(8,128)(2,1)} %bitcast.8, bf16[16,32,1024]{2,1,0:T(8,128)(2,1)} %bitcast.11, ...), custom_call_target="tpu_custom_call" | custom-call | flops 9900000256 | tf_op jit(solution)/shard_map/near_product/pallas_call | solution.py:232
  17.7 2.8 %far_product.4 = (bf16[64,2176]{1,0:T(8,128)(2,1)S(1)}, bf16[64,2176]{1,0:T(8,128)(2,1)S(1)}, f32[2,64,2176]{2,1,0:T(8,128)S(1)}) custom-call(s32[1]{0:T(128)} %bitcast.2.virt_ref, s32[1]{0:T(128)} %bitcast.3.me_ref, f32[1]{0:T(128)S(6)} %copy.7.energy_ref, bf16[2,128,1024]{2,1,0:T(8,128)(2,1)S(1)} %collective-permute-done.far_ref, ...), custom_call_target="tpu_custom_call" | custom-call | flops 110000000 | tf_op jit(solution)/shard_map/far_product/pallas_call | solution.py:283
  21.1 2.1 %collective-permute-start.7 = (bf16[2,128,1024]{2,1,0:T(8,128)(2,1)S(1)}, bf16[2,128,1024]{2,1,0:T(8,128)(2,1)S(1)}, u32[]{:S(2)}, u32[]{:S(2)}) collective-permute-start(bf16[2,128,1024]{2,1,0:T(8,128)(2,1)S(1)} %get-tuple-element.69.rest_0_), channel_id=1, source_target_pairs={{0,16},{16,0},{1,17},{17,1},{2,18},{18,2},{3,19},{19,3},{4,20},{20... | collective-permute-start | bytes 1572872 | tf_op jit(solution)/shard_map/ppermute | solution.py:80
  23.1 0.7 combine.9
  23.8 2.6 %collective-permute-start.3 = (bf16[32,2176]{1,0:T(8,128)(2,1)S(1)}, bf16[32,2176]{1,0:T(8,128)(2,1)S(1)}, u32[]{:S(2)}, u32[]{:S(2)}) collective-permute-start(bf16[32,2176]{1,0:T(8,128)(2,1)S(1)} %get-tuple-element.61), channel_id=1, source_target_pairs={{0,6},{1,7},{2,4},{3,5},{4,2},{5,3},{6,0},{7,1},{8,14},{9,15},{10,... | collective-permute-start | bytes 417800 | tf_op jit(solution)/shard_map/ppermute | solution.py:80
  27.4 1.5 %collective-permute-done.6.far_ref = bf16[2,128,1024]{2,1,0:T(8,128)(2,1)S(1)} collective-permute-done((bf16[2,128,1024]{2,1,0:T(8,128)(2,1)S(1)}, bf16[2,128,1024]{2,1,0:T(8,128)(2,1)S(1)}, u32[]{:S(2)}, u32[]{:S(2)}) %collective-permute-start.6) | collective-permute-done | bytes 524320 | tf_op jit(solution)/shard_map/ppermute | solution.py:80
  28.9 2.8 %far_product.5 = (bf16[64,2176]{1,0:T(8,128)(2,1)S(1)}, bf16[64,2176]{1,0:T(8,128)(2,1)S(1)}, f32[2,64,2176]{2,1,0:T(8,128)S(1)}) custom-call(s32[1]{0:T(128)} %bitcast.2.virt_ref, s32[1]{0:T(128)} %bitcast.3.me_ref, f32[1]{0:T(128)S(6)} %copy.7.energy_ref, bf16[2,128,1024]{2,1,0:T(8,128)(2,1)S(1)} %collective-permute-done.6.far_ref, ...), custom_call_target="tpu_custom_call" | custom-call | flops 1650000000 | tf_op jit(solution)/shard_map/far_product/pallas_call | solution.py:283
  32.3 1.0 %collective-permute-done.4.refs_2_ = bf16[32,2176]{1,0:T(8,128)(2,1)S(1)} collective-permute-done((bf16[32,2176]{1,0:T(8,128)(2,1)S(1)}, bf16[32,2176]{1,0:T(8,128)(2,1)S(1)}, u32[]{:S(2)}, u32[]{:S(2)}) %collective-permute-start.4) | collective-permute-done | bytes 139296 | tf_op jit(solution)/shard_map/ppermute | solution.py:80
  33.3 1.7 %collective-permute-start.11 = (bf16[2,128,1024]{2,1,0:T(8,128)(2,1)S(1)}, bf16[2,128,1024]{2,1,0:T(8,128)(2,1)S(1)}, u32[]{:S(2)}, u32[]{:S(2)}) collective-permute-start(bf16[2,128,1024]{2,1,0:T(8,128)(2,1)S(1)} %get-tuple-element.75.rest_1_), channel_id=1, source_target_pairs={{0,16},{16,0},{1,17},{17,1},{2,18},{18,2},{3,19},{19,3},{4,20},{20... | collective-permute-start | bytes 1572872 | tf_op jit(solution)/shard_map/ppermute | solution.py:80
  35.3 0.7 combine.11
  36.0 2.0 %collective-permute-start.14 = (bf16[32,2176]{1,0:T(8,128)(2,1)S(1)}, bf16[32,2176]{1,0:T(8,128)(2,1)S(1)}, u32[]{:S(2)}, u32[]{:S(2)}) collective-permute-start(bf16[32,2176]{1,0:T(8,128)(2,1)S(1)} %get-tuple-element.79), channel_id=1, source_target_pairs={{0,6},{1,7},{2,4},{3,5},{4,2},{5,3},{6,0},{7,1},{8,14},{9,15},{10,... | collective-permute-start | bytes 417800 | tf_op jit(solution)/shard_map/ppermute | solution.py:80
  38.0 1.1 %collective-permute-start.15 = (bf16[32,2176]{1,0:T(8,128)(2,1)S(1)}, bf16[32,2176]{1,0:T(8,128)(2,1)S(1)}, u32[]{:S(2)}, u32[]{:S(2)}) collective-permute-start(bf16[32,2176]{1,0:T(8,128)(2,1)S(1)} %get-tuple-element.80), channel_id=1, source_target_pairs={{0,2},{1,3},{2,0},{3,1},{4,6},{5,7},{6,4},{7,5},{8,10},{9,11},{10,... | collective-permute-start | bytes 417800 | tf_op jit(solution)/shard_map/ppermute | solution.py:80
  40.2 2.8 %far_product.6 = (bf16[64,2176]{1,0:T(8,128)(2,1)S(1)}, bf16[64,2176]{1,0:T(8,128)(2,1)S(1)}, f32[2,64,2176]{2,1,0:T(8,128)S(1)}) custom-call(s32[1]{0:T(128)} %bitcast.2.virt_ref, s32[1]{0:T(128)} %bitcast.3.me_ref, f32[1]{0:T(128)S(6)} %copy.7.energy_ref, bf16[2,128,1024]{2,1,0:T(8,128)(2,1)S(1)} %collective-permute-done.7.far_ref, ...), custom_call_target="tpu_custom_call" | custom-call | flops 110000000 | tf_op jit(solution)/shard_map/far_product/pallas_call | solution.py:283
  43.6 1.7 %collective-permute-done.15.refs_2_ = bf16[32,2176]{1,0:T(8,128)(2,1)S(1)} collective-permute-done((bf16[32,2176]{1,0:T(8,128)(2,1)S(1)}, bf16[32,2176]{1,0:T(8,128)(2,1)S(1)}, u32[]{:S(2)}, u32[]{:S(2)}) %collective-permute-start.15) | collective-permute-done | bytes 139296 | tf_op jit(solution)/shard_map/ppermute | solution.py:80
  45.3 2.6 %collective-permute-start.10 = (bf16[16,2176]{1,0:T(8,128)(2,1)S(1)}, bf16[16,2176]{1,0:T(8,128)(2,1)S(1)}, u32[]{:S(2)}, u32[]{:S(2)}) collective-permute-start(bf16[16,2176]{1,0:T(8,128)(2,1)S(1)} %get-tuple-element.74), channel_id=1, source_target_pairs={{0,8},{1,9},{2,10},{3,11},{4,12},{5,13},{6,14},{7,15},{8,0},{9,1},... | collective-permute-start | bytes 208904 | tf_op jit(solution)/shard_map/ppermute | solution.py:80
  48.3 0.7 combine.13
  49.0 1.8 %collective-permute-start.17 = (bf16[32,2176]{1,0:T(8,128)(2,1)S(1)}, bf16[32,2176]{1,0:T(8,128)(2,1)S(1)}, u32[]{:S(2)}, u32[]{:S(2)}) collective-permute-start(bf16[32,2176]{1,0:T(8,128)(2,1)S(1)} %get-tuple-element.85), channel_id=1, source_target_pairs={{0,6},{1,7},{2,4},{3,5},{4,2},{5,3},{6,0},{7,1},{8,14},{9,15},{10,... | collective-permute-start | bytes 417800 | tf_op jit(solution)/shard_map/ppermute | solution.py:80
  50.8 1.3 %collective-permute-start.18 = (bf16[32,2176]{1,0:T(8,128)(2,1)S(1)}, bf16[32,2176]{1,0:T(8,128)(2,1)S(1)}, u32[]{:S(2)}, u32[]{:S(2)}) collective-permute-start(bf16[32,2176]{1,0:T(8,128)(2,1)S(1)} %get-tuple-element.86), channel_id=1, source_target_pairs={{0,2},{1,3},{2,0},{3,1},{4,6},{5,7},{6,4},{7,5},{8,10},{9,11},{10,... | collective-permute-start | bytes 417800 | tf_op jit(solution)/shard_map/ppermute | solution.py:80
  52.5 3.0 %far_product.7 = (bf16[128,2176]{1,0:T(8,128)(2,1)S(1)}, f32[2,64,2176]{2,1,0:T(8,128)S(1)}) custom-call(s32[1]{0:T(128)} %bitcast.2.virt_ref, s32[1]{0:T(128)} %bitcast.3.me_ref, f32[1]{0:T(128)S(6)} %copy.7.energy_ref, bf16[2,128,1024]{2,1,0:T(8,128)(2,1)S(1)} %collective-permute-done.11.far_ref, f32[2,16,32,2048]{3,2,1,0:T(8,128)S(1)} %get-tuple-element.53.near_ref, ...), custom_call_target="tpu_custom_call" | custom-call | flops 1650000000 | tf_op jit(solution)/shard_map/far_product/pallas_call | solution.py:283
  55.7 1.8 %collective-permute-done.20.refs_1_ = bf16[128,2176]{1,0:T(8,128)(2,1)S(1)} collective-permute-done((bf16[128,2176]{1,0:T(8,128)(2,1)S(1)}, bf16[128,2176]{1,0:T(8,128)(2,1)S(1)}, u32[]{:S(2)}, u32[]{:S(2)}) %collective-permute-start.20) | collective-permute-done | bytes 557088 | tf_op jit(solution)/shard_map/ppermute | solution.py:80
  57.5 0.7 combine.15
  58.2 1.8 %collective-permute-start.21 = (bf16[32,2176]{1,0:T(8,128)(2,1)S(1)}, bf16[32,2176]{1,0:T(8,128)(2,1)S(1)}, u32[]{:S(2)}, u32[]{:S(2)}) collective-permute-start(bf16[32,2176]{1,0:T(8,128)(2,1)S(1)} %get-tuple-element.92), channel_id=1, source_target_pairs={{0,6},{1,7},{2,4},{3,5},{4,2},{5,3},{6,0},{7,1},{8,14},{9,15},{10,... | collective-permute-start | bytes 417800 | tf_op jit(solution)/shard_map/ppermute | solution.py:80
  60.1 1.3 %collective-permute-start.22 = (bf16[32,2176]{1,0:T(8,128)(2,1)S(1)}, bf16[32,2176]{1,0:T(8,128)(2,1)S(1)}, u32[]{:S(2)}, u32[]{:S(2)}) collective-permute-start(bf16[32,2176]{1,0:T(8,128)(2,1)S(1)} %get-tuple-element.93), channel_id=1, source_target_pairs={{0,2},{1,3},{2,0},{3,1},{4,6},{5,7},{6,4},{7,5},{8,10},{9,11},{10,... | collective-permute-start | bytes 417800 | tf_op jit(solution)/shard_map/ppermute | solution.py:80
  62.2 0.9 %collective-permute-start.24 = (bf16[32,2176]{1,0:T(8,128)(2,1)S(1)}, bf16[32,2176]{1,0:T(8,128)(2,1)S(1)}, u32[]{:S(2)}, u32[]{:S(2)}) collective-permute-start(bf16[32,2176]{1,0:T(8,128)(2,1)S(1)} %get-tuple-element.96), channel_id=1, source_target_pairs={{0,8},{1,9},{2,10},{3,11},{4,12},{5,13},{6,14},{7,15},{8,0},{9,1},... | collective-permute-start | bytes 417800 | tf_op jit(solution)/shard_map/ppermute | solution.py:80
  63.1 2.7 %collective-permute-done.21.refs_1_ = bf16[32,2176]{1,0:T(8,128)(2,1)S(1)} collective-permute-done((bf16[32,2176]{1,0:T(8,128)(2,1)S(1)}, bf16[32,2176]{1,0:T(8,128)(2,1)S(1)}, u32[]{:S(2)}, u32[]{:S(2)}) %collective-permute-start.21) | collective-permute-done | bytes 139296 | tf_op jit(solution)/shard_map/ppermute | solution.py:80
  65.7 2.2 %collective-permute-done.22.refs_2_ = bf16[32,2176]{1,0:T(8,128)(2,1)S(1)} collective-permute-done((bf16[32,2176]{1,0:T(8,128)(2,1)S(1)}, bf16[32,2176]{1,0:T(8,128)(2,1)S(1)}, u32[]{:S(2)}, u32[]{:S(2)}) %collective-permute-start.22) | collective-permute-done | bytes 139296 | tf_op jit(solution)/shard_map/ppermute | solution.py:80
  67.9 3.1 %collective-permute-done.23.refs_3_ = bf16[32,2176]{1,0:T(8,128)(2,1)S(1)} collective-permute-done((bf16[32,2176]{1,0:T(8,128)(2,1)S(1)}, bf16[32,2176]{1,0:T(8,128)(2,1)S(1)}, u32[]{:S(2)}, u32[]{:S(2)}) %collective-permute-start.23) | collective-permute-done | bytes 139296 | tf_op jit(solution)/shard_map/ppermute | solution.py:80
  71.5 5.1 %collective-permute-done.25.refs_4_ = bf16[16,2176]{1,0:T(8,128)(2,1)S(1)} collective-permute-done((bf16[16,2176]{1,0:T(8,128)(2,1)S(1)}, bf16[16,2176]{1,0:T(8,128)(2,1)S(1)}, u32[]{:S(2)}, u32[]{:S(2)}) %collective-permute-start.25) | collective-permute-done | bytes 69664 | tf_op jit(solution)/shard_map/ppermute | solution.py:80
  76.6 1.0 %finish.1 = (f32[32,2048]{1,0:T(8,128)}, f32[32,2048]{1,0:T(8,128)}) custom-call(f32[2,8,2048]{2,1,0:T(8,128)S(1)} %share.1.ready_ref, f32[2,8,2176]{2,1,0:T(8,128)S(1)} %get-tuple-element.82.refs_3_.refs_0_, f32[2,8,2176]{2,1,0:T(8,128)S(1)} %get-tuple-element.91.refs_1_.refs_4_, f32[2,8,2176]{2,1,0:T(8,128)S(1)} %get-tuple-element.95.refs_2_, ...), custom_call_target="tpu_custom_call" | custom-call | flops 110000000 | tf_op jit(solution)/shard_map/finish/pallas_call | solution.py:402
  (38 shorter events, 6.9 us)
Async XLA Ops:
  1.9 15.8 %collective-permute-start = (bf16[2,128,1024]{2,1,0:T(8,128)(2,1)S(1)}, bf16[2,128,1024]{2,1,0:T(8,128)(2,1)S(1)}, u32[]{:S(2)}, u32[]{:S(2)}) collective-permute-start(bf16[2,128,1024]{2,1,0:T(8,128)(2,1)S(1)} %get-tuple-element.51), channel_id=1, source_target_pairs={{0,16},{16,0},{1,17},{17,1},{2,18},{18,2},{3,19},{19,3},{4,20},{20... | collective-permute-start | bytes 1572872 | tf_op jit(solution)/shard_map/ppermute | solution.py:80
  4.9 24.0 %collective-permute-start.6 = (bf16[2,128,1024]{2,1,0:T(8,128)(2,1)S(1)}, bf16[2,128,1024]{2,1,0:T(8,128)(2,1)S(1)}, u32[]{:S(2)}, u32[]{:S(2)}) collective-permute-start(bf16[2,128,1024]{2,1,0:T(8,128)(2,1)S(1)} %get-tuple-element.64), channel_id=1, source_target_pairs={{0,16},{16,0},{1,17},{17,1},{2,18},{18,2},{3,19},{19,3},{4,20},{20... | collective-permute-start | bytes 1572872 | tf_op jit(solution)/shard_map/ppermute | solution.py:80
  20.5 2.6 %collective-permute-start.1 = (bf16[64,2176]{1,0:T(8,128)(2,1)S(1)}, bf16[64,2176]{1,0:T(8,128)(2,1)S(1)}, u32[]{:S(2)}, u32[]{:S(2)}) collective-permute-start(bf16[64,2176]{1,0:T(8,128)(2,1)S(1)} %get-tuple-element.58), channel_id=1, source_target_pairs={{0,1},{1,0},{2,3},{3,2},{4,5},{5,4},{6,7},{7,6},{8,9},{9,8},{10,11... | collective-permute-start | bytes 835592 | tf_op jit(solution)/shard_map/ppermute | solution.py:80
  20.6 2.6 %collective-permute-start.2 = (bf16[64,2176]{1,0:T(8,128)(2,1)S(1)}, bf16[64,2176]{1,0:T(8,128)(2,1)S(1)}, u32[]{:S(2)}, u32[]{:S(2)}) collective-permute-start(bf16[64,2176]{1,0:T(8,128)(2,1)S(1)} %get-tuple-element.59), channel_id=1, source_target_pairs={{0,1},{1,0},{2,3},{3,2},{4,5},{5,4},{6,7},{7,6},{8,9},{9,8},{10,11... | collective-permute-start | bytes 835592 | tf_op jit(solution)/shard_map/ppermute | solution.py:80
  21.1 19.1 %collective-permute-start.7 = (bf16[2,128,1024]{2,1,0:T(8,128)(2,1)S(1)}, bf16[2,128,1024]{2,1,0:T(8,128)(2,1)S(1)}, u32[]{:S(2)}, u32[]{:S(2)}) collective-permute-start(bf16[2,128,1024]{2,1,0:T(8,128)(2,1)S(1)} %get-tuple-element.69.rest_0_), channel_id=1, source_target_pairs={{0,16},{16,0},{1,17},{17,1},{2,18},{18,2},{3,19},{19,3},{4,20},{20... | collective-permute-start | bytes 1572872 | tf_op jit(solution)/shard_map/ppermute | solution.py:80
  23.8 8.0 %collective-permute-start.3 = (bf16[32,2176]{1,0:T(8,128)(2,1)S(1)}, bf16[32,2176]{1,0:T(8,128)(2,1)S(1)}, u32[]{:S(2)}, u32[]{:S(2)}) collective-permute-start(bf16[32,2176]{1,0:T(8,128)(2,1)S(1)} %get-tuple-element.61), channel_id=1, source_target_pairs={{0,6},{1,7},{2,4},{3,5},{4,2},{5,3},{6,0},{7,1},{8,14},{9,15},{10,... | collective-permute-start | bytes 417800 | tf_op jit(solution)/shard_map/ppermute | solution.py:80
  26.4 6.9 %collective-permute-start.4 = (bf16[32,2176]{1,0:T(8,128)(2,1)S(1)}, bf16[32,2176]{1,0:T(8,128)(2,1)S(1)}, u32[]{:S(2)}, u32[]{:S(2)}) collective-permute-start(bf16[32,2176]{1,0:T(8,128)(2,1)S(1)} %get-tuple-element.62), channel_id=1, source_target_pairs={{0,2},{1,3},{2,0},{3,1},{4,6},{5,7},{6,4},{7,5},{8,10},{9,11},{10,... | collective-permute-start | bytes 417800 | tf_op jit(solution)/shard_map/ppermute | solution.py:80
  27.0 8.0 %collective-permute-start.5 = (bf16[32,2176]{1,0:T(8,128)(2,1)S(1)}, bf16[32,2176]{1,0:T(8,128)(2,1)S(1)}, u32[]{:S(2)}, u32[]{:S(2)}) collective-permute-start(bf16[32,2176]{1,0:T(8,128)(2,1)S(1)} %get-tuple-element.63), channel_id=1, source_target_pairs={{0,4},{1,5},{2,6},{3,7},{4,0},{5,1},{6,2},{7,3},{8,12},{9,13},{10,... | collective-permute-start | bytes 417800 | tf_op jit(solution)/shard_map/ppermute | solution.py:80
  31.7 3.6 %collective-permute-start.8 = (bf16[64,2176]{1,0:T(8,128)(2,1)S(1)}, bf16[64,2176]{1,0:T(8,128)(2,1)S(1)}, u32[]{:S(2)}, u32[]{:S(2)}) collective-permute-start(bf16[64,2176]{1,0:T(8,128)(2,1)S(1)} %get-tuple-element.70), channel_id=1, source_target_pairs={{0,1},{1,0},{2,3},{3,2},{4,5},{5,4},{6,7},{7,6},{8,9},{9,8},{10,11... | collective-permute-start | bytes 835592 | tf_op jit(solution)/shard_map/ppermute | solution.py:80
  31.8 3.5 %collective-permute-start.9 = (bf16[64,2176]{1,0:T(8,128)(2,1)S(1)}, bf16[64,2176]{1,0:T(8,128)(2,1)S(1)}, u32[]{:S(2)}, u32[]{:S(2)}) collective-permute-start(bf16[64,2176]{1,0:T(8,128)(2,1)S(1)} %get-tuple-element.71), channel_id=1, source_target_pairs={{0,1},{1,0},{2,3},{3,2},{4,5},{5,4},{6,7},{7,6},{8,9},{9,8},{10,11... | collective-permute-start | bytes 835592 | tf_op jit(solution)/shard_map/ppermute | solution.py:80
  33.3 19.2 %collective-permute-start.11 = (bf16[2,128,1024]{2,1,0:T(8,128)(2,1)S(1)}, bf16[2,128,1024]{2,1,0:T(8,128)(2,1)S(1)}, u32[]{:S(2)}, u32[]{:S(2)}) collective-permute-start(bf16[2,128,1024]{2,1,0:T(8,128)(2,1)S(1)} %get-tuple-element.75.rest_1_), channel_id=1, source_target_pairs={{0,16},{16,0},{1,17},{17,1},{2,18},{18,2},{3,19},{19,3},{4,20},{20... | collective-permute-start | bytes 1572872 | tf_op jit(solution)/shard_map/ppermute | solution.py:80
  36.0 7.3 %collective-permute-start.14 = (bf16[32,2176]{1,0:T(8,128)(2,1)S(1)}, bf16[32,2176]{1,0:T(8,128)(2,1)S(1)}, u32[]{:S(2)}, u32[]{:S(2)}) collective-permute-start(bf16[32,2176]{1,0:T(8,128)(2,1)S(1)} %get-tuple-element.79), channel_id=1, source_target_pairs={{0,6},{1,7},{2,4},{3,5},{4,2},{5,3},{6,0},{7,1},{8,14},{9,15},{10,... | collective-permute-start | bytes 417800 | tf_op jit(solution)/shard_map/ppermute | solution.py:80
  38.0 7.3 %collective-permute-start.15 = (bf16[32,2176]{1,0:T(8,128)(2,1)S(1)}, bf16[32,2176]{1,0:T(8,128)(2,1)S(1)}, u32[]{:S(2)}, u32[]{:S(2)}) collective-permute-start(bf16[32,2176]{1,0:T(8,128)(2,1)S(1)} %get-tuple-element.80), channel_id=1, source_target_pairs={{0,2},{1,3},{2,0},{3,1},{4,6},{5,7},{6,4},{7,5},{8,10},{9,11},{10,... | collective-permute-start | bytes 417800 | tf_op jit(solution)/shard_map/ppermute | solution.py:80
  39.1 8.7 %collective-permute-start.16 = (bf16[32,2176]{1,0:T(8,128)(2,1)S(1)}, bf16[32,2176]{1,0:T(8,128)(2,1)S(1)}, u32[]{:S(2)}, u32[]{:S(2)}) collective-permute-start(bf16[32,2176]{1,0:T(8,128)(2,1)S(1)} %get-tuple-element.81), channel_id=1, source_target_pairs={{0,4},{1,5},{2,6},{3,7},{4,0},{5,1},{6,2},{7,3},{8,12},{9,13},{10,... | collective-permute-start | bytes 417800 | tf_op jit(solution)/shard_map/ppermute | solution.py:80
  43.0 5.3 %collective-permute-start.12 = (bf16[64,2176]{1,0:T(8,128)(2,1)S(1)}, bf16[64,2176]{1,0:T(8,128)(2,1)S(1)}, u32[]{:S(2)}, u32[]{:S(2)}) collective-permute-start(bf16[64,2176]{1,0:T(8,128)(2,1)S(1)} %get-tuple-element.77), channel_id=1, source_target_pairs={{0,1},{1,0},{2,3},{3,2},{4,5},{5,4},{6,7},{7,6},{8,9},{9,8},{10,11... | collective-permute-start | bytes 835592 | tf_op jit(solution)/shard_map/ppermute | solution.py:80
  43.3 4.9 %collective-permute-start.13 = (bf16[64,2176]{1,0:T(8,128)(2,1)S(1)}, bf16[64,2176]{1,0:T(8,128)(2,1)S(1)}, u32[]{:S(2)}, u32[]{:S(2)}) collective-permute-start(bf16[64,2176]{1,0:T(8,128)(2,1)S(1)} %get-tuple-element.78), channel_id=1, source_target_pairs={{0,1},{1,0},{2,3},{3,2},{4,5},{5,4},{6,7},{7,6},{8,9},{9,8},{10,11... | collective-permute-start | bytes 835592 | tf_op jit(solution)/shard_map/ppermute | solution.py:80
  45.3 10.3 %collective-permute-start.10 = (bf16[16,2176]{1,0:T(8,128)(2,1)S(1)}, bf16[16,2176]{1,0:T(8,128)(2,1)S(1)}, u32[]{:S(2)}, u32[]{:S(2)}) collective-permute-start(bf16[16,2176]{1,0:T(8,128)(2,1)S(1)} %get-tuple-element.74), channel_id=1, source_target_pairs={{0,8},{1,9},{2,10},{3,11},{4,12},{5,13},{6,14},{7,15},{8,0},{9,1},... | collective-permute-start | bytes 208904 | tf_op jit(solution)/shard_map/ppermute | solution.py:80
  49.0 12.4 %collective-permute-start.17 = (bf16[32,2176]{1,0:T(8,128)(2,1)S(1)}, bf16[32,2176]{1,0:T(8,128)(2,1)S(1)}, u32[]{:S(2)}, u32[]{:S(2)}) collective-permute-start(bf16[32,2176]{1,0:T(8,128)(2,1)S(1)} %get-tuple-element.85), channel_id=1, source_target_pairs={{0,6},{1,7},{2,4},{3,5},{4,2},{5,3},{6,0},{7,1},{8,14},{9,15},{10,... | collective-permute-start | bytes 417800 | tf_op jit(solution)/shard_map/ppermute | solution.py:80
  50.8 11.0 %collective-permute-start.18 = (bf16[32,2176]{1,0:T(8,128)(2,1)S(1)}, bf16[32,2176]{1,0:T(8,128)(2,1)S(1)}, u32[]{:S(2)}, u32[]{:S(2)}) collective-permute-start(bf16[32,2176]{1,0:T(8,128)(2,1)S(1)} %get-tuple-element.86), channel_id=1, source_target_pairs={{0,2},{1,3},{2,0},{3,1},{4,6},{5,7},{6,4},{7,5},{8,10},{9,11},{10,... | collective-permute-start | bytes 417800 | tf_op jit(solution)/shard_map/ppermute | solution.py:80
  52.1 9.7 %collective-permute-start.19 = (bf16[32,2176]{1,0:T(8,128)(2,1)S(1)}, bf16[32,2176]{1,0:T(8,128)(2,1)S(1)}, u32[]{:S(2)}, u32[]{:S(2)}) collective-permute-start(bf16[32,2176]{1,0:T(8,128)(2,1)S(1)} %get-tuple-element.87), channel_id=1, source_target_pairs={{0,4},{1,5},{2,6},{3,7},{4,0},{5,1},{6,2},{7,3},{8,12},{9,13},{10,... | collective-permute-start | bytes 417800 | tf_op jit(solution)/shard_map/ppermute | solution.py:80
  55.5 2.0 %collective-permute-start.20 = (bf16[128,2176]{1,0:T(8,128)(2,1)S(1)}, bf16[128,2176]{1,0:T(8,128)(2,1)S(1)}, u32[]{:S(2)}, u32[]{:S(2)}) collective-permute-start(bf16[128,2176]{1,0:T(8,128)(2,1)S(1)} %get-tuple-element.88), channel_id=1, source_target_pairs={{0,1},{1,0},{2,3},{3,2},{4,5},{5,4},{6,7},{7,6},{8,9},{9,8},{10,11... | collective-permute-start | bytes 1671176 | tf_op jit(solution)/shard_map/ppermute | solution.py:80
  58.2 7.5 %collective-permute-start.21 = (bf16[32,2176]{1,0:T(8,128)(2,1)S(1)}, bf16[32,2176]{1,0:T(8,128)(2,1)S(1)}, u32[]{:S(2)}, u32[]{:S(2)}) collective-permute-start(bf16[32,2176]{1,0:T(8,128)(2,1)S(1)} %get-tuple-element.92), channel_id=1, source_target_pairs={{0,6},{1,7},{2,4},{3,5},{4,2},{5,3},{6,0},{7,1},{8,14},{9,15},{10,... | collective-permute-start | bytes 417800 | tf_op jit(solution)/shard_map/ppermute | solution.py:80
  60.1 7.9 %collective-permute-start.22 = (bf16[32,2176]{1,0:T(8,128)(2,1)S(1)}, bf16[32,2176]{1,0:T(8,128)(2,1)S(1)}, u32[]{:S(2)}, u32[]{:S(2)}) collective-permute-start(bf16[32,2176]{1,0:T(8,128)(2,1)S(1)} %get-tuple-element.93), channel_id=1, source_target_pairs={{0,2},{1,3},{2,0},{3,1},{4,6},{5,7},{6,4},{7,5},{8,10},{9,11},{10,... | collective-permute-start | bytes 417800 | tf_op jit(solution)/shard_map/ppermute | solution.py:80
  61.4 9.6 %collective-permute-start.23 = (bf16[32,2176]{1,0:T(8,128)(2,1)S(1)}, bf16[32,2176]{1,0:T(8,128)(2,1)S(1)}, u32[]{:S(2)}, u32[]{:S(2)}) collective-permute-start(bf16[32,2176]{1,0:T(8,128)(2,1)S(1)} %get-tuple-element.94), channel_id=1, source_target_pairs={{0,4},{1,5},{2,6},{3,7},{4,0},{5,1},{6,2},{7,3},{8,12},{9,13},{10,... | collective-permute-start | bytes 417800 | tf_op jit(solution)/shard_map/ppermute | solution.py:80
  62.2 9.3 %collective-permute-start.24 = (bf16[32,2176]{1,0:T(8,128)(2,1)S(1)}, bf16[32,2176]{1,0:T(8,128)(2,1)S(1)}, u32[]{:S(2)}, u32[]{:S(2)}) collective-permute-start(bf16[32,2176]{1,0:T(8,128)(2,1)S(1)} %get-tuple-element.96), channel_id=1, source_target_pairs={{0,8},{1,9},{2,10},{3,11},{4,12},{5,13},{6,14},{7,15},{8,0},{9,1},... | collective-permute-start | bytes 417800 | tf_op jit(solution)/shard_map/ppermute | solution.py:80
  71.3 5.3 %collective-permute-start.25 = (bf16[16,2176]{1,0:T(8,128)(2,1)S(1)}, bf16[16,2176]{1,0:T(8,128)(2,1)S(1)}, u32[]{:S(2)}, u32[]{:S(2)}) collective-permute-start(bf16[16,2176]{1,0:T(8,128)(2,1)S(1)} %get-tuple-element.97), channel_id=1, source_target_pairs={{0,8},{1,9},{2,10},{3,11},{4,12},{5,13},{6,14},{7,15},{8,0},{9,1},... | collective-permute-start | bytes 208904 | tf_op jit(solution)/shard_map/ppermute | solution.py:80

commit v14 on v13

--- a/solution.py
+++ b/solution.py
@@ -9,9 +9,9 @@
 
 PIECES = 4
 GROUPS = ((0,), (1, 2), (3,))
-SPLIT = (2, 2, 2, 1)
-BESIDE = (0, 2.3, 2.3, 6)
-FAR = (0.1, 1.5, 0.1, 1.5)
+SPLIT = (2, 2, 1, 1)
+BESIDE = (0, 2.3, 6, 6)
+FAR = (0.1, 1.5, 1.5, 1.5)
 
 
 def product(left, right):
@@ -242,7 +242,7 @@
 
 
 def far_kernel(weights, count, tile, first, split, virt_ref, me_ref, energy_ref, far_ref, near_ref, values_ref, laps_ref, *rest):
-    send_refs, (keep_ref, place_ref) = rest[-split - 2 : -2], rest[-2:]
+    send_refs, place_ref = rest[-split - 1 : -1], rest[-1]
     _, height, depth = far_ref.shape
     width = near_ref.shape[3]
     rows = height // count
@@ -269,9 +269,8 @@
             place_ref[1, target, columns] = log[source]
 
     energy = jnp.full((8, EXTRA), energy_ref[0], f32)
-    keep_ref[:, :, :width] = place_ref[:, :half]
-    keep_ref[0, :8, width:] = energy
-    blocks = [place_ref[array, row : row + 8, :] for array in range(2) for row in range(half, height, 8)]
+    place_ref[0, :8, width:] = energy
+    blocks = [place_ref[array, row : row + 8, :width] for array in range(2) for row in range(half, height, 8)]
     store_coded(send_refs, blocks, energy)
 
 
@@ -283,10 +282,9 @@
     *sends, keep = pl.pallas_call(
         functools.partial(far_kernel, place_weights(stages), count, tile, first, split),
         out_shape=(jax.ShapeDtypeStruct((2 * half // split, width + EXTRA), jnp.bfloat16),) * split
-        + (jax.ShapeDtypeStruct((2, half, width + EXTRA), jnp.float32),),
+        + (jax.ShapeDtypeStruct((2, height, width + EXTRA), jnp.float32),),
         in_specs=[SCALAR, SCALAR, SCALAR, WHOLE, WHOLE, WHOLE, WHOLE] + [ANYWHERE] * len(after),
         out_specs=(WHOLE,) * (split + 1),
-        scratch_shapes=[pltpu.VMEM((2, height, width), jnp.float32)],
         compiler_params=limit(24),
         cost_estimate=cost(length),
         name="far_product",
@@ -294,9 +292,9 @@
     return [sends], keep
 
 
-def combine_kernel(layout, ordered, carried, *refs):
+def combine_kernel(layout, ordered, carried, height, *refs):
     count = len(layout)
-    keep_refs, refs = refs[:count], refs[count:]
+    keep_refs, refs = [ref.at[:, :height] for ref in refs[:count]], refs[count:]
     came = []
     for parts in layout:
         came.append([])
@@ -323,13 +321,14 @@
             store_coded([send_ref.at[rows, :]], [block for blocks in sums for block in blocks[first : first + kept]], energy)
 
 
-def combine(keeps, came, layout, sent, after, length, carry=()):
+def combine(keeps, came, layout, sent, after, length, carry=(), part=1):
     _, height, width = keeps[0].shape
+    height = height // part
     kept = height // (sent + 1)
     count = len(keeps)
     above = sum(array.shape[0] for array in carry)
     outs = pl.pallas_call(
-        functools.partial(combine_kernel, layout, len(after), len(carry)),
+        functools.partial(combine_kernel, layout, len(after), len(carry), height),
         out_shape=(jax.ShapeDtypeStruct((2, kept, width), jnp.float32),) * count
         + (jax.ShapeDtypeStruct((2 * kept * count + above, width), jnp.bfloat16),) * sent,
         in_specs=[WHOLE] * (count + len(came)) + [ANYWHERE] * len(after) + [WHOLE] * len(carry),
@@ -358,56 +357,59 @@
     return [block / count - correction * mean for block, mean in zip(gradient, log)], log
 
 
-def share_kernel(count, ordered, *refs):
-    out_ref, row = refs[-1], 0
-    for keep_ref in refs[: -1 - ordered]:
-        for gradient, log in zip(*outputs_of(keep_ref, [], count)):
-            out_ref[0, row : row + 8, :] = gradient
-            out_ref[1, row : row + 8, :] = log
+def share_kernel(count, *refs):
+    (gradient_ref, log_ref), refs = refs[-2:], refs[:-2]
+    early = GROUPS[1:-1]
+    came = [[] for piece in GROUPS[0]]
+    for ref, group in zip(refs[len(refs) - len(early) :], early):
+        came += [[[ref.at[16 * place : 16 * place + 16, :]]] for place in range(len(group))]
+    row = 0
+    for keep_ref, parts in zip(refs, came):
+        for gradient, log in zip(*outputs_of(keep_ref, parts, count)):
+            gradient_ref[row : row + 8, :] = gradient
+            log_ref[row : row + 8, :] = log
             row += 8
 
 
-def share(keeps, after, count):
-    _, rows, width = keeps[0].shape
+def share(keeps, came, rows, count):
+    width = keeps[0].shape[2] - EXTRA
+    out = pltpu.HBM((rows, width), jnp.float32)
+    block = pl.BlockSpec((sum(keep.shape[1] for keep in keeps), width), lambda step: (0, 0))
     return pl.pallas_call(
-        functools.partial(share_kernel, count, len(after)),
-        out_shape=jax.ShapeDtypeStruct((2, rows * len(keeps), width - EXTRA), jnp.float32),
-        in_specs=[WHOLE] * len(keeps) + [ANYWHERE] * len(after),
-        out_specs=WHOLE,
+        functools.partial(share_kernel, count),
+        out_shape=(out, out),
+        grid=(1,),
+        in_specs=[WHOLE] * (len(keeps) + len(came)),
+        out_specs=(block, block),
         compiler_params=limit(8),
         cost_estimate=cost(0.1),
         name="share",
-    )(*keeps, *after)
-
-
-def finish_kernel(count, ready_ref, *refs):
-    (gradient_ref, log_ref), refs = refs[-2:], refs[:-2]
-    later = GROUPS[1:]
-    came = []
-    for ref, group in zip(refs[-len(later) :], later):
-        came += [ref.at[16 * place : 16 * place + 16, :] for place in range(len(group))]
-    row = ready_ref.shape[1]
-    gradient_ref[:row, :] = ready_ref[0]
-    log_ref[:row, :] = ready_ref[1]
-    for keep_ref, part in zip(refs[: -len(later)], came):
-        for gradient, log in zip(*outputs_of(keep_ref, [[part]], count)):
-            gradient_ref[row : row + 8, :] = gradient
-            log_ref[row : row + 8, :] = log
-            row += 8
-
-
-def finish(ready, keeps, came, count):
-    _, rows, width = keeps[0].shape
-    out = jax.ShapeDtypeStruct((ready.shape[1] + rows * len(keeps), width - EXTRA), jnp.float32)
+    )(*keeps, *came)
+
+
+def finish_kernel(count, keep_ref, came_ref, *refs):
+    gradient, log = outputs_of(keep_ref, [[came_ref]], count)
+    for ref, blocks in zip(refs[-2:], (gradient, log)):
+        for index, block in enumerate(blocks):
+            ref[8 * index : 8 * index + 8, :] = block
+
+
+def finish(outputs, keep, came, count):
+    _, rows, width = keep.shape
+    out = pltpu.HBM(outputs[0].shape, jnp.float32)
+    last = outputs[0].shape[0] // rows - 1
+    block = pl.BlockSpec((rows, width - EXTRA), lambda step: (last, 0))
     return pl.pallas_call(
         functools.partial(finish_kernel, count),
         out_shape=(out, out),
-        in_specs=[WHOLE] * (1 + len(keeps) + len(came)),
-        out_specs=(WHOLE, WHOLE),
+        grid=(1,),
+        in_specs=[WHOLE, WHOLE, HELD, HELD],
+        out_specs=(block, block),
+        input_output_aliases={2: 0, 3: 1},
         compiler_params=limit(8),
         cost_estimate=cost(0.1),
         name="finish",
-    )(ready, *keeps, *came)
+    )(keep, came, *outputs)
 
 
 def pieced_body(pieces, tile, inverse_rows, kinetic_rows, virt_values, virt_laplacians, local_energy):
@@ -425,6 +427,7 @@
         for array in (inverse, kinetic, virt_values[0], virt_laplacians[0])
     )
     mine = [part for group in range(pieces // 2) for part in cut(inverse, kinetic, group)]
+    mine[1], mine[2] = lax.optimization_barrier((mine[1], mine[2]))
     theirs = [swap(part, "virt", 1) for part in mine[:2]]
     near, values, laplacians = near_product(virt, me, local_energy, inverse, kinetic, values, laplacians, mine[2:])
 
@@ -461,7 +464,7 @@
         elif turn:
             carry, last = second_sums(turn - 1, carry, last, BESIDE[turn])
         layout = first_layout(1, SPLIT[turn], first[0].shape[0])
-        sends, (keep[turn],) = combine([kept], first, layout, len(second), last, 0.1)
+        sends, (keep[turn],) = combine([kept], first, layout, len(second), last, 0.1, part=2)
         last = [keep[turn]]
         if final:
             carry, last = second_sums(turn - 1, carry, last, 0.1)
@@ -469,8 +472,8 @@
         sent = [swap(part, "walk", mask) for part, mask in reversed(list(zip(sends, second)))]
     second_sums(pieces - 1, (), last, 0.1)
     came.append(swap(held.pop(), "walk", stages[2][0]))
-    ready = share([keep[piece] for piece in GROUPS[0]], last, count)
-    return finish(ready, [keep[piece] for group in GROUPS[1:] for piece in group], came[1:], count)
+    outputs = share([keep[piece] for piece in range(pieces - 1)], came[1:-1], occupied // count, count)
+    return finish(outputs, keep[pieces - 1], came[-1], count)
 
 
 def solution(mesh):

time: 77.8 us -> 77.4 us (level)
  waiting for transfers between devices: 20.4 us -> 18.9 us
    ppermute x26 -> x25, waiting for transfers between devices: 20.4 us -> 18.9 us  [swap(): return lax.ppermute(array, axis, pairs)]
    pallas_call x1, Pallas kernels: 0.08 us -> 0.88 us  [share(): pl.pallas_call(functools.partial(share_kernel, count), out_shape=(out, ou...]
    ppermute x26 -> x25, starting transfers between devices: 26.1 us -> 26.6 us  [swap(): return lax.ppermute(array, axis, pairs)]
  transfers between devices with their start and end apart: 26 -> 25, of which waited for: 11 -> 10; matrix products, arithmetic and copies ran while one was open for 0% -> 0% of each run, Pallas kernels for 35% -> 36%
where the time goes in v14:
time: 77.4 us; the launch traced here: 77.3 us
  Pallas kernels  30.2 us (39%)
  starting transfers between devices  26.6 us (34%)
  waiting for transfers between devices  18.9 us (24%)
  between operations  1.46 us (2%)
    ppermute x25, starting transfers between devices, swap(): return lax.ppermute(array, axis, pairs)  26.6 us
    ppermute x25, waiting for transfers between devices, swap(): return lax.ppermute(array, axis, pairs)  18.9 us
    pallas_call x4, Pallas kernels, far_product(): pl.pallas_call(functools.partial(far_kernel, place_weights(stages), count...  11.5 us
    pallas_call x1, Pallas kernels, near_product(): pl.pallas_call(functools.partial(near_kernel, chunk, tile), out_shape=(ja...  10.3 us
    pallas_call x9, Pallas kernels, combine(): pl.pallas_call(functools.partial(combine_kernel, layout, len(after), len(...  4.27 us
    pallas_call x2, Pallas kernels, cut(): pl.pallas_call(cut_kernel, out_shape=(out, out), grid=(1,), in_specs=[blo...  2.55 us
  transfers between devices with their start and end apart: 25, of which 10 were waited for; matrix products, arithmetic and copies ran while one was open for 0% of the time, Pallas kernels for 36%

profile of v14, /device:TPU:0, one launch (start us, length us, event | category | flops | bytes accessed | tf_op | source)
XLA Modules:
  0.0 77.3 jit_solution(7183952219579819806)
XLA Ops:
  0.6 1.3 %cut.3 = (bf16[2,128,1024]{2,1,0:T(8,128)(2,1)S(1)}, bf16[2,128,1024]{2,1,0:T(8,128)(2,1)S(1)}) custom-call(bf16[16,32,1024]{2,1,0:T(8,128)(2,1)} %bitcast.6, bf16[16,32,1024]{2,1,0:T(8,128)(2,1)} %bitcast.9), custom_call_target="tpu_custom_call" | custom-call | flops 110000000 | tf_op jit(solution)/shard_map/cut/pallas_call | solution.py:166
  1.9 3.0 %collective-permute-start.1 = (bf16[2,128,1024]{2,1,0:T(8,128)(2,1)S(1)}, bf16[2,128,1024]{2,1,0:T(8,128)(2,1)S(1)}, u32[]{:S(2)}, u32[]{:S(2)}) collective-permute-start(bf16[2,128,1024]{2,1,0:T(8,128)(2,1)S(1)} %get-tuple-element.61), channel_id=1, source_target_pairs={{0,16},{16,0},{1,17},{17,1},{2,18},{18,2},{3,19},{19,3},{4,20},{20... | collective-permute-start | bytes 1572872 | tf_op jit(solution)/shard_map/ppermute | solution.py:80
  4.9 1.3 %cut.2 = (bf16[2,128,1024]{2,1,0:T(8,128)(2,1)S(1)}, bf16[2,128,1024]{2,1,0:T(8,128)(2,1)S(1)}) custom-call(bf16[16,32,1024]{2,1,0:T(8,128)(2,1)} %bitcast.7, bf16[16,32,1024]{2,1,0:T(8,128)(2,1)} %bitcast.10), custom_call_target="tpu_custom_call" | custom-call | flops 110000000 | tf_op jit(solution)/shard_map/cut/pallas_call | solution.py:166
  7.0 10.3 %near_product.1 = (f32[2,16,32,2048]{3,2,1,0:T(8,128)S(1)}, bf16[1024,2048]{1,0:T(8,128)(2,1)S(1)}, bf16[1024,2048]{1,0:T(8,128)(2,1)S(1)}) custom-call(s32[1]{0:T(128)} %bitcast.virt_ref, s32[1]{0:T(128)} %bitcast.1.me_ref, f32[1]{0:T(128)S(6)} %copy.11.energy_ref, bf16[16,32,1024]{2,1,0:T(8,128)(2,1)} %bitcast.8, bf16[16,32,1024]{2,1,0:T(8,128)(2,1)} %bitcast.11, ...), custom_call_target="tpu_custom_call" | custom-call | flops 9900000256 | tf_op jit(solution)/shard_map/near_product/pallas_call | solution.py:232
  17.7 2.8 %far_product.4 = (bf16[64,2176]{1,0:T(8,128)(2,1)S(1)}, bf16[64,2176]{1,0:T(8,128)(2,1)S(1)}, f32[2,128,2176]{2,1,0:T(8,128)S(1)}) custom-call(s32[1]{0:T(128)} %bitcast.virt_ref, s32[1]{0:T(128)} %bitcast.1.me_ref, f32[1]{0:T(128)S(6)} %copy.11.energy_ref, bf16[2,128,1024]{2,1,0:T(8,128)(2,1)S(1)} %collective-permute-done.1.far_ref, ...), custom_call_target="tpu_custom_call" | custom-call | flops 110000000 | tf_op jit(solution)/shard_map/far_product/pallas_call | solution.py:282
  21.1 2.1 %collective-permute-start.8 = (bf16[2,128,1024]{2,1,0:T(8,128)(2,1)S(1)}, bf16[2,128,1024]{2,1,0:T(8,128)(2,1)S(1)}, u32[]{:S(2)}, u32[]{:S(2)}) collective-permute-start(bf16[2,128,1024]{2,1,0:T(8,128)(2,1)S(1)} %get-tuple-element.74.rest_0_), channel_id=1, source_target_pairs={{0,16},{16,0},{1,17},{17,1},{2,18},{18,2},{3,19},{19,3},{4,20},{20... | collective-permute-start | bytes 1572872 | tf_op jit(solution)/shard_map/ppermute | solution.py:80
  23.2 0.7 combine.9
  23.9 2.6 %collective-permute-start.5 = (bf16[32,2176]{1,0:T(8,128)(2,1)S(1)}, bf16[32,2176]{1,0:T(8,128)(2,1)S(1)}, u32[]{:S(2)}, u32[]{:S(2)}) collective-permute-start(bf16[32,2176]{1,0:T(8,128)(2,1)S(1)} %get-tuple-element.69), channel_id=1, source_target_pairs={{0,6},{1,7},{2,4},{3,5},{4,2},{5,3},{6,0},{7,1},{8,14},{9,15},{10,... | collective-permute-start | bytes 417800 | tf_op jit(solution)/shard_map/ppermute | solution.py:80
  27.4 1.5 %collective-permute-done.far_ref = bf16[2,128,1024]{2,1,0:T(8,128)(2,1)S(1)} collective-permute-done((bf16[2,128,1024]{2,1,0:T(8,128)(2,1)S(1)}, bf16[2,128,1024]{2,1,0:T(8,128)(2,1)S(1)}, u32[]{:S(2)}, u32[]{:S(2)}) %collective-permute-start) | collective-permute-done | bytes 524320 | tf_op jit(solution)/shard_map/ppermute | solution.py:80
  28.9 2.8 %far_product.5 = (bf16[64,2176]{1,0:T(8,128)(2,1)S(1)}, bf16[64,2176]{1,0:T(8,128)(2,1)S(1)}, f32[2,128,2176]{2,1,0:T(8,128)S(1)}) custom-call(s32[1]{0:T(128)} %bitcast.virt_ref, s32[1]{0:T(128)} %bitcast.1.me_ref, f32[1]{0:T(128)S(6)} %copy.11.energy_ref, bf16[2,128,1024]{2,1,0:T(8,128)(2,1)S(1)} %collective-permute-done.far_ref, ...), custom_call_target="tpu_custom_call" | custom-call | flops 1650000000 | tf_op jit(solution)/shard_map/far_product/pallas_call | solution.py:282
  32.3 1.0 %collective-permute-done.6.refs_2_ = bf16[32,2176]{1,0:T(8,128)(2,1)S(1)} collective-permute-done((bf16[32,2176]{1,0:T(8,128)(2,1)S(1)}, bf16[32,2176]{1,0:T(8,128)(2,1)S(1)}, u32[]{:S(2)}, u32[]{:S(2)}) %collective-permute-start.6) | collective-permute-done | bytes 139296 | tf_op jit(solution)/shard_map/ppermute | solution.py:80
  33.3 1.7 %collective-permute-start.4 = (bf16[2,128,1024]{2,1,0:T(8,128)(2,1)S(1)}, bf16[2,128,1024]{2,1,0:T(8,128)(2,1)S(1)}, u32[]{:S(2)}, u32[]{:S(2)}) collective-permute-start(bf16[2,128,1024]{2,1,0:T(8,128)(2,1)S(1)} %get-tuple-element.68.rest_1_), channel_id=1, source_target_pairs={{0,16},{16,0},{1,17},{17,1},{2,18},{18,2},{3,19},{19,3},{4,20},{20... | collective-permute-start | bytes 1572872 | tf_op jit(solution)/shard_map/ppermute | solution.py:80
  35.3 0.7 combine.11
  36.0 2.0 %collective-permute-start.12 = (bf16[32,2176]{1,0:T(8,128)(2,1)S(1)}, bf16[32,2176]{1,0:T(8,128)(2,1)S(1)}, u32[]{:S(2)}, u32[]{:S(2)}) collective-permute-start(bf16[32,2176]{1,0:T(8,128)(2,1)S(1)} %get-tuple-element.82), channel_id=1, source_target_pairs={{0,6},{1,7},{2,4},{3,5},{4,2},{5,3},{6,0},{7,1},{8,14},{9,15},{10,... | collective-permute-start | bytes 417800 | tf_op jit(solution)/shard_map/ppermute | solution.py:80
  38.1 1.1 %collective-permute-start.13 = (bf16[32,2176]{1,0:T(8,128)(2,1)S(1)}, bf16[32,2176]{1,0:T(8,128)(2,1)S(1)}, u32[]{:S(2)}, u32[]{:S(2)}) collective-permute-start(bf16[32,2176]{1,0:T(8,128)(2,1)S(1)} %get-tuple-element.83), channel_id=1, source_target_pairs={{0,2},{1,3},{2,0},{3,1},{4,6},{5,7},{6,4},{7,5},{8,10},{9,11},{10,... | collective-permute-start | bytes 417800 | tf_op jit(solution)/shard_map/ppermute | solution.py:80
  39.6 0.6 collective-permute-done.8.far_ref
  40.2 2.8 %far_product.6 = (bf16[128,2176]{1,0:T(8,128)(2,1)S(1)}, f32[2,128,2176]{2,1,0:T(8,128)S(1)}) custom-call(s32[1]{0:T(128)} %bitcast.virt_ref, s32[1]{0:T(128)} %bitcast.1.me_ref, f32[1]{0:T(128)S(6)} %copy.11.energy_ref, bf16[2,128,1024]{2,1,0:T(8,128)(2,1)S(1)} %collective-permute-done.8.far_ref, f32[2,16,32,2048]{3,2,1,0:T(8,128)S(1)} %get-tuple-element.58.near_ref, ...), custom_call_target="tpu_custom_call" | custom-call | flops 1650000000 | tf_op jit(solution)/shard_map/far_product/pallas_call | solution.py:282
  43.0 3.2 %collective-permute-start.16 = (bf16[16,2176]{1,0:T(8,128)(2,1)S(1)}, bf16[16,2176]{1,0:T(8,128)(2,1)S(1)}, u32[]{:S(2)}, u32[]{:S(2)}) collective-permute-start(bf16[16,2176]{1,0:T(8,128)(2,1)S(1)} %get-tuple-element.89), channel_id=1, source_target_pairs={{0,8},{1,9},{2,10},{3,11},{4,12},{5,13},{6,14},{7,15},{8,0},{9,1},... | collective-permute-start | bytes 208904 | tf_op jit(solution)/shard_map/ppermute | solution.py:80
  46.6 1.6 %collective-permute-done.11.refs_1_ = bf16[128,2176]{1,0:T(8,128)(2,1)S(1)} collective-permute-done((bf16[128,2176]{1,0:T(8,128)(2,1)S(1)}, bf16[128,2176]{1,0:T(8,128)(2,1)S(1)}, u32[]{:S(2)}, u32[]{:S(2)}) %collective-permute-start.11) | collective-permute-done | bytes 557088 | tf_op jit(solution)/shard_map/ppermute | solution.py:80
  48.1 0.7 combine.13
  48.8 2.6 %collective-permute-start.20 = (bf16[32,2176]{1,0:T(8,128)(2,1)S(1)}, bf16[32,2176]{1,0:T(8,128)(2,1)S(1)}, u32[]{:S(2)}, u32[]{:S(2)}) collective-permute-start(bf16[32,2176]{1,0:T(8,128)(2,1)S(1)} %get-tuple-element.94), channel_id=1, source_target_pairs={{0,6},{1,7},{2,4},{3,5},{4,2},{5,3},{6,0},{7,1},{8,14},{9,15},{10,... | collective-permute-start | bytes 417800 | tf_op jit(solution)/shard_map/ppermute | solution.py:80
  52.4 3.0 %far_product.7 = (bf16[128,2176]{1,0:T(8,128)(2,1)S(1)}, f32[2,128,2176]{2,1,0:T(8,128)S(1)}) custom-call(s32[1]{0:T(128)} %bitcast.virt_ref, s32[1]{0:T(128)} %bitcast.1.me_ref, f32[1]{0:T(128)S(6)} %copy.11.energy_ref, bf16[2,128,1024]{2,1,0:T(8,128)(2,1)S(1)} %collective-permute-done.4.far_ref, f32[2,16,32,2048]{3,2,1,0:T(8,128)S(1)} %get-tuple-element.58.near_ref, ...), custom_call_target="tpu_custom_call" | custom-call | flops 1650000000 | tf_op jit(solution)/shard_map/far_product/pallas_call | solution.py:282
  55.6 1.8 %collective-permute-done.15.refs_1_ = bf16[128,2176]{1,0:T(8,128)(2,1)S(1)} collective-permute-done((bf16[128,2176]{1,0:T(8,128)(2,1)S(1)}, bf16[128,2176]{1,0:T(8,128)(2,1)S(1)}, u32[]{:S(2)}, u32[]{:S(2)}) %collective-permute-start.15) | collective-permute-done | bytes 557088 | tf_op jit(solution)/shard_map/ppermute | solution.py:80
  57.4 0.7 combine.15
  58.1 2.6 %collective-permute-start.17 = (bf16[32,2176]{1,0:T(8,128)(2,1)S(1)}, bf16[32,2176]{1,0:T(8,128)(2,1)S(1)}, u32[]{:S(2)}, u32[]{:S(2)}) collective-permute-start(bf16[32,2176]{1,0:T(8,128)(2,1)S(1)} %get-tuple-element.91), channel_id=1, source_target_pairs={{0,6},{1,7},{2,4},{3,5},{4,2},{5,3},{6,0},{7,1},{8,14},{9,15},{10,... | collective-permute-start | bytes 417800 | tf_op jit(solution)/shard_map/ppermute | solution.py:80
  62.1 1.0 %collective-permute-start.24 = (bf16[32,2176]{1,0:T(8,128)(2,1)S(1)}, bf16[32,2176]{1,0:T(8,128)(2,1)S(1)}, u32[]{:S(2)}, u32[]{:S(2)}) collective-permute-start(bf16[32,2176]{1,0:T(8,128)(2,1)S(1)} %get-tuple-element.101), channel_id=1, source_target_pairs={{0,8},{1,9},{2,10},{3,11},{4,12},{5,13},{6,14},{7,15},{8,0},{9,1},... | collective-permute-start | bytes 417800 | tf_op jit(solution)/shard_map/ppermute | solution.py:80
  63.1 2.1 %collective-permute-done.17.refs_1_ = bf16[32,2176]{1,0:T(8,128)(2,1)S(1)} collective-permute-done((bf16[32,2176]{1,0:T(8,128)(2,1)S(1)}, bf16[32,2176]{1,0:T(8,128)(2,1)S(1)}, u32[]{:S(2)}, u32[]{:S(2)}) %collective-permute-start.17) | collective-permute-done | bytes 139296 | tf_op jit(solution)/shard_map/ppermute | solution.py:80
  65.2 2.6 %collective-permute-done.18.refs_2_ = bf16[32,2176]{1,0:T(8,128)(2,1)S(1)} collective-permute-done((bf16[32,2176]{1,0:T(8,128)(2,1)S(1)}, bf16[32,2176]{1,0:T(8,128)(2,1)S(1)}, u32[]{:S(2)}, u32[]{:S(2)}) %collective-permute-start.18) | collective-permute-done | bytes 139296 | tf_op jit(solution)/shard_map/ppermute | solution.py:80
  67.8 3.1 %collective-permute-done.19.refs_3_ = bf16[32,2176]{1,0:T(8,128)(2,1)S(1)} collective-permute-done((bf16[32,2176]{1,0:T(8,128)(2,1)S(1)}, bf16[32,2176]{1,0:T(8,128)(2,1)S(1)}, u32[]{:S(2)}, u32[]{:S(2)}) %collective-permute-start.19) | collective-permute-done | bytes 139296 | tf_op jit(solution)/shard_map/ppermute | solution.py:80
  71.3 0.9 %share.1 = (f32[32,2048]{1,0:T(8,128)}, f32[32,2048]{1,0:T(8,128)}) custom-call(f32[2,8,2176]{2,1,0:T(8,128)S(1)} %combine.14.refs_2_.refs_0_, f32[2,8,2176]{2,1,0:T(8,128)S(1)} %get-tuple-element.85.refs_2_.refs_1_, f32[2,8,2176]{2,1,0:T(8,128)S(1)} %get-tuple-element.98.refs_4_.refs_2_, bf16[32,2176]{1,0:T(8,128)(2,1)S(1)} %collective-permute-done.24.refs_3_), custom_call_target="tpu_custom_call" | custom-call | flops 110000000 | tf_op jit(solution)/shard_map/share/pallas_call | solution.py:378
  72.2 4.2 %collective-permute-done.23.came_ref = bf16[16,2176]{1,0:T(8,128)(2,1)S(1)} collective-permute-done((bf16[16,2176]{1,0:T(8,128)(2,1)S(1)}, bf16[16,2176]{1,0:T(8,128)(2,1)S(1)}, u32[]{:S(2)}, u32[]{:S(2)}) %collective-permute-start.23) | collective-permute-done | bytes 69664 | tf_op jit(solution)/shard_map/ppermute | solution.py:80
  76.5 0.8 %finish.1 = (f32[32,2048]{1,0:T(8,128)}, f32[32,2048]{1,0:T(8,128)}) custom-call(f32[2,8,2176]{2,1,0:T(8,128)S(1)} %get-tuple-element.99.keep_ref, bf16[16,2176]{1,0:T(8,128)(2,1)S(1)} %collective-permute-done.23.came_ref, f32[32,2048]{1,0:T(8,128)} %get-tuple-element.102.refs_0_, ...), custom_call_target="tpu_custom_call", output_to_operand_aliasing={{0}: (2, {}), {1}: (3, {})} | custom-call | flops 110000000 | tf_op jit(solution)/shard_map/finish/pallas_call | solution.py:402
  (36 shorter events, 6.8 us)
Async XLA Ops:
  1.9 15.8 %collective-permute-start.1 = (bf16[2,128,1024]{2,1,0:T(8,128)(2,1)S(1)}, bf16[2,128,1024]{2,1,0:T(8,128)(2,1)S(1)}, u32[]{:S(2)}, u32[]{:S(2)}) collective-permute-start(bf16[2,128,1024]{2,1,0:T(8,128)(2,1)S(1)} %get-tuple-element.61), channel_id=1, source_target_pairs={{0,16},{16,0},{1,17},{17,1},{2,18},{18,2},{3,19},{19,3},{4,20},{20... | collective-permute-start | bytes 1572872 | tf_op jit(solution)/shard_map/ppermute | solution.py:80
  6.2 22.7 %collective-permute-start = (bf16[2,128,1024]{2,1,0:T(8,128)(2,1)S(1)}, bf16[2,128,1024]{2,1,0:T(8,128)(2,1)S(1)}, u32[]{:S(2)}, u32[]{:S(2)}) collective-permute-start(bf16[2,128,1024]{2,1,0:T(8,128)(2,1)S(1)} %get-tuple-element.56), channel_id=1, source_target_pairs={{0,16},{16,0},{1,17},{17,1},{2,18},{18,2},{3,19},{19,3},{4,20},{20... | collective-permute-start | bytes 1572872 | tf_op jit(solution)/shard_map/ppermute | solution.py:80
  20.5 2.6 %collective-permute-start.2 = (bf16[64,2176]{1,0:T(8,128)(2,1)S(1)}, bf16[64,2176]{1,0:T(8,128)(2,1)S(1)}, u32[]{:S(2)}, u32[]{:S(2)}) collective-permute-start(bf16[64,2176]{1,0:T(8,128)(2,1)S(1)} %get-tuple-element.64), channel_id=1, source_target_pairs={{0,1},{1,0},{2,3},{3,2},{4,5},{5,4},{6,7},{7,6},{8,9},{9,8},{10,11... | collective-permute-start | bytes 835592 | tf_op jit(solution)/shard_map/ppermute | solution.py:80
  20.6 2.6 %collective-permute-start.3 = (bf16[64,2176]{1,0:T(8,128)(2,1)S(1)}, bf16[64,2176]{1,0:T(8,128)(2,1)S(1)}, u32[]{:S(2)}, u32[]{:S(2)}) collective-permute-start(bf16[64,2176]{1,0:T(8,128)(2,1)S(1)} %get-tuple-element.65), channel_id=1, source_target_pairs={{0,1},{1,0},{2,3},{3,2},{4,5},{5,4},{6,7},{7,6},{8,9},{9,8},{10,11... | collective-permute-start | bytes 835592 | tf_op jit(solution)/shard_map/ppermute | solution.py:80
  21.1 19.1 %collective-permute-start.8 = (bf16[2,128,1024]{2,1,0:T(8,128)(2,1)S(1)}, bf16[2,128,1024]{2,1,0:T(8,128)(2,1)S(1)}, u32[]{:S(2)}, u32[]{:S(2)}) collective-permute-start(bf16[2,128,1024]{2,1,0:T(8,128)(2,1)S(1)} %get-tuple-element.74.rest_0_), channel_id=1, source_target_pairs={{0,16},{16,0},{1,17},{17,1},{2,18},{18,2},{3,19},{19,3},{4,20},{20... | collective-permute-start | bytes 1572872 | tf_op jit(solution)/shard_map/ppermute | solution.py:80
  23.9 8.0 %collective-permute-start.5 = (bf16[32,2176]{1,0:T(8,128)(2,1)S(1)}, bf16[32,2176]{1,0:T(8,128)(2,1)S(1)}, u32[]{:S(2)}, u32[]{:S(2)}) collective-permute-start(bf16[32,2176]{1,0:T(8,128)(2,1)S(1)} %get-tuple-element.69), channel_id=1, source_target_pairs={{0,6},{1,7},{2,4},{3,5},{4,2},{5,3},{6,0},{7,1},{8,14},{9,15},{10,... | collective-permute-start | bytes 417800 | tf_op jit(solution)/shard_map/ppermute | solution.py:80
  26.4 6.9 %collective-permute-start.6 = (bf16[32,2176]{1,0:T(8,128)(2,1)S(1)}, bf16[32,2176]{1,0:T(8,128)(2,1)S(1)}, u32[]{:S(2)}, u32[]{:S(2)}) collective-permute-start(bf16[32,2176]{1,0:T(8,128)(2,1)S(1)} %get-tuple-element.70), channel_id=1, source_target_pairs={{0,2},{1,3},{2,0},{3,1},{4,6},{5,7},{6,4},{7,5},{8,10},{9,11},{10,... | collective-permute-start | bytes 417800 | tf_op jit(solution)/shard_map/ppermute | solution.py:80
  27.0 8.0 %collective-permute-start.7 = (bf16[32,2176]{1,0:T(8,128)(2,1)S(1)}, bf16[32,2176]{1,0:T(8,128)(2,1)S(1)}, u32[]{:S(2)}, u32[]{:S(2)}) collective-permute-start(bf16[32,2176]{1,0:T(8,128)(2,1)S(1)} %get-tuple-element.71), channel_id=1, source_target_pairs={{0,4},{1,5},{2,6},{3,7},{4,0},{5,1},{6,2},{7,3},{8,12},{9,13},{10,... | collective-permute-start | bytes 417800 | tf_op jit(solution)/shard_map/ppermute | solution.py:80
  31.8 3.6 %collective-permute-start.9 = (bf16[64,2176]{1,0:T(8,128)(2,1)S(1)}, bf16[64,2176]{1,0:T(8,128)(2,1)S(1)}, u32[]{:S(2)}, u32[]{:S(2)}) collective-permute-start(bf16[64,2176]{1,0:T(8,128)(2,1)S(1)} %get-tuple-element.75), channel_id=1, source_target_pairs={{0,1},{1,0},{2,3},{3,2},{4,5},{5,4},{6,7},{7,6},{8,9},{9,8},{10,11... | collective-permute-start | bytes 835592 | tf_op jit(solution)/shard_map/ppermute | solution.py:80
  31.8 3.5 %collective-permute-start.10 = (bf16[64,2176]{1,0:T(8,128)(2,1)S(1)}, bf16[64,2176]{1,0:T(8,128)(2,1)S(1)}, u32[]{:S(2)}, u32[]{:S(2)}) collective-permute-start(bf16[64,2176]{1,0:T(8,128)(2,1)S(1)} %get-tuple-element.76), channel_id=1, source_target_pairs={{0,1},{1,0},{2,3},{3,2},{4,5},{5,4},{6,7},{7,6},{8,9},{9,8},{10,11... | collective-permute-start | bytes 835592 | tf_op jit(solution)/shard_map/ppermute | solution.py:80
  33.3 19.1 %collective-permute-start.4 = (bf16[2,128,1024]{2,1,0:T(8,128)(2,1)S(1)}, bf16[2,128,1024]{2,1,0:T(8,128)(2,1)S(1)}, u32[]{:S(2)}, u32[]{:S(2)}) collective-permute-start(bf16[2,128,1024]{2,1,0:T(8,128)(2,1)S(1)} %get-tuple-element.68.rest_1_), channel_id=1, source_target_pairs={{0,16},{16,0},{1,17},{17,1},{2,18},{18,2},{3,19},{19,3},{4,20},{20... | collective-permute-start | bytes 1572872 | tf_op jit(solution)/shard_map/ppermute | solution.py:80
  36.0 10.1 %collective-permute-start.12 = (bf16[32,2176]{1,0:T(8,128)(2,1)S(1)}, bf16[32,2176]{1,0:T(8,128)(2,1)S(1)}, u32[]{:S(2)}, u32[]{:S(2)}) collective-permute-start(bf16[32,2176]{1,0:T(8,128)(2,1)S(1)} %get-tuple-element.82), channel_id=1, source_target_pairs={{0,6},{1,7},{2,4},{3,5},{4,2},{5,3},{6,0},{7,1},{8,14},{9,15},{10,... | collective-permute-start | bytes 417800 | tf_op jit(solution)/shard_map/ppermute | solution.py:80
  38.1 8.1 %collective-permute-start.13 = (bf16[32,2176]{1,0:T(8,128)(2,1)S(1)}, bf16[32,2176]{1,0:T(8,128)(2,1)S(1)}, u32[]{:S(2)}, u32[]{:S(2)}) collective-permute-start(bf16[32,2176]{1,0:T(8,128)(2,1)S(1)} %get-tuple-element.83), channel_id=1, source_target_pairs={{0,2},{1,3},{2,0},{3,1},{4,6},{5,7},{6,4},{7,5},{8,10},{9,11},{10,... | collective-permute-start | bytes 417800 | tf_op jit(solution)/shard_map/ppermute | solution.py:80
  39.2 7.0 %collective-permute-start.14 = (bf16[32,2176]{1,0:T(8,128)(2,1)S(1)}, bf16[32,2176]{1,0:T(8,128)(2,1)S(1)}, u32[]{:S(2)}, u32[]{:S(2)}) collective-permute-start(bf16[32,2176]{1,0:T(8,128)(2,1)S(1)} %get-tuple-element.84), channel_id=1, source_target_pairs={{0,4},{1,5},{2,6},{3,7},{4,0},{5,1},{6,2},{7,3},{8,12},{9,13},{10,... | collective-permute-start | bytes 417800 | tf_op jit(solution)/shard_map/ppermute | solution.py:80
  43.0 12.5 %collective-permute-start.16 = (bf16[16,2176]{1,0:T(8,128)(2,1)S(1)}, bf16[16,2176]{1,0:T(8,128)(2,1)S(1)}, u32[]{:S(2)}, u32[]{:S(2)}) collective-permute-start(bf16[16,2176]{1,0:T(8,128)(2,1)S(1)} %get-tuple-element.89), channel_id=1, source_target_pairs={{0,8},{1,9},{2,10},{3,11},{4,12},{5,13},{6,14},{7,15},{8,0},{9,1},... | collective-permute-start | bytes 208904 | tf_op jit(solution)/shard_map/ppermute | solution.py:80
  46.2 2.0 %collective-permute-start.11 = (bf16[128,2176]{1,0:T(8,128)(2,1)S(1)}, bf16[128,2176]{1,0:T(8,128)(2,1)S(1)}, u32[]{:S(2)}, u32[]{:S(2)}) collective-permute-start(bf16[128,2176]{1,0:T(8,128)(2,1)S(1)} %get-tuple-element.81), channel_id=1, source_target_pairs={{0,1},{1,0},{2,3},{3,2},{4,5},{5,4},{6,7},{7,6},{8,9},{9,8},{10,11... | collective-permute-start | bytes 1671176 | tf_op jit(solution)/shard_map/ppermute | solution.py:80
  48.8 12.4 %collective-permute-start.20 = (bf16[32,2176]{1,0:T(8,128)(2,1)S(1)}, bf16[32,2176]{1,0:T(8,128)(2,1)S(1)}, u32[]{:S(2)}, u32[]{:S(2)}) collective-permute-start(bf16[32,2176]{1,0:T(8,128)(2,1)S(1)} %get-tuple-element.94), channel_id=1, source_target_pairs={{0,6},{1,7},{2,4},{3,5},{4,2},{5,3},{6,0},{7,1},{8,14},{9,15},{10,... | collective-permute-start | bytes 417800 | tf_op jit(solution)/shard_map/ppermute | solution.py:80
  51.4 10.3 %collective-permute-start.21 = (bf16[32,2176]{1,0:T(8,128)(2,1)S(1)}, bf16[32,2176]{1,0:T(8,128)(2,1)S(1)}, u32[]{:S(2)}, u32[]{:S(2)}) collective-permute-start(bf16[32,2176]{1,0:T(8,128)(2,1)S(1)} %get-tuple-element.95), channel_id=1, source_target_pairs={{0,2},{1,3},{2,0},{3,1},{4,6},{5,7},{6,4},{7,5},{8,10},{9,11},{10,... | collective-permute-start | bytes 417800 | tf_op jit(solution)/shard_map/ppermute | solution.py:80
  52.0 9.7 %collective-permute-start.22 = (bf16[32,2176]{1,0:T(8,128)(2,1)S(1)}, bf16[32,2176]{1,0:T(8,128)(2,1)S(1)}, u32[]{:S(2)}, u32[]{:S(2)}) collective-permute-start(bf16[32,2176]{1,0:T(8,128)(2,1)S(1)} %get-tuple-element.96), channel_id=1, source_target_pairs={{0,4},{1,5},{2,6},{3,7},{4,0},{5,1},{6,2},{7,3},{8,12},{9,13},{10,... | collective-permute-start | bytes 417800 | tf_op jit(solution)/shard_map/ppermute | solution.py:80
  55.4 2.0 %collective-permute-start.15 = (bf16[128,2176]{1,0:T(8,128)(2,1)S(1)}, bf16[128,2176]{1,0:T(8,128)(2,1)S(1)}, u32[]{:S(2)}, u32[]{:S(2)}) collective-permute-start(bf16[128,2176]{1,0:T(8,128)(2,1)S(1)} %get-tuple-element.88), channel_id=1, source_target_pairs={{0,1},{1,0},{2,3},{3,2},{4,5},{5,4},{6,7},{7,6},{8,9},{9,8},{10,11... | collective-permute-start | bytes 1671176 | tf_op jit(solution)/shard_map/ppermute | solution.py:80
  58.1 7.1 %collective-permute-start.17 = (bf16[32,2176]{1,0:T(8,128)(2,1)S(1)}, bf16[32,2176]{1,0:T(8,128)(2,1)S(1)}, u32[]{:S(2)}, u32[]{:S(2)}) collective-permute-start(bf16[32,2176]{1,0:T(8,128)(2,1)S(1)} %get-tuple-element.91), channel_id=1, source_target_pairs={{0,6},{1,7},{2,4},{3,5},{4,2},{5,3},{6,0},{7,1},{8,14},{9,15},{10,... | collective-permute-start | bytes 417800 | tf_op jit(solution)/shard_map/ppermute | solution.py:80
  60.7 7.1 %collective-permute-start.18 = (bf16[32,2176]{1,0:T(8,128)(2,1)S(1)}, bf16[32,2176]{1,0:T(8,128)(2,1)S(1)}, u32[]{:S(2)}, u32[]{:S(2)}) collective-permute-start(bf16[32,2176]{1,0:T(8,128)(2,1)S(1)} %get-tuple-element.92), channel_id=1, source_target_pairs={{0,2},{1,3},{2,0},{3,1},{4,6},{5,7},{6,4},{7,5},{8,10},{9,11},{10,... | collective-permute-start | bytes 417800 | tf_op jit(solution)/shard_map/ppermute | solution.py:80
  61.2 9.6 %collective-permute-start.19 = (bf16[32,2176]{1,0:T(8,128)(2,1)S(1)}, bf16[32,2176]{1,0:T(8,128)(2,1)S(1)}, u32[]{:S(2)}, u32[]{:S(2)}) collective-permute-start(bf16[32,2176]{1,0:T(8,128)(2,1)S(1)} %get-tuple-element.93), channel_id=1, source_target_pairs={{0,4},{1,5},{2,6},{3,7},{4,0},{5,1},{6,2},{7,3},{8,12},{9,13},{10,... | collective-permute-start | bytes 417800 | tf_op jit(solution)/shard_map/ppermute | solution.py:80
  62.1 9.3 %collective-permute-start.24 = (bf16[32,2176]{1,0:T(8,128)(2,1)S(1)}, bf16[32,2176]{1,0:T(8,128)(2,1)S(1)}, u32[]{:S(2)}, u32[]{:S(2)}) collective-permute-start(bf16[32,2176]{1,0:T(8,128)(2,1)S(1)} %get-tuple-element.101), channel_id=1, source_target_pairs={{0,8},{1,9},{2,10},{3,11},{4,12},{5,13},{6,14},{7,15},{8,0},{9,1},... | collective-permute-start | bytes 417800 | tf_op jit(solution)/shard_map/ppermute | solution.py:80
  71.2 5.3 %collective-permute-start.23 = (bf16[16,2176]{1,0:T(8,128)(2,1)S(1)}, bf16[16,2176]{1,0:T(8,128)(2,1)S(1)}, u32[]{:S(2)}, u32[]{:S(2)}) collective-permute-start(bf16[16,2176]{1,0:T(8,128)(2,1)S(1)} %get-tuple-element.100), channel_id=1, source_target_pairs={{0,8},{1,9},{2,10},{3,11},{4,12},{5,13},{6,14},{7,15},{8,0},{9,1},... | collective-permute-start | bytes 208904 | tf_op jit(solution)/shard_map/ppermute | solution.py:80

commit v15 on v14

--- a/solution.py
+++ b/solution.py
@@ -489,7 +489,7 @@
         count = mesh.shape["walk"]
         walkers, occupied, depth = inverse_rows.shape
         width = virt_values.shape[2]
-        tile = 512
+        tile = 1024
         fits = (
             walkers == 1
             and mesh.shape["virt"] == 2

time: 77.4 us -> 77.1 us (level)
  Pallas kernels: 30.2 us -> 29.1 us
    pallas_call x4, Pallas kernels: 11.5 us -> 10.4 us  [far_product(): pl.pallas_call(functools.partial(far_kernel, place_weights(stages), count...]
  transfers between devices with their start and end apart: 25 -> 25, of which waited for: 10 -> 10; matrix products, arithmetic and copies ran while one was open for 0% -> 0% of each run, Pallas kernels for 36% -> 35%
where the time goes in v15:
time: 77.1 us; the launch traced here: 76.9 us
  Pallas kernels  29.1 us (38%)
  starting transfers between devices  27.2 us (35%)
  waiting for transfers between devices  19.1 us (25%)
  between operations  1.47 us (2%)
    ppermute x25, starting transfers between devices, swap(): return lax.ppermute(array, axis, pairs)  27.2 us
    ppermute x25, waiting for transfers between devices, swap(): return lax.ppermute(array, axis, pairs)  19.1 us
    pallas_call x4, Pallas kernels, far_product(): pl.pallas_call(functools.partial(far_kernel, place_weights(stages), count...  10.4 us
    pallas_call x1, Pallas kernels, near_product(): pl.pallas_call(functools.partial(near_kernel, chunk, tile), out_shape=(ja...  10.3 us
    pallas_call x9, Pallas kernels, combine(): pl.pallas_call(functools.partial(combine_kernel, layout, len(after), len(...  4.27 us
    pallas_call x2, Pallas kernels, cut(): pl.pallas_call(cut_kernel, out_shape=(out, out), grid=(1,), in_specs=[blo...  2.55 us
  transfers between devices with their start and end apart: 25, of which 10 were waited for; matrix products, arithmetic and copies ran while one was open for 0% of the time, Pallas kernels for 35%

profile of v15, /device:TPU:0, one launch (start us, length us, event | category | flops | bytes accessed | tf_op | source)
XLA Modules:
  0.0 76.9 jit_solution(5699204155857587651)
XLA Ops:
  0.6 1.3 %cut.3 = (bf16[2,128,1024]{2,1,0:T(8,128)(2,1)S(1)}, bf16[2,128,1024]{2,1,0:T(8,128)(2,1)S(1)}) custom-call(bf16[16,32,1024]{2,1,0:T(8,128)(2,1)} %bitcast.6, bf16[16,32,1024]{2,1,0:T(8,128)(2,1)} %bitcast.9), custom_call_target="tpu_custom_call" | custom-call | flops 110000000 | tf_op jit(solution)/shard_map/cut/pallas_call | solution.py:166
  1.9 3.0 %collective-permute-start.1 = (bf16[2,128,1024]{2,1,0:T(8,128)(2,1)S(1)}, bf16[2,128,1024]{2,1,0:T(8,128)(2,1)S(1)}, u32[]{:S(2)}, u32[]{:S(2)}) collective-permute-start(bf16[2,128,1024]{2,1,0:T(8,128)(2,1)S(1)} %get-tuple-element.61), channel_id=1, source_target_pairs={{0,16},{16,0},{1,17},{17,1},{2,18},{18,2},{3,19},{19,3},{4,20},{20... | collective-permute-start | bytes 1572872 | tf_op jit(solution)/shard_map/ppermute | solution.py:80
  4.9 1.3 %cut.2 = (bf16[2,128,1024]{2,1,0:T(8,128)(2,1)S(1)}, bf16[2,128,1024]{2,1,0:T(8,128)(2,1)S(1)}) custom-call(bf16[16,32,1024]{2,1,0:T(8,128)(2,1)} %bitcast.7, bf16[16,32,1024]{2,1,0:T(8,128)(2,1)} %bitcast.10), custom_call_target="tpu_custom_call" | custom-call | flops 110000000 | tf_op jit(solution)/shard_map/cut/pallas_call | solution.py:166
  7.0 10.3 %near_product.1 = (f32[2,16,32,2048]{3,2,1,0:T(8,128)S(1)}, bf16[1024,2048]{1,0:T(8,128)(2,1)S(1)}, bf16[1024,2048]{1,0:T(8,128)(2,1)S(1)}) custom-call(s32[1]{0:T(128)} %bitcast.virt_ref, s32[1]{0:T(128)} %bitcast.1.me_ref, f32[1]{0:T(128)S(6)} %copy.11.energy_ref, bf16[16,32,1024]{2,1,0:T(8,128)(2,1)} %bitcast.8, bf16[16,32,1024]{2,1,0:T(8,128)(2,1)} %bitcast.11, ...), custom_call_target="tpu_custom_call" | custom-call | flops 9900000256 | tf_op jit(solution)/shard_map/near_product/pallas_call | solution.py:232
  17.7 2.5 %far_product.4 = (bf16[64,2176]{1,0:T(8,128)(2,1)S(1)}, bf16[64,2176]{1,0:T(8,128)(2,1)S(1)}, f32[2,128,2176]{2,1,0:T(8,128)S(1)}) custom-call(s32[1]{0:T(128)} %bitcast.virt_ref, s32[1]{0:T(128)} %bitcast.1.me_ref, f32[1]{0:T(128)S(6)} %copy.11.energy_ref, bf16[2,128,1024]{2,1,0:T(8,128)(2,1)S(1)} %collective-permute-done.1.far_ref, ...), custom_call_target="tpu_custom_call" | custom-call | flops 110000000 | tf_op jit(solution)/shard_map/far_product/pallas_call | solution.py:282
  20.8 2.1 %collective-permute-start.8 = (bf16[2,128,1024]{2,1,0:T(8,128)(2,1)S(1)}, bf16[2,128,1024]{2,1,0:T(8,128)(2,1)S(1)}, u32[]{:S(2)}, u32[]{:S(2)}) collective-permute-start(bf16[2,128,1024]{2,1,0:T(8,128)(2,1)S(1)} %get-tuple-element.74.rest_0_), channel_id=1, source_target_pairs={{0,16},{16,0},{1,17},{17,1},{2,18},{18,2},{3,19},{19,3},{4,20},{20... | collective-permute-start | bytes 1572872 | tf_op jit(solution)/shard_map/ppermute | solution.py:80
  22.9 0.7 combine.9
  23.6 2.6 %collective-permute-start.5 = (bf16[32,2176]{1,0:T(8,128)(2,1)S(1)}, bf16[32,2176]{1,0:T(8,128)(2,1)S(1)}, u32[]{:S(2)}, u32[]{:S(2)}) collective-permute-start(bf16[32,2176]{1,0:T(8,128)(2,1)S(1)} %get-tuple-element.69), channel_id=1, source_target_pairs={{0,6},{1,7},{2,4},{3,5},{4,2},{5,3},{6,0},{7,1},{8,14},{9,15},{10,... | collective-permute-start | bytes 417800 | tf_op jit(solution)/shard_map/ppermute | solution.py:80
  27.1 1.8 %collective-permute-done.far_ref = bf16[2,128,1024]{2,1,0:T(8,128)(2,1)S(1)} collective-permute-done((bf16[2,128,1024]{2,1,0:T(8,128)(2,1)S(1)}, bf16[2,128,1024]{2,1,0:T(8,128)(2,1)S(1)}, u32[]{:S(2)}, u32[]{:S(2)}) %collective-permute-start) | collective-permute-done | bytes 524320 | tf_op jit(solution)/shard_map/ppermute | solution.py:80
  28.9 2.5 %far_product.5 = (bf16[64,2176]{1,0:T(8,128)(2,1)S(1)}, bf16[64,2176]{1,0:T(8,128)(2,1)S(1)}, f32[2,128,2176]{2,1,0:T(8,128)S(1)}) custom-call(s32[1]{0:T(128)} %bitcast.virt_ref, s32[1]{0:T(128)} %bitcast.1.me_ref, f32[1]{0:T(128)S(6)} %copy.11.energy_ref, bf16[2,128,1024]{2,1,0:T(8,128)(2,1)S(1)} %collective-permute-done.far_ref, ...), custom_call_target="tpu_custom_call" | custom-call | flops 1650000000 | tf_op jit(solution)/shard_map/far_product/pallas_call | solution.py:282
  32.1 1.0 %collective-permute-done.6.refs_2_ = bf16[32,2176]{1,0:T(8,128)(2,1)S(1)} collective-permute-done((bf16[32,2176]{1,0:T(8,128)(2,1)S(1)}, bf16[32,2176]{1,0:T(8,128)(2,1)S(1)}, u32[]{:S(2)}, u32[]{:S(2)}) %collective-permute-start.6) | collective-permute-done | bytes 139296 | tf_op jit(solution)/shard_map/ppermute | solution.py:80
  33.0 1.7 %collective-permute-start.4 = (bf16[2,128,1024]{2,1,0:T(8,128)(2,1)S(1)}, bf16[2,128,1024]{2,1,0:T(8,128)(2,1)S(1)}, u32[]{:S(2)}, u32[]{:S(2)}) collective-permute-start(bf16[2,128,1024]{2,1,0:T(8,128)(2,1)S(1)} %get-tuple-element.68.rest_1_), channel_id=1, source_target_pairs={{0,16},{16,0},{1,17},{17,1},{2,18},{18,2},{3,19},{19,3},{4,20},{20... | collective-permute-start | bytes 1572872 | tf_op jit(solution)/shard_map/ppermute | solution.py:80
  35.1 0.7 combine.11
  35.8 2.0 %collective-permute-start.12 = (bf16[32,2176]{1,0:T(8,128)(2,1)S(1)}, bf16[32,2176]{1,0:T(8,128)(2,1)S(1)}, u32[]{:S(2)}, u32[]{:S(2)}) collective-permute-start(bf16[32,2176]{1,0:T(8,128)(2,1)S(1)} %get-tuple-element.82), channel_id=1, source_target_pairs={{0,6},{1,7},{2,4},{3,5},{4,2},{5,3},{6,0},{7,1},{8,14},{9,15},{10,... | collective-permute-start | bytes 417800 | tf_op jit(solution)/shard_map/ppermute | solution.py:80
  37.8 1.1 %collective-permute-start.13 = (bf16[32,2176]{1,0:T(8,128)(2,1)S(1)}, bf16[32,2176]{1,0:T(8,128)(2,1)S(1)}, u32[]{:S(2)}, u32[]{:S(2)}) collective-permute-start(bf16[32,2176]{1,0:T(8,128)(2,1)S(1)} %get-tuple-element.83), channel_id=1, source_target_pairs={{0,2},{1,3},{2,0},{3,1},{4,6},{5,7},{6,4},{7,5},{8,10},{9,11},{10,... | collective-permute-start | bytes 417800 | tf_op jit(solution)/shard_map/ppermute | solution.py:80
  39.3 0.8 %collective-permute-done.8.far_ref = bf16[2,128,1024]{2,1,0:T(8,128)(2,1)S(1)} collective-permute-done((bf16[2,128,1024]{2,1,0:T(8,128)(2,1)S(1)}, bf16[2,128,1024]{2,1,0:T(8,128)(2,1)S(1)}, u32[]{:S(2)}, u32[]{:S(2)}) %collective-permute-start.8) | collective-permute-done | bytes 524320 | tf_op jit(solution)/shard_map/ppermute | solution.py:80
  40.2 2.5 %far_product.6 = (bf16[128,2176]{1,0:T(8,128)(2,1)S(1)}, f32[2,128,2176]{2,1,0:T(8,128)S(1)}) custom-call(s32[1]{0:T(128)} %bitcast.virt_ref, s32[1]{0:T(128)} %bitcast.1.me_ref, f32[1]{0:T(128)S(6)} %copy.11.energy_ref, bf16[2,128,1024]{2,1,0:T(8,128)(2,1)S(1)} %collective-permute-done.8.far_ref, f32[2,16,32,2048]{3,2,1,0:T(8,128)S(1)} %get-tuple-element.58.near_ref, ...), custom_call_target="tpu_custom_call" | custom-call | flops 1650000000 | tf_op jit(solution)/shard_map/far_product/pallas_call | solution.py:282
  42.7 3.2 %collective-permute-start.16 = (bf16[16,2176]{1,0:T(8,128)(2,1)S(1)}, bf16[16,2176]{1,0:T(8,128)(2,1)S(1)}, u32[]{:S(2)}, u32[]{:S(2)}) collective-permute-start(bf16[16,2176]{1,0:T(8,128)(2,1)S(1)} %get-tuple-element.89), channel_id=1, source_target_pairs={{0,8},{1,9},{2,10},{3,11},{4,12},{5,13},{6,14},{7,15},{8,0},{9,1},... | collective-permute-start | bytes 208904 | tf_op jit(solution)/shard_map/ppermute | solution.py:80
  46.3 1.6 %collective-permute-done.11.refs_1_ = bf16[128,2176]{1,0:T(8,128)(2,1)S(1)} collective-permute-done((bf16[128,2176]{1,0:T(8,128)(2,1)S(1)}, bf16[128,2176]{1,0:T(8,128)(2,1)S(1)}, u32[]{:S(2)}, u32[]{:S(2)}) %collective-permute-start.11) | collective-permute-done | bytes 557088 | tf_op jit(solution)/shard_map/ppermute | solution.py:80
  47.9 0.7 combine.13
  48.6 2.6 %collective-permute-start.20 = (bf16[32,2176]{1,0:T(8,128)(2,1)S(1)}, bf16[32,2176]{1,0:T(8,128)(2,1)S(1)}, u32[]{:S(2)}, u32[]{:S(2)}) collective-permute-start(bf16[32,2176]{1,0:T(8,128)(2,1)S(1)} %get-tuple-element.94), channel_id=1, source_target_pairs={{0,6},{1,7},{2,4},{3,5},{4,2},{5,3},{6,0},{7,1},{8,14},{9,15},{10,... | collective-permute-start | bytes 417800 | tf_op jit(solution)/shard_map/ppermute | solution.py:80
  52.1 2.7 %far_product.7 = (bf16[128,2176]{1,0:T(8,128)(2,1)S(1)}, f32[2,128,2176]{2,1,0:T(8,128)S(1)}) custom-call(s32[1]{0:T(128)} %bitcast.virt_ref, s32[1]{0:T(128)} %bitcast.1.me_ref, f32[1]{0:T(128)S(6)} %copy.11.energy_ref, bf16[2,128,1024]{2,1,0:T(8,128)(2,1)S(1)} %collective-permute-done.4.far_ref, f32[2,16,32,2048]{3,2,1,0:T(8,128)S(1)} %get-tuple-element.58.near_ref, ...), custom_call_target="tpu_custom_call" | custom-call | flops 1650000000 | tf_op jit(solution)/shard_map/far_product/pallas_call | solution.py:282
  55.1 1.8 %collective-permute-done.15.refs_1_ = bf16[128,2176]{1,0:T(8,128)(2,1)S(1)} collective-permute-done((bf16[128,2176]{1,0:T(8,128)(2,1)S(1)}, bf16[128,2176]{1,0:T(8,128)(2,1)S(1)}, u32[]{:S(2)}, u32[]{:S(2)}) %collective-permute-start.15) | collective-permute-done | bytes 557088 | tf_op jit(solution)/shard_map/ppermute | solution.py:80
  56.9 0.7 combine.15
  57.6 2.6 %collective-permute-start.17 = (bf16[32,2176]{1,0:T(8,128)(2,1)S(1)}, bf16[32,2176]{1,0:T(8,128)(2,1)S(1)}, u32[]{:S(2)}, u32[]{:S(2)}) collective-permute-start(bf16[32,2176]{1,0:T(8,128)(2,1)S(1)} %get-tuple-element.91), channel_id=1, source_target_pairs={{0,6},{1,7},{2,4},{3,5},{4,2},{5,3},{6,0},{7,1},{8,14},{9,15},{10,... | collective-permute-start | bytes 417800 | tf_op jit(solution)/shard_map/ppermute | solution.py:80
  61.5 1.3 %collective-permute-start.24 = (bf16[32,2176]{1,0:T(8,128)(2,1)S(1)}, bf16[32,2176]{1,0:T(8,128)(2,1)S(1)}, u32[]{:S(2)}, u32[]{:S(2)}) collective-permute-start(bf16[32,2176]{1,0:T(8,128)(2,1)S(1)} %get-tuple-element.101), channel_id=1, source_target_pairs={{0,8},{1,9},{2,10},{3,11},{4,12},{5,13},{6,14},{7,15},{8,0},{9,1},... | collective-permute-start | bytes 417800 | tf_op jit(solution)/shard_map/ppermute | solution.py:80
  62.8 1.8 %collective-permute-done.17.refs_1_ = bf16[32,2176]{1,0:T(8,128)(2,1)S(1)} collective-permute-done((bf16[32,2176]{1,0:T(8,128)(2,1)S(1)}, bf16[32,2176]{1,0:T(8,128)(2,1)S(1)}, u32[]{:S(2)}, u32[]{:S(2)}) %collective-permute-start.17) | collective-permute-done | bytes 139296 | tf_op jit(solution)/shard_map/ppermute | solution.py:80
  64.7 2.6 %collective-permute-done.18.refs_2_ = bf16[32,2176]{1,0:T(8,128)(2,1)S(1)} collective-permute-done((bf16[32,2176]{1,0:T(8,128)(2,1)S(1)}, bf16[32,2176]{1,0:T(8,128)(2,1)S(1)}, u32[]{:S(2)}, u32[]{:S(2)}) %collective-permute-start.18) | collective-permute-done | bytes 139296 | tf_op jit(solution)/shard_map/ppermute | solution.py:80
  67.2 3.0 %collective-permute-done.19.refs_3_ = bf16[32,2176]{1,0:T(8,128)(2,1)S(1)} collective-permute-done((bf16[32,2176]{1,0:T(8,128)(2,1)S(1)}, bf16[32,2176]{1,0:T(8,128)(2,1)S(1)}, u32[]{:S(2)}, u32[]{:S(2)}) %collective-permute-start.19) | collective-permute-done | bytes 139296 | tf_op jit(solution)/shard_map/ppermute | solution.py:80
  71.1 0.9 %share.1 = (f32[32,2048]{1,0:T(8,128)}, f32[32,2048]{1,0:T(8,128)}) custom-call(f32[2,8,2176]{2,1,0:T(8,128)S(1)} %combine.14.refs_2_.refs_0_, f32[2,8,2176]{2,1,0:T(8,128)S(1)} %get-tuple-element.85.refs_2_.refs_1_, f32[2,8,2176]{2,1,0:T(8,128)S(1)} %get-tuple-element.98.refs_4_.refs_2_, bf16[32,2176]{1,0:T(8,128)(2,1)S(1)} %collective-permute-done.24.refs_3_), custom_call_target="tpu_custom_call" | custom-call | flops 110000000 | tf_op jit(solution)/shard_map/share/pallas_call | solution.py:378
  72.0 4.2 %collective-permute-done.23.came_ref = bf16[16,2176]{1,0:T(8,128)(2,1)S(1)} collective-permute-done((bf16[16,2176]{1,0:T(8,128)(2,1)S(1)}, bf16[16,2176]{1,0:T(8,128)(2,1)S(1)}, u32[]{:S(2)}, u32[]{:S(2)}) %collective-permute-start.23) | collective-permute-done | bytes 69664 | tf_op jit(solution)/shard_map/ppermute | solution.py:80
  76.1 0.8 %finish.1 = (f32[32,2048]{1,0:T(8,128)}, f32[32,2048]{1,0:T(8,128)}) custom-call(f32[2,8,2176]{2,1,0:T(8,128)S(1)} %get-tuple-element.99.keep_ref, bf16[16,2176]{1,0:T(8,128)(2,1)S(1)} %collective-permute-done.23.came_ref, f32[32,2048]{1,0:T(8,128)} %get-tuple-element.102.refs_0_, ...), custom_call_target="tpu_custom_call", output_to_operand_aliasing={{0}: (2, {}), {1}: (3, {})} | custom-call | flops 110000000 | tf_op jit(solution)/shard_map/finish/pallas_call | solution.py:402
  (36 shorter events, 7.1 us)
Async XLA Ops:
  1.9 15.8 %collective-permute-start.1 = (bf16[2,128,1024]{2,1,0:T(8,128)(2,1)S(1)}, bf16[2,128,1024]{2,1,0:T(8,128)(2,1)S(1)}, u32[]{:S(2)}, u32[]{:S(2)}) collective-permute-start(bf16[2,128,1024]{2,1,0:T(8,128)(2,1)S(1)} %get-tuple-element.61), channel_id=1, source_target_pairs={{0,16},{16,0},{1,17},{17,1},{2,18},{18,2},{3,19},{19,3},{4,20},{20... | collective-permute-start | bytes 1572872 | tf_op jit(solution)/shard_map/ppermute | solution.py:80
  6.2 22.7 %collective-permute-start = (bf16[2,128,1024]{2,1,0:T(8,128)(2,1)S(1)}, bf16[2,128,1024]{2,1,0:T(8,128)(2,1)S(1)}, u32[]{:S(2)}, u32[]{:S(2)}) collective-permute-start(bf16[2,128,1024]{2,1,0:T(8,128)(2,1)S(1)} %get-tuple-element.56), channel_id=1, source_target_pairs={{0,16},{16,0},{1,17},{17,1},{2,18},{18,2},{3,19},{19,3},{4,20},{20... | collective-permute-start | bytes 1572872 | tf_op jit(solution)/shard_map/ppermute | solution.py:80
  20.3 2.6 %collective-permute-start.2 = (bf16[64,2176]{1,0:T(8,128)(2,1)S(1)}, bf16[64,2176]{1,0:T(8,128)(2,1)S(1)}, u32[]{:S(2)}, u32[]{:S(2)}) collective-permute-start(bf16[64,2176]{1,0:T(8,128)(2,1)S(1)} %get-tuple-element.64), channel_id=1, source_target_pairs={{0,1},{1,0},{2,3},{3,2},{4,5},{5,4},{6,7},{7,6},{8,9},{9,8},{10,11... | collective-permute-start | bytes 835592 | tf_op jit(solution)/shard_map/ppermute | solution.py:80
  20.3 2.6 %collective-permute-start.3 = (bf16[64,2176]{1,0:T(8,128)(2,1)S(1)}, bf16[64,2176]{1,0:T(8,128)(2,1)S(1)}, u32[]{:S(2)}, u32[]{:S(2)}) collective-permute-start(bf16[64,2176]{1,0:T(8,128)(2,1)S(1)} %get-tuple-element.65), channel_id=1, source_target_pairs={{0,1},{1,0},{2,3},{3,2},{4,5},{5,4},{6,7},{7,6},{8,9},{9,8},{10,11... | collective-permute-start | bytes 835592 | tf_op jit(solution)/shard_map/ppermute | solution.py:80
  20.8 19.3 %collective-permute-start.8 = (bf16[2,128,1024]{2,1,0:T(8,128)(2,1)S(1)}, bf16[2,128,1024]{2,1,0:T(8,128)(2,1)S(1)}, u32[]{:S(2)}, u32[]{:S(2)}) collective-permute-start(bf16[2,128,1024]{2,1,0:T(8,128)(2,1)S(1)} %get-tuple-element.74.rest_0_), channel_id=1, source_target_pairs={{0,16},{16,0},{1,17},{17,1},{2,18},{18,2},{3,19},{19,3},{4,20},{20... | collective-permute-start | bytes 1572872 | tf_op jit(solution)/shard_map/ppermute | solution.py:80
  23.6 8.0 %collective-permute-start.5 = (bf16[32,2176]{1,0:T(8,128)(2,1)S(1)}, bf16[32,2176]{1,0:T(8,128)(2,1)S(1)}, u32[]{:S(2)}, u32[]{:S(2)}) collective-permute-start(bf16[32,2176]{1,0:T(8,128)(2,1)S(1)} %get-tuple-element.69), channel_id=1, source_target_pairs={{0,6},{1,7},{2,4},{3,5},{4,2},{5,3},{6,0},{7,1},{8,14},{9,15},{10,... | collective-permute-start | bytes 417800 | tf_op jit(solution)/shard_map/ppermute | solution.py:80
  26.2 6.9 %collective-permute-start.6 = (bf16[32,2176]{1,0:T(8,128)(2,1)S(1)}, bf16[32,2176]{1,0:T(8,128)(2,1)S(1)}, u32[]{:S(2)}, u32[]{:S(2)}) collective-permute-start(bf16[32,2176]{1,0:T(8,128)(2,1)S(1)} %get-tuple-element.70), channel_id=1, source_target_pairs={{0,2},{1,3},{2,0},{3,1},{4,6},{5,7},{6,4},{7,5},{8,10},{9,11},{10,... | collective-permute-start | bytes 417800 | tf_op jit(solution)/shard_map/ppermute | solution.py:80
  26.7 8.0 %collective-permute-start.7 = (bf16[32,2176]{1,0:T(8,128)(2,1)S(1)}, bf16[32,2176]{1,0:T(8,128)(2,1)S(1)}, u32[]{:S(2)}, u32[]{:S(2)}) collective-permute-start(bf16[32,2176]{1,0:T(8,128)(2,1)S(1)} %get-tuple-element.71), channel_id=1, source_target_pairs={{0,4},{1,5},{2,6},{3,7},{4,0},{5,1},{6,2},{7,3},{8,12},{9,13},{10,... | collective-permute-start | bytes 417800 | tf_op jit(solution)/shard_map/ppermute | solution.py:80
  31.5 3.6 %collective-permute-start.9 = (bf16[64,2176]{1,0:T(8,128)(2,1)S(1)}, bf16[64,2176]{1,0:T(8,128)(2,1)S(1)}, u32[]{:S(2)}, u32[]{:S(2)}) collective-permute-start(bf16[64,2176]{1,0:T(8,128)(2,1)S(1)} %get-tuple-element.75), channel_id=1, source_target_pairs={{0,1},{1,0},{2,3},{3,2},{4,5},{5,4},{6,7},{7,6},{8,9},{9,8},{10,11... | collective-permute-start | bytes 835592 | tf_op jit(solution)/shard_map/ppermute | solution.py:80
  31.6 3.5 %collective-permute-start.10 = (bf16[64,2176]{1,0:T(8,128)(2,1)S(1)}, bf16[64,2176]{1,0:T(8,128)(2,1)S(1)}, u32[]{:S(2)}, u32[]{:S(2)}) collective-permute-start(bf16[64,2176]{1,0:T(8,128)(2,1)S(1)} %get-tuple-element.76), channel_id=1, source_target_pairs={{0,1},{1,0},{2,3},{3,2},{4,5},{5,4},{6,7},{7,6},{8,9},{9,8},{10,11... | collective-permute-start | bytes 835592 | tf_op jit(solution)/shard_map/ppermute | solution.py:80
  33.0 19.1 %collective-permute-start.4 = (bf16[2,128,1024]{2,1,0:T(8,128)(2,1)S(1)}, bf16[2,128,1024]{2,1,0:T(8,128)(2,1)S(1)}, u32[]{:S(2)}, u32[]{:S(2)}) collective-permute-start(bf16[2,128,1024]{2,1,0:T(8,128)(2,1)S(1)} %get-tuple-element.68.rest_1_), channel_id=1, source_target_pairs={{0,16},{16,0},{1,17},{17,1},{2,18},{18,2},{3,19},{19,3},{4,20},{20... | collective-permute-start | bytes 1572872 | tf_op jit(solution)/shard_map/ppermute | solution.py:80
  35.8 10.1 %collective-permute-start.12 = (bf16[32,2176]{1,0:T(8,128)(2,1)S(1)}, bf16[32,2176]{1,0:T(8,128)(2,1)S(1)}, u32[]{:S(2)}, u32[]{:S(2)}) collective-permute-start(bf16[32,2176]{1,0:T(8,128)(2,1)S(1)} %get-tuple-element.82), channel_id=1, source_target_pairs={{0,6},{1,7},{2,4},{3,5},{4,2},{5,3},{6,0},{7,1},{8,14},{9,15},{10,... | collective-permute-start | bytes 417800 | tf_op jit(solution)/shard_map/ppermute | solution.py:80
  37.8 8.1 %collective-permute-start.13 = (bf16[32,2176]{1,0:T(8,128)(2,1)S(1)}, bf16[32,2176]{1,0:T(8,128)(2,1)S(1)}, u32[]{:S(2)}, u32[]{:S(2)}) collective-permute-start(bf16[32,2176]{1,0:T(8,128)(2,1)S(1)} %get-tuple-element.83), channel_id=1, source_target_pairs={{0,2},{1,3},{2,0},{3,1},{4,6},{5,7},{6,4},{7,5},{8,10},{9,11},{10,... | collective-permute-start | bytes 417800 | tf_op jit(solution)/shard_map/ppermute | solution.py:80
  38.9 7.0 %collective-permute-start.14 = (bf16[32,2176]{1,0:T(8,128)(2,1)S(1)}, bf16[32,2176]{1,0:T(8,128)(2,1)S(1)}, u32[]{:S(2)}, u32[]{:S(2)}) collective-permute-start(bf16[32,2176]{1,0:T(8,128)(2,1)S(1)} %get-tuple-element.84), channel_id=1, source_target_pairs={{0,4},{1,5},{2,6},{3,7},{4,0},{5,1},{6,2},{7,3},{8,12},{9,13},{10,... | collective-permute-start | bytes 417800 | tf_op jit(solution)/shard_map/ppermute | solution.py:80
  42.7 12.2 %collective-permute-start.16 = (bf16[16,2176]{1,0:T(8,128)(2,1)S(1)}, bf16[16,2176]{1,0:T(8,128)(2,1)S(1)}, u32[]{:S(2)}, u32[]{:S(2)}) collective-permute-start(bf16[16,2176]{1,0:T(8,128)(2,1)S(1)} %get-tuple-element.89), channel_id=1, source_target_pairs={{0,8},{1,9},{2,10},{3,11},{4,12},{5,13},{6,14},{7,15},{8,0},{9,1},... | collective-permute-start | bytes 208904 | tf_op jit(solution)/shard_map/ppermute | solution.py:80
  45.9 2.0 %collective-permute-start.11 = (bf16[128,2176]{1,0:T(8,128)(2,1)S(1)}, bf16[128,2176]{1,0:T(8,128)(2,1)S(1)}, u32[]{:S(2)}, u32[]{:S(2)}) collective-permute-start(bf16[128,2176]{1,0:T(8,128)(2,1)S(1)} %get-tuple-element.81), channel_id=1, source_target_pairs={{0,1},{1,0},{2,3},{3,2},{4,5},{5,4},{6,7},{7,6},{8,9},{9,8},{10,11... | collective-permute-start | bytes 1671176 | tf_op jit(solution)/shard_map/ppermute | solution.py:80
  48.6 12.1 %collective-permute-start.20 = (bf16[32,2176]{1,0:T(8,128)(2,1)S(1)}, bf16[32,2176]{1,0:T(8,128)(2,1)S(1)}, u32[]{:S(2)}, u32[]{:S(2)}) collective-permute-start(bf16[32,2176]{1,0:T(8,128)(2,1)S(1)} %get-tuple-element.94), channel_id=1, source_target_pairs={{0,6},{1,7},{2,4},{3,5},{4,2},{5,3},{6,0},{7,1},{8,14},{9,15},{10,... | collective-permute-start | bytes 417800 | tf_op jit(solution)/shard_map/ppermute | solution.py:80
  51.1 10.0 %collective-permute-start.21 = (bf16[32,2176]{1,0:T(8,128)(2,1)S(1)}, bf16[32,2176]{1,0:T(8,128)(2,1)S(1)}, u32[]{:S(2)}, u32[]{:S(2)}) collective-permute-start(bf16[32,2176]{1,0:T(8,128)(2,1)S(1)} %get-tuple-element.95), channel_id=1, source_target_pairs={{0,2},{1,3},{2,0},{3,1},{4,6},{5,7},{6,4},{7,5},{8,10},{9,11},{10,... | collective-permute-start | bytes 417800 | tf_op jit(solution)/shard_map/ppermute | solution.py:80
  51.7 9.5 %collective-permute-start.22 = (bf16[32,2176]{1,0:T(8,128)(2,1)S(1)}, bf16[32,2176]{1,0:T(8,128)(2,1)S(1)}, u32[]{:S(2)}, u32[]{:S(2)}) collective-permute-start(bf16[32,2176]{1,0:T(8,128)(2,1)S(1)} %get-tuple-element.96), channel_id=1, source_target_pairs={{0,4},{1,5},{2,6},{3,7},{4,0},{5,1},{6,2},{7,3},{8,12},{9,13},{10,... | collective-permute-start | bytes 417800 | tf_op jit(solution)/shard_map/ppermute | solution.py:80
  54.9 2.0 %collective-permute-start.15 = (bf16[128,2176]{1,0:T(8,128)(2,1)S(1)}, bf16[128,2176]{1,0:T(8,128)(2,1)S(1)}, u32[]{:S(2)}, u32[]{:S(2)}) collective-permute-start(bf16[128,2176]{1,0:T(8,128)(2,1)S(1)} %get-tuple-element.88), channel_id=1, source_target_pairs={{0,1},{1,0},{2,3},{3,2},{4,5},{5,4},{6,7},{7,6},{8,9},{9,8},{10,11... | collective-permute-start | bytes 1671176 | tf_op jit(solution)/shard_map/ppermute | solution.py:80
  57.6 7.1 %collective-permute-start.17 = (bf16[32,2176]{1,0:T(8,128)(2,1)S(1)}, bf16[32,2176]{1,0:T(8,128)(2,1)S(1)}, u32[]{:S(2)}, u32[]{:S(2)}) collective-permute-start(bf16[32,2176]{1,0:T(8,128)(2,1)S(1)} %get-tuple-element.91), channel_id=1, source_target_pairs={{0,6},{1,7},{2,4},{3,5},{4,2},{5,3},{6,0},{7,1},{8,14},{9,15},{10,... | collective-permute-start | bytes 417800 | tf_op jit(solution)/shard_map/ppermute | solution.py:80
  60.1 7.1 %collective-permute-start.18 = (bf16[32,2176]{1,0:T(8,128)(2,1)S(1)}, bf16[32,2176]{1,0:T(8,128)(2,1)S(1)}, u32[]{:S(2)}, u32[]{:S(2)}) collective-permute-start(bf16[32,2176]{1,0:T(8,128)(2,1)S(1)} %get-tuple-element.92), channel_id=1, source_target_pairs={{0,2},{1,3},{2,0},{3,1},{4,6},{5,7},{6,4},{7,5},{8,10},{9,11},{10,... | collective-permute-start | bytes 417800 | tf_op jit(solution)/shard_map/ppermute | solution.py:80
  60.7 9.6 %collective-permute-start.19 = (bf16[32,2176]{1,0:T(8,128)(2,1)S(1)}, bf16[32,2176]{1,0:T(8,128)(2,1)S(1)}, u32[]{:S(2)}, u32[]{:S(2)}) collective-permute-start(bf16[32,2176]{1,0:T(8,128)(2,1)S(1)} %get-tuple-element.93), channel_id=1, source_target_pairs={{0,4},{1,5},{2,6},{3,7},{4,0},{5,1},{6,2},{7,3},{8,12},{9,13},{10,... | collective-permute-start | bytes 417800 | tf_op jit(solution)/shard_map/ppermute | solution.py:80
  61.5 9.6 %collective-permute-start.24 = (bf16[32,2176]{1,0:T(8,128)(2,1)S(1)}, bf16[32,2176]{1,0:T(8,128)(2,1)S(1)}, u32[]{:S(2)}, u32[]{:S(2)}) collective-permute-start(bf16[32,2176]{1,0:T(8,128)(2,1)S(1)} %get-tuple-element.101), channel_id=1, source_target_pairs={{0,8},{1,9},{2,10},{3,11},{4,12},{5,13},{6,14},{7,15},{8,0},{9,1},... | collective-permute-start | bytes 417800 | tf_op jit(solution)/shard_map/ppermute | solution.py:80
  70.7 5.5 %collective-permute-start.23 = (bf16[16,2176]{1,0:T(8,128)(2,1)S(1)}, bf16[16,2176]{1,0:T(8,128)(2,1)S(1)}, u32[]{:S(2)}, u32[]{:S(2)}) collective-permute-start(bf16[16,2176]{1,0:T(8,128)(2,1)S(1)} %get-tuple-element.100), channel_id=1, source_target_pairs={{0,8},{1,9},{2,10},{3,11},{4,12},{5,13},{6,14},{7,15},{8,0},{9,1},... | collective-permute-start | bytes 208904 | tf_op jit(solution)/shard_map/ppermute | solution.py:80

commit v16 on v15

--- a/solution.py
+++ b/solution.py
@@ -489,7 +489,7 @@
         count = mesh.shape["walk"]
         walkers, occupied, depth = inverse_rows.shape
         width = virt_values.shape[2]
-        tile = 1024
+        tile = 2048
         fits = (
             walkers == 1
             and mesh.shape["virt"] == 2

time: 77.1 us -> 77.1 us (level)
  no operation moved by 1% of the time
where the time goes in v16:
time: 77.1 us; the launch traced here: 76.9 us
  Pallas kernels  29.3 us (38%)
  starting transfers between devices  27.2 us (35%)
  waiting for transfers between devices  19 us (25%)
  between operations  1.47 us (2%)
    ppermute x25, starting transfers between devices, swap(): return lax.ppermute(array, axis, pairs)  27.2 us
    ppermute x25, waiting for transfers between devices, swap(): return lax.ppermute(array, axis, pairs)  19 us
    pallas_call x1, Pallas kernels, near_product(): pl.pallas_call(functools.partial(near_kernel, chunk, tile), out_shape=(ja...  10.5 us
    pallas_call x4, Pallas kernels, far_product(): pl.pallas_call(functools.partial(far_kernel, place_weights(stages), count...  10.3 us
    pallas_call x9, Pallas kernels, combine(): pl.pallas_call(functools.partial(combine_kernel, layout, len(after), len(...  4.27 us
    pallas_call x2, Pallas kernels, cut(): pl.pallas_call(cut_kernel, out_shape=(out, out), grid=(1,), in_specs=[blo...  2.55 us
  transfers between devices with their start and end apart: 25, of which 10 were waited for; matrix products, arithmetic and copies ran while one was open for 0% of the time, Pallas kernels for 35%

profile of v16, /device:TPU:0, one launch (start us, length us, event | category | flops | bytes accessed | tf_op | source)
XLA Modules:
  0.0 76.9 jit_solution(2964051648095875114)
XLA Ops:
  0.6 1.3 %cut.3 = (bf16[2,128,1024]{2,1,0:T(8,128)(2,1)S(1)}, bf16[2,128,1024]{2,1,0:T(8,128)(2,1)S(1)}) custom-call(bf16[16,32,1024]{2,1,0:T(8,128)(2,1)} %bitcast.6, bf16[16,32,1024]{2,1,0:T(8,128)(2,1)} %bitcast.9), custom_call_target="tpu_custom_call" | custom-call | flops 110000000 | tf_op jit(solution)/shard_map/cut/pallas_call | solution.py:166
  1.9 3.0 %collective-permute-start.1 = (bf16[2,128,1024]{2,1,0:T(8,128)(2,1)S(1)}, bf16[2,128,1024]{2,1,0:T(8,128)(2,1)S(1)}, u32[]{:S(2)}, u32[]{:S(2)}) collective-permute-start(bf16[2,128,1024]{2,1,0:T(8,128)(2,1)S(1)} %get-tuple-element.61), channel_id=1, source_target_pairs={{0,16},{16,0},{1,17},{17,1},{2,18},{18,2},{3,19},{19,3},{4,20},{20... | collective-permute-start | bytes 1572872 | tf_op jit(solution)/shard_map/ppermute | solution.py:80
  4.9 1.3 %cut.2 = (bf16[2,128,1024]{2,1,0:T(8,128)(2,1)S(1)}, bf16[2,128,1024]{2,1,0:T(8,128)(2,1)S(1)}) custom-call(bf16[16,32,1024]{2,1,0:T(8,128)(2,1)} %bitcast.7, bf16[16,32,1024]{2,1,0:T(8,128)(2,1)} %bitcast.10), custom_call_target="tpu_custom_call" | custom-call | flops 110000000 | tf_op jit(solution)/shard_map/cut/pallas_call | solution.py:166
  7.0 10.5 %near_product.1 = (f32[2,16,32,2048]{3,2,1,0:T(8,128)S(1)}, bf16[1024,2048]{1,0:T(8,128)(2,1)S(1)}, bf16[1024,2048]{1,0:T(8,128)(2,1)S(1)}) custom-call(s32[1]{0:T(128)} %bitcast.virt_ref, s32[1]{0:T(128)} %bitcast.1.me_ref, f32[1]{0:T(128)S(6)} %copy.11.energy_ref, bf16[16,32,1024]{2,1,0:T(8,128)(2,1)} %bitcast.8, bf16[16,32,1024]{2,1,0:T(8,128)(2,1)} %bitcast.11, ...), custom_call_target="tpu_custom_call" | custom-call | flops 9900000256 | tf_op jit(solution)/shard_map/near_product/pallas_call | solution.py:232
  17.7 2.5 %far_product.4 = (bf16[64,2176]{1,0:T(8,128)(2,1)S(1)}, bf16[64,2176]{1,0:T(8,128)(2,1)S(1)}, f32[2,128,2176]{2,1,0:T(8,128)S(1)}) custom-call(s32[1]{0:T(128)} %bitcast.virt_ref, s32[1]{0:T(128)} %bitcast.1.me_ref, f32[1]{0:T(128)S(6)} %copy.11.energy_ref, bf16[2,128,1024]{2,1,0:T(8,128)(2,1)S(1)} %collective-permute-done.1.far_ref, ...), custom_call_target="tpu_custom_call" | custom-call | flops 110000000 | tf_op jit(solution)/shard_map/far_product/pallas_call | solution.py:282
  20.8 2.1 %collective-permute-start.8 = (bf16[2,128,1024]{2,1,0:T(8,128)(2,1)S(1)}, bf16[2,128,1024]{2,1,0:T(8,128)(2,1)S(1)}, u32[]{:S(2)}, u32[]{:S(2)}) collective-permute-start(bf16[2,128,1024]{2,1,0:T(8,128)(2,1)S(1)} %get-tuple-element.74.rest_0_), channel_id=1, source_target_pairs={{0,16},{16,0},{1,17},{17,1},{2,18},{18,2},{3,19},{19,3},{4,20},{20... | collective-permute-start | bytes 1572872 | tf_op jit(solution)/shard_map/ppermute | solution.py:80
  22.9 0.7 combine.9
  23.6 2.6 %collective-permute-start.5 = (bf16[32,2176]{1,0:T(8,128)(2,1)S(1)}, bf16[32,2176]{1,0:T(8,128)(2,1)S(1)}, u32[]{:S(2)}, u32[]{:S(2)}) collective-permute-start(bf16[32,2176]{1,0:T(8,128)(2,1)S(1)} %get-tuple-element.69), channel_id=1, source_target_pairs={{0,6},{1,7},{2,4},{3,5},{4,2},{5,3},{6,0},{7,1},{8,14},{9,15},{10,... | collective-permute-start | bytes 417800 | tf_op jit(solution)/shard_map/ppermute | solution.py:80
  27.1 1.8 %collective-permute-done.far_ref = bf16[2,128,1024]{2,1,0:T(8,128)(2,1)S(1)} collective-permute-done((bf16[2,128,1024]{2,1,0:T(8,128)(2,1)S(1)}, bf16[2,128,1024]{2,1,0:T(8,128)(2,1)S(1)}, u32[]{:S(2)}, u32[]{:S(2)}) %collective-permute-start) | collective-permute-done | bytes 524320 | tf_op jit(solution)/shard_map/ppermute | solution.py:80
  28.9 2.5 %far_product.5 = (bf16[64,2176]{1,0:T(8,128)(2,1)S(1)}, bf16[64,2176]{1,0:T(8,128)(2,1)S(1)}, f32[2,128,2176]{2,1,0:T(8,128)S(1)}) custom-call(s32[1]{0:T(128)} %bitcast.virt_ref, s32[1]{0:T(128)} %bitcast.1.me_ref, f32[1]{0:T(128)S(6)} %copy.11.energy_ref, bf16[2,128,1024]{2,1,0:T(8,128)(2,1)S(1)} %collective-permute-done.far_ref, ...), custom_call_target="tpu_custom_call" | custom-call | flops 1650000000 | tf_op jit(solution)/shard_map/far_product/pallas_call | solution.py:282
  32.0 1.0 %collective-permute-done.6.refs_2_ = bf16[32,2176]{1,0:T(8,128)(2,1)S(1)} collective-permute-done((bf16[32,2176]{1,0:T(8,128)(2,1)S(1)}, bf16[32,2176]{1,0:T(8,128)(2,1)S(1)}, u32[]{:S(2)}, u32[]{:S(2)}) %collective-permute-start.6) | collective-permute-done | bytes 139296 | tf_op jit(solution)/shard_map/ppermute | solution.py:80
  33.0 1.7 %collective-permute-start.4 = (bf16[2,128,1024]{2,1,0:T(8,128)(2,1)S(1)}, bf16[2,128,1024]{2,1,0:T(8,128)(2,1)S(1)}, u32[]{:S(2)}, u32[]{:S(2)}) collective-permute-start(bf16[2,128,1024]{2,1,0:T(8,128)(2,1)S(1)} %get-tuple-element.68.rest_1_), channel_id=1, source_target_pairs={{0,16},{16,0},{1,17},{17,1},{2,18},{18,2},{3,19},{19,3},{4,20},{20... | collective-permute-start | bytes 1572872 | tf_op jit(solution)/shard_map/ppermute | solution.py:80
  35.1 0.7 combine.11
  35.8 2.0 %collective-permute-start.12 = (bf16[32,2176]{1,0:T(8,128)(2,1)S(1)}, bf16[32,2176]{1,0:T(8,128)(2,1)S(1)}, u32[]{:S(2)}, u32[]{:S(2)}) collective-permute-start(bf16[32,2176]{1,0:T(8,128)(2,1)S(1)} %get-tuple-element.82), channel_id=1, source_target_pairs={{0,6},{1,7},{2,4},{3,5},{4,2},{5,3},{6,0},{7,1},{8,14},{9,15},{10,... | collective-permute-start | bytes 417800 | tf_op jit(solution)/shard_map/ppermute | solution.py:80
  37.8 1.1 %collective-permute-start.13 = (bf16[32,2176]{1,0:T(8,128)(2,1)S(1)}, bf16[32,2176]{1,0:T(8,128)(2,1)S(1)}, u32[]{:S(2)}, u32[]{:S(2)}) collective-permute-start(bf16[32,2176]{1,0:T(8,128)(2,1)S(1)} %get-tuple-element.83), channel_id=1, source_target_pairs={{0,2},{1,3},{2,0},{3,1},{4,6},{5,7},{6,4},{7,5},{8,10},{9,11},{10,... | collective-permute-start | bytes 417800 | tf_op jit(solution)/shard_map/ppermute | solution.py:80
  39.3 0.8 %collective-permute-done.8.far_ref = bf16[2,128,1024]{2,1,0:T(8,128)(2,1)S(1)} collective-permute-done((bf16[2,128,1024]{2,1,0:T(8,128)(2,1)S(1)}, bf16[2,128,1024]{2,1,0:T(8,128)(2,1)S(1)}, u32[]{:S(2)}, u32[]{:S(2)}) %collective-permute-start.8) | collective-permute-done | bytes 524320 | tf_op jit(solution)/shard_map/ppermute | solution.py:80
  40.2 2.5 %far_product.6 = (bf16[128,2176]{1,0:T(8,128)(2,1)S(1)}, f32[2,128,2176]{2,1,0:T(8,128)S(1)}) custom-call(s32[1]{0:T(128)} %bitcast.virt_ref, s32[1]{0:T(128)} %bitcast.1.me_ref, f32[1]{0:T(128)S(6)} %copy.11.energy_ref, bf16[2,128,1024]{2,1,0:T(8,128)(2,1)S(1)} %collective-permute-done.8.far_ref, f32[2,16,32,2048]{3,2,1,0:T(8,128)S(1)} %get-tuple-element.58.near_ref, ...), custom_call_target="tpu_custom_call" | custom-call | flops 1650000000 | tf_op jit(solution)/shard_map/far_product/pallas_call | solution.py:282
  42.7 3.2 %collective-permute-start.16 = (bf16[16,2176]{1,0:T(8,128)(2,1)S(1)}, bf16[16,2176]{1,0:T(8,128)(2,1)S(1)}, u32[]{:S(2)}, u32[]{:S(2)}) collective-permute-start(bf16[16,2176]{1,0:T(8,128)(2,1)S(1)} %get-tuple-element.89), channel_id=1, source_target_pairs={{0,8},{1,9},{2,10},{3,11},{4,12},{5,13},{6,14},{7,15},{8,0},{9,1},... | collective-permute-start | bytes 208904 | tf_op jit(solution)/shard_map/ppermute | solution.py:80
  46.3 1.6 %collective-permute-done.11.refs_1_ = bf16[128,2176]{1,0:T(8,128)(2,1)S(1)} collective-permute-done((bf16[128,2176]{1,0:T(8,128)(2,1)S(1)}, bf16[128,2176]{1,0:T(8,128)(2,1)S(1)}, u32[]{:S(2)}, u32[]{:S(2)}) %collective-permute-start.11) | collective-permute-done | bytes 557088 | tf_op jit(solution)/shard_map/ppermute | solution.py:80
  47.9 0.7 combine.13
  48.6 2.6 %collective-permute-start.20 = (bf16[32,2176]{1,0:T(8,128)(2,1)S(1)}, bf16[32,2176]{1,0:T(8,128)(2,1)S(1)}, u32[]{:S(2)}, u32[]{:S(2)}) collective-permute-start(bf16[32,2176]{1,0:T(8,128)(2,1)S(1)} %get-tuple-element.94), channel_id=1, source_target_pairs={{0,6},{1,7},{2,4},{3,5},{4,2},{5,3},{6,0},{7,1},{8,14},{9,15},{10,... | collective-permute-start | bytes 417800 | tf_op jit(solution)/shard_map/ppermute | solution.py:80
  52.1 2.7 %far_product.7 = (bf16[128,2176]{1,0:T(8,128)(2,1)S(1)}, f32[2,128,2176]{2,1,0:T(8,128)S(1)}) custom-call(s32[1]{0:T(128)} %bitcast.virt_ref, s32[1]{0:T(128)} %bitcast.1.me_ref, f32[1]{0:T(128)S(6)} %copy.11.energy_ref, bf16[2,128,1024]{2,1,0:T(8,128)(2,1)S(1)} %collective-permute-done.4.far_ref, f32[2,16,32,2048]{3,2,1,0:T(8,128)S(1)} %get-tuple-element.58.near_ref, ...), custom_call_target="tpu_custom_call" | custom-call | flops 1650000000 | tf_op jit(solution)/shard_map/far_product/pallas_call | solution.py:282
  55.0 1.8 %collective-permute-done.15.refs_1_ = bf16[128,2176]{1,0:T(8,128)(2,1)S(1)} collective-permute-done((bf16[128,2176]{1,0:T(8,128)(2,1)S(1)}, bf16[128,2176]{1,0:T(8,128)(2,1)S(1)}, u32[]{:S(2)}, u32[]{:S(2)}) %collective-permute-start.15) | collective-permute-done | bytes 557088 | tf_op jit(solution)/shard_map/ppermute | solution.py:80
  56.9 0.7 combine.15
  57.6 2.6 %collective-permute-start.17 = (bf16[32,2176]{1,0:T(8,128)(2,1)S(1)}, bf16[32,2176]{1,0:T(8,128)(2,1)S(1)}, u32[]{:S(2)}, u32[]{:S(2)}) collective-permute-start(bf16[32,2176]{1,0:T(8,128)(2,1)S(1)} %get-tuple-element.91), channel_id=1, source_target_pairs={{0,6},{1,7},{2,4},{3,5},{4,2},{5,3},{6,0},{7,1},{8,14},{9,15},{10,... | collective-permute-start | bytes 417800 | tf_op jit(solution)/shard_map/ppermute | solution.py:80
  61.5 1.3 %collective-permute-start.24 = (bf16[32,2176]{1,0:T(8,128)(2,1)S(1)}, bf16[32,2176]{1,0:T(8,128)(2,1)S(1)}, u32[]{:S(2)}, u32[]{:S(2)}) collective-permute-start(bf16[32,2176]{1,0:T(8,128)(2,1)S(1)} %get-tuple-element.101), channel_id=1, source_target_pairs={{0,8},{1,9},{2,10},{3,11},{4,12},{5,13},{6,14},{7,15},{8,0},{9,1},... | collective-permute-start | bytes 417800 | tf_op jit(solution)/shard_map/ppermute | solution.py:80
  62.8 1.8 %collective-permute-done.17.refs_1_ = bf16[32,2176]{1,0:T(8,128)(2,1)S(1)} collective-permute-done((bf16[32,2176]{1,0:T(8,128)(2,1)S(1)}, bf16[32,2176]{1,0:T(8,128)(2,1)S(1)}, u32[]{:S(2)}, u32[]{:S(2)}) %collective-permute-start.17) | collective-permute-done | bytes 139296 | tf_op jit(solution)/shard_map/ppermute | solution.py:80
  64.7 2.6 %collective-permute-done.18.refs_2_ = bf16[32,2176]{1,0:T(8,128)(2,1)S(1)} collective-permute-done((bf16[32,2176]{1,0:T(8,128)(2,1)S(1)}, bf16[32,2176]{1,0:T(8,128)(2,1)S(1)}, u32[]{:S(2)}, u32[]{:S(2)}) %collective-permute-start.18) | collective-permute-done | bytes 139296 | tf_op jit(solution)/shard_map/ppermute | solution.py:80
  67.2 3.0 %collective-permute-done.19.refs_3_ = bf16[32,2176]{1,0:T(8,128)(2,1)S(1)} collective-permute-done((bf16[32,2176]{1,0:T(8,128)(2,1)S(1)}, bf16[32,2176]{1,0:T(8,128)(2,1)S(1)}, u32[]{:S(2)}, u32[]{:S(2)}) %collective-permute-start.19) | collective-permute-done | bytes 139296 | tf_op jit(solution)/shard_map/ppermute | solution.py:80
  71.1 0.9 %share.1 = (f32[32,2048]{1,0:T(8,128)}, f32[32,2048]{1,0:T(8,128)}) custom-call(f32[2,8,2176]{2,1,0:T(8,128)S(1)} %combine.14.refs_2_.refs_0_, f32[2,8,2176]{2,1,0:T(8,128)S(1)} %get-tuple-element.85.refs_2_.refs_1_, f32[2,8,2176]{2,1,0:T(8,128)S(1)} %get-tuple-element.98.refs_4_.refs_2_, bf16[32,2176]{1,0:T(8,128)(2,1)S(1)} %collective-permute-done.24.refs_3_), custom_call_target="tpu_custom_call" | custom-call | flops 110000000 | tf_op jit(solution)/shard_map/share/pallas_call | solution.py:378
  72.0 4.2 %collective-permute-done.23.came_ref = bf16[16,2176]{1,0:T(8,128)(2,1)S(1)} collective-permute-done((bf16[16,2176]{1,0:T(8,128)(2,1)S(1)}, bf16[16,2176]{1,0:T(8,128)(2,1)S(1)}, u32[]{:S(2)}, u32[]{:S(2)}) %collective-permute-start.23) | collective-permute-done | bytes 69664 | tf_op jit(solution)/shard_map/ppermute | solution.py:80
  76.2 0.8 %finish.1 = (f32[32,2048]{1,0:T(8,128)}, f32[32,2048]{1,0:T(8,128)}) custom-call(f32[2,8,2176]{2,1,0:T(8,128)S(1)} %get-tuple-element.99.keep_ref, bf16[16,2176]{1,0:T(8,128)(2,1)S(1)} %collective-permute-done.23.came_ref, f32[32,2048]{1,0:T(8,128)} %get-tuple-element.102.refs_0_, ...), custom_call_target="tpu_custom_call", output_to_operand_aliasing={{0}: (2, {}), {1}: (3, {})} | custom-call | flops 110000000 | tf_op jit(solution)/shard_map/finish/pallas_call | solution.py:402
  (36 shorter events, 7.0 us)
Async XLA Ops:
  1.9 15.8 %collective-permute-start.1 = (bf16[2,128,1024]{2,1,0:T(8,128)(2,1)S(1)}, bf16[2,128,1024]{2,1,0:T(8,128)(2,1)S(1)}, u32[]{:S(2)}, u32[]{:S(2)}) collective-permute-start(bf16[2,128,1024]{2,1,0:T(8,128)(2,1)S(1)} %get-tuple-element.61), channel_id=1, source_target_pairs={{0,16},{16,0},{1,17},{17,1},{2,18},{18,2},{3,19},{19,3},{4,20},{20... | collective-permute-start | bytes 1572872 | tf_op jit(solution)/shard_map/ppermute | solution.py:80
  6.2 22.7 %collective-permute-start = (bf16[2,128,1024]{2,1,0:T(8,128)(2,1)S(1)}, bf16[2,128,1024]{2,1,0:T(8,128)(2,1)S(1)}, u32[]{:S(2)}, u32[]{:S(2)}) collective-permute-start(bf16[2,128,1024]{2,1,0:T(8,128)(2,1)S(1)} %get-tuple-element.56), channel_id=1, source_target_pairs={{0,16},{16,0},{1,17},{17,1},{2,18},{18,2},{3,19},{19,3},{4,20},{20... | collective-permute-start | bytes 1572872 | tf_op jit(solution)/shard_map/ppermute | solution.py:80
  20.2 2.6 %collective-permute-start.2 = (bf16[64,2176]{1,0:T(8,128)(2,1)S(1)}, bf16[64,2176]{1,0:T(8,128)(2,1)S(1)}, u32[]{:S(2)}, u32[]{:S(2)}) collective-permute-start(bf16[64,2176]{1,0:T(8,128)(2,1)S(1)} %get-tuple-element.64), channel_id=1, source_target_pairs={{0,1},{1,0},{2,3},{3,2},{4,5},{5,4},{6,7},{7,6},{8,9},{9,8},{10,11... | collective-permute-start | bytes 835592 | tf_op jit(solution)/shard_map/ppermute | solution.py:80
  20.3 2.6 %collective-permute-start.3 = (bf16[64,2176]{1,0:T(8,128)(2,1)S(1)}, bf16[64,2176]{1,0:T(8,128)(2,1)S(1)}, u32[]{:S(2)}, u32[]{:S(2)}) collective-permute-start(bf16[64,2176]{1,0:T(8,128)(2,1)S(1)} %get-tuple-element.65), channel_id=1, source_target_pairs={{0,1},{1,0},{2,3},{3,2},{4,5},{5,4},{6,7},{7,6},{8,9},{9,8},{10,11... | collective-permute-start | bytes 835592 | tf_op jit(solution)/shard_map/ppermute | solution.py:80
  20.8 19.4 %collective-permute-start.8 = (bf16[2,128,1024]{2,1,0:T(8,128)(2,1)S(1)}, bf16[2,128,1024]{2,1,0:T(8,128)(2,1)S(1)}, u32[]{:S(2)}, u32[]{:S(2)}) collective-permute-start(bf16[2,128,1024]{2,1,0:T(8,128)(2,1)S(1)} %get-tuple-element.74.rest_0_), channel_id=1, source_target_pairs={{0,16},{16,0},{1,17},{17,1},{2,18},{18,2},{3,19},{19,3},{4,20},{20... | collective-permute-start | bytes 1572872 | tf_op jit(solution)/shard_map/ppermute | solution.py:80
  23.6 8.0 %collective-permute-start.5 = (bf16[32,2176]{1,0:T(8,128)(2,1)S(1)}, bf16[32,2176]{1,0:T(8,128)(2,1)S(1)}, u32[]{:S(2)}, u32[]{:S(2)}) collective-permute-start(bf16[32,2176]{1,0:T(8,128)(2,1)S(1)} %get-tuple-element.69), channel_id=1, source_target_pairs={{0,6},{1,7},{2,4},{3,5},{4,2},{5,3},{6,0},{7,1},{8,14},{9,15},{10,... | collective-permute-start | bytes 417800 | tf_op jit(solution)/shard_map/ppermute | solution.py:80
  26.1 6.9 %collective-permute-start.6 = (bf16[32,2176]{1,0:T(8,128)(2,1)S(1)}, bf16[32,2176]{1,0:T(8,128)(2,1)S(1)}, u32[]{:S(2)}, u32[]{:S(2)}) collective-permute-start(bf16[32,2176]{1,0:T(8,128)(2,1)S(1)} %get-tuple-element.70), channel_id=1, source_target_pairs={{0,2},{1,3},{2,0},{3,1},{4,6},{5,7},{6,4},{7,5},{8,10},{9,11},{10,... | collective-permute-start | bytes 417800 | tf_op jit(solution)/shard_map/ppermute | solution.py:80
  26.7 8.0 %collective-permute-start.7 = (bf16[32,2176]{1,0:T(8,128)(2,1)S(1)}, bf16[32,2176]{1,0:T(8,128)(2,1)S(1)}, u32[]{:S(2)}, u32[]{:S(2)}) collective-permute-start(bf16[32,2176]{1,0:T(8,128)(2,1)S(1)} %get-tuple-element.71), channel_id=1, source_target_pairs={{0,4},{1,5},{2,6},{3,7},{4,0},{5,1},{6,2},{7,3},{8,12},{9,13},{10,... | collective-permute-start | bytes 417800 | tf_op jit(solution)/shard_map/ppermute | solution.py:80
  31.5 3.6 %collective-permute-start.9 = (bf16[64,2176]{1,0:T(8,128)(2,1)S(1)}, bf16[64,2176]{1,0:T(8,128)(2,1)S(1)}, u32[]{:S(2)}, u32[]{:S(2)}) collective-permute-start(bf16[64,2176]{1,0:T(8,128)(2,1)S(1)} %get-tuple-element.75), channel_id=1, source_target_pairs={{0,1},{1,0},{2,3},{3,2},{4,5},{5,4},{6,7},{7,6},{8,9},{9,8},{10,11... | collective-permute-start | bytes 835592 | tf_op jit(solution)/shard_map/ppermute | solution.py:80
  31.6 3.5 %collective-permute-start.10 = (bf16[64,2176]{1,0:T(8,128)(2,1)S(1)}, bf16[64,2176]{1,0:T(8,128)(2,1)S(1)}, u32[]{:S(2)}, u32[]{:S(2)}) collective-permute-start(bf16[64,2176]{1,0:T(8,128)(2,1)S(1)} %get-tuple-element.76), channel_id=1, source_target_pairs={{0,1},{1,0},{2,3},{3,2},{4,5},{5,4},{6,7},{7,6},{8,9},{9,8},{10,11... | collective-permute-start | bytes 835592 | tf_op jit(solution)/shard_map/ppermute | solution.py:80
  33.0 19.1 %collective-permute-start.4 = (bf16[2,128,1024]{2,1,0:T(8,128)(2,1)S(1)}, bf16[2,128,1024]{2,1,0:T(8,128)(2,1)S(1)}, u32[]{:S(2)}, u32[]{:S(2)}) collective-permute-start(bf16[2,128,1024]{2,1,0:T(8,128)(2,1)S(1)} %get-tuple-element.68.rest_1_), channel_id=1, source_target_pairs={{0,16},{16,0},{1,17},{17,1},{2,18},{18,2},{3,19},{19,3},{4,20},{20... | collective-permute-start | bytes 1572872 | tf_op jit(solution)/shard_map/ppermute | solution.py:80
  35.8 10.1 %collective-permute-start.12 = (bf16[32,2176]{1,0:T(8,128)(2,1)S(1)}, bf16[32,2176]{1,0:T(8,128)(2,1)S(1)}, u32[]{:S(2)}, u32[]{:S(2)}) collective-permute-start(bf16[32,2176]{1,0:T(8,128)(2,1)S(1)} %get-tuple-element.82), channel_id=1, source_target_pairs={{0,6},{1,7},{2,4},{3,5},{4,2},{5,3},{6,0},{7,1},{8,14},{9,15},{10,... | collective-permute-start | bytes 417800 | tf_op jit(solution)/shard_map/ppermute | solution.py:80
  37.8 8.1 %collective-permute-start.13 = (bf16[32,2176]{1,0:T(8,128)(2,1)S(1)}, bf16[32,2176]{1,0:T(8,128)(2,1)S(1)}, u32[]{:S(2)}, u32[]{:S(2)}) collective-permute-start(bf16[32,2176]{1,0:T(8,128)(2,1)S(1)} %get-tuple-element.83), channel_id=1, source_target_pairs={{0,2},{1,3},{2,0},{3,1},{4,6},{5,7},{6,4},{7,5},{8,10},{9,11},{10,... | collective-permute-start | bytes 417800 | tf_op jit(solution)/shard_map/ppermute | solution.py:80
  38.9 7.0 %collective-permute-start.14 = (bf16[32,2176]{1,0:T(8,128)(2,1)S(1)}, bf16[32,2176]{1,0:T(8,128)(2,1)S(1)}, u32[]{:S(2)}, u32[]{:S(2)}) collective-permute-start(bf16[32,2176]{1,0:T(8,128)(2,1)S(1)} %get-tuple-element.84), channel_id=1, source_target_pairs={{0,4},{1,5},{2,6},{3,7},{4,0},{5,1},{6,2},{7,3},{8,12},{9,13},{10,... | collective-permute-start | bytes 417800 | tf_op jit(solution)/shard_map/ppermute | solution.py:80
  42.7 12.2 %collective-permute-start.16 = (bf16[16,2176]{1,0:T(8,128)(2,1)S(1)}, bf16[16,2176]{1,0:T(8,128)(2,1)S(1)}, u32[]{:S(2)}, u32[]{:S(2)}) collective-permute-start(bf16[16,2176]{1,0:T(8,128)(2,1)S(1)} %get-tuple-element.89), channel_id=1, source_target_pairs={{0,8},{1,9},{2,10},{3,11},{4,12},{5,13},{6,14},{7,15},{8,0},{9,1},... | collective-permute-start | bytes 208904 | tf_op jit(solution)/shard_map/ppermute | solution.py:80
  45.9 2.0 %collective-permute-start.11 = (bf16[128,2176]{1,0:T(8,128)(2,1)S(1)}, bf16[128,2176]{1,0:T(8,128)(2,1)S(1)}, u32[]{:S(2)}, u32[]{:S(2)}) collective-permute-start(bf16[128,2176]{1,0:T(8,128)(2,1)S(1)} %get-tuple-element.81), channel_id=1, source_target_pairs={{0,1},{1,0},{2,3},{3,2},{4,5},{5,4},{6,7},{7,6},{8,9},{9,8},{10,11... | collective-permute-start | bytes 1671176 | tf_op jit(solution)/shard_map/ppermute | solution.py:80
  48.6 12.1 %collective-permute-start.20 = (bf16[32,2176]{1,0:T(8,128)(2,1)S(1)}, bf16[32,2176]{1,0:T(8,128)(2,1)S(1)}, u32[]{:S(2)}, u32[]{:S(2)}) collective-permute-start(bf16[32,2176]{1,0:T(8,128)(2,1)S(1)} %get-tuple-element.94), channel_id=1, source_target_pairs={{0,6},{1,7},{2,4},{3,5},{4,2},{5,3},{6,0},{7,1},{8,14},{9,15},{10,... | collective-permute-start | bytes 417800 | tf_op jit(solution)/shard_map/ppermute | solution.py:80
  51.1 10.0 %collective-permute-start.21 = (bf16[32,2176]{1,0:T(8,128)(2,1)S(1)}, bf16[32,2176]{1,0:T(8,128)(2,1)S(1)}, u32[]{:S(2)}, u32[]{:S(2)}) collective-permute-start(bf16[32,2176]{1,0:T(8,128)(2,1)S(1)} %get-tuple-element.95), channel_id=1, source_target_pairs={{0,2},{1,3},{2,0},{3,1},{4,6},{5,7},{6,4},{7,5},{8,10},{9,11},{10,... | collective-permute-start | bytes 417800 | tf_op jit(solution)/shard_map/ppermute | solution.py:80
  51.7 9.5 %collective-permute-start.22 = (bf16[32,2176]{1,0:T(8,128)(2,1)S(1)}, bf16[32,2176]{1,0:T(8,128)(2,1)S(1)}, u32[]{:S(2)}, u32[]{:S(2)}) collective-permute-start(bf16[32,2176]{1,0:T(8,128)(2,1)S(1)} %get-tuple-element.96), channel_id=1, source_target_pairs={{0,4},{1,5},{2,6},{3,7},{4,0},{5,1},{6,2},{7,3},{8,12},{9,13},{10,... | collective-permute-start | bytes 417800 | tf_op jit(solution)/shard_map/ppermute | solution.py:80
  54.9 2.0 %collective-permute-start.15 = (bf16[128,2176]{1,0:T(8,128)(2,1)S(1)}, bf16[128,2176]{1,0:T(8,128)(2,1)S(1)}, u32[]{:S(2)}, u32[]{:S(2)}) collective-permute-start(bf16[128,2176]{1,0:T(8,128)(2,1)S(1)} %get-tuple-element.88), channel_id=1, source_target_pairs={{0,1},{1,0},{2,3},{3,2},{4,5},{5,4},{6,7},{7,6},{8,9},{9,8},{10,11... | collective-permute-start | bytes 1671176 | tf_op jit(solution)/shard_map/ppermute | solution.py:80
  57.6 7.1 %collective-permute-start.17 = (bf16[32,2176]{1,0:T(8,128)(2,1)S(1)}, bf16[32,2176]{1,0:T(8,128)(2,1)S(1)}, u32[]{:S(2)}, u32[]{:S(2)}) collective-permute-start(bf16[32,2176]{1,0:T(8,128)(2,1)S(1)} %get-tuple-element.91), channel_id=1, source_target_pairs={{0,6},{1,7},{2,4},{3,5},{4,2},{5,3},{6,0},{7,1},{8,14},{9,15},{10,... | collective-permute-start | bytes 417800 | tf_op jit(solution)/shard_map/ppermute | solution.py:80
  60.1 7.1 %collective-permute-start.18 = (bf16[32,2176]{1,0:T(8,128)(2,1)S(1)}, bf16[32,2176]{1,0:T(8,128)(2,1)S(1)}, u32[]{:S(2)}, u32[]{:S(2)}) collective-permute-start(bf16[32,2176]{1,0:T(8,128)(2,1)S(1)} %get-tuple-element.92), channel_id=1, source_target_pairs={{0,2},{1,3},{2,0},{3,1},{4,6},{5,7},{6,4},{7,5},{8,10},{9,11},{10,... | collective-permute-start | bytes 417800 | tf_op jit(solution)/shard_map/ppermute | solution.py:80
  60.7 9.6 %collective-permute-start.19 = (bf16[32,2176]{1,0:T(8,128)(2,1)S(1)}, bf16[32,2176]{1,0:T(8,128)(2,1)S(1)}, u32[]{:S(2)}, u32[]{:S(2)}) collective-permute-start(bf16[32,2176]{1,0:T(8,128)(2,1)S(1)} %get-tuple-element.93), channel_id=1, source_target_pairs={{0,4},{1,5},{2,6},{3,7},{4,0},{5,1},{6,2},{7,3},{8,12},{9,13},{10,... | collective-permute-start | bytes 417800 | tf_op jit(solution)/shard_map/ppermute | solution.py:80
  61.5 9.6 %collective-permute-start.24 = (bf16[32,2176]{1,0:T(8,128)(2,1)S(1)}, bf16[32,2176]{1,0:T(8,128)(2,1)S(1)}, u32[]{:S(2)}, u32[]{:S(2)}) collective-permute-start(bf16[32,2176]{1,0:T(8,128)(2,1)S(1)} %get-tuple-element.101), channel_id=1, source_target_pairs={{0,8},{1,9},{2,10},{3,11},{4,12},{5,13},{6,14},{7,15},{8,0},{9,1},... | collective-permute-start | bytes 417800 | tf_op jit(solution)/shard_map/ppermute | solution.py:80
  70.6 5.5 %collective-permute-start.23 = (bf16[16,2176]{1,0:T(8,128)(2,1)S(1)}, bf16[16,2176]{1,0:T(8,128)(2,1)S(1)}, u32[]{:S(2)}, u32[]{:S(2)}) collective-permute-start(bf16[16,2176]{1,0:T(8,128)(2,1)S(1)} %get-tuple-element.100), channel_id=1, source_target_pairs={{0,8},{1,9},{2,10},{3,11},{4,12},{5,13},{6,14},{7,15},{8,0},{9,1},... | collective-permute-start | bytes 208904 | tf_op jit(solution)/shard_map/ppermute | solution.py:80

commit v17 on v16

--- a/solution.py
+++ b/solution.py
@@ -8,7 +8,7 @@
 from jax.sharding import PartitionSpec as P
 
 PIECES = 4
-GROUPS = ((0,), (1, 2), (3,))
+GROUPS = ((0, 1), (2,), (3,))
 SPLIT = (2, 2, 1, 1)
 BESIDE = (0, 2.3, 6, 6)
 FAR = (0.1, 1.5, 1.5, 1.5)
@@ -452,17 +452,18 @@
         if turn + 2 < pieces:
             part, kept = lax.optimization_barrier((mine[turn + 2], kept))
             theirs.append(swap(part, "virt", 1))
-        if held and turn == pieces - 2:
-            held[0], kept = lax.optimization_barrier((held[0], kept))
-            came.append(swap(held.pop(), "walk", stages[2][0]))
         first = [swap(part, "walk", stages[0][0]) for part in send[0]]
         last = [kept]
         if final:
-            layout = joint_layout(1, 1, came[0].shape[0])
-            _, (keep[0],) = combine([keep[0]], came[:1], layout, 0, last, BESIDE[turn])
-            last = [keep[0]]
+            group = GROUPS[0]
+            layout = joint_layout(len(group), 1, came[0].shape[0] // len(group))
+            _, keeps = combine([keep[piece] for piece in group], came[:1], layout, 0, last, BESIDE[turn])
+            keep.update(zip(group, keeps))
+            last = [keep[group[0]]]
         elif turn:
             carry, last = second_sums(turn - 1, carry, last, BESIDE[turn])
+            if held:
+                came.append(swap(held.pop(), "walk", stages[2][0]))
         layout = first_layout(1, SPLIT[turn], first[0].shape[0])
         sends, (keep[turn],) = combine([kept], first, layout, len(second), last, 0.1, part=2)
         last = [keep[turn]]

time: 77.1 us -> 76.2 us (0.988)
  transfers between devices with their start and end apart: 25 -> 25, of which waited for: 10 -> 11; matrix products, arithmetic and copies ran while one was open for 0% -> 0% of each run, Pallas kernels for 35% -> 36%
where the time goes in v17:
time: 76.2 us; the launch traced here: 76 us
  Pallas kernels  29.3 us (38%)
  starting transfers between devices  26.5 us (35%)
  waiting for transfers between devices  18.8 us (25%)
  between operations  1.47 us (2%)
    ppermute x25, starting transfers between devices, swap(): return lax.ppermute(array, axis, pairs)  26.5 us
    ppermute x25, waiting for transfers between devices, swap(): return lax.ppermute(array, axis, pairs)  18.8 us
    pallas_call x1, Pallas kernels, near_product(): pl.pallas_call(functools.partial(near_kernel, chunk, tile), out_shape=(ja...  10.5 us
    pallas_call x4, Pallas kernels, far_product(): pl.pallas_call(functools.partial(far_kernel, place_weights(stages), count...  10.3 us
    pallas_call x9, Pallas kernels, combine(): pl.pallas_call(functools.partial(combine_kernel, layout, len(after), len(...  4.3 us
    pallas_call x2, Pallas kernels, cut(): pl.pallas_call(cut_kernel, out_shape=(out, out), grid=(1,), in_specs=[blo...  2.55 us
  transfers between devices with their start and end apart: 25, of which 11 were waited for; matrix products, arithmetic and copies ran while one was open for 0% of the time, Pallas kernels for 36%

profile of v17, /device:TPU:0, one launch (start us, length us, event | category | flops | bytes accessed | tf_op | source)
XLA Modules:
  0.0 76.0 jit_solution(1083422833935726290)
XLA Ops:
  0.6 1.3 %cut.3 = (bf16[2,128,1024]{2,1,0:T(8,128)(2,1)S(1)}, bf16[2,128,1024]{2,1,0:T(8,128)(2,1)S(1)}) custom-call(bf16[16,32,1024]{2,1,0:T(8,128)(2,1)} %bitcast.6, bf16[16,32,1024]{2,1,0:T(8,128)(2,1)} %bitcast.9), custom_call_target="tpu_custom_call" | custom-call | flops 110000000 | tf_op jit(solution)/shard_map/cut/pallas_call | solution.py:166
  1.9 3.0 %collective-permute-start.1 = (bf16[2,128,1024]{2,1,0:T(8,128)(2,1)S(1)}, bf16[2,128,1024]{2,1,0:T(8,128)(2,1)S(1)}, u32[]{:S(2)}, u32[]{:S(2)}) collective-permute-start(bf16[2,128,1024]{2,1,0:T(8,128)(2,1)S(1)} %get-tuple-element.61), channel_id=1, source_target_pairs={{0,16},{16,0},{1,17},{17,1},{2,18},{18,2},{3,19},{19,3},{4,20},{20... | collective-permute-start | bytes 1572872 | tf_op jit(solution)/shard_map/ppermute | solution.py:80
  4.9 1.3 %cut.2 = (bf16[2,128,1024]{2,1,0:T(8,128)(2,1)S(1)}, bf16[2,128,1024]{2,1,0:T(8,128)(2,1)S(1)}) custom-call(bf16[16,32,1024]{2,1,0:T(8,128)(2,1)} %bitcast.7, bf16[16,32,1024]{2,1,0:T(8,128)(2,1)} %bitcast.10), custom_call_target="tpu_custom_call" | custom-call | flops 110000000 | tf_op jit(solution)/shard_map/cut/pallas_call | solution.py:166
  7.0 10.5 %near_product.1 = (f32[2,16,32,2048]{3,2,1,0:T(8,128)S(1)}, bf16[1024,2048]{1,0:T(8,128)(2,1)S(1)}, bf16[1024,2048]{1,0:T(8,128)(2,1)S(1)}) custom-call(s32[1]{0:T(128)} %bitcast.virt_ref, s32[1]{0:T(128)} %bitcast.1.me_ref, f32[1]{0:T(128)S(6)} %copy.11.energy_ref, bf16[16,32,1024]{2,1,0:T(8,128)(2,1)} %bitcast.8, bf16[16,32,1024]{2,1,0:T(8,128)(2,1)} %bitcast.11, ...), custom_call_target="tpu_custom_call" | custom-call | flops 9900000256 | tf_op jit(solution)/shard_map/near_product/pallas_call | solution.py:232
  17.7 2.5 %far_product.4 = (bf16[64,2176]{1,0:T(8,128)(2,1)S(1)}, bf16[64,2176]{1,0:T(8,128)(2,1)S(1)}, f32[2,128,2176]{2,1,0:T(8,128)S(1)}) custom-call(s32[1]{0:T(128)} %bitcast.virt_ref, s32[1]{0:T(128)} %bitcast.1.me_ref, f32[1]{0:T(128)S(6)} %copy.11.energy_ref, bf16[2,128,1024]{2,1,0:T(8,128)(2,1)S(1)} %collective-permute-done.1.far_ref, ...), custom_call_target="tpu_custom_call" | custom-call | flops 110000000 | tf_op jit(solution)/shard_map/far_product/pallas_call | solution.py:282
  20.8 2.1 %collective-permute-start.5 = (bf16[2,128,1024]{2,1,0:T(8,128)(2,1)S(1)}, bf16[2,128,1024]{2,1,0:T(8,128)(2,1)S(1)}, u32[]{:S(2)}, u32[]{:S(2)}) collective-permute-start(bf16[2,128,1024]{2,1,0:T(8,128)(2,1)S(1)} %get-tuple-element.69.rest_0_), channel_id=1, source_target_pairs={{0,16},{16,0},{1,17},{17,1},{2,18},{18,2},{3,19},{19,3},{4,20},{20... | collective-permute-start | bytes 1572872 | tf_op jit(solution)/shard_map/ppermute | solution.py:80
  22.9 0.7 combine.9
  23.6 2.6 %collective-permute-start.8 = (bf16[32,2176]{1,0:T(8,128)(2,1)S(1)}, bf16[32,2176]{1,0:T(8,128)(2,1)S(1)}, u32[]{:S(2)}, u32[]{:S(2)}) collective-permute-start(bf16[32,2176]{1,0:T(8,128)(2,1)S(1)} %get-tuple-element.73), channel_id=1, source_target_pairs={{0,6},{1,7},{2,4},{3,5},{4,2},{5,3},{6,0},{7,1},{8,14},{9,15},{10,... | collective-permute-start | bytes 417800 | tf_op jit(solution)/shard_map/ppermute | solution.py:80
  27.1 1.8 %collective-permute-done.far_ref = bf16[2,128,1024]{2,1,0:T(8,128)(2,1)S(1)} collective-permute-done((bf16[2,128,1024]{2,1,0:T(8,128)(2,1)S(1)}, bf16[2,128,1024]{2,1,0:T(8,128)(2,1)S(1)}, u32[]{:S(2)}, u32[]{:S(2)}) %collective-permute-start) | collective-permute-done | bytes 524320 | tf_op jit(solution)/shard_map/ppermute | solution.py:80
  28.9 2.5 %far_product.5 = (bf16[64,2176]{1,0:T(8,128)(2,1)S(1)}, bf16[64,2176]{1,0:T(8,128)(2,1)S(1)}, f32[2,128,2176]{2,1,0:T(8,128)S(1)}) custom-call(s32[1]{0:T(128)} %bitcast.virt_ref, s32[1]{0:T(128)} %bitcast.1.me_ref, f32[1]{0:T(128)S(6)} %copy.11.energy_ref, bf16[2,128,1024]{2,1,0:T(8,128)(2,1)S(1)} %collective-permute-done.far_ref, ...), custom_call_target="tpu_custom_call" | custom-call | flops 1650000000 | tf_op jit(solution)/shard_map/far_product/pallas_call | solution.py:282
  32.0 1.0 %collective-permute-done.9.refs_2_ = bf16[32,2176]{1,0:T(8,128)(2,1)S(1)} collective-permute-done((bf16[32,2176]{1,0:T(8,128)(2,1)S(1)}, bf16[32,2176]{1,0:T(8,128)(2,1)S(1)}, u32[]{:S(2)}, u32[]{:S(2)}) %collective-permute-start.9) | collective-permute-done | bytes 139296 | tf_op jit(solution)/shard_map/ppermute | solution.py:80
  33.0 1.7 %collective-permute-start.4 = (bf16[2,128,1024]{2,1,0:T(8,128)(2,1)S(1)}, bf16[2,128,1024]{2,1,0:T(8,128)(2,1)S(1)}, u32[]{:S(2)}, u32[]{:S(2)}) collective-permute-start(bf16[2,128,1024]{2,1,0:T(8,128)(2,1)S(1)} %get-tuple-element.68.rest_1_), channel_id=1, source_target_pairs={{0,16},{16,0},{1,17},{17,1},{2,18},{18,2},{3,19},{19,3},{4,20},{20... | collective-permute-start | bytes 1572872 | tf_op jit(solution)/shard_map/ppermute | solution.py:80
  35.1 0.7 combine.11
  35.8 2.0 %collective-permute-start.12 = (bf16[32,2176]{1,0:T(8,128)(2,1)S(1)}, bf16[32,2176]{1,0:T(8,128)(2,1)S(1)}, u32[]{:S(2)}, u32[]{:S(2)}) collective-permute-start(bf16[32,2176]{1,0:T(8,128)(2,1)S(1)} %get-tuple-element.80), channel_id=1, source_target_pairs={{0,6},{1,7},{2,4},{3,5},{4,2},{5,3},{6,0},{7,1},{8,14},{9,15},{10,... | collective-permute-start | bytes 417800 | tf_op jit(solution)/shard_map/ppermute | solution.py:80
  37.8 1.1 %collective-permute-start.13 = (bf16[32,2176]{1,0:T(8,128)(2,1)S(1)}, bf16[32,2176]{1,0:T(8,128)(2,1)S(1)}, u32[]{:S(2)}, u32[]{:S(2)}) collective-permute-start(bf16[32,2176]{1,0:T(8,128)(2,1)S(1)} %get-tuple-element.81), channel_id=1, source_target_pairs={{0,2},{1,3},{2,0},{3,1},{4,6},{5,7},{6,4},{7,5},{8,10},{9,11},{10,... | collective-permute-start | bytes 417800 | tf_op jit(solution)/shard_map/ppermute | solution.py:80
  39.3 0.8 %collective-permute-done.5.far_ref = bf16[2,128,1024]{2,1,0:T(8,128)(2,1)S(1)} collective-permute-done((bf16[2,128,1024]{2,1,0:T(8,128)(2,1)S(1)}, bf16[2,128,1024]{2,1,0:T(8,128)(2,1)S(1)}, u32[]{:S(2)}, u32[]{:S(2)}) %collective-permute-start.5) | collective-permute-done | bytes 524320 | tf_op jit(solution)/shard_map/ppermute | solution.py:80
  40.2 2.5 %far_product.6 = (bf16[128,2176]{1,0:T(8,128)(2,1)S(1)}, f32[2,128,2176]{2,1,0:T(8,128)S(1)}) custom-call(s32[1]{0:T(128)} %bitcast.virt_ref, s32[1]{0:T(128)} %bitcast.1.me_ref, f32[1]{0:T(128)S(6)} %copy.11.energy_ref, bf16[2,128,1024]{2,1,0:T(8,128)(2,1)S(1)} %collective-permute-done.5.far_ref, f32[2,16,32,2048]{3,2,1,0:T(8,128)S(1)} %get-tuple-element.58.near_ref, ...), custom_call_target="tpu_custom_call" | custom-call | flops 1650000000 | tf_op jit(solution)/shard_map/far_product/pallas_call | solution.py:282
  43.1 2.0 %collective-permute-done.13.refs_2_ = bf16[32,2176]{1,0:T(8,128)(2,1)S(1)} collective-permute-done((bf16[32,2176]{1,0:T(8,128)(2,1)S(1)}, bf16[32,2176]{1,0:T(8,128)(2,1)S(1)}, u32[]{:S(2)}, u32[]{:S(2)}) %collective-permute-start.13) | collective-permute-done | bytes 139296 | tf_op jit(solution)/shard_map/ppermute | solution.py:80
  45.4 2.7 %collective-permute-start.16 = (bf16[32,2176]{1,0:T(8,128)(2,1)S(1)}, bf16[32,2176]{1,0:T(8,128)(2,1)S(1)}, u32[]{:S(2)}, u32[]{:S(2)}) collective-permute-start(bf16[32,2176]{1,0:T(8,128)(2,1)S(1)} %get-tuple-element.88), channel_id=1, source_target_pairs={{0,8},{1,9},{2,10},{3,11},{4,12},{5,13},{6,14},{7,15},{8,0},{9,1},... | collective-permute-start | bytes 417800 | tf_op jit(solution)/shard_map/ppermute | solution.py:80
  48.8 1.8 %collective-permute-start.20 = (bf16[32,2176]{1,0:T(8,128)(2,1)S(1)}, bf16[32,2176]{1,0:T(8,128)(2,1)S(1)}, u32[]{:S(2)}, u32[]{:S(2)}) collective-permute-start(bf16[32,2176]{1,0:T(8,128)(2,1)S(1)} %get-tuple-element.94), channel_id=1, source_target_pairs={{0,6},{1,7},{2,4},{3,5},{4,2},{5,3},{6,0},{7,1},{8,14},{9,15},{10,... | collective-permute-start | bytes 417800 | tf_op jit(solution)/shard_map/ppermute | solution.py:80
  50.6 1.3 %collective-permute-start.21 = (bf16[32,2176]{1,0:T(8,128)(2,1)S(1)}, bf16[32,2176]{1,0:T(8,128)(2,1)S(1)}, u32[]{:S(2)}, u32[]{:S(2)}) collective-permute-start(bf16[32,2176]{1,0:T(8,128)(2,1)S(1)} %get-tuple-element.95), channel_id=1, source_target_pairs={{0,2},{1,3},{2,0},{3,1},{4,6},{5,7},{6,4},{7,5},{8,10},{9,11},{10,... | collective-permute-start | bytes 417800 | tf_op jit(solution)/shard_map/ppermute | solution.py:80
  52.3 2.7 %far_product.7 = (bf16[128,2176]{1,0:T(8,128)(2,1)S(1)}, f32[2,128,2176]{2,1,0:T(8,128)S(1)}) custom-call(s32[1]{0:T(128)} %bitcast.virt_ref, s32[1]{0:T(128)} %bitcast.1.me_ref, f32[1]{0:T(128)S(6)} %copy.11.energy_ref, bf16[2,128,1024]{2,1,0:T(8,128)(2,1)S(1)} %collective-permute-done.4.far_ref, f32[2,16,32,2048]{3,2,1,0:T(8,128)S(1)} %get-tuple-element.58.near_ref, ...), custom_call_target="tpu_custom_call" | custom-call | flops 1650000000 | tf_op jit(solution)/shard_map/far_product/pallas_call | solution.py:282
  55.3 1.8 %collective-permute-done.15.refs_1_ = bf16[128,2176]{1,0:T(8,128)(2,1)S(1)} collective-permute-done((bf16[128,2176]{1,0:T(8,128)(2,1)S(1)}, bf16[128,2176]{1,0:T(8,128)(2,1)S(1)}, u32[]{:S(2)}, u32[]{:S(2)}) %collective-permute-start.15) | collective-permute-done | bytes 557088 | tf_op jit(solution)/shard_map/ppermute | solution.py:80
  57.8 1.8 %collective-permute-start.17 = (bf16[32,2176]{1,0:T(8,128)(2,1)S(1)}, bf16[32,2176]{1,0:T(8,128)(2,1)S(1)}, u32[]{:S(2)}, u32[]{:S(2)}) collective-permute-start(bf16[32,2176]{1,0:T(8,128)(2,1)S(1)} %get-tuple-element.91), channel_id=1, source_target_pairs={{0,6},{1,7},{2,4},{3,5},{4,2},{5,3},{6,0},{7,1},{8,14},{9,15},{10,... | collective-permute-start | bytes 417800 | tf_op jit(solution)/shard_map/ppermute | solution.py:80
  59.6 1.3 %collective-permute-start.18 = (bf16[32,2176]{1,0:T(8,128)(2,1)S(1)}, bf16[32,2176]{1,0:T(8,128)(2,1)S(1)}, u32[]{:S(2)}, u32[]{:S(2)}) collective-permute-start(bf16[32,2176]{1,0:T(8,128)(2,1)S(1)} %get-tuple-element.92), channel_id=1, source_target_pairs={{0,2},{1,3},{2,0},{3,1},{4,6},{5,7},{6,4},{7,5},{8,10},{9,11},{10,... | collective-permute-start | bytes 417800 | tf_op jit(solution)/shard_map/ppermute | solution.py:80
  61.7 1.1 %collective-permute-start.24 = (bf16[16,2176]{1,0:T(8,128)(2,1)S(1)}, bf16[16,2176]{1,0:T(8,128)(2,1)S(1)}, u32[]{:S(2)}, u32[]{:S(2)}) collective-permute-start(bf16[16,2176]{1,0:T(8,128)(2,1)S(1)} %get-tuple-element.101), channel_id=1, source_target_pairs={{0,8},{1,9},{2,10},{3,11},{4,12},{5,13},{6,14},{7,15},{8,0},{9,1},... | collective-permute-start | bytes 208904 | tf_op jit(solution)/shard_map/ppermute | solution.py:80
  62.8 2.4 %collective-permute-done.17.refs_1_ = bf16[32,2176]{1,0:T(8,128)(2,1)S(1)} collective-permute-done((bf16[32,2176]{1,0:T(8,128)(2,1)S(1)}, bf16[32,2176]{1,0:T(8,128)(2,1)S(1)}, u32[]{:S(2)}, u32[]{:S(2)}) %collective-permute-start.17) | collective-permute-done | bytes 139296 | tf_op jit(solution)/shard_map/ppermute | solution.py:80
  65.3 2.2 %collective-permute-done.18.refs_2_ = bf16[32,2176]{1,0:T(8,128)(2,1)S(1)} collective-permute-done((bf16[32,2176]{1,0:T(8,128)(2,1)S(1)}, bf16[32,2176]{1,0:T(8,128)(2,1)S(1)}, u32[]{:S(2)}, u32[]{:S(2)}) %collective-permute-start.18) | collective-permute-done | bytes 139296 | tf_op jit(solution)/shard_map/ppermute | solution.py:80
  67.5 1.5 %collective-permute-done.19.refs_3_ = bf16[32,2176]{1,0:T(8,128)(2,1)S(1)} collective-permute-done((bf16[32,2176]{1,0:T(8,128)(2,1)S(1)}, bf16[32,2176]{1,0:T(8,128)(2,1)S(1)}, u32[]{:S(2)}, u32[]{:S(2)}) %collective-permute-start.19) | collective-permute-done | bytes 139296 | tf_op jit(solution)/shard_map/ppermute | solution.py:80
  69.7 0.8 %share.1 = (f32[32,2048]{1,0:T(8,128)}, f32[32,2048]{1,0:T(8,128)}) custom-call(f32[2,8,2176]{2,1,0:T(8,128)S(1)} %get-tuple-element.89.refs_2_.refs_0_, f32[2,8,2176]{2,1,0:T(8,128)S(1)} %get-tuple-element.100.refs_1_, f32[2,8,2176]{2,1,0:T(8,128)S(1)} %get-tuple-element.97.refs_4_.refs_2_, bf16[16,2176]{1,0:T(8,128)(2,1)S(1)} %collective-permute-done.24.refs_3_), custom_call_target="tpu_custom_call" | custom-call | flops 110000000 | tf_op jit(solution)/shard_map/share/pallas_call | solution.py:378
  70.6 4.6 %collective-permute-done.23.came_ref = bf16[16,2176]{1,0:T(8,128)(2,1)S(1)} collective-permute-done((bf16[16,2176]{1,0:T(8,128)(2,1)S(1)}, bf16[16,2176]{1,0:T(8,128)(2,1)S(1)}, u32[]{:S(2)}, u32[]{:S(2)}) %collective-permute-start.23) | collective-permute-done | bytes 69664 | tf_op jit(solution)/shard_map/ppermute | solution.py:80
  75.2 0.8 %finish.1 = (f32[32,2048]{1,0:T(8,128)}, f32[32,2048]{1,0:T(8,128)}) custom-call(f32[2,8,2176]{2,1,0:T(8,128)S(1)} %get-tuple-element.98.keep_ref, bf16[16,2176]{1,0:T(8,128)(2,1)S(1)} %collective-permute-done.23.came_ref, f32[32,2048]{1,0:T(8,128)} %get-tuple-element.102.refs_0_, ...), custom_call_target="tpu_custom_call", output_to_operand_aliasing={{0}: (2, {}), {1}: (3, {})} | custom-call | flops 110000000 | tf_op jit(solution)/shard_map/finish/pallas_call | solution.py:402
  (36 shorter events, 7.7 us)
Async XLA Ops:
  1.9 15.8 %collective-permute-start.1 = (bf16[2,128,1024]{2,1,0:T(8,128)(2,1)S(1)}, bf16[2,128,1024]{2,1,0:T(8,128)(2,1)S(1)}, u32[]{:S(2)}, u32[]{:S(2)}) collective-permute-start(bf16[2,128,1024]{2,1,0:T(8,128)(2,1)S(1)} %get-tuple-element.61), channel_id=1, source_target_pairs={{0,16},{16,0},{1,17},{17,1},{2,18},{18,2},{3,19},{19,3},{4,20},{20... | collective-permute-start | bytes 1572872 | tf_op jit(solution)/shard_map/ppermute | solution.py:80
  6.2 22.7 %collective-permute-start = (bf16[2,128,1024]{2,1,0:T(8,128)(2,1)S(1)}, bf16[2,128,1024]{2,1,0:T(8,128)(2,1)S(1)}, u32[]{:S(2)}, u32[]{:S(2)}) collective-permute-start(bf16[2,128,1024]{2,1,0:T(8,128)(2,1)S(1)} %get-tuple-element.56), channel_id=1, source_target_pairs={{0,16},{16,0},{1,17},{17,1},{2,18},{18,2},{3,19},{19,3},{4,20},{20... | collective-permute-start | bytes 1572872 | tf_op jit(solution)/shard_map/ppermute | solution.py:80
  20.2 2.6 %collective-permute-start.2 = (bf16[64,2176]{1,0:T(8,128)(2,1)S(1)}, bf16[64,2176]{1,0:T(8,128)(2,1)S(1)}, u32[]{:S(2)}, u32[]{:S(2)}) collective-permute-start(bf16[64,2176]{1,0:T(8,128)(2,1)S(1)} %get-tuple-element.64), channel_id=1, source_target_pairs={{0,1},{1,0},{2,3},{3,2},{4,5},{5,4},{6,7},{7,6},{8,9},{9,8},{10,11... | collective-permute-start | bytes 835592 | tf_op jit(solution)/shard_map/ppermute | solution.py:80
  20.3 2.6 %collective-permute-start.3 = (bf16[64,2176]{1,0:T(8,128)(2,1)S(1)}, bf16[64,2176]{1,0:T(8,128)(2,1)S(1)}, u32[]{:S(2)}, u32[]{:S(2)}) collective-permute-start(bf16[64,2176]{1,0:T(8,128)(2,1)S(1)} %get-tuple-element.65), channel_id=1, source_target_pairs={{0,1},{1,0},{2,3},{3,2},{4,5},{5,4},{6,7},{7,6},{8,9},{9,8},{10,11... | collective-permute-start | bytes 835592 | tf_op jit(solution)/shard_map/ppermute | solution.py:80
  20.8 19.4 %collective-permute-start.5 = (bf16[2,128,1024]{2,1,0:T(8,128)(2,1)S(1)}, bf16[2,128,1024]{2,1,0:T(8,128)(2,1)S(1)}, u32[]{:S(2)}, u32[]{:S(2)}) collective-permute-start(bf16[2,128,1024]{2,1,0:T(8,128)(2,1)S(1)} %get-tuple-element.69.rest_0_), channel_id=1, source_target_pairs={{0,16},{16,0},{1,17},{17,1},{2,18},{18,2},{3,19},{19,3},{4,20},{20... | collective-permute-start | bytes 1572872 | tf_op jit(solution)/shard_map/ppermute | solution.py:80
  23.6 8.0 %collective-permute-start.8 = (bf16[32,2176]{1,0:T(8,128)(2,1)S(1)}, bf16[32,2176]{1,0:T(8,128)(2,1)S(1)}, u32[]{:S(2)}, u32[]{:S(2)}) collective-permute-start(bf16[32,2176]{1,0:T(8,128)(2,1)S(1)} %get-tuple-element.73), channel_id=1, source_target_pairs={{0,6},{1,7},{2,4},{3,5},{4,2},{5,3},{6,0},{7,1},{8,14},{9,15},{10,... | collective-permute-start | bytes 417800 | tf_op jit(solution)/shard_map/ppermute | solution.py:80
  26.1 6.9 %collective-permute-start.9 = (bf16[32,2176]{1,0:T(8,128)(2,1)S(1)}, bf16[32,2176]{1,0:T(8,128)(2,1)S(1)}, u32[]{:S(2)}, u32[]{:S(2)}) collective-permute-start(bf16[32,2176]{1,0:T(8,128)(2,1)S(1)} %get-tuple-element.74), channel_id=1, source_target_pairs={{0,2},{1,3},{2,0},{3,1},{4,6},{5,7},{6,4},{7,5},{8,10},{9,11},{10,... | collective-permute-start | bytes 417800 | tf_op jit(solution)/shard_map/ppermute | solution.py:80
  26.7 8.0 %collective-permute-start.10 = (bf16[32,2176]{1,0:T(8,128)(2,1)S(1)}, bf16[32,2176]{1,0:T(8,128)(2,1)S(1)}, u32[]{:S(2)}, u32[]{:S(2)}) collective-permute-start(bf16[32,2176]{1,0:T(8,128)(2,1)S(1)} %get-tuple-element.75), channel_id=1, source_target_pairs={{0,4},{1,5},{2,6},{3,7},{4,0},{5,1},{6,2},{7,3},{8,12},{9,13},{10,... | collective-permute-start | bytes 417800 | tf_op jit(solution)/shard_map/ppermute | solution.py:80
  31.5 3.6 %collective-permute-start.6 = (bf16[64,2176]{1,0:T(8,128)(2,1)S(1)}, bf16[64,2176]{1,0:T(8,128)(2,1)S(1)}, u32[]{:S(2)}, u32[]{:S(2)}) collective-permute-start(bf16[64,2176]{1,0:T(8,128)(2,1)S(1)} %get-tuple-element.71), channel_id=1, source_target_pairs={{0,1},{1,0},{2,3},{3,2},{4,5},{5,4},{6,7},{7,6},{8,9},{9,8},{10,11... | collective-permute-start | bytes 835592 | tf_op jit(solution)/shard_map/ppermute | solution.py:80
  31.6 3.5 %collective-permute-start.7 = (bf16[64,2176]{1,0:T(8,128)(2,1)S(1)}, bf16[64,2176]{1,0:T(8,128)(2,1)S(1)}, u32[]{:S(2)}, u32[]{:S(2)}) collective-permute-start(bf16[64,2176]{1,0:T(8,128)(2,1)S(1)} %get-tuple-element.72), channel_id=1, source_target_pairs={{0,1},{1,0},{2,3},{3,2},{4,5},{5,4},{6,7},{7,6},{8,9},{9,8},{10,11... | collective-permute-start | bytes 835592 | tf_op jit(solution)/shard_map/ppermute | solution.py:80
  33.0 19.3 %collective-permute-start.4 = (bf16[2,128,1024]{2,1,0:T(8,128)(2,1)S(1)}, bf16[2,128,1024]{2,1,0:T(8,128)(2,1)S(1)}, u32[]{:S(2)}, u32[]{:S(2)}) collective-permute-start(bf16[2,128,1024]{2,1,0:T(8,128)(2,1)S(1)} %get-tuple-element.68.rest_1_), channel_id=1, source_target_pairs={{0,16},{16,0},{1,17},{17,1},{2,18},{18,2},{3,19},{19,3},{4,20},{20... | collective-permute-start | bytes 1572872 | tf_op jit(solution)/shard_map/ppermute | solution.py:80
  35.8 7.3 %collective-permute-start.12 = (bf16[32,2176]{1,0:T(8,128)(2,1)S(1)}, bf16[32,2176]{1,0:T(8,128)(2,1)S(1)}, u32[]{:S(2)}, u32[]{:S(2)}) collective-permute-start(bf16[32,2176]{1,0:T(8,128)(2,1)S(1)} %get-tuple-element.80), channel_id=1, source_target_pairs={{0,6},{1,7},{2,4},{3,5},{4,2},{5,3},{6,0},{7,1},{8,14},{9,15},{10,... | collective-permute-start | bytes 417800 | tf_op jit(solution)/shard_map/ppermute | solution.py:80
  37.8 7.3 %collective-permute-start.13 = (bf16[32,2176]{1,0:T(8,128)(2,1)S(1)}, bf16[32,2176]{1,0:T(8,128)(2,1)S(1)}, u32[]{:S(2)}, u32[]{:S(2)}) collective-permute-start(bf16[32,2176]{1,0:T(8,128)(2,1)S(1)} %get-tuple-element.81), channel_id=1, source_target_pairs={{0,2},{1,3},{2,0},{3,1},{4,6},{5,7},{6,4},{7,5},{8,10},{9,11},{10,... | collective-permute-start | bytes 417800 | tf_op jit(solution)/shard_map/ppermute | solution.py:80
  38.9 6.2 %collective-permute-start.14 = (bf16[32,2176]{1,0:T(8,128)(2,1)S(1)}, bf16[32,2176]{1,0:T(8,128)(2,1)S(1)}, u32[]{:S(2)}, u32[]{:S(2)}) collective-permute-start(bf16[32,2176]{1,0:T(8,128)(2,1)S(1)} %get-tuple-element.82), channel_id=1, source_target_pairs={{0,4},{1,5},{2,6},{3,7},{4,0},{5,1},{6,2},{7,3},{8,12},{9,13},{10,... | collective-permute-start | bytes 417800 | tf_op jit(solution)/shard_map/ppermute | solution.py:80
  42.7 5.4 %collective-permute-start.11 = (bf16[128,2176]{1,0:T(8,128)(2,1)S(1)}, bf16[128,2176]{1,0:T(8,128)(2,1)S(1)}, u32[]{:S(2)}, u32[]{:S(2)}) collective-permute-start(bf16[128,2176]{1,0:T(8,128)(2,1)S(1)} %get-tuple-element.79), channel_id=1, source_target_pairs={{0,1},{1,0},{2,3},{3,2},{4,5},{5,4},{6,7},{7,6},{8,9},{9,8},{10,11... | collective-permute-start | bytes 1671176 | tf_op jit(solution)/shard_map/ppermute | solution.py:80
  45.4 9.7 %collective-permute-start.16 = (bf16[32,2176]{1,0:T(8,128)(2,1)S(1)}, bf16[32,2176]{1,0:T(8,128)(2,1)S(1)}, u32[]{:S(2)}, u32[]{:S(2)}) collective-permute-start(bf16[32,2176]{1,0:T(8,128)(2,1)S(1)} %get-tuple-element.88), channel_id=1, source_target_pairs={{0,8},{1,9},{2,10},{3,11},{4,12},{5,13},{6,14},{7,15},{8,0},{9,1},... | collective-permute-start | bytes 417800 | tf_op jit(solution)/shard_map/ppermute | solution.py:80
  48.8 12.1 %collective-permute-start.20 = (bf16[32,2176]{1,0:T(8,128)(2,1)S(1)}, bf16[32,2176]{1,0:T(8,128)(2,1)S(1)}, u32[]{:S(2)}, u32[]{:S(2)}) collective-permute-start(bf16[32,2176]{1,0:T(8,128)(2,1)S(1)} %get-tuple-element.94), channel_id=1, source_target_pairs={{0,6},{1,7},{2,4},{3,5},{4,2},{5,3},{6,0},{7,1},{8,14},{9,15},{10,... | collective-permute-start | bytes 417800 | tf_op jit(solution)/shard_map/ppermute | solution.py:80
  50.6 10.8 %collective-permute-start.21 = (bf16[32,2176]{1,0:T(8,128)(2,1)S(1)}, bf16[32,2176]{1,0:T(8,128)(2,1)S(1)}, u32[]{:S(2)}, u32[]{:S(2)}) collective-permute-start(bf16[32,2176]{1,0:T(8,128)(2,1)S(1)} %get-tuple-element.95), channel_id=1, source_target_pairs={{0,2},{1,3},{2,0},{3,1},{4,6},{5,7},{6,4},{7,5},{8,10},{9,11},{10,... | collective-permute-start | bytes 417800 | tf_op jit(solution)/shard_map/ppermute | solution.py:80
  51.8 9.5 %collective-permute-start.22 = (bf16[32,2176]{1,0:T(8,128)(2,1)S(1)}, bf16[32,2176]{1,0:T(8,128)(2,1)S(1)}, u32[]{:S(2)}, u32[]{:S(2)}) collective-permute-start(bf16[32,2176]{1,0:T(8,128)(2,1)S(1)} %get-tuple-element.96), channel_id=1, source_target_pairs={{0,4},{1,5},{2,6},{3,7},{4,0},{5,1},{6,2},{7,3},{8,12},{9,13},{10,... | collective-permute-start | bytes 417800 | tf_op jit(solution)/shard_map/ppermute | solution.py:80
  55.1 2.0 %collective-permute-start.15 = (bf16[128,2176]{1,0:T(8,128)(2,1)S(1)}, bf16[128,2176]{1,0:T(8,128)(2,1)S(1)}, u32[]{:S(2)}, u32[]{:S(2)}) collective-permute-start(bf16[128,2176]{1,0:T(8,128)(2,1)S(1)} %get-tuple-element.87), channel_id=1, source_target_pairs={{0,1},{1,0},{2,3},{3,2},{4,5},{5,4},{6,7},{7,6},{8,9},{9,8},{10,11... | collective-permute-start | bytes 1671176 | tf_op jit(solution)/shard_map/ppermute | solution.py:80
  57.8 7.5 %collective-permute-start.17 = (bf16[32,2176]{1,0:T(8,128)(2,1)S(1)}, bf16[32,2176]{1,0:T(8,128)(2,1)S(1)}, u32[]{:S(2)}, u32[]{:S(2)}) collective-permute-start(bf16[32,2176]{1,0:T(8,128)(2,1)S(1)} %get-tuple-element.91), channel_id=1, source_target_pairs={{0,6},{1,7},{2,4},{3,5},{4,2},{5,3},{6,0},{7,1},{8,14},{9,15},{10,... | collective-permute-start | bytes 417800 | tf_op jit(solution)/shard_map/ppermute | solution.py:80
  59.6 7.9 %collective-permute-start.18 = (bf16[32,2176]{1,0:T(8,128)(2,1)S(1)}, bf16[32,2176]{1,0:T(8,128)(2,1)S(1)}, u32[]{:S(2)}, u32[]{:S(2)}) collective-permute-start(bf16[32,2176]{1,0:T(8,128)(2,1)S(1)} %get-tuple-element.92), channel_id=1, source_target_pairs={{0,2},{1,3},{2,0},{3,1},{4,6},{5,7},{6,4},{7,5},{8,10},{9,11},{10,... | collective-permute-start | bytes 417800 | tf_op jit(solution)/shard_map/ppermute | solution.py:80
  60.9 8.1 %collective-permute-start.19 = (bf16[32,2176]{1,0:T(8,128)(2,1)S(1)}, bf16[32,2176]{1,0:T(8,128)(2,1)S(1)}, u32[]{:S(2)}, u32[]{:S(2)}) collective-permute-start(bf16[32,2176]{1,0:T(8,128)(2,1)S(1)} %get-tuple-element.93), channel_id=1, source_target_pairs={{0,4},{1,5},{2,6},{3,7},{4,0},{5,1},{6,2},{7,3},{8,12},{9,13},{10,... | collective-permute-start | bytes 417800 | tf_op jit(solution)/shard_map/ppermute | solution.py:80
  61.7 8.0 %collective-permute-start.24 = (bf16[16,2176]{1,0:T(8,128)(2,1)S(1)}, bf16[16,2176]{1,0:T(8,128)(2,1)S(1)}, u32[]{:S(2)}, u32[]{:S(2)}) collective-permute-start(bf16[16,2176]{1,0:T(8,128)(2,1)S(1)} %get-tuple-element.101), channel_id=1, source_target_pairs={{0,8},{1,9},{2,10},{3,11},{4,12},{5,13},{6,14},{7,15},{8,0},{9,1},... | collective-permute-start | bytes 208904 | tf_op jit(solution)/shard_map/ppermute | solution.py:80
  69.4 5.9 %collective-permute-start.23 = (bf16[16,2176]{1,0:T(8,128)(2,1)S(1)}, bf16[16,2176]{1,0:T(8,128)(2,1)S(1)}, u32[]{:S(2)}, u32[]{:S(2)}) collective-permute-start(bf16[16,2176]{1,0:T(8,128)(2,1)S(1)} %get-tuple-element.99), channel_id=1, source_target_pairs={{0,8},{1,9},{2,10},{3,11},{4,12},{5,13},{6,14},{7,15},{8,0},{9,1},... | collective-permute-start | bytes 208904 | tf_op jit(solution)/shard_map/ppermute | solution.py:80

commit v18 on v17

--- a/solution.py
+++ b/solution.py
@@ -9,8 +9,8 @@
 
 PIECES = 4
 GROUPS = ((0, 1), (2,), (3,))
-SPLIT = (2, 2, 1, 1)
-BESIDE = (0, 2.3, 6, 6)
+SPLIT = (2, 1, 1, 1)
+BESIDE = (0, 6, 6, 6)
 FAR = (0.1, 1.5, 1.5, 1.5)
 
 

time: 76.2 us -> 76.8 us (level)
  waiting for transfers between devices: 18.8 us -> 20.8 us
  starting transfers between devices: 26.5 us -> 25.4 us
    ppermute x25 -> x24, waiting for transfers between devices: 18.8 us -> 20.8 us  [swap(): return lax.ppermute(array, axis, pairs)]
    ppermute x25 -> x24, starting transfers between devices: 26.5 us -> 25.4 us  [swap(): return lax.ppermute(array, axis, pairs)]
  transfers between devices with their start and end apart: 25 -> 24, of which waited for: 11 -> 13; matrix products, arithmetic and copies ran while one was open for 0% -> 0% of each run, Pallas kernels for 36% -> 35%
where the time goes in v18:
time: 76.8 us; the launch traced here: 76.7 us
  Pallas kernels  29 us (38%)
  starting transfers between devices  25.4 us (33%)
  waiting for transfers between devices  20.8 us (27%)
  between operations  1.46 us (2%)
    ppermute x24, starting transfers between devices, swap(): return lax.ppermute(array, axis, pairs)  25.4 us
    ppermute x24, waiting for transfers between devices, swap(): return lax.ppermute(array, axis, pairs)  20.8 us
    pallas_call x1, Pallas kernels, near_product(): pl.pallas_call(functools.partial(near_kernel, chunk, tile), out_shape=(ja...  10.5 us
    pallas_call x4, Pallas kernels, far_product(): pl.pallas_call(functools.partial(far_kernel, place_weights(stages), count...  10.1 us
    pallas_call x9, Pallas kernels, combine(): pl.pallas_call(functools.partial(combine_kernel, layout, len(after), len(...  4.3 us
    pallas_call x2, Pallas kernels, cut(): pl.pallas_call(cut_kernel, out_shape=(out, out), grid=(1,), in_specs=[blo...  2.55 us
  transfers between devices with their start and end apart: 24, of which 13 were waited for; matrix products, arithmetic and copies ran while one was open for 0% of the time, Pallas kernels for 35%

profile of v18, /device:TPU:0, one launch (start us, length us, event | category | flops | bytes accessed | tf_op | source)
XLA Modules:
  0.0 76.7 jit_solution(3800960090790480943)
XLA Ops:
  0.6 1.3 %cut.3 = (bf16[2,128,1024]{2,1,0:T(8,128)(2,1)S(1)}, bf16[2,128,1024]{2,1,0:T(8,128)(2,1)S(1)}) custom-call(bf16[16,32,1024]{2,1,0:T(8,128)(2,1)} %bitcast.6, bf16[16,32,1024]{2,1,0:T(8,128)(2,1)} %bitcast.9), custom_call_target="tpu_custom_call" | custom-call | flops 110000000 | tf_op jit(solution)/shard_map/cut/pallas_call | solution.py:166
  1.9 3.0 %collective-permute-start.1 = (bf16[2,128,1024]{2,1,0:T(8,128)(2,1)S(1)}, bf16[2,128,1024]{2,1,0:T(8,128)(2,1)S(1)}, u32[]{:S(2)}, u32[]{:S(2)}) collective-permute-start(bf16[2,128,1024]{2,1,0:T(8,128)(2,1)S(1)} %get-tuple-element.60), channel_id=1, source_target_pairs={{0,16},{16,0},{1,17},{17,1},{2,18},{18,2},{3,19},{19,3},{4,20},{20... | collective-permute-start | bytes 1572872 | tf_op jit(solution)/shard_map/ppermute | solution.py:80
  4.9 1.3 %cut.2 = (bf16[2,128,1024]{2,1,0:T(8,128)(2,1)S(1)}, bf16[2,128,1024]{2,1,0:T(8,128)(2,1)S(1)}) custom-call(bf16[16,32,1024]{2,1,0:T(8,128)(2,1)} %bitcast.7, bf16[16,32,1024]{2,1,0:T(8,128)(2,1)} %bitcast.10), custom_call_target="tpu_custom_call" | custom-call | flops 110000000 | tf_op jit(solution)/shard_map/cut/pallas_call | solution.py:166
  7.0 10.5 %near_product.1 = (f32[2,16,32,2048]{3,2,1,0:T(8,128)S(1)}, bf16[1024,2048]{1,0:T(8,128)(2,1)S(1)}, bf16[1024,2048]{1,0:T(8,128)(2,1)S(1)}) custom-call(s32[1]{0:T(128)} %bitcast.virt_ref, s32[1]{0:T(128)} %bitcast.1.me_ref, f32[1]{0:T(128)S(6)} %copy.11.energy_ref, bf16[16,32,1024]{2,1,0:T(8,128)(2,1)} %bitcast.8, bf16[16,32,1024]{2,1,0:T(8,128)(2,1)} %bitcast.11, ...), custom_call_target="tpu_custom_call" | custom-call | flops 9900000256 | tf_op jit(solution)/shard_map/near_product/pallas_call | solution.py:232
  17.7 2.5 %far_product.4 = (bf16[64,2176]{1,0:T(8,128)(2,1)S(1)}, bf16[64,2176]{1,0:T(8,128)(2,1)S(1)}, f32[2,128,2176]{2,1,0:T(8,128)S(1)}) custom-call(s32[1]{0:T(128)} %bitcast.virt_ref, s32[1]{0:T(128)} %bitcast.1.me_ref, f32[1]{0:T(128)S(6)} %copy.11.energy_ref, bf16[2,128,1024]{2,1,0:T(8,128)(2,1)S(1)} %collective-permute-done.1.far_ref, ...), custom_call_target="tpu_custom_call" | custom-call | flops 110000000 | tf_op jit(solution)/shard_map/far_product/pallas_call | solution.py:282
  20.8 2.1 %collective-permute-start.5 = (bf16[2,128,1024]{2,1,0:T(8,128)(2,1)S(1)}, bf16[2,128,1024]{2,1,0:T(8,128)(2,1)S(1)}, u32[]{:S(2)}, u32[]{:S(2)}) collective-permute-start(bf16[2,128,1024]{2,1,0:T(8,128)(2,1)S(1)} %get-tuple-element.68.rest_0_), channel_id=1, source_target_pairs={{0,16},{16,0},{1,17},{17,1},{2,18},{18,2},{3,19},{19,3},{4,20},{20... | collective-permute-start | bytes 1572872 | tf_op jit(solution)/shard_map/ppermute | solution.py:80
  22.9 0.7 combine.9
  23.6 2.6 %collective-permute-start.7 = (bf16[32,2176]{1,0:T(8,128)(2,1)S(1)}, bf16[32,2176]{1,0:T(8,128)(2,1)S(1)}, u32[]{:S(2)}, u32[]{:S(2)}) collective-permute-start(bf16[32,2176]{1,0:T(8,128)(2,1)S(1)} %get-tuple-element.71), channel_id=1, source_target_pairs={{0,6},{1,7},{2,4},{3,5},{4,2},{5,3},{6,0},{7,1},{8,14},{9,15},{10,... | collective-permute-start | bytes 417800 | tf_op jit(solution)/shard_map/ppermute | solution.py:80
  27.1 1.8 %collective-permute-done.far_ref = bf16[2,128,1024]{2,1,0:T(8,128)(2,1)S(1)} collective-permute-done((bf16[2,128,1024]{2,1,0:T(8,128)(2,1)S(1)}, bf16[2,128,1024]{2,1,0:T(8,128)(2,1)S(1)}, u32[]{:S(2)}, u32[]{:S(2)}) %collective-permute-start) | collective-permute-done | bytes 524320 | tf_op jit(solution)/shard_map/ppermute | solution.py:80
  28.9 2.5 %far_product.5 = (bf16[128,2176]{1,0:T(8,128)(2,1)S(1)}, f32[2,128,2176]{2,1,0:T(8,128)S(1)}) custom-call(s32[1]{0:T(128)} %bitcast.virt_ref, s32[1]{0:T(128)} %bitcast.1.me_ref, f32[1]{0:T(128)S(6)} %copy.11.energy_ref, bf16[2,128,1024]{2,1,0:T(8,128)(2,1)S(1)} %collective-permute-done.far_ref, f32[2,16,32,2048]{3,2,1,0:T(8,128)S(1)} %get-tuple-element.57.near_ref, ...), custom_call_target="tpu_custom_call" | custom-call | flops 1650000000 | tf_op jit(solution)/shard_map/far_product/pallas_call | solution.py:282
  31.5 2.1 %collective-permute-start.4 = (bf16[2,128,1024]{2,1,0:T(8,128)(2,1)S(1)}, bf16[2,128,1024]{2,1,0:T(8,128)(2,1)S(1)}, u32[]{:S(2)}, u32[]{:S(2)}) collective-permute-start(bf16[2,128,1024]{2,1,0:T(8,128)(2,1)S(1)} %get-tuple-element.67.rest_1_), channel_id=1, source_target_pairs={{0,16},{16,0},{1,17},{17,1},{2,18},{18,2},{3,19},{19,3},{4,20},{20... | collective-permute-start | bytes 1572872 | tf_op jit(solution)/shard_map/ppermute | solution.py:80
  34.0 1.6 %collective-permute-done.6.refs_1_ = bf16[128,2176]{1,0:T(8,128)(2,1)S(1)} collective-permute-done((bf16[128,2176]{1,0:T(8,128)(2,1)S(1)}, bf16[128,2176]{1,0:T(8,128)(2,1)S(1)}, u32[]{:S(2)}, u32[]{:S(2)}) %collective-permute-start.6) | collective-permute-done | bytes 557088 | tf_op jit(solution)/shard_map/ppermute | solution.py:80
  35.6 0.7 combine.11
  36.3 2.6 %collective-permute-start.11 = (bf16[32,2176]{1,0:T(8,128)(2,1)S(1)}, bf16[32,2176]{1,0:T(8,128)(2,1)S(1)}, u32[]{:S(2)}, u32[]{:S(2)}) collective-permute-start(bf16[32,2176]{1,0:T(8,128)(2,1)S(1)} %get-tuple-element.78), channel_id=1, source_target_pairs={{0,6},{1,7},{2,4},{3,5},{4,2},{5,3},{6,0},{7,1},{8,14},{9,15},{10,... | collective-permute-start | bytes 417800 | tf_op jit(solution)/shard_map/ppermute | solution.py:80
  40.2 2.5 %far_product.6 = (bf16[128,2176]{1,0:T(8,128)(2,1)S(1)}, f32[2,128,2176]{2,1,0:T(8,128)S(1)}) custom-call(s32[1]{0:T(128)} %bitcast.virt_ref, s32[1]{0:T(128)} %bitcast.1.me_ref, f32[1]{0:T(128)S(6)} %copy.11.energy_ref, bf16[2,128,1024]{2,1,0:T(8,128)(2,1)S(1)} %collective-permute-done.5.far_ref, f32[2,16,32,2048]{3,2,1,0:T(8,128)S(1)} %get-tuple-element.57.near_ref, ...), custom_call_target="tpu_custom_call" | custom-call | flops 1650000000 | tf_op jit(solution)/shard_map/far_product/pallas_call | solution.py:282
  42.8 0.6 collective-permute-done.11.refs_1_
  43.4 2.6 %collective-permute-done.12.refs_2_ = bf16[32,2176]{1,0:T(8,128)(2,1)S(1)} collective-permute-done((bf16[32,2176]{1,0:T(8,128)(2,1)S(1)}, bf16[32,2176]{1,0:T(8,128)(2,1)S(1)}, u32[]{:S(2)}, u32[]{:S(2)}) %collective-permute-start.12) | collective-permute-done | bytes 139296 | tf_op jit(solution)/shard_map/ppermute | solution.py:80
  46.3 2.7 %collective-permute-start.15 = (bf16[32,2176]{1,0:T(8,128)(2,1)S(1)}, bf16[32,2176]{1,0:T(8,128)(2,1)S(1)}, u32[]{:S(2)}, u32[]{:S(2)}) collective-permute-start(bf16[32,2176]{1,0:T(8,128)(2,1)S(1)} %get-tuple-element.86), channel_id=1, source_target_pairs={{0,8},{1,9},{2,10},{3,11},{4,12},{5,13},{6,14},{7,15},{8,0},{9,1},... | collective-permute-start | bytes 417800 | tf_op jit(solution)/shard_map/ppermute | solution.py:80
  49.0 0.7 combine.13
  49.7 1.7 %collective-permute-start.19 = (bf16[32,2176]{1,0:T(8,128)(2,1)S(1)}, bf16[32,2176]{1,0:T(8,128)(2,1)S(1)}, u32[]{:S(2)}, u32[]{:S(2)}) collective-permute-start(bf16[32,2176]{1,0:T(8,128)(2,1)S(1)} %get-tuple-element.92), channel_id=1, source_target_pairs={{0,6},{1,7},{2,4},{3,5},{4,2},{5,3},{6,0},{7,1},{8,14},{9,15},{10,... | collective-permute-start | bytes 417800 | tf_op jit(solution)/shard_map/ppermute | solution.py:80
  51.4 1.4 %collective-permute-start.20 = (bf16[32,2176]{1,0:T(8,128)(2,1)S(1)}, bf16[32,2176]{1,0:T(8,128)(2,1)S(1)}, u32[]{:S(2)}, u32[]{:S(2)}) collective-permute-start(bf16[32,2176]{1,0:T(8,128)(2,1)S(1)} %get-tuple-element.93), channel_id=1, source_target_pairs={{0,2},{1,3},{2,0},{3,1},{4,6},{5,7},{6,4},{7,5},{8,10},{9,11},{10,... | collective-permute-start | bytes 417800 | tf_op jit(solution)/shard_map/ppermute | solution.py:80
  53.3 2.5 %far_product.7 = (bf16[128,2176]{1,0:T(8,128)(2,1)S(1)}, f32[2,128,2176]{2,1,0:T(8,128)S(1)}) custom-call(s32[1]{0:T(128)} %bitcast.virt_ref, s32[1]{0:T(128)} %bitcast.1.me_ref, f32[1]{0:T(128)S(6)} %copy.11.energy_ref, bf16[2,128,1024]{2,1,0:T(8,128)(2,1)S(1)} %collective-permute-done.4.far_ref, f32[2,16,32,2048]{3,2,1,0:T(8,128)S(1)} %get-tuple-element.57.near_ref, ...), custom_call_target="tpu_custom_call" | custom-call | flops 1650000000 | tf_op jit(solution)/shard_map/far_product/pallas_call | solution.py:282
  56.1 1.8 %collective-permute-done.14.refs_1_ = bf16[128,2176]{1,0:T(8,128)(2,1)S(1)} collective-permute-done((bf16[128,2176]{1,0:T(8,128)(2,1)S(1)}, bf16[128,2176]{1,0:T(8,128)(2,1)S(1)}, u32[]{:S(2)}, u32[]{:S(2)}) %collective-permute-start.14) | collective-permute-done | bytes 557088 | tf_op jit(solution)/shard_map/ppermute | solution.py:80
  57.8 0.7 combine.15
  58.5 1.7 %collective-permute-start.16 = (bf16[32,2176]{1,0:T(8,128)(2,1)S(1)}, bf16[32,2176]{1,0:T(8,128)(2,1)S(1)}, u32[]{:S(2)}, u32[]{:S(2)}) collective-permute-start(bf16[32,2176]{1,0:T(8,128)(2,1)S(1)} %get-tuple-element.89), channel_id=1, source_target_pairs={{0,6},{1,7},{2,4},{3,5},{4,2},{5,3},{6,0},{7,1},{8,14},{9,15},{10,... | collective-permute-start | bytes 417800 | tf_op jit(solution)/shard_map/ppermute | solution.py:80
  60.3 1.4 %collective-permute-start.17 = (bf16[32,2176]{1,0:T(8,128)(2,1)S(1)}, bf16[32,2176]{1,0:T(8,128)(2,1)S(1)}, u32[]{:S(2)}, u32[]{:S(2)}) collective-permute-start(bf16[32,2176]{1,0:T(8,128)(2,1)S(1)} %get-tuple-element.90), channel_id=1, source_target_pairs={{0,2},{1,3},{2,0},{3,1},{4,6},{5,7},{6,4},{7,5},{8,10},{9,11},{10,... | collective-permute-start | bytes 417800 | tf_op jit(solution)/shard_map/ppermute | solution.py:80
  62.8 3.2 %collective-permute-done.16.refs_1_ = bf16[32,2176]{1,0:T(8,128)(2,1)S(1)} collective-permute-done((bf16[32,2176]{1,0:T(8,128)(2,1)S(1)}, bf16[32,2176]{1,0:T(8,128)(2,1)S(1)}, u32[]{:S(2)}, u32[]{:S(2)}) %collective-permute-start.16) | collective-permute-done | bytes 139296 | tf_op jit(solution)/shard_map/ppermute | solution.py:80
  66.0 2.2 %collective-permute-done.17.refs_2_ = bf16[32,2176]{1,0:T(8,128)(2,1)S(1)} collective-permute-done((bf16[32,2176]{1,0:T(8,128)(2,1)S(1)}, bf16[32,2176]{1,0:T(8,128)(2,1)S(1)}, u32[]{:S(2)}, u32[]{:S(2)}) %collective-permute-start.17) | collective-permute-done | bytes 139296 | tf_op jit(solution)/shard_map/ppermute | solution.py:80
  68.2 1.5 %collective-permute-done.18.refs_3_ = bf16[32,2176]{1,0:T(8,128)(2,1)S(1)} collective-permute-done((bf16[32,2176]{1,0:T(8,128)(2,1)S(1)}, bf16[32,2176]{1,0:T(8,128)(2,1)S(1)}, u32[]{:S(2)}, u32[]{:S(2)}) %collective-permute-start.18) | collective-permute-done | bytes 139296 | tf_op jit(solution)/shard_map/ppermute | solution.py:80
  70.1 0.9 %share.1 = (f32[32,2048]{1,0:T(8,128)}, f32[32,2048]{1,0:T(8,128)}) custom-call(f32[2,8,2176]{2,1,0:T(8,128)S(1)} %get-tuple-element.87.refs_2_.refs_0_, f32[2,8,2176]{2,1,0:T(8,128)S(1)} %get-tuple-element.98.refs_1_, f32[2,8,2176]{2,1,0:T(8,128)S(1)} %get-tuple-element.95.refs_4_.refs_2_, bf16[16,2176]{1,0:T(8,128)(2,1)S(1)} %collective-permute-done.23.refs_3_), custom_call_target="tpu_custom_call" | custom-call | flops 110000000 | tf_op jit(solution)/shard_map/share/pallas_call | solution.py:378
  71.0 4.9 %collective-permute-done.22.came_ref = bf16[16,2176]{1,0:T(8,128)(2,1)S(1)} collective-permute-done((bf16[16,2176]{1,0:T(8,128)(2,1)S(1)}, bf16[16,2176]{1,0:T(8,128)(2,1)S(1)}, u32[]{:S(2)}, u32[]{:S(2)}) %collective-permute-start.22) | collective-permute-done | bytes 69664 | tf_op jit(solution)/shard_map/ppermute | solution.py:80
  75.9 0.8 %finish.1 = (f32[32,2048]{1,0:T(8,128)}, f32[32,2048]{1,0:T(8,128)}) custom-call(f32[2,8,2176]{2,1,0:T(8,128)S(1)} %get-tuple-element.96.keep_ref, bf16[16,2176]{1,0:T(8,128)(2,1)S(1)} %collective-permute-done.22.came_ref, f32[32,2048]{1,0:T(8,128)} %get-tuple-element.100.refs_0_, ...), custom_call_target="tpu_custom_call", output_to_operand_aliasing={{0}: (2, {}), {1}: (3, {})} | custom-call | flops 110000000 | tf_op jit(solution)/shard_map/finish/pallas_call | solution.py:402
  (34 shorter events, 6.4 us)
Async XLA Ops:
  1.9 15.8 %collective-permute-start.1 = (bf16[2,128,1024]{2,1,0:T(8,128)(2,1)S(1)}, bf16[2,128,1024]{2,1,0:T(8,128)(2,1)S(1)}, u32[]{:S(2)}, u32[]{:S(2)}) collective-permute-start(bf16[2,128,1024]{2,1,0:T(8,128)(2,1)S(1)} %get-tuple-element.60), channel_id=1, source_target_pairs={{0,16},{16,0},{1,17},{17,1},{2,18},{18,2},{3,19},{19,3},{4,20},{20... | collective-permute-start | bytes 1572872 | tf_op jit(solution)/shard_map/ppermute | solution.py:80
  6.2 22.7 %collective-permute-start = (bf16[2,128,1024]{2,1,0:T(8,128)(2,1)S(1)}, bf16[2,128,1024]{2,1,0:T(8,128)(2,1)S(1)}, u32[]{:S(2)}, u32[]{:S(2)}) collective-permute-start(bf16[2,128,1024]{2,1,0:T(8,128)(2,1)S(1)} %get-tuple-element.55), channel_id=1, source_target_pairs={{0,16},{16,0},{1,17},{17,1},{2,18},{18,2},{3,19},{19,3},{4,20},{20... | collective-permute-start | bytes 1572872 | tf_op jit(solution)/shard_map/ppermute | solution.py:80
  20.2 2.6 %collective-permute-start.2 = (bf16[64,2176]{1,0:T(8,128)(2,1)S(1)}, bf16[64,2176]{1,0:T(8,128)(2,1)S(1)}, u32[]{:S(2)}, u32[]{:S(2)}) collective-permute-start(bf16[64,2176]{1,0:T(8,128)(2,1)S(1)} %get-tuple-element.63), channel_id=1, source_target_pairs={{0,1},{1,0},{2,3},{3,2},{4,5},{5,4},{6,7},{7,6},{8,9},{9,8},{10,11... | collective-permute-start | bytes 835592 | tf_op jit(solution)/shard_map/ppermute | solution.py:80
  20.3 2.6 %collective-permute-start.3 = (bf16[64,2176]{1,0:T(8,128)(2,1)S(1)}, bf16[64,2176]{1,0:T(8,128)(2,1)S(1)}, u32[]{:S(2)}, u32[]{:S(2)}) collective-permute-start(bf16[64,2176]{1,0:T(8,128)(2,1)S(1)} %get-tuple-element.64), channel_id=1, source_target_pairs={{0,1},{1,0},{2,3},{3,2},{4,5},{5,4},{6,7},{7,6},{8,9},{9,8},{10,11... | collective-permute-start | bytes 835592 | tf_op jit(solution)/shard_map/ppermute | solution.py:80
  20.8 19.4 %collective-permute-start.5 = (bf16[2,128,1024]{2,1,0:T(8,128)(2,1)S(1)}, bf16[2,128,1024]{2,1,0:T(8,128)(2,1)S(1)}, u32[]{:S(2)}, u32[]{:S(2)}) collective-permute-start(bf16[2,128,1024]{2,1,0:T(8,128)(2,1)S(1)} %get-tuple-element.68.rest_0_), channel_id=1, source_target_pairs={{0,16},{16,0},{1,17},{17,1},{2,18},{18,2},{3,19},{19,3},{4,20},{20... | collective-permute-start | bytes 1572872 | tf_op jit(solution)/shard_map/ppermute | solution.py:80
  23.6 10.0 %collective-permute-start.7 = (bf16[32,2176]{1,0:T(8,128)(2,1)S(1)}, bf16[32,2176]{1,0:T(8,128)(2,1)S(1)}, u32[]{:S(2)}, u32[]{:S(2)}) collective-permute-start(bf16[32,2176]{1,0:T(8,128)(2,1)S(1)} %get-tuple-element.71), channel_id=1, source_target_pairs={{0,6},{1,7},{2,4},{3,5},{4,2},{5,3},{6,0},{7,1},{8,14},{9,15},{10,... | collective-permute-start | bytes 417800 | tf_op jit(solution)/shard_map/ppermute | solution.py:80
  26.1 7.5 %collective-permute-start.8 = (bf16[32,2176]{1,0:T(8,128)(2,1)S(1)}, bf16[32,2176]{1,0:T(8,128)(2,1)S(1)}, u32[]{:S(2)}, u32[]{:S(2)}) collective-permute-start(bf16[32,2176]{1,0:T(8,128)(2,1)S(1)} %get-tuple-element.72), channel_id=1, source_target_pairs={{0,2},{1,3},{2,0},{3,1},{4,6},{5,7},{6,4},{7,5},{8,10},{9,11},{10,... | collective-permute-start | bytes 417800 | tf_op jit(solution)/shard_map/ppermute | solution.py:80
  26.7 6.9 %collective-permute-start.9 = (bf16[32,2176]{1,0:T(8,128)(2,1)S(1)}, bf16[32,2176]{1,0:T(8,128)(2,1)S(1)}, u32[]{:S(2)}, u32[]{:S(2)}) collective-permute-start(bf16[32,2176]{1,0:T(8,128)(2,1)S(1)} %get-tuple-element.73), channel_id=1, source_target_pairs={{0,4},{1,5},{2,6},{3,7},{4,0},{5,1},{6,2},{7,3},{8,12},{9,13},{10,... | collective-permute-start | bytes 417800 | tf_op jit(solution)/shard_map/ppermute | solution.py:80
  31.5 21.8 %collective-permute-start.4 = (bf16[2,128,1024]{2,1,0:T(8,128)(2,1)S(1)}, bf16[2,128,1024]{2,1,0:T(8,128)(2,1)S(1)}, u32[]{:S(2)}, u32[]{:S(2)}) collective-permute-start(bf16[2,128,1024]{2,1,0:T(8,128)(2,1)S(1)} %get-tuple-element.67.rest_1_), channel_id=1, source_target_pairs={{0,16},{16,0},{1,17},{17,1},{2,18},{18,2},{3,19},{19,3},{4,20},{20... | collective-permute-start | bytes 1572872 | tf_op jit(solution)/shard_map/ppermute | solution.py:80
  33.6 2.0 %collective-permute-start.6 = (bf16[128,2176]{1,0:T(8,128)(2,1)S(1)}, bf16[128,2176]{1,0:T(8,128)(2,1)S(1)}, u32[]{:S(2)}, u32[]{:S(2)}) collective-permute-start(bf16[128,2176]{1,0:T(8,128)(2,1)S(1)} %get-tuple-element.70), channel_id=1, source_target_pairs={{0,1},{1,0},{2,3},{3,2},{4,5},{5,4},{6,7},{7,6},{8,9},{9,8},{10,11... | collective-permute-start | bytes 1671176 | tf_op jit(solution)/shard_map/ppermute | solution.py:80
  36.3 7.1 %collective-permute-start.11 = (bf16[32,2176]{1,0:T(8,128)(2,1)S(1)}, bf16[32,2176]{1,0:T(8,128)(2,1)S(1)}, u32[]{:S(2)}, u32[]{:S(2)}) collective-permute-start(bf16[32,2176]{1,0:T(8,128)(2,1)S(1)} %get-tuple-element.78), channel_id=1, source_target_pairs={{0,6},{1,7},{2,4},{3,5},{4,2},{5,3},{6,0},{7,1},{8,14},{9,15},{10,... | collective-permute-start | bytes 417800 | tf_op jit(solution)/shard_map/ppermute | solution.py:80
  38.8 7.1 %collective-permute-start.12 = (bf16[32,2176]{1,0:T(8,128)(2,1)S(1)}, bf16[32,2176]{1,0:T(8,128)(2,1)S(1)}, u32[]{:S(2)}, u32[]{:S(2)}) collective-permute-start(bf16[32,2176]{1,0:T(8,128)(2,1)S(1)} %get-tuple-element.79), channel_id=1, source_target_pairs={{0,2},{1,3},{2,0},{3,1},{4,6},{5,7},{6,4},{7,5},{8,10},{9,11},{10,... | collective-permute-start | bytes 417800 | tf_op jit(solution)/shard_map/ppermute | solution.py:80
  39.4 6.6 %collective-permute-start.13 = (bf16[32,2176]{1,0:T(8,128)(2,1)S(1)}, bf16[32,2176]{1,0:T(8,128)(2,1)S(1)}, u32[]{:S(2)}, u32[]{:S(2)}) collective-permute-start(bf16[32,2176]{1,0:T(8,128)(2,1)S(1)} %get-tuple-element.80), channel_id=1, source_target_pairs={{0,4},{1,5},{2,6},{3,7},{4,0},{5,1},{6,2},{7,3},{8,12},{9,13},{10,... | collective-permute-start | bytes 417800 | tf_op jit(solution)/shard_map/ppermute | solution.py:80
  42.7 6.3 %collective-permute-start.10 = (bf16[128,2176]{1,0:T(8,128)(2,1)S(1)}, bf16[128,2176]{1,0:T(8,128)(2,1)S(1)}, u32[]{:S(2)}, u32[]{:S(2)}) collective-permute-start(bf16[128,2176]{1,0:T(8,128)(2,1)S(1)} %get-tuple-element.77), channel_id=1, source_target_pairs={{0,1},{1,0},{2,3},{3,2},{4,5},{5,4},{6,7},{7,6},{8,9},{9,8},{10,11... | collective-permute-start | bytes 1671176 | tf_op jit(solution)/shard_map/ppermute | solution.py:80
  46.3 9.6 %collective-permute-start.15 = (bf16[32,2176]{1,0:T(8,128)(2,1)S(1)}, bf16[32,2176]{1,0:T(8,128)(2,1)S(1)}, u32[]{:S(2)}, u32[]{:S(2)}) collective-permute-start(bf16[32,2176]{1,0:T(8,128)(2,1)S(1)} %get-tuple-element.86), channel_id=1, source_target_pairs={{0,8},{1,9},{2,10},{3,11},{4,12},{5,13},{6,14},{7,15},{8,0},{9,1},... | collective-permute-start | bytes 417800 | tf_op jit(solution)/shard_map/ppermute | solution.py:80
  49.7 11.9 %collective-permute-start.19 = (bf16[32,2176]{1,0:T(8,128)(2,1)S(1)}, bf16[32,2176]{1,0:T(8,128)(2,1)S(1)}, u32[]{:S(2)}, u32[]{:S(2)}) collective-permute-start(bf16[32,2176]{1,0:T(8,128)(2,1)S(1)} %get-tuple-element.92), channel_id=1, source_target_pairs={{0,6},{1,7},{2,4},{3,5},{4,2},{5,3},{6,0},{7,1},{8,14},{9,15},{10,... | collective-permute-start | bytes 417800 | tf_op jit(solution)/shard_map/ppermute | solution.py:80
  51.4 10.6 %collective-permute-start.20 = (bf16[32,2176]{1,0:T(8,128)(2,1)S(1)}, bf16[32,2176]{1,0:T(8,128)(2,1)S(1)}, u32[]{:S(2)}, u32[]{:S(2)}) collective-permute-start(bf16[32,2176]{1,0:T(8,128)(2,1)S(1)} %get-tuple-element.93), channel_id=1, source_target_pairs={{0,2},{1,3},{2,0},{3,1},{4,6},{5,7},{6,4},{7,5},{8,10},{9,11},{10,... | collective-permute-start | bytes 417800 | tf_op jit(solution)/shard_map/ppermute | solution.py:80
  52.8 9.3 %collective-permute-start.21 = (bf16[32,2176]{1,0:T(8,128)(2,1)S(1)}, bf16[32,2176]{1,0:T(8,128)(2,1)S(1)}, u32[]{:S(2)}, u32[]{:S(2)}) collective-permute-start(bf16[32,2176]{1,0:T(8,128)(2,1)S(1)} %get-tuple-element.94), channel_id=1, source_target_pairs={{0,4},{1,5},{2,6},{3,7},{4,0},{5,1},{6,2},{7,3},{8,12},{9,13},{10,... | collective-permute-start | bytes 417800 | tf_op jit(solution)/shard_map/ppermute | solution.py:80
  55.8 2.0 %collective-permute-start.14 = (bf16[128,2176]{1,0:T(8,128)(2,1)S(1)}, bf16[128,2176]{1,0:T(8,128)(2,1)S(1)}, u32[]{:S(2)}, u32[]{:S(2)}) collective-permute-start(bf16[128,2176]{1,0:T(8,128)(2,1)S(1)} %get-tuple-element.85), channel_id=1, source_target_pairs={{0,1},{1,0},{2,3},{3,2},{4,5},{5,4},{6,7},{7,6},{8,9},{9,8},{10,11... | collective-permute-start | bytes 1671176 | tf_op jit(solution)/shard_map/ppermute | solution.py:80
  58.5 7.5 %collective-permute-start.16 = (bf16[32,2176]{1,0:T(8,128)(2,1)S(1)}, bf16[32,2176]{1,0:T(8,128)(2,1)S(1)}, u32[]{:S(2)}, u32[]{:S(2)}) collective-permute-start(bf16[32,2176]{1,0:T(8,128)(2,1)S(1)} %get-tuple-element.89), channel_id=1, source_target_pairs={{0,6},{1,7},{2,4},{3,5},{4,2},{5,3},{6,0},{7,1},{8,14},{9,15},{10,... | collective-permute-start | bytes 417800 | tf_op jit(solution)/shard_map/ppermute | solution.py:80
  60.3 7.9 %collective-permute-start.17 = (bf16[32,2176]{1,0:T(8,128)(2,1)S(1)}, bf16[32,2176]{1,0:T(8,128)(2,1)S(1)}, u32[]{:S(2)}, u32[]{:S(2)}) collective-permute-start(bf16[32,2176]{1,0:T(8,128)(2,1)S(1)} %get-tuple-element.90), channel_id=1, source_target_pairs={{0,2},{1,3},{2,0},{3,1},{4,6},{5,7},{6,4},{7,5},{8,10},{9,11},{10,... | collective-permute-start | bytes 417800 | tf_op jit(solution)/shard_map/ppermute | solution.py:80
  61.6 8.0 %collective-permute-start.18 = (bf16[32,2176]{1,0:T(8,128)(2,1)S(1)}, bf16[32,2176]{1,0:T(8,128)(2,1)S(1)}, u32[]{:S(2)}, u32[]{:S(2)}) collective-permute-start(bf16[32,2176]{1,0:T(8,128)(2,1)S(1)} %get-tuple-element.91), channel_id=1, source_target_pairs={{0,4},{1,5},{2,6},{3,7},{4,0},{5,1},{6,2},{7,3},{8,12},{9,13},{10,... | collective-permute-start | bytes 417800 | tf_op jit(solution)/shard_map/ppermute | solution.py:80
  62.4 7.7 %collective-permute-start.23 = (bf16[16,2176]{1,0:T(8,128)(2,1)S(1)}, bf16[16,2176]{1,0:T(8,128)(2,1)S(1)}, u32[]{:S(2)}, u32[]{:S(2)}) collective-permute-start(bf16[16,2176]{1,0:T(8,128)(2,1)S(1)} %get-tuple-element.99), channel_id=1, source_target_pairs={{0,8},{1,9},{2,10},{3,11},{4,12},{5,13},{6,14},{7,15},{8,0},{9,1},... | collective-permute-start | bytes 208904 | tf_op jit(solution)/shard_map/ppermute | solution.py:80
  70.0 5.9 %collective-permute-start.22 = (bf16[16,2176]{1,0:T(8,128)(2,1)S(1)}, bf16[16,2176]{1,0:T(8,128)(2,1)S(1)}, u32[]{:S(2)}, u32[]{:S(2)}) collective-permute-start(bf16[16,2176]{1,0:T(8,128)(2,1)S(1)} %get-tuple-element.97), channel_id=1, source_target_pairs={{0,8},{1,9},{2,10},{3,11},{4,12},{5,13},{6,14},{7,15},{8,0},{9,1},... | collective-permute-start | bytes 208904 | tf_op jit(solution)/shard_map/ppermute | solution.py:80

commit v19 on v17

--- a/solution.py
+++ b/solution.py
@@ -470,7 +470,8 @@
         if final:
             carry, last = second_sums(turn - 1, carry, last, 0.1)
             came.append(swap(held.pop(), "walk", stages[2][0]))
-        sent = [swap(part, "walk", mask) for part, mask in reversed(list(zip(sends, second)))]
+        pairs = list(zip(sends, second))
+        sent = [swap(part, "walk", mask) for part, mask in (pairs if final else reversed(pairs))]
     second_sums(pieces - 1, (), last, 0.1)
     came.append(swap(held.pop(), "walk", stages[2][0]))
     outputs = share([keep[piece] for piece in range(pieces - 1)], came[1:-1], occupied // count, count)

time: 76.2 us -> 75.8 us (level)
  no operation moved by 1% of the time
where the time goes in v19:
time: 75.8 us; the launch traced here: 75.6 us
  Pallas kernels  29.3 us (39%)
  starting transfers between devices  26.5 us (35%)
  waiting for transfers between devices  18.4 us (24%)
  between operations  1.47 us (2%)
    ppermute x25, starting transfers between devices, swap(): return lax.ppermute(array, axis, pairs)  26.5 us
    ppermute x25, waiting for transfers between devices, swap(): return lax.ppermute(array, axis, pairs)  18.4 us
    pallas_call x1, Pallas kernels, near_product(): pl.pallas_call(functools.partial(near_kernel, chunk, tile), out_shape=(ja...  10.5 us
    pallas_call x4, Pallas kernels, far_product(): pl.pallas_call(functools.partial(far_kernel, place_weights(stages), count...  10.3 us
    pallas_call x9, Pallas kernels, combine(): pl.pallas_call(functools.partial(combine_kernel, layout, len(after), len(...  4.3 us
    pallas_call x2, Pallas kernels, cut(): pl.pallas_call(cut_kernel, out_shape=(out, out), grid=(1,), in_specs=[blo...  2.55 us
  transfers between devices with their start and end apart: 25, of which 11 were waited for; matrix products, arithmetic and copies ran while one was open for 0% of the time, Pallas kernels for 36%

profile of v19, /device:TPU:0, one launch (start us, length us, event | category | flops | bytes accessed | tf_op | source)
XLA Modules:
  0.0 75.6 jit_solution(11219665293826861258)
XLA Ops:
  0.6 1.3 %cut.3 = (bf16[2,128,1024]{2,1,0:T(8,128)(2,1)S(1)}, bf16[2,128,1024]{2,1,0:T(8,128)(2,1)S(1)}) custom-call(bf16[16,32,1024]{2,1,0:T(8,128)(2,1)} %bitcast.6, bf16[16,32,1024]{2,1,0:T(8,128)(2,1)} %bitcast.9), custom_call_target="tpu_custom_call" | custom-call | flops 110000000 | tf_op jit(solution)/shard_map/cut/pallas_call | solution.py:166
  1.9 3.0 %collective-permute-start.1 = (bf16[2,128,1024]{2,1,0:T(8,128)(2,1)S(1)}, bf16[2,128,1024]{2,1,0:T(8,128)(2,1)S(1)}, u32[]{:S(2)}, u32[]{:S(2)}) collective-permute-start(bf16[2,128,1024]{2,1,0:T(8,128)(2,1)S(1)} %get-tuple-element.61), channel_id=1, source_target_pairs={{0,16},{16,0},{1,17},{17,1},{2,18},{18,2},{3,19},{19,3},{4,20},{20... | collective-permute-start | bytes 1572872 | tf_op jit(solution)/shard_map/ppermute | solution.py:80
  4.9 1.3 %cut.2 = (bf16[2,128,1024]{2,1,0:T(8,128)(2,1)S(1)}, bf16[2,128,1024]{2,1,0:T(8,128)(2,1)S(1)}) custom-call(bf16[16,32,1024]{2,1,0:T(8,128)(2,1)} %bitcast.7, bf16[16,32,1024]{2,1,0:T(8,128)(2,1)} %bitcast.10), custom_call_target="tpu_custom_call" | custom-call | flops 110000000 | tf_op jit(solution)/shard_map/cut/pallas_call | solution.py:166
  7.0 10.5 %near_product.1 = (f32[2,16,32,2048]{3,2,1,0:T(8,128)S(1)}, bf16[1024,2048]{1,0:T(8,128)(2,1)S(1)}, bf16[1024,2048]{1,0:T(8,128)(2,1)S(1)}) custom-call(s32[1]{0:T(128)} %bitcast.virt_ref, s32[1]{0:T(128)} %bitcast.1.me_ref, f32[1]{0:T(128)S(6)} %copy.11.energy_ref, bf16[16,32,1024]{2,1,0:T(8,128)(2,1)} %bitcast.8, bf16[16,32,1024]{2,1,0:T(8,128)(2,1)} %bitcast.11, ...), custom_call_target="tpu_custom_call" | custom-call | flops 9900000256 | tf_op jit(solution)/shard_map/near_product/pallas_call | solution.py:232
  17.7 2.5 %far_product.4 = (bf16[64,2176]{1,0:T(8,128)(2,1)S(1)}, bf16[64,2176]{1,0:T(8,128)(2,1)S(1)}, f32[2,128,2176]{2,1,0:T(8,128)S(1)}) custom-call(s32[1]{0:T(128)} %bitcast.virt_ref, s32[1]{0:T(128)} %bitcast.1.me_ref, f32[1]{0:T(128)S(6)} %copy.11.energy_ref, bf16[2,128,1024]{2,1,0:T(8,128)(2,1)S(1)} %collective-permute-done.1.far_ref, ...), custom_call_target="tpu_custom_call" | custom-call | flops 110000000 | tf_op jit(solution)/shard_map/far_product/pallas_call | solution.py:282
  20.8 2.1 %collective-permute-start.5 = (bf16[2,128,1024]{2,1,0:T(8,128)(2,1)S(1)}, bf16[2,128,1024]{2,1,0:T(8,128)(2,1)S(1)}, u32[]{:S(2)}, u32[]{:S(2)}) collective-permute-start(bf16[2,128,1024]{2,1,0:T(8,128)(2,1)S(1)} %get-tuple-element.69.rest_0_), channel_id=1, source_target_pairs={{0,16},{16,0},{1,17},{17,1},{2,18},{18,2},{3,19},{19,3},{4,20},{20... | collective-permute-start | bytes 1572872 | tf_op jit(solution)/shard_map/ppermute | solution.py:80
  23.6 2.6 %collective-permute-start.8 = (bf16[32,2176]{1,0:T(8,128)(2,1)S(1)}, bf16[32,2176]{1,0:T(8,128)(2,1)S(1)}, u32[]{:S(2)}, u32[]{:S(2)}) collective-permute-start(bf16[32,2176]{1,0:T(8,128)(2,1)S(1)} %get-tuple-element.73), channel_id=1, source_target_pairs={{0,6},{1,7},{2,4},{3,5},{4,2},{5,3},{6,0},{7,1},{8,14},{9,15},{10,... | collective-permute-start | bytes 417800 | tf_op jit(solution)/shard_map/ppermute | solution.py:80
  27.1 1.8 %collective-permute-done.far_ref = bf16[2,128,1024]{2,1,0:T(8,128)(2,1)S(1)} collective-permute-done((bf16[2,128,1024]{2,1,0:T(8,128)(2,1)S(1)}, bf16[2,128,1024]{2,1,0:T(8,128)(2,1)S(1)}, u32[]{:S(2)}, u32[]{:S(2)}) %collective-permute-start) | collective-permute-done | bytes 524320 | tf_op jit(solution)/shard_map/ppermute | solution.py:80
  28.9 2.5 %far_product.5 = (bf16[64,2176]{1,0:T(8,128)(2,1)S(1)}, bf16[64,2176]{1,0:T(8,128)(2,1)S(1)}, f32[2,128,2176]{2,1,0:T(8,128)S(1)}) custom-call(s32[1]{0:T(128)} %bitcast.virt_ref, s32[1]{0:T(128)} %bitcast.1.me_ref, f32[1]{0:T(128)S(6)} %copy.11.energy_ref, bf16[2,128,1024]{2,1,0:T(8,128)(2,1)S(1)} %collective-permute-done.far_ref, ...), custom_call_target="tpu_custom_call" | custom-call | flops 1650000000 | tf_op jit(solution)/shard_map/far_product/pallas_call | solution.py:282
  32.0 1.0 %collective-permute-done.9.refs_2_ = bf16[32,2176]{1,0:T(8,128)(2,1)S(1)} collective-permute-done((bf16[32,2176]{1,0:T(8,128)(2,1)S(1)}, bf16[32,2176]{1,0:T(8,128)(2,1)S(1)}, u32[]{:S(2)}, u32[]{:S(2)}) %collective-permute-start.9) | collective-permute-done | bytes 139296 | tf_op jit(solution)/shard_map/ppermute | solution.py:80
  33.0 1.7 %collective-permute-start.4 = (bf16[2,128,1024]{2,1,0:T(8,128)(2,1)S(1)}, bf16[2,128,1024]{2,1,0:T(8,128)(2,1)S(1)}, u32[]{:S(2)}, u32[]{:S(2)}) collective-permute-start(bf16[2,128,1024]{2,1,0:T(8,128)(2,1)S(1)} %get-tuple-element.68.rest_1_), channel_id=1, source_target_pairs={{0,16},{16,0},{1,17},{17,1},{2,18},{18,2},{3,19},{19,3},{4,20},{20... | collective-permute-start | bytes 1572872 | tf_op jit(solution)/shard_map/ppermute | solution.py:80
  35.1 0.7 combine.11
  35.8 2.0 %collective-permute-start.12 = (bf16[32,2176]{1,0:T(8,128)(2,1)S(1)}, bf16[32,2176]{1,0:T(8,128)(2,1)S(1)}, u32[]{:S(2)}, u32[]{:S(2)}) collective-permute-start(bf16[32,2176]{1,0:T(8,128)(2,1)S(1)} %get-tuple-element.80), channel_id=1, source_target_pairs={{0,6},{1,7},{2,4},{3,5},{4,2},{5,3},{6,0},{7,1},{8,14},{9,15},{10,... | collective-permute-start | bytes 417800 | tf_op jit(solution)/shard_map/ppermute | solution.py:80
  37.8 1.1 %collective-permute-start.13 = (bf16[32,2176]{1,0:T(8,128)(2,1)S(1)}, bf16[32,2176]{1,0:T(8,128)(2,1)S(1)}, u32[]{:S(2)}, u32[]{:S(2)}) collective-permute-start(bf16[32,2176]{1,0:T(8,128)(2,1)S(1)} %get-tuple-element.81), channel_id=1, source_target_pairs={{0,2},{1,3},{2,0},{3,1},{4,6},{5,7},{6,4},{7,5},{8,10},{9,11},{10,... | collective-permute-start | bytes 417800 | tf_op jit(solution)/shard_map/ppermute | solution.py:80
  39.3 0.8 %collective-permute-done.5.far_ref = bf16[2,128,1024]{2,1,0:T(8,128)(2,1)S(1)} collective-permute-done((bf16[2,128,1024]{2,1,0:T(8,128)(2,1)S(1)}, bf16[2,128,1024]{2,1,0:T(8,128)(2,1)S(1)}, u32[]{:S(2)}, u32[]{:S(2)}) %collective-permute-start.5) | collective-permute-done | bytes 524320 | tf_op jit(solution)/shard_map/ppermute | solution.py:80
  40.2 2.5 %far_product.6 = (bf16[128,2176]{1,0:T(8,128)(2,1)S(1)}, f32[2,128,2176]{2,1,0:T(8,128)S(1)}) custom-call(s32[1]{0:T(128)} %bitcast.virt_ref, s32[1]{0:T(128)} %bitcast.1.me_ref, f32[1]{0:T(128)S(6)} %copy.11.energy_ref, bf16[2,128,1024]{2,1,0:T(8,128)(2,1)S(1)} %collective-permute-done.5.far_ref, f32[2,16,32,2048]{3,2,1,0:T(8,128)S(1)} %get-tuple-element.58.near_ref, ...), custom_call_target="tpu_custom_call" | custom-call | flops 1650000000 | tf_op jit(solution)/shard_map/far_product/pallas_call | solution.py:282
  43.1 2.0 %collective-permute-done.13.refs_2_ = bf16[32,2176]{1,0:T(8,128)(2,1)S(1)} collective-permute-done((bf16[32,2176]{1,0:T(8,128)(2,1)S(1)}, bf16[32,2176]{1,0:T(8,128)(2,1)S(1)}, u32[]{:S(2)}, u32[]{:S(2)}) %collective-permute-start.13) | collective-permute-done | bytes 139296 | tf_op jit(solution)/shard_map/ppermute | solution.py:80
  45.4 2.7 %collective-permute-start.16 = (bf16[32,2176]{1,0:T(8,128)(2,1)S(1)}, bf16[32,2176]{1,0:T(8,128)(2,1)S(1)}, u32[]{:S(2)}, u32[]{:S(2)}) collective-permute-start(bf16[32,2176]{1,0:T(8,128)(2,1)S(1)} %get-tuple-element.88), channel_id=1, source_target_pairs={{0,8},{1,9},{2,10},{3,11},{4,12},{5,13},{6,14},{7,15},{8,0},{9,1},... | collective-permute-start | bytes 417800 | tf_op jit(solution)/shard_map/ppermute | solution.py:80
  48.8 1.8 %collective-permute-start.20 = (bf16[32,2176]{1,0:T(8,128)(2,1)S(1)}, bf16[32,2176]{1,0:T(8,128)(2,1)S(1)}, u32[]{:S(2)}, u32[]{:S(2)}) collective-permute-start(bf16[32,2176]{1,0:T(8,128)(2,1)S(1)} %get-tuple-element.94), channel_id=1, source_target_pairs={{0,6},{1,7},{2,4},{3,5},{4,2},{5,3},{6,0},{7,1},{8,14},{9,15},{10,... | collective-permute-start | bytes 417800 | tf_op jit(solution)/shard_map/ppermute | solution.py:80
  50.6 1.3 %collective-permute-start.21 = (bf16[32,2176]{1,0:T(8,128)(2,1)S(1)}, bf16[32,2176]{1,0:T(8,128)(2,1)S(1)}, u32[]{:S(2)}, u32[]{:S(2)}) collective-permute-start(bf16[32,2176]{1,0:T(8,128)(2,1)S(1)} %get-tuple-element.95), channel_id=1, source_target_pairs={{0,2},{1,3},{2,0},{3,1},{4,6},{5,7},{6,4},{7,5},{8,10},{9,11},{10,... | collective-permute-start | bytes 417800 | tf_op jit(solution)/shard_map/ppermute | solution.py:80
  52.3 2.7 %far_product.7 = (bf16[128,2176]{1,0:T(8,128)(2,1)S(1)}, f32[2,128,2176]{2,1,0:T(8,128)S(1)}) custom-call(s32[1]{0:T(128)} %bitcast.virt_ref, s32[1]{0:T(128)} %bitcast.1.me_ref, f32[1]{0:T(128)S(6)} %copy.11.energy_ref, bf16[2,128,1024]{2,1,0:T(8,128)(2,1)S(1)} %collective-permute-done.4.far_ref, f32[2,16,32,2048]{3,2,1,0:T(8,128)S(1)} %get-tuple-element.58.near_ref, ...), custom_call_target="tpu_custom_call" | custom-call | flops 1650000000 | tf_op jit(solution)/shard_map/far_product/pallas_call | solution.py:282
  55.3 1.8 %collective-permute-done.15.refs_1_ = bf16[128,2176]{1,0:T(8,128)(2,1)S(1)} collective-permute-done((bf16[128,2176]{1,0:T(8,128)(2,1)S(1)}, bf16[128,2176]{1,0:T(8,128)(2,1)S(1)}, u32[]{:S(2)}, u32[]{:S(2)}) %collective-permute-start.15) | collective-permute-done | bytes 557088 | tf_op jit(solution)/shard_map/ppermute | solution.py:80
  57.8 1.6 %collective-permute-start.17 = (bf16[32,2176]{1,0:T(8,128)(2,1)S(1)}, bf16[32,2176]{1,0:T(8,128)(2,1)S(1)}, u32[]{:S(2)}, u32[]{:S(2)}) collective-permute-start(bf16[32,2176]{1,0:T(8,128)(2,1)S(1)} %get-tuple-element.91), channel_id=1, source_target_pairs={{0,4},{1,5},{2,6},{3,7},{4,0},{5,1},{6,2},{7,3},{8,12},{9,13},{10,... | collective-permute-start | bytes 417800 | tf_op jit(solution)/shard_map/ppermute | solution.py:80
  59.4 0.7 collective-permute-start.18
  60.1 1.2 %collective-permute-start.19 = (bf16[32,2176]{1,0:T(8,128)(2,1)S(1)}, bf16[32,2176]{1,0:T(8,128)(2,1)S(1)}, u32[]{:S(2)}, u32[]{:S(2)}) collective-permute-start(bf16[32,2176]{1,0:T(8,128)(2,1)S(1)} %get-tuple-element.93), channel_id=1, source_target_pairs={{0,6},{1,7},{2,4},{3,5},{4,2},{5,3},{6,0},{7,1},{8,14},{9,15},{10,... | collective-permute-start | bytes 417800 | tf_op jit(solution)/shard_map/ppermute | solution.py:80
  61.7 1.1 %collective-permute-start.24 = (bf16[16,2176]{1,0:T(8,128)(2,1)S(1)}, bf16[16,2176]{1,0:T(8,128)(2,1)S(1)}, u32[]{:S(2)}, u32[]{:S(2)}) collective-permute-start(bf16[16,2176]{1,0:T(8,128)(2,1)S(1)} %get-tuple-element.101), channel_id=1, source_target_pairs={{0,8},{1,9},{2,10},{3,11},{4,12},{5,13},{6,14},{7,15},{8,0},{9,1},... | collective-permute-start | bytes 208904 | tf_op jit(solution)/shard_map/ppermute | solution.py:80
  62.8 1.2 %collective-permute-done.17.refs_1_ = bf16[32,2176]{1,0:T(8,128)(2,1)S(1)} collective-permute-done((bf16[32,2176]{1,0:T(8,128)(2,1)S(1)}, bf16[32,2176]{1,0:T(8,128)(2,1)S(1)}, u32[]{:S(2)}, u32[]{:S(2)}) %collective-permute-start.17) | collective-permute-done | bytes 139296 | tf_op jit(solution)/shard_map/ppermute | solution.py:80
  64.0 1.9 %collective-permute-done.18.refs_2_ = bf16[32,2176]{1,0:T(8,128)(2,1)S(1)} collective-permute-done((bf16[32,2176]{1,0:T(8,128)(2,1)S(1)}, bf16[32,2176]{1,0:T(8,128)(2,1)S(1)}, u32[]{:S(2)}, u32[]{:S(2)}) %collective-permute-start.18) | collective-permute-done | bytes 139296 | tf_op jit(solution)/shard_map/ppermute | solution.py:80
  65.9 3.0 %collective-permute-done.19.refs_3_ = bf16[32,2176]{1,0:T(8,128)(2,1)S(1)} collective-permute-done((bf16[32,2176]{1,0:T(8,128)(2,1)S(1)}, bf16[32,2176]{1,0:T(8,128)(2,1)S(1)}, u32[]{:S(2)}, u32[]{:S(2)}) %collective-permute-start.19) | collective-permute-done | bytes 139296 | tf_op jit(solution)/shard_map/ppermute | solution.py:80
  69.8 0.8 %share.1 = (f32[32,2048]{1,0:T(8,128)}, f32[32,2048]{1,0:T(8,128)}) custom-call(f32[2,8,2176]{2,1,0:T(8,128)S(1)} %get-tuple-element.89.refs_2_.refs_0_, f32[2,8,2176]{2,1,0:T(8,128)S(1)} %get-tuple-element.100.refs_1_, f32[2,8,2176]{2,1,0:T(8,128)S(1)} %get-tuple-element.97.refs_4_.refs_2_, bf16[16,2176]{1,0:T(8,128)(2,1)S(1)} %collective-permute-done.24.refs_3_), custom_call_target="tpu_custom_call" | custom-call | flops 110000000 | tf_op jit(solution)/shard_map/share/pallas_call | solution.py:378
  70.6 4.2 %collective-permute-done.23.came_ref = bf16[16,2176]{1,0:T(8,128)(2,1)S(1)} collective-permute-done((bf16[16,2176]{1,0:T(8,128)(2,1)S(1)}, bf16[16,2176]{1,0:T(8,128)(2,1)S(1)}, u32[]{:S(2)}, u32[]{:S(2)}) %collective-permute-start.23) | collective-permute-done | bytes 69664 | tf_op jit(solution)/shard_map/ppermute | solution.py:80
  74.8 0.8 %finish.1 = (f32[32,2048]{1,0:T(8,128)}, f32[32,2048]{1,0:T(8,128)}) custom-call(f32[2,8,2176]{2,1,0:T(8,128)S(1)} %get-tuple-element.98.keep_ref, bf16[16,2176]{1,0:T(8,128)(2,1)S(1)} %collective-permute-done.23.came_ref, f32[32,2048]{1,0:T(8,128)} %get-tuple-element.102.refs_0_, ...), custom_call_target="tpu_custom_call", output_to_operand_aliasing={{0}: (2, {}), {1}: (3, {})} | custom-call | flops 110000000 | tf_op jit(solution)/shard_map/finish/pallas_call | solution.py:402
  (36 shorter events, 7.9 us)
Async XLA Ops:
  1.9 15.8 %collective-permute-start.1 = (bf16[2,128,1024]{2,1,0:T(8,128)(2,1)S(1)}, bf16[2,128,1024]{2,1,0:T(8,128)(2,1)S(1)}, u32[]{:S(2)}, u32[]{:S(2)}) collective-permute-start(bf16[2,128,1024]{2,1,0:T(8,128)(2,1)S(1)} %get-tuple-element.61), channel_id=1, source_target_pairs={{0,16},{16,0},{1,17},{17,1},{2,18},{18,2},{3,19},{19,3},{4,20},{20... | collective-permute-start | bytes 1572872 | tf_op jit(solution)/shard_map/ppermute | solution.py:80
  6.2 22.7 %collective-permute-start = (bf16[2,128,1024]{2,1,0:T(8,128)(2,1)S(1)}, bf16[2,128,1024]{2,1,0:T(8,128)(2,1)S(1)}, u32[]{:S(2)}, u32[]{:S(2)}) collective-permute-start(bf16[2,128,1024]{2,1,0:T(8,128)(2,1)S(1)} %get-tuple-element.56), channel_id=1, source_target_pairs={{0,16},{16,0},{1,17},{17,1},{2,18},{18,2},{3,19},{19,3},{4,20},{20... | collective-permute-start | bytes 1572872 | tf_op jit(solution)/shard_map/ppermute | solution.py:80
  20.2 2.6 %collective-permute-start.2 = (bf16[64,2176]{1,0:T(8,128)(2,1)S(1)}, bf16[64,2176]{1,0:T(8,128)(2,1)S(1)}, u32[]{:S(2)}, u32[]{:S(2)}) collective-permute-start(bf16[64,2176]{1,0:T(8,128)(2,1)S(1)} %get-tuple-element.64), channel_id=1, source_target_pairs={{0,1},{1,0},{2,3},{3,2},{4,5},{5,4},{6,7},{7,6},{8,9},{9,8},{10,11... | collective-permute-start | bytes 835592 | tf_op jit(solution)/shard_map/ppermute | solution.py:80
  20.3 2.6 %collective-permute-start.3 = (bf16[64,2176]{1,0:T(8,128)(2,1)S(1)}, bf16[64,2176]{1,0:T(8,128)(2,1)S(1)}, u32[]{:S(2)}, u32[]{:S(2)}) collective-permute-start(bf16[64,2176]{1,0:T(8,128)(2,1)S(1)} %get-tuple-element.65), channel_id=1, source_target_pairs={{0,1},{1,0},{2,3},{3,2},{4,5},{5,4},{6,7},{7,6},{8,9},{9,8},{10,11... | collective-permute-start | bytes 835592 | tf_op jit(solution)/shard_map/ppermute | solution.py:80
  20.8 19.4 %collective-permute-start.5 = (bf16[2,128,1024]{2,1,0:T(8,128)(2,1)S(1)}, bf16[2,128,1024]{2,1,0:T(8,128)(2,1)S(1)}, u32[]{:S(2)}, u32[]{:S(2)}) collective-permute-start(bf16[2,128,1024]{2,1,0:T(8,128)(2,1)S(1)} %get-tuple-element.69.rest_0_), channel_id=1, source_target_pairs={{0,16},{16,0},{1,17},{17,1},{2,18},{18,2},{3,19},{19,3},{4,20},{20... | collective-permute-start | bytes 1572872 | tf_op jit(solution)/shard_map/ppermute | solution.py:80
  23.6 8.0 %collective-permute-start.8 = (bf16[32,2176]{1,0:T(8,128)(2,1)S(1)}, bf16[32,2176]{1,0:T(8,128)(2,1)S(1)}, u32[]{:S(2)}, u32[]{:S(2)}) collective-permute-start(bf16[32,2176]{1,0:T(8,128)(2,1)S(1)} %get-tuple-element.73), channel_id=1, source_target_pairs={{0,6},{1,7},{2,4},{3,5},{4,2},{5,3},{6,0},{7,1},{8,14},{9,15},{10,... | collective-permute-start | bytes 417800 | tf_op jit(solution)/shard_map/ppermute | solution.py:80
  26.1 6.9 %collective-permute-start.9 = (bf16[32,2176]{1,0:T(8,128)(2,1)S(1)}, bf16[32,2176]{1,0:T(8,128)(2,1)S(1)}, u32[]{:S(2)}, u32[]{:S(2)}) collective-permute-start(bf16[32,2176]{1,0:T(8,128)(2,1)S(1)} %get-tuple-element.74), channel_id=1, source_target_pairs={{0,2},{1,3},{2,0},{3,1},{4,6},{5,7},{6,4},{7,5},{8,10},{9,11},{10,... | collective-permute-start | bytes 417800 | tf_op jit(solution)/shard_map/ppermute | solution.py:80
  26.7 8.0 %collective-permute-start.10 = (bf16[32,2176]{1,0:T(8,128)(2,1)S(1)}, bf16[32,2176]{1,0:T(8,128)(2,1)S(1)}, u32[]{:S(2)}, u32[]{:S(2)}) collective-permute-start(bf16[32,2176]{1,0:T(8,128)(2,1)S(1)} %get-tuple-element.75), channel_id=1, source_target_pairs={{0,4},{1,5},{2,6},{3,7},{4,0},{5,1},{6,2},{7,3},{8,12},{9,13},{10,... | collective-permute-start | bytes 417800 | tf_op jit(solution)/shard_map/ppermute | solution.py:80
  31.5 3.6 %collective-permute-start.6 = (bf16[64,2176]{1,0:T(8,128)(2,1)S(1)}, bf16[64,2176]{1,0:T(8,128)(2,1)S(1)}, u32[]{:S(2)}, u32[]{:S(2)}) collective-permute-start(bf16[64,2176]{1,0:T(8,128)(2,1)S(1)} %get-tuple-element.71), channel_id=1, source_target_pairs={{0,1},{1,0},{2,3},{3,2},{4,5},{5,4},{6,7},{7,6},{8,9},{9,8},{10,11... | collective-permute-start | bytes 835592 | tf_op jit(solution)/shard_map/ppermute | solution.py:80
  31.6 3.5 %collective-permute-start.7 = (bf16[64,2176]{1,0:T(8,128)(2,1)S(1)}, bf16[64,2176]{1,0:T(8,128)(2,1)S(1)}, u32[]{:S(2)}, u32[]{:S(2)}) collective-permute-start(bf16[64,2176]{1,0:T(8,128)(2,1)S(1)} %get-tuple-element.72), channel_id=1, source_target_pairs={{0,1},{1,0},{2,3},{3,2},{4,5},{5,4},{6,7},{7,6},{8,9},{9,8},{10,11... | collective-permute-start | bytes 835592 | tf_op jit(solution)/shard_map/ppermute | solution.py:80
  33.0 19.3 %collective-permute-start.4 = (bf16[2,128,1024]{2,1,0:T(8,128)(2,1)S(1)}, bf16[2,128,1024]{2,1,0:T(8,128)(2,1)S(1)}, u32[]{:S(2)}, u32[]{:S(2)}) collective-permute-start(bf16[2,128,1024]{2,1,0:T(8,128)(2,1)S(1)} %get-tuple-element.68.rest_1_), channel_id=1, source_target_pairs={{0,16},{16,0},{1,17},{17,1},{2,18},{18,2},{3,19},{19,3},{4,20},{20... | collective-permute-start | bytes 1572872 | tf_op jit(solution)/shard_map/ppermute | solution.py:80
  35.8 7.3 %collective-permute-start.12 = (bf16[32,2176]{1,0:T(8,128)(2,1)S(1)}, bf16[32,2176]{1,0:T(8,128)(2,1)S(1)}, u32[]{:S(2)}, u32[]{:S(2)}) collective-permute-start(bf16[32,2176]{1,0:T(8,128)(2,1)S(1)} %get-tuple-element.80), channel_id=1, source_target_pairs={{0,6},{1,7},{2,4},{3,5},{4,2},{5,3},{6,0},{7,1},{8,14},{9,15},{10,... | collective-permute-start | bytes 417800 | tf_op jit(solution)/shard_map/ppermute | solution.py:80
  37.8 7.3 %collective-permute-start.13 = (bf16[32,2176]{1,0:T(8,128)(2,1)S(1)}, bf16[32,2176]{1,0:T(8,128)(2,1)S(1)}, u32[]{:S(2)}, u32[]{:S(2)}) collective-permute-start(bf16[32,2176]{1,0:T(8,128)(2,1)S(1)} %get-tuple-element.81), channel_id=1, source_target_pairs={{0,2},{1,3},{2,0},{3,1},{4,6},{5,7},{6,4},{7,5},{8,10},{9,11},{10,... | collective-permute-start | bytes 417800 | tf_op jit(solution)/shard_map/ppermute | solution.py:80
  38.9 6.2 %collective-permute-start.14 = (bf16[32,2176]{1,0:T(8,128)(2,1)S(1)}, bf16[32,2176]{1,0:T(8,128)(2,1)S(1)}, u32[]{:S(2)}, u32[]{:S(2)}) collective-permute-start(bf16[32,2176]{1,0:T(8,128)(2,1)S(1)} %get-tuple-element.82), channel_id=1, source_target_pairs={{0,4},{1,5},{2,6},{3,7},{4,0},{5,1},{6,2},{7,3},{8,12},{9,13},{10,... | collective-permute-start | bytes 417800 | tf_op jit(solution)/shard_map/ppermute | solution.py:80
  42.7 5.4 %collective-permute-start.11 = (bf16[128,2176]{1,0:T(8,128)(2,1)S(1)}, bf16[128,2176]{1,0:T(8,128)(2,1)S(1)}, u32[]{:S(2)}, u32[]{:S(2)}) collective-permute-start(bf16[128,2176]{1,0:T(8,128)(2,1)S(1)} %get-tuple-element.79), channel_id=1, source_target_pairs={{0,1},{1,0},{2,3},{3,2},{4,5},{5,4},{6,7},{7,6},{8,9},{9,8},{10,11... | collective-permute-start | bytes 1671176 | tf_op jit(solution)/shard_map/ppermute | solution.py:80
  45.4 9.7 %collective-permute-start.16 = (bf16[32,2176]{1,0:T(8,128)(2,1)S(1)}, bf16[32,2176]{1,0:T(8,128)(2,1)S(1)}, u32[]{:S(2)}, u32[]{:S(2)}) collective-permute-start(bf16[32,2176]{1,0:T(8,128)(2,1)S(1)} %get-tuple-element.88), channel_id=1, source_target_pairs={{0,8},{1,9},{2,10},{3,11},{4,12},{5,13},{6,14},{7,15},{8,0},{9,1},... | collective-permute-start | bytes 417800 | tf_op jit(solution)/shard_map/ppermute | solution.py:80
  48.8 11.4 %collective-permute-start.20 = (bf16[32,2176]{1,0:T(8,128)(2,1)S(1)}, bf16[32,2176]{1,0:T(8,128)(2,1)S(1)}, u32[]{:S(2)}, u32[]{:S(2)}) collective-permute-start(bf16[32,2176]{1,0:T(8,128)(2,1)S(1)} %get-tuple-element.94), channel_id=1, source_target_pairs={{0,6},{1,7},{2,4},{3,5},{4,2},{5,3},{6,0},{7,1},{8,14},{9,15},{10,... | collective-permute-start | bytes 417800 | tf_op jit(solution)/shard_map/ppermute | solution.py:80
  50.6 10.8 %collective-permute-start.21 = (bf16[32,2176]{1,0:T(8,128)(2,1)S(1)}, bf16[32,2176]{1,0:T(8,128)(2,1)S(1)}, u32[]{:S(2)}, u32[]{:S(2)}) collective-permute-start(bf16[32,2176]{1,0:T(8,128)(2,1)S(1)} %get-tuple-element.95), channel_id=1, source_target_pairs={{0,2},{1,3},{2,0},{3,1},{4,6},{5,7},{6,4},{7,5},{8,10},{9,11},{10,... | collective-permute-start | bytes 417800 | tf_op jit(solution)/shard_map/ppermute | solution.py:80
  51.8 9.5 %collective-permute-start.22 = (bf16[32,2176]{1,0:T(8,128)(2,1)S(1)}, bf16[32,2176]{1,0:T(8,128)(2,1)S(1)}, u32[]{:S(2)}, u32[]{:S(2)}) collective-permute-start(bf16[32,2176]{1,0:T(8,128)(2,1)S(1)} %get-tuple-element.96), channel_id=1, source_target_pairs={{0,4},{1,5},{2,6},{3,7},{4,0},{5,1},{6,2},{7,3},{8,12},{9,13},{10,... | collective-permute-start | bytes 417800 | tf_op jit(solution)/shard_map/ppermute | solution.py:80
  55.1 2.0 %collective-permute-start.15 = (bf16[128,2176]{1,0:T(8,128)(2,1)S(1)}, bf16[128,2176]{1,0:T(8,128)(2,1)S(1)}, u32[]{:S(2)}, u32[]{:S(2)}) collective-permute-start(bf16[128,2176]{1,0:T(8,128)(2,1)S(1)} %get-tuple-element.87), channel_id=1, source_target_pairs={{0,1},{1,0},{2,3},{3,2},{4,5},{5,4},{6,7},{7,6},{8,9},{9,8},{10,11... | collective-permute-start | bytes 1671176 | tf_op jit(solution)/shard_map/ppermute | solution.py:80
  57.8 6.2 %collective-permute-start.17 = (bf16[32,2176]{1,0:T(8,128)(2,1)S(1)}, bf16[32,2176]{1,0:T(8,128)(2,1)S(1)}, u32[]{:S(2)}, u32[]{:S(2)}) collective-permute-start(bf16[32,2176]{1,0:T(8,128)(2,1)S(1)} %get-tuple-element.91), channel_id=1, source_target_pairs={{0,4},{1,5},{2,6},{3,7},{4,0},{5,1},{6,2},{7,3},{8,12},{9,13},{10,... | collective-permute-start | bytes 417800 | tf_op jit(solution)/shard_map/ppermute | solution.py:80
  59.4 6.5 %collective-permute-start.18 = (bf16[32,2176]{1,0:T(8,128)(2,1)S(1)}, bf16[32,2176]{1,0:T(8,128)(2,1)S(1)}, u32[]{:S(2)}, u32[]{:S(2)}) collective-permute-start(bf16[32,2176]{1,0:T(8,128)(2,1)S(1)} %get-tuple-element.92), channel_id=1, source_target_pairs={{0,2},{1,3},{2,0},{3,1},{4,6},{5,7},{6,4},{7,5},{8,10},{9,11},{10,... | collective-permute-start | bytes 417800 | tf_op jit(solution)/shard_map/ppermute | solution.py:80
  60.1 8.8 %collective-permute-start.19 = (bf16[32,2176]{1,0:T(8,128)(2,1)S(1)}, bf16[32,2176]{1,0:T(8,128)(2,1)S(1)}, u32[]{:S(2)}, u32[]{:S(2)}) collective-permute-start(bf16[32,2176]{1,0:T(8,128)(2,1)S(1)} %get-tuple-element.93), channel_id=1, source_target_pairs={{0,6},{1,7},{2,4},{3,5},{4,2},{5,3},{6,0},{7,1},{8,14},{9,15},{10,... | collective-permute-start | bytes 417800 | tf_op jit(solution)/shard_map/ppermute | solution.py:80
  61.7 8.0 %collective-permute-start.24 = (bf16[16,2176]{1,0:T(8,128)(2,1)S(1)}, bf16[16,2176]{1,0:T(8,128)(2,1)S(1)}, u32[]{:S(2)}, u32[]{:S(2)}) collective-permute-start(bf16[16,2176]{1,0:T(8,128)(2,1)S(1)} %get-tuple-element.101), channel_id=1, source_target_pairs={{0,8},{1,9},{2,10},{3,11},{4,12},{5,13},{6,14},{7,15},{8,0},{9,1},... | collective-permute-start | bytes 208904 | tf_op jit(solution)/shard_map/ppermute | solution.py:80
  69.3 5.5 %collective-permute-start.23 = (bf16[16,2176]{1,0:T(8,128)(2,1)S(1)}, bf16[16,2176]{1,0:T(8,128)(2,1)S(1)}, u32[]{:S(2)}, u32[]{:S(2)}) collective-permute-start(bf16[16,2176]{1,0:T(8,128)(2,1)S(1)} %get-tuple-element.99), channel_id=1, source_target_pairs={{0,8},{1,9},{2,10},{3,11},{4,12},{5,13},{6,14},{7,15},{8,0},{9,1},... | collective-permute-start | bytes 208904 | tf_op jit(solution)/shard_map/ppermute | solution.py:80
